TPU v7x, 32 devices: a whole 2x2x4 slice. The times are simulated.
32 devices in a mesh: groups: 2 (over y), dp: 8 (over z, x), mp: 2 (over core).
Axes of the slice: x: 2, y: 2, z: 4, core: 2. Of those that a mesh axis runs over, the one named last changes fastest.
Arguments:
- hidden_states: bfloat16 [32, 256, 5120], P(('groups', 'dp'), None, 'mp'), parts along dimension 0, may hold values from -6 to 6
- passage_states: bfloat16 [32, 256, 2048], P(('groups', 'dp')), parts along dimension 0, may hold values from -6 to 6
- down_weight: bfloat16 [2048, 5120], P('dp', 'mp'), may hold values from -0.078125 to 0.078125
- block_question: int32 [32, 1], P('groups'), parts along dimension 0, may hold values from 0 to 7; in each aligned block of 16 rows (0 to 15, 16 to 31, ...) at most 4 rows name the same one
- question_owner: int32 [16], P('groups'), parts along dimension 0, may hold values from 0 to 7, each once
- decoder_states: bfloat16 [16, 16, 2048], P(('groups', 'dp')), parts along dimension 0, may hold values from -60 to 60
Outputs:
- attended: bfloat16 [16, 16, 2048], P(('groups', 'dp')), parts along dimension 0
There are 2 independent parts, one for each index of `groups`. A program takes and returns all parts, laid end to end along the dimension named above; an argument that names none is the same for every part. Nothing has to cross between parts.
Inputs may be any that keep to these rules, and one draw needn't show every extreme that they name: `block_question`: no question is named by more than 4 passages, one by exactly 4; every question is named by some passage. `question_owner`: A permutation: every decoder slot owns exactly one question.
All inputs are finite; a program needn't handle non-finite values.
Results may differ from a plain program's by a relative error of at most 0.009.
The roundings to bfloat16 on the way count: a program that leaves them out, or rounds other values in their place, can miss the bound.
Values may be sent and summed in bfloat16 or wider, within the bound.
No kernel may reach another device: no remote copies, remote signals or barrier semaphores. Data moves between devices by JAX's collectives and lax.ppermute only.
A program may use at most 64 MiB of HBM per device.

v0:
```python
import jax
import jax.numpy as jnp
from jax import lax
from jax.sharding import PartitionSpec as P

HEAD_DIM = 64


def body(
    hidden_states, passage_states, down_weight, block_question, question_owner, decoder_states
):
    slot_count, block_len, unit_local = hidden_states.shape
    width = passage_states.shape[2]
    devices = lax.axis_size("dp")
    halves = lax.axis_size("mp")
    core_index = lax.axis_index("mp")
    owner_index = lax.axis_index("dp")
    block_total = block_question.shape[0]
    question_total = question_owner.shape[0]
    most = 2 * slot_count
    flat_hidden = hidden_states.reshape(slot_count * block_len, unit_local)
    partial_sums = lax.dot_general(
        flat_hidden,
        lax.all_gather(down_weight, "dp", axis=0, tiled=True),
        (((1,), (1,)), ((), ())),
        preferred_element_type=jnp.float32,
    )
    partial_sums = partial_sums.reshape(slot_count, block_len, width)
    summed = lax.psum_scatter(partial_sums, "mp", scatter_dimension=1, tiled=True)
    span = block_len // halves
    residual = lax.dynamic_slice_in_dim(passage_states, core_index * span, span, axis=1)
    encoded = (residual.astype(jnp.float32) + summed).astype(jnp.bfloat16)
    spread = lax.all_to_all(encoded, "dp", split_axis=1, concat_axis=0, tiled=True)
    questions = block_question[:, 0]
    question_ids = jnp.arange(question_total, dtype=jnp.int32)
    named = questions[:, None] == question_ids[None, :]
    dest_owner = jnp.sum(jnp.where(named, question_owner[None, :], 0), axis=1)
    positions = jnp.arange(block_total, dtype=jnp.int32)
    earlier = (questions[:, None] == questions[None, :]) & (positions[None, :] < positions[:, None])
    owner_rank = jnp.sum(earlier.astype(jnp.int32), axis=1)
    target = dest_owner * most + owner_rank
    slot_hits = jnp.arange(devices * most, dtype=jnp.int32)[:, None] == target[None, :]
    slot_block = jnp.sum(jnp.where(slot_hits, positions[None, :], 0), axis=1)
    slot_full = jnp.any(slot_hits, axis=1)
    picked = jnp.take(spread, slot_block, axis=0)
    picked = jnp.where(slot_full[:, None, None], picked, jnp.zeros_like(picked))
    outgoing = picked.reshape(devices, most, picked.shape[1], picked.shape[2])
    incoming = lax.all_to_all(outgoing, "dp", split_axis=0, concat_axis=0, tiled=True)
    my_question = jnp.sum(jnp.where(question_owner == owner_index, question_ids, 0))
    block_count = jnp.sum((questions == my_question).astype(jnp.int32))
    live = jnp.arange(most, dtype=jnp.int32) < block_count
    usable = jnp.broadcast_to(live[None, :, None], incoming.shape[:3]).reshape(-1)
    held_width = incoming.shape[3]
    heads_held = held_width // HEAD_DIM
    key_rows = incoming.reshape(-1, heads_held, HEAD_DIM)
    query_len = decoder_states.shape[1]
    query_rows = decoder_states.reshape(query_len, heads_held, HEAD_DIM)
    scores = jnp.einsum("qhd,khd->hqk", query_rows, key_rows, preferred_element_type=jnp.float32)
    masked = jnp.where(usable[None, None, :], scores, -jnp.inf)
    local_top = jnp.max(masked, axis=2)
    row_top = lax.pmax(local_top, "mp")
    weights = jnp.exp(masked - row_top[:, :, None])
    local_totals = jnp.sum(weights, axis=2)
    rounded = weights.astype(jnp.bfloat16)
    local_blend = jnp.einsum("hqk,khd->hqd", rounded, key_rows, preferred_element_type=jnp.float32)
    totals, blended = lax.psum((local_totals, local_blend), "mp")
    result = blended / totals[:, :, None]
    merged = jnp.transpose(result, (1, 0, 2)).reshape(query_len, held_width).astype(jnp.bfloat16)
    return merged.reshape(1, query_len, merged.shape[1])


def solution(mesh):
    placed = (
        P(("groups", "dp"), None, "mp"),
        P(("groups", "dp"), None, None),
        P("dp", "mp"),
        P("groups", None),
        P("groups"),
        P(("groups", "dp"), None, None),
    )
    return jax.shard_map(
        body, mesh=mesh, in_specs=placed, out_specs=P(("groups", "dp"), None, None), check_vma=False
    )
```

profile of v0, /device:TPU:0, one launch (start us, length us, event | category | flops | bytes accessed | tf_op | source)
XLA Modules:
  0.0 329.2 jit_solution(17047061799658095664)
XLA Ops:
  6.5 0.7 all-gather.2.cloned.1.call-update
  7.3 155.8 %all-gather.2.cloned.1.call-done = bf16[2048,2560]{1,0:T(8,128)(2,1)} async-done(((bf16[256,2560]{1,0:T(8,128)(2,1)}), bf16[2048,2560]{1,0:T(8,128)(2,1)}) %all-gather.2.cloned.1.call-update) | async-done | bytes 10485776 | tf_op jit(solution)/shard_map/all_gather | solution.py:24
  163.1 9.6 %fusion = f32[2,256,2048]{2,1,0:T(8,128)} fusion(bf16[2,256,2560]{2,1,0:T(8,128)(2,1)S(1)} %copy-done, bf16[2048,2560]{1,0:T(8,128)(2,1)} %all-gather.2.cloned.1.call-done), kind=kOutput, calls=%fused_computation.1 | convolution fusion | flops 5368709120 | bytes 17301504 | tf_op jit(solution)/shard_map/dot_general | solution.py:22
  172.8 10.4 %reduce-scatter.2.cloned.1.call-done = f32[2,128,2048]{2,1,0:T(8,128)} async-done(((f32[2,256,2048]{2,1,0:T(8,128)}), f32[2,128,2048]{2,1,0:T(8,128)}) %reduce-scatter.2.cloned.1.call-update) | async-done | bytes 2097168 | tf_op jit(solution)/shard_map/reduce_scatter | solution.py:29
  183.2 2.1 add_convert_fusion
  185.3 2.1 copy.25
  187.4 5.9 %all-to-all-start = ((bf16[2,128,2048]{2,0,1:T(2,128)(2,1)}), bf16[2,128,2048]{2,0,1:T(2,128)(2,1)}, u32[]{:S(2)}, u32[]{:S(2)}) async-start(bf16[2,128,2048]{2,0,1:T(2,128)(2,1)} %copy.25), calls=%async_computation.1 | async-start | bytes 2097152 | tf_op jit(solution)/shard_map/all_to_all | solution.py:33
  193.3 0.2 convert_reduce_fusion
  193.6 0.1 select_reduce_fusion
  193.8 0.1 fusion.10
  194.0 25.6 %all-to-all-done = bf16[2,128,2048]{2,0,1:T(2,128)(2,1)} async-done(((bf16[2,128,2048]{2,0,1:T(2,128)(2,1)}), bf16[2,128,2048]{2,0,1:T(2,128)(2,1)}, u32[]{:S(2)}, u32[]{:S(2)}) %all-to-all-start) | async-done | bytes 1048608 | tf_op jit(solution)/shard_map/all_to_all | solution.py:33
  219.5 1.6 copy.26
  221.1 1.1 copy.27
  222.2 3.2 gather_fusion
  225.4 3.3 select_select_fusion
  228.7 4.5 %all-to-all-start.1 = ((bf16[8,4,16,2048]{3,2,1,0:T(8,128)(2,1)}), bf16[8,4,16,2048]{3,2,1,0:T(8,128)(2,1)}, u32[]{:S(2)}, u32[]{:S(2)}) async-start(bf16[8,4,16,2048]{3,2,1,0:T(8,128)(2,1)} %select_select_fusion), calls=%async_computation.2 | async-start | bytes 4194304 | tf_op jit(solution)/shard_map/all_to_all | solution.py:48
  233.2 0.2 reshape.64
  233.4 0.6 fusion.12
  234.0 1.3 fusion.13
  235.3 0.6 iota_compare_fusion.3
  236.0 0.1 broadcast_in_dim.83
  236.1 44.9 %all-to-all-done.1 = bf16[8,4,16,2048]{3,2,1,0:T(8,128)(2,1)} async-done(((bf16[8,4,16,2048]{3,2,1,0:T(8,128)(2,1)}), bf16[8,4,16,2048]{3,2,1,0:T(8,128)(2,1)}, u32[]{:S(2)}, u32[]{:S(2)}) %all-to-all-start.1) | async-done | bytes 2097184 | tf_op jit(solution)/shard_map/all_to_all | solution.py:48
  281.0 7.1 %reshape.63 = bf16[512,32,64]{2,1,0:T(8,128)(2,1)} reshape(bf16[8,4,16,2048]{3,2,1,0:T(8,128)(2,1)} %all-to-all-done.1) | data formatting | bytes 4194304 | tf_op jit(solution)/shard_map/reshape | solution.py:55
  288.1 5.5 %copy.28 = bf16[512,32,64]{0,2,1:T(8,128)(2,1)} copy(bf16[512,32,64]{2,1,0:T(8,128)(2,1)} %reshape.63) | data formatting | bytes 4194304 | tf_op jit(solution)/shard_map/reshape | solution.py:55
  293.5 3.0 fusion.15
  296.5 3.3 %pmax.7 = f32[32,16]{1,0:T(8,128)S(1)} all-reduce(f32[32,16]{1,0:T(8,128)S(1)} %get-tuple-element.5), channel_id=1, replica_groups=mesh['groups'=2,'dp'=8,'mp'=2] {'mp'}, use_global_device_ids=true, to_apply=%region_8.9 | all-reduce | flops 512 | bytes 4096 | tf_op jit(solution)/shard_map/pmax | solution.py:61
  299.9 3.4 %fusion.5 = f32[32,16,64]{2,1,0:T(8,128)} fusion(bf16[512,32,64]{0,2,1:T(8,128)(2,1)} %copy.28, f32[32,16,512]{2,1,0:T(8,128)} %get-tuple-element.6, f32[32,16]{1,0:T(8,128)S(1)} %pmax.7), kind=kOutput, calls=%fused_computation.10 | convolution fusion | flops 34078720 | bytes 3278848 | tf_op jit(solution)/shard_map/hqk,khd->hqd/dot_general | solution.py:65
  303.2 1.5 fusion.3
  304.8 3.5 %psum.15 = f32[32,16]{1,0:T(8,128)S(1)} all-reduce(f32[32,16]{1,0:T(8,128)S(1)} %fusion.3), channel_id=1, replica_groups=mesh['groups'=2,'dp'=8,'mp'=2] {'mp'}, use_global_device_ids=true, to_apply=%region_11.12 | all-reduce | flops 512 | bytes 4096 | tf_op jit(solution)/shard_map/psum | solution.py:66
  308.3 12.4 %all-reduce.2.cloned.1.call-done = f32[32,16,64]{2,1,0:T(8,128)} async-done(((f32[32,16,64]{2,1,0:T(8,128)}), f32[32,16,64]{2,1,0:T(8,128)}) %all-reduce.2.cloned.1.call-update) | async-done | bytes 131088 | tf_op jit(solution)/shard_map/psum | solution.py:66
  320.7 1.1 fusion.9
  321.8 0.8 convert_element_type.38
  (22 shorter events, 0.5 us)
Async XLA Ops:
  6.5 156.6 %copy-start = (bf16[2,256,2560]{2,1,0:T(8,128)(2,1)S(1)}, bf16[2,256,2560]{2,1,0:T(8,128)(2,1)}, u32[]{:S(2)}) copy-start(bf16[2,256,2560]{2,1,0:T(8,128)(2,1)} %param.6) | copy-start | bytes 7864324
  6.5 156.6 %all-gather.2.cloned.1.call-start = ((), (), s32[]{:S(2)}) async-start(), calls=%async_computation.3 | async-start | bytes 11796480 | tf_op jit(solution)/shard_map/all_gather | solution.py:24
  7.3 175.9 %reduce-scatter.2.cloned.1.call-start = ((), (), s32[]{:S(2)}) async-start(), calls=%async_computation.4 | async-start | bytes 6291456 | tf_op jit(solution)/shard_map/reduce_scatter | solution.py:29
  185.3 8.0 %copy-start.3 = (s32[16,1]{0,1:T(1,128)S(1)}, s32[16,1]{0,1:T(1,128)}, u32[]{:S(2)}) copy-start(s32[16,1]{0,1:T(1,128)} %param.9) | copy-start | bytes 196
  185.3 8.2 %copy-start.2 = (s32[8]{0:T(128)S(1)}, s32[8]{0:T(128)}, u32[]{:S(2)}) copy-start(s32[8]{0:T(128)} %param.10) | copy-start | bytes 100
  187.4 32.1 %all-to-all-start = ((bf16[2,128,2048]{2,0,1:T(2,128)(2,1)}), bf16[2,128,2048]{2,0,1:T(2,128)(2,1)}, u32[]{:S(2)}, u32[]{:S(2)}) async-start(bf16[2,128,2048]{2,0,1:T(2,128)(2,1)} %copy.25), calls=%async_computation.1 | async-start | bytes 2097152 | tf_op jit(solution)/shard_map/all_to_all | solution.py:33
  228.7 4.5 %copy-start.1 = (bf16[1,16,2048]{2,1,0:T(8,128)(2,1)S(1)}, bf16[1,16,2048]{2,1,0:T(8,128)(2,1)}, u32[]{:S(2)}) copy-start(bf16[1,16,2048]{2,1,0:T(8,128)(2,1)} %param.11) | copy-start | bytes 196612
  228.7 52.3 %all-to-all-start.1 = ((bf16[8,4,16,2048]{3,2,1,0:T(8,128)(2,1)}), bf16[8,4,16,2048]{3,2,1,0:T(8,128)(2,1)}, u32[]{:S(2)}, u32[]{:S(2)}) async-start(bf16[8,4,16,2048]{3,2,1,0:T(8,128)(2,1)} %select_select_fusion), calls=%async_computation.2 | async-start | bytes 4194304 | tf_op jit(solution)/shard_map/all_to_all | solution.py:48
  233.1 87.6 %all-reduce.2.cloned.1.call-start = ((), (), s32[]{:S(2)}) async-start(), calls=%async_computation.5 | async-start | bytes 524288 | tf_op jit(solution)/shard_map/psum | solution.py:66
Sparse Core Ops, SparseCore 0:
  9.5 153.5 all-gather.1
  172.9 10.2 reduce-scatter.1
  303.4 17.2 all-reduce.1
where the time goes:
time: 330 us; the launch traced here: 329 us
  waiting for transfers between devices  250 us (76%)
  local copies, waits for them, and re-layouts  21.9 us (7%)
  matrix products  16 us (5%)
  between operations  13.2 us (4%)
  other arithmetic  11 us (3%)
  starting transfers between devices  10.4 us (3%)
  blocking collectives  6.88 us (2%)
    all_gather x1, waiting for transfers between devices, body(): lax.all_gather(down_weight, 'dp', axis=0, tiled=True)  156 us
    all_to_all x1, waiting for transfers between devices, body(): lax.all_to_all(outgoing, 'dp', split_axis=0, concat_axis=0, tiled=True)  44.9 us
    all_to_all x1, waiting for transfers between devices, body(): lax.all_to_all(encoded, 'dp', split_axis=1, concat_axis=0, tiled=True)  25.6 us
    reshape x2, local copies, waits for them, and re-layouts, body(): key_rows = incoming.reshape(-1, heads_held, HEAD_DIM)  12.5 us
    psum x1, waiting for transfers between devices, body(): totals, blended = lax.psum((local_totals, local_blend), 'mp')  12.4 us
    reduce_scatter x1, waiting for transfers between devices, body(): lax.psum_scatter(partial_sums, 'mp', scatter_dimension=1, tiled=True)  10.4 us
    dot_general x1, matrix products, body(): lax.dot_general(flat_hidden, lax.all_gather(down_weight, 'dp', axis=0, ti...  9.61 us
  transfers between devices with their start and end apart: 5, of which 5 were waited for; matrix products, arithmetic and copies ran while one was open for 2% of the time, Pallas kernels for 0%

commit v1 on v0

v1 whole, which is shorter than its diff:
```python
import functools

import jax
import jax.numpy as jnp
from jax import lax
from jax.experimental import pallas as pl
from jax.experimental.pallas import tpu as pltpu
from jax.sharding import Mesh, PartitionSpec as P

HEAD_DIM = 64
EMPTY = -3e38
VMEM_LIMIT = 40 * 1024 * 1024
SWAP = [(0, 1), (1, 0)]
CROSS = [(0, 3), (3, 0), (1, 2), (2, 1)]


def head_pick(tall, query_len):
    lanes = tall.shape[1]
    lane_head = lax.broadcasted_iota(jnp.int32, (query_len, lanes), 1) // HEAD_DIM
    picked = jnp.zeros((query_len, lanes), jnp.float32)
    for head in range(lanes // HEAD_DIM):
        picked = jnp.where(lane_head == head, tall[head * query_len : (head + 1) * query_len, :], picked)
    return picked


def attend_kernel(place_ref, query_ref, *refs):
    out_ref = refs[-1]
    pieces = refs[:-1]
    query_len, held = query_ref.shape[1:]
    heads = held // HEAD_DIM
    tall = heads * query_len
    out_ref[:, :, :held] = jnp.zeros(out_ref.shape[:2] + (held,), jnp.float32)
    ext_row = lax.broadcasted_iota(jnp.int32, out_ref.shape[:2] + (tall,), 1)
    out_ref[:, :, held:] = jnp.where(ext_row == 0, EMPTY, 0.0)
    row_head = lax.broadcasted_iota(jnp.int32, (tall, held), 0) // query_len
    lane_head = lax.broadcasted_iota(jnp.int32, (tall, held), 1) // HEAD_DIM
    diagonal = row_head == lane_head
    square = lax.broadcasted_iota(jnp.int32, (tall, tall), 0) == lax.broadcasted_iota(jnp.int32, (tall, tall), 1)
    ext = lax.broadcasted_iota(jnp.int32, (query_len, tall), 0)
    places, keys, scores, tops = [], [], [], []
    for piece in range(len(pieces) // 3):
        mine, other, residual = pieces[3 * piece : 3 * piece + 3]
        for block in range(mine.shape[0]):
            place = place_ref[len(places)]
            rows = residual[block].astype(jnp.float32) + (mine[block] + other[block])
            key_rows = rows.astype(jnp.bfloat16)
            query = jnp.concatenate([query_ref[place]] * heads, axis=0)
            query = jnp.where(diagonal, query, jnp.zeros_like(query))
            score = lax.dot_general(
                query, key_rows, (((1,), (1,)), ((), ())), preferred_element_type=jnp.float32
            )
            places.append(place)
            keys.append(key_rows)
            scores.append(score)
            tops.append(jnp.max(score, axis=1, keepdims=True))
    for at, place in enumerate(places):
        top = tops[at]
        for other_at, other_place in enumerate(places):
            if other_at != at:
                top = jnp.maximum(top, jnp.where(other_place == place, tops[other_at], EMPTY))
        weights = jnp.exp(scores[at] - top)
        total = jnp.sum(weights, axis=1, keepdims=True)
        blend = lax.dot_general(
            weights.astype(jnp.bfloat16), keys[at], (((1,), (0,)), ((), ())),
            preferred_element_type=jnp.float32,
        )
        top_row = jnp.sum(jnp.where(square, top, 0.0), axis=0, keepdims=True)
        total_row = jnp.sum(jnp.where(square, total, 0.0), axis=0, keepdims=True)
        out_ref[place, :, :held] = out_ref[place, :, :held] + head_pick(blend, query_len)
        before = out_ref[place, :, held:]
        out_ref[place, :, held:] = jnp.where(
            ext == 0, top_row, jnp.where(ext == 1, before + total_row, 0.0)
        )


def merge_kernel(*refs):
    out_ref = refs[-1]
    parts = refs[:-1]
    query_len, held = out_ref.shape[1:]
    tall = held // HEAD_DIM * query_len
    square = lax.broadcasted_iota(jnp.int32, (tall, tall), 0) == lax.broadcasted_iota(jnp.int32, (tall, tall), 1)

    def over(start, step):
        for part in parts:
            start = lax.fori_loop(
                0, part.shape[0], functools.partial(step, part), start, unroll=part.shape[0] <= 8
            )
        return start

    for slot in range(out_ref.shape[0]):
        def top_step(part, at, top):
            return jnp.maximum(top, part[at, slot, 0:1, held:])

        def total_step(part, at, total):
            return total + jnp.exp(part[at, slot, 0:1, held:] - top) * part[at, slot, 1:2, held:]

        def blend_step(part, at, blend):
            share = jnp.exp(part[at, slot, 0:1, held:] - top) / total
            column = jnp.sum(jnp.where(square, share, 0.0), axis=1, keepdims=True)
            spread = head_pick(jnp.broadcast_to(column, (tall, held)), query_len)
            return blend + spread * part[at, slot, :, :held]

        top = over(jnp.full((1, tall), EMPTY, jnp.float32), top_step)
        total = over(jnp.zeros((1, tall), jnp.float32), total_step)
        blend = over(jnp.zeros((query_len, held), jnp.float32), blend_step)
        out_ref[slot] = blend.astype(out_ref.dtype)


def in_vmem(count):
    return [pl.BlockSpec(memory_space=pltpu.VMEM)] * count


def body(hidden_states, passage_states, down_weight, block_question, question_owner, decoder_states):
    blocks, block_len, units = hidden_states.shape
    width = passage_states.shape[2]
    query_len = decoder_states.shape[1]
    highs, lows, cores = lax.axis_size("high"), lax.axis_size("low"), lax.axis_size("mp")
    group, high, side, low, core = (lax.axis_index(name) for name in ("groups", "high", "side", "low", "mp"))
    shard = down_weight.shape[0]
    stride = lows * shard
    held = width // 2 // cores
    heads = held // HEAD_DIM
    per_core = highs // cores
    members = highs * lows
    slot_total = question_owner.shape[0]
    rows = blocks * block_len

    def features(array, of_side):
        first = (core * per_core * 2 + of_side) * stride
        return jnp.concatenate(
            [
                lax.dynamic_slice_in_dim(array, first + at * 2 * stride, stride, axis=array.ndim - 1)
                for at in range(per_core)
            ],
            axis=-1,
        )

    partner_hidden = [lax.ppermute(hidden_states[at], "side", SWAP) for at in range(blocks)]
    partner_residual = lax.ppermute(features(passage_states, 1 - side), "side", SWAP)
    own_residual = features(passage_states, side)
    own_query = features(decoder_states, side)
    partner_query = lax.ppermute(features(decoder_states, 1 - side), "side", SWAP)
    queries = jnp.where(
        side == 0,
        jnp.concatenate([own_query, partner_query], axis=0),
        jnp.concatenate([partner_query, own_query], axis=0),
    )
    queries = lax.all_gather(queries, ("high", "low"), axis=0, tiled=True)

    if highs == 4 and lows == 1:
        half = shard // 2
        sent = lax.dynamic_slice_in_dim(down_weight, group * half, half, axis=0)
        after = [(at, (at + 1) % highs) for at in range(highs)]
        ahead = [(at, (at - 1) % highs) for at in range(highs)]
        from_one = lax.ppermute(sent, "high", after)
        from_three = lax.ppermute(sent, "high", ahead)
        from_two = lax.ppermute(from_one, "high", after)
        weight = jnp.zeros((highs * shard, units), down_weight.dtype)

        def placed(weight, piece, offset, of_half):
            at = lax.rem(high + offset + 2 * highs - core * per_core, highs)
            return lax.dynamic_update_slice_in_dim(weight, piece, at * shard + of_half * half, axis=0)

        weight = placed(weight, down_weight, 0, 0)
        for piece, offset in ((from_one, -1), (from_three, 1), (from_two, -2)):
            weight = placed(weight, piece, offset, group)
            weight = placed(weight, lax.ppermute(piece, "groups", SWAP), offset, 1 - group)
    else:
        weight = lax.all_gather(down_weight, ("high", "low"), axis=0, tiled=True)
        weight = jnp.where(core == 0, weight, jnp.roll(weight, held, axis=0))

    def project(flat):
        def part(rows_of):
            return lax.dot_general(
                flat, rows_of, (((1,), (1,)), ((), ())), preferred_element_type=jnp.float32
            ).reshape(-1, block_len, held)

        other = lax.ppermute(part(weight[held:]), "mp", SWAP)
        return part(weight[:held]), other

    questions = block_question[:, 0]
    question_ids = jnp.arange(slot_total, dtype=jnp.int32)
    owners = jnp.sum(jnp.where(questions[:, None] == question_ids[None, :], question_owner[None, :], 0), axis=1)
    owner_high, owner_side, owner_low = owners // (2 * lows), (owners // lows) % 2, owners % lows
    owner_place = (owner_high * lows + owner_low) * 2 + owner_side
    own_at = ((high * 2 + side) * lows + low) * blocks
    partner_at = ((high * 2 + 1 - side) * lows + low) * blocks
    places = jnp.concatenate(
        [lax.dynamic_slice_in_dim(owner_place, at, blocks) for at in (own_at, partner_at)]
    )

    pieces = [*project(hidden_states.reshape(rows, units)), own_residual]
    for at in range(blocks):
        pieces += [*project(partner_hidden[at]), partner_residual[at : at + 1]]
    partials = pl.pallas_call(
        attend_kernel,
        out_shape=jax.ShapeDtypeStruct((2 * members, query_len, held + heads * query_len), jnp.float32),
        in_specs=[pl.BlockSpec(memory_space=pltpu.SMEM)] + in_vmem(1 + len(pieces)),
        out_specs=pl.BlockSpec(memory_space=pltpu.VMEM),
        compiler_params=pltpu.CompilerParams(vmem_limit_bytes=VMEM_LIMIT),
        name="attend",
    )(places, queries, *pieces)
    partials = partials.reshape((members, 2) + partials.shape[1:])

    if highs == 4 and lows == 1:
        received = []
        for shift in range(highs):
            outgoing = lax.dynamic_slice_in_dim(partials, lax.rem(high + shift, highs), 1, axis=0)
            pairs = [(at, (at + shift) % highs) for at in range(highs)]
            received.append(lax.ppermute(outgoing, "high", pairs) if shift else outgoing)
    else:
        received = [lax.all_to_all(partials, ("high", "low"), split_axis=0, concat_axis=0, tiled=True)]
    merged = pl.pallas_call(
        merge_kernel,
        out_shape=jax.ShapeDtypeStruct((2, query_len, held), decoder_states.dtype),
        in_specs=in_vmem(len(received)),
        out_specs=pl.BlockSpec(memory_space=pltpu.VMEM),
        compiler_params=pltpu.CompilerParams(vmem_limit_bytes=VMEM_LIMIT),
        name="merge",
    )(*received)

    mine = lax.dynamic_slice_in_dim(merged, side, 1, axis=0)
    away = lax.dynamic_slice_in_dim(merged, 1 - side, 1, axis=0)
    by_core = lax.ppermute(mine, "mp", SWAP)
    by_side = lax.ppermute(away, "side", SWAP)
    by_both = lax.ppermute(away, ("side", "mp"), CROSS)
    near = [jnp.where(core == at, mine, by_core) for at in range(cores)]
    far = [jnp.where(core == at, by_side, by_both) for at in range(cores)]
    columns = []
    for at in range(highs):
        span = slice(at % per_core * stride, (at % per_core + 1) * stride)
        mine_span, away_span = near[at // per_core][:, :, span], far[at // per_core][:, :, span]
        columns += [jnp.where(side == 0, mine_span, away_span), jnp.where(side == 0, away_span, mine_span)]
    return jnp.concatenate(columns, axis=-1)


def solution(mesh):
    groups, dp, cores = mesh.shape["groups"], mesh.shape["dp"], mesh.shape["mp"]

    def run(hidden_states, passage_states, down_weight, block_question, question_owner, decoder_states):
        lows = max(1, HEAD_DIM * dp // down_weight.shape[0])
        fine = Mesh(
            mesh.devices.reshape(groups, dp // (2 * lows), 2, lows, cores),
            ("groups", "high", "side", "low", "mp"),
        )
        split = ("groups", "high", "side", "low")
        placed = (
            P(split, None, "mp"),
            P(split, None, None),
            P(("high", "side", "low"), "mp"),
            P("groups", None),
            P("groups"),
            P(split, None, None),
        )
        return jax.shard_map(
            body, mesh=fine, in_specs=placed, out_specs=P(split, None, None), check_vma=False
        )(hidden_states, passage_states, down_weight, block_question, question_owner, decoder_states)

    return run
```

time: 330 us -> 142 us (0.43)
  waiting for transfers between devices: 250 us -> 53.9 us
  blocking collectives: 6.88 us -> 25.6 us
  between operations: 13.2 us -> 0.29 us
  starting transfers between devices: 10.4 us -> 20.5 us
  other arithmetic: 11 us -> 2.71 us
    all_gather x1 -> x0, waiting for transfers between devices: 156 us -> none  [body(): lax.all_gather(down_weight, 'dp', axis=0, tiled=True)]
    all_to_all x2 -> x0, waiting for transfers between devices: 70.4 us -> none  [the longest x1 44.9 us: body(): lax.all_to_all(outgoing, 'dp', split_axis=0, concat_axis=0, tiled=True)]
    ppermute x0 -> x19, waiting for transfers between devices: none -> 53.9 us  [the longest x1 26.1 us: body(): lax.ppermute(features(decoder_states, 1 - side), 'side', SWAP)]
    all_gather x0 -> x1, blocking collectives: none -> 25.6 us  [body(): queries = lax.all_gather(queries, ('high', 'low'), axis=0, tiled=True)]
    ppermute x0 -> x19, starting transfers between devices: none -> 20.5 us  [the longest x3 3.87 us: body(): lax.ppermute(outgoing, 'high', pairs)]
    reshape x3 -> x0, local copies, waits for them, and re-layouts: 12.7 us -> none  [the longest x2 12.5 us: body(): key_rows = incoming.reshape(-1, heads_held, HEAD_DIM)]
    psum x1 -> x0, waiting for transfers between devices: 12.4 us -> none  [body(): totals, blended = lax.psum((local_totals, local_blend), 'mp')]
    reduce_scatter x1 -> x0, waiting for transfers between devices: 10.4 us -> none  [body(): lax.psum_scatter(partial_sums, 'mp', scatter_dimension=1, tiled=True)]
  transfers between devices with their start and end apart: 5 -> 19, of which waited for: 5 -> 8; matrix products, arithmetic and copies ran while one was open for 2% -> 26% of each run, Pallas kernels for 0% -> 0%
where the time goes in v1:
time: 142 us
  waiting for transfers between devices  53.9 us (38%)
  blocking collectives  25.6 us (18%)
  starting transfers between devices  20.5 us (14%)
  local copies, waits for them, and re-layouts  19 us (13%)
  matrix products  17.9 us (13%)
  other arithmetic  2.71 us (2%)
  Pallas kernels  1.71 us (1%)
    ppermute x1, waiting for transfers between devices, body(): lax.ppermute(features(decoder_states, 1 - side), 'side', SWAP)  26.1 us
    all_gather x1, blocking collectives, body(): queries = lax.all_gather(queries, ('high', 'low'), axis=0, tiled=True)  25.6 us
    dot_general x6, matrix products, part(): lax.dot_general(flat, rows_of, (((1,), (1,)), ((), ())), preferred_elemen...  17.9 us
    ppermute x3, waiting for transfers between devices, body(): lax.ppermute(piece, 'groups', SWAP)  17.4 us
    dynamic_update_slice x7, local copies, waits for them, and re-layouts, placed(): lax.dynamic_update_slice_in_dim(weight, piece, at * shard + of_half * hal...  8.67 us
    ppermute x3, waiting for transfers between devices, body(): lax.ppermute(outgoing, 'high', pairs)  5.93 us
    ppermute x3, starting transfers between devices, body(): lax.ppermute(outgoing, 'high', pairs)  3.87 us
    ppermute x3, starting transfers between devices, body(): lax.ppermute(piece, 'groups', SWAP)  3.86 us
  transfers between devices with their start and end apart: 19, of which 8 were waited for; matrix products, arithmetic and copies ran while one was open for 26% of the time, Pallas kernels for 0%

profile of v1, /device:TPU:0, one launch (start us, length us, event | category | flops | bytes accessed | tf_op | source)
XLA Modules:
  0.0 141.7 jit_solution(13023409217376870372)
XLA Ops:
  0.0 2.0 %constant_dynamic-slice_fusion.10 = bf16[128,2560]{1,0:T(8,128)(2,1)} fusion(bf16[256,2560]{1,0:T(8,128)(2,1)} %param.8, s32[]{:T(128)S(6)} %select_n.163), kind=kLoop, calls=%fused_computation.50 | loop fusion | bytes 1310724 | tf_op jit(solution)/shard_map/dynamic_slice | solution.py:152
  2.0 3.0 %collective-permute-start.1 = (bf16[128,2560]{1,0:T(8,128)(2,1)}, bf16[128,2560]{1,0:T(8,128)(2,1)}, u32[]{:S(2)}, u32[]{:S(2)}) collective-permute-start(bf16[128,2560]{1,0:T(8,128)(2,1)} %constant_dynamic-slice_fusion.10), channel_id=1, source_target_pairs={{0,4},{4,8},{8,12},{12,0},{1,5},{5,9},{9,13},{13,1},{2,6},{6,10},{... | collective-permute-start | bytes 1966088 | tf_op jit(solution)/shard_map/ppermute | solution.py:155
  5.1 2.0 %collective-permute-start.3 = (bf16[128,2560]{1,0:T(8,128)(2,1)}, bf16[128,2560]{1,0:T(8,128)(2,1)}, u32[]{:S(2)}, u32[]{:S(2)}) collective-permute-start(bf16[128,2560]{1,0:T(8,128)(2,1)} %constant_dynamic-slice_fusion.10), channel_id=1, source_target_pairs={{0,12},{4,0},{8,4},{12,8},{1,13},{5,1},{9,5},{13,9},{2,14},{6,2},{... | collective-permute-start | bytes 1966088 | tf_op jit(solution)/shard_map/ppermute | solution.py:156
  7.1 1.9 %slice_bitcast_fusion = (bf16[256,2560]{1,0:T(8,128)(2,1)S(1)}, bf16[256,2560]{1,0:T(8,128)(2,1)S(1)}) fusion(bf16[2,256,2560]{2,1,0:T(8,128)(2,1)} %param.6), kind=kLoop, calls=%fused_computation.12 | loop fusion | bytes 5242880 | tf_op jit(solution)/shard_map/squeeze | solution.py:138
  9.0 1.8 %collective-permute-start.11 = (bf16[256,2560]{1,0:T(8,128)(2,1)S(1)}, bf16[256,2560]{1,0:T(8,128)(2,1)}, u32[]{:S(2)}, u32[]{:S(2)}) collective-permute-start(bf16[256,2560]{1,0:T(8,128)(2,1)S(1)} %get-tuple-element.5), channel_id=1, source_target_pairs={{0,2},{2,0},{1,3},{3,1},{4,6},{6,4},{5,7},{7,5},{8,10},{10,8},{9,1... | collective-permute-start | bytes 3932168 | tf_op jit(solution)/shard_map/ppermute | solution.py:138
  10.8 2.0 %constant_dynamic-slice_fusion.7 = (bf16[2,256,256]{2,1,0:T(8,128)(2,1)S(1)}, bf16[2,256,256]{2,1,0:T(8,128)(2,1)S(1)}, bf16[2,256,256]{2,1,0:T(8,128)(2,1)}, bf16[2,256,256]{2,1,0:T(8,128)(2,1)S(1)}) fusion(bf16[2,256,2048]{2,1,0:T(8,128)(2,1)} %param.7, s32[]{:T(128)S(6)} %select_n.159, s32[]{:T(128)S(6)} %select_n.158, s32[]{:T(128)S(6)} %select_n.157, ...), kind=kLoop, calls=%fused_computation.41 | loop fusion | bytes 2097168 | tf_op jit(solution)/shard_map/dynamic_slice | solution.py:132
  13.9 1.8 %collective-permute-start = (bf16[1,16,512]{2,1,0:T(8,128)(2,1)S(1)}, bf16[1,16,512]{2,1,0:T(8,128)(2,1)S(1)}, u32[]{:S(2)}, u32[]{:S(2)}) collective-permute-start(bf16[1,16,512]{2,1,0:T(8,128)(2,1)S(1)} %pad_maximum_fusion.2), channel_id=1, source_target_pairs={{0,2},{2,0},{1,3},{3,1},{4,6},{6,4},{5,7},{7,5},{8,10},{10,8},{9,1... | collective-permute-start | bytes 49160 | tf_op jit(solution)/shard_map/ppermute | solution.py:142
  15.7 2.7 %broadcast_in_dim.19 = bf16[1024,2560]{1,0:T(8,128)(2,1)} broadcast(bf16[]{:T(256)} %constant.102.clone.1), dimensions={} | broadcast | bytes 5242882 | tf_op jit(solution)/shard_map/broadcast_in_dim | solution.py:158
  18.4 1.2 constant_dynamic-update-slice_fusion.14
  20.8 2.2 %collective-permute-done.1 = bf16[128,2560]{1,0:T(8,128)(2,1)} collective-permute-done((bf16[128,2560]{1,0:T(8,128)(2,1)}, bf16[128,2560]{1,0:T(8,128)(2,1)}, u32[]{:S(2)}, u32[]{:S(2)}) %collective-permute-start.1) | collective-permute-done | bytes 655392 | tf_op jit(solution)/shard_map/ppermute | solution.py:155
  23.0 1.8 %collective-permute-start.2 = (bf16[128,2560]{1,0:T(8,128)(2,1)}, bf16[128,2560]{1,0:T(8,128)(2,1)S(1)}, u32[]{:S(2)}, u32[]{:S(2)}) collective-permute-start(bf16[128,2560]{1,0:T(8,128)(2,1)} %collective-permute-done.1), channel_id=1, source_target_pairs={{0,16},{16,0},{1,17},{17,1},{2,18},{18,2},{3,19},{19,3},{4,20},{20... | collective-permute-start | bytes 1966088 | tf_op jit(solution)/shard_map/ppermute | solution.py:167
  24.8 26.1 %collective-permute-done = bf16[1,16,512]{2,1,0:T(8,128)(2,1)S(1)} collective-permute-done((bf16[1,16,512]{2,1,0:T(8,128)(2,1)S(1)}, bf16[1,16,512]{2,1,0:T(8,128)(2,1)S(1)}, u32[]{:S(2)}, u32[]{:S(2)}) %collective-permute-start) | collective-permute-done | bytes 16416 | tf_op jit(solution)/shard_map/ppermute | solution.py:142
  50.9 25.6 %all_gather.3.query_ref = bf16[8,16,512]{2,1,0:T(8,128)(2,1)S(1)} all-gather(bf16[2,16,512]{2,1,0:T(8,128)(2,1)S(1)} %maximum_select_fusion), channel_id=1, replica_groups=mesh['groups'=2,'high'=4,'side'=2,'low'=1,'mp'=2] {'high','low'}, dimensions={0}, use_global_device_ids=true | all-gather | bytes 163840 | tf_op jit(solution)/shard_map/all_gather | solution.py:148
  76.5 1.2 collective-permute-start.8
  77.8 1.1 fusion.25
  78.8 1.6 %collective-permute-start.4 = (bf16[128,2560]{1,0:T(8,128)(2,1)}, bf16[128,2560]{1,0:T(8,128)(2,1)S(1)}, u32[]{:S(2)}, u32[]{:S(2)}) collective-permute-start(bf16[128,2560]{1,0:T(8,128)(2,1)} %collective-permute-done.3), channel_id=1, source_target_pairs={{0,16},{16,0},{1,17},{17,1},{2,18},{18,2},{3,19},{19,3},{4,20},{20... | collective-permute-start | bytes 1966088 | tf_op jit(solution)/shard_map/ppermute | solution.py:167
  80.4 2.0 %constant_dynamic-update-slice_fusion.13 = bf16[1024,2560]{1,0:T(8,128)(2,1)} fusion(bf16[1024,2560]{1,0:T(8,128)(2,1)} %constant_dynamic-update-slice_fusion.14, bf16[128,2560]{1,0:T(8,128)(2,1)} %collective-permute-done.1, s32[]{:T(128)S(6)} %select_n.164), kind=kLoop, calls=%fused_computation.49 | loop fusion | bytes 1310724 | tf_op jit(solution)/shard_map/dynamic_update_slice | solution.py:162
  83.8 2.0 %constant_dynamic-update-slice_fusion.11 = bf16[1024,2560]{1,0:T(8,128)(2,1)} fusion(bf16[1024,2560]{1,0:T(8,128)(2,1)} %constant_dynamic-update-slice_fusion.12, bf16[128,2560]{1,0:T(8,128)(2,1)} %collective-permute-done.3, s32[]{:T(128)S(6)} %select_n.166), kind=kLoop, calls=%fused_computation.47 | loop fusion | bytes 1310724 | tf_op jit(solution)/shard_map/dynamic_update_slice | solution.py:162
  85.8 11.0 %collective-permute-done.4 = bf16[128,2560]{1,0:T(8,128)(2,1)S(1)} collective-permute-done((bf16[128,2560]{1,0:T(8,128)(2,1)}, bf16[128,2560]{1,0:T(8,128)(2,1)S(1)}, u32[]{:S(2)}, u32[]{:S(2)}) %collective-permute-start.4) | collective-permute-done | bytes 655392 | tf_op jit(solution)/shard_map/ppermute | solution.py:167
  98.6 6.4 %collective-permute-done.6 = bf16[128,2560]{1,0:T(8,128)(2,1)S(1)} collective-permute-done((bf16[128,2560]{1,0:T(8,128)(2,1)S(1)}, bf16[128,2560]{1,0:T(8,128)(2,1)S(1)}, u32[]{:S(2)}, u32[]{:S(2)}) %collective-permute-start.6) | collective-permute-done | bytes 655392 | tf_op jit(solution)/shard_map/ppermute | solution.py:167
  105.8 3.0 %fusion.21 = f32[1,256,512]{2,1,0:T(8,128)S(1)} fusion(bf16[256,2560]{1,0:T(8,128)(2,1)} %collective-permute-done.11, bf16[1024,2560]{1,0:T(8,128)(2,1)} %constant_dynamic-update-slice_fusion.8), kind=kOutput, calls=%fused_computation.17 | convolution fusion | flops 671088640 | bytes 4456448 | tf_op jit(solution)/shard_map/dot_general | solution.py:174
  108.9 2.8 %fusion.18 = f32[1,256,512]{2,1,0:T(8,128)S(1)} fusion(bf16[256,2560]{1,0:T(8,128)(2,1)S(1)} %collective-permute-done.8, bf16[1024,2560]{1,0:T(8,128)(2,1)} %constant_dynamic-update-slice_fusion.8), kind=kOutput, calls=%fused_computation.16 | convolution fusion | flops 671088640 | bytes 4456448 | tf_op jit(solution)/shard_map/dot_general | solution.py:174
  112.1 3.3 %fusion.4 = f32[512,512]{0,1:T(8,128)S(1)} fusion(bf16[512,2560]{1,0:T(8,128)(2,1)S(1)} %bitcast.37, bf16[1024,2560]{1,0:T(8,128)(2,1)} %constant_dynamic-update-slice_fusion.8), kind=kOutput, calls=%fused_computation.4 | convolution fusion | flops 1342177280 | bytes 6291456 | tf_op jit(solution)/shard_map/dot_general | solution.py:174
  115.6 2.6 %fusion.12.refs_3_ = f32[1,256,512]{2,1,0:T(8,128)S(1)} fusion(bf16[256,2560]{1,0:T(8,128)(2,1)S(1)} %collective-permute-done.8, bf16[1024,2560]{1,0:T(8,128)(2,1)} %constant_dynamic-update-slice_fusion.8), kind=kOutput, calls=%fused_computation.14 | convolution fusion | flops 671088640 | bytes 4456448 | tf_op jit(solution)/shard_map/dot_general | solution.py:174
  118.2 3.0 %fusion.15.refs_6_ = f32[1,256,512]{2,1,0:T(8,128)S(1)} fusion(bf16[256,2560]{1,0:T(8,128)(2,1)} %collective-permute-done.11, bf16[1024,2560]{1,0:T(8,128)(2,1)} %constant_dynamic-update-slice_fusion.8), kind=kOutput, calls=%fused_computation.15 | convolution fusion | flops 671088640 | bytes 4456448 | tf_op jit(solution)/shard_map/dot_general | solution.py:174
  121.2 3.3 %fusion.10 = f32[512,512]{0,1:T(8,128)S(1)} fusion(bf16[512,2560]{1,0:T(8,128)(2,1)S(1)} %bitcast.38, bf16[1024,2560]{1,0:T(8,128)(2,1)} %constant_dynamic-update-slice_fusion.8), kind=kOutput, calls=%fused_computation.10 | convolution fusion | flops 1342177280 | bytes 6291456 | tf_op jit(solution)/shard_map/dot_general | solution.py:174
  124.5 1.5 %attend.1 = f32[8,16,640]{2,1,0:T(8,128)S(1)} custom-call(s32[4]{0:T(128)S(1)} %pad_add_fusion.place_ref, bf16[8,16,512]{2,1,0:T(8,128)(2,1)S(1)} %all_gather.3.query_ref, f32[2,256,512]{2,1,0:T(8,128)S(1)} %bitcast.36, f32[2,256,512]{2,1,0:T(8,128)S(1)} %collective-permute-done.7.refs_1_, bf16[2,256,512]{2,1,0:T(8,128)(2,1)S(1)} %pad_maximum_fusion.refs_2_, ...), custom_call_target="tpu_custom_call" | custom-call | tf_op jit(solution)/shard_map/attend/pallas_call | solution.py:195
  126.1 1.8 %collective-permute-start.14 = (f32[1,2,16,640]{3,2,1,0:T(8,128)S(1)}, f32[1,2,16,640]{3,2,1,0:T(8,128)S(1)}, u32[]{:S(2)}, u32[]{:S(2)}) collective-permute-start(f32[1,2,16,640]{3,2,1,0:T(8,128)S(1)} %get-tuple-element.14), channel_id=1, source_target_pairs={{0,8},{4,12},{8,0},{12,4},{1,9},{5,13},{9,1},{13,5},{2,10},{6,14},... | collective-permute-start | bytes 245768 | tf_op jit(solution)/shard_map/ppermute | solution.py:210
  127.9 2.0 %collective-permute-start.15 = (f32[1,2,16,640]{3,2,1,0:T(8,128)S(1)}, f32[1,2,16,640]{3,2,1,0:T(8,128)S(1)}, u32[]{:S(2)}, u32[]{:S(2)}) collective-permute-start(f32[1,2,16,640]{3,2,1,0:T(8,128)S(1)} %get-tuple-element.13), channel_id=1, source_target_pairs={{0,12},{4,0},{8,4},{12,8},{1,13},{5,1},{9,5},{13,9},{2,14},{6,2},{... | collective-permute-start | bytes 245768 | tf_op jit(solution)/shard_map/ppermute | solution.py:210
  129.9 3.3 %collective-permute-done.13.refs_1_ = f32[1,2,16,640]{3,2,1,0:T(8,128)S(1)} collective-permute-done((f32[1,2,16,640]{3,2,1,0:T(8,128)S(1)}, f32[1,2,16,640]{3,2,1,0:T(8,128)S(1)}, u32[]{:S(2)}, u32[]{:S(2)}) %collective-permute-start.13) | collective-permute-done | bytes 81952 | tf_op jit(solution)/shard_map/ppermute | solution.py:210
  133.2 2.6 %collective-permute-done.14.refs_2_ = f32[1,2,16,640]{3,2,1,0:T(8,128)S(1)} collective-permute-done((f32[1,2,16,640]{3,2,1,0:T(8,128)S(1)}, f32[1,2,16,640]{3,2,1,0:T(8,128)S(1)}, u32[]{:S(2)}, u32[]{:S(2)}) %collective-permute-start.14) | collective-permute-done | bytes 81952 | tf_op jit(solution)/shard_map/ppermute | solution.py:210
  138.0 1.9 %collective-permute-done.17 = bf16[1,16,512]{2,1,0:T(8,128)(2,1)S(1)} collective-permute-done((bf16[1,16,512]{2,1,0:T(8,128)(2,1)S(1)}, bf16[1,16,512]{2,1,0:T(8,128)(2,1)S(1)}, u32[]{:S(2)}, u32[]{:S(2)}) %collective-permute-start.17) | collective-permute-done | bytes 16416 | tf_op jit(solution)/shard_map/ppermute | solution.py:225
  (60 shorter events, 11.2 us)
Async XLA Ops:
  2.0 21.0 %collective-permute-start.1 = (bf16[128,2560]{1,0:T(8,128)(2,1)}, bf16[128,2560]{1,0:T(8,128)(2,1)}, u32[]{:S(2)}, u32[]{:S(2)}) collective-permute-start(bf16[128,2560]{1,0:T(8,128)(2,1)} %constant_dynamic-slice_fusion.10), channel_id=1, source_target_pairs={{0,4},{4,8},{8,12},{12,0},{1,5},{5,9},{9,13},{13,1},{2,6},{6,10},{... | collective-permute-start | bytes 1966088 | tf_op jit(solution)/shard_map/ppermute | solution.py:155
  5.1 73.8 %collective-permute-start.3 = (bf16[128,2560]{1,0:T(8,128)(2,1)}, bf16[128,2560]{1,0:T(8,128)(2,1)}, u32[]{:S(2)}, u32[]{:S(2)}) collective-permute-start(bf16[128,2560]{1,0:T(8,128)(2,1)} %constant_dynamic-slice_fusion.10), channel_id=1, source_target_pairs={{0,12},{4,0},{8,4},{12,8},{1,13},{5,1},{9,5},{13,9},{2,14},{6,2},{... | collective-permute-start | bytes 1966088 | tf_op jit(solution)/shard_map/ppermute | solution.py:156
  9.0 4.9 %copy-start.2 = (bf16[1,16,2048]{2,1,0:T(8,128)(2,1)S(1)}, bf16[1,16,2048]{2,1,0:T(8,128)(2,1)}, u32[]{:S(2)}) copy-start(bf16[1,16,2048]{2,1,0:T(8,128)(2,1)} %param.11) | copy-start | bytes 196612
  9.0 96.8 %collective-permute-start.11 = (bf16[256,2560]{1,0:T(8,128)(2,1)S(1)}, bf16[256,2560]{1,0:T(8,128)(2,1)}, u32[]{:S(2)}, u32[]{:S(2)}) collective-permute-start(bf16[256,2560]{1,0:T(8,128)(2,1)S(1)} %get-tuple-element.5), channel_id=1, source_target_pairs={{0,2},{2,0},{1,3},{3,1},{4,6},{6,4},{5,7},{7,5},{8,10},{10,8},{9,1... | collective-permute-start | bytes 3932168 | tf_op jit(solution)/shard_map/ppermute | solution.py:138
  13.6 62.9 %collective-permute-start.10 = (bf16[2,256,512]{2,1,0:T(8,128)(2,1)}, bf16[2,256,512]{2,1,0:T(8,128)(2,1)}, u32[]{:S(2)}, u32[]{:S(2)}) collective-permute-start(bf16[2,256,512]{2,1,0:T(8,128)(2,1)} %pad_maximum_fusion.1), channel_id=1, source_target_pairs={{0,2},{2,0},{1,3},{3,1},{4,6},{6,4},{5,7},{7,5},{8,10},{10,8},{9,1... | collective-permute-start | bytes 1572872 | tf_op jit(solution)/shard_map/ppermute | solution.py:139
  13.9 36.9 %collective-permute-start = (bf16[1,16,512]{2,1,0:T(8,128)(2,1)S(1)}, bf16[1,16,512]{2,1,0:T(8,128)(2,1)S(1)}, u32[]{:S(2)}, u32[]{:S(2)}) collective-permute-start(bf16[1,16,512]{2,1,0:T(8,128)(2,1)S(1)} %pad_maximum_fusion.2), channel_id=1, source_target_pairs={{0,2},{2,0},{1,3},{3,1},{4,6},{6,4},{5,7},{7,5},{8,10},{10,8},{9,1... | collective-permute-start | bytes 49160 | tf_op jit(solution)/shard_map/ppermute | solution.py:142
  15.7 2.7 %copy-start = (bf16[256,2560]{1,0:T(8,128)(2,1)S(1)}, bf16[256,2560]{1,0:T(8,128)(2,1)}, u32[]{:S(2)}) copy-start(bf16[256,2560]{1,0:T(8,128)(2,1)} %param.8) | copy-start | bytes 3932164
  18.4 1.2 copy-start.4
  18.4 1.2 copy-start.5
  23.0 59.9 %collective-permute-start.2 = (bf16[128,2560]{1,0:T(8,128)(2,1)}, bf16[128,2560]{1,0:T(8,128)(2,1)S(1)}, u32[]{:S(2)}, u32[]{:S(2)}) collective-permute-start(bf16[128,2560]{1,0:T(8,128)(2,1)} %collective-permute-done.1), channel_id=1, source_target_pairs={{0,16},{16,0},{1,17},{17,1},{2,18},{18,2},{3,19},{19,3},{4,20},{20... | collective-permute-start | bytes 1966088 | tf_op jit(solution)/shard_map/ppermute | solution.py:167
  50.9 31.5 %collective-permute-start.5 = (bf16[128,2560]{1,0:T(8,128)(2,1)}, bf16[128,2560]{1,0:T(8,128)(2,1)S(1)}, u32[]{:S(2)}, u32[]{:S(2)}) collective-permute-start(bf16[128,2560]{1,0:T(8,128)(2,1)} %collective-permute-done.1), channel_id=1, source_target_pairs={{0,4},{4,8},{8,12},{12,0},{1,5},{5,9},{9,13},{13,1},{2,6},{6,10},{... | collective-permute-start | bytes 1966088 | tf_op jit(solution)/shard_map/ppermute | solution.py:157
  76.5 32.3 %collective-permute-start.8 = (bf16[256,2560]{1,0:T(8,128)(2,1)S(1)}, bf16[256,2560]{1,0:T(8,128)(2,1)S(1)}, u32[]{:S(2)}, u32[]{:S(2)}) collective-permute-start(bf16[256,2560]{1,0:T(8,128)(2,1)S(1)} %get-tuple-element.6), channel_id=1, source_target_pairs={{0,2},{2,0},{1,3},{3,1},{4,6},{6,4},{5,7},{7,5},{8,10},{10,8},{9,1... | collective-permute-start | bytes 3932168 | tf_op jit(solution)/shard_map/ppermute | solution.py:138
  78.8 17.9 %collective-permute-start.4 = (bf16[128,2560]{1,0:T(8,128)(2,1)}, bf16[128,2560]{1,0:T(8,128)(2,1)S(1)}, u32[]{:S(2)}, u32[]{:S(2)}) collective-permute-start(bf16[128,2560]{1,0:T(8,128)(2,1)} %collective-permute-done.3), channel_id=1, source_target_pairs={{0,16},{16,0},{1,17},{17,1},{2,18},{18,2},{3,19},{19,3},{4,20},{20... | collective-permute-start | bytes 1966088 | tf_op jit(solution)/shard_map/ppermute | solution.py:167
  82.4 22.5 %collective-permute-start.6 = (bf16[128,2560]{1,0:T(8,128)(2,1)S(1)}, bf16[128,2560]{1,0:T(8,128)(2,1)S(1)}, u32[]{:S(2)}, u32[]{:S(2)}) collective-permute-start(bf16[128,2560]{1,0:T(8,128)(2,1)S(1)} %collective-permute-done.5), channel_id=1, source_target_pairs={{0,16},{16,0},{1,17},{17,1},{2,18},{18,2},{3,19},{19,3},{4,20},{20... | collective-permute-start | bytes 1966088 | tf_op jit(solution)/shard_map/ppermute | solution.py:167
  108.8 3.3 %copy-start.1 = (bf16[2,256,2560]{2,1,0:T(8,128)(2,1)S(1)}, bf16[2,256,2560]{2,1,0:T(8,128)(2,1)}, u32[]{:S(2)}) copy-start(bf16[2,256,2560]{2,1,0:T(8,128)(2,1)} %param.6) | copy-start | bytes 7864324
  108.8 15.7 %collective-permute-start.12 = (f32[1,256,512]{2,1,0:T(8,128)S(1)}, f32[1,256,512]{2,1,0:T(8,128)S(1)}, u32[]{:S(2)}, u32[]{:S(2)}) collective-permute-start(f32[1,256,512]{2,1,0:T(8,128)S(1)} %fusion.21), channel_id=1, source_target_pairs={{0,1},{1,0},{2,3},{3,2},{4,5},{5,4},{6,7},{7,6},{8,9},{9,8},{10,11... | collective-permute-start | bytes 1572872 | tf_op jit(solution)/shard_map/ppermute | solution.py:178
  111.6 12.8 %collective-permute-start.9 = (f32[1,256,512]{2,1,0:T(8,128)S(1)}, f32[1,256,512]{2,1,0:T(8,128)S(1)}, u32[]{:S(2)}, u32[]{:S(2)}) collective-permute-start(f32[1,256,512]{2,1,0:T(8,128)S(1)} %fusion.18), channel_id=1, source_target_pairs={{0,1},{1,0},{2,3},{3,2},{4,5},{5,4},{6,7},{7,6},{8,9},{9,8},{10,11... | collective-permute-start | bytes 1572872 | tf_op jit(solution)/shard_map/ppermute | solution.py:178
  115.3 9.1 %collective-permute-start.7 = (f32[2,256,512]{2,1,0:T(8,128)S(1)}, f32[2,256,512]{2,1,0:T(8,128)S(1)}, u32[]{:S(2)}, u32[]{:S(2)}) collective-permute-start(f32[2,256,512]{2,1,0:T(8,128)S(1)} %bitcast.39), channel_id=1, source_target_pairs={{0,1},{1,0},{2,3},{3,2},{4,5},{5,4},{6,7},{7,6},{8,9},{9,8},{10,11... | collective-permute-start | bytes 3145736 | tf_op jit(solution)/shard_map/ppermute | solution.py:178
  126.0 7.2 %collective-permute-start.13 = (f32[1,2,16,640]{3,2,1,0:T(8,128)S(1)}, f32[1,2,16,640]{3,2,1,0:T(8,128)S(1)}, u32[]{:S(2)}, u32[]{:S(2)}) collective-permute-start(f32[1,2,16,640]{3,2,1,0:T(8,128)S(1)} %get-tuple-element.15), channel_id=1, source_target_pairs={{0,4},{4,8},{8,12},{12,0},{1,5},{5,9},{9,13},{13,1},{2,6},{6,10},{... | collective-permute-start | bytes 245768 | tf_op jit(solution)/shard_map/ppermute | solution.py:210
  126.1 9.7 %collective-permute-start.14 = (f32[1,2,16,640]{3,2,1,0:T(8,128)S(1)}, f32[1,2,16,640]{3,2,1,0:T(8,128)S(1)}, u32[]{:S(2)}, u32[]{:S(2)}) collective-permute-start(f32[1,2,16,640]{3,2,1,0:T(8,128)S(1)} %get-tuple-element.14), channel_id=1, source_target_pairs={{0,8},{4,12},{8,0},{12,4},{1,9},{5,13},{9,1},{13,5},{2,10},{6,14},... | collective-permute-start | bytes 245768 | tf_op jit(solution)/shard_map/ppermute | solution.py:210
  127.9 7.9 %collective-permute-start.15 = (f32[1,2,16,640]{3,2,1,0:T(8,128)S(1)}, f32[1,2,16,640]{3,2,1,0:T(8,128)S(1)}, u32[]{:S(2)}, u32[]{:S(2)}) collective-permute-start(f32[1,2,16,640]{3,2,1,0:T(8,128)S(1)} %get-tuple-element.13), channel_id=1, source_target_pairs={{0,12},{4,0},{8,4},{12,8},{1,13},{5,1},{9,5},{13,9},{2,14},{6,2},{... | collective-permute-start | bytes 245768 | tf_op jit(solution)/shard_map/ppermute | solution.py:210
  136.1 1.9 %collective-permute-start.16 = (bf16[1,16,512]{2,1,0:T(8,128)(2,1)S(1)}, bf16[1,16,512]{2,1,0:T(8,128)(2,1)S(1)}, u32[]{:S(2)}, u32[]{:S(2)}) collective-permute-start(bf16[1,16,512]{2,1,0:T(8,128)(2,1)S(1)} %get-tuple-element.25), channel_id=1, source_target_pairs={{0,1},{1,0},{2,3},{3,2},{4,5},{5,4},{6,7},{7,6},{8,9},{9,8},{10,11... | collective-permute-start | bytes 49160 | tf_op jit(solution)/shard_map/ppermute | solution.py:224
  136.2 3.8 %collective-permute-start.17 = (bf16[1,16,512]{2,1,0:T(8,128)(2,1)S(1)}, bf16[1,16,512]{2,1,0:T(8,128)(2,1)S(1)}, u32[]{:S(2)}, u32[]{:S(2)}) collective-permute-start(bf16[1,16,512]{2,1,0:T(8,128)(2,1)S(1)} %get-tuple-element.26), channel_id=1, source_target_pairs={{0,2},{2,0},{1,3},{3,1},{4,6},{6,4},{5,7},{7,5},{8,10},{10,8},{9,1... | collective-permute-start | bytes 49160 | tf_op jit(solution)/shard_map/ppermute | solution.py:225
  137.2 3.2 %collective-permute-start.18 = (bf16[1,16,512]{2,1,0:T(8,128)(2,1)S(1)}, bf16[1,16,512]{2,1,0:T(8,128)(2,1)S(1)}, u32[]{:S(2)}, u32[]{:S(2)}) collective-permute-start(bf16[1,16,512]{2,1,0:T(8,128)(2,1)S(1)} %get-tuple-element.26), channel_id=1, source_target_pairs={{0,3},{3,0},{1,2},{2,1},{4,7},{7,4},{5,6},{6,5},{8,11},{11,8},{9,1... | collective-permute-start | bytes 49160 | tf_op jit(solution)/shard_map/ppermute | solution.py:226
  140.4 0.6 copy-start.3

commit v2 on v1

v2 whole, which is shorter than its diff:
```python
import functools

import jax
import jax.numpy as jnp
from jax import lax
from jax.experimental import pallas as pl
from jax.experimental.pallas import tpu as pltpu
from jax.sharding import Mesh, PartitionSpec as P

HEAD_DIM = 64
EMPTY = -3e38
VMEM_LIMIT = 40 * 1024 * 1024
SWAP = [(0, 1), (1, 0)]
CROSS = [(0, 3), (3, 0), (1, 2), (2, 1)]


def head_pick(tall, query_len):
    lanes = tall.shape[1]
    lane_head = lax.broadcasted_iota(jnp.int32, (query_len, lanes), 1) // HEAD_DIM
    picked = jnp.zeros((query_len, lanes), jnp.float32)
    for head in range(lanes // HEAD_DIM):
        picked = jnp.where(lane_head == head, tall[head * query_len : (head + 1) * query_len, :], picked)
    return picked


def project_kernel(flag_ref, *refs, jobs, sends):
    keep_ref, *send_refs = refs[-1 - len(sends) :]
    slots = [(ref, at) for ref in send_refs for at in range(ref.shape[0])]
    core, same = flag_ref[0], flag_ref[1]
    half = keep_ref.shape[2]
    for at, (rows_of, blocks_of) in enumerate(jobs):
        if len(blocks_of) == 1:
            whole = refs[blocks_of[0]]
            keep = whole[pl.ds(pl.multiple_of(core * half, half), half), :]
            send = whole[pl.ds(pl.multiple_of((1 - core) * half, half), half), :]
        else:
            first, second = (refs[block][...] for block in blocks_of)
            keep = jnp.where(same == 1, first, second)
            send = jnp.where(same == 1, second, first)
        product = lax.dot_general(
            refs[rows_of][...],
            jnp.concatenate([keep, send], axis=0),
            (((1,), (1,)), ((), ())),
            preferred_element_type=jnp.float32,
        )
        keep_ref[at] = product[:, :half]
        send_ref, slot = slots[at]
        send_ref[slot] = product[:, half:]


def attend_kernel(place_ref, spot_ref, query_ref, *refs, pieces):
    *refs, own_ref, partner_ref, out_ref, key_ref = refs
    residuals = own_ref, partner_ref
    partner_queries = own_ref.shape[0]
    query_len, held = query_ref.shape[1:]
    block_len = key_ref.shape[1]
    heads = held // HEAD_DIM
    tall = heads * query_len
    out_ref[:, :, :held] = jnp.zeros(out_ref.shape[:2] + (held,), jnp.float32)
    ext_row = lax.broadcasted_iota(jnp.int32, out_ref.shape[:2] + (tall,), 1)
    out_ref[:, :, held:] = jnp.where(ext_row == 0, EMPTY, 0.0)
    row_head = lax.broadcasted_iota(jnp.int32, (tall, held), 0) // query_len
    lane_head = lax.broadcasted_iota(jnp.int32, (tall, held), 1) // HEAD_DIM
    diagonal = row_head == lane_head
    square = lax.broadcasted_iota(jnp.int32, (tall, tall), 0) == lax.broadcasted_iota(jnp.int32, (tall, tall), 1)
    ext = lax.broadcasted_iota(jnp.int32, (query_len, tall), 0)
    blocks = key_ref.shape[0] // 2
    for source, kept, sent, spot in pieces:
        keep, other = (refs[summand].at[piece] for summand, piece in (kept, sent))
        residual = residuals[source]
        span = keep.shape[1]
        lanes = pl.ds(pl.multiple_of(spot_ref[spot] * span, span), span)
        for block in range(blocks):
            rows = slice(block * block_len, (block + 1) * block_len)
            key_ref[source * blocks + block, :, lanes] = (
                residual[rows, lanes].astype(jnp.float32) + (keep[rows, :] + other[rows, :])
            ).astype(jnp.bfloat16)
    places, scores, tops = [], [], []
    for at in range(key_ref.shape[0]):
        place = place_ref[at]
        first = pl.multiple_of(partner_queries + place // 2 * query_len, query_len)
        query = jnp.where(place % 2 == 0, query_ref[place // 2], partner_ref[pl.ds(first, query_len), :])
        query = jnp.concatenate([query] * heads, axis=0)
        query = jnp.where(diagonal, query, jnp.zeros_like(query))
        score = lax.dot_general(
            query, key_ref[at], (((1,), (1,)), ((), ())), preferred_element_type=jnp.float32
        )
        places.append(place)
        scores.append(score)
        tops.append(jnp.max(score, axis=1, keepdims=True))
    for at, place in enumerate(places):
        top = tops[at]
        for other_at, other_place in enumerate(places):
            if other_at != at:
                top = jnp.maximum(top, jnp.where(other_place == place, tops[other_at], EMPTY))
        weights = jnp.exp(scores[at] - top)
        total = jnp.sum(weights, axis=1, keepdims=True)
        blend = lax.dot_general(
            weights.astype(jnp.bfloat16), key_ref[at], (((1,), (0,)), ((), ())),
            preferred_element_type=jnp.float32,
        )
        top_row = jnp.sum(jnp.where(square, top, 0.0), axis=0, keepdims=True)
        total_row = jnp.sum(jnp.where(square, total, 0.0), axis=0, keepdims=True)
        out_ref[place, :, :held] = out_ref[place, :, :held] + head_pick(blend, query_len)
        before = out_ref[place, :, held:]
        out_ref[place, :, held:] = jnp.where(
            ext == 0, top_row, jnp.where(ext == 1, before + total_row, 0.0)
        )


def merge_kernel(*refs):
    out_ref = refs[-1]
    parts = refs[:-1]
    query_len, held = out_ref.shape[1:]
    tall = held // HEAD_DIM * query_len
    square = lax.broadcasted_iota(jnp.int32, (tall, tall), 0) == lax.broadcasted_iota(jnp.int32, (tall, tall), 1)

    def over(start, step):
        for part in parts:
            start = lax.fori_loop(
                0, part.shape[0], functools.partial(step, part), start, unroll=part.shape[0] <= 8
            )
        return start

    for slot in range(out_ref.shape[0]):
        def top_step(part, at, top):
            return jnp.maximum(top, part[at, slot, 0:1, held:])

        def total_step(part, at, total):
            return total + jnp.exp(part[at, slot, 0:1, held:] - top) * part[at, slot, 1:2, held:]

        def blend_step(part, at, blend):
            share = jnp.exp(part[at, slot, 0:1, held:] - top) / total
            column = jnp.sum(jnp.where(square, share, 0.0), axis=1, keepdims=True)
            spread = head_pick(jnp.broadcast_to(column, (tall, held)), query_len)
            return blend + spread * part[at, slot, :, :held]

        top = over(jnp.full((1, tall), EMPTY, jnp.float32), top_step)
        total = over(jnp.zeros((1, tall), jnp.float32), total_step)
        blend = over(jnp.zeros((query_len, held), jnp.float32), blend_step)
        out_ref[slot] = blend.astype(out_ref.dtype)


def in_vmem(count):
    return [pl.BlockSpec(memory_space=pltpu.VMEM)] * count


def in_smem(count):
    return [pl.BlockSpec(memory_space=pltpu.SMEM)] * count


def project(flags, operands, jobs, sends, name):
    rows, units = operands[0].shape
    half = min(operand.shape[0] for operand in operands)
    shapes = [jax.ShapeDtypeStruct((count, rows, half), jnp.float32) for count in [len(jobs)] + sends]
    return pl.pallas_call(
        functools.partial(project_kernel, jobs=jobs, sends=sends),
        out_shape=shapes,
        in_specs=in_smem(1) + in_vmem(len(operands)),
        out_specs=in_vmem(len(shapes)),
        compiler_params=pltpu.CompilerParams(vmem_limit_bytes=VMEM_LIMIT),
        cost_estimate=pl.CostEstimate(flops=1, bytes_accessed=1, transcendentals=0),
        name=name,
    )(flags, *operands)


def body(hidden_states, passage_states, down_weight, block_question, question_owner, decoder_states):
    blocks, block_len, units = hidden_states.shape
    width = passage_states.shape[2]
    query_len = decoder_states.shape[1]
    highs, lows, cores = lax.axis_size("high"), lax.axis_size("low"), lax.axis_size("mp")
    group, high, side, low, core = (lax.axis_index(name) for name in ("groups", "high", "side", "low", "mp"))
    shard = down_weight.shape[0]
    stride = lows * shard
    held = width // 2 // cores
    heads = held // HEAD_DIM
    members = highs * lows
    slot_total = question_owner.shape[0]
    rows = blocks * block_len
    lined = highs == 4 and lows == 1 and stride % (cores * 128) == 0
    span = stride // cores if lined else stride
    spans = held // span

    def features(array, of_side):
        if lined:
            starts = [(at * 2 + of_side) * stride + core * span for at in range(spans)]
        else:
            starts = [((core * spans + at) * 2 + of_side) * stride for at in range(spans)]
        taken = [lax.dynamic_slice_in_dim(array, start, span, axis=array.ndim - 1) for start in starts]
        return jnp.concatenate(taken, axis=-1)

    def shifted(array, shift):
        return lax.ppermute(array, "high", [(at, (at + shift) % highs) for at in range(highs)])

    hidden = hidden_states.reshape(rows, units)
    partner_hidden = lax.ppermute(hidden, "side", SWAP)
    queries = jnp.concatenate([features(decoder_states, side), features(decoder_states, 1 - side)], axis=0)[None]
    passages = passage_states.reshape(rows, width)
    own_residual = features(passages, side)
    leaving = features(passages, 1 - side)

    if lined:
        half = shard // 2
        sent = lax.dynamic_slice_in_dim(down_weight, group * half, half, axis=0)
        below = shifted(sent, 1)
        above = shifted(sent, -1)
        opposite = shifted(below, 1)
        queries, _ = lax.optimization_barrier((queries, opposite))
        queries = jnp.concatenate([queries] + [shifted(queries, -ahead) for ahead in range(1, highs)], axis=0)
        weights = [down_weight]
        for piece in (above, below, opposite):
            weights += [piece, lax.ppermute(piece, "groups", SWAP)]
        flags = jnp.stack([core, (group == core).astype(core.dtype)])
        blocks_of = [(0,), (1, 2), (3, 4), (5, 6)]
        spots = lax.rem(high + jnp.array([0, 1, 3, 2], jnp.int32), highs)

        def jobs_of(rows_of, chosen, count):
            return [(rows_of, tuple(at + count for at in blocks_of[one])) for one in chosen]

        kept, *away = project(flags, [hidden] + weights[:5], jobs_of(0, (0, 1, 2), 1), [3], "project_own")
        flags, kept, away = lax.optimization_barrier((flags, kept, away))
        late_kept, *late_away = project(
            flags,
            [hidden, partner_hidden] + weights,
            jobs_of(0, (3,), 2) + jobs_of(1, range(4), 2),
            [2, 2, 1],
            "project_rest",
        )
        others = [lax.ppermute(piece, "mp", SWAP) for piece in away + late_away]
        summands = [kept, late_kept] + others
        pieces = [(0, (0, at), (2, at), at) for at in range(3)] + [(0, (1, 0), (3, 0), 3)]
        pieces += [(1, (1, 1 + at), (3 + (1 + at) // 2, (1 + at) % 2), at) for at in range(4)]
        origin = high
    else:
        queries = lax.all_gather(queries, ("high", "low"), axis=0, tiled=True)
        weight = lax.all_gather(down_weight, ("high", "low"), axis=0, tiled=True)
        weight = jnp.where(core == 0, weight, jnp.roll(weight, held, axis=0))
        spots = jnp.zeros((1,), jnp.int32)
        summands, pieces = [], []
        for source, flat in enumerate((hidden, partner_hidden)):
            kept, away = (
                lax.dot_general(flat, part, (((1,), (1,)), ((), ())), preferred_element_type=jnp.float32)[None]
                for part in (weight[:held], weight[held:])
            )
            summands += [kept, lax.ppermute(away, "mp", SWAP)]
            pieces.append((source, (2 * source, 0), (2 * source + 1, 0), 0))
        origin = 0

    questions = block_question[:, 0]
    question_ids = jnp.arange(slot_total, dtype=jnp.int32)
    owners = jnp.sum(jnp.where(questions[:, None] == question_ids[None, :], question_owner[None, :], 0), axis=1)
    owner_high, owner_side, owner_low = owners // (2 * lows), (owners // lows) % 2, owners % lows
    owner_high = lax.rem(owner_high - origin + highs, highs)
    owner_place = (owner_high * lows + owner_low) * 2 + (owner_side != side)
    own_at = ((high * 2 + side) * lows + low) * blocks
    partner_at = ((high * 2 + 1 - side) * lows + low) * blocks
    places = jnp.concatenate(
        [lax.dynamic_slice_in_dim(owner_place, at, blocks) for at in (own_at, partner_at)]
    )

    leaving = jnp.concatenate([leaving, queries[:, 1].reshape(-1, held)], axis=0)
    partner = lax.ppermute(leaving, "side", SWAP)
    operands = summands + [own_residual, partner]
    partials = pl.pallas_call(
        functools.partial(attend_kernel, pieces=pieces),
        out_shape=jax.ShapeDtypeStruct((2 * members, query_len, held + heads * query_len), jnp.float32),
        in_specs=in_smem(2) + in_vmem(1 + len(operands)),
        out_specs=pl.BlockSpec(memory_space=pltpu.VMEM),
        scratch_shapes=[pltpu.VMEM((2 * blocks, block_len, held), jnp.bfloat16)],
        compiler_params=pltpu.CompilerParams(vmem_limit_bytes=VMEM_LIMIT),
        name="attend",
    )(places, spots, queries[:, 0], *operands)
    partials = partials.reshape((members, 2) + partials.shape[1:])

    if lined:
        received = [partials[0:1]] + [shifted(partials[ahead : ahead + 1], ahead) for ahead in range(1, highs)]
    else:
        received = [lax.all_to_all(partials, ("high", "low"), split_axis=0, concat_axis=0, tiled=True)]
    merged = pl.pallas_call(
        merge_kernel,
        out_shape=jax.ShapeDtypeStruct((2, query_len, held), decoder_states.dtype),
        in_specs=in_vmem(len(received)),
        out_specs=pl.BlockSpec(memory_space=pltpu.VMEM),
        compiler_params=pltpu.CompilerParams(vmem_limit_bytes=VMEM_LIMIT),
        name="merge",
    )(*received)

    mine, away = merged[0:1], merged[1:2]
    by_core = lax.ppermute(mine, "mp", SWAP)
    by_side = lax.ppermute(away, "side", SWAP)
    by_both = lax.ppermute(away, ("side", "mp"), CROSS)
    near = [jnp.where(core == at, mine, by_core) for at in range(cores)]
    far = [jnp.where(core == at, by_side, by_both) for at in range(cores)]
    sides = [[jnp.where(side == at, near[of], far[of]) for of in range(cores)] for at in range(2)]
    columns = []
    if lined:
        order = [(at, of_side, of) for at in range(spans) for of_side in range(2) for of in range(cores)]
    else:
        order = [(at, of_side, of) for of in range(cores) for at in range(spans) for of_side in range(2)]
    for at, of_side, of in order:
        columns.append(sides[of_side][of][:, :, at * span : (at + 1) * span])
    return jnp.concatenate(columns, axis=-1)


def solution(mesh):
    groups, dp, cores = mesh.shape["groups"], mesh.shape["dp"], mesh.shape["mp"]

    def run(hidden_states, passage_states, down_weight, block_question, question_owner, decoder_states):
        lows = max(1, HEAD_DIM * dp // down_weight.shape[0])
        fine = Mesh(
            mesh.devices.reshape(groups, dp // (2 * lows), 2, lows, cores),
            ("groups", "high", "side", "low", "mp"),
        )
        split = ("groups", "high", "side", "low")
        placed = (
            P(split, None, "mp"),
            P(split, None, None),
            P(("high", "side", "low"), "mp"),
            P("groups", None),
            P("groups"),
            P(split, None, None),
        )
        return jax.shard_map(
            body, mesh=fine, in_specs=placed, out_specs=P(split, None, None), check_vma=False
        )(hidden_states, passage_states, down_weight, block_question, question_owner, decoder_states)

    return run
```

time: 142 us -> 111 us (0.78)
  blocking collectives: 25.6 us -> 0 us
  matrix products: 17.9 us -> 0 us
  Pallas kernels: 1.71 us -> 13.9 us
  local copies, waits for them, and re-layouts: 19 us -> 7.7 us
  starting transfers between devices: 20.5 us -> 27.7 us
  waiting for transfers between devices: 53.9 us -> 59.7 us
    all_gather x1 -> x0, blocking collectives: 25.6 us -> none  [body(): queries = lax.all_gather(queries, ('high', 'low'), axis=0, tiled=True)]
    dot_general x6 -> x0, matrix products: 17.9 us -> none  [part(): lax.dot_general(flat, rows_of, (((1,), (1,)), ((), ())), preferred_elemen...]
    pallas_call x1 -> x3, Pallas kernels: 1.47 us -> 13.7 us  [the longest x2 11 us: project(): pl.pallas_call(functools.partial(project_kernel, jobs=jobs, sends=sends),...]
    dynamic_update_slice x7 -> x0, local copies, waits for them, and re-layouts: 8.67 us -> none  [placed(): lax.dynamic_update_slice_in_dim(weight, piece, at * shard + of_half * hal...]
    ppermute x16 -> x18, starting transfers between devices: 18.6 us -> 25.8 us  [the longest x9 17 us: shifted(): lax.ppermute(array, 'high', [(at, (at + shift) % highs) for at in range(h...]
    ppermute x16 -> x18, waiting for transfers between devices: 51.6 us -> 57.6 us  [the longest x9 41.1 us: shifted(): lax.ppermute(array, 'high', [(at, (at + shift) % highs) for at in range(h...]
    unnamed x12 -> x40, local copies, waits for them, and re-layouts: 0.65 us -> 4.3 us
    broadcast_in_dim x1 -> x0, local copies, waits for them, and re-layouts: 2.66 us -> none  [body(): weight = jnp.zeros((highs * shard, units), down_weight.dtype)]
  transfers between devices with their start and end apart: 19 -> 21, of which waited for: 8 -> 8; matrix products, arithmetic and copies ran while one was open for 26% -> 4% of each run, Pallas kernels for 0% -> 10%
where the time goes in v2:
time: 111 us
  waiting for transfers between devices  59.7 us (54%)
  starting transfers between devices  27.7 us (25%)
  Pallas kernels  13.9 us (13%)
  local copies, waits for them, and re-layouts  7.7 us (7%)
  other arithmetic  1.98 us (2%)
    ppermute x9, waiting for transfers between devices, shifted(): lax.ppermute(array, 'high', [(at, (at + shift) % highs) for at in range(h...  41.1 us
    ppermute x9, starting transfers between devices, shifted(): lax.ppermute(array, 'high', [(at, (at + shift) % highs) for at in range(h...  17 us
    ppermute x3, waiting for transfers between devices, body(): weights += [piece, lax.ppermute(piece, 'groups', SWAP)]  14.3 us
    pallas_call x2, Pallas kernels, project(): pl.pallas_call(functools.partial(project_kernel, jobs=jobs, sends=sends),...  11 us
    ppermute x3, starting transfers between devices, body(): weights += [piece, lax.ppermute(piece, 'groups', SWAP)]  4.62 us
    unnamed x40, local copies, waits for them, and re-layouts  4.3 us
    ppermute x1, starting transfers between devices, body(): partner_hidden = lax.ppermute(hidden, 'side', SWAP)  2.94 us
    pallas_call x1, Pallas kernels, body(): pl.pallas_call(functools.partial(attend_kernel, pieces=pieces), out_shape...  2.7 us
  transfers between devices with their start and end apart: 21, of which 8 were waited for; matrix products, arithmetic and copies ran while one was open for 4% of the time, Pallas kernels for 10%

profile of v2, /device:TPU:0, one launch (start us, length us, event | category | flops | bytes accessed | tf_op | source)
XLA Modules:
  0.0 111.2 jit_solution(6775836864270974048)
XLA Ops:
  0.0 2.9 %collective-permute-start.8 = (bf16[512,2560]{1,0:T(8,128)(2,1)}, bf16[512,2560]{1,0:T(8,128)(2,1)}, u32[]{:S(2)}, u32[]{:S(2)}) collective-permute-start(bf16[512,2560]{1,0:T(8,128)(2,1)} %bitcast.18), channel_id=1, source_target_pairs={{0,2},{2,0},{1,3},{3,1},{4,6},{6,4},{5,7},{7,5},{8,10},{10,8},{9,1... | collective-permute-start | bytes 7864328 | tf_op jit(solution)/shard_map/ppermute | solution.py:196
  2.9 1.1 %constant_dynamic-slice_fusion.8 = bf16[128,2560]{1,0:T(8,128)(2,1)S(1)} fusion(bf16[256,2560]{1,0:T(8,128)(2,1)} %refs_2_.1, s32[]{:T(128)S(6)} %select_n.117), kind=kLoop, calls=%fused_computation.44 | loop fusion | bytes 1310724 | tf_op jit(solution)/shard_map/dynamic_slice | solution.py:204
  4.1 1.6 %collective-permute-start = (bf16[128,2560]{1,0:T(8,128)(2,1)S(1)}, bf16[128,2560]{1,0:T(8,128)(2,1)S(1)}, u32[]{:S(2)}, u32[]{:S(2)}) collective-permute-start(bf16[128,2560]{1,0:T(8,128)(2,1)S(1)} %constant_dynamic-slice_fusion.8), channel_id=1, source_target_pairs={{0,4},{4,8},{8,12},{12,0},{1,5},{5,9},{9,13},{13,1},{2,6},{6,10},{... | collective-permute-start | bytes 1966088 | tf_op jit(solution)/shard_map/ppermute | solution.py:193
  5.7 2.2 %collective-permute-start.5 = (bf16[128,2560]{1,0:T(8,128)(2,1)S(1)}, bf16[128,2560]{1,0:T(8,128)(2,1)}, u32[]{:S(2)}, u32[]{:S(2)}) collective-permute-start(bf16[128,2560]{1,0:T(8,128)(2,1)S(1)} %constant_dynamic-slice_fusion.8), channel_id=1, source_target_pairs={{0,12},{4,0},{8,4},{12,8},{1,13},{5,1},{9,5},{13,9},{2,14},{6,2},{... | collective-permute-start | bytes 1966088 | tf_op jit(solution)/shard_map/ppermute | solution.py:193
  8.0 15.7 %collective-permute-done.refs_4_.refs_5_ = bf16[128,2560]{1,0:T(8,128)(2,1)S(1)} collective-permute-done((bf16[128,2560]{1,0:T(8,128)(2,1)S(1)}, bf16[128,2560]{1,0:T(8,128)(2,1)S(1)}, u32[]{:S(2)}, u32[]{:S(2)}) %collective-permute-start) | collective-permute-done | bytes 655392 | tf_op jit(solution)/shard_map/ppermute | solution.py:193
  23.6 1.5 %collective-permute-start.7 = (bf16[128,2560]{1,0:T(8,128)(2,1)S(1)}, bf16[128,2560]{1,0:T(8,128)(2,1)}, u32[]{:S(2)}, u32[]{:S(2)}) collective-permute-start(bf16[128,2560]{1,0:T(8,128)(2,1)S(1)} %collective-permute-done.refs_4_.refs_5_), channel_id=1, source_target_pairs={{0,16},{16,0},{1,17},{17,1},{2,18},{18,2},{3,19},{19,3},{4,20},{20... | collective-permute-start | bytes 1966088 | tf_op jit(solution)/shard_map/ppermute | solution.py:212
  25.1 11.4 %collective-permute-done.5.refs_2_.refs_3_ = bf16[128,2560]{1,0:T(8,128)(2,1)} collective-permute-done((bf16[128,2560]{1,0:T(8,128)(2,1)S(1)}, bf16[128,2560]{1,0:T(8,128)(2,1)}, u32[]{:S(2)}, u32[]{:S(2)}) %collective-permute-start.5) | collective-permute-done | bytes 655392 | tf_op jit(solution)/shard_map/ppermute | solution.py:193
  36.6 1.5 %collective-permute-start.6 = (bf16[128,2560]{1,0:T(8,128)(2,1)}, bf16[128,2560]{1,0:T(8,128)(2,1)}, u32[]{:S(2)}, u32[]{:S(2)}) collective-permute-start(bf16[128,2560]{1,0:T(8,128)(2,1)} %collective-permute-done.5.refs_2_.refs_3_), channel_id=1, source_target_pairs={{0,16},{16,0},{1,17},{17,1},{2,18},{18,2},{3,19},{19,3},{4,20},{20... | collective-permute-start | bytes 1966088 | tf_op jit(solution)/shard_map/ppermute | solution.py:212
  38.2 1.5 %constant_dynamic-slice_fusion.3 = (bf16[512,128]{1,0:T(8,128)(2,1)S(1)}, bf16[512,128]{1,0:T(8,128)(2,1)S(1)}, bf16[512,128]{1,0:T(8,128)(2,1)S(1)}, bf16[512,1...) fusion(bf16[512,2048]{1,0:T(8,128)(2,1)} %bitcast.21, ...), kind=kLoop, calls=%fused_computation.39 | loop fusion | bytes 2097184 | tf_op jit(solution)/shard_map/dynamic_slice | solution.py:189
  39.8 0.8 pad_maximum_fusion.1.refs_6_
  40.6 9.8 %collective-permute-done.1.refs_7_ = bf16[128,2560]{1,0:T(8,128)(2,1)} collective-permute-done((bf16[128,2560]{1,0:T(8,128)(2,1)S(1)}, bf16[128,2560]{1,0:T(8,128)(2,1)}, u32[]{:S(2)}, u32[]{:S(2)}) %collective-permute-start.1) | collective-permute-done | bytes 655392 | tf_op jit(solution)/shard_map/ppermute | solution.py:193
  50.4 1.7 %collective-permute-start.2 = (bf16[1,2,16,512]{3,2,0,1:T(8,128)(2,1)S(1)}, bf16[1,2,16,512]{3,2,0,1:T(8,128)(2,1)S(1)}, u32[]{:S(2)}, u32[]{:S(2)}) collective-permute-start(bf16[1,2,16,512]{3,2,0,1:T(8,128)(2,1)S(1)} %maximum_bitcast_fusion), channel_id=1, source_target_pairs={{0,12},{4,0},{8,4},{12,8},{1,13},{5,1},{9,5},{13,9},{2,14},{6,2},{... | collective-permute-start | bytes 98312 | tf_op jit(solution)/shard_map/ppermute | solution.py:193
  52.1 1.0 collective-permute-start.4
  53.1 1.3 %copy-done.1 = bf16[256,2560]{1,0:T(8,128)(2,1)S(1)} copy-done((bf16[256,2560]{1,0:T(8,128)(2,1)S(1)}, bf16[256,2560]{1,0:T(8,128)(2,1)}, u32[]{:S(2)}) %copy-start.1) | copy-done | bytes 1310744
  54.5 4.6 %project_own.1 = (f32[3,512,128]{2,1,0:T(8,128)S(1)}, f32[3,512,128]{2,1,0:T(8,128)}) custom-call(s32[2]{0:T(128)S(1)} %pad_add_fusion.1.flag_ref, bf16[512,2560]{1,0:T(8,128)(2,1)S(1)} %bitcast.19, bf16[256,2560]{1,0:T(8,128)(2,1)S(1)} %copy-done.1, bf16[128,2560]{1,0:T(8,128)(2,1)} %collective-permute-done.5.refs_2_.refs_3_, ...), custom_call_target="tpu_custom_call" | custom-call | flops 1 | bytes 1 | tf_op jit(solution)/shard_map/project_own/pallas_call | solution.py:156
  59.1 0.9 copy-done.4
  60.0 1.6 %collective-permute-start.9 = (bf16[128,2560]{1,0:T(8,128)(2,1)}, bf16[128,2560]{1,0:T(8,128)(2,1)}, u32[]{:S(2)}, u32[]{:S(2)}) collective-permute-start(bf16[128,2560]{1,0:T(8,128)(2,1)} %collective-permute-done.1.refs_7_), channel_id=1, source_target_pairs={{0,16},{16,0},{1,17},{17,1},{2,18},{18,2},{3,19},{19,3},{4,20},{20... | collective-permute-start | bytes 1966088 | tf_op jit(solution)/shard_map/ppermute | solution.py:212
  61.6 0.9 pad_maximum_fusion
  62.5 0.5 collective-permute-start.14
  63.1 14.3 %collective-permute-done.9.refs_8_ = bf16[128,2560]{1,0:T(8,128)(2,1)} collective-permute-done((bf16[128,2560]{1,0:T(8,128)(2,1)}, bf16[128,2560]{1,0:T(8,128)(2,1)}, u32[]{:S(2)}, u32[]{:S(2)}) %collective-permute-start.9) | collective-permute-done | bytes 655392 | tf_op jit(solution)/shard_map/ppermute | solution.py:212
  77.5 1.3 %copy-done.2 = bf16[256,2560]{1,0:T(8,128)(2,1)S(1)} copy-done((bf16[256,2560]{1,0:T(8,128)(2,1)S(1)}, bf16[256,2560]{1,0:T(8,128)(2,1)}, u32[]{:S(2)}) %copy-start.2) | copy-done | bytes 1310744
  78.8 6.4 %project_rest.1 = (f32[5,512,128]{2,1,0:T(8,128)S(1)}, f32[2,512,128]{2,1,0:T(8,128)S(1)}, f32[2,512,128]{2,1,0:T(8,128)S(1)}, f32[1,512,128]{2,1,0:T(8,128)S(1)}) custom-call(s32[2]{0:T(128)S(1)} %pad_add_fusion.1.flag_ref, bf16[512,2560]{1,0:T(8,128)(2,1)S(1)} %bitcast.20, bf16[512,2560]{1,0:T(8,128)(2,1)} %collective-permute-done.8.refs_1_, ...), custom_call_target="tpu_custom_call" | custom-call | flops 1 | bytes 1 | tf_op jit(solution)/shard_map/project_rest/pallas_call | solution.py:156
  86.0 2.2 %collective-permute-done.13.refs_5_ = f32[1,512,128]{2,1,0:T(8,128)S(1)} collective-permute-done((f32[1,512,128]{2,1,0:T(8,128)S(1)}, f32[1,512,128]{2,1,0:T(8,128)S(1)}, u32[]{:S(2)}, u32[]{:S(2)}) %collective-permute-start.13) | collective-permute-done | bytes 262176 | tf_op jit(solution)/shard_map/ppermute | solution.py:229
  88.3 2.7 %attend.1 = f32[8,16,640]{2,1,0:T(8,128)S(1)} custom-call(s32[4]{0:T(128)S(1)} %get-tuple-element.56.place_ref, s32[4]{0:T(128)S(1)} %get-tuple-element.55.spot_ref, bf16[4,16,512]{2,1,0:T(8,128)(2,1)S(1)} %get-tuple-element.38.query_ref, f32[3,512,128]{2,1,0:T(8,128)S(1)} %copy-done.5, f32[5,512,128]{2,1,0:T(8,128)S(1)} %get-tuple-element.20.refs_1_, ...), custom_call_target="tpu_custom_call" | custom-call | tf_op jit(solution)/shard_map/attend/pallas_call | solution.py:264
  91.0 7.8 %collective-permute-start.15 = (f32[1,2,16,640]{3,2,1,0:T(8,128)S(1)}, f32[1,2,16,640]{3,2,1,0:T(8,128)S(1)}, u32[]{:S(2)}, u32[]{:S(2)}) collective-permute-start(f32[1,2,16,640]{3,2,1,0:T(8,128)S(1)} %get-tuple-element.35), channel_id=1, source_target_pairs={{0,4},{4,8},{8,12},{12,0},{1,5},{5,9},{9,13},{13,1},{2,6},{6,10},{... | collective-permute-start | bytes 245768 | tf_op jit(solution)/shard_map/ppermute | solution.py:193
  99.0 2.4 %collective-permute-start.17 = (f32[1,2,16,640]{3,2,1,0:T(8,128)S(1)}, f32[1,2,16,640]{3,2,1,0:T(8,128)S(1)}, u32[]{:S(2)}, u32[]{:S(2)}) collective-permute-start(f32[1,2,16,640]{3,2,1,0:T(8,128)S(1)} %get-tuple-element.33), channel_id=1, source_target_pairs={{0,12},{4,0},{8,4},{12,8},{1,13},{5,1},{9,5},{13,9},{2,14},{6,2},{... | collective-permute-start | bytes 245768 | tf_op jit(solution)/shard_map/ppermute | solution.py:193
  101.6 4.0 %collective-permute-done.16.refs_2_ = f32[1,2,16,640]{3,2,1,0:T(8,128)S(1)} collective-permute-done((f32[1,2,16,640]{3,2,1,0:T(8,128)S(1)}, f32[1,2,16,640]{3,2,1,0:T(8,128)S(1)}, u32[]{:S(2)}, u32[]{:S(2)}) %collective-permute-start.16) | collective-permute-done | bytes 81952 | tf_op jit(solution)/shard_map/ppermute | solution.py:193
  105.9 0.6 collective-permute-start.19
  106.4 1.3 %collective-permute-start.20 = (bf16[1,16,512]{2,1,0:T(8,128)(2,1)S(1)}, bf16[1,16,512]{2,1,0:T(8,128)(2,1)S(1)}, u32[]{:S(2)}, u32[]{:S(2)}) collective-permute-start(bf16[1,16,512]{2,1,0:T(8,128)(2,1)S(1)} %get-tuple-element.51), channel_id=1, source_target_pairs={{0,3},{3,0},{1,2},{2,1},{4,7},{7,4},{5,6},{6,5},{8,11},{11,8},{9,1... | collective-permute-start | bytes 49160 | tf_op jit(solution)/shard_map/ppermute | solution.py:291
  107.7 2.0 %collective-permute-done.19 = bf16[1,16,512]{2,1,0:T(8,128)(2,1)S(1)} collective-permute-done((bf16[1,16,512]{2,1,0:T(8,128)(2,1)S(1)}, bf16[1,16,512]{2,1,0:T(8,128)(2,1)S(1)}, u32[]{:S(2)}, u32[]{:S(2)}) %collective-permute-start.19) | collective-permute-done | bytes 16416 | tf_op jit(solution)/shard_map/ppermute | solution.py:290
  110.0 0.6 copy-done.8
  110.6 0.6 constant_dynamic-update-slice_fusion.4
  (71 shorter events, 2.1 us)
Async XLA Ops:
  0.0 38.2 %copy-start.6 = (bf16[1,16,2048]{2,1,0:T(8,128)(2,1)S(1)}, bf16[1,16,2048]{2,1,0:T(8,128)(2,1)}, u32[]{:S(2)}) copy-start(bf16[1,16,2048]{2,1,0:T(8,128)(2,1)} %param.12) | copy-start | bytes 196612
  0.0 77.5 %collective-permute-start.8 = (bf16[512,2560]{1,0:T(8,128)(2,1)}, bf16[512,2560]{1,0:T(8,128)(2,1)}, u32[]{:S(2)}, u32[]{:S(2)}) collective-permute-start(bf16[512,2560]{1,0:T(8,128)(2,1)} %bitcast.18), channel_id=1, source_target_pairs={{0,2},{2,0},{1,3},{3,1},{4,6},{6,4},{5,7},{7,5},{8,10},{10,8},{9,1... | collective-permute-start | bytes 7864328 | tf_op jit(solution)/shard_map/ppermute | solution.py:196
  4.1 19.6 %collective-permute-start = (bf16[128,2560]{1,0:T(8,128)(2,1)S(1)}, bf16[128,2560]{1,0:T(8,128)(2,1)S(1)}, u32[]{:S(2)}, u32[]{:S(2)}) collective-permute-start(bf16[128,2560]{1,0:T(8,128)(2,1)S(1)} %constant_dynamic-slice_fusion.8), channel_id=1, source_target_pairs={{0,4},{4,8},{8,12},{12,0},{1,5},{5,9},{9,13},{13,1},{2,6},{6,10},{... | collective-permute-start | bytes 1966088 | tf_op jit(solution)/shard_map/ppermute | solution.py:193
  5.7 30.9 %collective-permute-start.5 = (bf16[128,2560]{1,0:T(8,128)(2,1)S(1)}, bf16[128,2560]{1,0:T(8,128)(2,1)}, u32[]{:S(2)}, u32[]{:S(2)}) collective-permute-start(bf16[128,2560]{1,0:T(8,128)(2,1)S(1)} %constant_dynamic-slice_fusion.8), channel_id=1, source_target_pairs={{0,12},{4,0},{8,4},{12,8},{1,13},{5,1},{9,5},{13,9},{2,14},{6,2},{... | collective-permute-start | bytes 1966088 | tf_op jit(solution)/shard_map/ppermute | solution.py:193
  23.6 26.8 %collective-permute-start.1 = (bf16[128,2560]{1,0:T(8,128)(2,1)S(1)}, bf16[128,2560]{1,0:T(8,128)(2,1)}, u32[]{:S(2)}, u32[]{:S(2)}) collective-permute-start(bf16[128,2560]{1,0:T(8,128)(2,1)S(1)} %collective-permute-done.refs_4_.refs_5_), channel_id=1, source_target_pairs={{0,4},{4,8},{8,12},{12,0},{1,5},{5,9},{9,13},{13,1},{2,6},{6,10},{... | collective-permute-start | bytes 1966088 | tf_op jit(solution)/shard_map/ppermute | solution.py:193
  23.6 28.5 %collective-permute-start.7 = (bf16[128,2560]{1,0:T(8,128)(2,1)S(1)}, bf16[128,2560]{1,0:T(8,128)(2,1)}, u32[]{:S(2)}, u32[]{:S(2)}) collective-permute-start(bf16[128,2560]{1,0:T(8,128)(2,1)S(1)} %collective-permute-done.refs_4_.refs_5_), channel_id=1, source_target_pairs={{0,16},{16,0},{1,17},{17,1},{2,18},{18,2},{3,19},{19,3},{4,20},{20... | collective-permute-start | bytes 1966088 | tf_op jit(solution)/shard_map/ppermute | solution.py:212
  36.6 16.6 %collective-permute-start.6 = (bf16[128,2560]{1,0:T(8,128)(2,1)}, bf16[128,2560]{1,0:T(8,128)(2,1)}, u32[]{:S(2)}, u32[]{:S(2)}) collective-permute-start(bf16[128,2560]{1,0:T(8,128)(2,1)} %collective-permute-done.5.refs_2_.refs_3_), channel_id=1, source_target_pairs={{0,16},{16,0},{1,17},{17,1},{2,18},{18,2},{3,19},{19,3},{4,20},{20... | collective-permute-start | bytes 1966088 | tf_op jit(solution)/shard_map/ppermute | solution.py:212
  38.2 15.0 %copy-start = (bf16[2,256,2560]{2,1,0:T(8,128)(2,1)S(1)}, bf16[2,256,2560]{2,1,0:T(8,128)(2,1)}, u32[]{:S(2)}) copy-start(bf16[2,256,2560]{2,1,0:T(8,128)(2,1)} %param.7) | copy-start | bytes 7864324
  50.4 9.6 %collective-permute-start.2 = (bf16[1,2,16,512]{3,2,0,1:T(8,128)(2,1)S(1)}, bf16[1,2,16,512]{3,2,0,1:T(8,128)(2,1)S(1)}, u32[]{:S(2)}, u32[]{:S(2)}) collective-permute-start(bf16[1,2,16,512]{3,2,0,1:T(8,128)(2,1)S(1)} %maximum_bitcast_fusion), channel_id=1, source_target_pairs={{0,12},{4,0},{8,4},{12,8},{1,13},{5,1},{9,5},{13,9},{2,14},{6,2},{... | collective-permute-start | bytes 98312 | tf_op jit(solution)/shard_map/ppermute | solution.py:193
  52.1 9.5 %collective-permute-start.3 = (bf16[1,2,16,512]{3,2,0,1:T(8,128)(2,1)S(1)}, bf16[1,2,16,512]{3,2,0,1:T(8,128)(2,1)S(1)}, u32[]{:S(2)}, u32[]{:S(2)}) collective-permute-start(bf16[1,2,16,512]{3,2,0,1:T(8,128)(2,1)S(1)} %maximum_bitcast_fusion), channel_id=1, source_target_pairs={{0,8},{4,12},{8,0},{12,4},{1,9},{5,13},{9,1},{13,5},{2,10},{6,14},... | collective-permute-start | bytes 98312 | tf_op jit(solution)/shard_map/ppermute | solution.py:193
  52.1 9.5 %collective-permute-start.4 = (bf16[1,2,16,512]{3,2,0,1:T(8,128)(2,1)S(1)}, bf16[1,2,16,512]{3,2,0,1:T(8,128)(2,1)S(1)}, u32[]{:S(2)}, u32[]{:S(2)}) collective-permute-start(bf16[1,2,16,512]{3,2,0,1:T(8,128)(2,1)S(1)} %maximum_bitcast_fusion), channel_id=1, source_target_pairs={{0,4},{4,8},{8,12},{12,0},{1,5},{5,9},{9,13},{13,1},{2,6},{6,10},{... | collective-permute-start | bytes 98312 | tf_op jit(solution)/shard_map/ppermute | solution.py:193
  53.1 1.3 %copy-start.1 = (bf16[256,2560]{1,0:T(8,128)(2,1)S(1)}, bf16[256,2560]{1,0:T(8,128)(2,1)}, u32[]{:S(2)}) copy-start(bf16[256,2560]{1,0:T(8,128)(2,1)} %refs_2_.1) | copy-start | bytes 3932164
  59.1 0.9 copy-start.4
  60.0 3.1 %copy-start.9 = (s32[8]{0:T(128)S(1)}, s32[8]{0:T(128)}, u32[]{:S(2)}) copy-start(s32[8]{0:T(128)} %param.11) | copy-start | bytes 100
  60.0 3.1 %copy-start.10 = (s32[16,1]{0,1:T(1,128)S(1)}, s32[16,1]{0,1:T(1,128)}, u32[]{:S(2)}) copy-start(s32[16,1]{0,1:T(1,128)} %param.10) | copy-start | bytes 196
  60.0 26.1 %collective-permute-start.10 = (f32[3,512,128]{2,1,0:T(8,128)}, f32[3,512,128]{2,1,0:T(8,128)}, u32[]{:S(2)}, u32[]{:S(2)}) collective-permute-start(f32[3,512,128]{2,1,0:T(8,128)} %get-tuple-element.21), channel_id=1, source_target_pairs={{0,1},{1,0},{2,3},{3,2},{4,5},{5,4},{6,7},{7,6},{8,9},{9,8},{10,11... | collective-permute-start | bytes 2359304 | tf_op jit(solution)/shard_map/ppermute | solution.py:229
  60.0 17.5 %collective-permute-start.9 = (bf16[128,2560]{1,0:T(8,128)(2,1)}, bf16[128,2560]{1,0:T(8,128)(2,1)}, u32[]{:S(2)}, u32[]{:S(2)}) collective-permute-start(bf16[128,2560]{1,0:T(8,128)(2,1)} %collective-permute-done.1.refs_7_), channel_id=1, source_target_pairs={{0,16},{16,0},{1,17},{17,1},{2,18},{18,2},{3,19},{19,3},{4,20},{20... | collective-permute-start | bytes 1966088 | tf_op jit(solution)/shard_map/ppermute | solution.py:212
  62.5 23.5 %collective-permute-start.14 = (bf16[576,512]{1,0:T(8,128)(2,1)}, bf16[576,512]{1,0:T(8,128)(2,1)}, u32[]{:S(2)}, u32[]{:S(2)}) collective-permute-start(bf16[576,512]{1,0:T(8,128)(2,1)} %pad_maximum_fusion), channel_id=1, source_target_pairs={{0,2},{2,0},{1,3},{3,1},{4,6},{6,4},{5,7},{7,5},{8,10},{10,8},{9,1... | collective-permute-start | bytes 1769480 | tf_op jit(solution)/shard_map/ppermute | solution.py:262
  63.1 22.8 %copy-start.7 = (s32[4]{0:T(128)S(1)}, s32[4]{0:T(128)}, u32[]{:S(2)}) copy-start(s32[4]{0:T(128)} %constant.88.clone) | copy-start | bytes 52
  77.5 1.3 %copy-start.2 = (bf16[256,2560]{1,0:T(8,128)(2,1)S(1)}, bf16[256,2560]{1,0:T(8,128)(2,1)}, u32[]{:S(2)}) copy-start(bf16[256,2560]{1,0:T(8,128)(2,1)} %refs_2_.1) | copy-start | bytes 3932164
  78.8 9.5 %copy-start.3 = (bf16[512,512]{1,0:T(8,128)(2,1)S(1)}, bf16[512,512]{1,0:T(8,128)(2,1)}, u32[]{:S(2)}) copy-start(bf16[512,512]{1,0:T(8,128)(2,1)} %pad_maximum_fusion.1.refs_6_) | copy-start | bytes 1572868
  78.8 9.5 %copy-start.5 = (f32[3,512,128]{2,1,0:T(8,128)S(1)}, f32[3,512,128]{2,1,0:T(8,128)}, u32[]{:S(2)}) copy-start(f32[3,512,128]{2,1,0:T(8,128)} %copy-done.4) | copy-start | bytes 2359300
  85.1 3.1 %collective-permute-start.11 = (f32[2,512,128]{2,1,0:T(8,128)S(1)}, f32[2,512,128]{2,1,0:T(8,128)S(1)}, u32[]{:S(2)}, u32[]{:S(2)}) collective-permute-start(f32[2,512,128]{2,1,0:T(8,128)S(1)} %get-tuple-element.22), channel_id=1, source_target_pairs={{0,1},{1,0},{2,3},{3,2},{4,5},{5,4},{6,7},{7,6},{8,9},{9,8},{10,11... | collective-permute-start | bytes 1572872 | tf_op jit(solution)/shard_map/ppermute | solution.py:229
  85.2 3.0 %collective-permute-start.12 = (f32[2,512,128]{2,1,0:T(8,128)S(1)}, f32[2,512,128]{2,1,0:T(8,128)S(1)}, u32[]{:S(2)}, u32[]{:S(2)}) collective-permute-start(f32[2,512,128]{2,1,0:T(8,128)S(1)} %get-tuple-element.23), channel_id=1, source_target_pairs={{0,1},{1,0},{2,3},{3,2},{4,5},{5,4},{6,7},{7,6},{8,9},{9,8},{10,11... | collective-permute-start | bytes 1572872 | tf_op jit(solution)/shard_map/ppermute | solution.py:229
  85.7 2.5 %collective-permute-start.13 = (f32[1,512,128]{2,1,0:T(8,128)S(1)}, f32[1,512,128]{2,1,0:T(8,128)S(1)}, u32[]{:S(2)}, u32[]{:S(2)}) collective-permute-start(f32[1,512,128]{2,1,0:T(8,128)S(1)} %get-tuple-element.24), channel_id=1, source_target_pairs={{0,1},{1,0},{2,3},{3,2},{4,5},{5,4},{6,7},{7,6},{8,9},{9,8},{10,11... | collective-permute-start | bytes 786440 | tf_op jit(solution)/shard_map/ppermute | solution.py:229
  91.0 10.6 %collective-permute-start.15 = (f32[1,2,16,640]{3,2,1,0:T(8,128)S(1)}, f32[1,2,16,640]{3,2,1,0:T(8,128)S(1)}, u32[]{:S(2)}, u32[]{:S(2)}) collective-permute-start(f32[1,2,16,640]{3,2,1,0:T(8,128)S(1)} %get-tuple-element.35), channel_id=1, source_target_pairs={{0,4},{4,8},{8,12},{12,0},{1,5},{5,9},{9,13},{13,1},{2,6},{6,10},{... | collective-permute-start | bytes 245768 | tf_op jit(solution)/shard_map/ppermute | solution.py:193
  98.8 6.8 %collective-permute-start.16 = (f32[1,2,16,640]{3,2,1,0:T(8,128)S(1)}, f32[1,2,16,640]{3,2,1,0:T(8,128)S(1)}, u32[]{:S(2)}, u32[]{:S(2)}) collective-permute-start(f32[1,2,16,640]{3,2,1,0:T(8,128)S(1)} %get-tuple-element.34), channel_id=1, source_target_pairs={{0,8},{4,12},{8,0},{12,4},{1,9},{5,13},{9,1},{13,5},{2,10},{6,14},... | collective-permute-start | bytes 245768 | tf_op jit(solution)/shard_map/ppermute | solution.py:193
  99.0 6.5 %collective-permute-start.17 = (f32[1,2,16,640]{3,2,1,0:T(8,128)S(1)}, f32[1,2,16,640]{3,2,1,0:T(8,128)S(1)}, u32[]{:S(2)}, u32[]{:S(2)}) collective-permute-start(f32[1,2,16,640]{3,2,1,0:T(8,128)S(1)} %get-tuple-element.33), channel_id=1, source_target_pairs={{0,12},{4,0},{8,4},{12,8},{1,13},{5,1},{9,5},{13,9},{2,14},{6,2},{... | collective-permute-start | bytes 245768 | tf_op jit(solution)/shard_map/ppermute | solution.py:193
  105.8 1.9 %collective-permute-start.18 = (bf16[1,16,512]{2,1,0:T(8,128)(2,1)S(1)}, bf16[1,16,512]{2,1,0:T(8,128)(2,1)S(1)}, u32[]{:S(2)}, u32[]{:S(2)}) collective-permute-start(bf16[1,16,512]{2,1,0:T(8,128)(2,1)S(1)} %get-tuple-element.52), channel_id=1, source_target_pairs={{0,1},{1,0},{2,3},{3,2},{4,5},{5,4},{6,7},{7,6},{8,9},{9,8},{10,11... | collective-permute-start | bytes 49160 | tf_op jit(solution)/shard_map/ppermute | solution.py:289
  105.9 3.9 %collective-permute-start.19 = (bf16[1,16,512]{2,1,0:T(8,128)(2,1)S(1)}, bf16[1,16,512]{2,1,0:T(8,128)(2,1)S(1)}, u32[]{:S(2)}, u32[]{:S(2)}) collective-permute-start(bf16[1,16,512]{2,1,0:T(8,128)(2,1)S(1)} %get-tuple-element.51), channel_id=1, source_target_pairs={{0,2},{2,0},{1,3},{3,1},{4,6},{6,4},{5,7},{7,5},{8,10},{10,8},{9,1... | collective-permute-start | bytes 49160 | tf_op jit(solution)/shard_map/ppermute | solution.py:290
  106.4 3.3 %collective-permute-start.20 = (bf16[1,16,512]{2,1,0:T(8,128)(2,1)S(1)}, bf16[1,16,512]{2,1,0:T(8,128)(2,1)S(1)}, u32[]{:S(2)}, u32[]{:S(2)}) collective-permute-start(bf16[1,16,512]{2,1,0:T(8,128)(2,1)S(1)} %get-tuple-element.51), channel_id=1, source_target_pairs={{0,3},{3,0},{1,2},{2,1},{4,7},{7,4},{5,6},{6,5},{8,11},{11,8},{9,1... | collective-permute-start | bytes 49160 | tf_op jit(solution)/shard_map/ppermute | solution.py:291
  110.0 0.6 copy-start.8

commit v3 on v2

--- a/solution.py
+++ b/solution.py
@@ -8,7 +8,8 @@
 from jax.sharding import Mesh, PartitionSpec as P
 
 HEAD_DIM = 64
-EMPTY = -3e38
+EMPTY = -(2.0**127)
+CHUNKS = 2
 VMEM_LIMIT = 40 * 1024 * 1024
 SWAP = [(0, 1), (1, 0)]
 CROSS = [(0, 3), (3, 0), (1, 2), (2, 1)]
@@ -34,7 +35,10 @@
             keep = whole[pl.ds(pl.multiple_of(core * half, half), half), :]
             send = whole[pl.ds(pl.multiple_of((1 - core) * half, half), half), :]
         else:
-            first, second = (refs[block][...] for block in blocks_of)
+            parts = [refs[block][...] for block in blocks_of]
+            first, second = (
+                jnp.concatenate(part, axis=0) for part in (parts[: len(parts) // 2], parts[len(parts) // 2 :])
+            )
             keep = jnp.where(same == 1, first, second)
             send = jnp.where(same == 1, second, first)
         product = lax.dot_general(
@@ -49,7 +53,7 @@
 
 
 def attend_kernel(place_ref, spot_ref, query_ref, *refs, pieces):
-    *refs, own_ref, partner_ref, out_ref, key_ref = refs
+    *refs, own_ref, partner_ref, packed_ref, key_ref, out_ref = refs
     residuals = own_ref, partner_ref
     partner_queries = own_ref.shape[0]
     query_len, held = query_ref.shape[1:]
@@ -106,6 +110,13 @@
         out_ref[place, :, held:] = jnp.where(
             ext == 0, top_row, jnp.where(ext == 1, before + total_row, 0.0)
         )
+    packed_ref[:, :, :held] = out_ref[:, :, :held].astype(jnp.bfloat16)
+    rest = out_ref[:, 0:2, held:]
+    for part in range(3):
+        rounded = rest.astype(jnp.bfloat16)
+        rest = rest - rounded.astype(jnp.float32)
+        packed_ref[:, 2 * part : 2 * part + 2, held:] = rounded
+    packed_ref[:, 6:, held:] = jnp.zeros_like(packed_ref[:, 6:, held:])
 
 
 def merge_kernel(*refs):
@@ -122,18 +133,22 @@
             )
         return start
 
+    def row_of(part, at, slot, row):
+        packed = part[at, slot, :, held:].astype(jnp.float32)
+        return packed[row : row + 1] + packed[row + 2 : row + 3] + packed[row + 4 : row + 5]
+
     for slot in range(out_ref.shape[0]):
         def top_step(part, at, top):
-            return jnp.maximum(top, part[at, slot, 0:1, held:])
+            return jnp.maximum(top, row_of(part, at, slot, 0))
 
         def total_step(part, at, total):
-            return total + jnp.exp(part[at, slot, 0:1, held:] - top) * part[at, slot, 1:2, held:]
+            return total + jnp.exp(row_of(part, at, slot, 0) - top) * row_of(part, at, slot, 1)
 
         def blend_step(part, at, blend):
-            share = jnp.exp(part[at, slot, 0:1, held:] - top) / total
+            share = jnp.exp(row_of(part, at, slot, 0) - top) / total
             column = jnp.sum(jnp.where(square, share, 0.0), axis=1, keepdims=True)
             spread = head_pick(jnp.broadcast_to(column, (tall, held)), query_len)
-            return blend + spread * part[at, slot, :, :held]
+            return blend + spread * part[at, slot, :, :held].astype(jnp.float32)
 
         top = over(jnp.full((1, tall), EMPTY, jnp.float32), top_step)
         total = over(jnp.zeros((1, tall), jnp.float32), total_step)
@@ -141,6 +156,20 @@
         out_ref[slot] = blend.astype(out_ref.dtype)
 
 
+def assemble_kernel(flag_ref, mine_ref, core_ref, side_ref, both_ref, out_ref, *, order, span):
+    side, core = flag_ref[0], flag_ref[1]
+    mine, by_core, by_side, by_both = (ref[0] for ref in (mine_ref, core_ref, side_ref, both_ref))
+    taken = {}
+    for of_side in range(2):
+        for of in range(2):
+            near = jnp.where(core == of, mine, by_core)
+            far = jnp.where(core == of, by_side, by_both)
+            taken[of_side, of] = jnp.where(side == of_side, near, far)
+    out_ref[0] = jnp.concatenate(
+        [taken[of_side, of][:, first : first + span] for of_side, of, first in order], axis=1
+    )
+
+
 def in_vmem(count):
     return [pl.BlockSpec(memory_space=pltpu.VMEM)] * count
 
@@ -149,9 +178,9 @@
     return [pl.BlockSpec(memory_space=pltpu.SMEM)] * count
 
 
-def project(flags, operands, jobs, sends, name):
+def project(flags, operands, jobs, sends, flops, name):
     rows, units = operands[0].shape
-    half = min(operand.shape[0] for operand in operands)
+    half = operands[-1].shape[0] * CHUNKS
     shapes = [jax.ShapeDtypeStruct((count, rows, half), jnp.float32) for count in [len(jobs)] + sends]
     return pl.pallas_call(
         functools.partial(project_kernel, jobs=jobs, sends=sends),
@@ -159,9 +188,13 @@
         in_specs=in_smem(1) + in_vmem(len(operands)),
         out_specs=in_vmem(len(shapes)),
         compiler_params=pltpu.CompilerParams(vmem_limit_bytes=VMEM_LIMIT),
-        cost_estimate=pl.CostEstimate(flops=1, bytes_accessed=1, transcendentals=0),
+        cost_estimate=pl.CostEstimate(flops=flops, bytes_accessed=1, transcendentals=0),
         name=name,
     )(flags, *operands)
+
+
+def after(array, earlier):
+    return lax.optimization_barrier((array, *earlier))[0] if earlier else array
 
 
 def body(hidden_states, passage_states, down_weight, block_question, question_owner, decoder_states):
@@ -201,29 +234,37 @@
 
     if lined:
         half = shard // 2
-        sent = lax.dynamic_slice_in_dim(down_weight, group * half, half, axis=0)
-        below = shifted(sent, 1)
-        above = shifted(sent, -1)
-        opposite = shifted(below, 1)
-        queries, _ = lax.optimization_barrier((queries, opposite))
+        chunk = half // CHUNKS
+        sent = [
+            lax.dynamic_slice_in_dim(down_weight, group * half + at * chunk, chunk, axis=0) for at in range(CHUNKS)
+        ]
+        below, above, opposite = [], [], []
+        for at in range(CHUNKS):
+            below.append(shifted(after(sent[at], below[-1:]), 1))
+            above.append(shifted(after(sent[at], above[-1:]), -1))
+        opposite.append(shifted(after(below[0], below[-1:]), 1))
+        opposite.append(shifted(after(below[1], above[-1:]), 1))
+        swapped = []
+        for at, piece in enumerate([below[0], above[0], below[1], above[1]] + opposite):
+            swapped.append(lax.ppermute(after(piece, swapped[max(at - 2, 0) : max(at - 1, 0)]), "groups", SWAP))
+        weights = [down_weight] + above + swapped[1:4:2] + below + swapped[0:4:2] + opposite + swapped[4:]
+        queries = after(queries, opposite)
         queries = jnp.concatenate([queries] + [shifted(queries, -ahead) for ahead in range(1, highs)], axis=0)
-        weights = [down_weight]
-        for piece in (above, below, opposite):
-            weights += [piece, lax.ppermute(piece, "groups", SWAP)]
-        flags = jnp.stack([core, (group == core).astype(core.dtype)])
-        blocks_of = [(0,), (1, 2), (3, 4), (5, 6)]
+        flags = after(jnp.stack([core, (group == core).astype(core.dtype)]), opposite)
+        blocks_of = [(0,)] + [tuple(range(1 + at * 2 * CHUNKS, 1 + (at + 1) * 2 * CHUNKS)) for at in range(3)]
         spots = lax.rem(high + jnp.array([0, 1, 3, 2], jnp.int32), highs)
 
         def jobs_of(rows_of, chosen, count):
             return [(rows_of, tuple(at + count for at in blocks_of[one])) for one in chosen]
 
-        kept, *away = project(flags, [hidden] + weights[:5], jobs_of(0, (0, 1, 2), 1), [3], "project_own")
+        kept, *away = project(flags, [hidden] + weights[: 1 + 4 * CHUNKS], jobs_of(0, (0, 1, 2), 1), [3], 12 * rows * half * units, "project_own")
         flags, kept, away = lax.optimization_barrier((flags, kept, away))
         late_kept, *late_away = project(
             flags,
             [hidden, partner_hidden] + weights,
             jobs_of(0, (3,), 2) + jobs_of(1, range(4), 2),
             [2, 2, 1],
+            1,
             "project_rest",
         )
         others = [lax.ppermute(piece, "mp", SWAP) for piece in away + late_away]
@@ -260,13 +301,17 @@
 
     leaving = jnp.concatenate([leaving, queries[:, 1].reshape(-1, held)], axis=0)
     partner = lax.ppermute(leaving, "side", SWAP)
+    packed = (2 * members, query_len, held + heads * query_len)
     operands = summands + [own_residual, partner]
     partials = pl.pallas_call(
         functools.partial(attend_kernel, pieces=pieces),
-        out_shape=jax.ShapeDtypeStruct((2 * members, query_len, held + heads * query_len), jnp.float32),
+        out_shape=jax.ShapeDtypeStruct(packed, jnp.bfloat16),
         in_specs=in_smem(2) + in_vmem(1 + len(operands)),
         out_specs=pl.BlockSpec(memory_space=pltpu.VMEM),
-        scratch_shapes=[pltpu.VMEM((2 * blocks, block_len, held), jnp.bfloat16)],
+        scratch_shapes=[
+            pltpu.VMEM((2 * blocks, block_len, held), jnp.bfloat16),
+            pltpu.VMEM(packed, jnp.float32),
+        ],
         compiler_params=pltpu.CompilerParams(vmem_limit_bytes=VMEM_LIMIT),
         name="attend",
     )(places, spots, queries[:, 0], *operands)
@@ -289,17 +334,20 @@
     by_core = lax.ppermute(mine, "mp", SWAP)
     by_side = lax.ppermute(away, "side", SWAP)
     by_both = lax.ppermute(away, ("side", "mp"), CROSS)
-    near = [jnp.where(core == at, mine, by_core) for at in range(cores)]
-    far = [jnp.where(core == at, by_side, by_both) for at in range(cores)]
-    sides = [[jnp.where(side == at, near[of], far[of]) for of in range(cores)] for at in range(2)]
-    columns = []
     if lined:
         order = [(at, of_side, of) for at in range(spans) for of_side in range(2) for of in range(cores)]
     else:
         order = [(at, of_side, of) for of in range(cores) for at in range(spans) for of_side in range(2)]
-    for at, of_side, of in order:
-        columns.append(sides[of_side][of][:, :, at * span : (at + 1) * span])
-    return jnp.concatenate(columns, axis=-1)
+    flags = jnp.stack([side, core])
+    order = [(of_side, of, at * span) for at, of_side, of in order]
+    return pl.pallas_call(
+        functools.partial(assemble_kernel, order=order, span=span),
+        out_shape=jax.ShapeDtypeStruct((1, query_len, width), decoder_states.dtype),
+        in_specs=in_smem(1) + in_vmem(4),
+        out_specs=pl.BlockSpec(memory_space=pltpu.VMEM),
+        compiler_params=pltpu.CompilerParams(vmem_limit_bytes=VMEM_LIMIT),
+        name="assemble",
+    )(flags, mine, by_core, by_side, by_both)
 
 
 def solution(mesh):

time: 111 us -> 109 us (0.982)
  waiting for transfers between devices: 59.7 us -> 48.4 us
  local copies, waits for them, and re-layouts: 7.7 us -> 17.5 us
    unnamed x40 -> x55, local copies, waits for them, and re-layouts: 4.3 us -> 14 us
    ppermute x3 -> x6, waiting for transfers between devices: 14.3 us -> 6.06 us  [body(): lax.ppermute(after(piece, swapped[max(at - 2, 0):max(at - 1, 0)]), 'group...]
    ppermute x9 -> x12, waiting for transfers between devices: 41.1 us -> 38.4 us  [shifted(): lax.ppermute(array, 'high', [(at, (at + shift) % highs) for at in range(h...]
    ppermute x3 -> x6, starting transfers between devices: 4.62 us -> 6.3 us  [body(): lax.ppermute(after(piece, swapped[max(at - 2, 0):max(at - 1, 0)]), 'group...]
    pallas_call x2, Pallas kernels: 11 us -> 9.43 us  [project(): pl.pallas_call(functools.partial(project_kernel, jobs=jobs, sends=sends),...]
    ppermute x9 -> x12, starting transfers between devices: 17 us -> 15.4 us  [shifted(): lax.ppermute(array, 'high', [(at, (at + shift) % highs) for at in range(h...]
    ppermute x1, starting transfers between devices: 0.07 us -> 1.54 us  [body(): by_core = lax.ppermute(mine, 'mp', SWAP)]
    ppermute x1, starting transfers between devices: 1.3 us -> 0.07 us  [body(): by_both = lax.ppermute(away, ('side', 'mp'), CROSS)]
  transfers between devices with their start and end apart: 21 -> 27, of which waited for: 8 -> 13; matrix products, arithmetic and copies ran while one was open for 4% -> 4% of each run, Pallas kernels for 10% -> 9%
where the time goes in v3:
time: 109 us
  waiting for transfers between devices  48.4 us (44%)
  starting transfers between devices  28.1 us (26%)
  local copies, waits for them, and re-layouts  17.5 us (16%)
  Pallas kernels  13.4 us (12%)
  other arithmetic  1.27 us (1%)
    ppermute x12, waiting for transfers between devices, shifted(): lax.ppermute(array, 'high', [(at, (at + shift) % highs) for at in range(h...  38.4 us
    ppermute x12, starting transfers between devices, shifted(): lax.ppermute(array, 'high', [(at, (at + shift) % highs) for at in range(h...  15.4 us
    unnamed x55, local copies, waits for them, and re-layouts  14 us
    pallas_call x2, Pallas kernels, project(): pl.pallas_call(functools.partial(project_kernel, jobs=jobs, sends=sends),...  9.43 us
    ppermute x6, starting transfers between devices, body(): lax.ppermute(after(piece, swapped[max(at - 2, 0):max(at - 1, 0)]), 'group...  6.3 us
    ppermute x6, waiting for transfers between devices, body(): lax.ppermute(after(piece, swapped[max(at - 2, 0):max(at - 1, 0)]), 'group...  6.06 us
    ppermute x1, starting transfers between devices, body(): partner_hidden = lax.ppermute(hidden, 'side', SWAP)  2.94 us
    pallas_call x1, Pallas kernels, body(): pl.pallas_call(functools.partial(attend_kernel, pieces=pieces), out_shape...  2.49 us
  transfers between devices with their start and end apart: 27, of which 13 were waited for; matrix products, arithmetic and copies ran while one was open for 4% of the time, Pallas kernels for 9%

profile of v3, /device:TPU:0, one launch (start us, length us, event | category | flops | bytes accessed | tf_op | source)
XLA Modules:
  0.0 108.8 jit_solution(556852890121647150)
XLA Ops:
  0.0 2.9 %collective-permute-start.13 = (bf16[512,2560]{1,0:T(8,128)(2,1)}, bf16[512,2560]{1,0:T(8,128)(2,1)}, u32[]{:S(2)}, u32[]{:S(2)}) collective-permute-start(bf16[512,2560]{1,0:T(8,128)(2,1)} %bitcast.19), channel_id=1, source_target_pairs={{0,2},{2,0},{1,3},{3,1},{4,6},{6,4},{5,7},{7,5},{8,10},{10,8},{9,1... | collective-permute-start | bytes 7864328 | tf_op jit(solution)/shard_map/ppermute | solution.py:229
  2.9 1.8 %constant_dynamic-slice_fusion.8 = (bf16[64,2560]{1,0:T(8,128)(2,1)}, bf16[64,2560]{1,0:T(8,128)(2,1)S(1)}) fusion(bf16[256,2560]{1,0:T(8,128)(2,1)} %refs_2_.1, s32[]{:T(128)S(6)} %select_n.77, s32[]{:T(128)S(6)} %select_n.76), kind=kLoop, calls=%fused_computation.20 | loop fusion | bytes 1310728 | tf_op jit(solution)/shard_map/dynamic_slice | solution.py:239
  4.8 1.6 %collective-permute-start = (bf16[64,2560]{1,0:T(8,128)(2,1)S(1)}, bf16[64,2560]{1,0:T(8,128)(2,1)S(1)}, u32[]{:S(2)}, u32[]{:S(2)}) collective-permute-start(bf16[64,2560]{1,0:T(8,128)(2,1)S(1)} %get-tuple-element.52), channel_id=1, source_target_pairs={{0,4},{4,8},{8,12},{12,0},{1,5},{5,9},{9,13},{13,1},{2,6},{6,10},{... | collective-permute-start | bytes 983048 | tf_op jit(solution)/shard_map/ppermute | solution.py:226
  6.3 2.2 %collective-permute-start.3 = (bf16[64,2560]{1,0:T(8,128)(2,1)S(1)}, bf16[64,2560]{1,0:T(8,128)(2,1)S(1)}, u32[]{:S(2)}, u32[]{:S(2)}) collective-permute-start(bf16[64,2560]{1,0:T(8,128)(2,1)S(1)} %get-tuple-element.52), channel_id=1, source_target_pairs={{0,12},{4,0},{8,4},{12,8},{1,13},{5,1},{9,5},{13,9},{2,14},{6,2},{... | collective-permute-start | bytes 983048 | tf_op jit(solution)/shard_map/ppermute | solution.py:226
  8.6 8.7 %collective-permute-done.refs_6_.refs_7_ = bf16[64,2560]{1,0:T(8,128)(2,1)S(1)} collective-permute-done((bf16[64,2560]{1,0:T(8,128)(2,1)S(1)}, bf16[64,2560]{1,0:T(8,128)(2,1)S(1)}, u32[]{:S(2)}, u32[]{:S(2)}) %collective-permute-start) | collective-permute-done | bytes 327712 | tf_op jit(solution)/shard_map/ppermute | solution.py:226
  17.3 5.8 %collective-permute-done.3.refs_2_.refs_3_ = bf16[64,2560]{1,0:T(8,128)(2,1)S(1)} collective-permute-done((bf16[64,2560]{1,0:T(8,128)(2,1)S(1)}, bf16[64,2560]{1,0:T(8,128)(2,1)S(1)}, u32[]{:S(2)}, u32[]{:S(2)}) %collective-permute-start.3) | collective-permute-done | bytes 327712 | tf_op jit(solution)/shard_map/ppermute | solution.py:226
  23.1 2.8 %collective-permute-start.4 = (bf16[64,2560]{1,0:T(8,128)(2,1)}, bf16[64,2560]{1,0:T(8,128)(2,1)S(1)}, u32[]{:S(2)}, u32[]{:S(2)}) collective-permute-start(bf16[64,2560]{1,0:T(8,128)(2,1)} %get-tuple-element.26), channel_id=1, source_target_pairs={{0,12},{4,0},{8,4},{12,8},{1,13},{5,1},{9,5},{13,9},{2,14},{6,2},{... | collective-permute-start | bytes 983048 | tf_op jit(solution)/shard_map/ppermute | solution.py:226
  25.9 1.5 %collective-permute-start.9 = (bf16[64,2560]{1,0:T(8,128)(2,1)S(1)}, bf16[64,2560]{1,0:T(8,128)(2,1)S(1)}, u32[]{:S(2)}, u32[]{:S(2)}) collective-permute-start(bf16[64,2560]{1,0:T(8,128)(2,1)S(1)} %collective-permute-done.3.refs_2_.refs_3_), channel_id=1, source_target_pairs={{0,16},{16,0},{1,17},{17,1},{2,18},{18,2},{3,19},{19,3},{4,20},{20... | collective-permute-start | bytes 983048 | tf_op jit(solution)/shard_map/ppermute | solution.py:249
  27.9 1.5 %constant_dynamic-slice_fusion.3 = (bf16[512,128]{1,0:T(8,128)(2,1)S(1)}, bf16[512,128]{1,0:T(8,128)(2,1)S(1)}, bf16[512,128]{1,0:T(8,128)(2,1)S(1)}, bf16[512,1...) fusion(bf16[512,2048]{1,0:T(8,128)(2,1)} %bitcast.22, ...), kind=kLoop, calls=%fused_computation.15 | loop fusion | bytes 2097184 | tf_op jit(solution)/shard_map/dynamic_slice | solution.py:222
  29.4 2.7 %collective-permute-done.1.refs_7_.refs_8_ = bf16[64,2560]{1,0:T(8,128)(2,1)S(1)} collective-permute-done((bf16[64,2560]{1,0:T(8,128)(2,1)}, bf16[64,2560]{1,0:T(8,128)(2,1)S(1)}, u32[]{:S(2)}, u32[]{:S(2)}) %collective-permute-start.1) | collective-permute-done | bytes 327712 | tf_op jit(solution)/shard_map/ppermute | solution.py:226
  32.1 4.8 %collective-permute-done.4.refs_3_.refs_4_ = bf16[64,2560]{1,0:T(8,128)(2,1)S(1)} collective-permute-done((bf16[64,2560]{1,0:T(8,128)(2,1)}, bf16[64,2560]{1,0:T(8,128)(2,1)S(1)}, u32[]{:S(2)}, u32[]{:S(2)}) %collective-permute-start.4) | collective-permute-done | bytes 327712 | tf_op jit(solution)/shard_map/ppermute | solution.py:226
  38.2 1.5 %collective-permute-start.10 = (bf16[64,2560]{1,0:T(8,128)(2,1)S(1)}, bf16[64,2560]{1,0:T(8,128)(2,1)S(1)}, u32[]{:S(2)}, u32[]{:S(2)}) collective-permute-start(bf16[64,2560]{1,0:T(8,128)(2,1)S(1)} %collective-permute-done.4.refs_3_.refs_4_), channel_id=1, source_target_pairs={{0,16},{16,0},{1,17},{17,1},{2,18},{18,2},{3,19},{19,3},{4,20},{20... | collective-permute-start | bytes 983048 | tf_op jit(solution)/shard_map/ppermute | solution.py:249
  41.0 8.3 %collective-permute-done.5.refs_12_ = bf16[64,2560]{1,0:T(8,128)(2,1)} collective-permute-done((bf16[64,2560]{1,0:T(8,128)(2,1)S(1)}, bf16[64,2560]{1,0:T(8,128)(2,1)}, u32[]{:S(2)}, u32[]{:S(2)}) %collective-permute-start.5) | collective-permute-done | bytes 327712 | tf_op jit(solution)/shard_map/ppermute | solution.py:226
  49.4 6.4 %collective-permute-done.2.refs_11_ = bf16[64,2560]{1,0:T(8,128)(2,1)} collective-permute-done((bf16[64,2560]{1,0:T(8,128)(2,1)S(1)}, bf16[64,2560]{1,0:T(8,128)(2,1)}, u32[]{:S(2)}, u32[]{:S(2)}) %collective-permute-start.2) | collective-permute-done | bytes 327712 | tf_op jit(solution)/shard_map/ppermute | solution.py:226
  55.8 2.1 %collective-permute-start.8 = (bf16[1,2,16,512]{3,2,0,1:T(8,128)(2,1)S(1)}, bf16[1,2,16,512]{3,2,0,1:T(8,128)(2,1)S(1)}, u32[]{:S(2)}, u32[]{:S(2)}) collective-permute-start(bf16[1,2,16,512]{3,2,0,1:T(8,128)(2,1)S(1)} %maximum_bitcast_fusion), channel_id=1, source_target_pairs={{0,4},{4,8},{8,12},{12,0},{1,5},{5,9},{9,13},{13,1},{2,6},{6,10},{... | collective-permute-start | bytes 98312 | tf_op jit(solution)/shard_map/ppermute | solution.py:226
  57.9 1.6 %collective-permute-start.15 = (bf16[64,2560]{1,0:T(8,128)(2,1)}, bf16[64,2560]{1,0:T(8,128)(2,1)}, u32[]{:S(2)}, u32[]{:S(2)}) collective-permute-start(bf16[64,2560]{1,0:T(8,128)(2,1)} %collective-permute-done.5.refs_12_), channel_id=1, source_target_pairs={{0,16},{16,0},{1,17},{17,1},{2,18},{18,2},{3,19},{19,3},{4,20},{20... | collective-permute-start | bytes 983048 | tf_op jit(solution)/shard_map/ppermute | solution.py:249
  59.6 1.7 %copy-done.1 = bf16[2,256,2560]{2,1,0:T(8,128)(2,1)S(1)} copy-done((bf16[2,256,2560]{2,1,0:T(8,128)(2,1)S(1)}, bf16[2,256,2560]{2,1,0:T(8,128)(2,1)}, u32[]{:S(2)}) %copy-start.1) | copy-done | bytes 2621464
  63.2 3.7 %project_own.1 = (f32[3,512,128]{2,1,0:T(8,128)S(1)}, f32[3,512,128]{2,1,0:T(8,128)}) custom-call(s32[2]{0:T(128)S(1)} %pad_add_fusion.2.flag_ref, bf16[512,2560]{1,0:T(8,128)(2,1)S(1)} %bitcast.20, bf16[256,2560]{1,0:T(8,128)(2,1)S(1)} %copy-done, bf16[64,2560]{1,0:T(8,128)(2,1)S(1)} %collective-permute-done.3.refs_2_.refs_3_, ...), custom_call_target="tpu_custom_call" | custom-call | flops 2013265920 | bytes 1 | tf_op jit(solution)/shard_map/project_own/pallas_call | solution.py:185
  69.1 6.1 %collective-permute-done.14.refs_13_ = bf16[64,2560]{1,0:T(8,128)(2,1)} collective-permute-done((bf16[64,2560]{1,0:T(8,128)(2,1)}, bf16[64,2560]{1,0:T(8,128)(2,1)}, u32[]{:S(2)}, u32[]{:S(2)}) %collective-permute-start.14) | collective-permute-done | bytes 327712 | tf_op jit(solution)/shard_map/ppermute | solution.py:249
  75.2 1.7 %copy-done.2 = bf16[2,256,2560]{2,1,0:T(8,128)(2,1)S(1)} copy-done((bf16[2,256,2560]{2,1,0:T(8,128)(2,1)S(1)}, bf16[2,256,2560]{2,1,0:T(8,128)(2,1)}, u32[]{:S(2)}) %copy-start.2) | copy-done | bytes 2621464
  77.9 1.0 copy-done.6
  78.9 1.0 copy-done.9
  79.8 1.0 copy-done.12
  84.7 5.8 %project_rest.1 = (f32[5,512,128]{2,1,0:T(8,128)S(1)}, f32[2,512,128]{2,1,0:T(8,128)S(1)}, f32[2,512,128]{2,1,0:T(8,128)S(1)}, f32[1,512,128]{2,1,0:T(8,128)S(1)}) custom-call(s32[2]{0:T(128)S(1)} %pad_add_fusion.2.flag_ref, bf16[512,2560]{1,0:T(8,128)(2,1)S(1)} %bitcast.21, bf16[512,2560]{1,0:T(8,128)(2,1)} %collective-permute-done.13.refs_1_, ...), custom_call_target="tpu_custom_call" | custom-call | flops 1 | bytes 1 | tf_op jit(solution)/shard_map/project_rest/pallas_call | solution.py:185
  91.4 2.2 %collective-permute-done.19.refs_5_ = f32[1,512,128]{2,1,0:T(8,128)S(1)} collective-permute-done((f32[1,512,128]{2,1,0:T(8,128)S(1)}, f32[1,512,128]{2,1,0:T(8,128)S(1)}, u32[]{:S(2)}, u32[]{:S(2)}) %collective-permute-start.19) | collective-permute-done | bytes 262176 | tf_op jit(solution)/shard_map/ppermute | solution.py:270
  93.6 2.5 %attend.1 = bf16[8,16,640]{2,1,0:T(8,128)(2,1)S(1)} custom-call(s32[4]{0:T(128)S(1)} %get-tuple-element.72.place_ref, s32[4]{0:T(128)S(1)} %get-tuple-element.71.spot_ref, bf16[4,16,512]{2,1,0:T(8,128)(2,1)S(1)} %get-tuple-element.58.query_ref, f32[3,512,128]{2,1,0:T(8,128)S(1)} %get-tuple-element.34.refs_0_, f32[5,512,128]{2,1,0:T(8,128)S(1)} %get-tuple-element.38.refs_1_, ...), custom_call_target="tpu_custom_call" | custom-call | tf_op jit(solution)/shard_map/attend/pallas_call | solution.py:306
  96.1 1.5 %collective-permute-start.21 = (bf16[1,2,16,640]{3,2,1,0:T(8,128)(2,1)S(1)}, bf16[1,2,16,640]{3,2,1,0:T(8,128)(2,1)S(1)}, u32[]{:S(2)}, u32[]{:S(2)}) collective-permute-start(bf16[1,2,16,640]{3,2,1,0:T(8,128)(2,1)S(1)} %get-tuple-element.55), channel_id=1, source_target_pairs={{0,4},{4,8},{8,12},{12,0},{1,5},{5,9},{9,13},{13,1},{2,6},{6,10},{... | collective-permute-start | bytes 122888 | tf_op jit(solution)/shard_map/ppermute | solution.py:226
  97.5 1.5 %collective-permute-start.22 = (bf16[1,2,16,640]{3,2,1,0:T(8,128)(2,1)S(1)}, bf16[1,2,16,640]{3,2,1,0:T(8,128)(2,1)S(1)}, u32[]{:S(2)}, u32[]{:S(2)}) collective-permute-start(bf16[1,2,16,640]{3,2,1,0:T(8,128)(2,1)S(1)} %get-tuple-element.54), channel_id=1, source_target_pairs={{0,8},{4,12},{8,0},{12,4},{1,9},{5,13},{9,1},{13,5},{2,10},{6,14},... | collective-permute-start | bytes 122888 | tf_op jit(solution)/shard_map/ppermute | solution.py:226
  99.0 2.6 %collective-permute-start.23 = (bf16[1,2,16,640]{3,2,1,0:T(8,128)(2,1)S(1)}, bf16[1,2,16,640]{3,2,1,0:T(8,128)(2,1)S(1)}, u32[]{:S(2)}, u32[]{:S(2)}) collective-permute-start(bf16[1,2,16,640]{3,2,1,0:T(8,128)(2,1)S(1)} %get-tuple-element.53), channel_id=1, source_target_pairs={{0,12},{4,0},{8,4},{12,8},{1,13},{5,1},{9,5},{13,9},{2,14},{6,2},{... | collective-permute-start | bytes 122888 | tf_op jit(solution)/shard_map/ppermute | solution.py:226
  102.0 1.3 %collective-permute-done.22.refs_2_ = bf16[1,2,16,640]{3,2,1,0:T(8,128)(2,1)S(1)} collective-permute-done((bf16[1,2,16,640]{3,2,1,0:T(8,128)(2,1)S(1)}, bf16[1,2,16,640]{3,2,1,0:T(8,128)(2,1)S(1)}, u32[]{:S(2)}, u32[]{:S(2)}) %collective-permute-start.22) | collective-permute-done | bytes 40992 | tf_op jit(solution)/shard_map/ppermute | solution.py:226
  104.3 1.5 %collective-permute-start.24 = (bf16[1,16,512]{2,1,0:T(8,128)(2,1)S(1)}, bf16[1,16,512]{2,1,0:T(8,128)(2,1)S(1)}, u32[]{:S(2)}, u32[]{:S(2)}) collective-permute-start(bf16[1,16,512]{2,1,0:T(8,128)(2,1)S(1)} %get-tuple-element.68.mine_ref), channel_id=1, source_target_pairs={{0,1},{1,0},{2,3},{3,2},{4,5},{5,4},{6,7},{7,6},{8,9},{9,8},{10,11... | collective-permute-start | bytes 49160 | tf_op jit(solution)/shard_map/ppermute | solution.py:334
  107.6 1.2 %assemble.1 = bf16[1,16,2048]{2,1,0:T(8,128)(2,1)} custom-call(s32[2]{0:T(128)S(1)} %pad_add_fusion.flag_ref, bf16[1,16,512]{2,1,0:T(8,128)(2,1)S(1)} %get-tuple-element.68.mine_ref, bf16[1,16,512]{2,1,0:T(8,128)(2,1)S(1)} %collective-permute-done.24.core_ref, bf16[1,16,512]{2,1,0:T(8,128)(2,1)S(1)} %collective-permute-done.25.side_ref, ...), custom_call_target="tpu_custom_call" | custom-call | tf_op jit(solution)/shard_map/assemble/pallas_call | solution.py:343
  (98 shorter events, 16.1 us)
Async XLA Ops:
  0.0 27.9 %copy-start.22 = (bf16[1,16,2048]{2,1,0:T(8,128)(2,1)S(1)}, bf16[1,16,2048]{2,1,0:T(8,128)(2,1)}, u32[]{:S(2)}) copy-start(bf16[1,16,2048]{2,1,0:T(8,128)(2,1)} %param.12) | copy-start | bytes 196612
  0.0 75.2 %collective-permute-start.13 = (bf16[512,2560]{1,0:T(8,128)(2,1)}, bf16[512,2560]{1,0:T(8,128)(2,1)}, u32[]{:S(2)}, u32[]{:S(2)}) collective-permute-start(bf16[512,2560]{1,0:T(8,128)(2,1)} %bitcast.19), channel_id=1, source_target_pairs={{0,2},{2,0},{1,3},{3,1},{4,6},{6,4},{5,7},{7,5},{8,10},{10,8},{9,1... | collective-permute-start | bytes 7864328 | tf_op jit(solution)/shard_map/ppermute | solution.py:229
  4.8 12.5 %collective-permute-start = (bf16[64,2560]{1,0:T(8,128)(2,1)S(1)}, bf16[64,2560]{1,0:T(8,128)(2,1)S(1)}, u32[]{:S(2)}, u32[]{:S(2)}) collective-permute-start(bf16[64,2560]{1,0:T(8,128)(2,1)S(1)} %get-tuple-element.52), channel_id=1, source_target_pairs={{0,4},{4,8},{8,12},{12,0},{1,5},{5,9},{9,13},{13,1},{2,6},{6,10},{... | collective-permute-start | bytes 983048 | tf_op jit(solution)/shard_map/ppermute | solution.py:226
  6.3 16.7 %collective-permute-start.3 = (bf16[64,2560]{1,0:T(8,128)(2,1)S(1)}, bf16[64,2560]{1,0:T(8,128)(2,1)S(1)}, u32[]{:S(2)}, u32[]{:S(2)}) collective-permute-start(bf16[64,2560]{1,0:T(8,128)(2,1)S(1)} %get-tuple-element.52), channel_id=1, source_target_pairs={{0,12},{4,0},{8,4},{12,8},{1,13},{5,1},{9,5},{13,9},{2,14},{6,2},{... | collective-permute-start | bytes 983048 | tf_op jit(solution)/shard_map/ppermute | solution.py:226
  17.2 42.3 %copy-start.3 = (bf16[64,2560]{1,0:T(8,128)(2,1)}, bf16[64,2560]{1,0:T(8,128)(2,1)S(1)}, u32[]{:S(2)}) copy-start(bf16[64,2560]{1,0:T(8,128)(2,1)S(1)} %collective-permute-done.refs_6_.refs_7_) | copy-start | bytes 983044
  17.2 14.9 %collective-permute-start.1 = (bf16[64,2560]{1,0:T(8,128)(2,1)}, bf16[64,2560]{1,0:T(8,128)(2,1)S(1)}, u32[]{:S(2)}, u32[]{:S(2)}) collective-permute-start(bf16[64,2560]{1,0:T(8,128)(2,1)} %get-tuple-element.26), channel_id=1, source_target_pairs={{0,4},{4,8},{8,12},{12,0},{1,5},{5,9},{9,13},{13,1},{2,6},{6,10},{... | collective-permute-start | bytes 983048 | tf_op jit(solution)/shard_map/ppermute | solution.py:226
  23.1 36.5 %copy-start.5 = (bf16[64,2560]{1,0:T(8,128)(2,1)}, bf16[64,2560]{1,0:T(8,128)(2,1)S(1)}, u32[]{:S(2)}) copy-start(bf16[64,2560]{1,0:T(8,128)(2,1)S(1)} %collective-permute-done.3.refs_2_.refs_3_) | copy-start | bytes 983044
  23.1 13.9 %collective-permute-start.4 = (bf16[64,2560]{1,0:T(8,128)(2,1)}, bf16[64,2560]{1,0:T(8,128)(2,1)S(1)}, u32[]{:S(2)}, u32[]{:S(2)}) collective-permute-start(bf16[64,2560]{1,0:T(8,128)(2,1)} %get-tuple-element.26), channel_id=1, source_target_pairs={{0,12},{4,0},{8,4},{12,8},{1,13},{5,1},{9,5},{13,9},{2,14},{6,2},{... | collective-permute-start | bytes 983048 | tf_op jit(solution)/shard_map/ppermute | solution.py:226
  25.9 11.6 %collective-permute-start.9 = (bf16[64,2560]{1,0:T(8,128)(2,1)S(1)}, bf16[64,2560]{1,0:T(8,128)(2,1)S(1)}, u32[]{:S(2)}, u32[]{:S(2)}) collective-permute-start(bf16[64,2560]{1,0:T(8,128)(2,1)S(1)} %collective-permute-done.3.refs_2_.refs_3_), channel_id=1, source_target_pairs={{0,16},{16,0},{1,17},{17,1},{2,18},{18,2},{3,19},{19,3},{4,20},{20... | collective-permute-start | bytes 983048 | tf_op jit(solution)/shard_map/ppermute | solution.py:249
  27.4 12.9 %collective-permute-start.11 = (bf16[64,2560]{1,0:T(8,128)(2,1)S(1)}, bf16[64,2560]{1,0:T(8,128)(2,1)S(1)}, u32[]{:S(2)}, u32[]{:S(2)}) collective-permute-start(bf16[64,2560]{1,0:T(8,128)(2,1)S(1)} %collective-permute-done.refs_6_.refs_7_), channel_id=1, source_target_pairs={{0,16},{16,0},{1,17},{17,1},{2,18},{18,2},{3,19},{19,3},{4,20},{20... | collective-permute-start | bytes 983048 | tf_op jit(solution)/shard_map/ppermute | solution.py:249
  27.9 31.6 %copy-start = (bf16[256,2560]{1,0:T(8,128)(2,1)S(1)}, bf16[256,2560]{1,0:T(8,128)(2,1)}, u32[]{:S(2)}) copy-start(bf16[256,2560]{1,0:T(8,128)(2,1)} %refs_2_.1) | copy-start | bytes 3932164
  36.9 12.5 %collective-permute-start.5 = (bf16[64,2560]{1,0:T(8,128)(2,1)S(1)}, bf16[64,2560]{1,0:T(8,128)(2,1)}, u32[]{:S(2)}, u32[]{:S(2)}) collective-permute-start(bf16[64,2560]{1,0:T(8,128)(2,1)S(1)} %collective-permute-done.1.refs_7_.refs_8_), channel_id=1, source_target_pairs={{0,4},{4,8},{8,12},{12,0},{1,5},{5,9},{9,13},{13,1},{2,6},{6,10},{... | collective-permute-start | bytes 983048 | tf_op jit(solution)/shard_map/ppermute | solution.py:226
  38.2 17.6 %collective-permute-start.10 = (bf16[64,2560]{1,0:T(8,128)(2,1)S(1)}, bf16[64,2560]{1,0:T(8,128)(2,1)S(1)}, u32[]{:S(2)}, u32[]{:S(2)}) collective-permute-start(bf16[64,2560]{1,0:T(8,128)(2,1)S(1)} %collective-permute-done.4.refs_3_.refs_4_), channel_id=1, source_target_pairs={{0,16},{16,0},{1,17},{17,1},{2,18},{18,2},{3,19},{19,3},{4,20},{20... | collective-permute-start | bytes 983048 | tf_op jit(solution)/shard_map/ppermute | solution.py:249
  39.7 16.1 %collective-permute-start.2 = (bf16[64,2560]{1,0:T(8,128)(2,1)S(1)}, bf16[64,2560]{1,0:T(8,128)(2,1)}, u32[]{:S(2)}, u32[]{:S(2)}) collective-permute-start(bf16[64,2560]{1,0:T(8,128)(2,1)S(1)} %collective-permute-done.refs_6_.refs_7_), channel_id=1, source_target_pairs={{0,4},{4,8},{8,12},{12,0},{1,5},{5,9},{9,13},{13,1},{2,6},{6,10},{... | collective-permute-start | bytes 983048 | tf_op jit(solution)/shard_map/ppermute | solution.py:226
  40.3 26.6 %copy-start.16 = (bf16[64,2560]{1,0:T(8,128)(2,1)}, bf16[64,2560]{1,0:T(8,128)(2,1)S(1)}, u32[]{:S(2)}) copy-start(bf16[64,2560]{1,0:T(8,128)(2,1)S(1)} %collective-permute-done.11.refs_8_.refs_9_) | copy-start | bytes 983044
  40.3 17.6 %collective-permute-start.12 = (bf16[64,2560]{1,0:T(8,128)(2,1)S(1)}, bf16[64,2560]{1,0:T(8,128)(2,1)S(1)}, u32[]{:S(2)}, u32[]{:S(2)}) collective-permute-start(bf16[64,2560]{1,0:T(8,128)(2,1)S(1)} %collective-permute-done.1.refs_7_.refs_8_), channel_id=1, source_target_pairs={{0,16},{16,0},{1,17},{17,1},{2,18},{18,2},{3,19},{19,3},{4,20},{20... | collective-permute-start | bytes 983048 | tf_op jit(solution)/shard_map/ppermute | solution.py:249
  55.8 11.1 %collective-permute-start.6 = (bf16[1,2,16,512]{3,2,0,1:T(8,128)(2,1)S(1)}, bf16[1,2,16,512]{3,2,0,1:T(8,128)(2,1)S(1)}, u32[]{:S(2)}, u32[]{:S(2)}) collective-permute-start(bf16[1,2,16,512]{3,2,0,1:T(8,128)(2,1)S(1)} %maximum_bitcast_fusion), channel_id=1, source_target_pairs={{0,12},{4,0},{8,4},{12,8},{1,13},{5,1},{9,5},{13,9},{2,14},{6,2},{... | collective-permute-start | bytes 98312 | tf_op jit(solution)/shard_map/ppermute | solution.py:226
  55.8 11.7 %collective-permute-start.7 = (bf16[1,2,16,512]{3,2,0,1:T(8,128)(2,1)S(1)}, bf16[1,2,16,512]{3,2,0,1:T(8,128)(2,1)S(1)}, u32[]{:S(2)}, u32[]{:S(2)}) collective-permute-start(bf16[1,2,16,512]{3,2,0,1:T(8,128)(2,1)S(1)} %maximum_bitcast_fusion), channel_id=1, source_target_pairs={{0,8},{4,12},{8,0},{12,4},{1,9},{5,13},{9,1},{13,5},{2,10},{6,14},... | collective-permute-start | bytes 98312 | tf_op jit(solution)/shard_map/ppermute | solution.py:226
  55.8 11.7 %collective-permute-start.8 = (bf16[1,2,16,512]{3,2,0,1:T(8,128)(2,1)S(1)}, bf16[1,2,16,512]{3,2,0,1:T(8,128)(2,1)S(1)}, u32[]{:S(2)}, u32[]{:S(2)}) collective-permute-start(bf16[1,2,16,512]{3,2,0,1:T(8,128)(2,1)S(1)} %maximum_bitcast_fusion), channel_id=1, source_target_pairs={{0,4},{4,8},{8,12},{12,0},{1,5},{5,9},{9,13},{13,1},{2,6},{6,10},{... | collective-permute-start | bytes 98312 | tf_op jit(solution)/shard_map/ppermute | solution.py:226
  57.9 11.2 %collective-permute-start.15 = (bf16[64,2560]{1,0:T(8,128)(2,1)}, bf16[64,2560]{1,0:T(8,128)(2,1)}, u32[]{:S(2)}, u32[]{:S(2)}) collective-permute-start(bf16[64,2560]{1,0:T(8,128)(2,1)} %collective-permute-done.5.refs_12_), channel_id=1, source_target_pairs={{0,16},{16,0},{1,17},{17,1},{2,18},{18,2},{3,19},{19,3},{4,20},{20... | collective-permute-start | bytes 983048 | tf_op jit(solution)/shard_map/ppermute | solution.py:249
  67.0 8.2 %collective-permute-start.14 = (bf16[64,2560]{1,0:T(8,128)(2,1)}, bf16[64,2560]{1,0:T(8,128)(2,1)}, u32[]{:S(2)}, u32[]{:S(2)}) collective-permute-start(bf16[64,2560]{1,0:T(8,128)(2,1)} %collective-permute-done.2.refs_11_), channel_id=1, source_target_pairs={{0,16},{16,0},{1,17},{17,1},{2,18},{18,2},{3,19},{19,3},{4,20},{20... | collective-permute-start | bytes 983048 | tf_op jit(solution)/shard_map/ppermute | solution.py:249
  67.6 23.8 %collective-permute-start.16 = (f32[3,512,128]{2,1,0:T(8,128)}, f32[3,512,128]{2,1,0:T(8,128)S(1)}, u32[]{:S(2)}, u32[]{:S(2)}) collective-permute-start(f32[3,512,128]{2,1,0:T(8,128)} %get-tuple-element.39), channel_id=1, source_target_pairs={{0,1},{1,0},{2,3},{3,2},{4,5},{5,4},{6,7},{7,6},{8,9},{9,8},{10,11... | collective-permute-start | bytes 2359304 | tf_op jit(solution)/shard_map/ppermute | solution.py:270
  68.5 22.9 %collective-permute-start.20 = (bf16[576,512]{1,0:T(8,128)(2,1)}, bf16[576,512]{1,0:T(8,128)(2,1)}, u32[]{:S(2)}, u32[]{:S(2)}) collective-permute-start(bf16[576,512]{1,0:T(8,128)(2,1)} %pad_maximum_fusion), channel_id=1, source_target_pairs={{0,2},{2,0},{1,3},{3,1},{4,6},{6,4},{5,7},{7,5},{8,10},{10,8},{9,1... | collective-permute-start | bytes 1769480 | tf_op jit(solution)/shard_map/ppermute | solution.py:303
  90.5 3.1 %collective-permute-start.17 = (f32[2,512,128]{2,1,0:T(8,128)S(1)}, f32[2,512,128]{2,1,0:T(8,128)S(1)}, u32[]{:S(2)}, u32[]{:S(2)}) collective-permute-start(f32[2,512,128]{2,1,0:T(8,128)S(1)} %get-tuple-element.40), channel_id=1, source_target_pairs={{0,1},{1,0},{2,3},{3,2},{4,5},{5,4},{6,7},{7,6},{8,9},{9,8},{10,11... | collective-permute-start | bytes 1572872 | tf_op jit(solution)/shard_map/ppermute | solution.py:270
  90.5 3.0 %collective-permute-start.18 = (f32[2,512,128]{2,1,0:T(8,128)S(1)}, f32[2,512,128]{2,1,0:T(8,128)S(1)}, u32[]{:S(2)}, u32[]{:S(2)}) collective-permute-start(f32[2,512,128]{2,1,0:T(8,128)S(1)} %get-tuple-element.41), channel_id=1, source_target_pairs={{0,1},{1,0},{2,3},{3,2},{4,5},{5,4},{6,7},{7,6},{8,9},{9,8},{10,11... | collective-permute-start | bytes 1572872 | tf_op jit(solution)/shard_map/ppermute | solution.py:270
  91.0 2.5 %collective-permute-start.19 = (f32[1,512,128]{2,1,0:T(8,128)S(1)}, f32[1,512,128]{2,1,0:T(8,128)S(1)}, u32[]{:S(2)}, u32[]{:S(2)}) collective-permute-start(f32[1,512,128]{2,1,0:T(8,128)S(1)} %get-tuple-element.42), channel_id=1, source_target_pairs={{0,1},{1,0},{2,3},{3,2},{4,5},{5,4},{6,7},{7,6},{8,9},{9,8},{10,11... | collective-permute-start | bytes 786440 | tf_op jit(solution)/shard_map/ppermute | solution.py:270
  96.1 5.9 %collective-permute-start.21 = (bf16[1,2,16,640]{3,2,1,0:T(8,128)(2,1)S(1)}, bf16[1,2,16,640]{3,2,1,0:T(8,128)(2,1)S(1)}, u32[]{:S(2)}, u32[]{:S(2)}) collective-permute-start(bf16[1,2,16,640]{3,2,1,0:T(8,128)(2,1)S(1)} %get-tuple-element.55), channel_id=1, source_target_pairs={{0,4},{4,8},{8,12},{12,0},{1,5},{5,9},{9,13},{13,1},{2,6},{6,10},{... | collective-permute-start | bytes 122888 | tf_op jit(solution)/shard_map/ppermute | solution.py:226
  97.5 5.7 %collective-permute-start.22 = (bf16[1,2,16,640]{3,2,1,0:T(8,128)(2,1)S(1)}, bf16[1,2,16,640]{3,2,1,0:T(8,128)(2,1)S(1)}, u32[]{:S(2)}, u32[]{:S(2)}) collective-permute-start(bf16[1,2,16,640]{3,2,1,0:T(8,128)(2,1)S(1)} %get-tuple-element.54), channel_id=1, source_target_pairs={{0,8},{4,12},{8,0},{12,4},{1,9},{5,13},{9,1},{13,5},{2,10},{6,14},... | collective-permute-start | bytes 122888 | tf_op jit(solution)/shard_map/ppermute | solution.py:226
  99.0 4.3 %collective-permute-start.23 = (bf16[1,2,16,640]{3,2,1,0:T(8,128)(2,1)S(1)}, bf16[1,2,16,640]{3,2,1,0:T(8,128)(2,1)S(1)}, u32[]{:S(2)}, u32[]{:S(2)}) collective-permute-start(bf16[1,2,16,640]{3,2,1,0:T(8,128)(2,1)S(1)} %get-tuple-element.53), channel_id=1, source_target_pairs={{0,12},{4,0},{8,4},{12,8},{1,13},{5,1},{9,5},{13,9},{2,14},{6,2},{... | collective-permute-start | bytes 122888 | tf_op jit(solution)/shard_map/ppermute | solution.py:226
  103.6 3.9 %collective-permute-start.25 = (bf16[1,16,512]{2,1,0:T(8,128)(2,1)S(1)}, bf16[1,16,512]{2,1,0:T(8,128)(2,1)S(1)}, u32[]{:S(2)}, u32[]{:S(2)}) collective-permute-start(bf16[1,16,512]{2,1,0:T(8,128)(2,1)S(1)} %get-tuple-element.67), channel_id=1, source_target_pairs={{0,2},{2,0},{1,3},{3,1},{4,6},{6,4},{5,7},{7,5},{8,10},{10,8},{9,1... | collective-permute-start | bytes 49160 | tf_op jit(solution)/shard_map/ppermute | solution.py:335
  104.2 3.3 %collective-permute-start.26 = (bf16[1,16,512]{2,1,0:T(8,128)(2,1)S(1)}, bf16[1,16,512]{2,1,0:T(8,128)(2,1)S(1)}, u32[]{:S(2)}, u32[]{:S(2)}) collective-permute-start(bf16[1,16,512]{2,1,0:T(8,128)(2,1)S(1)} %get-tuple-element.67), channel_id=1, source_target_pairs={{0,3},{3,0},{1,2},{2,1},{4,7},{7,4},{5,6},{6,5},{8,11},{11,8},{9,1... | collective-permute-start | bytes 49160 | tf_op jit(solution)/shard_map/ppermute | solution.py:336
  104.3 2.4 %collective-permute-start.24 = (bf16[1,16,512]{2,1,0:T(8,128)(2,1)S(1)}, bf16[1,16,512]{2,1,0:T(8,128)(2,1)S(1)}, u32[]{:S(2)}, u32[]{:S(2)}) collective-permute-start(bf16[1,16,512]{2,1,0:T(8,128)(2,1)S(1)} %get-tuple-element.68.mine_ref), channel_id=1, source_target_pairs={{0,1},{1,0},{2,3},{3,2},{4,5},{5,4},{6,7},{7,6},{8,9},{9,8},{10,11... | collective-permute-start | bytes 49160 | tf_op jit(solution)/shard_map/ppermute | solution.py:334
  (21 other events, 127.0 us)

commit v4 on v3

--- a/solution.py
+++ b/solution.py
@@ -1,4 +1,5 @@
 import functools
+import math
 
 import jax
 import jax.numpy as jnp
@@ -8,9 +9,9 @@
 from jax.sharding import Mesh, PartitionSpec as P
 
 HEAD_DIM = 64
-EMPTY = -(2.0**127)
-CHUNKS = 2
-VMEM_LIMIT = 40 * 1024 * 1024
+EMPTY = -3e38
+FIRST_EIGHTHS = 4
+VMEM_LIMIT = 22 * 1024 * 1024
 SWAP = [(0, 1), (1, 0)]
 CROSS = [(0, 3), (3, 0), (1, 2), (2, 1)]
 
@@ -31,11 +32,11 @@
     half = keep_ref.shape[2]
     for at, (rows_of, blocks_of) in enumerate(jobs):
         if len(blocks_of) == 1:
-            whole = refs[blocks_of[0]]
+            whole = refs[blocks_of[0][0]]
             keep = whole[pl.ds(pl.multiple_of(core * half, half), half), :]
             send = whole[pl.ds(pl.multiple_of((1 - core) * half, half), half), :]
         else:
-            parts = [refs[block][...] for block in blocks_of]
+            parts = [refs[block][:length] for block, length in blocks_of]
             first, second = (
                 jnp.concatenate(part, axis=0) for part in (parts[: len(parts) // 2], parts[len(parts) // 2 :])
             )
@@ -53,7 +54,7 @@
 
 
 def attend_kernel(place_ref, spot_ref, query_ref, *refs, pieces):
-    *refs, own_ref, partner_ref, packed_ref, key_ref, out_ref = refs
+    *refs, own_ref, partner_ref, out_ref, key_ref = refs
     residuals = own_ref, partner_ref
     partner_queries = own_ref.shape[0]
     query_len, held = query_ref.shape[1:]
@@ -73,11 +74,11 @@
         keep, other = (refs[summand].at[piece] for summand, piece in (kept, sent))
         residual = residuals[source]
         span = keep.shape[1]
-        lanes = pl.ds(pl.multiple_of(spot_ref[spot] * span, span), span)
+        lanes, given = (pl.ds(pl.multiple_of(spot_ref[of, spot], 128), span) for of in (1, source))
         for block in range(blocks):
             rows = slice(block * block_len, (block + 1) * block_len)
             key_ref[source * blocks + block, :, lanes] = (
-                residual[rows, lanes].astype(jnp.float32) + (keep[rows, :] + other[rows, :])
+                residual[rows, given].astype(jnp.float32) + (keep[rows, :] + other[rows, :])
             ).astype(jnp.bfloat16)
     places, scores, tops = [], [], []
     for at in range(key_ref.shape[0]):
@@ -110,13 +111,6 @@
         out_ref[place, :, held:] = jnp.where(
             ext == 0, top_row, jnp.where(ext == 1, before + total_row, 0.0)
         )
-    packed_ref[:, :, :held] = out_ref[:, :, :held].astype(jnp.bfloat16)
-    rest = out_ref[:, 0:2, held:]
-    for part in range(3):
-        rounded = rest.astype(jnp.bfloat16)
-        rest = rest - rounded.astype(jnp.float32)
-        packed_ref[:, 2 * part : 2 * part + 2, held:] = rounded
-    packed_ref[:, 6:, held:] = jnp.zeros_like(packed_ref[:, 6:, held:])
 
 
 def merge_kernel(*refs):
@@ -134,8 +128,7 @@
         return start
 
     def row_of(part, at, slot, row):
-        packed = part[at, slot, :, held:].astype(jnp.float32)
-        return packed[row : row + 1] + packed[row + 2 : row + 3] + packed[row + 4 : row + 5]
+        return part[at, slot, row : row + 1, held:]
 
     for slot in range(out_ref.shape[0]):
         def top_step(part, at, top):
@@ -148,7 +141,7 @@
             share = jnp.exp(row_of(part, at, slot, 0) - top) / total
             column = jnp.sum(jnp.where(square, share, 0.0), axis=1, keepdims=True)
             spread = head_pick(jnp.broadcast_to(column, (tall, held)), query_len)
-            return blend + spread * part[at, slot, :, :held].astype(jnp.float32)
+            return blend + spread * part[at, slot, :, :held]
 
         top = over(jnp.full((1, tall), EMPTY, jnp.float32), top_step)
         total = over(jnp.zeros((1, tall), jnp.float32), total_step)
@@ -178,9 +171,8 @@
     return [pl.BlockSpec(memory_space=pltpu.SMEM)] * count
 
 
-def project(flags, operands, jobs, sends, flops, name):
+def project(flags, operands, jobs, sends, half, flops, name):
     rows, units = operands[0].shape
-    half = operands[-1].shape[0] * CHUNKS
     shapes = [jax.ShapeDtypeStruct((count, rows, half), jnp.float32) for count in [len(jobs)] + sends]
     return pl.pallas_call(
         functools.partial(project_kernel, jobs=jobs, sends=sends),
@@ -195,6 +187,17 @@
 
 def after(array, earlier):
     return lax.optimization_barrier((array, *earlier))[0] if earlier else array
+
+
+def with_rows(array, units):
+    flat = array.reshape(-1, array.shape[-1])
+    spread = jnp.concatenate([flat[at : at + 8] for at in range(0, flat.shape[0], 8)], axis=1)
+    return jnp.pad(spread, ((0, 0), (0, units - spread.shape[1])))
+
+
+def from_rows(spread, shape):
+    pieces = [spread[:, at : at + shape[-1]] for at in range(0, math.prod(shape) // 8, shape[-1])]
+    return jnp.concatenate(pieces, axis=0).reshape(shape)
 
 
 def body(hidden_states, passage_states, down_weight, block_question, question_owner, decoder_states):
@@ -229,54 +232,63 @@
     partner_hidden = lax.ppermute(hidden, "side", SWAP)
     queries = jnp.concatenate([features(decoder_states, side), features(decoder_states, 1 - side)], axis=0)[None]
     passages = passage_states.reshape(rows, width)
-    own_residual = features(passages, side)
     leaving = features(passages, 1 - side)
 
     if lined:
         half = shard // 2
-        chunk = half // CHUNKS
+        lengths = [half * FIRST_EIGHTHS // 8, half - half * FIRST_EIGHTHS // 8]
         sent = [
-            lax.dynamic_slice_in_dim(down_weight, group * half + at * chunk, chunk, axis=0) for at in range(CHUNKS)
+            lax.dynamic_slice_in_dim(down_weight, group * half + first, length, axis=0)
+            for first, length in zip((0, lengths[0]), lengths)
         ]
-        below, above, opposite = [], [], []
-        for at in range(CHUNKS):
+        sent[1] = jnp.concatenate([sent[1], with_rows(queries, units)], axis=0)
+        below, above = [], []
+        for at in range(2):
             below.append(shifted(after(sent[at], below[-1:]), 1))
             above.append(shifted(after(sent[at], above[-1:]), -1))
-        opposite.append(shifted(after(below[0], below[-1:]), 1))
-        opposite.append(shifted(after(below[1], above[-1:]), 1))
+        opposite = [jnp.concatenate([shifted(after(below[0], below[1:]), 1), shifted(below[1], 1)], axis=0)]
+        around = [from_rows(piece[-1][-8:], queries.shape) for piece in (above, opposite, below)]
+        queries = jnp.concatenate([queries] + around, axis=0)
         swapped = []
         for at, piece in enumerate([below[0], above[0], below[1], above[1]] + opposite):
             swapped.append(lax.ppermute(after(piece, swapped[max(at - 2, 0) : max(at - 1, 0)]), "groups", SWAP))
         weights = [down_weight] + above + swapped[1:4:2] + below + swapped[0:4:2] + opposite + swapped[4:]
-        queries = after(queries, opposite)
-        queries = jnp.concatenate([queries] + [shifted(queries, -ahead) for ahead in range(1, highs)], axis=0)
-        flags = after(jnp.stack([core, (group == core).astype(core.dtype)]), opposite)
-        blocks_of = [(0,)] + [tuple(range(1 + at * 2 * CHUNKS, 1 + (at + 1) * 2 * CHUNKS)) for at in range(3)]
+        flags = jnp.stack([core, (group == core).astype(core.dtype)])
+        blocks_of = [[(2, shard)], list(zip(range(3, 7), 2 * lengths)), list(zip(range(7, 11), 2 * lengths))]
         spots = lax.rem(high + jnp.array([0, 1, 3, 2], jnp.int32), highs)
-
-        def jobs_of(rows_of, chosen, count):
-            return [(rows_of, tuple(at + count for at in blocks_of[one])) for one in chosen]
-
-        kept, *away = project(flags, [hidden] + weights[: 1 + 4 * CHUNKS], jobs_of(0, (0, 1, 2), 1), [3], 12 * rows * half * units, "project_own")
-        flags, kept, away = lax.optimization_barrier((flags, kept, away))
+        spots = jnp.stack([(spots * 2 + side) * stride + core * span, spots * span])
+        own_residual = passages
+
+        kept, *away = project(
+            flags,
+            [hidden, partner_hidden] + weights[:9],
+            [(source, blocks_of[at]) for source in range(2) for at in range(3)],
+            [2, 2, 2],
+            half,
+            24 * rows * half * units,
+            "project_near",
+        )
+        flags, kept, *away = lax.optimization_barrier((flags, kept, *away))
         late_kept, *late_away = project(
             flags,
-            [hidden, partner_hidden] + weights,
-            jobs_of(0, (3,), 2) + jobs_of(1, range(4), 2),
-            [2, 2, 1],
+            [hidden, partner_hidden] + weights[9:],
+            [(source, [(2, half), (3, half)]) for source in range(2)],
+            [2],
+            half,
             1,
-            "project_rest",
+            "project_far",
         )
         others = [lax.ppermute(piece, "mp", SWAP) for piece in away + late_away]
         summands = [kept, late_kept] + others
-        pieces = [(0, (0, at), (2, at), at) for at in range(3)] + [(0, (1, 0), (3, 0), 3)]
-        pieces += [(1, (1, 1 + at), (3 + (1 + at) // 2, (1 + at) % 2), at) for at in range(4)]
+        pieces = [(at // 3, (0, at), (2 + at // 2, at % 2), at % 3) for at in range(6)]
+        pieces += [(source, (1, source), (5, source), 3) for source in range(2)]
         origin = high
     else:
         queries = lax.all_gather(queries, ("high", "low"), axis=0, tiled=True)
         weight = lax.all_gather(down_weight, ("high", "low"), axis=0, tiled=True)
         weight = jnp.where(core == 0, weight, jnp.roll(weight, held, axis=0))
-        spots = jnp.zeros((1,), jnp.int32)
+        spots = jnp.zeros((2, 1), jnp.int32)
+        own_residual = features(passages, side)
         summands, pieces = [], []
         for source, flat in enumerate((hidden, partner_hidden)):
             kept, away = (
@@ -305,13 +317,10 @@
     operands = summands + [own_residual, partner]
     partials = pl.pallas_call(
         functools.partial(attend_kernel, pieces=pieces),
-        out_shape=jax.ShapeDtypeStruct(packed, jnp.bfloat16),
+        out_shape=jax.ShapeDtypeStruct(packed, jnp.float32),
         in_specs=in_smem(2) + in_vmem(1 + len(operands)),
         out_specs=pl.BlockSpec(memory_space=pltpu.VMEM),
-        scratch_shapes=[
-            pltpu.VMEM((2 * blocks, block_len, held), jnp.bfloat16),
-            pltpu.VMEM(packed, jnp.float32),
-        ],
+        scratch_shapes=[pltpu.VMEM((2 * blocks, block_len, held), jnp.bfloat16)],
         compiler_params=pltpu.CompilerParams(vmem_limit_bytes=VMEM_LIMIT),
         name="attend",
     )(places, spots, queries[:, 0], *operands)

time: 109 us -> 97.4 us (0.89)
  local copies, waits for them, and re-layouts: 17.5 us -> 2.45 us
  waiting for transfers between devices: 48.4 us -> 51.7 us
    unnamed x55 -> x13, local copies, waits for them, and re-layouts: 14 us -> 0.05 us
    ppermute x1, waiting for transfers between devices: 0.01 us -> 5.38 us  [body(): partner_hidden = lax.ppermute(hidden, 'side', SWAP)]
    ppermute x12 -> x9, waiting for transfers between devices: 38.4 us -> 33.1 us  [shifted(): lax.ppermute(array, 'high', [(at, (at + shift) % highs) for at in range(h...]
    ppermute x6 -> x5, waiting for transfers between devices: 6.06 us -> 9.02 us  [body(): lax.ppermute(after(piece, swapped[max(at - 2, 0):max(at - 1, 0)]), 'group...]
    ppermute x1, starting transfers between devices: 2.94 us -> 1.65 us  [body(): partner_hidden = lax.ppermute(hidden, 'side', SWAP)]
    ppermute x12 -> x9, starting transfers between devices: 15.4 us -> 16.5 us  [shifted(): lax.ppermute(array, 'high', [(at, (at + shift) % highs) for at in range(h...]
    ppermute x6 -> x5, starting transfers between devices: 6.3 us -> 6.24 us  [body(): lax.ppermute(after(piece, swapped[max(at - 2, 0):max(at - 1, 0)]), 'group...]
  transfers between devices with their start and end apart: 27 -> 23, of which waited for: 13 -> 15; matrix products, arithmetic and copies ran while one was open for 4% -> 2% of each run, Pallas kernels for 9% -> 10%
where the time goes in v4:
time: 97.4 us; the launch traced here: 97.2 us
  waiting for transfers between devices  51.7 us (53%)
  starting transfers between devices  28.8 us (30%)
  Pallas kernels  12.7 us (13%)
  local copies, waits for them, and re-layouts  2.45 us (3%)
  other arithmetic  1.23 us (1%)
    ppermute x9, waiting for transfers between devices, shifted(): lax.ppermute(array, 'high', [(at, (at + shift) % highs) for at in range(h...  33.1 us
    ppermute x9, starting transfers between devices, shifted(): lax.ppermute(array, 'high', [(at, (at + shift) % highs) for at in range(h...  16.5 us
    pallas_call x2, Pallas kernels, project(): pl.pallas_call(functools.partial(project_kernel, jobs=jobs, sends=sends),...  9.32 us
    ppermute x5, waiting for transfers between devices, body(): lax.ppermute(after(piece, swapped[max(at - 2, 0):max(at - 1, 0)]), 'group...  9.02 us
    ppermute x5, starting transfers between devices, body(): lax.ppermute(after(piece, swapped[max(at - 2, 0):max(at - 1, 0)]), 'group...  6.24 us
    ppermute x1, waiting for transfers between devices, body(): partner_hidden = lax.ppermute(hidden, 'side', SWAP)  5.38 us
    pallas_call x1, Pallas kernels, body(): pl.pallas_call(functools.partial(attend_kernel, pieces=pieces), out_shape...  1.99 us
  transfers between devices with their start and end apart: 23, of which 15 were waited for; matrix products, arithmetic and copies ran while one was open for 2% of the time, Pallas kernels for 10%

profile of v4, /device:TPU:0, one launch (start us, length us, event | category | flops | bytes accessed | tf_op | source)
XLA Modules:
  0.0 97.2 jit_solution(17970968937301541308)
XLA Ops:
  0.0 1.3 %constant_dynamic-slice_fusion.4 = (bf16[64,2560]{1,0:T(8,128)(2,1)S(1)}, bf16[64,2560]{1,0:T(8,128)(2,1)S(1)}) fusion(bf16[256,2560]{1,0:T(8,128)(2,1)} %refs_2_.1, s32[]{:T(128)S(6)} %select_n.73, s32[]{:T(128)S(6)} %select_n.72), kind=kLoop, calls=%fused_computation.28 | loop fusion | bytes 1310728 | tf_op jit(solution)/shard_map/dynamic_slice | solution.py:241
  1.3 3.1 %collective-permute-start.2 = (bf16[64,2560]{1,0:T(8,128)(2,1)S(1)}, bf16[64,2560]{1,0:T(8,128)(2,1)S(1)}, u32[]{:S(2)}, u32[]{:S(2)}) collective-permute-start(bf16[64,2560]{1,0:T(8,128)(2,1)S(1)} %get-tuple-element.45), channel_id=1, source_target_pairs={{0,4},{4,8},{8,12},{12,0},{1,5},{5,9},{9,13},{13,1},{2,6},{6,10},{... | collective-permute-start | bytes 983048 | tf_op jit(solution)/shard_map/ppermute | solution.py:229
  4.4 2.1 %collective-permute-start = (bf16[64,2560]{1,0:T(8,128)(2,1)S(1)}, bf16[64,2560]{1,0:T(8,128)(2,1)S(1)}, u32[]{:S(2)}, u32[]{:S(2)}) collective-permute-start(bf16[64,2560]{1,0:T(8,128)(2,1)S(1)} %get-tuple-element.45), channel_id=1, source_target_pairs={{0,12},{4,0},{8,4},{12,8},{1,13},{5,1},{9,5},{13,9},{2,14},{6,2},{... | collective-permute-start | bytes 983048 | tf_op jit(solution)/shard_map/ppermute | solution.py:229
  6.5 1.6 %collective-permute-start.5 = (bf16[512,2560]{1,0:T(8,128)(2,1)}, bf16[512,2560]{1,0:T(8,128)(2,1)}, u32[]{:S(2)}, u32[]{:S(2)}) collective-permute-start(bf16[512,2560]{1,0:T(8,128)(2,1)} %bitcast.29), channel_id=1, source_target_pairs={{0,2},{2,0},{1,3},{3,1},{4,6},{6,4},{5,7},{7,5},{8,10},{10,8},{9,1... | collective-permute-start | bytes 7864328 | tf_op jit(solution)/shard_map/ppermute | solution.py:232
  8.2 0.8 constant_dynamic-slice_fusion.13
  9.9 5.1 %collective-permute-done.2.refs_7_ = bf16[64,2560]{1,0:T(8,128)(2,1)S(1)} collective-permute-done((bf16[64,2560]{1,0:T(8,128)(2,1)S(1)}, bf16[64,2560]{1,0:T(8,128)(2,1)S(1)}, u32[]{:S(2)}, u32[]{:S(2)}) %collective-permute-start.2) | collective-permute-done | bytes 327712 | tf_op jit(solution)/shard_map/ppermute | solution.py:229
  15.0 5.8 %collective-permute-done.refs_3_ = bf16[64,2560]{1,0:T(8,128)(2,1)S(1)} collective-permute-done((bf16[64,2560]{1,0:T(8,128)(2,1)S(1)}, bf16[64,2560]{1,0:T(8,128)(2,1)S(1)}, u32[]{:S(2)}, u32[]{:S(2)}) %collective-permute-start) | collective-permute-done | bytes 327712 | tf_op jit(solution)/shard_map/ppermute | solution.py:229
  20.8 3.1 %collective-permute-start.1 = (bf16[72,2560]{1,0:T(8,128)(2,1)}, bf16[72,2560]{1,0:T(8,128)(2,1)S(1)}, u32[]{:S(2)}, u32[]{:S(2)}) collective-permute-start(bf16[72,2560]{1,0:T(8,128)(2,1)} %pad_maximum_fusion.1), channel_id=1, source_target_pairs={{0,12},{4,0},{8,4},{12,8},{1,13},{5,1},{9,5},{13,9},{2,14},{6,2},{... | collective-permute-start | bytes 1105928 | tf_op jit(solution)/shard_map/ppermute | solution.py:229
  23.9 1.5 %collective-permute-start.6 = (bf16[64,2560]{1,0:T(8,128)(2,1)S(1)}, bf16[64,2560]{1,0:T(8,128)(2,1)S(1)}, u32[]{:S(2)}, u32[]{:S(2)}) collective-permute-start(bf16[64,2560]{1,0:T(8,128)(2,1)S(1)} %collective-permute-done.refs_3_), channel_id=1, source_target_pairs={{0,16},{16,0},{1,17},{17,1},{2,18},{18,2},{3,19},{19,3},{4,20},{20... | collective-permute-start | bytes 983048 | tf_op jit(solution)/shard_map/ppermute | solution.py:254
  26.2 8.4 %collective-permute-done.6.refs_5_ = bf16[64,2560]{1,0:T(8,128)(2,1)S(1)} collective-permute-done((bf16[64,2560]{1,0:T(8,128)(2,1)S(1)}, bf16[64,2560]{1,0:T(8,128)(2,1)S(1)}, u32[]{:S(2)}, u32[]{:S(2)}) %collective-permute-start.6) | collective-permute-done | bytes 327712 | tf_op jit(solution)/shard_map/ppermute | solution.py:254
  34.6 2.4 %collective-permute-done.1.refs_4_ = bf16[72,2560]{1,0:T(8,128)(2,1)S(1)} collective-permute-done((bf16[72,2560]{1,0:T(8,128)(2,1)}, bf16[72,2560]{1,0:T(8,128)(2,1)S(1)}, u32[]{:S(2)}, u32[]{:S(2)}) %collective-permute-start.1) | collective-permute-done | bytes 368672 | tf_op jit(solution)/shard_map/ppermute | solution.py:229
  37.0 1.5 %collective-permute-start.7 = (bf16[72,2560]{1,0:T(8,128)(2,1)S(1)}, bf16[72,2560]{1,0:T(8,128)(2,1)S(1)}, u32[]{:S(2)}, u32[]{:S(2)}) collective-permute-start(bf16[72,2560]{1,0:T(8,128)(2,1)S(1)} %collective-permute-done.1.refs_4_), channel_id=1, source_target_pairs={{0,16},{16,0},{1,17},{17,1},{2,18},{18,2},{3,19},{19,3},{4,20},{20... | collective-permute-start | bytes 1105928 | tf_op jit(solution)/shard_map/ppermute | solution.py:254
  38.5 1.1 %collective-permute-start.9 = (bf16[72,2560]{1,0:T(8,128)(2,1)S(1)}, bf16[72,2560]{1,0:T(8,128)(2,1)S(1)}, u32[]{:S(2)}, u32[]{:S(2)}) collective-permute-start(bf16[72,2560]{1,0:T(8,128)(2,1)S(1)} %collective-permute-done.3.refs_8_), channel_id=1, source_target_pairs={{0,16},{16,0},{1,17},{17,1},{2,18},{18,2},{3,19},{19,3},{4,20},{20... | collective-permute-start | bytes 1105928 | tf_op jit(solution)/shard_map/ppermute | solution.py:254
  39.6 1.4 %collective-permute-start.10 = (bf16[64,2560]{1,0:T(8,128)(2,1)S(1)}, bf16[64,2560]{1,0:T(8,128)(2,1)S(1)}, u32[]{:S(2)}, u32[]{:S(2)}) collective-permute-start(bf16[64,2560]{1,0:T(8,128)(2,1)S(1)} %collective-permute-done.2.refs_7_), channel_id=1, source_target_pairs={{0,4},{4,8},{8,12},{12,0},{1,5},{5,9},{9,13},{13,1},{2,6},{6,10},{... | collective-permute-start | bytes 983048 | tf_op jit(solution)/shard_map/ppermute | solution.py:229
  41.0 3.0 %collective-permute-start.4 = (bf16[72,2560]{1,0:T(8,128)(2,1)S(1)}, bf16[72,2560]{1,0:T(8,128)(2,1)S(1)}, u32[]{:S(2)}, u32[]{:S(2)}) collective-permute-start(bf16[72,2560]{1,0:T(8,128)(2,1)S(1)} %collective-permute-done.3.refs_8_), channel_id=1, source_target_pairs={{0,4},{4,8},{8,12},{12,0},{1,5},{5,9},{9,13},{13,1},{2,6},{6,10},{... | collective-permute-start | bytes 1105928 | tf_op jit(solution)/shard_map/ppermute | solution.py:229
  44.0 8.0 %collective-permute-done.10 = bf16[64,2560]{1,0:T(8,128)(2,1)S(1)} collective-permute-done((bf16[64,2560]{1,0:T(8,128)(2,1)S(1)}, bf16[64,2560]{1,0:T(8,128)(2,1)S(1)}, u32[]{:S(2)}, u32[]{:S(2)}) %collective-permute-start.10) | collective-permute-done | bytes 327712 | tf_op jit(solution)/shard_map/ppermute | solution.py:229
  52.1 5.8 %collective-permute-done.4 = bf16[72,2560]{1,0:T(8,128)(2,1)S(1)} collective-permute-done((bf16[72,2560]{1,0:T(8,128)(2,1)S(1)}, bf16[72,2560]{1,0:T(8,128)(2,1)S(1)}, u32[]{:S(2)}, u32[]{:S(2)}) %collective-permute-start.4) | collective-permute-done | bytes 368672 | tf_op jit(solution)/shard_map/ppermute | solution.py:229
  57.9 1.6 %collective-permute-start.11 = (bf16[136,2560]{1,0:T(8,128)(2,1)S(1)}, bf16[136,2560]{1,0:T(8,128)(2,1)S(1)}, u32[]{:S(2)}, u32[]{:S(2)}) collective-permute-start(bf16[136,2560]{1,0:T(8,128)(2,1)S(1)} %constant_dynamic-update-slice_fusion.refs_2_), channel_id=1, source_target_pairs={{0,16},{16,0},{1,17},{17,1},{2,18},{18,2},{3,19},{19,3},{4,20},{20... | collective-permute-start | bytes 2088968 | tf_op jit(solution)/shard_map/ppermute | solution.py:254
  59.6 1.6 %collective-permute-start.16 = (bf16[576,512]{1,0:T(8,128)(2,1)S(1)}, bf16[576,512]{1,0:T(8,128)(2,1)S(1)}, u32[]{:S(2)}, u32[]{:S(2)}) collective-permute-start(bf16[576,512]{1,0:T(8,128)(2,1)S(1)} %pad_maximum_fusion), channel_id=1, source_target_pairs={{0,2},{2,0},{1,3},{3,1},{4,6},{6,4},{5,7},{7,5},{8,10},{10,8},{9,1... | collective-permute-start | bytes 1769480 | tf_op jit(solution)/shard_map/ppermute | solution.py:315
  61.2 5.4 %collective-permute-done.5.refs_1_ = bf16[512,2560]{1,0:T(8,128)(2,1)} collective-permute-done((bf16[512,2560]{1,0:T(8,128)(2,1)}, bf16[512,2560]{1,0:T(8,128)(2,1)}, u32[]{:S(2)}, u32[]{:S(2)}) %collective-permute-start.5) | collective-permute-done | bytes 2621472 | tf_op jit(solution)/shard_map/ppermute | solution.py:232
  66.6 6.0 %project_near.1 = (f32[6,512,128]{2,1,0:T(8,128)S(1)}, f32[2,512,128]{2,1,0:T(8,128)S(1)}, f32[2,512,128]{2,1,0:T(8,128)S(1)}, f32[2,512,128]{2,1,0:T(8,128)S(1)}) custom-call(s32[2]{0:T(128)S(1)} %pad_add_fusion.3.flag_ref, bf16[512,2560]{1,0:T(8,128)(2,1)S(1)} %bitcast.30, bf16[512,2560]{1,0:T(8,128)(2,1)} %collective-permute-done.5.refs_1_, ...), custom_call_target="tpu_custom_call" | custom-call | flops 4026531840 | bytes 1 | tf_op jit(solution)/shard_map/project_near/pallas_call | solution.py:177
  73.9 3.3 %project_far.1 = (f32[2,512,128]{2,1,0:T(8,128)S(1)}, f32[2,512,128]{2,1,0:T(8,128)S(1)}) custom-call(s32[2]{0:T(128)S(1)} %pad_add_fusion.3.flag_ref, bf16[512,2560]{1,0:T(8,128)(2,1)S(1)} %bitcast.31, bf16[512,2560]{1,0:T(8,128)(2,1)} %collective-permute-done.5.refs_1_, bf16[136,2560]{1,0:T(8,128)(2,1)S(1)} %constant_dynamic-update-slice_fusion.refs_2_, ...), custom_call_target="tpu_custom_call" | custom-call | flops 1 | bytes 1 | tf_op jit(solution)/shard_map/project_far/pallas_call | solution.py:177
  77.6 1.5 %collective-permute-done.15.refs_5_ = f32[2,512,128]{2,1,0:T(8,128)S(1)} collective-permute-done((f32[2,512,128]{2,1,0:T(8,128)S(1)}, f32[2,512,128]{2,1,0:T(8,128)S(1)}, u32[]{:S(2)}, u32[]{:S(2)}) %collective-permute-start.15) | collective-permute-done | bytes 524320 | tf_op jit(solution)/shard_map/ppermute | solution.py:281
  79.2 2.0 %attend.1 = f32[8,16,640]{2,1,0:T(8,128)S(1)} custom-call(s32[4]{0:T(128)S(1)} %pad_add_fusion.2.place_ref, s32[2,4]{1,0:T(2,128)S(1)} %pad_add_fusion.spot_ref, bf16[4,16,512]{2,1,0:T(8,128)(2,1)S(1)} %get-tuple-element.64.query_ref, f32[6,512,128]{2,1,0:T(8,128)S(1)} %get-tuple-element.30.refs_0_, f32[2,512,128]{2,1,0:T(8,128)S(1)} %get-tuple-element.34.refs_1_, ...), custom_call_target="tpu_custom_call" | custom-call | tf_op jit(solution)/shard_map/attend/pallas_call | solution.py:318
  81.3 2.0 %collective-permute-start.18 = (f32[1,2,16,640]{3,2,1,0:T(8,128)S(1)}, f32[1,2,16,640]{3,2,1,0:T(8,128)S(1)}, u32[]{:S(2)}, u32[]{:S(2)}) collective-permute-start(f32[1,2,16,640]{3,2,1,0:T(8,128)S(1)} %get-tuple-element.60), channel_id=1, source_target_pairs={{0,8},{4,12},{8,0},{12,4},{1,9},{5,13},{9,1},{13,5},{2,10},{6,14},... | collective-permute-start | bytes 245768 | tf_op jit(solution)/shard_map/ppermute | solution.py:229
  83.2 1.9 %collective-permute-start.19 = (f32[1,2,16,640]{3,2,1,0:T(8,128)S(1)}, f32[1,2,16,640]{3,2,1,0:T(8,128)S(1)}, u32[]{:S(2)}, u32[]{:S(2)}) collective-permute-start(f32[1,2,16,640]{3,2,1,0:T(8,128)S(1)} %get-tuple-element.59), channel_id=1, source_target_pairs={{0,12},{4,0},{8,4},{12,8},{1,13},{5,1},{9,5},{13,9},{2,14},{6,2},{... | collective-permute-start | bytes 245768 | tf_op jit(solution)/shard_map/ppermute | solution.py:229
  85.1 3.4 %collective-permute-done.17.refs_1_ = f32[1,2,16,640]{3,2,1,0:T(8,128)S(1)} collective-permute-done((f32[1,2,16,640]{3,2,1,0:T(8,128)S(1)}, f32[1,2,16,640]{3,2,1,0:T(8,128)S(1)}, u32[]{:S(2)}, u32[]{:S(2)}) %collective-permute-start.17) | collective-permute-done | bytes 81952 | tf_op jit(solution)/shard_map/ppermute | solution.py:229
  88.5 2.6 %collective-permute-done.18.refs_2_ = f32[1,2,16,640]{3,2,1,0:T(8,128)S(1)} collective-permute-done((f32[1,2,16,640]{3,2,1,0:T(8,128)S(1)}, f32[1,2,16,640]{3,2,1,0:T(8,128)S(1)}, u32[]{:S(2)}, u32[]{:S(2)}) %collective-permute-start.18) | collective-permute-done | bytes 81952 | tf_op jit(solution)/shard_map/ppermute | solution.py:229
  91.3 1.5 %collective-permute-start.21 = (bf16[1,16,512]{2,1,0:T(8,128)(2,1)S(1)}, bf16[1,16,512]{2,1,0:T(8,128)(2,1)S(1)}, u32[]{:S(2)}, u32[]{:S(2)}) collective-permute-start(bf16[1,16,512]{2,1,0:T(8,128)(2,1)S(1)} %get-tuple-element.73), channel_id=1, source_target_pairs={{0,2},{2,0},{1,3},{3,1},{4,6},{6,4},{5,7},{7,5},{8,10},{10,8},{9,1... | collective-permute-start | bytes 49160 | tf_op jit(solution)/shard_map/ppermute | solution.py:344
  93.6 0.8 collective-permute-done.20.core_ref
  95.1 0.9 collective-permute-done.22.both_ref
  96.0 1.2 %assemble.1 = bf16[1,16,2048]{2,1,0:T(8,128)(2,1)} custom-call(s32[2]{0:T(128)S(1)} %pad_add_fusion.1.flag_ref, bf16[1,16,512]{2,1,0:T(8,128)(2,1)S(1)} %get-tuple-element.74.mine_ref, bf16[1,16,512]{2,1,0:T(8,128)(2,1)S(1)} %collective-permute-done.20.core_ref, bf16[1,16,512]{2,1,0:T(8,128)(2,1)S(1)} %collective-permute-done.21.side_ref, ...), custom_call_target="tpu_custom_call" | custom-call | tf_op jit(solution)/shard_map/assemble/pallas_call | solution.py:352
  (61 shorter events, 5.5 us)
Async XLA Ops:
  0.0 8.1 %copy-start.4 = (s32[8]{0:T(128)S(1)}, s32[8]{0:T(128)}, u32[]{:S(2)}) copy-start(s32[8]{0:T(128)} %param.11) | copy-start | bytes 100
  0.0 8.1 %copy-start.5 = (s32[16,1]{0,1:T(1,128)S(1)}, s32[16,1]{0,1:T(1,128)}, u32[]{:S(2)}) copy-start(s32[16,1]{0,1:T(1,128)} %param.10) | copy-start | bytes 196
  0.0 26.0 %copy-start = (bf16[2,256,2048]{2,1,0:T(8,128)(2,1)S(1)}, bf16[2,256,2048]{2,1,0:T(8,128)(2,1)}, u32[]{:S(2)}) copy-start(bf16[2,256,2048]{2,1,0:T(8,128)(2,1)} %param.8) | copy-start | bytes 6291460
  1.3 13.7 %collective-permute-start.2 = (bf16[64,2560]{1,0:T(8,128)(2,1)S(1)}, bf16[64,2560]{1,0:T(8,128)(2,1)S(1)}, u32[]{:S(2)}, u32[]{:S(2)}) collective-permute-start(bf16[64,2560]{1,0:T(8,128)(2,1)S(1)} %get-tuple-element.45), channel_id=1, source_target_pairs={{0,4},{4,8},{8,12},{12,0},{1,5},{5,9},{9,13},{13,1},{2,6},{6,10},{... | collective-permute-start | bytes 983048 | tf_op jit(solution)/shard_map/ppermute | solution.py:229
  4.4 16.4 %collective-permute-start = (bf16[64,2560]{1,0:T(8,128)(2,1)S(1)}, bf16[64,2560]{1,0:T(8,128)(2,1)S(1)}, u32[]{:S(2)}, u32[]{:S(2)}) collective-permute-start(bf16[64,2560]{1,0:T(8,128)(2,1)S(1)} %get-tuple-element.45), channel_id=1, source_target_pairs={{0,12},{4,0},{8,4},{12,8},{1,13},{5,1},{9,5},{13,9},{2,14},{6,2},{... | collective-permute-start | bytes 983048 | tf_op jit(solution)/shard_map/ppermute | solution.py:229
  6.5 60.1 %collective-permute-start.5 = (bf16[512,2560]{1,0:T(8,128)(2,1)}, bf16[512,2560]{1,0:T(8,128)(2,1)}, u32[]{:S(2)}, u32[]{:S(2)}) collective-permute-start(bf16[512,2560]{1,0:T(8,128)(2,1)} %bitcast.29), channel_id=1, source_target_pairs={{0,2},{2,0},{1,3},{3,1},{4,6},{6,4},{5,7},{7,5},{8,10},{10,8},{9,1... | collective-permute-start | bytes 7864328 | tf_op jit(solution)/shard_map/ppermute | solution.py:232
  15.0 23.5 %collective-permute-start.3 = (bf16[72,2560]{1,0:T(8,128)(2,1)}, bf16[72,2560]{1,0:T(8,128)(2,1)S(1)}, u32[]{:S(2)}, u32[]{:S(2)}) collective-permute-start(bf16[72,2560]{1,0:T(8,128)(2,1)} %pad_maximum_fusion.1), channel_id=1, source_target_pairs={{0,4},{4,8},{8,12},{12,0},{1,5},{5,9},{9,13},{13,1},{2,6},{6,10},{... | collective-permute-start | bytes 1105928 | tf_op jit(solution)/shard_map/ppermute | solution.py:229
  20.8 16.2 %collective-permute-start.1 = (bf16[72,2560]{1,0:T(8,128)(2,1)}, bf16[72,2560]{1,0:T(8,128)(2,1)S(1)}, u32[]{:S(2)}, u32[]{:S(2)}) collective-permute-start(bf16[72,2560]{1,0:T(8,128)(2,1)} %pad_maximum_fusion.1), channel_id=1, source_target_pairs={{0,12},{4,0},{8,4},{12,8},{1,13},{5,1},{9,5},{13,9},{2,14},{6,2},{... | collective-permute-start | bytes 1105928 | tf_op jit(solution)/shard_map/ppermute | solution.py:229
  23.9 10.6 %collective-permute-start.6 = (bf16[64,2560]{1,0:T(8,128)(2,1)S(1)}, bf16[64,2560]{1,0:T(8,128)(2,1)S(1)}, u32[]{:S(2)}, u32[]{:S(2)}) collective-permute-start(bf16[64,2560]{1,0:T(8,128)(2,1)S(1)} %collective-permute-done.refs_3_), channel_id=1, source_target_pairs={{0,16},{16,0},{1,17},{17,1},{2,18},{18,2},{3,19},{19,3},{4,20},{20... | collective-permute-start | bytes 983048 | tf_op jit(solution)/shard_map/ppermute | solution.py:254
  25.4 13.1 %collective-permute-start.8 = (bf16[64,2560]{1,0:T(8,128)(2,1)S(1)}, bf16[64,2560]{1,0:T(8,128)(2,1)S(1)}, u32[]{:S(2)}, u32[]{:S(2)}) collective-permute-start(bf16[64,2560]{1,0:T(8,128)(2,1)S(1)} %collective-permute-done.2.refs_7_), channel_id=1, source_target_pairs={{0,16},{16,0},{1,17},{17,1},{2,18},{18,2},{3,19},{19,3},{4,20},{20... | collective-permute-start | bytes 983048 | tf_op jit(solution)/shard_map/ppermute | solution.py:254
  26.0 40.5 %copy-start.2 = (bf16[256,2560]{1,0:T(8,128)(2,1)S(1)}, bf16[256,2560]{1,0:T(8,128)(2,1)}, u32[]{:S(2)}) copy-start(bf16[256,2560]{1,0:T(8,128)(2,1)} %refs_2_.1) | copy-start | bytes 3932164
  37.0 24.2 %collective-permute-start.7 = (bf16[72,2560]{1,0:T(8,128)(2,1)S(1)}, bf16[72,2560]{1,0:T(8,128)(2,1)S(1)}, u32[]{:S(2)}, u32[]{:S(2)}) collective-permute-start(bf16[72,2560]{1,0:T(8,128)(2,1)S(1)} %collective-permute-done.1.refs_4_), channel_id=1, source_target_pairs={{0,16},{16,0},{1,17},{17,1},{2,18},{18,2},{3,19},{19,3},{4,20},{20... | collective-permute-start | bytes 1105928 | tf_op jit(solution)/shard_map/ppermute | solution.py:254
  38.5 19.4 %collective-permute-start.9 = (bf16[72,2560]{1,0:T(8,128)(2,1)S(1)}, bf16[72,2560]{1,0:T(8,128)(2,1)S(1)}, u32[]{:S(2)}, u32[]{:S(2)}) collective-permute-start(bf16[72,2560]{1,0:T(8,128)(2,1)S(1)} %collective-permute-done.3.refs_8_), channel_id=1, source_target_pairs={{0,16},{16,0},{1,17},{17,1},{2,18},{18,2},{3,19},{19,3},{4,20},{20... | collective-permute-start | bytes 1105928 | tf_op jit(solution)/shard_map/ppermute | solution.py:254
  39.6 12.4 %collective-permute-start.10 = (bf16[64,2560]{1,0:T(8,128)(2,1)S(1)}, bf16[64,2560]{1,0:T(8,128)(2,1)S(1)}, u32[]{:S(2)}, u32[]{:S(2)}) collective-permute-start(bf16[64,2560]{1,0:T(8,128)(2,1)S(1)} %collective-permute-done.2.refs_7_), channel_id=1, source_target_pairs={{0,4},{4,8},{8,12},{12,0},{1,5},{5,9},{9,13},{13,1},{2,6},{6,10},{... | collective-permute-start | bytes 983048 | tf_op jit(solution)/shard_map/ppermute | solution.py:229
  41.0 16.9 %collective-permute-start.4 = (bf16[72,2560]{1,0:T(8,128)(2,1)S(1)}, bf16[72,2560]{1,0:T(8,128)(2,1)S(1)}, u32[]{:S(2)}, u32[]{:S(2)}) collective-permute-start(bf16[72,2560]{1,0:T(8,128)(2,1)S(1)} %collective-permute-done.3.refs_8_), channel_id=1, source_target_pairs={{0,4},{4,8},{8,12},{12,0},{1,5},{5,9},{9,13},{13,1},{2,6},{6,10},{... | collective-permute-start | bytes 1105928 | tf_op jit(solution)/shard_map/ppermute | solution.py:229
  52.0 14.5 %copy-start.1 = (bf16[2,256,2560]{2,1,0:T(8,128)(2,1)S(1)}, bf16[2,256,2560]{2,1,0:T(8,128)(2,1)}, u32[]{:S(2)}) copy-start(bf16[2,256,2560]{2,1,0:T(8,128)(2,1)} %param.7) | copy-start | bytes 7864324
  57.9 16.0 %collective-permute-start.11 = (bf16[136,2560]{1,0:T(8,128)(2,1)S(1)}, bf16[136,2560]{1,0:T(8,128)(2,1)S(1)}, u32[]{:S(2)}, u32[]{:S(2)}) collective-permute-start(bf16[136,2560]{1,0:T(8,128)(2,1)S(1)} %constant_dynamic-update-slice_fusion.refs_2_), channel_id=1, source_target_pairs={{0,16},{16,0},{1,17},{17,1},{2,18},{18,2},{3,19},{19,3},{4,20},{20... | collective-permute-start | bytes 2088968 | tf_op jit(solution)/shard_map/ppermute | solution.py:254
  59.6 18.0 %collective-permute-start.16 = (bf16[576,512]{1,0:T(8,128)(2,1)S(1)}, bf16[576,512]{1,0:T(8,128)(2,1)S(1)}, u32[]{:S(2)}, u32[]{:S(2)}) collective-permute-start(bf16[576,512]{1,0:T(8,128)(2,1)S(1)} %pad_maximum_fusion), channel_id=1, source_target_pairs={{0,2},{2,0},{1,3},{3,1},{4,6},{6,4},{5,7},{7,5},{8,10},{10,8},{9,1... | collective-permute-start | bytes 1769480 | tf_op jit(solution)/shard_map/ppermute | solution.py:315
  72.6 4.7 %copy-start.3 = (s32[4]{0:T(128)S(1)}, s32[4]{0:T(128)}, u32[]{:S(2)}) copy-start(s32[4]{0:T(128)} %constant.97.clone) | copy-start | bytes 52
  72.6 5.0 %collective-permute-start.12 = (f32[2,512,128]{2,1,0:T(8,128)S(1)}, f32[2,512,128]{2,1,0:T(8,128)S(1)}, u32[]{:S(2)}, u32[]{:S(2)}) collective-permute-start(f32[2,512,128]{2,1,0:T(8,128)S(1)} %get-tuple-element.35), channel_id=1, source_target_pairs={{0,1},{1,0},{2,3},{3,2},{4,5},{5,4},{6,7},{7,6},{8,9},{9,8},{10,11... | collective-permute-start | bytes 1572872 | tf_op jit(solution)/shard_map/ppermute | solution.py:281
  72.7 5.0 %collective-permute-start.13 = (f32[2,512,128]{2,1,0:T(8,128)S(1)}, f32[2,512,128]{2,1,0:T(8,128)S(1)}, u32[]{:S(2)}, u32[]{:S(2)}) collective-permute-start(f32[2,512,128]{2,1,0:T(8,128)S(1)} %get-tuple-element.36), channel_id=1, source_target_pairs={{0,1},{1,0},{2,3},{3,2},{4,5},{5,4},{6,7},{7,6},{8,9},{9,8},{10,11... | collective-permute-start | bytes 1572872 | tf_op jit(solution)/shard_map/ppermute | solution.py:281
  73.2 4.5 %collective-permute-start.14 = (f32[2,512,128]{2,1,0:T(8,128)S(1)}, f32[2,512,128]{2,1,0:T(8,128)S(1)}, u32[]{:S(2)}, u32[]{:S(2)}) collective-permute-start(f32[2,512,128]{2,1,0:T(8,128)S(1)} %get-tuple-element.37), channel_id=1, source_target_pairs={{0,1},{1,0},{2,3},{3,2},{4,5},{5,4},{6,7},{7,6},{8,9},{9,8},{10,11... | collective-permute-start | bytes 1572872 | tf_op jit(solution)/shard_map/ppermute | solution.py:281
  77.2 2.0 %collective-permute-start.15 = (f32[2,512,128]{2,1,0:T(8,128)S(1)}, f32[2,512,128]{2,1,0:T(8,128)S(1)}, u32[]{:S(2)}, u32[]{:S(2)}) collective-permute-start(f32[2,512,128]{2,1,0:T(8,128)S(1)} %get-tuple-element.38), channel_id=1, source_target_pairs={{0,1},{1,0},{2,3},{3,2},{4,5},{5,4},{6,7},{7,6},{8,9},{9,8},{10,11... | collective-permute-start | bytes 1572872 | tf_op jit(solution)/shard_map/ppermute | solution.py:281
  81.2 7.2 %collective-permute-start.17 = (f32[1,2,16,640]{3,2,1,0:T(8,128)S(1)}, f32[1,2,16,640]{3,2,1,0:T(8,128)S(1)}, u32[]{:S(2)}, u32[]{:S(2)}) collective-permute-start(f32[1,2,16,640]{3,2,1,0:T(8,128)S(1)} %get-tuple-element.61), channel_id=1, source_target_pairs={{0,4},{4,8},{8,12},{12,0},{1,5},{5,9},{9,13},{13,1},{2,6},{6,10},{... | collective-permute-start | bytes 245768 | tf_op jit(solution)/shard_map/ppermute | solution.py:229
  81.3 9.8 %collective-permute-start.18 = (f32[1,2,16,640]{3,2,1,0:T(8,128)S(1)}, f32[1,2,16,640]{3,2,1,0:T(8,128)S(1)}, u32[]{:S(2)}, u32[]{:S(2)}) collective-permute-start(f32[1,2,16,640]{3,2,1,0:T(8,128)S(1)} %get-tuple-element.60), channel_id=1, source_target_pairs={{0,8},{4,12},{8,0},{12,4},{1,9},{5,13},{9,1},{13,5},{2,10},{6,14},... | collective-permute-start | bytes 245768 | tf_op jit(solution)/shard_map/ppermute | solution.py:229
  83.2 7.8 %collective-permute-start.19 = (f32[1,2,16,640]{3,2,1,0:T(8,128)S(1)}, f32[1,2,16,640]{3,2,1,0:T(8,128)S(1)}, u32[]{:S(2)}, u32[]{:S(2)}) collective-permute-start(f32[1,2,16,640]{3,2,1,0:T(8,128)S(1)} %get-tuple-element.59), channel_id=1, source_target_pairs={{0,12},{4,0},{8,4},{12,8},{1,13},{5,1},{9,5},{13,9},{2,14},{6,2},{... | collective-permute-start | bytes 245768 | tf_op jit(solution)/shard_map/ppermute | solution.py:229
  91.3 3.8 %collective-permute-start.21 = (bf16[1,16,512]{2,1,0:T(8,128)(2,1)S(1)}, bf16[1,16,512]{2,1,0:T(8,128)(2,1)S(1)}, u32[]{:S(2)}, u32[]{:S(2)}) collective-permute-start(bf16[1,16,512]{2,1,0:T(8,128)(2,1)S(1)} %get-tuple-element.73), channel_id=1, source_target_pairs={{0,2},{2,0},{1,3},{3,1},{4,6},{6,4},{5,7},{7,5},{8,10},{10,8},{9,1... | collective-permute-start | bytes 49160 | tf_op jit(solution)/shard_map/ppermute | solution.py:344
  92.8 3.2 %collective-permute-start.22 = (bf16[1,16,512]{2,1,0:T(8,128)(2,1)S(1)}, bf16[1,16,512]{2,1,0:T(8,128)(2,1)S(1)}, u32[]{:S(2)}, u32[]{:S(2)}) collective-permute-start(bf16[1,16,512]{2,1,0:T(8,128)(2,1)S(1)} %get-tuple-element.73), channel_id=1, source_target_pairs={{0,3},{3,0},{1,2},{2,1},{4,7},{7,4},{5,6},{6,5},{8,11},{11,8},{9,1... | collective-permute-start | bytes 49160 | tf_op jit(solution)/shard_map/ppermute | solution.py:345
  92.8 1.5 %collective-permute-start.20 = (bf16[1,16,512]{2,1,0:T(8,128)(2,1)S(1)}, bf16[1,16,512]{2,1,0:T(8,128)(2,1)S(1)}, u32[]{:S(2)}, u32[]{:S(2)}) collective-permute-start(bf16[1,16,512]{2,1,0:T(8,128)(2,1)S(1)} %get-tuple-element.74.mine_ref), channel_id=1, source_target_pairs={{0,1},{1,0},{2,3},{3,2},{4,5},{5,4},{6,7},{7,6},{8,9},{9,8},{10,11... | collective-permute-start | bytes 49160 | tf_op jit(solution)/shard_map/ppermute | solution.py:343

commit v5 on v4

--- a/solution.py
+++ b/solution.py
@@ -61,14 +61,15 @@
     block_len = key_ref.shape[1]
     heads = held // HEAD_DIM
     tall = heads * query_len
-    out_ref[:, :, :held] = jnp.zeros(out_ref.shape[:2] + (held,), jnp.float32)
-    ext_row = lax.broadcasted_iota(jnp.int32, out_ref.shape[:2] + (tall,), 1)
-    out_ref[:, :, held:] = jnp.where(ext_row == 0, EMPTY, 0.0)
+    members, packed_rows, lanes_packed = out_ref.shape
+    extra = packed_rows - 8
+    row = lax.broadcasted_iota(jnp.int32, out_ref.shape, 1)
+    out_ref[...] = jnp.where((row == extra) | (row == extra + 1), EMPTY, 0.0)
     row_head = lax.broadcasted_iota(jnp.int32, (tall, held), 0) // query_len
     lane_head = lax.broadcasted_iota(jnp.int32, (tall, held), 1) // HEAD_DIM
     diagonal = row_head == lane_head
     square = lax.broadcasted_iota(jnp.int32, (tall, tall), 0) == lax.broadcasted_iota(jnp.int32, (tall, tall), 1)
-    ext = lax.broadcasted_iota(jnp.int32, (query_len, tall), 0)
+    ext = lax.broadcasted_iota(jnp.int32, (8, tall), 0)
     blocks = key_ref.shape[0] // 2
     for source, kept, sent, spot in pieces:
         keep, other = (refs[summand].at[piece] for summand, piece in (kept, sent))
@@ -106,10 +107,16 @@
         )
         top_row = jnp.sum(jnp.where(square, top, 0.0), axis=0, keepdims=True)
         total_row = jnp.sum(jnp.where(square, total, 0.0), axis=0, keepdims=True)
-        out_ref[place, :, :held] = out_ref[place, :, :held] + head_pick(blend, query_len)
-        before = out_ref[place, :, held:]
-        out_ref[place, :, held:] = jnp.where(
-            ext == 0, top_row, jnp.where(ext == 1, before + total_row, 0.0)
+        blend = head_pick(blend, query_len)
+        member, slot = place // 2, place % 2
+        for block in range(held // lanes_packed):
+            first = pl.multiple_of(slot * (extra // 2) + block * query_len, query_len)
+            lanes = slice(block * lanes_packed, (block + 1) * lanes_packed)
+            spot = pl.ds(first, query_len)
+            out_ref[member, spot, :] = out_ref[member, spot, :] + blend[:, lanes]
+        before = out_ref[member, extra:, :]
+        out_ref[member, extra:, :] = jnp.where(
+            ext == slot, top_row, jnp.where(ext == slot + 2, before + total_row, before)
         )
 
 
@@ -127,21 +134,27 @@
             )
         return start
 
-    def row_of(part, at, slot, row):
-        return part[at, slot, row : row + 1, held:]
-
+    packed_rows, lanes_packed = parts[0].shape[1:]
+    extra = packed_rows - 8
     for slot in range(out_ref.shape[0]):
+        top_row, total_row = (slice(extra + slot + at, extra + slot + at + 1) for at in (0, 2))
+
         def top_step(part, at, top):
-            return jnp.maximum(top, row_of(part, at, slot, 0))
+            return jnp.maximum(top, part[at, top_row, :])
 
         def total_step(part, at, total):
-            return total + jnp.exp(row_of(part, at, slot, 0) - top) * row_of(part, at, slot, 1)
+            return total + jnp.exp(part[at, top_row, :] - top) * part[at, total_row, :]
 
         def blend_step(part, at, blend):
-            share = jnp.exp(row_of(part, at, slot, 0) - top) / total
+            share = jnp.exp(part[at, top_row, :] - top) / total
             column = jnp.sum(jnp.where(square, share, 0.0), axis=1, keepdims=True)
             spread = head_pick(jnp.broadcast_to(column, (tall, held)), query_len)
-            return blend + spread * part[at, slot, :, :held]
+            first = slot * (extra // 2)
+            rows = [
+                part[at, first + block * query_len : first + (block + 1) * query_len, :]
+                for block in range(held // lanes_packed)
+            ]
+            return blend + spread * jnp.concatenate(rows, axis=1)
 
         top = over(jnp.full((1, tall), EMPTY, jnp.float32), top_step)
         total = over(jnp.zeros((1, tall), jnp.float32), total_step)
@@ -242,11 +255,12 @@
             for first, length in zip((0, lengths[0]), lengths)
         ]
         sent[1] = jnp.concatenate([sent[1], with_rows(queries, units)], axis=0)
-        below, above = [], []
-        for at in range(2):
-            below.append(shifted(after(sent[at], below[-1:]), 1))
-            above.append(shifted(after(sent[at], above[-1:]), -1))
-        opposite = [jnp.concatenate([shifted(after(below[0], below[1:]), 1), shifted(below[1], 1)], axis=0)]
+        below = [shifted(sent[0], 1)]
+        sent = [after(piece, below) for piece in sent]
+        below.append(shifted(sent[1], 1))
+        above = [shifted(sent[0], -1)]
+        above.append(shifted(after(sent[1], above), -1))
+        opposite = [shifted(after(below[0], below[1:]), 1), shifted(below[1], 1)]
         around = [from_rows(piece[-1][-8:], queries.shape) for piece in (above, opposite, below)]
         queries = jnp.concatenate([queries] + around, axis=0)
         swapped = []
@@ -254,34 +268,29 @@
             swapped.append(lax.ppermute(after(piece, swapped[max(at - 2, 0) : max(at - 1, 0)]), "groups", SWAP))
         weights = [down_weight] + above + swapped[1:4:2] + below + swapped[0:4:2] + opposite + swapped[4:]
         flags = jnp.stack([core, (group == core).astype(core.dtype)])
-        blocks_of = [[(2, shard)], list(zip(range(3, 7), 2 * lengths)), list(zip(range(7, 11), 2 * lengths))]
+        blocks_of = [[(1, shard)]] + [list(zip(range(at, at + 4), 2 * lengths)) for at in (2, 6, 10)]
         spots = lax.rem(high + jnp.array([0, 1, 3, 2], jnp.int32), highs)
         spots = jnp.stack([(spots * 2 + side) * stride + core * span, spots * span])
         own_residual = passages
 
+        flags = after(flags, swapped[4:5])
         kept, *away = project(
-            flags,
-            [hidden, partner_hidden] + weights[:9],
-            [(source, blocks_of[at]) for source in range(2) for at in range(3)],
-            [2, 2, 2],
-            half,
-            24 * rows * half * units,
-            "project_near",
+            flags, [hidden] + weights[:9], [(0, blocks_of[at]) for at in range(3)], [3], half, 1, "project_own"
         )
         flags, kept, *away = lax.optimization_barrier((flags, kept, *away))
         late_kept, *late_away = project(
             flags,
-            [hidden, partner_hidden] + weights[9:],
-            [(source, [(2, half), (3, half)]) for source in range(2)],
-            [2],
+            [hidden] + weights + [partner_hidden],
+            [(14, blocks_of[at]) for at in range(4)] + [(0, blocks_of[3])],
+            [2, 2, 1],
             half,
             1,
-            "project_far",
+            "project_rest",
         )
         others = [lax.ppermute(piece, "mp", SWAP) for piece in away + late_away]
         summands = [kept, late_kept] + others
-        pieces = [(at // 3, (0, at), (2 + at // 2, at % 2), at % 3) for at in range(6)]
-        pieces += [(source, (1, source), (5, source), 3) for source in range(2)]
+        pieces = [(0, (0, at), (2, at), at) for at in range(3)] + [(0, (1, 4), (5, 0), 3)]
+        pieces += [(1, (1, at), (3 + at // 2, at % 2), at) for at in range(4)]
         origin = high
     else:
         queries = lax.all_gather(queries, ("high", "low"), axis=0, tiled=True)
@@ -313,7 +322,7 @@
 
     leaving = jnp.concatenate([leaving, queries[:, 1].reshape(-1, held)], axis=0)
     partner = lax.ppermute(leaving, "side", SWAP)
-    packed = (2 * members, query_len, held + heads * query_len)
+    packed = (members, 2 * held // 128 * query_len + 8, 128)
     operands = summands + [own_residual, partner]
     partials = pl.pallas_call(
         functools.partial(attend_kernel, pieces=pieces),
@@ -324,8 +333,6 @@
         compiler_params=pltpu.CompilerParams(vmem_limit_bytes=VMEM_LIMIT),
         name="attend",
     )(places, spots, queries[:, 0], *operands)
-    partials = partials.reshape((members, 2) + partials.shape[1:])
-
     if lined:
         received = [partials[0:1]] + [shifted(partials[ahead : ahead + 1], ahead) for ahead in range(1, highs)]
     else:

time: 97.4 us -> 112 us (1.15)
  local copies, waits for them, and re-layouts: 2.45 us -> 14.3 us
  waiting for transfers between devices: 51.7 us -> 57 us
  starting transfers between devices: 28.8 us -> 24.1 us
  Pallas kernels: 12.7 us -> 14.3 us
    unnamed x13 -> x52, local copies, waits for them, and re-layouts: 0.05 us -> 10.2 us
    ppermute x5 -> x6, waiting for transfers between devices: 9.02 us -> 15.6 us  [body(): lax.ppermute(after(piece, swapped[max(at - 2, 0):max(at - 1, 0)]), 'group...]
    ppermute x1, waiting for transfers between devices: 5.38 us -> 0.01 us  [body(): partner_hidden = lax.ppermute(hidden, 'side', SWAP)]
    ppermute x9, starting transfers between devices: 16.5 us -> 12.7 us  [shifted(): lax.ppermute(array, 'high', [(at, (at + shift) % highs) for at in range(h...]
    ppermute x9, waiting for transfers between devices: 33.1 us -> 36.8 us  [shifted(): lax.ppermute(array, 'high', [(at, (at + shift) % highs) for at in range(h...]
    ppermute x1, starting transfers between devices: 1.56 us -> 0.01 us  [body(): partner = lax.ppermute(leaving, 'side', SWAP)]
    ppermute x1, waiting for transfers between devices: 0.29 us -> 1.71 us  [body(): partner = lax.ppermute(leaving, 'side', SWAP)]
    ppermute x4, waiting for transfers between devices: 1.55 us -> 0.28 us  [body(): others = [lax.ppermute(piece, 'mp', SWAP) for piece in away + late_away]]
  transfers between devices with their start and end apart: 23 -> 24, of which waited for: 15 -> 14; matrix products, arithmetic and copies ran while one was open for 2% -> 4% of each run, Pallas kernels for 10% -> 9%
where the time goes in v5:
time: 112 us
  waiting for transfers between devices  57 us (51%)
  starting transfers between devices  24.1 us (22%)
  local copies, waits for them, and re-layouts  14.3 us (13%)
  Pallas kernels  14.3 us (13%)
  other arithmetic  2.04 us (2%)
    ppermute x9, waiting for transfers between devices, shifted(): lax.ppermute(array, 'high', [(at, (at + shift) % highs) for at in range(h...  36.8 us
    ppermute x6, waiting for transfers between devices, body(): lax.ppermute(after(piece, swapped[max(at - 2, 0):max(at - 1, 0)]), 'group...  15.6 us
    ppermute x9, starting transfers between devices, shifted(): lax.ppermute(array, 'high', [(at, (at + shift) % highs) for at in range(h...  12.7 us
    unnamed x52, local copies, waits for them, and re-layouts  10.2 us
    pallas_call x2, Pallas kernels, project(): pl.pallas_call(functools.partial(project_kernel, jobs=jobs, sends=sends),...  10.1 us
    ppermute x6, starting transfers between devices, body(): lax.ppermute(after(piece, swapped[max(at - 2, 0):max(at - 1, 0)]), 'group...  6.61 us
    pallas_call x1, Pallas kernels, body(): pl.pallas_call(functools.partial(attend_kernel, pieces=pieces), out_shape...  2.72 us
  transfers between devices with their start and end apart: 24, of which 14 were waited for; matrix products, arithmetic and copies ran while one was open for 4% of the time, Pallas kernels for 9%

profile of v5, /device:TPU:0, one launch (start us, length us, event | category | flops | bytes accessed | tf_op | source)
XLA Modules:
  0.0 111.9 jit_solution(7465167582041352485)
XLA Ops:
  0.0 1.1 %constant_dynamic-slice_fusion.4 = (bf16[64,2560]{1,0:T(8,128)(2,1)S(1)}, bf16[64,2560]{1,0:T(8,128)(2,1)S(1)}) fusion(bf16[256,2560]{1,0:T(8,128)(2,1)} %refs_1_.3, s32[]{:T(128)S(6)} %select_n.73, s32[]{:T(128)S(6)} %select_n.72), kind=kLoop, calls=%fused_computation.22 | loop fusion | bytes 1310728 | tf_op jit(solution)/shard_map/dynamic_slice | solution.py:254
  1.2 3.1 %collective-permute-start = (bf16[64,2560]{1,0:T(8,128)(2,1)S(1)}, bf16[64,2560]{1,0:T(8,128)(2,1)}, u32[]{:S(2)}, u32[]{:S(2)}) collective-permute-start(bf16[64,2560]{1,0:T(8,128)(2,1)S(1)} %get-tuple-element.24), channel_id=1, source_target_pairs={{0,4},{4,8},{8,12},{12,0},{1,5},{5,9},{9,13},{13,1},{2,6},{6,10},{... | collective-permute-start | bytes 983048 | tf_op jit(solution)/shard_map/ppermute | solution.py:242
  4.3 1.5 %collective-permute-start.12 = (bf16[512,2560]{1,0:T(8,128)(2,1)}, bf16[512,2560]{1,0:T(8,128)(2,1)}, u32[]{:S(2)}, u32[]{:S(2)}) collective-permute-start(bf16[512,2560]{1,0:T(8,128)(2,1)} %bitcast.19), channel_id=1, source_target_pairs={{0,2},{2,0},{1,3},{3,1},{4,6},{6,4},{5,7},{7,5},{8,10},{10,8},{9,1... | collective-permute-start | bytes 7864328 | tf_op jit(solution)/shard_map/ppermute | solution.py:245
  5.8 2.1 %constant_dynamic-slice_fusion.3 = (bf16[512,128]{1,0:T(8,128)(2,1)}, bf16[512,128]{1,0:T(8,128)(2,1)}, bf16[512,128]{1,0:T(8,128)(2,1)}, bf16[512,128]{1,0:T(8,128)(2,1)}) fusion(bf16[512,2048]{1,0:T(8,128)(2,1)} %bitcast.22, s32[]{:T(128)S(6)} %select_n.68, s32[]{:T(128)S(6)} %select_n.71, s32[]{:T(128)S(6)} %select_n.70, s32[]{:T(128)S(6)} %select_n.69), kind=kLoop, calls=%fused_computation.21 | loop fusion | bytes 1048592 | tf_op jit(solution)/shard_map/dynamic_slice | solution.py:238
  8.7 5.4 %collective-permute-done.refs_6_ = bf16[64,2560]{1,0:T(8,128)(2,1)} collective-permute-done((bf16[64,2560]{1,0:T(8,128)(2,1)S(1)}, bf16[64,2560]{1,0:T(8,128)(2,1)}, u32[]{:S(2)}, u32[]{:S(2)}) %collective-permute-start) | collective-permute-done | bytes 327712 | tf_op jit(solution)/shard_map/ppermute | solution.py:242
  14.1 1.7 %collective-permute-start.1 = (bf16[64,2560]{1,0:T(8,128)(2,1)S(1)}, bf16[64,2560]{1,0:T(8,128)(2,1)}, u32[]{:S(2)}, u32[]{:S(2)}) collective-permute-start(bf16[64,2560]{1,0:T(8,128)(2,1)S(1)} %get-tuple-element.24), channel_id=1, source_target_pairs={{0,12},{4,0},{8,4},{12,8},{1,13},{5,1},{9,5},{13,9},{2,14},{6,2},{... | collective-permute-start | bytes 983048 | tf_op jit(solution)/shard_map/ppermute | solution.py:242
  16.1 1.5 %collective-permute-start.6 = (bf16[64,2560]{1,0:T(8,128)(2,1)}, bf16[64,2560]{1,0:T(8,128)(2,1)S(1)}, u32[]{:S(2)}, u32[]{:S(2)}) collective-permute-start(bf16[64,2560]{1,0:T(8,128)(2,1)} %collective-permute-done.refs_6_), channel_id=1, source_target_pairs={{0,16},{16,0},{1,17},{17,1},{2,18},{18,2},{3,19},{19,3},{4,20},{20... | collective-permute-start | bytes 983048 | tf_op jit(solution)/shard_map/ppermute | solution.py:268
  17.7 11.7 %collective-permute-done.1.refs_2_ = bf16[64,2560]{1,0:T(8,128)(2,1)} collective-permute-done((bf16[64,2560]{1,0:T(8,128)(2,1)S(1)}, bf16[64,2560]{1,0:T(8,128)(2,1)}, u32[]{:S(2)}, u32[]{:S(2)}) %collective-permute-start.1) | collective-permute-done | bytes 327712 | tf_op jit(solution)/shard_map/ppermute | solution.py:242
  29.5 1.5 %collective-permute-start.9 = (bf16[64,2560]{1,0:T(8,128)(2,1)}, bf16[64,2560]{1,0:T(8,128)(2,1)S(1)}, u32[]{:S(2)}, u32[]{:S(2)}) collective-permute-start(bf16[64,2560]{1,0:T(8,128)(2,1)} %collective-permute-done.1.refs_2_), channel_id=1, source_target_pairs={{0,16},{16,0},{1,17},{17,1},{2,18},{18,2},{3,19},{19,3},{4,20},{20... | collective-permute-start | bytes 983048 | tf_op jit(solution)/shard_map/ppermute | solution.py:268
  31.0 1.9 %collective-permute-done.3.refs_7_ = bf16[72,2560]{1,0:T(8,128)(2,1)S(1)} collective-permute-done((bf16[72,2560]{1,0:T(8,128)(2,1)}, bf16[72,2560]{1,0:T(8,128)(2,1)S(1)}, u32[]{:S(2)}, u32[]{:S(2)}) %collective-permute-start.3) | collective-permute-done | bytes 368672 | tf_op jit(solution)/shard_map/ppermute | solution.py:242
  32.9 1.5 %collective-permute-start.7 = (bf16[72,2560]{1,0:T(8,128)(2,1)S(1)}, bf16[72,2560]{1,0:T(8,128)(2,1)S(1)}, u32[]{:S(2)}, u32[]{:S(2)}) collective-permute-start(bf16[72,2560]{1,0:T(8,128)(2,1)S(1)} %collective-permute-done.3.refs_7_), channel_id=1, source_target_pairs={{0,16},{16,0},{1,17},{17,1},{2,18},{18,2},{3,19},{19,3},{4,20},{20... | collective-permute-start | bytes 1105928 | tf_op jit(solution)/shard_map/ppermute | solution.py:268
  34.4 1.5 %collective-permute-start.4 = (bf16[72,2560]{1,0:T(8,128)(2,1)S(1)}, bf16[72,2560]{1,0:T(8,128)(2,1)}, u32[]{:S(2)}, u32[]{:S(2)}) collective-permute-start(bf16[72,2560]{1,0:T(8,128)(2,1)S(1)} %collective-permute-done.3.refs_7_), channel_id=1, source_target_pairs={{0,4},{4,8},{8,12},{12,0},{1,5},{5,9},{9,13},{13,1},{2,6},{6,10},{... | collective-permute-start | bytes 1105928 | tf_op jit(solution)/shard_map/ppermute | solution.py:242
  35.9 3.0 %collective-permute-done.9.refs_4_ = bf16[64,2560]{1,0:T(8,128)(2,1)S(1)} collective-permute-done((bf16[64,2560]{1,0:T(8,128)(2,1)}, bf16[64,2560]{1,0:T(8,128)(2,1)S(1)}, u32[]{:S(2)}, u32[]{:S(2)}) %collective-permute-start.9) | collective-permute-done | bytes 327712 | tf_op jit(solution)/shard_map/ppermute | solution.py:268
  38.9 2.2 %collective-permute-start.5 = (bf16[64,2560]{1,0:T(8,128)(2,1)}, bf16[64,2560]{1,0:T(8,128)(2,1)S(1)}, u32[]{:S(2)}, u32[]{:S(2)}) collective-permute-start(bf16[64,2560]{1,0:T(8,128)(2,1)} %collective-permute-done.refs_6_), channel_id=1, source_target_pairs={{0,4},{4,8},{8,12},{12,0},{1,5},{5,9},{9,13},{13,1},{2,6},{6,10},{... | collective-permute-start | bytes 983048 | tf_op jit(solution)/shard_map/ppermute | solution.py:242
  41.1 12.7 %collective-permute-done.2.refs_3_ = bf16[72,2560]{1,0:T(8,128)(2,1)S(1)} collective-permute-done((bf16[72,2560]{1,0:T(8,128)(2,1)}, bf16[72,2560]{1,0:T(8,128)(2,1)S(1)}, u32[]{:S(2)}, u32[]{:S(2)}) %collective-permute-start.2) | collective-permute-done | bytes 368672 | tf_op jit(solution)/shard_map/ppermute | solution.py:242
  53.8 2.1 %collective-permute-start.8 = (bf16[64,2560]{1,0:T(8,128)(2,1)S(1)}, bf16[64,2560]{1,0:T(8,128)(2,1)S(1)}, u32[]{:S(2)}, u32[]{:S(2)}) collective-permute-start(bf16[64,2560]{1,0:T(8,128)(2,1)S(1)} %collective-permute-done.5.refs_10_), channel_id=1, source_target_pairs={{0,16},{16,0},{1,17},{17,1},{2,18},{18,2},{3,19},{19,3},{4,20},{20... | collective-permute-start | bytes 983048 | tf_op jit(solution)/shard_map/ppermute | solution.py:268
  56.6 8.6 %collective-permute-done.10.refs_5_ = bf16[72,2560]{1,0:T(8,128)(2,1)S(1)} collective-permute-done((bf16[72,2560]{1,0:T(8,128)(2,1)S(1)}, bf16[72,2560]{1,0:T(8,128)(2,1)S(1)}, u32[]{:S(2)}, u32[]{:S(2)}) %collective-permute-start.10) | collective-permute-done | bytes 368672 | tf_op jit(solution)/shard_map/ppermute | solution.py:268
  65.3 4.0 %collective-permute-done.8.refs_12_ = bf16[64,2560]{1,0:T(8,128)(2,1)S(1)} collective-permute-done((bf16[64,2560]{1,0:T(8,128)(2,1)S(1)}, bf16[64,2560]{1,0:T(8,128)(2,1)S(1)}, u32[]{:S(2)}, u32[]{:S(2)}) %collective-permute-start.8) | collective-permute-done | bytes 327712 | tf_op jit(solution)/shard_map/ppermute | solution.py:268
  70.0 1.3 %copy-done.1 = bf16[256,2560]{1,0:T(8,128)(2,1)S(1)} copy-done((bf16[256,2560]{1,0:T(8,128)(2,1)S(1)}, bf16[256,2560]{1,0:T(8,128)(2,1)}, u32[]{:S(2)}) %copy-start.1) | copy-done | bytes 1310744
  71.3 4.3 %project_own.1 = (f32[3,512,128]{2,1,0:T(8,128)S(1)}, f32[3,512,128]{2,1,0:T(8,128)}) custom-call(s32[2]{0:T(128)S(1)} %pad_add_fusion.3.flag_ref, bf16[512,2560]{1,0:T(8,128)(2,1)S(1)} %bitcast.20, bf16[256,2560]{1,0:T(8,128)(2,1)S(1)} %copy-done.1, bf16[64,2560]{1,0:T(8,128)(2,1)} %collective-permute-done.1.refs_2_, ...), custom_call_target="tpu_custom_call" | custom-call | flops 1 | bytes 1 | tf_op jit(solution)/shard_map/project_own/pallas_call | solution.py:190
  77.5 1.3 %copy-done.2 = bf16[256,2560]{1,0:T(8,128)(2,1)S(1)} copy-done((bf16[256,2560]{1,0:T(8,128)(2,1)S(1)}, bf16[256,2560]{1,0:T(8,128)(2,1)}, u32[]{:S(2)}) %copy-start.2) | copy-done | bytes 1310744
  78.8 1.0 copy-done.5
  79.8 1.0 copy-done.7
  84.6 5.8 %project_rest.1 = (f32[5,512,128]{2,1,0:T(8,128)S(1)}, f32[2,512,128]{2,1,0:T(8,128)S(1)}, f32[2,512,128]{2,1,0:T(8,128)S(1)}, f32[1,512,128]{2,1,0:T(8,128)S(1)}) custom-call(s32[2]{0:T(128)S(1)} %pad_add_fusion.3.flag_ref, bf16[512,2560]{1,0:T(8,128)(2,1)S(1)} %bitcast.21, bf16[256,2560]{1,0:T(8,128)(2,1)S(1)} %copy-done.2, ...), custom_call_target="tpu_custom_call" | custom-call | flops 1 | bytes 1 | tf_op jit(solution)/shard_map/project_rest/pallas_call | solution.py:190
  91.7 1.7 %collective-permute-done.17.refs_7_ = bf16[576,512]{1,0:T(8,128)(2,1)} collective-permute-done((bf16[576,512]{1,0:T(8,128)(2,1)}, bf16[576,512]{1,0:T(8,128)(2,1)}, u32[]{:S(2)}, u32[]{:S(2)}) %collective-permute-start.17) | collective-permute-done | bytes 589856 | tf_op jit(solution)/shard_map/ppermute | solution.py:324
  93.7 2.7 %attend.1 = f32[4,136,128]{2,1,0:T(8,128)S(1)} custom-call(s32[4]{0:T(128)S(1)} %pad_add_fusion.2.place_ref, s32[2,4]{1,0:T(2,128)S(1)} %pad_add_fusion.spot_ref, bf16[4,16,512]{2,1,0:T(8,128)(2,1)S(1)} %get-tuple-element.66.query_ref, f32[3,512,128]{2,1,0:T(8,128)S(1)} %copy-done.13, f32[5,512,128]{2,1,0:T(8,128)S(1)} %get-tuple-element.36.refs_1_, ...), custom_call_target="tpu_custom_call" | custom-call | tf_op jit(solution)/shard_map/attend/pallas_call | solution.py:327
  96.6 3.7 %collective-permute-start.20 = (f32[1,136,128]{2,1,0:T(8,128)S(1)}, f32[1,136,128]{2,1,0:T(8,128)S(1)}, u32[]{:S(2)}, u32[]{:S(2)}) collective-permute-start(f32[1,136,128]{2,1,0:T(8,128)S(1)} %get-tuple-element.61), channel_id=1, source_target_pairs={{0,12},{4,0},{8,4},{12,8},{1,13},{5,1},{9,5},{13,9},{2,14},{6,2},{... | collective-permute-start | bytes 208904 | tf_op jit(solution)/shard_map/ppermute | solution.py:242
  100.4 3.1 %collective-permute-done.18.refs_1_ = f32[1,136,128]{2,1,0:T(8,128)S(1)} collective-permute-done((f32[1,136,128]{2,1,0:T(8,128)S(1)}, f32[1,136,128]{2,1,0:T(8,128)S(1)}, u32[]{:S(2)}, u32[]{:S(2)}) %collective-permute-start.18) | collective-permute-done | bytes 69664 | tf_op jit(solution)/shard_map/ppermute | solution.py:242
  103.5 2.1 %collective-permute-done.19.refs_2_ = f32[1,136,128]{2,1,0:T(8,128)S(1)} collective-permute-done((f32[1,136,128]{2,1,0:T(8,128)S(1)}, f32[1,136,128]{2,1,0:T(8,128)S(1)}, u32[]{:S(2)}, u32[]{:S(2)}) %collective-permute-start.19) | collective-permute-done | bytes 69664 | tf_op jit(solution)/shard_map/ppermute | solution.py:242
  105.8 1.8 %collective-permute-start.22 = (bf16[1,16,512]{2,1,0:T(8,128)(2,1)S(1)}, bf16[1,16,512]{2,1,0:T(8,128)(2,1)S(1)}, u32[]{:S(2)}, u32[]{:S(2)}) collective-permute-start(bf16[1,16,512]{2,1,0:T(8,128)(2,1)S(1)} %get-tuple-element.75), channel_id=1, source_target_pairs={{0,2},{2,0},{1,3},{3,1},{4,6},{6,4},{5,7},{7,5},{8,10},{10,8},{9,1... | collective-permute-start | bytes 49160 | tf_op jit(solution)/shard_map/ppermute | solution.py:351
  109.6 1.2 %collective-permute-done.23.both_ref = bf16[1,16,512]{2,1,0:T(8,128)(2,1)S(1)} collective-permute-done((bf16[1,16,512]{2,1,0:T(8,128)(2,1)S(1)}, bf16[1,16,512]{2,1,0:T(8,128)(2,1)S(1)}, u32[]{:S(2)}, u32[]{:S(2)}) %collective-permute-start.23) | collective-permute-done | bytes 16416 | tf_op jit(solution)/shard_map/ppermute | solution.py:352
  110.8 1.2 %assemble.1 = bf16[1,16,2048]{2,1,0:T(8,128)(2,1)} custom-call(s32[2]{0:T(128)S(1)} %pad_add_fusion.1.flag_ref, bf16[1,16,512]{2,1,0:T(8,128)(2,1)S(1)} %get-tuple-element.76.mine_ref, bf16[1,16,512]{2,1,0:T(8,128)(2,1)S(1)} %collective-permute-done.21.core_ref, bf16[1,16,512]{2,1,0:T(8,128)(2,1)S(1)} %collective-permute-done.22.side_ref, ...), custom_call_target="tpu_custom_call" | custom-call | tf_op jit(solution)/shard_map/assemble/pallas_call | solution.py:359
  (101 shorter events, 12.5 us)
Async XLA Ops:
  1.2 12.9 %collective-permute-start = (bf16[64,2560]{1,0:T(8,128)(2,1)S(1)}, bf16[64,2560]{1,0:T(8,128)(2,1)}, u32[]{:S(2)}, u32[]{:S(2)}) collective-permute-start(bf16[64,2560]{1,0:T(8,128)(2,1)S(1)} %get-tuple-element.24), channel_id=1, source_target_pairs={{0,4},{4,8},{8,12},{12,0},{1,5},{5,9},{9,13},{13,1},{2,6},{6,10},{... | collective-permute-start | bytes 983048 | tf_op jit(solution)/shard_map/ppermute | solution.py:242
  4.3 73.2 %collective-permute-start.12 = (bf16[512,2560]{1,0:T(8,128)(2,1)}, bf16[512,2560]{1,0:T(8,128)(2,1)}, u32[]{:S(2)}, u32[]{:S(2)}) collective-permute-start(bf16[512,2560]{1,0:T(8,128)(2,1)} %bitcast.19), channel_id=1, source_target_pairs={{0,2},{2,0},{1,3},{3,1},{4,6},{6,4},{5,7},{7,5},{8,10},{10,8},{9,1... | collective-permute-start | bytes 7864328 | tf_op jit(solution)/shard_map/ppermute | solution.py:245
  5.8 64.2 %copy-start = (bf16[2,256,2560]{2,1,0:T(8,128)(2,1)S(1)}, bf16[2,256,2560]{2,1,0:T(8,128)(2,1)}, u32[]{:S(2)}) copy-start(bf16[2,256,2560]{2,1,0:T(8,128)(2,1)} %param.7) | copy-start | bytes 7864324
  14.1 15.3 %collective-permute-start.1 = (bf16[64,2560]{1,0:T(8,128)(2,1)S(1)}, bf16[64,2560]{1,0:T(8,128)(2,1)}, u32[]{:S(2)}, u32[]{:S(2)}) collective-permute-start(bf16[64,2560]{1,0:T(8,128)(2,1)S(1)} %get-tuple-element.24), channel_id=1, source_target_pairs={{0,12},{4,0},{8,4},{12,8},{1,13},{5,1},{9,5},{13,9},{2,14},{6,2},{... | collective-permute-start | bytes 983048 | tf_op jit(solution)/shard_map/ppermute | solution.py:242
  15.8 17.0 %collective-permute-start.3 = (bf16[72,2560]{1,0:T(8,128)(2,1)}, bf16[72,2560]{1,0:T(8,128)(2,1)S(1)}, u32[]{:S(2)}, u32[]{:S(2)}) collective-permute-start(bf16[72,2560]{1,0:T(8,128)(2,1)} %pad_maximum_fusion.1), channel_id=1, source_target_pairs={{0,4},{4,8},{8,12},{12,0},{1,5},{5,9},{9,13},{13,1},{2,6},{6,10},{... | collective-permute-start | bytes 1105928 | tf_op jit(solution)/shard_map/ppermute | solution.py:242
  16.1 14.8 %collective-permute-start.6 = (bf16[64,2560]{1,0:T(8,128)(2,1)}, bf16[64,2560]{1,0:T(8,128)(2,1)S(1)}, u32[]{:S(2)}, u32[]{:S(2)}) collective-permute-start(bf16[64,2560]{1,0:T(8,128)(2,1)} %collective-permute-done.refs_6_), channel_id=1, source_target_pairs={{0,16},{16,0},{1,17},{17,1},{2,18},{18,2},{3,19},{19,3},{4,20},{20... | collective-permute-start | bytes 983048 | tf_op jit(solution)/shard_map/ppermute | solution.py:268
  29.4 24.3 %collective-permute-start.2 = (bf16[72,2560]{1,0:T(8,128)(2,1)}, bf16[72,2560]{1,0:T(8,128)(2,1)S(1)}, u32[]{:S(2)}, u32[]{:S(2)}) collective-permute-start(bf16[72,2560]{1,0:T(8,128)(2,1)} %pad_maximum_fusion.1), channel_id=1, source_target_pairs={{0,12},{4,0},{8,4},{12,8},{1,13},{5,1},{9,5},{13,9},{2,14},{6,2},{... | collective-permute-start | bytes 1105928 | tf_op jit(solution)/shard_map/ppermute | solution.py:242
  29.5 9.4 %collective-permute-start.9 = (bf16[64,2560]{1,0:T(8,128)(2,1)}, bf16[64,2560]{1,0:T(8,128)(2,1)S(1)}, u32[]{:S(2)}, u32[]{:S(2)}) collective-permute-start(bf16[64,2560]{1,0:T(8,128)(2,1)} %collective-permute-done.1.refs_2_), channel_id=1, source_target_pairs={{0,16},{16,0},{1,17},{17,1},{2,18},{18,2},{3,19},{19,3},{4,20},{20... | collective-permute-start | bytes 983048 | tf_op jit(solution)/shard_map/ppermute | solution.py:268
  31.0 44.6 %copy-start.8 = (bf16[64,2560]{1,0:T(8,128)(2,1)}, bf16[64,2560]{1,0:T(8,128)(2,1)S(1)}, u32[]{:S(2)}) copy-start(bf16[64,2560]{1,0:T(8,128)(2,1)S(1)} %collective-permute-done.6.refs_8_) | copy-start | bytes 983044
  32.9 20.9 %collective-permute-start.7 = (bf16[72,2560]{1,0:T(8,128)(2,1)S(1)}, bf16[72,2560]{1,0:T(8,128)(2,1)S(1)}, u32[]{:S(2)}, u32[]{:S(2)}) collective-permute-start(bf16[72,2560]{1,0:T(8,128)(2,1)S(1)} %collective-permute-done.3.refs_7_), channel_id=1, source_target_pairs={{0,16},{16,0},{1,17},{17,1},{2,18},{18,2},{3,19},{19,3},{4,20},{20... | collective-permute-start | bytes 1105928 | tf_op jit(solution)/shard_map/ppermute | solution.py:268
  34.4 21.5 %collective-permute-start.4 = (bf16[72,2560]{1,0:T(8,128)(2,1)S(1)}, bf16[72,2560]{1,0:T(8,128)(2,1)}, u32[]{:S(2)}, u32[]{:S(2)}) collective-permute-start(bf16[72,2560]{1,0:T(8,128)(2,1)S(1)} %collective-permute-done.3.refs_7_), channel_id=1, source_target_pairs={{0,4},{4,8},{8,12},{12,0},{1,5},{5,9},{9,13},{13,1},{2,6},{6,10},{... | collective-permute-start | bytes 1105928 | tf_op jit(solution)/shard_map/ppermute | solution.py:242
  38.9 36.7 %copy-start.10 = (bf16[64,2560]{1,0:T(8,128)(2,1)}, bf16[64,2560]{1,0:T(8,128)(2,1)S(1)}, u32[]{:S(2)}) copy-start(bf16[64,2560]{1,0:T(8,128)(2,1)S(1)} %collective-permute-done.9.refs_4_) | copy-start | bytes 983044
  38.9 14.8 %collective-permute-start.5 = (bf16[64,2560]{1,0:T(8,128)(2,1)}, bf16[64,2560]{1,0:T(8,128)(2,1)S(1)}, u32[]{:S(2)}, u32[]{:S(2)}) collective-permute-start(bf16[64,2560]{1,0:T(8,128)(2,1)} %collective-permute-done.refs_6_), channel_id=1, source_target_pairs={{0,4},{4,8},{8,12},{12,0},{1,5},{5,9},{9,13},{13,1},{2,6},{6,10},{... | collective-permute-start | bytes 983048 | tf_op jit(solution)/shard_map/ppermute | solution.py:242
  53.7 11.5 %collective-permute-start.10 = (bf16[72,2560]{1,0:T(8,128)(2,1)S(1)}, bf16[72,2560]{1,0:T(8,128)(2,1)S(1)}, u32[]{:S(2)}, u32[]{:S(2)}) collective-permute-start(bf16[72,2560]{1,0:T(8,128)(2,1)S(1)} %collective-permute-done.2.refs_3_), channel_id=1, source_target_pairs={{0,16},{16,0},{1,17},{17,1},{2,18},{18,2},{3,19},{19,3},{4,20},{20... | collective-permute-start | bytes 1105928 | tf_op jit(solution)/shard_map/ppermute | solution.py:268
  53.7 21.8 %copy-start.14 = (bf16[64,2560]{1,0:T(8,128)(2,1)}, bf16[64,2560]{1,0:T(8,128)(2,1)S(1)}, u32[]{:S(2)}) copy-start(bf16[64,2560]{1,0:T(8,128)(2,1)S(1)} %collective-permute-done.5.refs_10_) | copy-start | bytes 983044
  53.8 21.8 %copy-start.4 = (bf16[72,2560]{1,0:T(8,128)(2,1)}, bf16[72,2560]{1,0:T(8,128)(2,1)S(1)}, u32[]{:S(2)}) copy-start(bf16[72,2560]{1,0:T(8,128)(2,1)S(1)} %collective-permute-done.7.refs_9_) | copy-start | bytes 1105924
  53.8 15.5 %collective-permute-start.8 = (bf16[64,2560]{1,0:T(8,128)(2,1)S(1)}, bf16[64,2560]{1,0:T(8,128)(2,1)S(1)}, u32[]{:S(2)}, u32[]{:S(2)}) collective-permute-start(bf16[64,2560]{1,0:T(8,128)(2,1)S(1)} %collective-permute-done.5.refs_10_), channel_id=1, source_target_pairs={{0,16},{16,0},{1,17},{17,1},{2,18},{18,2},{3,19},{19,3},{4,20},{20... | collective-permute-start | bytes 983048 | tf_op jit(solution)/shard_map/ppermute | solution.py:268
  65.2 10.4 %copy-start.6 = (bf16[72,2560]{1,0:T(8,128)(2,1)}, bf16[72,2560]{1,0:T(8,128)(2,1)S(1)}, u32[]{:S(2)}) copy-start(bf16[72,2560]{1,0:T(8,128)(2,1)S(1)} %collective-permute-done.10.refs_5_) | copy-start | bytes 1105924
  65.2 12.2 %collective-permute-start.11 = (bf16[72,2560]{1,0:T(8,128)(2,1)}, bf16[72,2560]{1,0:T(8,128)(2,1)}, u32[]{:S(2)}, u32[]{:S(2)}) collective-permute-start(bf16[72,2560]{1,0:T(8,128)(2,1)} %collective-permute-done.4.refs_11_), channel_id=1, source_target_pairs={{0,16},{16,0},{1,17},{17,1},{2,18},{18,2},{3,19},{19,3},{4,20},{20... | collective-permute-start | bytes 1105928 | tf_op jit(solution)/shard_map/ppermute | solution.py:268
  76.5 17.0 %collective-permute-start.13 = (f32[3,512,128]{2,1,0:T(8,128)}, f32[3,512,128]{2,1,0:T(8,128)}, u32[]{:S(2)}, u32[]{:S(2)}) collective-permute-start(f32[3,512,128]{2,1,0:T(8,128)} %get-tuple-element.37), channel_id=1, source_target_pairs={{0,1},{1,0},{2,3},{3,2},{4,5},{5,4},{6,7},{7,6},{8,9},{9,8},{10,11... | collective-permute-start | bytes 2359304 | tf_op jit(solution)/shard_map/ppermute | solution.py:290
  77.4 16.0 %collective-permute-start.17 = (bf16[576,512]{1,0:T(8,128)(2,1)}, bf16[576,512]{1,0:T(8,128)(2,1)}, u32[]{:S(2)}, u32[]{:S(2)}) collective-permute-start(bf16[576,512]{1,0:T(8,128)(2,1)} %pad_maximum_fusion), channel_id=1, source_target_pairs={{0,2},{2,0},{1,3},{3,1},{4,6},{6,4},{5,7},{7,5},{8,10},{10,8},{9,1... | collective-permute-start | bytes 1769480 | tf_op jit(solution)/shard_map/ppermute | solution.py:324
  84.6 9.1 %copy-start.3 = (bf16[2,256,2048]{2,1,0:T(8,128)(2,1)S(1)}, bf16[2,256,2048]{2,1,0:T(8,128)(2,1)}, u32[]{:S(2)}) copy-start(bf16[2,256,2048]{2,1,0:T(8,128)(2,1)} %param.8) | copy-start | bytes 6291460
  84.6 9.1 %copy-start.13 = (f32[3,512,128]{2,1,0:T(8,128)S(1)}, f32[3,512,128]{2,1,0:T(8,128)}, u32[]{:S(2)}) copy-start(f32[3,512,128]{2,1,0:T(8,128)} %copy-done.12) | copy-start | bytes 2359300
  90.5 3.2 %collective-permute-start.14 = (f32[2,512,128]{2,1,0:T(8,128)S(1)}, f32[2,512,128]{2,1,0:T(8,128)S(1)}, u32[]{:S(2)}, u32[]{:S(2)}) collective-permute-start(f32[2,512,128]{2,1,0:T(8,128)S(1)} %get-tuple-element.38), channel_id=1, source_target_pairs={{0,1},{1,0},{2,3},{3,2},{4,5},{5,4},{6,7},{7,6},{8,9},{9,8},{10,11... | collective-permute-start | bytes 1572872 | tf_op jit(solution)/shard_map/ppermute | solution.py:290
  91.1 2.7 %collective-permute-start.15 = (f32[2,512,128]{2,1,0:T(8,128)S(1)}, f32[2,512,128]{2,1,0:T(8,128)S(1)}, u32[]{:S(2)}, u32[]{:S(2)}) collective-permute-start(f32[2,512,128]{2,1,0:T(8,128)S(1)} %get-tuple-element.39), channel_id=1, source_target_pairs={{0,1},{1,0},{2,3},{3,2},{4,5},{5,4},{6,7},{7,6},{8,9},{9,8},{10,11... | collective-permute-start | bytes 1572872 | tf_op jit(solution)/shard_map/ppermute | solution.py:290
  91.1 2.6 %collective-permute-start.16 = (f32[1,512,128]{2,1,0:T(8,128)S(1)}, f32[1,512,128]{2,1,0:T(8,128)S(1)}, u32[]{:S(2)}, u32[]{:S(2)}) collective-permute-start(f32[1,512,128]{2,1,0:T(8,128)S(1)} %get-tuple-element.40), channel_id=1, source_target_pairs={{0,1},{1,0},{2,3},{3,2},{4,5},{5,4},{6,7},{7,6},{8,9},{9,8},{10,11... | collective-permute-start | bytes 786440 | tf_op jit(solution)/shard_map/ppermute | solution.py:290
  96.5 7.0 %collective-permute-start.18 = (f32[1,136,128]{2,1,0:T(8,128)S(1)}, f32[1,136,128]{2,1,0:T(8,128)S(1)}, u32[]{:S(2)}, u32[]{:S(2)}) collective-permute-start(f32[1,136,128]{2,1,0:T(8,128)S(1)} %get-tuple-element.63), channel_id=1, source_target_pairs={{0,4},{4,8},{8,12},{12,0},{1,5},{5,9},{9,13},{13,1},{2,6},{6,10},{... | collective-permute-start | bytes 208904 | tf_op jit(solution)/shard_map/ppermute | solution.py:242
  96.6 9.0 %collective-permute-start.19 = (f32[1,136,128]{2,1,0:T(8,128)S(1)}, f32[1,136,128]{2,1,0:T(8,128)S(1)}, u32[]{:S(2)}, u32[]{:S(2)}) collective-permute-start(f32[1,136,128]{2,1,0:T(8,128)S(1)} %get-tuple-element.62), channel_id=1, source_target_pairs={{0,8},{4,12},{8,0},{12,4},{1,9},{5,13},{9,1},{13,5},{2,10},{6,14},... | collective-permute-start | bytes 208904 | tf_op jit(solution)/shard_map/ppermute | solution.py:242
  96.6 8.9 %collective-permute-start.20 = (f32[1,136,128]{2,1,0:T(8,128)S(1)}, f32[1,136,128]{2,1,0:T(8,128)S(1)}, u32[]{:S(2)}, u32[]{:S(2)}) collective-permute-start(f32[1,136,128]{2,1,0:T(8,128)S(1)} %get-tuple-element.61), channel_id=1, source_target_pairs={{0,12},{4,0},{8,4},{12,8},{1,13},{5,1},{9,5},{13,9},{2,14},{6,2},{... | collective-permute-start | bytes 208904 | tf_op jit(solution)/shard_map/ppermute | solution.py:242
  105.8 3.8 %collective-permute-start.22 = (bf16[1,16,512]{2,1,0:T(8,128)(2,1)S(1)}, bf16[1,16,512]{2,1,0:T(8,128)(2,1)S(1)}, u32[]{:S(2)}, u32[]{:S(2)}) collective-permute-start(bf16[1,16,512]{2,1,0:T(8,128)(2,1)S(1)} %get-tuple-element.75), channel_id=1, source_target_pairs={{0,2},{2,0},{1,3},{3,1},{4,6},{6,4},{5,7},{7,5},{8,10},{10,8},{9,1... | collective-permute-start | bytes 49160 | tf_op jit(solution)/shard_map/ppermute | solution.py:351
  107.6 3.2 %collective-permute-start.23 = (bf16[1,16,512]{2,1,0:T(8,128)(2,1)S(1)}, bf16[1,16,512]{2,1,0:T(8,128)(2,1)S(1)}, u32[]{:S(2)}, u32[]{:S(2)}) collective-permute-start(bf16[1,16,512]{2,1,0:T(8,128)(2,1)S(1)} %get-tuple-element.75), channel_id=1, source_target_pairs={{0,3},{3,0},{1,2},{2,1},{4,7},{7,4},{5,6},{6,5},{8,11},{11,8},{9,1... | collective-permute-start | bytes 49160 | tf_op jit(solution)/shard_map/ppermute | solution.py:352
  107.6 1.2 %collective-permute-start.21 = (bf16[1,16,512]{2,1,0:T(8,128)(2,1)S(1)}, bf16[1,16,512]{2,1,0:T(8,128)(2,1)S(1)}, u32[]{:S(2)}, u32[]{:S(2)}) collective-permute-start(bf16[1,16,512]{2,1,0:T(8,128)(2,1)S(1)} %get-tuple-element.76.mine_ref), channel_id=1, source_target_pairs={{0,1},{1,0},{2,3},{3,2},{4,5},{5,4},{6,7},{7,6},{8,9},{9,8},{10,11... | collective-permute-start | bytes 49160 | tf_op jit(solution)/shard_map/ppermute | solution.py:350
  (18 other events, 53.4 us)

commit v6 on v5

--- a/solution.py
+++ b/solution.py
@@ -25,39 +25,46 @@
     return picked
 
 
-def project_kernel(flag_ref, *refs, jobs, sends):
+def project_kernel(flag_ref, partner_ref, hidden_ref, *refs, blocks, sends):
+    *refs, rows_ref, semaphore = refs
     keep_ref, *send_refs = refs[-1 - len(sends) :]
     slots = [(ref, at) for ref in send_refs for at in range(ref.shape[0])]
     core, same = flag_ref[0], flag_ref[1]
     half = keep_ref.shape[2]
-    for at, (rows_of, blocks_of) in enumerate(jobs):
-        if len(blocks_of) == 1:
-            whole = refs[blocks_of[0][0]]
-            keep = whole[pl.ds(pl.multiple_of(core * half, half), half), :]
-            send = whole[pl.ds(pl.multiple_of((1 - core) * half, half), half), :]
-        else:
-            parts = [refs[block][:length] for block, length in blocks_of]
-            first, second = (
-                jnp.concatenate(part, axis=0) for part in (parts[: len(parts) // 2], parts[len(parts) // 2 :])
+    copy = pltpu.make_async_copy(partner_ref, rows_ref, semaphore)
+    copy.start()
+    for source in range(2):
+        if source == 1:
+            copy.wait()
+        for at, pieces in enumerate(blocks):
+            if len(pieces) == 1:
+                whole = refs[pieces[0][0]]
+                keep = whole[pl.ds(pl.multiple_of(core * half, half), half), :]
+                send = whole[pl.ds(pl.multiple_of((1 - core) * half, half), half), :]
+            else:
+                parts = [refs[piece][:length] for piece, length in pieces]
+                first, second = (
+                    jnp.concatenate(part, axis=0) for part in (parts[: len(parts) // 2], parts[len(parts) // 2 :])
+                )
+                keep = jnp.where(same == 1, first, second)
+                send = jnp.where(same == 1, second, first)
+            product = lax.dot_general(
+                (rows_ref if source else hidden_ref)[...],
+                jnp.concatenate([keep, send], axis=0),
+                (((1,), (1,)), ((), ())),
+                preferred_element_type=jnp.float32,
             )
-            keep = jnp.where(same == 1, first, second)
-            send = jnp.where(same == 1, second, first)
-        product = lax.dot_general(
-            refs[rows_of][...],
-            jnp.concatenate([keep, send], axis=0),
-            (((1,), (1,)), ((), ())),
-            preferred_element_type=jnp.float32,
-        )
-        keep_ref[at] = product[:, :half]
-        send_ref, slot = slots[at]
-        send_ref[slot] = product[:, half:]
+            keep_ref[source * len(blocks) + at] = product[:, :half]
+            send_ref, slot = slots[source * len(blocks) + at]
+            send_ref[slot] = product[:, half:]
 
 
 def attend_kernel(place_ref, spot_ref, query_ref, *refs, pieces):
     *refs, own_ref, partner_ref, out_ref, key_ref = refs
     residuals = own_ref, partner_ref
     partner_queries = own_ref.shape[0]
-    query_len, held = query_ref.shape[1:]
+    held = query_ref.shape[1]
+    query_len = query_ref.shape[0] // out_ref.shape[0]
     block_len = key_ref.shape[1]
     heads = held // HEAD_DIM
     tall = heads * query_len
@@ -84,8 +91,10 @@
     places, scores, tops = [], [], []
     for at in range(key_ref.shape[0]):
         place = place_ref[at]
-        first = pl.multiple_of(partner_queries + place // 2 * query_len, query_len)
-        query = jnp.where(place % 2 == 0, query_ref[place // 2], partner_ref[pl.ds(first, query_len), :])
+        first = pl.multiple_of(place // 2 * query_len, query_len)
+        own_query = query_ref[pl.ds(first, query_len), :]
+        partner_query = partner_ref[pl.ds(partner_queries + first, query_len), :]
+        query = jnp.where(place % 2 == 0, own_query, partner_query)
         query = jnp.concatenate([query] * heads, axis=0)
         query = jnp.where(diagonal, query, jnp.zeros_like(query))
         score = lax.dot_general(
@@ -184,18 +193,19 @@
     return [pl.BlockSpec(memory_space=pltpu.SMEM)] * count
 
 
-def project(flags, operands, jobs, sends, half, flops, name):
-    rows, units = operands[0].shape
-    shapes = [jax.ShapeDtypeStruct((count, rows, half), jnp.float32) for count in [len(jobs)] + sends]
+def project(flags, hidden, partner, weights, blocks, sends, half, name):
+    rows, units = hidden.shape
+    counts = [2 * len(blocks)] + sends
     return pl.pallas_call(
-        functools.partial(project_kernel, jobs=jobs, sends=sends),
-        out_shape=shapes,
-        in_specs=in_smem(1) + in_vmem(len(operands)),
-        out_specs=in_vmem(len(shapes)),
+        functools.partial(project_kernel, blocks=blocks, sends=sends),
+        out_shape=[jax.ShapeDtypeStruct((count, rows, half), jnp.float32) for count in counts],
+        in_specs=in_smem(1) + [pl.BlockSpec(memory_space=pl.ANY)] + in_vmem(1 + len(weights)),
+        out_specs=in_vmem(len(counts)),
+        scratch_shapes=[pltpu.VMEM((rows, units), hidden.dtype), pltpu.SemaphoreType.DMA(())],
         compiler_params=pltpu.CompilerParams(vmem_limit_bytes=VMEM_LIMIT),
-        cost_estimate=pl.CostEstimate(flops=flops, bytes_accessed=1, transcendentals=0),
+        cost_estimate=pl.CostEstimate(flops=1, bytes_accessed=1, transcendentals=0),
         name=name,
-    )(flags, *operands)
+    )(flags, partner, hidden, *weights)
 
 
 def after(array, earlier):
@@ -208,9 +218,13 @@
     return jnp.pad(spread, ((0, 0), (0, units - spread.shape[1])))
 
 
-def from_rows(spread, shape):
-    pieces = [spread[:, at : at + shape[-1]] for at in range(0, math.prod(shape) // 8, shape[-1])]
-    return jnp.concatenate(pieces, axis=0).reshape(shape)
+def from_rows(spreads, slot, shape):
+    taken = []
+    for spread in spreads:
+        for at in range(shape[0] // 8):
+            first = (slot * shape[0] // 8 + at) * shape[1]
+            taken.append(spread[-8:, first : first + shape[1]])
+    return jnp.concatenate(taken, axis=0)
 
 
 def body(hidden_states, passage_states, down_weight, block_question, question_owner, decoder_states):
@@ -255,45 +269,38 @@
             for first, length in zip((0, lengths[0]), lengths)
         ]
         sent[1] = jnp.concatenate([sent[1], with_rows(queries, units)], axis=0)
-        below = [shifted(sent[0], 1)]
-        sent = [after(piece, below) for piece in sent]
-        below.append(shifted(sent[1], 1))
-        above = [shifted(sent[0], -1)]
-        above.append(shifted(after(sent[1], above), -1))
+        below, above = [], []
+        for at in range(2):
+            below.append(shifted(after(sent[at], below[-1:]), 1))
+            above.append(shifted(after(sent[at], above[-1:]), -1))
         opposite = [shifted(after(below[0], below[1:]), 1), shifted(below[1], 1)]
-        around = [from_rows(piece[-1][-8:], queries.shape) for piece in (above, opposite, below)]
-        queries = jnp.concatenate([queries] + around, axis=0)
+        spreads = [sent[1], above[1], opposite[1], below[1]]
+        own_queries, partner_queries = (from_rows(spreads, slot, (query_len, held)) for slot in range(2))
         swapped = []
         for at, piece in enumerate([below[0], above[0], below[1], above[1]] + opposite):
             swapped.append(lax.ppermute(after(piece, swapped[max(at - 2, 0) : max(at - 1, 0)]), "groups", SWAP))
         weights = [down_weight] + above + swapped[1:4:2] + below + swapped[0:4:2] + opposite + swapped[4:]
         flags = jnp.stack([core, (group == core).astype(core.dtype)])
-        blocks_of = [[(1, shard)]] + [list(zip(range(at, at + 4), 2 * lengths)) for at in (2, 6, 10)]
+        blocks_of = [[(0, shard)]] + [list(zip(range(at, at + 4), 2 * lengths)) for at in (1, 5, 0)]
         spots = lax.rem(high + jnp.array([0, 1, 3, 2], jnp.int32), highs)
         spots = jnp.stack([(spots * 2 + side) * stride + core * span, spots * span])
         own_residual = passages
 
-        flags = after(flags, swapped[4:5])
         kept, *away = project(
-            flags, [hidden] + weights[:9], [(0, blocks_of[at]) for at in range(3)], [3], half, 1, "project_own"
+            flags, hidden, partner_hidden, weights[:9], blocks_of[:3], [2, 2, 2], half, "project_near"
         )
         flags, kept, *away = lax.optimization_barrier((flags, kept, *away))
         late_kept, *late_away = project(
-            flags,
-            [hidden] + weights + [partner_hidden],
-            [(14, blocks_of[at]) for at in range(4)] + [(0, blocks_of[3])],
-            [2, 2, 1],
-            half,
-            1,
-            "project_rest",
+            flags, hidden, partner_hidden, weights[9:], blocks_of[3:], [2], half, "project_far"
         )
         others = [lax.ppermute(piece, "mp", SWAP) for piece in away + late_away]
         summands = [kept, late_kept] + others
-        pieces = [(0, (0, at), (2, at), at) for at in range(3)] + [(0, (1, 4), (5, 0), 3)]
-        pieces += [(1, (1, at), (3 + at // 2, at % 2), at) for at in range(4)]
+        pieces = [(at // 3, (0, at), (2 + at // 2, at % 2), at % 3) for at in range(6)]
+        pieces += [(source, (1, source), (5, source), 3) for source in range(2)]
         origin = high
     else:
         queries = lax.all_gather(queries, ("high", "low"), axis=0, tiled=True)
+        own_queries, partner_queries = (queries[:, slot].reshape(-1, held) for slot in range(2))
         weight = lax.all_gather(down_weight, ("high", "low"), axis=0, tiled=True)
         weight = jnp.where(core == 0, weight, jnp.roll(weight, held, axis=0))
         spots = jnp.zeros((2, 1), jnp.int32)
@@ -320,7 +327,7 @@
         [lax.dynamic_slice_in_dim(owner_place, at, blocks) for at in (own_at, partner_at)]
     )
 
-    leaving = jnp.concatenate([leaving, queries[:, 1].reshape(-1, held)], axis=0)
+    leaving = jnp.concatenate([leaving, partner_queries], axis=0)
     partner = lax.ppermute(leaving, "side", SWAP)
     packed = (members, 2 * held // 128 * query_len + 8, 128)
     operands = summands + [own_residual, partner]
@@ -332,7 +339,7 @@
         scratch_shapes=[pltpu.VMEM((2 * blocks, block_len, held), jnp.bfloat16)],
         compiler_params=pltpu.CompilerParams(vmem_limit_bytes=VMEM_LIMIT),
         name="attend",
-    )(places, spots, queries[:, 0], *operands)
+    )(places, spots, own_queries, *operands)
     if lined:
         received = [partials[0:1]] + [shifted(partials[ahead : ahead + 1], ahead) for ahead in range(1, highs)]
     else:

time: 112 us -> 100 us (0.89)
  local copies, waits for them, and re-layouts: 14.3 us -> 5.25 us
  waiting for transfers between devices: 57 us -> 51.1 us
  starting transfers between devices: 24.1 us -> 26.5 us
    ppermute x9, waiting for transfers between devices: 36.8 us -> 23.3 us  [shifted(): lax.ppermute(array, 'high', [(at, (at + shift) % highs) for at in range(h...]
    unnamed x52 -> x13, local copies, waits for them, and re-layouts: 10.2 us -> 1.35 us
    ppermute x1, waiting for transfers between devices: 0.01 us -> 5.69 us  [body(): partner_hidden = lax.ppermute(hidden, 'side', SWAP)]
    ppermute x4, waiting for transfers between devices: 0.28 us -> 3.09 us  [body(): others = [lax.ppermute(piece, 'mp', SWAP) for piece in away + late_away]]
    ppermute x1, waiting for transfers between devices: 1.71 us -> 0.01 us  [body(): partner = lax.ppermute(leaving, 'side', SWAP)]
    ppermute x1, starting transfers between devices: 0.01 us -> 1.56 us  [body(): partner = lax.ppermute(leaving, 'side', SWAP)]
  transfers between devices with their start and end apart: 24 -> 24, of which waited for: 14 -> 17; matrix products, arithmetic and copies ran while one was open for 4% -> 6% of each run, Pallas kernels for 9% -> 11%
where the time goes in v6:
time: 100 us
  waiting for transfers between devices  51.1 us (51%)
  starting transfers between devices  26.5 us (26%)
  Pallas kernels  14.2 us (14%)
  local copies, waits for them, and re-layouts  5.25 us (5%)
  other arithmetic  2.89 us (3%)
    ppermute x9, waiting for transfers between devices, shifted(): lax.ppermute(array, 'high', [(at, (at + shift) % highs) for at in range(h...  23.3 us
    ppermute x6, waiting for transfers between devices, body(): lax.ppermute(after(piece, swapped[max(at - 2, 0):max(at - 1, 0)]), 'group...  16.4 us
    ppermute x9, starting transfers between devices, shifted(): lax.ppermute(array, 'high', [(at, (at + shift) % highs) for at in range(h...  13 us
    pallas_call x2, Pallas kernels, project(): pl.pallas_call(functools.partial(project_kernel, blocks=blocks, sends=sen...  10.8 us
    ppermute x6, starting transfers between devices, body(): lax.ppermute(after(piece, swapped[max(at - 2, 0):max(at - 1, 0)]), 'group...  6.96 us
    ppermute x1, waiting for transfers between devices, body(): partner_hidden = lax.ppermute(hidden, 'side', SWAP)  5.69 us
    ppermute x4, waiting for transfers between devices, body(): others = [lax.ppermute(piece, 'mp', SWAP) for piece in away + late_away]  3.09 us
    dynamic_slice x2, local copies, waits for them, and re-layouts, features(): lax.dynamic_slice_in_dim(array, start, span, axis=array.ndim - 1)  2.68 us
  transfers between devices with their start and end apart: 24, of which 17 were waited for; matrix products, arithmetic and copies ran while one was open for 6% of the time, Pallas kernels for 11%

profile of v6, /device:TPU:0, one launch (start us, length us, event | category | flops | bytes accessed | tf_op | source)
XLA Modules:
  0.0 100.1 jit_solution(15679527623399448484)
XLA Ops:
  0.0 1.1 %constant_dynamic-slice_fusion.4 = (bf16[64,2560]{1,0:T(8,128)(2,1)S(1)}, bf16[64,2560]{1,0:T(8,128)(2,1)S(1)}) fusion(bf16[256,2560]{1,0:T(8,128)(2,1)} %refs_0_.1, s32[]{:T(128)S(6)} %select_n.73, s32[]{:T(128)S(6)} %select_n.68), kind=kLoop, calls=%fused_computation.33 | loop fusion | bytes 1310728 | tf_op jit(solution)/shard_map/dynamic_slice | solution.py:268
  1.1 3.1 %collective-permute-start.2 = (bf16[64,2560]{1,0:T(8,128)(2,1)S(1)}, bf16[64,2560]{1,0:T(8,128)(2,1)}, u32[]{:S(2)}, u32[]{:S(2)}) collective-permute-start(bf16[64,2560]{1,0:T(8,128)(2,1)S(1)} %get-tuple-element.47), channel_id=1, source_target_pairs={{0,4},{4,8},{8,12},{12,0},{1,5},{5,9},{9,13},{13,1},{2,6},{6,10},{... | collective-permute-start | bytes 983048 | tf_op jit(solution)/shard_map/ppermute | solution.py:256
  4.2 2.1 %collective-permute-start = (bf16[64,2560]{1,0:T(8,128)(2,1)S(1)}, bf16[64,2560]{1,0:T(8,128)(2,1)}, u32[]{:S(2)}, u32[]{:S(2)}) collective-permute-start(bf16[64,2560]{1,0:T(8,128)(2,1)S(1)} %get-tuple-element.47), channel_id=1, source_target_pairs={{0,12},{4,0},{8,4},{12,8},{1,13},{5,1},{9,5},{13,9},{2,14},{6,2},{... | collective-permute-start | bytes 983048 | tf_op jit(solution)/shard_map/ppermute | solution.py:256
  6.3 1.6 %collective-permute-start.5 = (bf16[512,2560]{1,0:T(8,128)(2,1)}, bf16[512,2560]{1,0:T(8,128)(2,1)}, u32[]{:S(2)}, u32[]{:S(2)}) collective-permute-start(bf16[512,2560]{1,0:T(8,128)(2,1)} %bitcast.19), channel_id=1, source_target_pairs={{0,2},{2,0},{1,3},{3,1},{4,6},{6,4},{5,7},{7,5},{8,10},{10,8},{9,1... | collective-permute-start | bytes 7864328 | tf_op jit(solution)/shard_map/ppermute | solution.py:259
  9.6 1.9 %constant_dynamic-slice_fusion.3 = (bf16[512,128]{1,0:T(8,128)(2,1)S(1)}, bf16[512,128]{1,0:T(8,128)(2,1)}, bf16[512,128]{1,0:T(8,128)(2,1)}, bf16[512,128]{1,0:T(8,128)(2,1)}) fusion(bf16[512,2048]{1,0:T(8,128)(2,1)} %bitcast.22, s32[]{:T(128)S(6)} %select_n.69, s32[]{:T(128)S(6)} %select_n.72, s32[]{:T(128)S(6)} %select_n.71, s32[]{:T(128)S(6)} %select_n.70), kind=kLoop, calls=%fused_computation.32 | loop fusion | bytes 1048592 | tf_op jit(solution)/shard_map/dynamic_slice | solution.py:252
  12.2 2.7 %collective-permute-done.2.refs_5_ = bf16[64,2560]{1,0:T(8,128)(2,1)} collective-permute-done((bf16[64,2560]{1,0:T(8,128)(2,1)S(1)}, bf16[64,2560]{1,0:T(8,128)(2,1)}, u32[]{:S(2)}, u32[]{:S(2)}) %collective-permute-start.2) | collective-permute-done | bytes 327712 | tf_op jit(solution)/shard_map/ppermute | solution.py:256
  14.9 5.8 %collective-permute-done.refs_1_ = bf16[64,2560]{1,0:T(8,128)(2,1)} collective-permute-done((bf16[64,2560]{1,0:T(8,128)(2,1)S(1)}, bf16[64,2560]{1,0:T(8,128)(2,1)}, u32[]{:S(2)}, u32[]{:S(2)}) %collective-permute-start) | collective-permute-done | bytes 327712 | tf_op jit(solution)/shard_map/ppermute | solution.py:256
  20.7 3.1 %collective-permute-start.1 = (bf16[72,2560]{1,0:T(8,128)(2,1)}, bf16[72,2560]{1,0:T(8,128)(2,1)S(1)}, u32[]{:S(2)}, u32[]{:S(2)}) collective-permute-start(bf16[72,2560]{1,0:T(8,128)(2,1)} %pad_maximum_fusion), channel_id=1, source_target_pairs={{0,12},{4,0},{8,4},{12,8},{1,13},{5,1},{9,5},{13,9},{2,14},{6,2},{... | collective-permute-start | bytes 1105928 | tf_op jit(solution)/shard_map/ppermute | solution.py:256
  23.9 1.5 %collective-permute-start.8 = (bf16[64,2560]{1,0:T(8,128)(2,1)}, bf16[64,2560]{1,0:T(8,128)(2,1)S(1)}, u32[]{:S(2)}, u32[]{:S(2)}) collective-permute-start(bf16[64,2560]{1,0:T(8,128)(2,1)} %collective-permute-done.2.refs_5_), channel_id=1, source_target_pairs={{0,16},{16,0},{1,17},{17,1},{2,18},{18,2},{3,19},{19,3},{4,20},{20... | collective-permute-start | bytes 983048 | tf_op jit(solution)/shard_map/ppermute | solution.py:281
  26.0 1.1 %maximum_dynamic-update-slice_fusion = bf16[576,512]{1,0:T(8,128)(2,1)S(1)} fusion(bf16[512,128]{1,0:T(8,128)(2,1)} %get-tuple-element.44, bf16[512,128]{1,0:T(8,128)(2,1)} %get-tuple-element.45, bf16[512,128]{1,0:T(8,128)(2,1)} %get-tuple-element.46, bf16[512,128]{1,0:T(8,128)(2,1)S(1)} %get-tuple-element.43), kind=kLoop, calls=%fused_computation | loop fusion | flops 2097151 | bytes 1048576
  27.1 7.6 %collective-permute-done.8.refs_7_ = bf16[64,2560]{1,0:T(8,128)(2,1)S(1)} collective-permute-done((bf16[64,2560]{1,0:T(8,128)(2,1)}, bf16[64,2560]{1,0:T(8,128)(2,1)S(1)}, u32[]{:S(2)}, u32[]{:S(2)}) %collective-permute-start.8) | collective-permute-done | bytes 327712 | tf_op jit(solution)/shard_map/ppermute | solution.py:281
  34.7 1.5 %collective-permute-start.9 = (bf16[72,2560]{1,0:T(8,128)(2,1)S(1)}, bf16[72,2560]{1,0:T(8,128)(2,1)S(1)}, u32[]{:S(2)}, u32[]{:S(2)}) collective-permute-start(bf16[72,2560]{1,0:T(8,128)(2,1)S(1)} %collective-permute-done.3.refs_6_), channel_id=1, source_target_pairs={{0,16},{16,0},{1,17},{17,1},{2,18},{18,2},{3,19},{19,3},{4,20},{20... | collective-permute-start | bytes 1105928 | tf_op jit(solution)/shard_map/ppermute | solution.py:281
  36.2 5.5 %collective-permute-done.6.refs_3_ = bf16[64,2560]{1,0:T(8,128)(2,1)S(1)} collective-permute-done((bf16[64,2560]{1,0:T(8,128)(2,1)}, bf16[64,2560]{1,0:T(8,128)(2,1)S(1)}, u32[]{:S(2)}, u32[]{:S(2)}) %collective-permute-start.6) | collective-permute-done | bytes 327712 | tf_op jit(solution)/shard_map/ppermute | solution.py:281
  41.7 1.5 %collective-permute-start.7 = (bf16[72,2560]{1,0:T(8,128)(2,1)S(1)}, bf16[72,2560]{1,0:T(8,128)(2,1)S(1)}, u32[]{:S(2)}, u32[]{:S(2)}) collective-permute-start(bf16[72,2560]{1,0:T(8,128)(2,1)S(1)} %collective-permute-done.1.refs_2_), channel_id=1, source_target_pairs={{0,16},{16,0},{1,17},{17,1},{2,18},{18,2},{3,19},{19,3},{4,20},{20... | collective-permute-start | bytes 1105928 | tf_op jit(solution)/shard_map/ppermute | solution.py:281
  43.3 0.9 collective-permute-start.4
  44.2 9.6 %collective-permute-done.10.refs_0_ = bf16[64,2560]{1,0:T(8,128)(2,1)S(1)} collective-permute-done((bf16[64,2560]{1,0:T(8,128)(2,1)}, bf16[64,2560]{1,0:T(8,128)(2,1)S(1)}, u32[]{:S(2)}, u32[]{:S(2)}) %collective-permute-start.10) | collective-permute-done | bytes 327712 | tf_op jit(solution)/shard_map/ppermute | solution.py:256
  54.3 3.3 %collective-permute-done.7.refs_4_ = bf16[72,2560]{1,0:T(8,128)(2,1)S(1)} collective-permute-done((bf16[72,2560]{1,0:T(8,128)(2,1)S(1)}, bf16[72,2560]{1,0:T(8,128)(2,1)S(1)}, u32[]{:S(2)}, u32[]{:S(2)}) %collective-permute-start.7) | collective-permute-done | bytes 368672 | tf_op jit(solution)/shard_map/ppermute | solution.py:281
  57.7 1.4 %collective-permute-start.12 = (bf16[72,2560]{1,0:T(8,128)(2,1)S(1)}, bf16[72,2560]{1,0:T(8,128)(2,1)S(1)}, u32[]{:S(2)}, u32[]{:S(2)}) collective-permute-start(bf16[72,2560]{1,0:T(8,128)(2,1)S(1)} %collective-permute-done.4.refs_1_), channel_id=1, source_target_pairs={{0,16},{16,0},{1,17},{17,1},{2,18},{18,2},{3,19},{19,3},{4,20},{20... | collective-permute-start | bytes 1105928 | tf_op jit(solution)/shard_map/ppermute | solution.py:281
  59.1 1.6 %collective-permute-start.17 = (bf16[576,512]{1,0:T(8,128)(2,1)S(1)}, bf16[576,512]{1,0:T(8,128)(2,1)S(1)}, u32[]{:S(2)}, u32[]{:S(2)}) collective-permute-start(bf16[576,512]{1,0:T(8,128)(2,1)S(1)} %get-tuple-element.49), channel_id=1, source_target_pairs={{0,2},{2,0},{1,3},{3,1},{4,6},{6,4},{5,7},{7,5},{8,10},{10,8},{9,1... | collective-permute-start | bytes 1769480 | tf_op jit(solution)/shard_map/ppermute | solution.py:331
  60.7 5.7 %collective-permute-done.5.partner_ref = bf16[512,2560]{1,0:T(8,128)(2,1)} collective-permute-done((bf16[512,2560]{1,0:T(8,128)(2,1)}, bf16[512,2560]{1,0:T(8,128)(2,1)}, u32[]{:S(2)}, u32[]{:S(2)}) %collective-permute-start.5) | collective-permute-done | bytes 2621472 | tf_op jit(solution)/shard_map/ppermute | solution.py:259
  66.4 1.3 %copy-done.2 = bf16[256,2560]{1,0:T(8,128)(2,1)S(1)} copy-done((bf16[256,2560]{1,0:T(8,128)(2,1)S(1)}, bf16[256,2560]{1,0:T(8,128)(2,1)}, u32[]{:S(2)}) %copy-start.2) | copy-done | bytes 1310744
  67.7 6.9 %project_near.1 = (f32[6,512,128]{2,1,0:T(8,128)S(1)}, f32[2,512,128]{2,1,0:T(8,128)S(1)}, f32[2,512,128]{2,1,0:T(8,128)S(1)}, f32[2,512,128]{2,1,0:T(8,128)S(1)}) custom-call(s32[2]{0:T(128)S(1)} %pad_add_fusion.3.flag_ref, bf16[512,2560]{1,0:T(8,128)(2,1)} %collective-permute-done.5.partner_ref, bf16[512,2560]{1,0:T(8,128)(2,1)S(1)} %bitcast.20, ...), custom_call_target="tpu_custom_call" | custom-call | flops 1 | bytes 1 | tf_op jit(solution)/shard_map/project_near/pallas_call | solution.py:199
  74.6 3.9 %project_far.1 = (f32[2,512,128]{2,1,0:T(8,128)S(1)}, f32[2,512,128]{2,1,0:T(8,128)S(1)}) custom-call(s32[2]{0:T(128)S(1)} %pad_add_fusion.3.flag_ref, bf16[512,2560]{1,0:T(8,128)(2,1)} %collective-permute-done.5.partner_ref, bf16[512,2560]{1,0:T(8,128)(2,1)S(1)} %bitcast.21, bf16[64,2560]{1,0:T(8,128)(2,1)S(1)} %collective-permute-done.10.refs_0_, ...), custom_call_target="tpu_custom_call" | custom-call | flops 1 | bytes 1 | tf_op jit(solution)/shard_map/project_far/pallas_call | solution.py:199
  79.7 0.8 collective-permute-done.16.refs_5_
  82.8 2.0 %attend.1 = f32[4,136,128]{2,1,0:T(8,128)S(1)} custom-call(s32[4]{0:T(128)S(1)} %pad_add_fusion.2.place_ref, s32[2,4]{1,0:T(2,128)S(1)} %pad_add_fusion.spot_ref, bf16[64,512]{1,0:T(8,128)(2,1)S(1)} %get-tuple-element.50.query_ref, f32[6,512,128]{2,1,0:T(8,128)S(1)} %get-tuple-element.31.refs_0_, f32[2,512,128]{2,1,0:T(8,128)S(1)} %get-tuple-element.36.refs_1_, ...), custom_call_target="tpu_custom_call" | custom-call | tf_op jit(solution)/shard_map/attend/pallas_call | solution.py:334
  84.9 2.5 %collective-permute-start.19 = (f32[1,136,128]{2,1,0:T(8,128)S(1)}, f32[1,136,128]{2,1,0:T(8,128)S(1)}, u32[]{:S(2)}, u32[]{:S(2)}) collective-permute-start(f32[1,136,128]{2,1,0:T(8,128)S(1)} %get-tuple-element.62), channel_id=1, source_target_pairs={{0,8},{4,12},{8,0},{12,4},{1,9},{5,13},{9,1},{13,5},{2,10},{6,14},... | collective-permute-start | bytes 208904 | tf_op jit(solution)/shard_map/ppermute | solution.py:256
  87.4 1.3 %collective-permute-start.20 = (f32[1,136,128]{2,1,0:T(8,128)S(1)}, f32[1,136,128]{2,1,0:T(8,128)S(1)}, u32[]{:S(2)}, u32[]{:S(2)}) collective-permute-start(f32[1,136,128]{2,1,0:T(8,128)S(1)} %get-tuple-element.61), channel_id=1, source_target_pairs={{0,12},{4,0},{8,4},{12,8},{1,13},{5,1},{9,5},{13,9},{2,14},{6,2},{... | collective-permute-start | bytes 208904 | tf_op jit(solution)/shard_map/ppermute | solution.py:256
  88.7 3.0 %collective-permute-done.18.refs_1_ = f32[1,136,128]{2,1,0:T(8,128)S(1)} collective-permute-done((f32[1,136,128]{2,1,0:T(8,128)S(1)}, f32[1,136,128]{2,1,0:T(8,128)S(1)}, u32[]{:S(2)}, u32[]{:S(2)}) %collective-permute-start.18) | collective-permute-done | bytes 69664 | tf_op jit(solution)/shard_map/ppermute | solution.py:256
  91.7 2.0 %collective-permute-done.19.refs_2_ = f32[1,136,128]{2,1,0:T(8,128)S(1)} collective-permute-done((f32[1,136,128]{2,1,0:T(8,128)S(1)}, f32[1,136,128]{2,1,0:T(8,128)S(1)}, u32[]{:S(2)}, u32[]{:S(2)}) %collective-permute-start.19) | collective-permute-done | bytes 69664 | tf_op jit(solution)/shard_map/ppermute | solution.py:256
  94.0 1.7 %collective-permute-start.22 = (bf16[1,16,512]{2,1,0:T(8,128)(2,1)S(1)}, bf16[1,16,512]{2,1,0:T(8,128)(2,1)S(1)}, u32[]{:S(2)}, u32[]{:S(2)}) collective-permute-start(bf16[1,16,512]{2,1,0:T(8,128)(2,1)S(1)} %get-tuple-element.73), channel_id=1, source_target_pairs={{0,2},{2,0},{1,3},{3,1},{4,6},{6,4},{5,7},{7,5},{8,10},{10,8},{9,1... | collective-permute-start | bytes 49160 | tf_op jit(solution)/shard_map/ppermute | solution.py:358
  97.8 1.1 %collective-permute-done.23.both_ref = bf16[1,16,512]{2,1,0:T(8,128)(2,1)S(1)} collective-permute-done((bf16[1,16,512]{2,1,0:T(8,128)(2,1)S(1)}, bf16[1,16,512]{2,1,0:T(8,128)(2,1)S(1)}, u32[]{:S(2)}, u32[]{:S(2)}) %collective-permute-start.23) | collective-permute-done | bytes 16416 | tf_op jit(solution)/shard_map/ppermute | solution.py:359
  98.9 1.2 %assemble.1 = bf16[1,16,2048]{2,1,0:T(8,128)(2,1)} custom-call(s32[2]{0:T(128)S(1)} %pad_add_fusion.1.flag_ref, bf16[1,16,512]{2,1,0:T(8,128)(2,1)S(1)} %get-tuple-element.74.mine_ref, bf16[1,16,512]{2,1,0:T(8,128)(2,1)S(1)} %collective-permute-done.21.core_ref, bf16[1,16,512]{2,1,0:T(8,128)(2,1)S(1)} %collective-permute-done.22.side_ref, ...), custom_call_target="tpu_custom_call" | custom-call | tf_op jit(solution)/shard_map/assemble/pallas_call | solution.py:366
  (55 shorter events, 9.6 us)
Async XLA Ops:
  1.1 65.3 %copy-start = (bf16[2,256,2560]{2,1,0:T(8,128)(2,1)S(1)}, bf16[2,256,2560]{2,1,0:T(8,128)(2,1)}, u32[]{:S(2)}) copy-start(bf16[2,256,2560]{2,1,0:T(8,128)(2,1)} %param.7) | copy-start | bytes 7864324
  1.1 13.8 %collective-permute-start.2 = (bf16[64,2560]{1,0:T(8,128)(2,1)S(1)}, bf16[64,2560]{1,0:T(8,128)(2,1)}, u32[]{:S(2)}, u32[]{:S(2)}) collective-permute-start(bf16[64,2560]{1,0:T(8,128)(2,1)S(1)} %get-tuple-element.47), channel_id=1, source_target_pairs={{0,4},{4,8},{8,12},{12,0},{1,5},{5,9},{9,13},{13,1},{2,6},{6,10},{... | collective-permute-start | bytes 983048 | tf_op jit(solution)/shard_map/ppermute | solution.py:256
  4.2 16.5 %collective-permute-start = (bf16[64,2560]{1,0:T(8,128)(2,1)S(1)}, bf16[64,2560]{1,0:T(8,128)(2,1)}, u32[]{:S(2)}, u32[]{:S(2)}) collective-permute-start(bf16[64,2560]{1,0:T(8,128)(2,1)S(1)} %get-tuple-element.47), channel_id=1, source_target_pairs={{0,12},{4,0},{8,4},{12,8},{1,13},{5,1},{9,5},{13,9},{2,14},{6,2},{... | collective-permute-start | bytes 983048 | tf_op jit(solution)/shard_map/ppermute | solution.py:256
  6.3 60.1 %collective-permute-start.5 = (bf16[512,2560]{1,0:T(8,128)(2,1)}, bf16[512,2560]{1,0:T(8,128)(2,1)}, u32[]{:S(2)}, u32[]{:S(2)}) collective-permute-start(bf16[512,2560]{1,0:T(8,128)(2,1)} %bitcast.19), channel_id=1, source_target_pairs={{0,2},{2,0},{1,3},{3,1},{4,6},{6,4},{5,7},{7,5},{8,10},{10,8},{9,1... | collective-permute-start | bytes 7864328 | tf_op jit(solution)/shard_map/ppermute | solution.py:259
  14.9 19.8 %collective-permute-start.3 = (bf16[72,2560]{1,0:T(8,128)(2,1)}, bf16[72,2560]{1,0:T(8,128)(2,1)S(1)}, u32[]{:S(2)}, u32[]{:S(2)}) collective-permute-start(bf16[72,2560]{1,0:T(8,128)(2,1)} %pad_maximum_fusion), channel_id=1, source_target_pairs={{0,4},{4,8},{8,12},{12,0},{1,5},{5,9},{9,13},{13,1},{2,6},{6,10},{... | collective-permute-start | bytes 1105928 | tf_op jit(solution)/shard_map/ppermute | solution.py:256
  20.7 21.0 %collective-permute-start.1 = (bf16[72,2560]{1,0:T(8,128)(2,1)}, bf16[72,2560]{1,0:T(8,128)(2,1)S(1)}, u32[]{:S(2)}, u32[]{:S(2)}) collective-permute-start(bf16[72,2560]{1,0:T(8,128)(2,1)} %pad_maximum_fusion), channel_id=1, source_target_pairs={{0,12},{4,0},{8,4},{12,8},{1,13},{5,1},{9,5},{13,9},{2,14},{6,2},{... | collective-permute-start | bytes 1105928 | tf_op jit(solution)/shard_map/ppermute | solution.py:256
  23.9 10.9 %collective-permute-start.8 = (bf16[64,2560]{1,0:T(8,128)(2,1)}, bf16[64,2560]{1,0:T(8,128)(2,1)S(1)}, u32[]{:S(2)}, u32[]{:S(2)}) collective-permute-start(bf16[64,2560]{1,0:T(8,128)(2,1)} %collective-permute-done.2.refs_5_), channel_id=1, source_target_pairs={{0,16},{16,0},{1,17},{17,1},{2,18},{18,2},{3,19},{19,3},{4,20},{20... | collective-permute-start | bytes 983048 | tf_op jit(solution)/shard_map/ppermute | solution.py:281
  25.4 16.4 %collective-permute-start.6 = (bf16[64,2560]{1,0:T(8,128)(2,1)}, bf16[64,2560]{1,0:T(8,128)(2,1)S(1)}, u32[]{:S(2)}, u32[]{:S(2)}) collective-permute-start(bf16[64,2560]{1,0:T(8,128)(2,1)} %collective-permute-done.refs_1_), channel_id=1, source_target_pairs={{0,16},{16,0},{1,17},{17,1},{2,18},{18,2},{3,19},{19,3},{4,20},{20... | collective-permute-start | bytes 983048 | tf_op jit(solution)/shard_map/ppermute | solution.py:281
  34.7 19.0 %collective-permute-start.9 = (bf16[72,2560]{1,0:T(8,128)(2,1)S(1)}, bf16[72,2560]{1,0:T(8,128)(2,1)S(1)}, u32[]{:S(2)}, u32[]{:S(2)}) collective-permute-start(bf16[72,2560]{1,0:T(8,128)(2,1)S(1)} %collective-permute-done.3.refs_6_), channel_id=1, source_target_pairs={{0,16},{16,0},{1,17},{17,1},{2,18},{18,2},{3,19},{19,3},{4,20},{20... | collective-permute-start | bytes 1105928 | tf_op jit(solution)/shard_map/ppermute | solution.py:281
  41.7 15.8 %collective-permute-start.7 = (bf16[72,2560]{1,0:T(8,128)(2,1)S(1)}, bf16[72,2560]{1,0:T(8,128)(2,1)S(1)}, u32[]{:S(2)}, u32[]{:S(2)}) collective-permute-start(bf16[72,2560]{1,0:T(8,128)(2,1)S(1)} %collective-permute-done.1.refs_2_), channel_id=1, source_target_pairs={{0,16},{16,0},{1,17},{17,1},{2,18},{18,2},{3,19},{19,3},{4,20},{20... | collective-permute-start | bytes 1105928 | tf_op jit(solution)/shard_map/ppermute | solution.py:281
  43.3 10.5 %collective-permute-start.10 = (bf16[64,2560]{1,0:T(8,128)(2,1)}, bf16[64,2560]{1,0:T(8,128)(2,1)S(1)}, u32[]{:S(2)}, u32[]{:S(2)}) collective-permute-start(bf16[64,2560]{1,0:T(8,128)(2,1)} %collective-permute-done.2.refs_5_), channel_id=1, source_target_pairs={{0,4},{4,8},{8,12},{12,0},{1,5},{5,9},{9,13},{13,1},{2,6},{6,10},{... | collective-permute-start | bytes 983048 | tf_op jit(solution)/shard_map/ppermute | solution.py:256
  43.3 14.4 %collective-permute-start.4 = (bf16[72,2560]{1,0:T(8,128)(2,1)S(1)}, bf16[72,2560]{1,0:T(8,128)(2,1)S(1)}, u32[]{:S(2)}, u32[]{:S(2)}) collective-permute-start(bf16[72,2560]{1,0:T(8,128)(2,1)S(1)} %collective-permute-done.3.refs_6_), channel_id=1, source_target_pairs={{0,4},{4,8},{8,12},{12,0},{1,5},{5,9},{9,13},{13,1},{2,6},{6,10},{... | collective-permute-start | bytes 1105928 | tf_op jit(solution)/shard_map/ppermute | solution.py:256
  53.7 20.9 %collective-permute-start.11 = (bf16[64,2560]{1,0:T(8,128)(2,1)S(1)}, bf16[64,2560]{1,0:T(8,128)(2,1)S(1)}, u32[]{:S(2)}, u32[]{:S(2)}) collective-permute-start(bf16[64,2560]{1,0:T(8,128)(2,1)S(1)} %collective-permute-done.10.refs_0_), channel_id=1, source_target_pairs={{0,16},{16,0},{1,17},{17,1},{2,18},{18,2},{3,19},{19,3},{4,20},{20... | collective-permute-start | bytes 983048 | tf_op jit(solution)/shard_map/ppermute | solution.py:281
  57.7 16.9 %collective-permute-start.12 = (bf16[72,2560]{1,0:T(8,128)(2,1)S(1)}, bf16[72,2560]{1,0:T(8,128)(2,1)S(1)}, u32[]{:S(2)}, u32[]{:S(2)}) collective-permute-start(bf16[72,2560]{1,0:T(8,128)(2,1)S(1)} %collective-permute-done.4.refs_1_), channel_id=1, source_target_pairs={{0,16},{16,0},{1,17},{17,1},{2,18},{18,2},{3,19},{19,3},{4,20},{20... | collective-permute-start | bytes 1105928 | tf_op jit(solution)/shard_map/ppermute | solution.py:281
  59.1 20.6 %collective-permute-start.17 = (bf16[576,512]{1,0:T(8,128)(2,1)S(1)}, bf16[576,512]{1,0:T(8,128)(2,1)S(1)}, u32[]{:S(2)}, u32[]{:S(2)}) collective-permute-start(bf16[576,512]{1,0:T(8,128)(2,1)S(1)} %get-tuple-element.49), channel_id=1, source_target_pairs={{0,2},{2,0},{1,3},{3,1},{4,6},{6,4},{5,7},{7,5},{8,10},{10,8},{9,1... | collective-permute-start | bytes 1769480 | tf_op jit(solution)/shard_map/ppermute | solution.py:331
  66.4 1.3 %copy-start.2 = (bf16[256,2560]{1,0:T(8,128)(2,1)S(1)}, bf16[256,2560]{1,0:T(8,128)(2,1)}, u32[]{:S(2)}) copy-start(bf16[256,2560]{1,0:T(8,128)(2,1)} %refs_0_.1) | copy-start | bytes 3932164
  74.6 5.0 %copy-start.3 = (s32[4]{0:T(128)S(1)}, s32[4]{0:T(128)}, u32[]{:S(2)}) copy-start(s32[4]{0:T(128)} %constant.97.clone) | copy-start | bytes 52
  74.6 8.2 %copy-start.1 = (bf16[2,256,2048]{2,1,0:T(8,128)(2,1)S(1)}, bf16[2,256,2048]{2,1,0:T(8,128)(2,1)}, u32[]{:S(2)}) copy-start(bf16[2,256,2048]{2,1,0:T(8,128)(2,1)} %param.8) | copy-start | bytes 6291460
  78.5 2.0 %collective-permute-start.16 = (f32[2,512,128]{2,1,0:T(8,128)S(1)}, f32[2,512,128]{2,1,0:T(8,128)S(1)}, u32[]{:S(2)}, u32[]{:S(2)}) collective-permute-start(f32[2,512,128]{2,1,0:T(8,128)S(1)} %get-tuple-element.40), channel_id=1, source_target_pairs={{0,1},{1,0},{2,3},{3,2},{4,5},{5,4},{6,7},{7,6},{8,9},{9,8},{10,11... | collective-permute-start | bytes 1572872 | tf_op jit(solution)/shard_map/ppermute | solution.py:296
  78.6 2.6 %collective-permute-start.13 = (f32[2,512,128]{2,1,0:T(8,128)S(1)}, f32[2,512,128]{2,1,0:T(8,128)S(1)}, u32[]{:S(2)}, u32[]{:S(2)}) collective-permute-start(f32[2,512,128]{2,1,0:T(8,128)S(1)} %get-tuple-element.37), channel_id=1, source_target_pairs={{0,1},{1,0},{2,3},{3,2},{4,5},{5,4},{6,7},{7,6},{8,9},{9,8},{10,11... | collective-permute-start | bytes 1572872 | tf_op jit(solution)/shard_map/ppermute | solution.py:296
  79.1 2.9 %collective-permute-start.14 = (f32[2,512,128]{2,1,0:T(8,128)S(1)}, f32[2,512,128]{2,1,0:T(8,128)S(1)}, u32[]{:S(2)}, u32[]{:S(2)}) collective-permute-start(f32[2,512,128]{2,1,0:T(8,128)S(1)} %get-tuple-element.38), channel_id=1, source_target_pairs={{0,1},{1,0},{2,3},{3,2},{4,5},{5,4},{6,7},{7,6},{8,9},{9,8},{10,11... | collective-permute-start | bytes 1572872 | tf_op jit(solution)/shard_map/ppermute | solution.py:296
  79.2 3.6 %collective-permute-start.15 = (f32[2,512,128]{2,1,0:T(8,128)S(1)}, f32[2,512,128]{2,1,0:T(8,128)S(1)}, u32[]{:S(2)}, u32[]{:S(2)}) collective-permute-start(f32[2,512,128]{2,1,0:T(8,128)S(1)} %get-tuple-element.39), channel_id=1, source_target_pairs={{0,1},{1,0},{2,3},{3,2},{4,5},{5,4},{6,7},{7,6},{8,9},{9,8},{10,11... | collective-permute-start | bytes 1572872 | tf_op jit(solution)/shard_map/ppermute | solution.py:296
  84.8 6.9 %collective-permute-start.18 = (f32[1,136,128]{2,1,0:T(8,128)S(1)}, f32[1,136,128]{2,1,0:T(8,128)S(1)}, u32[]{:S(2)}, u32[]{:S(2)}) collective-permute-start(f32[1,136,128]{2,1,0:T(8,128)S(1)} %get-tuple-element.63), channel_id=1, source_target_pairs={{0,4},{4,8},{8,12},{12,0},{1,5},{5,9},{9,13},{13,1},{2,6},{6,10},{... | collective-permute-start | bytes 208904 | tf_op jit(solution)/shard_map/ppermute | solution.py:256
  84.9 8.9 %collective-permute-start.19 = (f32[1,136,128]{2,1,0:T(8,128)S(1)}, f32[1,136,128]{2,1,0:T(8,128)S(1)}, u32[]{:S(2)}, u32[]{:S(2)}) collective-permute-start(f32[1,136,128]{2,1,0:T(8,128)S(1)} %get-tuple-element.62), channel_id=1, source_target_pairs={{0,8},{4,12},{8,0},{12,4},{1,9},{5,13},{9,1},{13,5},{2,10},{6,14},... | collective-permute-start | bytes 208904 | tf_op jit(solution)/shard_map/ppermute | solution.py:256
  87.4 6.4 %collective-permute-start.20 = (f32[1,136,128]{2,1,0:T(8,128)S(1)}, f32[1,136,128]{2,1,0:T(8,128)S(1)}, u32[]{:S(2)}, u32[]{:S(2)}) collective-permute-start(f32[1,136,128]{2,1,0:T(8,128)S(1)} %get-tuple-element.61), channel_id=1, source_target_pairs={{0,12},{4,0},{8,4},{12,8},{1,13},{5,1},{9,5},{13,9},{2,14},{6,2},{... | collective-permute-start | bytes 208904 | tf_op jit(solution)/shard_map/ppermute | solution.py:256
  94.0 3.8 %collective-permute-start.22 = (bf16[1,16,512]{2,1,0:T(8,128)(2,1)S(1)}, bf16[1,16,512]{2,1,0:T(8,128)(2,1)S(1)}, u32[]{:S(2)}, u32[]{:S(2)}) collective-permute-start(bf16[1,16,512]{2,1,0:T(8,128)(2,1)S(1)} %get-tuple-element.73), channel_id=1, source_target_pairs={{0,2},{2,0},{1,3},{3,1},{4,6},{6,4},{5,7},{7,5},{8,10},{10,8},{9,1... | collective-permute-start | bytes 49160 | tf_op jit(solution)/shard_map/ppermute | solution.py:358
  95.7 3.2 %collective-permute-start.23 = (bf16[1,16,512]{2,1,0:T(8,128)(2,1)S(1)}, bf16[1,16,512]{2,1,0:T(8,128)(2,1)S(1)}, u32[]{:S(2)}, u32[]{:S(2)}) collective-permute-start(bf16[1,16,512]{2,1,0:T(8,128)(2,1)S(1)} %get-tuple-element.73), channel_id=1, source_target_pairs={{0,3},{3,0},{1,2},{2,1},{4,7},{7,4},{5,6},{6,5},{8,11},{11,8},{9,1... | collective-permute-start | bytes 49160 | tf_op jit(solution)/shard_map/ppermute | solution.py:359
  95.8 1.3 %collective-permute-start.21 = (bf16[1,16,512]{2,1,0:T(8,128)(2,1)S(1)}, bf16[1,16,512]{2,1,0:T(8,128)(2,1)S(1)}, u32[]{:S(2)}, u32[]{:S(2)}) collective-permute-start(bf16[1,16,512]{2,1,0:T(8,128)(2,1)S(1)} %get-tuple-element.74.mine_ref), channel_id=1, source_target_pairs={{0,1},{1,0},{2,3},{3,2},{4,5},{5,4},{6,7},{7,6},{8,9},{9,8},{10,11... | collective-permute-start | bytes 49160 | tf_op jit(solution)/shard_map/ppermute | solution.py:357

commit v7 on v6

--- a/solution.py
+++ b/solution.py
@@ -25,16 +25,23 @@
     return picked
 
 
-def project_kernel(flag_ref, partner_ref, hidden_ref, *refs, blocks, sends):
-    *refs, rows_ref, semaphore = refs
+def project_kernel(flag_ref, hidden_ref, partner_ref, *refs, blocks, sends, copies):
+    waiting = []
+    if copies:
+        *refs, semaphores = refs
+        *refs, rows_ref = refs
+        step = partner_ref.shape[1] // copies
+        for at in range(copies):
+            rows = pl.ds(at * step, step)
+            waiting.append(pltpu.make_async_copy(partner_ref.at[flag_ref[2], rows], rows_ref.at[rows], semaphores.at[at]))
+            waiting[-1].start()
+        partner_ref = rows_ref
     keep_ref, *send_refs = refs[-1 - len(sends) :]
     slots = [(ref, at) for ref in send_refs for at in range(ref.shape[0])]
     core, same = flag_ref[0], flag_ref[1]
     half = keep_ref.shape[2]
-    copy = pltpu.make_async_copy(partner_ref, rows_ref, semaphore)
-    copy.start()
     for source in range(2):
-        if source == 1:
+        for copy in waiting if source else []:
             copy.wait()
         for at, pieces in enumerate(blocks):
             if len(pieces) == 1:
@@ -49,7 +56,7 @@
                 keep = jnp.where(same == 1, first, second)
                 send = jnp.where(same == 1, second, first)
             product = lax.dot_general(
-                (rows_ref if source else hidden_ref)[...],
+                (partner_ref if source else hidden_ref)[...],
                 jnp.concatenate([keep, send], axis=0),
                 (((1,), (1,)), ((), ())),
                 preferred_element_type=jnp.float32,
@@ -193,19 +200,22 @@
     return [pl.BlockSpec(memory_space=pltpu.SMEM)] * count
 
 
-def project(flags, hidden, partner, weights, blocks, sends, half, name):
+def project(flags, hidden, partner, weights, blocks, sends, half, copies, name):
     rows, units = hidden.shape
-    counts = [2 * len(blocks)] + sends
+    shapes = [jax.ShapeDtypeStruct((count, rows, half), jnp.float32) for count in [2 * len(blocks)] + sends]
+    if copies:
+        shapes.append(jax.ShapeDtypeStruct((rows, units), hidden.dtype))
+    held = [pl.BlockSpec(memory_space=pl.ANY)] if copies else in_vmem(1)
     return pl.pallas_call(
-        functools.partial(project_kernel, blocks=blocks, sends=sends),
-        out_shape=[jax.ShapeDtypeStruct((count, rows, half), jnp.float32) for count in counts],
-        in_specs=in_smem(1) + [pl.BlockSpec(memory_space=pl.ANY)] + in_vmem(1 + len(weights)),
-        out_specs=in_vmem(len(counts)),
-        scratch_shapes=[pltpu.VMEM((rows, units), hidden.dtype), pltpu.SemaphoreType.DMA(())],
+        functools.partial(project_kernel, blocks=blocks, sends=sends, copies=copies),
+        out_shape=shapes,
+        in_specs=in_smem(1) + in_vmem(1) + held + in_vmem(len(weights)),
+        out_specs=in_vmem(len(shapes)),
+        scratch_shapes=[pltpu.SemaphoreType.DMA((copies,))] if copies else [],
         compiler_params=pltpu.CompilerParams(vmem_limit_bytes=VMEM_LIMIT),
         cost_estimate=pl.CostEstimate(flops=1, bytes_accessed=1, transcendentals=0),
         name=name,
-    )(flags, partner, hidden, *weights)
+    )(flags, hidden, partner, *weights)
 
 
 def after(array, earlier):
@@ -256,7 +266,7 @@
         return lax.ppermute(array, "high", [(at, (at + shift) % highs) for at in range(highs)])
 
     hidden = hidden_states.reshape(rows, units)
-    partner_hidden = lax.ppermute(hidden, "side", SWAP)
+    partner_hidden = lax.all_gather(hidden, "side")
     queries = jnp.concatenate([features(decoder_states, side), features(decoder_states, 1 - side)], axis=0)[None]
     passages = passage_states.reshape(rows, width)
     leaving = features(passages, 1 - side)
@@ -276,22 +286,24 @@
         opposite = [shifted(after(below[0], below[1:]), 1), shifted(below[1], 1)]
         spreads = [sent[1], above[1], opposite[1], below[1]]
         own_queries, partner_queries = (from_rows(spreads, slot, (query_len, held)) for slot in range(2))
+        leaving = jnp.concatenate([leaving, partner_queries], axis=0)
+        leaving_pieces = [below[0], above[0], below[1], above[1], opposite[0], after(opposite[1], [leaving])]
         swapped = []
-        for at, piece in enumerate([below[0], above[0], below[1], above[1]] + opposite):
+        for at, piece in enumerate(leaving_pieces):
             swapped.append(lax.ppermute(after(piece, swapped[max(at - 2, 0) : max(at - 1, 0)]), "groups", SWAP))
         weights = [down_weight] + above + swapped[1:4:2] + below + swapped[0:4:2] + opposite + swapped[4:]
-        flags = jnp.stack([core, (group == core).astype(core.dtype)])
+        flags = jnp.stack([core, (group == core).astype(core.dtype), 1 - side])
         blocks_of = [[(0, shard)]] + [list(zip(range(at, at + 4), 2 * lengths)) for at in (1, 5, 0)]
         spots = lax.rem(high + jnp.array([0, 1, 3, 2], jnp.int32), highs)
         spots = jnp.stack([(spots * 2 + side) * stride + core * span, spots * span])
         own_residual = passages
 
-        kept, *away = project(
-            flags, hidden, partner_hidden, weights[:9], blocks_of[:3], [2, 2, 2], half, "project_near"
+        kept, *away, partner_rows = project(
+            flags, hidden, partner_hidden, weights[:9], blocks_of[:3], [2, 2, 2], half, 4, "project_near"
         )
         flags, kept, *away = lax.optimization_barrier((flags, kept, *away))
         late_kept, *late_away = project(
-            flags, hidden, partner_hidden, weights[9:], blocks_of[3:], [2], half, "project_far"
+            flags, hidden, partner_rows, weights[9:], blocks_of[3:], [2], half, 0, "project_far"
         )
         others = [lax.ppermute(piece, "mp", SWAP) for piece in away + late_away]
         summands = [kept, late_kept] + others
@@ -301,11 +313,13 @@
     else:
         queries = lax.all_gather(queries, ("high", "low"), axis=0, tiled=True)
         own_queries, partner_queries = (queries[:, slot].reshape(-1, held) for slot in range(2))
+        leaving = jnp.concatenate([leaving, partner_queries], axis=0)
         weight = lax.all_gather(down_weight, ("high", "low"), axis=0, tiled=True)
         weight = jnp.where(core == 0, weight, jnp.roll(weight, held, axis=0))
         spots = jnp.zeros((2, 1), jnp.int32)
         own_residual = features(passages, side)
         summands, pieces = [], []
+        partner_hidden = lax.dynamic_index_in_dim(partner_hidden, 1 - side, keepdims=False)
         for source, flat in enumerate((hidden, partner_hidden)):
             kept, away = (
                 lax.dot_general(flat, part, (((1,), (1,)), ((), ())), preferred_element_type=jnp.float32)[None]
@@ -327,7 +341,7 @@
         [lax.dynamic_slice_in_dim(owner_place, at, blocks) for at in (own_at, partner_at)]
     )
 
-    leaving = jnp.concatenate([leaving, partner_queries], axis=0)
+    leaving = after(leaving, [partner_hidden])
     partner = lax.ppermute(leaving, "side", SWAP)
     packed = (members, 2 * held // 128 * query_len + 8, 128)
     operands = summands + [own_residual, partner]

time: 100 us -> 126 us (1.26)
  between operations: 0.19 us -> 13.7 us
  local copies, waits for them, and re-layouts: 5.25 us -> 14.4 us
    unnamed x13 -> x49, local copies, waits for them, and re-layouts: 1.35 us -> 12.3 us
    all_gather x0 -> x1, waiting for transfers between devices: none -> 9.01 us  [body(): partner_hidden = lax.all_gather(hidden, 'side')]
    ppermute x1 -> x0, waiting for transfers between devices: 5.69 us -> none  [body(): partner_hidden = lax.ppermute(hidden, 'side', SWAP)]
    ppermute x6, waiting for transfers between devices: 16.4 us -> 11 us  [body(): lax.ppermute(after(piece, swapped[max(at - 2, 0):max(at - 1, 0)]), 'group...]
    ppermute x9, waiting for transfers between devices: 23.3 us -> 27.3 us  [shifted(): lax.ppermute(array, 'high', [(at, (at + shift) % highs) for at in range(h...]
    ppermute x9, starting transfers between devices: 13 us -> 16.8 us  [shifted(): lax.ppermute(array, 'high', [(at, (at + shift) % highs) for at in range(h...]
    ppermute x1 -> x0, starting transfers between devices: 1.65 us -> none  [body(): partner_hidden = lax.ppermute(hidden, 'side', SWAP)]
    ppermute x4, waiting for transfers between devices: 3.09 us -> 1.47 us  [body(): others = [lax.ppermute(piece, 'mp', SWAP) for piece in away + late_away]]
  transfers between devices with their start and end apart: 24 -> 24, of which waited for: 17 -> 13; matrix products, arithmetic and copies ran while one was open for 6% -> 6% of each run, Pallas kernels for 11% -> 9%
where the time goes in v7:
time: 126 us
  waiting for transfers between devices  52.1 us (41%)
  starting transfers between devices  27.6 us (22%)
  local copies, waits for them, and re-layouts  14.4 us (11%)
  Pallas kernels  14.2 us (11%)
  between operations  13.7 us (11%)
  other arithmetic  3.67 us (3%)
    ppermute x9, waiting for transfers between devices, shifted(): lax.ppermute(array, 'high', [(at, (at + shift) % highs) for at in range(h...  27.3 us
    ppermute x9, starting transfers between devices, shifted(): lax.ppermute(array, 'high', [(at, (at + shift) % highs) for at in range(h...  16.8 us
    unnamed x49, local copies, waits for them, and re-layouts  12.3 us
    ppermute x6, waiting for transfers between devices, body(): lax.ppermute(after(piece, swapped[max(at - 2, 0):max(at - 1, 0)]), 'group...  11 us
    pallas_call x2, Pallas kernels, project(): pl.pallas_call(functools.partial(project_kernel, blocks=blocks, sends=sen...  10.8 us
    all_gather x1, waiting for transfers between devices, body(): partner_hidden = lax.all_gather(hidden, 'side')  9.01 us
    ppermute x6, starting transfers between devices, body(): lax.ppermute(after(piece, swapped[max(at - 2, 0):max(at - 1, 0)]), 'group...  7.16 us
  transfers between devices with their start and end apart: 24, of which 13 were waited for; matrix products, arithmetic and copies ran while one was open for 6% of the time, Pallas kernels for 9%

profile of v7, /device:TPU:0, one launch (start us, length us, event | category | flops | bytes accessed | tf_op | source)
XLA Modules:
  0.0 125.7 jit_solution(12882804385145458803)
XLA Ops:
  7.9 5.1 %collective-permute-start = (bf16[64,2560]{1,0:T(8,128)(2,1)S(1)}, bf16[64,2560]{1,0:T(8,128)(2,1)}, u32[]{:S(2)}, u32[]{:S(2)}) collective-permute-start(bf16[64,2560]{1,0:T(8,128)(2,1)S(1)} %get-tuple-element.53), channel_id=1, source_target_pairs={{0,12},{4,0},{8,4},{12,8},{1,13},{5,1},{9,5},{13,9},{2,14},{6,2},{... | collective-permute-start | bytes 983048 | tf_op jit(solution)/shard_map/ppermute | solution.py:266
  14.5 6.7 %collective-permute-done.refs_1_ = bf16[64,2560]{1,0:T(8,128)(2,1)} collective-permute-done((bf16[64,2560]{1,0:T(8,128)(2,1)S(1)}, bf16[64,2560]{1,0:T(8,128)(2,1)}, u32[]{:S(2)}, u32[]{:S(2)}) %collective-permute-start) | collective-permute-done | bytes 327712 | tf_op jit(solution)/shard_map/ppermute | solution.py:266
  21.1 4.4 %collective-permute-start.1 = (bf16[72,2560]{1,0:T(8,128)(2,1)}, bf16[72,2560]{1,0:T(8,128)(2,1)S(1)}, u32[]{:S(2)}, u32[]{:S(2)}) collective-permute-start(bf16[72,2560]{1,0:T(8,128)(2,1)} %pad_maximum_fusion), channel_id=1, source_target_pairs={{0,12},{4,0},{8,4},{12,8},{1,13},{5,1},{9,5},{13,9},{2,14},{6,2},{... | collective-permute-start | bytes 1105928 | tf_op jit(solution)/shard_map/ppermute | solution.py:266
  25.5 3.7 %collective-permute-done.2.refs_5_ = bf16[64,2560]{1,0:T(8,128)(2,1)} collective-permute-done((bf16[64,2560]{1,0:T(8,128)(2,1)S(1)}, bf16[64,2560]{1,0:T(8,128)(2,1)}, u32[]{:S(2)}, u32[]{:S(2)}) %collective-permute-start.2) | collective-permute-done | bytes 327712 | tf_op jit(solution)/shard_map/ppermute | solution.py:266
  29.2 1.5 %collective-permute-start.3 = (bf16[72,2560]{1,0:T(8,128)(2,1)}, bf16[72,2560]{1,0:T(8,128)(2,1)S(1)}, u32[]{:S(2)}, u32[]{:S(2)}) collective-permute-start(bf16[72,2560]{1,0:T(8,128)(2,1)} %pad_maximum_fusion), channel_id=1, source_target_pairs={{0,4},{4,8},{8,12},{12,0},{1,5},{5,9},{9,13},{13,1},{2,6},{6,10},{... | collective-permute-start | bytes 1105928 | tf_op jit(solution)/shard_map/ppermute | solution.py:266
  30.7 1.9 %constant_dynamic-slice_fusion.3 = (bf16[512,128]{1,0:T(8,128)(2,1)S(1)}, bf16[512,128]{1,0:T(8,128)(2,1)}, bf16[512,128]{1,0:T(8,128)(2,1)}, bf16[512,128]{1,0:T(8,128)(2,1)}) fusion(bf16[512,2048]{1,0:T(8,128)(2,1)} %bitcast.24, s32[]{:T(128)S(6)} %select_n.69, s32[]{:T(128)S(6)} %select_n.72, s32[]{:T(128)S(6)} %select_n.71, s32[]{:T(128)S(6)} %select_n.70), kind=kLoop, calls=%fused_computation.32 | loop fusion | bytes 1048592 | tf_op jit(solution)/shard_map/dynamic_slice | solution.py:262
  32.6 1.5 %collective-permute-start.5 = (bf16[64,2560]{1,0:T(8,128)(2,1)}, bf16[64,2560]{1,0:T(8,128)(2,1)S(1)}, u32[]{:S(2)}, u32[]{:S(2)}) collective-permute-start(bf16[64,2560]{1,0:T(8,128)(2,1)} %collective-permute-done.refs_1_), channel_id=1, source_target_pairs={{0,16},{16,0},{1,17},{17,1},{2,18},{18,2},{3,19},{19,3},{4,20},{20... | collective-permute-start | bytes 983048 | tf_op jit(solution)/shard_map/ppermute | solution.py:293
  34.6 1.1 maximum_dynamic-update-slice_fusion
  37.3 6.2 %collective-permute-done.5.refs_3_ = bf16[64,2560]{1,0:T(8,128)(2,1)S(1)} collective-permute-done((bf16[64,2560]{1,0:T(8,128)(2,1)}, bf16[64,2560]{1,0:T(8,128)(2,1)S(1)}, u32[]{:S(2)}, u32[]{:S(2)}) %collective-permute-start.5) | collective-permute-done | bytes 327712 | tf_op jit(solution)/shard_map/ppermute | solution.py:293
  44.2 1.5 %collective-permute-start.6 = (bf16[72,2560]{1,0:T(8,128)(2,1)S(1)}, bf16[72,2560]{1,0:T(8,128)(2,1)S(1)}, u32[]{:S(2)}, u32[]{:S(2)}) collective-permute-start(bf16[72,2560]{1,0:T(8,128)(2,1)S(1)} %collective-permute-done.1.refs_2_), channel_id=1, source_target_pairs={{0,16},{16,0},{1,17},{17,1},{2,18},{18,2},{3,19},{19,3},{4,20},{20... | collective-permute-start | bytes 1105928 | tf_op jit(solution)/shard_map/ppermute | solution.py:293
  45.7 4.8 %collective-permute-done.7.refs_7_ = bf16[64,2560]{1,0:T(8,128)(2,1)S(1)} collective-permute-done((bf16[64,2560]{1,0:T(8,128)(2,1)}, bf16[64,2560]{1,0:T(8,128)(2,1)S(1)}, u32[]{:S(2)}, u32[]{:S(2)}) %collective-permute-start.7) | collective-permute-done | bytes 327712 | tf_op jit(solution)/shard_map/ppermute | solution.py:293
  51.2 1.5 %collective-permute-start.8 = (bf16[72,2560]{1,0:T(8,128)(2,1)S(1)}, bf16[72,2560]{1,0:T(8,128)(2,1)}, u32[]{:S(2)}, u32[]{:S(2)}) collective-permute-start(bf16[72,2560]{1,0:T(8,128)(2,1)S(1)} %collective-permute-done.3.refs_6_), channel_id=1, source_target_pairs={{0,16},{16,0},{1,17},{17,1},{2,18},{18,2},{3,19},{19,3},{4,20},{20... | collective-permute-start | bytes 1105928 | tf_op jit(solution)/shard_map/ppermute | solution.py:293
  52.9 13.0 %collective-permute-done.4.refs_1_ = bf16[72,2560]{1,0:T(8,128)(2,1)} collective-permute-done((bf16[72,2560]{1,0:T(8,128)(2,1)S(1)}, bf16[72,2560]{1,0:T(8,128)(2,1)}, u32[]{:S(2)}, u32[]{:S(2)}) %collective-permute-start.4) | collective-permute-done | bytes 368672 | tf_op jit(solution)/shard_map/ppermute | solution.py:266
  69.4 1.6 %collective-permute-start.10 = (bf16[64,2560]{1,0:T(8,128)(2,1)}, bf16[64,2560]{1,0:T(8,128)(2,1)}, u32[]{:S(2)}, u32[]{:S(2)}) collective-permute-start(bf16[64,2560]{1,0:T(8,128)(2,1)} %collective-permute-done.9.refs_0_), channel_id=1, source_target_pairs={{0,16},{16,0},{1,17},{17,1},{2,18},{18,2},{3,19},{19,3},{4,20},{20... | collective-permute-start | bytes 983048 | tf_op jit(solution)/shard_map/ppermute | solution.py:293
  71.2 9.0 %all-gather.2.cloned.1.call-done.partner_ref = bf16[2,512,2560]{2,1,0:T(8,128)(2,1)} async-done(((bf16[1,512,2560]{2,1,0:T(8,128)(2,1)}), bf16[2,512,2560]{2,1,0:T(8,128)(2,1)}) %all-gather.2.cloned.1.call-update) | async-done | bytes 5242896 | tf_op jit(solution)/shard_map/all_gather | solution.py:269
  80.6 2.5 %copy-done.1 = bf16[2,512,2560]{2,1,0:T(8,128)(2,1)S(1)} copy-done((bf16[2,512,2560]{2,1,0:T(8,128)(2,1)S(1)}, bf16[2,512,2560]{2,1,0:T(8,128)(2,1)}, u32[]{:S(2)}) %copy-start.1) | copy-done | bytes 5242904
  83.1 1.3 %copy-done.4 = bf16[256,2560]{1,0:T(8,128)(2,1)S(1)} copy-done((bf16[256,2560]{1,0:T(8,128)(2,1)S(1)}, bf16[256,2560]{1,0:T(8,128)(2,1)}, u32[]{:S(2)}) %copy-start.4) | copy-done | bytes 1310744
  84.4 1.0 copy-done.6
  85.4 1.0 copy-done.8
  86.4 1.0 copy-done.10
  87.3 7.8 %project_near.1 = (f32[6,512,128]{2,1,0:T(8,128)S(1)}, f32[2,512,128]{2,1,0:T(8,128)S(1)}, f32[2,512,128]{2,1,0:T(8,128)S(1)}, f32[2,512,128]{2,1,0:T(8,128)S(1)}, bf16[512,2560]{1,0:T(8,128)(2,1)S(1)}) custom-call(s32[3]{0:T(128)S(1)} %pad_add_fusion.3.flag_ref, bf16[512,2560]{1,0:T(8,128)(2,1)S(1)} %bitcast.22, bf16[2,512,2560]{2,1,0:T(8,128)(2,1)S(1)} %copy-done.1, ...), custom_call_target="tpu_custom_call" | custom-call | flops 1 | bytes 1 | tf_op jit(solution)/shard_map/project_near/pallas_call | solution.py:209
  95.8 3.0 %project_far.1 = (f32[2,512,128]{2,1,0:T(8,128)S(1)}, f32[2,512,128]{2,1,0:T(8,128)S(1)}) custom-call(s32[3]{0:T(128)S(1)} %pad_add_fusion.3.flag_ref, bf16[512,2560]{1,0:T(8,128)(2,1)S(1)} %bitcast.23, bf16[512,2560]{1,0:T(8,128)(2,1)S(1)} %get-tuple-element.36.partner_ref, bf16[64,2560]{1,0:T(8,128)(2,1)} %collective-permute-done.9.refs_0_, ...), custom_call_target="tpu_custom_call" | custom-call | flops 1 | bytes 1 | tf_op jit(solution)/shard_map/project_far/pallas_call | solution.py:209
  99.4 1.5 %collective-permute-done.15.refs_5_ = f32[2,512,128]{2,1,0:T(8,128)S(1)} collective-permute-done((f32[2,512,128]{2,1,0:T(8,128)S(1)}, f32[2,512,128]{2,1,0:T(8,128)S(1)}, u32[]{:S(2)}, u32[]{:S(2)}) %collective-permute-start.15) | collective-permute-done | bytes 524320 | tf_op jit(solution)/shard_map/ppermute | solution.py:308
  100.9 2.0 %attend.1 = f32[4,136,128]{2,1,0:T(8,128)S(1)} custom-call(s32[4]{0:T(128)S(1)} %pad_add_fusion.2.place_ref, s32[2,4]{1,0:T(2,128)S(1)} %pad_add_fusion.spot_ref, bf16[64,512]{1,0:T(8,128)(2,1)S(1)} %get-tuple-element.56.query_ref, f32[6,512,128]{2,1,0:T(8,128)S(1)} %get-tuple-element.34.refs_0_, f32[2,512,128]{2,1,0:T(8,128)S(1)} %get-tuple-element.41.refs_1_, ...), custom_call_target="tpu_custom_call" | custom-call | tf_op jit(solution)/shard_map/attend/pallas_call | solution.py:348
  102.9 1.8 %collective-permute-start.17 = (f32[1,136,128]{2,1,0:T(8,128)S(1)}, f32[1,136,128]{2,1,0:T(8,128)S(1)}, u32[]{:S(2)}, u32[]{:S(2)}) collective-permute-start(f32[1,136,128]{2,1,0:T(8,128)S(1)} %get-tuple-element.69), channel_id=1, source_target_pairs={{0,4},{4,8},{8,12},{12,0},{1,5},{5,9},{9,13},{13,1},{2,6},{6,10},{... | collective-permute-start | bytes 208904 | tf_op jit(solution)/shard_map/ppermute | solution.py:266
  104.7 2.4 %collective-permute-start.18 = (f32[1,136,128]{2,1,0:T(8,128)S(1)}, f32[1,136,128]{2,1,0:T(8,128)S(1)}, u32[]{:S(2)}, u32[]{:S(2)}) collective-permute-start(f32[1,136,128]{2,1,0:T(8,128)S(1)} %get-tuple-element.68), channel_id=1, source_target_pairs={{0,8},{4,12},{8,0},{12,4},{1,9},{5,13},{9,1},{13,5},{2,10},{6,14},... | collective-permute-start | bytes 208904 | tf_op jit(solution)/shard_map/ppermute | solution.py:266
  107.1 1.4 %collective-permute-start.19 = (f32[1,136,128]{2,1,0:T(8,128)S(1)}, f32[1,136,128]{2,1,0:T(8,128)S(1)}, u32[]{:S(2)}, u32[]{:S(2)}) collective-permute-start(f32[1,136,128]{2,1,0:T(8,128)S(1)} %get-tuple-element.67), channel_id=1, source_target_pairs={{0,12},{4,0},{8,4},{12,8},{1,13},{5,1},{9,5},{13,9},{2,14},{6,2},{... | collective-permute-start | bytes 208904 | tf_op jit(solution)/shard_map/ppermute | solution.py:266
  108.5 0.9 collective-permute-done.17.refs_1_
  109.4 2.9 %collective-permute-done.18.refs_2_ = f32[1,136,128]{2,1,0:T(8,128)S(1)} collective-permute-done((f32[1,136,128]{2,1,0:T(8,128)S(1)}, f32[1,136,128]{2,1,0:T(8,128)S(1)}, u32[]{:S(2)}, u32[]{:S(2)}) %collective-permute-start.18) | collective-permute-done | bytes 69664 | tf_op jit(solution)/shard_map/ppermute | solution.py:266
  112.8 1.8 %collective-permute-start.21 = (bf16[1,16,512]{2,1,0:T(8,128)(2,1)S(1)}, bf16[1,16,512]{2,1,0:T(8,128)(2,1)S(1)}, u32[]{:S(2)}, u32[]{:S(2)}) collective-permute-start(bf16[1,16,512]{2,1,0:T(8,128)(2,1)S(1)} %get-tuple-element.79), channel_id=1, source_target_pairs={{0,2},{2,0},{1,3},{3,1},{4,6},{6,4},{5,7},{7,5},{8,10},{10,8},{9,1... | collective-permute-start | bytes 49160 | tf_op jit(solution)/shard_map/ppermute | solution.py:372
  116.6 1.1 collective-permute-done.22.both_ref
  117.7 1.2 assemble.1
  (92 shorter events, 14.1 us)
Async XLA Ops:
  6.5 6.5 %copy-start.20 = (bf16[1,16,2048]{2,1,0:T(8,128)(2,1)S(1)}, bf16[1,16,2048]{2,1,0:T(8,128)(2,1)}, u32[]{:S(2)}) copy-start(bf16[1,16,2048]{2,1,0:T(8,128)(2,1)} %param.12) | copy-start | bytes 196612
  6.5 73.7 %all-gather.2.cloned.1.call-start = ((), (), s32[]{:S(2)}) async-start(), calls=%async_computation | async-start | bytes 7864320 | tf_op jit(solution)/shard_map/all_gather | solution.py:269
  7.9 72.7 %copy-start = (bf16[2,256,2560]{2,1,0:T(8,128)(2,1)S(1)}, bf16[2,256,2560]{2,1,0:T(8,128)(2,1)}, u32[]{:S(2)}) copy-start(bf16[2,256,2560]{2,1,0:T(8,128)(2,1)} %param.7) | copy-start | bytes 7864324
  7.9 13.2 %collective-permute-start = (bf16[64,2560]{1,0:T(8,128)(2,1)S(1)}, bf16[64,2560]{1,0:T(8,128)(2,1)}, u32[]{:S(2)}, u32[]{:S(2)}) collective-permute-start(bf16[64,2560]{1,0:T(8,128)(2,1)S(1)} %get-tuple-element.53), channel_id=1, source_target_pairs={{0,12},{4,0},{8,4},{12,8},{1,13},{5,1},{9,5},{13,9},{2,14},{6,2},{... | collective-permute-start | bytes 983048 | tf_op jit(solution)/shard_map/ppermute | solution.py:266
  13.0 16.2 %collective-permute-start.2 = (bf16[64,2560]{1,0:T(8,128)(2,1)S(1)}, bf16[64,2560]{1,0:T(8,128)(2,1)}, u32[]{:S(2)}, u32[]{:S(2)}) collective-permute-start(bf16[64,2560]{1,0:T(8,128)(2,1)S(1)} %get-tuple-element.53), channel_id=1, source_target_pairs={{0,4},{4,8},{8,12},{12,0},{1,5},{5,9},{9,13},{13,1},{2,6},{6,10},{... | collective-permute-start | bytes 983048 | tf_op jit(solution)/shard_map/ppermute | solution.py:266
  13.1 1.4 %copy-start.14 = (bf16[1,16,128]{2,1,0:T(8,128)(2,1)}, bf16[1,16,128]{2,1,0:T(8,128)(2,1)S(1)}, u32[]{:S(2)}) copy-start(bf16[1,16,128]{2,1,0:T(8,128)(2,1)S(1)} %get-tuple-element.73) | copy-start | bytes 12292
  13.1 1.4 %copy-start.15 = (bf16[1,16,128]{2,1,0:T(8,128)(2,1)}, bf16[1,16,128]{2,1,0:T(8,128)(2,1)S(1)}, u32[]{:S(2)}) copy-start(bf16[1,16,128]{2,1,0:T(8,128)(2,1)S(1)} %get-tuple-element.74) | copy-start | bytes 12292
  13.1 1.4 %copy-start.16 = (bf16[1,16,128]{2,1,0:T(8,128)(2,1)}, bf16[1,16,128]{2,1,0:T(8,128)(2,1)S(1)}, u32[]{:S(2)}) copy-start(bf16[1,16,128]{2,1,0:T(8,128)(2,1)S(1)} %get-tuple-element.75) | copy-start | bytes 12292
  21.1 23.1 %collective-permute-start.1 = (bf16[72,2560]{1,0:T(8,128)(2,1)}, bf16[72,2560]{1,0:T(8,128)(2,1)S(1)}, u32[]{:S(2)}, u32[]{:S(2)}) collective-permute-start(bf16[72,2560]{1,0:T(8,128)(2,1)} %pad_maximum_fusion), channel_id=1, source_target_pairs={{0,12},{4,0},{8,4},{12,8},{1,13},{5,1},{9,5},{13,9},{2,14},{6,2},{... | collective-permute-start | bytes 1105928 | tf_op jit(solution)/shard_map/ppermute | solution.py:266
  29.2 22.0 %collective-permute-start.3 = (bf16[72,2560]{1,0:T(8,128)(2,1)}, bf16[72,2560]{1,0:T(8,128)(2,1)S(1)}, u32[]{:S(2)}, u32[]{:S(2)}) collective-permute-start(bf16[72,2560]{1,0:T(8,128)(2,1)} %pad_maximum_fusion), channel_id=1, source_target_pairs={{0,4},{4,8},{8,12},{12,0},{1,5},{5,9},{9,13},{13,1},{2,6},{6,10},{... | collective-permute-start | bytes 1105928 | tf_op jit(solution)/shard_map/ppermute | solution.py:266
  32.6 10.9 %collective-permute-start.5 = (bf16[64,2560]{1,0:T(8,128)(2,1)}, bf16[64,2560]{1,0:T(8,128)(2,1)S(1)}, u32[]{:S(2)}, u32[]{:S(2)}) collective-permute-start(bf16[64,2560]{1,0:T(8,128)(2,1)} %collective-permute-done.refs_1_), channel_id=1, source_target_pairs={{0,16},{16,0},{1,17},{17,1},{2,18},{18,2},{3,19},{19,3},{4,20},{20... | collective-permute-start | bytes 983048 | tf_op jit(solution)/shard_map/ppermute | solution.py:293
  34.1 16.4 %collective-permute-start.7 = (bf16[64,2560]{1,0:T(8,128)(2,1)}, bf16[64,2560]{1,0:T(8,128)(2,1)S(1)}, u32[]{:S(2)}, u32[]{:S(2)}) collective-permute-start(bf16[64,2560]{1,0:T(8,128)(2,1)} %collective-permute-done.2.refs_5_), channel_id=1, source_target_pairs={{0,16},{16,0},{1,17},{17,1},{2,18},{18,2},{3,19},{19,3},{4,20},{20... | collective-permute-start | bytes 983048 | tf_op jit(solution)/shard_map/ppermute | solution.py:293
  44.2 23.1 %collective-permute-start.6 = (bf16[72,2560]{1,0:T(8,128)(2,1)S(1)}, bf16[72,2560]{1,0:T(8,128)(2,1)S(1)}, u32[]{:S(2)}, u32[]{:S(2)}) collective-permute-start(bf16[72,2560]{1,0:T(8,128)(2,1)S(1)} %collective-permute-done.1.refs_2_), channel_id=1, source_target_pairs={{0,16},{16,0},{1,17},{17,1},{2,18},{18,2},{3,19},{19,3},{4,20},{20... | collective-permute-start | bytes 1105928 | tf_op jit(solution)/shard_map/ppermute | solution.py:293
  51.2 18.2 %collective-permute-start.8 = (bf16[72,2560]{1,0:T(8,128)(2,1)S(1)}, bf16[72,2560]{1,0:T(8,128)(2,1)}, u32[]{:S(2)}, u32[]{:S(2)}) collective-permute-start(bf16[72,2560]{1,0:T(8,128)(2,1)S(1)} %collective-permute-done.3.refs_6_), channel_id=1, source_target_pairs={{0,16},{16,0},{1,17},{17,1},{2,18},{18,2},{3,19},{19,3},{4,20},{20... | collective-permute-start | bytes 1105928 | tf_op jit(solution)/shard_map/ppermute | solution.py:293
  52.7 16.7 %collective-permute-start.9 = (bf16[64,2560]{1,0:T(8,128)(2,1)}, bf16[64,2560]{1,0:T(8,128)(2,1)}, u32[]{:S(2)}, u32[]{:S(2)}) collective-permute-start(bf16[64,2560]{1,0:T(8,128)(2,1)} %collective-permute-done.2.refs_5_), channel_id=1, source_target_pairs={{0,4},{4,8},{8,12},{12,0},{1,5},{5,9},{9,13},{13,1},{2,6},{6,10},{... | collective-permute-start | bytes 983048 | tf_op jit(solution)/shard_map/ppermute | solution.py:266
  52.7 13.1 %collective-permute-start.4 = (bf16[72,2560]{1,0:T(8,128)(2,1)S(1)}, bf16[72,2560]{1,0:T(8,128)(2,1)}, u32[]{:S(2)}, u32[]{:S(2)}) collective-permute-start(bf16[72,2560]{1,0:T(8,128)(2,1)S(1)} %collective-permute-done.3.refs_6_), channel_id=1, source_target_pairs={{0,4},{4,8},{8,12},{12,0},{1,5},{5,9},{9,13},{13,1},{2,6},{6,10},{... | collective-permute-start | bytes 1105928 | tf_op jit(solution)/shard_map/ppermute | solution.py:266
  68.9 27.0 %collective-permute-start.11 = (bf16[72,2560]{1,0:T(8,128)(2,1)}, bf16[72,2560]{1,0:T(8,128)(2,1)}, u32[]{:S(2)}, u32[]{:S(2)}) collective-permute-start(bf16[72,2560]{1,0:T(8,128)(2,1)} %collective-permute-done.4.refs_1_), channel_id=1, source_target_pairs={{0,16},{16,0},{1,17},{17,1},{2,18},{18,2},{3,19},{19,3},{4,20},{20... | collective-permute-start | bytes 1105928 | tf_op jit(solution)/shard_map/ppermute | solution.py:293
  69.4 26.3 %collective-permute-start.10 = (bf16[64,2560]{1,0:T(8,128)(2,1)}, bf16[64,2560]{1,0:T(8,128)(2,1)}, u32[]{:S(2)}, u32[]{:S(2)}) collective-permute-start(bf16[64,2560]{1,0:T(8,128)(2,1)} %collective-permute-done.9.refs_0_), channel_id=1, source_target_pairs={{0,16},{16,0},{1,17},{17,1},{2,18},{18,2},{3,19},{19,3},{4,20},{20... | collective-permute-start | bytes 983048 | tf_op jit(solution)/shard_map/ppermute | solution.py:293
  80.2 20.7 %collective-permute-start.16 = (bf16[576,512]{1,0:T(8,128)(2,1)}, bf16[576,512]{1,0:T(8,128)(2,1)S(1)}, u32[]{:S(2)}, u32[]{:S(2)}) collective-permute-start(bf16[576,512]{1,0:T(8,128)(2,1)} %copy-done.11), channel_id=1, source_target_pairs={{0,2},{2,0},{1,3},{3,1},{4,6},{6,4},{5,7},{7,5},{8,10},{10,8},{9,1... | collective-permute-start | bytes 1769480 | tf_op jit(solution)/shard_map/ppermute | solution.py:345
  80.6 2.5 %copy-start.1 = (bf16[2,512,2560]{2,1,0:T(8,128)(2,1)S(1)}, bf16[2,512,2560]{2,1,0:T(8,128)(2,1)}, u32[]{:S(2)}) copy-start(bf16[2,512,2560]{2,1,0:T(8,128)(2,1)} %all-gather.2.cloned.1.call-done.partner_ref) | copy-start | bytes 15728644
  95.2 4.2 %collective-permute-start.12 = (f32[2,512,128]{2,1,0:T(8,128)S(1)}, f32[2,512,128]{2,1,0:T(8,128)S(1)}, u32[]{:S(2)}, u32[]{:S(2)}) collective-permute-start(f32[2,512,128]{2,1,0:T(8,128)S(1)} %get-tuple-element.42), channel_id=1, source_target_pairs={{0,1},{1,0},{2,3},{3,2},{4,5},{5,4},{6,7},{7,6},{8,9},{9,8},{10,11... | collective-permute-start | bytes 1572872 | tf_op jit(solution)/shard_map/ppermute | solution.py:308
  95.3 4.1 %collective-permute-start.13 = (f32[2,512,128]{2,1,0:T(8,128)S(1)}, f32[2,512,128]{2,1,0:T(8,128)S(1)}, u32[]{:S(2)}, u32[]{:S(2)}) collective-permute-start(f32[2,512,128]{2,1,0:T(8,128)S(1)} %get-tuple-element.43), channel_id=1, source_target_pairs={{0,1},{1,0},{2,3},{3,2},{4,5},{5,4},{6,7},{7,6},{8,9},{9,8},{10,11... | collective-permute-start | bytes 1572872 | tf_op jit(solution)/shard_map/ppermute | solution.py:308
  95.8 3.7 %collective-permute-start.14 = (f32[2,512,128]{2,1,0:T(8,128)S(1)}, f32[2,512,128]{2,1,0:T(8,128)S(1)}, u32[]{:S(2)}, u32[]{:S(2)}) collective-permute-start(f32[2,512,128]{2,1,0:T(8,128)S(1)} %get-tuple-element.44), channel_id=1, source_target_pairs={{0,1},{1,0},{2,3},{3,2},{4,5},{5,4},{6,7},{7,6},{8,9},{9,8},{10,11... | collective-permute-start | bytes 1572872 | tf_op jit(solution)/shard_map/ppermute | solution.py:308
  95.8 3.5 %copy-start.21 = (s32[4]{0:T(128)S(1)}, s32[4]{0:T(128)}, u32[]{:S(2)}) copy-start(s32[4]{0:T(128)} %constant.97.clone) | copy-start | bytes 52
  95.8 5.0 %copy-start.2 = (bf16[2,256,2048]{2,1,0:T(8,128)(2,1)S(1)}, bf16[2,256,2048]{2,1,0:T(8,128)(2,1)}, u32[]{:S(2)}) copy-start(bf16[2,256,2048]{2,1,0:T(8,128)(2,1)} %param.8) | copy-start | bytes 6291460
  98.9 2.0 %collective-permute-start.15 = (f32[2,512,128]{2,1,0:T(8,128)S(1)}, f32[2,512,128]{2,1,0:T(8,128)S(1)}, u32[]{:S(2)}, u32[]{:S(2)}) collective-permute-start(f32[2,512,128]{2,1,0:T(8,128)S(1)} %get-tuple-element.45), channel_id=1, source_target_pairs={{0,1},{1,0},{2,3},{3,2},{4,5},{5,4},{6,7},{7,6},{8,9},{9,8},{10,11... | collective-permute-start | bytes 1572872 | tf_op jit(solution)/shard_map/ppermute | solution.py:308
  102.9 6.5 %collective-permute-start.17 = (f32[1,136,128]{2,1,0:T(8,128)S(1)}, f32[1,136,128]{2,1,0:T(8,128)S(1)}, u32[]{:S(2)}, u32[]{:S(2)}) collective-permute-start(f32[1,136,128]{2,1,0:T(8,128)S(1)} %get-tuple-element.69), channel_id=1, source_target_pairs={{0,4},{4,8},{8,12},{12,0},{1,5},{5,9},{9,13},{13,1},{2,6},{6,10},{... | collective-permute-start | bytes 208904 | tf_op jit(solution)/shard_map/ppermute | solution.py:266
  104.7 7.6 %collective-permute-start.18 = (f32[1,136,128]{2,1,0:T(8,128)S(1)}, f32[1,136,128]{2,1,0:T(8,128)S(1)}, u32[]{:S(2)}, u32[]{:S(2)}) collective-permute-start(f32[1,136,128]{2,1,0:T(8,128)S(1)} %get-tuple-element.68), channel_id=1, source_target_pairs={{0,8},{4,12},{8,0},{12,4},{1,9},{5,13},{9,1},{13,5},{2,10},{6,14},... | collective-permute-start | bytes 208904 | tf_op jit(solution)/shard_map/ppermute | solution.py:266
  107.1 5.4 %collective-permute-start.19 = (f32[1,136,128]{2,1,0:T(8,128)S(1)}, f32[1,136,128]{2,1,0:T(8,128)S(1)}, u32[]{:S(2)}, u32[]{:S(2)}) collective-permute-start(f32[1,136,128]{2,1,0:T(8,128)S(1)} %get-tuple-element.67), channel_id=1, source_target_pairs={{0,12},{4,0},{8,4},{12,8},{1,13},{5,1},{9,5},{13,9},{2,14},{6,2},{... | collective-permute-start | bytes 208904 | tf_op jit(solution)/shard_map/ppermute | solution.py:266
  112.8 3.8 %collective-permute-start.21 = (bf16[1,16,512]{2,1,0:T(8,128)(2,1)S(1)}, bf16[1,16,512]{2,1,0:T(8,128)(2,1)S(1)}, u32[]{:S(2)}, u32[]{:S(2)}) collective-permute-start(bf16[1,16,512]{2,1,0:T(8,128)(2,1)S(1)} %get-tuple-element.79), channel_id=1, source_target_pairs={{0,2},{2,0},{1,3},{3,1},{4,6},{6,4},{5,7},{7,5},{8,10},{10,8},{9,1... | collective-permute-start | bytes 49160 | tf_op jit(solution)/shard_map/ppermute | solution.py:372
  114.5 3.2 %collective-permute-start.22 = (bf16[1,16,512]{2,1,0:T(8,128)(2,1)S(1)}, bf16[1,16,512]{2,1,0:T(8,128)(2,1)S(1)}, u32[]{:S(2)}, u32[]{:S(2)}) collective-permute-start(bf16[1,16,512]{2,1,0:T(8,128)(2,1)S(1)} %get-tuple-element.79), channel_id=1, source_target_pairs={{0,3},{3,0},{1,2},{2,1},{4,7},{7,4},{5,6},{6,5},{8,11},{11,8},{9,1... | collective-permute-start | bytes 49160 | tf_op jit(solution)/shard_map/ppermute | solution.py:373
  114.5 1.3 %collective-permute-start.20 = (bf16[1,16,512]{2,1,0:T(8,128)(2,1)S(1)}, bf16[1,16,512]{2,1,0:T(8,128)(2,1)S(1)}, u32[]{:S(2)}, u32[]{:S(2)}) collective-permute-start(bf16[1,16,512]{2,1,0:T(8,128)(2,1)S(1)} %get-tuple-element.80.mine_ref), channel_id=1, source_target_pairs={{0,1},{1,0},{2,3},{3,2},{4,5},{5,4},{6,7},{7,6},{8,9},{9,8},{10,11... | collective-permute-start | bytes 49160 | tf_op jit(solution)/shard_map/ppermute | solution.py:371
  (14 other events, 13.9 us)
Sparse Core Ops, SparseCore 0:
  8.9 71.2 all-gather.1

commit v8 on v7

--- a/solution.py
+++ b/solution.py
@@ -26,25 +26,30 @@
 
 
 def project_kernel(flag_ref, hidden_ref, partner_ref, *refs, blocks, sends, copies):
-    waiting = []
+    partner_copies, weight_copies = [], []
     if copies:
-        *refs, semaphores = refs
-        *refs, rows_ref = refs
-        step = partner_ref.shape[1] // copies
-        for at in range(copies):
-            rows = pl.ds(at * step, step)
-            waiting.append(pltpu.make_async_copy(partner_ref.at[flag_ref[2], rows], rows_ref.at[rows], semaphores.at[at]))
-            waiting[-1].start()
+        *refs, rows_ref, shard_ref, semaphores = refs
+        for of, (source, target) in enumerate(((partner_ref, rows_ref), (refs[0], shard_ref))):
+            step = source.shape[0] // copies
+            for at in range(copies):
+                rows = pl.ds(at * step, step)
+                copy = pltpu.make_async_copy(source.at[rows], target.at[rows], semaphores.at[of, at])
+                (weight_copies if of else partner_copies).append(copy)
+        for copy in weight_copies + partner_copies:
+            copy.start()
         partner_ref = rows_ref
+        refs = [shard_ref] + refs[1:]
     keep_ref, *send_refs = refs[-1 - len(sends) :]
     slots = [(ref, at) for ref in send_refs for at in range(ref.shape[0])]
     core, same = flag_ref[0], flag_ref[1]
     half = keep_ref.shape[2]
     for source in range(2):
-        for copy in waiting if source else []:
+        for copy in partner_copies if source else []:
             copy.wait()
         for at, pieces in enumerate(blocks):
             if len(pieces) == 1:
+                for copy in [] if source else weight_copies:
+                    copy.wait()
                 whole = refs[pieces[0][0]]
                 keep = whole[pl.ds(pl.multiple_of(core * half, half), half), :]
                 send = whole[pl.ds(pl.multiple_of((1 - core) * half, half), half), :]
@@ -205,13 +210,14 @@
     shapes = [jax.ShapeDtypeStruct((count, rows, half), jnp.float32) for count in [2 * len(blocks)] + sends]
     if copies:
         shapes.append(jax.ShapeDtypeStruct((rows, units), hidden.dtype))
-    held = [pl.BlockSpec(memory_space=pl.ANY)] if copies else in_vmem(1)
+    held = [pl.BlockSpec(memory_space=pltpu.HBM)] * 2 if copies else in_vmem(2)
+    scratch = [pltpu.VMEM(weights[0].shape, weights[0].dtype), pltpu.SemaphoreType.DMA((2, copies))]
     return pl.pallas_call(
         functools.partial(project_kernel, blocks=blocks, sends=sends, copies=copies),
         out_shape=shapes,
-        in_specs=in_smem(1) + in_vmem(1) + held + in_vmem(len(weights)),
+        in_specs=in_smem(1) + in_vmem(1) + held + in_vmem(len(weights) - 1),
         out_specs=in_vmem(len(shapes)),
-        scratch_shapes=[pltpu.SemaphoreType.DMA((copies,))] if copies else [],
+        scratch_shapes=scratch if copies else [],
         compiler_params=pltpu.CompilerParams(vmem_limit_bytes=VMEM_LIMIT),
         cost_estimate=pl.CostEstimate(flops=1, bytes_accessed=1, transcendentals=0),
         name=name,
@@ -266,7 +272,7 @@
         return lax.ppermute(array, "high", [(at, (at + shift) % highs) for at in range(highs)])
 
     hidden = hidden_states.reshape(rows, units)
-    partner_hidden = lax.all_gather(hidden, "side")
+    partner_hidden = lax.ppermute(hidden, "side", SWAP)
     queries = jnp.concatenate([features(decoder_states, side), features(decoder_states, 1 - side)], axis=0)[None]
     passages = passage_states.reshape(rows, width)
     leaving = features(passages, 1 - side)
@@ -284,17 +290,21 @@
             below.append(shifted(after(sent[at], below[-1:]), 1))
             above.append(shifted(after(sent[at], above[-1:]), -1))
         opposite = [shifted(after(below[0], below[1:]), 1), shifted(below[1], 1)]
-        spreads = [sent[1], above[1], opposite[1], below[1]]
+        spreads = [piece[1][-8:] for piece in (sent, above, opposite, below)]
+        *spreads, leaving, _ = lax.optimization_barrier(
+            (*spreads, jnp.pad(leaving, ((0, highs * query_len), (0, 0))), partner_hidden)
+        )
         own_queries, partner_queries = (from_rows(spreads, slot, (query_len, held)) for slot in range(2))
-        leaving = jnp.concatenate([leaving, partner_queries], axis=0)
-        leaving_pieces = [below[0], above[0], below[1], above[1], opposite[0], after(opposite[1], [leaving])]
+        leaving = lax.dynamic_update_slice(leaving, partner_queries, (rows, 0))
+        leaving_pieces = [below[0], above[0], below[1], above[1], opposite[0], opposite[1]]
         swapped = []
         for at, piece in enumerate(leaving_pieces):
             swapped.append(lax.ppermute(after(piece, swapped[max(at - 2, 0) : max(at - 1, 0)]), "groups", SWAP))
         weights = [down_weight] + above + swapped[1:4:2] + below + swapped[0:4:2] + opposite + swapped[4:]
-        flags = jnp.stack([core, (group == core).astype(core.dtype), 1 - side])
-        blocks_of = [[(0, shard)]] + [list(zip(range(at, at + 4), 2 * lengths)) for at in (1, 5, 0)]
-        spots = lax.rem(high + jnp.array([0, 1, 3, 2], jnp.int32), highs)
+        flags = jnp.stack([core, (group == core).astype(core.dtype)])
+        blocks_of = [list(zip(range(at, at + 4), 2 * lengths)) for at in (1, 5, 0)]
+        blocks_of.insert(2, [(0, shard)])
+        spots = lax.rem(high + jnp.array([1, 3, 0, 2], jnp.int32), highs)
         spots = jnp.stack([(spots * 2 + side) * stride + core * span, spots * span])
         own_residual = passages
 
@@ -319,7 +329,6 @@
         spots = jnp.zeros((2, 1), jnp.int32)
         own_residual = features(passages, side)
         summands, pieces = [], []
-        partner_hidden = lax.dynamic_index_in_dim(partner_hidden, 1 - side, keepdims=False)
         for source, flat in enumerate((hidden, partner_hidden)):
             kept, away = (
                 lax.dot_general(flat, part, (((1,), (1,)), ((), ())), preferred_element_type=jnp.float32)[None]
@@ -341,7 +350,6 @@
         [lax.dynamic_slice_in_dim(owner_place, at, blocks) for at in (own_at, partner_at)]
     )
 
-    leaving = after(leaving, [partner_hidden])
     partner = lax.ppermute(leaving, "side", SWAP)
     packed = (members, 2 * held // 128 * query_len + 8, 128)
     operands = summands + [own_residual, partner]

time: 126 us -> 97.8 us (0.78)
  between operations: 13.7 us -> 0.26 us
  local copies, waits for them, and re-layouts: 14.4 us -> 8.82 us
  waiting for transfers between devices: 52.1 us -> 46.6 us
  other arithmetic: 3.67 us -> 1.2 us
    all_gather x1 -> x0, waiting for transfers between devices: 9.01 us -> none  [body(): partner_hidden = lax.all_gather(hidden, 'side')]
    unnamed x49 -> x35, local copies, waits for them, and re-layouts: 12.3 us -> 6.48 us
    ppermute x9, starting transfers between devices: 16.8 us -> 13.1 us  [shifted(): lax.ppermute(array, 'high', [(at, (at + shift) % highs) for at in range(h...]
    ppermute x0 -> x1, starting transfers between devices: none -> 2.94 us  [body(): partner_hidden = lax.ppermute(hidden, 'side', SWAP)]
    unnamed x2 -> x0, other arithmetic: 1.86 us -> none
    ppermute x9, waiting for transfers between devices: 27.3 us -> 29 us  [shifted(): lax.ppermute(array, 'high', [(at, (at + shift) % highs) for at in range(h...]
    ppermute x4, waiting for transfers between devices: 1.47 us -> 3.1 us  [body(): others = [lax.ppermute(piece, 'mp', SWAP) for piece in away + late_away]]
    ppermute x6, waiting for transfers between devices: 11 us -> 12.6 us  [body(): lax.ppermute(after(piece, swapped[max(at - 2, 0):max(at - 1, 0)]), 'group...]
  transfers between devices with their start and end apart: 24 -> 24, of which waited for: 13 -> 15; matrix products, arithmetic and copies ran while one was open for 6% -> 4% of each run, Pallas kernels for 9% -> 10%
where the time goes in v8:
time: 97.8 us; the launch traced here: 97.4 us
  waiting for transfers between devices  46.6 us (48%)
  starting transfers between devices  27.5 us (28%)
  Pallas kernels  13.1 us (13%)
  local copies, waits for them, and re-layouts  8.82 us (9%)
  other arithmetic  1.2 us (1%)
    ppermute x9, waiting for transfers between devices, shifted(): lax.ppermute(array, 'high', [(at, (at + shift) % highs) for at in range(h...  29 us
    ppermute x9, starting transfers between devices, shifted(): lax.ppermute(array, 'high', [(at, (at + shift) % highs) for at in range(h...  13.1 us
    ppermute x6, waiting for transfers between devices, body(): lax.ppermute(after(piece, swapped[max(at - 2, 0):max(at - 1, 0)]), 'group...  12.6 us
    pallas_call x2, Pallas kernels, project(): pl.pallas_call(functools.partial(project_kernel, blocks=blocks, sends=sen...  9.72 us
    ppermute x6, starting transfers between devices, body(): lax.ppermute(after(piece, swapped[max(at - 2, 0):max(at - 1, 0)]), 'group...  7.09 us
    unnamed x35, local copies, waits for them, and re-layouts  6.48 us
    ppermute x4, waiting for transfers between devices, body(): others = [lax.ppermute(piece, 'mp', SWAP) for piece in away + late_away]  3.1 us
    ppermute x1, starting transfers between devices, body(): partner_hidden = lax.ppermute(hidden, 'side', SWAP)  2.94 us
  transfers between devices with their start and end apart: 24, of which 15 were waited for; matrix products, arithmetic and copies ran while one was open for 4% of the time, Pallas kernels for 10%

profile of v8, /device:TPU:0, one launch (start us, length us, event | category | flops | bytes accessed | tf_op | source)
XLA Modules:
  0.0 97.4 jit_solution(9302220449073541719)
XLA Ops:
  0.0 2.9 %collective-permute-start.5 = (bf16[512,2560]{1,0:T(8,128)(2,1)}, bf16[512,2560]{1,0:T(8,128)(2,1)}, u32[]{:S(2)}, u32[]{:S(2)}) collective-permute-start(bf16[512,2560]{1,0:T(8,128)(2,1)} %bitcast.11), channel_id=1, source_target_pairs={{0,2},{2,0},{1,3},{3,1},{4,6},{6,4},{5,7},{7,5},{8,10},{10,8},{9,1... | collective-permute-start | bytes 7864328 | tf_op jit(solution)/shard_map/ppermute | solution.py:275
  2.9 1.3 %constant_dynamic-slice_fusion.4 = (bf16[64,2560]{1,0:T(8,128)(2,1)S(1)}, bf16[64,2560]{1,0:T(8,128)(2,1)S(1)}) fusion(bf16[256,2560]{1,0:T(8,128)(2,1)} %refs_0_.1, s32[]{:T(128)S(6)} %select_n.73, s32[]{:T(128)S(6)} %select_n.72), kind=kLoop, calls=%fused_computation.41 | loop fusion | bytes 1310728 | tf_op jit(solution)/shard_map/dynamic_slice | solution.py:284
  4.2 1.6 %collective-permute-start.2 = (bf16[64,2560]{1,0:T(8,128)(2,1)S(1)}, bf16[64,2560]{1,0:T(8,128)(2,1)S(1)}, u32[]{:S(2)}, u32[]{:S(2)}) collective-permute-start(bf16[64,2560]{1,0:T(8,128)(2,1)S(1)} %get-tuple-element.59), channel_id=1, source_target_pairs={{0,4},{4,8},{8,12},{12,0},{1,5},{5,9},{9,13},{13,1},{2,6},{6,10},{... | collective-permute-start | bytes 983048 | tf_op jit(solution)/shard_map/ppermute | solution.py:272
  5.8 2.2 %collective-permute-start = (bf16[64,2560]{1,0:T(8,128)(2,1)S(1)}, bf16[64,2560]{1,0:T(8,128)(2,1)S(1)}, u32[]{:S(2)}, u32[]{:S(2)}) collective-permute-start(bf16[64,2560]{1,0:T(8,128)(2,1)S(1)} %get-tuple-element.59), channel_id=1, source_target_pairs={{0,12},{4,0},{8,4},{12,8},{1,13},{5,1},{9,5},{13,9},{2,14},{6,2},{... | collective-permute-start | bytes 983048 | tf_op jit(solution)/shard_map/ppermute | solution.py:272
  9.7 7.0 %collective-permute-done.2.refs_5_ = bf16[64,2560]{1,0:T(8,128)(2,1)S(1)} collective-permute-done((bf16[64,2560]{1,0:T(8,128)(2,1)S(1)}, bf16[64,2560]{1,0:T(8,128)(2,1)S(1)}, u32[]{:S(2)}, u32[]{:S(2)}) %collective-permute-start.2) | collective-permute-done | bytes 327712 | tf_op jit(solution)/shard_map/ppermute | solution.py:272
  16.7 5.8 %collective-permute-done.refs_1_ = bf16[64,2560]{1,0:T(8,128)(2,1)S(1)} collective-permute-done((bf16[64,2560]{1,0:T(8,128)(2,1)S(1)}, bf16[64,2560]{1,0:T(8,128)(2,1)S(1)}, u32[]{:S(2)}, u32[]{:S(2)}) %collective-permute-start) | collective-permute-done | bytes 327712 | tf_op jit(solution)/shard_map/ppermute | solution.py:272
  22.5 2.8 %collective-permute-start.1 = (bf16[72,2560]{1,0:T(8,128)(2,1)}, bf16[72,2560]{1,0:T(8,128)(2,1)S(1)}, u32[]{:S(2)}, u32[]{:S(2)}) collective-permute-start(bf16[72,2560]{1,0:T(8,128)(2,1)} %pad_maximum_fusion), channel_id=1, source_target_pairs={{0,12},{4,0},{8,4},{12,8},{1,13},{5,1},{9,5},{13,9},{2,14},{6,2},{... | collective-permute-start | bytes 1105928 | tf_op jit(solution)/shard_map/ppermute | solution.py:272
  25.4 1.5 %collective-permute-start.8 = (bf16[64,2560]{1,0:T(8,128)(2,1)S(1)}, bf16[64,2560]{1,0:T(8,128)(2,1)S(1)}, u32[]{:S(2)}, u32[]{:S(2)}) collective-permute-start(bf16[64,2560]{1,0:T(8,128)(2,1)S(1)} %collective-permute-done.2.refs_5_), channel_id=1, source_target_pairs={{0,16},{16,0},{1,17},{17,1},{2,18},{18,2},{3,19},{19,3},{4,20},{20... | collective-permute-start | bytes 983048 | tf_op jit(solution)/shard_map/ppermute | solution.py:302
  28.2 7.8 %collective-permute-done.8.refs_7_ = bf16[64,2560]{1,0:T(8,128)(2,1)S(1)} collective-permute-done((bf16[64,2560]{1,0:T(8,128)(2,1)S(1)}, bf16[64,2560]{1,0:T(8,128)(2,1)S(1)}, u32[]{:S(2)}, u32[]{:S(2)}) %collective-permute-start.8) | collective-permute-done | bytes 327712 | tf_op jit(solution)/shard_map/ppermute | solution.py:302
  36.7 1.5 %collective-permute-start.9 = (bf16[72,2560]{1,0:T(8,128)(2,1)S(1)}, bf16[72,2560]{1,0:T(8,128)(2,1)}, u32[]{:S(2)}, u32[]{:S(2)}) collective-permute-start(bf16[72,2560]{1,0:T(8,128)(2,1)S(1)} %collective-permute-done.3.refs_6_), channel_id=1, source_target_pairs={{0,16},{16,0},{1,17},{17,1},{2,18},{18,2},{3,19},{19,3},{4,20},{20... | collective-permute-start | bytes 1105928 | tf_op jit(solution)/shard_map/ppermute | solution.py:302
  38.3 4.8 %collective-permute-done.6.refs_3_ = bf16[64,2560]{1,0:T(8,128)(2,1)S(1)} collective-permute-done((bf16[64,2560]{1,0:T(8,128)(2,1)S(1)}, bf16[64,2560]{1,0:T(8,128)(2,1)S(1)}, u32[]{:S(2)}, u32[]{:S(2)}) %collective-permute-start.6) | collective-permute-done | bytes 327712 | tf_op jit(solution)/shard_map/ppermute | solution.py:302
  43.8 1.5 %collective-permute-start.7 = (bf16[72,2560]{1,0:T(8,128)(2,1)S(1)}, bf16[72,2560]{1,0:T(8,128)(2,1)}, u32[]{:S(2)}, u32[]{:S(2)}) collective-permute-start(bf16[72,2560]{1,0:T(8,128)(2,1)S(1)} %collective-permute-done.1.refs_2_), channel_id=1, source_target_pairs={{0,16},{16,0},{1,17},{17,1},{2,18},{18,2},{3,19},{19,3},{4,20},{20... | collective-permute-start | bytes 1105928 | tf_op jit(solution)/shard_map/ppermute | solution.py:302
  45.4 0.9 collective-permute-start.10
  46.6 12.3 %collective-permute-done.10.refs_0_ = bf16[64,2560]{1,0:T(8,128)(2,1)S(1)} collective-permute-done((bf16[64,2560]{1,0:T(8,128)(2,1)S(1)}, bf16[64,2560]{1,0:T(8,128)(2,1)S(1)}, u32[]{:S(2)}, u32[]{:S(2)}) %collective-permute-start.10) | collective-permute-done | bytes 327712 | tf_op jit(solution)/shard_map/ppermute | solution.py:272
  59.4 1.5 %collective-permute-start.12 = (bf16[72,2560]{1,0:T(8,128)(2,1)S(1)}, bf16[72,2560]{1,0:T(8,128)(2,1)S(1)}, u32[]{:S(2)}, u32[]{:S(2)}) collective-permute-start(bf16[72,2560]{1,0:T(8,128)(2,1)S(1)} %collective-permute-done.4.refs_1_), channel_id=1, source_target_pairs={{0,16},{16,0},{1,17},{17,1},{2,18},{18,2},{3,19},{19,3},{4,20},{20... | collective-permute-start | bytes 1105928 | tf_op jit(solution)/shard_map/ppermute | solution.py:302
  61.0 1.0 %collective-permute-start.17 = (bf16[576,512]{1,0:T(8,128)(2,1)S(1)}, bf16[576,512]{1,0:T(8,128)(2,1)S(1)}, u32[]{:S(2)}, u32[]{:S(2)}) collective-permute-start(bf16[576,512]{1,0:T(8,128)(2,1)S(1)} %constant_dynamic-update-slice_fusion.16), channel_id=1, source_target_pairs={{0,2},{2,0},{1,3},{3,1},{4,6},{6,4},{5,7},{7,5},{8,10},{10,8},{9,1... | collective-permute-start | bytes 1769480 | tf_op jit(solution)/shard_map/ppermute | solution.py:353
  62.1 1.3 %copy-done.2 = bf16[256,2560]{1,0:T(8,128)(2,1)S(1)} copy-done((bf16[256,2560]{1,0:T(8,128)(2,1)S(1)}, bf16[256,2560]{1,0:T(8,128)(2,1)}, u32[]{:S(2)}) %copy-start.2) | copy-done | bytes 1310744
  63.4 1.0 copy-done.4
  64.4 1.0 copy-done.6
  65.4 1.0 copy-done.8
  66.3 7.6 %project_near.1 = (f32[6,512,128]{2,1,0:T(8,128)S(1)}, f32[2,512,128]{2,1,0:T(8,128)S(1)}, f32[2,512,128]{2,1,0:T(8,128)S(1)}, f32[2,512,128]{2,1,0:T(8,128)S(1)}, bf16[512,2560]{1,0:T(8,128)(2,1)S(1)}) custom-call(s32[2]{0:T(128)S(1)} %pad_add_fusion.3.flag_ref, bf16[512,2560]{1,0:T(8,128)(2,1)S(1)} %bitcast.12, ...), custom_call_target="tpu_custom_call" | custom-call | flops 1 | bytes 1 | tf_op jit(solution)/shard_map/project_near/pallas_call | solution.py:215
  74.0 2.1 %project_far.1 = (f32[2,512,128]{2,1,0:T(8,128)S(1)}, f32[2,512,128]{2,1,0:T(8,128)S(1)}) custom-call(s32[2]{0:T(128)S(1)} %pad_add_fusion.3.flag_ref, bf16[512,2560]{1,0:T(8,128)(2,1)S(1)} %bitcast.13, bf16[512,2560]{1,0:T(8,128)(2,1)S(1)} %get-tuple-element.43.partner_ref, bf16[64,2560]{1,0:T(8,128)(2,1)S(1)} %collective-permute-done.10.refs_0_, ...), custom_call_target="tpu_custom_call" | custom-call | flops 1 | bytes 1 | tf_op jit(solution)/shard_map/project_far/pallas_call | solution.py:215
  77.2 0.8 collective-permute-done.16.refs_5_
  80.3 2.0 %attend.1 = f32[4,136,128]{2,1,0:T(8,128)S(1)} custom-call(s32[4]{0:T(128)S(1)} %pad_add_fusion.2.place_ref, s32[2,4]{1,0:T(2,128)S(1)} %pad_add_fusion.spot_ref, bf16[64,512]{1,0:T(8,128)(2,1)S(1)} %get-tuple-element.74.query_ref, f32[6,512,128]{2,1,0:T(8,128)S(1)} %get-tuple-element.41.refs_0_, f32[2,512,128]{2,1,0:T(8,128)S(1)} %get-tuple-element.47.refs_1_, ...), custom_call_target="tpu_custom_call" | custom-call | tf_op jit(solution)/shard_map/attend/pallas_call | solution.py:356
  82.4 1.6 %collective-permute-start.18 = (f32[1,136,128]{2,1,0:T(8,128)S(1)}, f32[1,136,128]{2,1,0:T(8,128)S(1)}, u32[]{:S(2)}, u32[]{:S(2)}) collective-permute-start(f32[1,136,128]{2,1,0:T(8,128)S(1)} %get-tuple-element.63), channel_id=1, source_target_pairs={{0,4},{4,8},{8,12},{12,0},{1,5},{5,9},{9,13},{13,1},{2,6},{6,10},{... | collective-permute-start | bytes 208904 | tf_op jit(solution)/shard_map/ppermute | solution.py:272
  84.0 2.6 %collective-permute-start.19 = (f32[1,136,128]{2,1,0:T(8,128)S(1)}, f32[1,136,128]{2,1,0:T(8,128)S(1)}, u32[]{:S(2)}, u32[]{:S(2)}) collective-permute-start(f32[1,136,128]{2,1,0:T(8,128)S(1)} %get-tuple-element.62), channel_id=1, source_target_pairs={{0,8},{4,12},{8,0},{12,4},{1,9},{5,13},{9,1},{13,5},{2,10},{6,14},... | collective-permute-start | bytes 208904 | tf_op jit(solution)/shard_map/ppermute | solution.py:272
  86.6 1.3 %collective-permute-start.20 = (f32[1,136,128]{2,1,0:T(8,128)S(1)}, f32[1,136,128]{2,1,0:T(8,128)S(1)}, u32[]{:S(2)}, u32[]{:S(2)}) collective-permute-start(f32[1,136,128]{2,1,0:T(8,128)S(1)} %get-tuple-element.61), channel_id=1, source_target_pairs={{0,12},{4,0},{8,4},{12,8},{1,13},{5,1},{9,5},{13,9},{2,14},{6,2},{... | collective-permute-start | bytes 208904 | tf_op jit(solution)/shard_map/ppermute | solution.py:272
  87.9 0.9 collective-permute-done.18.refs_1_
  88.8 2.7 %collective-permute-done.19.refs_2_ = f32[1,136,128]{2,1,0:T(8,128)S(1)} collective-permute-done((f32[1,136,128]{2,1,0:T(8,128)S(1)}, f32[1,136,128]{2,1,0:T(8,128)S(1)}, u32[]{:S(2)}, u32[]{:S(2)}) %collective-permute-start.19) | collective-permute-done | bytes 69664 | tf_op jit(solution)/shard_map/ppermute | solution.py:272
  92.1 0.8 collective-permute-start.22
  93.2 1.1 %collective-permute-start.21 = (bf16[1,16,512]{2,1,0:T(8,128)(2,1)S(1)}, bf16[1,16,512]{2,1,0:T(8,128)(2,1)S(1)}, u32[]{:S(2)}, u32[]{:S(2)}) collective-permute-start(bf16[1,16,512]{2,1,0:T(8,128)(2,1)S(1)} %get-tuple-element.90.mine_ref), channel_id=1, source_target_pairs={{0,1},{1,0},{2,3},{3,2},{4,5},{5,4},{6,7},{7,6},{8,9},{9,8},{10,11... | collective-permute-start | bytes 49160 | tf_op jit(solution)/shard_map/ppermute | solution.py:379
  96.2 1.2 %assemble.1 = bf16[1,16,2048]{2,1,0:T(8,128)(2,1)} custom-call(s32[2]{0:T(128)S(1)} %pad_add_fusion.1.flag_ref, bf16[1,16,512]{2,1,0:T(8,128)(2,1)S(1)} %get-tuple-element.90.mine_ref, bf16[1,16,512]{2,1,0:T(8,128)(2,1)S(1)} %collective-permute-done.21.core_ref, bf16[1,16,512]{2,1,0:T(8,128)(2,1)S(1)} %collective-permute-done.22.side_ref, ...), custom_call_target="tpu_custom_call" | custom-call | tf_op jit(solution)/shard_map/assemble/pallas_call | solution.py:388
  (80 shorter events, 11.5 us)
Async XLA Ops:
  0.0 60.9 %collective-permute-start.5 = (bf16[512,2560]{1,0:T(8,128)(2,1)}, bf16[512,2560]{1,0:T(8,128)(2,1)}, u32[]{:S(2)}, u32[]{:S(2)}) collective-permute-start(bf16[512,2560]{1,0:T(8,128)(2,1)} %bitcast.11), channel_id=1, source_target_pairs={{0,2},{2,0},{1,3},{3,1},{4,6},{6,4},{5,7},{7,5},{8,10},{10,8},{9,1... | collective-permute-start | bytes 7864328 | tf_op jit(solution)/shard_map/ppermute | solution.py:275
  2.9 25.2 %copy-start.12 = (s32[8]{0:T(128)S(1)}, s32[8]{0:T(128)}, u32[]{:S(2)}) copy-start(s32[8]{0:T(128)} %param.11) | copy-start | bytes 100
  2.9 25.2 %copy-start.13 = (s32[16,1]{0,1:T(1,128)S(1)}, s32[16,1]{0,1:T(1,128)}, u32[]{:S(2)}) copy-start(s32[16,1]{0,1:T(1,128)} %param.10) | copy-start | bytes 196
  2.9 43.4 %copy-start.1 = (bf16[2,256,2048]{2,1,0:T(8,128)(2,1)S(1)}, bf16[2,256,2048]{2,1,0:T(8,128)(2,1)}, u32[]{:S(2)}) copy-start(bf16[2,256,2048]{2,1,0:T(8,128)(2,1)} %param.8) | copy-start | bytes 6291460
  4.2 12.5 %collective-permute-start.2 = (bf16[64,2560]{1,0:T(8,128)(2,1)S(1)}, bf16[64,2560]{1,0:T(8,128)(2,1)S(1)}, u32[]{:S(2)}, u32[]{:S(2)}) collective-permute-start(bf16[64,2560]{1,0:T(8,128)(2,1)S(1)} %get-tuple-element.59), channel_id=1, source_target_pairs={{0,4},{4,8},{8,12},{12,0},{1,5},{5,9},{9,13},{13,1},{2,6},{6,10},{... | collective-permute-start | bytes 983048 | tf_op jit(solution)/shard_map/ppermute | solution.py:272
  5.8 16.7 %collective-permute-start = (bf16[64,2560]{1,0:T(8,128)(2,1)S(1)}, bf16[64,2560]{1,0:T(8,128)(2,1)S(1)}, u32[]{:S(2)}, u32[]{:S(2)}) collective-permute-start(bf16[64,2560]{1,0:T(8,128)(2,1)S(1)} %get-tuple-element.59), channel_id=1, source_target_pairs={{0,12},{4,0},{8,4},{12,8},{1,13},{5,1},{9,5},{13,9},{2,14},{6,2},{... | collective-permute-start | bytes 983048 | tf_op jit(solution)/shard_map/ppermute | solution.py:272
  16.7 20.0 %collective-permute-start.3 = (bf16[72,2560]{1,0:T(8,128)(2,1)}, bf16[72,2560]{1,0:T(8,128)(2,1)S(1)}, u32[]{:S(2)}, u32[]{:S(2)}) collective-permute-start(bf16[72,2560]{1,0:T(8,128)(2,1)} %pad_maximum_fusion), channel_id=1, source_target_pairs={{0,4},{4,8},{8,12},{12,0},{1,5},{5,9},{9,13},{13,1},{2,6},{6,10},{... | collective-permute-start | bytes 1105928 | tf_op jit(solution)/shard_map/ppermute | solution.py:272
  22.5 21.2 %collective-permute-start.1 = (bf16[72,2560]{1,0:T(8,128)(2,1)}, bf16[72,2560]{1,0:T(8,128)(2,1)S(1)}, u32[]{:S(2)}, u32[]{:S(2)}) collective-permute-start(bf16[72,2560]{1,0:T(8,128)(2,1)} %pad_maximum_fusion), channel_id=1, source_target_pairs={{0,12},{4,0},{8,4},{12,8},{1,13},{5,1},{9,5},{13,9},{2,14},{6,2},{... | collective-permute-start | bytes 1105928 | tf_op jit(solution)/shard_map/ppermute | solution.py:272
  25.4 10.6 %collective-permute-start.8 = (bf16[64,2560]{1,0:T(8,128)(2,1)S(1)}, bf16[64,2560]{1,0:T(8,128)(2,1)S(1)}, u32[]{:S(2)}, u32[]{:S(2)}) collective-permute-start(bf16[64,2560]{1,0:T(8,128)(2,1)S(1)} %collective-permute-done.2.refs_5_), channel_id=1, source_target_pairs={{0,16},{16,0},{1,17},{17,1},{2,18},{18,2},{3,19},{19,3},{4,20},{20... | collective-permute-start | bytes 983048 | tf_op jit(solution)/shard_map/ppermute | solution.py:302
  26.9 16.1 %collective-permute-start.6 = (bf16[64,2560]{1,0:T(8,128)(2,1)S(1)}, bf16[64,2560]{1,0:T(8,128)(2,1)S(1)}, u32[]{:S(2)}, u32[]{:S(2)}) collective-permute-start(bf16[64,2560]{1,0:T(8,128)(2,1)S(1)} %collective-permute-done.refs_1_), channel_id=1, source_target_pairs={{0,16},{16,0},{1,17},{17,1},{2,18},{18,2},{3,19},{19,3},{4,20},{20... | collective-permute-start | bytes 983048 | tf_op jit(solution)/shard_map/ppermute | solution.py:302
  36.7 22.1 %collective-permute-start.9 = (bf16[72,2560]{1,0:T(8,128)(2,1)S(1)}, bf16[72,2560]{1,0:T(8,128)(2,1)}, u32[]{:S(2)}, u32[]{:S(2)}) collective-permute-start(bf16[72,2560]{1,0:T(8,128)(2,1)S(1)} %collective-permute-done.3.refs_6_), channel_id=1, source_target_pairs={{0,16},{16,0},{1,17},{17,1},{2,18},{18,2},{3,19},{19,3},{4,20},{20... | collective-permute-start | bytes 1105928 | tf_op jit(solution)/shard_map/ppermute | solution.py:302
  43.8 15.6 %collective-permute-start.7 = (bf16[72,2560]{1,0:T(8,128)(2,1)S(1)}, bf16[72,2560]{1,0:T(8,128)(2,1)}, u32[]{:S(2)}, u32[]{:S(2)}) collective-permute-start(bf16[72,2560]{1,0:T(8,128)(2,1)S(1)} %collective-permute-done.1.refs_2_), channel_id=1, source_target_pairs={{0,16},{16,0},{1,17},{17,1},{2,18},{18,2},{3,19},{19,3},{4,20},{20... | collective-permute-start | bytes 1105928 | tf_op jit(solution)/shard_map/ppermute | solution.py:302
  45.3 14.1 %collective-permute-start.4 = (bf16[72,2560]{1,0:T(8,128)(2,1)S(1)}, bf16[72,2560]{1,0:T(8,128)(2,1)S(1)}, u32[]{:S(2)}, u32[]{:S(2)}) collective-permute-start(bf16[72,2560]{1,0:T(8,128)(2,1)S(1)} %collective-permute-done.3.refs_6_), channel_id=1, source_target_pairs={{0,4},{4,8},{8,12},{12,0},{1,5},{5,9},{9,13},{13,1},{2,6},{6,10},{... | collective-permute-start | bytes 1105928 | tf_op jit(solution)/shard_map/ppermute | solution.py:272
  45.4 13.5 %collective-permute-start.10 = (bf16[64,2560]{1,0:T(8,128)(2,1)S(1)}, bf16[64,2560]{1,0:T(8,128)(2,1)S(1)}, u32[]{:S(2)}, u32[]{:S(2)}) collective-permute-start(bf16[64,2560]{1,0:T(8,128)(2,1)S(1)} %collective-permute-done.2.refs_5_), channel_id=1, source_target_pairs={{0,4},{4,8},{8,12},{12,0},{1,5},{5,9},{9,13},{13,1},{2,6},{6,10},{... | collective-permute-start | bytes 983048 | tf_op jit(solution)/shard_map/ppermute | solution.py:272
  46.3 14.6 %copy-start.10 = (bf16[8,2560]{1,0:T(8,128)(2,1)S(1)}, bf16[8,2560]{1,0:T(8,128)(2,1)}, u32[]{:S(2)}) copy-start(bf16[8,2560]{1,0:T(8,128)(2,1)} %copy-done.9) | copy-start | bytes 122884
  46.3 15.8 %copy-start = (bf16[2,256,2560]{2,1,0:T(8,128)(2,1)S(1)}, bf16[2,256,2560]{2,1,0:T(8,128)(2,1)}, u32[]{:S(2)}) copy-start(bf16[2,256,2560]{2,1,0:T(8,128)(2,1)} %param.7) | copy-start | bytes 7864324
  58.8 15.1 %collective-permute-start.11 = (bf16[64,2560]{1,0:T(8,128)(2,1)S(1)}, bf16[64,2560]{1,0:T(8,128)(2,1)S(1)}, u32[]{:S(2)}, u32[]{:S(2)}) collective-permute-start(bf16[64,2560]{1,0:T(8,128)(2,1)S(1)} %collective-permute-done.10.refs_0_), channel_id=1, source_target_pairs={{0,16},{16,0},{1,17},{17,1},{2,18},{18,2},{3,19},{19,3},{4,20},{20... | collective-permute-start | bytes 983048 | tf_op jit(solution)/shard_map/ppermute | solution.py:302
  59.4 14.6 %collective-permute-start.12 = (bf16[72,2560]{1,0:T(8,128)(2,1)S(1)}, bf16[72,2560]{1,0:T(8,128)(2,1)S(1)}, u32[]{:S(2)}, u32[]{:S(2)}) collective-permute-start(bf16[72,2560]{1,0:T(8,128)(2,1)S(1)} %collective-permute-done.4.refs_1_), channel_id=1, source_target_pairs={{0,16},{16,0},{1,17},{17,1},{2,18},{18,2},{3,19},{19,3},{4,20},{20... | collective-permute-start | bytes 1105928 | tf_op jit(solution)/shard_map/ppermute | solution.py:302
  61.0 19.3 %collective-permute-start.17 = (bf16[576,512]{1,0:T(8,128)(2,1)S(1)}, bf16[576,512]{1,0:T(8,128)(2,1)S(1)}, u32[]{:S(2)}, u32[]{:S(2)}) collective-permute-start(bf16[576,512]{1,0:T(8,128)(2,1)S(1)} %constant_dynamic-update-slice_fusion.16), channel_id=1, source_target_pairs={{0,2},{2,0},{1,3},{3,1},{4,6},{6,4},{5,7},{7,5},{8,10},{10,8},{9,1... | collective-permute-start | bytes 1769480 | tf_op jit(solution)/shard_map/ppermute | solution.py:353
  62.1 1.3 %copy-start.2 = (bf16[256,2560]{1,0:T(8,128)(2,1)S(1)}, bf16[256,2560]{1,0:T(8,128)(2,1)}, u32[]{:S(2)}) copy-start(bf16[256,2560]{1,0:T(8,128)(2,1)} %refs_0_.1) | copy-start | bytes 3932164
  63.4 1.0 copy-start.4
  74.0 3.2 %copy-start.11 = (s32[4]{0:T(128)S(1)}, s32[4]{0:T(128)}, u32[]{:S(2)}) copy-start(s32[4]{0:T(128)} %constant.99.clone) | copy-start | bytes 52
  76.1 2.0 %collective-permute-start.16 = (f32[2,512,128]{2,1,0:T(8,128)S(1)}, f32[2,512,128]{2,1,0:T(8,128)S(1)}, u32[]{:S(2)}, u32[]{:S(2)}) collective-permute-start(f32[2,512,128]{2,1,0:T(8,128)S(1)} %get-tuple-element.51), channel_id=1, source_target_pairs={{0,1},{1,0},{2,3},{3,2},{4,5},{5,4},{6,7},{7,6},{8,9},{9,8},{10,11... | collective-permute-start | bytes 1572872 | tf_op jit(solution)/shard_map/ppermute | solution.py:318
  76.2 2.6 %collective-permute-start.13 = (f32[2,512,128]{2,1,0:T(8,128)S(1)}, f32[2,512,128]{2,1,0:T(8,128)S(1)}, u32[]{:S(2)}, u32[]{:S(2)}) collective-permute-start(f32[2,512,128]{2,1,0:T(8,128)S(1)} %get-tuple-element.48), channel_id=1, source_target_pairs={{0,1},{1,0},{2,3},{3,2},{4,5},{5,4},{6,7},{7,6},{8,9},{9,8},{10,11... | collective-permute-start | bytes 1572872 | tf_op jit(solution)/shard_map/ppermute | solution.py:318
  76.7 2.9 %collective-permute-start.14 = (f32[2,512,128]{2,1,0:T(8,128)S(1)}, f32[2,512,128]{2,1,0:T(8,128)S(1)}, u32[]{:S(2)}, u32[]{:S(2)}) collective-permute-start(f32[2,512,128]{2,1,0:T(8,128)S(1)} %get-tuple-element.49), channel_id=1, source_target_pairs={{0,1},{1,0},{2,3},{3,2},{4,5},{5,4},{6,7},{7,6},{8,9},{9,8},{10,11... | collective-permute-start | bytes 1572872 | tf_op jit(solution)/shard_map/ppermute | solution.py:318
  76.8 3.6 %collective-permute-start.15 = (f32[2,512,128]{2,1,0:T(8,128)S(1)}, f32[2,512,128]{2,1,0:T(8,128)S(1)}, u32[]{:S(2)}, u32[]{:S(2)}) collective-permute-start(f32[2,512,128]{2,1,0:T(8,128)S(1)} %get-tuple-element.50), channel_id=1, source_target_pairs={{0,1},{1,0},{2,3},{3,2},{4,5},{5,4},{6,7},{7,6},{8,9},{9,8},{10,11... | collective-permute-start | bytes 1572872 | tf_op jit(solution)/shard_map/ppermute | solution.py:318
  82.4 6.5 %collective-permute-start.18 = (f32[1,136,128]{2,1,0:T(8,128)S(1)}, f32[1,136,128]{2,1,0:T(8,128)S(1)}, u32[]{:S(2)}, u32[]{:S(2)}) collective-permute-start(f32[1,136,128]{2,1,0:T(8,128)S(1)} %get-tuple-element.63), channel_id=1, source_target_pairs={{0,4},{4,8},{8,12},{12,0},{1,5},{5,9},{9,13},{13,1},{2,6},{6,10},{... | collective-permute-start | bytes 208904 | tf_op jit(solution)/shard_map/ppermute | solution.py:272
  84.0 7.6 %collective-permute-start.19 = (f32[1,136,128]{2,1,0:T(8,128)S(1)}, f32[1,136,128]{2,1,0:T(8,128)S(1)}, u32[]{:S(2)}, u32[]{:S(2)}) collective-permute-start(f32[1,136,128]{2,1,0:T(8,128)S(1)} %get-tuple-element.62), channel_id=1, source_target_pairs={{0,8},{4,12},{8,0},{12,4},{1,9},{5,13},{9,1},{13,5},{2,10},{6,14},... | collective-permute-start | bytes 208904 | tf_op jit(solution)/shard_map/ppermute | solution.py:272
  86.6 5.2 %collective-permute-start.20 = (f32[1,136,128]{2,1,0:T(8,128)S(1)}, f32[1,136,128]{2,1,0:T(8,128)S(1)}, u32[]{:S(2)}, u32[]{:S(2)}) collective-permute-start(f32[1,136,128]{2,1,0:T(8,128)S(1)} %get-tuple-element.61), channel_id=1, source_target_pairs={{0,12},{4,0},{8,4},{12,8},{1,13},{5,1},{9,5},{13,9},{2,14},{6,2},{... | collective-permute-start | bytes 208904 | tf_op jit(solution)/shard_map/ppermute | solution.py:272
  92.1 3.8 %collective-permute-start.22 = (bf16[1,16,512]{2,1,0:T(8,128)(2,1)S(1)}, bf16[1,16,512]{2,1,0:T(8,128)(2,1)S(1)}, u32[]{:S(2)}, u32[]{:S(2)}) collective-permute-start(bf16[1,16,512]{2,1,0:T(8,128)(2,1)S(1)} %get-tuple-element.89), channel_id=1, source_target_pairs={{0,2},{2,0},{1,3},{3,1},{4,6},{6,4},{5,7},{7,5},{8,10},{10,8},{9,1... | collective-permute-start | bytes 49160 | tf_op jit(solution)/shard_map/ppermute | solution.py:380
  92.9 3.3 %collective-permute-start.23 = (bf16[1,16,512]{2,1,0:T(8,128)(2,1)S(1)}, bf16[1,16,512]{2,1,0:T(8,128)(2,1)S(1)}, u32[]{:S(2)}, u32[]{:S(2)}) collective-permute-start(bf16[1,16,512]{2,1,0:T(8,128)(2,1)S(1)} %get-tuple-element.89), channel_id=1, source_target_pairs={{0,3},{3,0},{1,2},{2,1},{4,7},{7,4},{5,6},{6,5},{8,11},{11,8},{9,1... | collective-permute-start | bytes 49160 | tf_op jit(solution)/shard_map/ppermute | solution.py:381
  93.2 1.9 %collective-permute-start.21 = (bf16[1,16,512]{2,1,0:T(8,128)(2,1)S(1)}, bf16[1,16,512]{2,1,0:T(8,128)(2,1)S(1)}, u32[]{:S(2)}, u32[]{:S(2)}) collective-permute-start(bf16[1,16,512]{2,1,0:T(8,128)(2,1)S(1)} %get-tuple-element.90.mine_ref), channel_id=1, source_target_pairs={{0,1},{1,0},{2,3},{3,2},{4,5},{5,4},{6,7},{7,6},{8,9},{9,8},{10,11... | collective-permute-start | bytes 49160 | tf_op jit(solution)/shard_map/ppermute | solution.py:379
  (6 other events, 4.9 us)

commit v9 on v6

--- a/solution.py
+++ b/solution.py
@@ -11,6 +11,8 @@
 HEAD_DIM = 64
 EMPTY = -3e38
 FIRST_EIGHTHS = 4
+ROW_COPIES = 4
+PROJECT_LIMIT = 48 * 1024 * 1024
 VMEM_LIMIT = 22 * 1024 * 1024
 SWAP = [(0, 1), (1, 0)]
 CROSS = [(0, 3), (3, 0), (1, 2), (2, 1)]
@@ -25,34 +27,43 @@
     return picked
 
 
-def project_kernel(flag_ref, partner_ref, hidden_ref, *refs, blocks, sends):
-    *refs, rows_ref, semaphore = refs
+def project_kernel(flag_ref, *refs, sources, blocks, sends):
+    *refs, rows_ref, block_ref, row_sems, block_sems = refs
     keep_ref, *send_refs = refs[-1 - len(sends) :]
     slots = [(ref, at) for ref in send_refs for at in range(ref.shape[0])]
     core, same = flag_ref[0], flag_ref[1]
     half = keep_ref.shape[2]
-    copy = pltpu.make_async_copy(partner_ref, rows_ref, semaphore)
-    copy.start()
-    for source in range(2):
-        if source == 1:
+    row_copies, block_copies = [], []
+    for at in range(sources):
+        step = rows_ref.shape[1] // ROW_COPIES
+        row_copies.append([])
+        for part in range(ROW_COPIES):
+            rows = pl.ds(part * step, step)
+            row_copies[-1].append(
+                pltpu.make_async_copy(refs[at].at[rows], rows_ref.at[at, rows], row_sems.at[at, part])
+            )
+    for at, pieces in enumerate(blocks):
+        block_copies.append([])
+        for part, (operand, first, rows, where) in enumerate(pieces):
+            place = where + half * {"came": 1 - same, "swapped": same, "low": core, "high": 1 - core}[operand[0]]
+            block_copies[-1].append(
+                pltpu.make_async_copy(
+                    refs[operand[1]].at[pl.ds(first, rows)],
+                    block_ref.at[at, pl.ds(pl.multiple_of(place, 16), rows)],
+                    block_sems.at[at, part],
+                )
+            )
+    for copies in row_copies[:1] + block_copies + row_copies[1:]:
+        for copy in copies:
+            copy.start()
+    for source in range(sources):
+        for copy in row_copies[source]:
             copy.wait()
-        for at, pieces in enumerate(blocks):
-            if len(pieces) == 1:
-                whole = refs[pieces[0][0]]
-                keep = whole[pl.ds(pl.multiple_of(core * half, half), half), :]
-                send = whole[pl.ds(pl.multiple_of((1 - core) * half, half), half), :]
-            else:
-                parts = [refs[piece][:length] for piece, length in pieces]
-                first, second = (
-                    jnp.concatenate(part, axis=0) for part in (parts[: len(parts) // 2], parts[len(parts) // 2 :])
-                )
-                keep = jnp.where(same == 1, first, second)
-                send = jnp.where(same == 1, second, first)
+        for at in range(len(blocks)):
+            for copy in [] if source else block_copies[at]:
+                copy.wait()
             product = lax.dot_general(
-                (rows_ref if source else hidden_ref)[...],
-                jnp.concatenate([keep, send], axis=0),
-                (((1,), (1,)), ((), ())),
-                preferred_element_type=jnp.float32,
+                rows_ref[source], block_ref[at], (((1,), (1,)), ((), ())), preferred_element_type=jnp.float32
             )
             keep_ref[source * len(blocks) + at] = product[:, :half]
             send_ref, slot = slots[source * len(blocks) + at]
@@ -193,19 +204,26 @@
     return [pl.BlockSpec(memory_space=pltpu.SMEM)] * count
 
 
-def project(flags, hidden, partner, weights, blocks, sends, half, name):
-    rows, units = hidden.shape
-    counts = [2 * len(blocks)] + sends
+def project(flags, sources, weights, blocks, sends, half, name):
+    rows, units = sources[0].shape
+    counts = [len(sources) * len(blocks)] + sends
+    parts = max(len(pieces) for pieces in blocks)
+    blocks = [[((piece[0], piece[1] + len(sources)), *rest) for piece, *rest in pieces] for pieces in blocks]
     return pl.pallas_call(
-        functools.partial(project_kernel, blocks=blocks, sends=sends),
+        functools.partial(project_kernel, sources=len(sources), blocks=blocks, sends=sends),
         out_shape=[jax.ShapeDtypeStruct((count, rows, half), jnp.float32) for count in counts],
-        in_specs=in_smem(1) + [pl.BlockSpec(memory_space=pl.ANY)] + in_vmem(1 + len(weights)),
+        in_specs=in_smem(1) + [pl.BlockSpec(memory_space=pl.ANY)] * (len(sources) + len(weights)),
         out_specs=in_vmem(len(counts)),
-        scratch_shapes=[pltpu.VMEM((rows, units), hidden.dtype), pltpu.SemaphoreType.DMA(())],
-        compiler_params=pltpu.CompilerParams(vmem_limit_bytes=VMEM_LIMIT),
+        scratch_shapes=[
+            pltpu.VMEM((len(sources), rows, units), sources[0].dtype),
+            pltpu.VMEM((len(blocks), 2 * half, units), sources[0].dtype),
+            pltpu.SemaphoreType.DMA((len(sources), ROW_COPIES)),
+            pltpu.SemaphoreType.DMA((len(blocks), parts)),
+        ],
+        compiler_params=pltpu.CompilerParams(vmem_limit_bytes=PROJECT_LIMIT),
         cost_estimate=pl.CostEstimate(flops=1, bytes_accessed=1, transcendentals=0),
         name=name,
-    )(flags, partner, hidden, *weights)
+    )(flags, *sources, *weights)
 
 
 def after(array, earlier):
@@ -273,34 +291,66 @@
         for at in range(2):
             below.append(shifted(after(sent[at], below[-1:]), 1))
             above.append(shifted(after(sent[at], above[-1:]), -1))
-        opposite = [shifted(after(below[0], below[1:]), 1), shifted(below[1], 1)]
-        spreads = [sent[1], above[1], opposite[1], below[1]]
+        opposite = [shifted(piece, 1) for piece in below]
+        spreads = [piece[1][-8:] for piece in (sent, above, opposite, below)]
+        *spreads, leaving, _ = lax.optimization_barrier(
+            (*spreads, jnp.pad(leaving, ((0, highs * query_len), (0, 0))), partner_hidden)
+        )
         own_queries, partner_queries = (from_rows(spreads, slot, (query_len, held)) for slot in range(2))
+        leaving = lax.dynamic_update_slice(leaving, partner_queries, (rows, 0))
+        first, second = lengths
         swapped = []
-        for at, piece in enumerate([below[0], above[0], below[1], above[1]] + opposite):
+        for at, piece in enumerate([below[0], above[0], opposite[0], below[1], above[1], opposite[1]]):
             swapped.append(lax.ppermute(after(piece, swapped[max(at - 2, 0) : max(at - 1, 0)]), "groups", SWAP))
-        weights = [down_weight] + above + swapped[1:4:2] + below + swapped[0:4:2] + opposite + swapped[4:]
+        far = swapped[2::3]
         flags = jnp.stack([core, (group == core).astype(core.dtype)])
-        blocks_of = [[(0, shard)]] + [list(zip(range(at, at + 4), 2 * lengths)) for at in (1, 5, 0)]
+        near_weights = [down_weight] + above + below + swapped[:2] + swapped[3:5]
+        near = [
+            [(("low", 0), 0, half, 0), (("high", 0), half, half, 0)],
+            [
+                (("came", 1), 0, first, 0),
+                (("came", 2), 0, second, first),
+                (("swapped", 6), 0, first, 0),
+                (("swapped", 8), 0, second, first),
+            ],
+            [
+                (("came", 3), 0, first, 0),
+                (("came", 4), 0, second, first),
+                (("swapped", 5), 0, first, 0),
+                (("swapped", 7), 0, second, first),
+            ],
+        ]
+        far_block = [
+            (("came", 0), 0, first, 0),
+            (("came", 1), 0, second, first),
+            (("swapped", 2), 0, first, 0),
+            (("swapped", 3), 0, second, first),
+        ]
         spots = lax.rem(high + jnp.array([0, 1, 3, 2], jnp.int32), highs)
         spots = jnp.stack([(spots * 2 + side) * stride + core * span, spots * span])
         own_residual = passages
 
         kept, *away = project(
-            flags, hidden, partner_hidden, weights[:9], blocks_of[:3], [2, 2, 2], half, "project_near"
+            flags, [hidden], near_weights, near, [2, 1], half, "project_own"
         )
         flags, kept, *away = lax.optimization_barrier((flags, kept, *away))
-        late_kept, *late_away = project(
-            flags, hidden, partner_hidden, weights[9:], blocks_of[3:], [2], half, "project_far"
-        )
-        others = [lax.ppermute(piece, "mp", SWAP) for piece in away + late_away]
-        summands = [kept, late_kept] + others
-        pieces = [(at // 3, (0, at), (2 + at // 2, at % 2), at % 3) for at in range(6)]
-        pieces += [(source, (1, source), (5, source), 3) for source in range(2)]
+        partner_kept, *partner_away = project(
+            flags, [partner_hidden], near_weights, near, [2, 1], half, "project_partner"
+        )
+        flags, partner_kept, *partner_away = lax.optimization_barrier((flags, partner_kept, *partner_away))
+        far_kept, *far_away = project(
+            flags, [hidden, partner_hidden], opposite + far, [far_block], [2], half, "project_far"
+        )
+        others = [lax.ppermute(piece, "mp", SWAP) for piece in away + partner_away + far_away]
+        summands = [kept, partner_kept, far_kept] + others
+        pieces = [(0, (0, at), [(3, 0), (3, 1), (4, 0)][at], at) for at in range(3)]
+        pieces += [(1, (1, at), (5 + at // 2, at % 2), at) for at in range(3)]
+        pieces += [(source, (2, source), (7, source), 3) for source in range(2)]
         origin = high
     else:
         queries = lax.all_gather(queries, ("high", "low"), axis=0, tiled=True)
         own_queries, partner_queries = (queries[:, slot].reshape(-1, held) for slot in range(2))
+        leaving = jnp.concatenate([leaving, partner_queries], axis=0)
         weight = lax.all_gather(down_weight, ("high", "low"), axis=0, tiled=True)
         weight = jnp.where(core == 0, weight, jnp.roll(weight, held, axis=0))
         spots = jnp.zeros((2, 1), jnp.int32)
@@ -327,7 +377,6 @@
         [lax.dynamic_slice_in_dim(owner_place, at, blocks) for at in (own_at, partner_at)]
     )
 
-    leaving = jnp.concatenate([leaving, partner_queries], axis=0)
     partner = lax.ppermute(leaving, "side", SWAP)
     packed = (members, 2 * held // 128 * query_len + 8, 128)
     operands = summands + [own_residual, partner]

time: 100 us -> 108 us (1.080)
  waiting for transfers between devices: 51.1 us -> 39 us
  Pallas kernels: 14.2 us -> 23.9 us
  starting transfers between devices: 26.5 us -> 31.2 us
  local copies, waits for them, and re-layouts: 5.25 us -> 9.74 us
    ppermute x6, waiting for transfers between devices: 16.4 us -> 7.16 us  [body(): lax.ppermute(after(piece, swapped[max(at - 2, 0):max(at - 1, 0)]), 'group...]
    pallas_call x2 -> x3, Pallas kernels: 10.8 us -> 20 us  [project(): pl.pallas_call(functools.partial(project_kernel, sources=len(sources), bl...]
    ppermute x9, starting transfers between devices: 13 us -> 19.4 us  [shifted(): lax.ppermute(array, 'high', [(at, (at + shift) % highs) for at in range(h...]
    ppermute x1, waiting for transfers between devices: 5.69 us -> 0.01 us  [body(): partner_hidden = lax.ppermute(hidden, 'side', SWAP)]
    ppermute x9, waiting for transfers between devices: 23.3 us -> 27.2 us  [shifted(): lax.ppermute(array, 'high', [(at, (at + shift) % highs) for at in range(h...]
    unnamed x13 -> x43, local copies, waits for them, and re-layouts: 1.35 us -> 4.48 us
    slice x0 -> x3, local copies, waits for them, and re-layouts: none -> 2.38 us  [body(): spreads = [piece[1][-8:] for piece in (sent, above, opposite, below)]]
    ppermute x6, starting transfers between devices: 6.96 us -> 4.93 us  [body(): lax.ppermute(after(piece, swapped[max(at - 2, 0):max(at - 1, 0)]), 'group...]
  transfers between devices with their start and end apart: 24 -> 25, of which waited for: 17 -> 13; matrix products, arithmetic and copies ran while one was open for 6% -> 8% of each run, Pallas kernels for 11% -> 19%
where the time goes in v9:
time: 108 us; the launch traced here: 107 us
  waiting for transfers between devices  39 us (36%)
  starting transfers between devices  31.2 us (29%)
  Pallas kernels  23.9 us (22%)
  local copies, waits for them, and re-layouts  9.74 us (9%)
  other arithmetic  3.1 us (3%)
    ppermute x9, waiting for transfers between devices, shifted(): lax.ppermute(array, 'high', [(at, (at + shift) % highs) for at in range(h...  27.2 us
    pallas_call x3, Pallas kernels, project(): pl.pallas_call(functools.partial(project_kernel, sources=len(sources), bl...  20 us
    ppermute x9, starting transfers between devices, shifted(): lax.ppermute(array, 'high', [(at, (at + shift) % highs) for at in range(h...  19.4 us
    ppermute x6, waiting for transfers between devices, body(): lax.ppermute(after(piece, swapped[max(at - 2, 0):max(at - 1, 0)]), 'group...  7.16 us
    ppermute x6, starting transfers between devices, body(): lax.ppermute(after(piece, swapped[max(at - 2, 0):max(at - 1, 0)]), 'group...  4.93 us
    unnamed x43, local copies, waits for them, and re-layouts  4.48 us
    ppermute x1, starting transfers between devices, body(): partner_hidden = lax.ppermute(hidden, 'side', SWAP)  2.94 us
    pallas_call x1, Pallas kernels, body(): pl.pallas_call(functools.partial(attend_kernel, pieces=pieces), out_shape...  2.55 us
  transfers between devices with their start and end apart: 25, of which 13 were waited for; matrix products, arithmetic and copies ran while one was open for 8% of the time, Pallas kernels for 19%

profile of v9, /device:TPU:0, one launch (start us, length us, event | category | flops | bytes accessed | tf_op | source)
XLA Modules:
  0.0 107.2 jit_solution(97830491534292736)
XLA Ops:
  0.0 2.9 %collective-permute-start.5 = (bf16[512,2560]{1,0:T(8,128)(2,1)}, bf16[512,2560]{1,0:T(8,128)(2,1)}, u32[]{:S(2)}, u32[]{:S(2)}) collective-permute-start(bf16[512,2560]{1,0:T(8,128)(2,1)} %bitcast.11), channel_id=1, source_target_pairs={{0,2},{2,0},{1,3},{3,1},{4,6},{6,4},{5,7},{7,5},{8,10},{10,8},{9,1... | collective-permute-start | bytes 7864328 | tf_op jit(solution)/shard_map/ppermute | solution.py:277
  2.9 1.3 %constant_dynamic-slice_fusion.4 = (bf16[64,2560]{1,0:T(8,128)(2,1)S(1)}, bf16[64,2560]{1,0:T(8,128)(2,1)S(1)}) fusion(bf16[256,2560]{1,0:T(8,128)(2,1)} %refs_1_.3, s32[]{:T(128)S(6)} %select_n.73, s32[]{:T(128)S(6)} %select_n.72), kind=kLoop, calls=%fused_computation.41 | loop fusion | bytes 1310728 | tf_op jit(solution)/shard_map/dynamic_slice | solution.py:286
  4.2 1.6 %collective-permute-start.2 = (bf16[64,2560]{1,0:T(8,128)(2,1)S(1)}, bf16[64,2560]{1,0:T(8,128)(2,1)S(1)}, u32[]{:S(2)}, u32[]{:S(2)}) collective-permute-start(bf16[64,2560]{1,0:T(8,128)(2,1)S(1)} %get-tuple-element.65), channel_id=1, source_target_pairs={{0,4},{4,8},{8,12},{12,0},{1,5},{5,9},{9,13},{13,1},{2,6},{6,10},{... | collective-permute-start | bytes 983048 | tf_op jit(solution)/shard_map/ppermute | solution.py:274
  5.8 2.2 %collective-permute-start = (bf16[64,2560]{1,0:T(8,128)(2,1)S(1)}, bf16[64,2560]{1,0:T(8,128)(2,1)}, u32[]{:S(2)}, u32[]{:S(2)}) collective-permute-start(bf16[64,2560]{1,0:T(8,128)(2,1)S(1)} %get-tuple-element.65), channel_id=1, source_target_pairs={{0,12},{4,0},{8,4},{12,8},{1,13},{5,1},{9,5},{13,9},{2,14},{6,2},{... | collective-permute-start | bytes 983048 | tf_op jit(solution)/shard_map/ppermute | solution.py:274
  8.2 8.6 %collective-permute-done.2.refs_4_ = bf16[64,2560]{1,0:T(8,128)(2,1)S(1)} collective-permute-done((bf16[64,2560]{1,0:T(8,128)(2,1)S(1)}, bf16[64,2560]{1,0:T(8,128)(2,1)S(1)}, u32[]{:S(2)}, u32[]{:S(2)}) %collective-permute-start.2) | collective-permute-done | bytes 327712 | tf_op jit(solution)/shard_map/ppermute | solution.py:274
  16.7 1.5 %collective-permute-start.6 = (bf16[64,2560]{1,0:T(8,128)(2,1)S(1)}, bf16[64,2560]{1,0:T(8,128)(2,1)S(1)}, u32[]{:S(2)}, u32[]{:S(2)}) collective-permute-start(bf16[64,2560]{1,0:T(8,128)(2,1)S(1)} %collective-permute-done.2.refs_4_), channel_id=1, source_target_pairs={{0,16},{16,0},{1,17},{17,1},{2,18},{18,2},{3,19},{19,3},{4,20},{20... | collective-permute-start | bytes 983048 | tf_op jit(solution)/shard_map/ppermute | solution.py:304
  19.0 5.5 %collective-permute-start.3 = (bf16[72,2560]{1,0:T(8,128)(2,1)}, bf16[72,2560]{1,0:T(8,128)(2,1)}, u32[]{:S(2)}, u32[]{:S(2)}) collective-permute-start(bf16[72,2560]{1,0:T(8,128)(2,1)} %pad_maximum_fusion), channel_id=1, source_target_pairs={{0,4},{4,8},{8,12},{12,0},{1,5},{5,9},{9,13},{13,1},{2,6},{6,10},{... | collective-permute-start | bytes 1105928 | tf_op jit(solution)/shard_map/ppermute | solution.py:274
  24.5 1.0 collective-permute-start.1
  26.2 1.5 %collective-permute-start.7 = (bf16[64,2560]{1,0:T(8,128)(2,1)}, bf16[64,2560]{1,0:T(8,128)(2,1)}, u32[]{:S(2)}, u32[]{:S(2)}) collective-permute-start(bf16[64,2560]{1,0:T(8,128)(2,1)} %collective-permute-done.refs_2_), channel_id=1, source_target_pairs={{0,16},{16,0},{1,17},{17,1},{2,18},{18,2},{3,19},{19,3},{4,20},{20... | collective-permute-start | bytes 983048 | tf_op jit(solution)/shard_map/ppermute | solution.py:304
  27.7 5.5 %collective-permute-done.9.refs_2_ = bf16[64,2560]{1,0:T(8,128)(2,1)} collective-permute-done((bf16[64,2560]{1,0:T(8,128)(2,1)S(1)}, bf16[64,2560]{1,0:T(8,128)(2,1)}, u32[]{:S(2)}, u32[]{:S(2)}) %collective-permute-start.9) | collective-permute-done | bytes 327712 | tf_op jit(solution)/shard_map/ppermute | solution.py:274
  33.8 0.9 constant_dynamic-slice_fusion.3
  34.7 2.1 %collective-permute-done.7.refs_7_ = bf16[64,2560]{1,0:T(8,128)(2,1)} collective-permute-done((bf16[64,2560]{1,0:T(8,128)(2,1)}, bf16[64,2560]{1,0:T(8,128)(2,1)}, u32[]{:S(2)}, u32[]{:S(2)}) %collective-permute-start.7) | collective-permute-done | bytes 327712 | tf_op jit(solution)/shard_map/ppermute | solution.py:304
  36.8 4.2 %collective-permute-done.3.refs_5_ = bf16[72,2560]{1,0:T(8,128)(2,1)} collective-permute-done((bf16[72,2560]{1,0:T(8,128)(2,1)}, bf16[72,2560]{1,0:T(8,128)(2,1)}, u32[]{:S(2)}, u32[]{:S(2)}) %collective-permute-start.3) | collective-permute-done | bytes 368672 | tf_op jit(solution)/shard_map/ppermute | solution.py:274
  41.5 3.0 %collective-permute-start.4 = (bf16[72,2560]{1,0:T(8,128)(2,1)}, bf16[72,2560]{1,0:T(8,128)(2,1)}, u32[]{:S(2)}, u32[]{:S(2)}) collective-permute-start(bf16[72,2560]{1,0:T(8,128)(2,1)} %collective-permute-done.3.refs_5_), channel_id=1, source_target_pairs={{0,4},{4,8},{8,12},{12,0},{1,5},{5,9},{9,13},{13,1},{2,6},{6,10},{... | collective-permute-start | bytes 1105928 | tf_op jit(solution)/shard_map/ppermute | solution.py:274
  44.5 4.3 %collective-permute-done.1.refs_3_ = bf16[72,2560]{1,0:T(8,128)(2,1)} collective-permute-done((bf16[72,2560]{1,0:T(8,128)(2,1)}, bf16[72,2560]{1,0:T(8,128)(2,1)}, u32[]{:S(2)}, u32[]{:S(2)}) %collective-permute-start.1) | collective-permute-done | bytes 368672 | tf_op jit(solution)/shard_map/ppermute | solution.py:274
  49.4 2.0 %fusion.6 = bf16[576,512]{1,0:T(8,128)(2,1)} fusion(bf16[512,128]{1,0:T(8,128)(2,1)} %get-tuple-element.62, bf16[512,128]{1,0:T(8,128)(2,1)} %get-tuple-element.63, bf16[512,128]{1,0:T(8,128)(2,1)} %get-tuple-element.64, bf16[512,128]{1,0:T(8,128)(2,1)S(1)} %get-tuple-element.61), kind=kLoop, calls=%fused_computation.7 | loop fusion | flops 3833856 | bytes 1114112 | tf_op jit(solution)/shard_map/concatenate | solution.py:271
  52.9 1.4 %collective-permute-done.4.refs_3_ = bf16[72,2560]{1,0:T(8,128)(2,1)} collective-permute-done((bf16[72,2560]{1,0:T(8,128)(2,1)}, bf16[72,2560]{1,0:T(8,128)(2,1)}, u32[]{:S(2)}, u32[]{:S(2)}) %collective-permute-start.4) | collective-permute-done | bytes 368672 | tf_op jit(solution)/shard_map/ppermute | solution.py:274
  55.6 5.0 %collective-permute-done.11.refs_9_ = bf16[72,2560]{1,0:T(8,128)(2,1)} collective-permute-done((bf16[72,2560]{1,0:T(8,128)(2,1)}, bf16[72,2560]{1,0:T(8,128)(2,1)}, u32[]{:S(2)}, u32[]{:S(2)}) %collective-permute-start.11) | collective-permute-done | bytes 368672 | tf_op jit(solution)/shard_map/ppermute | solution.py:304
  60.6 7.0 %project_own.1 = (f32[3,512,128]{2,1,0:T(8,128)S(1)}, f32[2,512,128]{2,1,0:T(8,128)S(1)}, f32[1,512,128]{2,1,0:T(8,128)}) custom-call(s32[2]{0:T(128)S(1)} %pad_add_fusion.3.flag_ref, bf16[512,2560]{1,0:T(8,128)(2,1)} %bitcast.12, bf16[256,2560]{1,0:T(8,128)(2,1)S(1)} %copy-done.1, bf16[64,2560]{1,0:T(8,128)(2,1)} %collective-permute-done.refs_2_, ...), custom_call_target="tpu_custom_call" | custom-call | flops 1 | bytes 1 | tf_op jit(solution)/shard_map/project_own/pallas_call | solution.py:212
  67.6 0.9 copy-done.9
  71.0 1.0 copy-done.5
  71.9 1.0 copy-done.8
  72.9 6.6 %project_partner.1 = (f32[3,512,128]{2,1,0:T(8,128)S(1)}, f32[2,512,128]{2,1,0:T(8,128)S(1)}, f32[1,512,128]{2,1,0:T(8,128)S(1)}) custom-call(s32[2]{0:T(128)S(1)} %pad_add_fusion.3.flag_ref, bf16[512,2560]{1,0:T(8,128)(2,1)} %collective-permute-done.5.refs_0_.refs_1_, bf16[256,2560]{1,0:T(8,128)(2,1)S(1)} %copy-done.1, ...), custom_call_target="tpu_custom_call" | custom-call | flops 1 | bytes 1 | tf_op jit(solution)/shard_map/project_partner/pallas_call | solution.py:212
  79.5 6.4 %project_far.1 = (f32[2,512,128]{2,1,0:T(8,128)S(1)}, f32[2,512,128]{2,1,0:T(8,128)S(1)}) custom-call(s32[2]{0:T(128)S(1)} %pad_add_fusion.3.flag_ref, bf16[512,2560]{1,0:T(8,128)(2,1)S(1)} %bitcast.13, bf16[512,2560]{1,0:T(8,128)(2,1)} %collective-permute-done.5.refs_0_.refs_1_, bf16[64,2560]{1,0:T(8,128)(2,1)} %collective-permute-done.9.refs_2_, ...), custom_call_target="tpu_custom_call" | custom-call | flops 1 | bytes 1 | tf_op jit(solution)/shard_map/project_far/pallas_call | solution.py:212
  87.0 2.1 %collective-permute-done.16.refs_6_ = f32[1,512,128]{2,1,0:T(8,128)S(1)} collective-permute-done((f32[1,512,128]{2,1,0:T(8,128)S(1)}, f32[1,512,128]{2,1,0:T(8,128)S(1)}, u32[]{:S(2)}, u32[]{:S(2)}) %collective-permute-start.16) | collective-permute-done | bytes 262176 | tf_op jit(solution)/shard_map/ppermute | solution.py:344
  89.0 2.5 %attend.1 = f32[4,136,128]{2,1,0:T(8,128)S(1)} custom-call(s32[4]{0:T(128)S(1)} %pad_add_fusion.2.place_ref, s32[2,4]{1,0:T(2,128)S(1)} %pad_add_fusion.spot_ref, bf16[64,512]{1,0:T(8,128)(2,1)S(1)} %get-tuple-element.80.query_ref, f32[3,512,128]{2,1,0:T(8,128)S(1)} %copy-done.10, f32[3,512,128]{2,1,0:T(8,128)S(1)} %get-tuple-element.49.refs_1_, ...), custom_call_target="tpu_custom_call" | custom-call | tf_op jit(solution)/shard_map/attend/pallas_call | solution.py:383
  92.2 3.6 %collective-permute-start.20 = (f32[1,136,128]{2,1,0:T(8,128)S(1)}, f32[1,136,128]{2,1,0:T(8,128)S(1)}, u32[]{:S(2)}, u32[]{:S(2)}) collective-permute-start(f32[1,136,128]{2,1,0:T(8,128)S(1)} %get-tuple-element.68), channel_id=1, source_target_pairs={{0,8},{4,12},{8,0},{12,4},{1,9},{5,13},{9,1},{13,5},{2,10},{6,14},... | collective-permute-start | bytes 208904 | tf_op jit(solution)/shard_map/ppermute | solution.py:274
  95.9 1.9 %collective-permute-start.21 = (f32[1,136,128]{2,1,0:T(8,128)S(1)}, f32[1,136,128]{2,1,0:T(8,128)S(1)}, u32[]{:S(2)}, u32[]{:S(2)}) collective-permute-start(f32[1,136,128]{2,1,0:T(8,128)S(1)} %get-tuple-element.67), channel_id=1, source_target_pairs={{0,12},{4,0},{8,4},{12,8},{1,13},{5,1},{9,5},{13,9},{2,14},{6,2},{... | collective-permute-start | bytes 208904 | tf_op jit(solution)/shard_map/ppermute | solution.py:274
  98.0 3.0 %collective-permute-done.20.refs_2_ = f32[1,136,128]{2,1,0:T(8,128)S(1)} collective-permute-done((f32[1,136,128]{2,1,0:T(8,128)S(1)}, f32[1,136,128]{2,1,0:T(8,128)S(1)}, u32[]{:S(2)}, u32[]{:S(2)}) %collective-permute-start.20) | collective-permute-done | bytes 69664 | tf_op jit(solution)/shard_map/ppermute | solution.py:274
  101.2 1.6 %collective-permute-start.23 = (bf16[1,16,512]{2,1,0:T(8,128)(2,1)S(1)}, bf16[1,16,512]{2,1,0:T(8,128)(2,1)S(1)}, u32[]{:S(2)}, u32[]{:S(2)}) collective-permute-start(bf16[1,16,512]{2,1,0:T(8,128)(2,1)S(1)} %get-tuple-element.95), channel_id=1, source_target_pairs={{0,2},{2,0},{1,3},{3,1},{4,6},{6,4},{5,7},{7,5},{8,10},{10,8},{9,1... | collective-permute-start | bytes 49160 | tf_op jit(solution)/shard_map/ppermute | solution.py:407
  105.0 1.0 collective-permute-done.24.both_ref
  106.0 1.2 %assemble.1 = bf16[1,16,2048]{2,1,0:T(8,128)(2,1)} custom-call(s32[2]{0:T(128)S(1)} %pad_add_fusion.1.flag_ref, bf16[1,16,512]{2,1,0:T(8,128)(2,1)S(1)} %get-tuple-element.96.mine_ref, bf16[1,16,512]{2,1,0:T(8,128)(2,1)S(1)} %collective-permute-done.22.core_ref, bf16[1,16,512]{2,1,0:T(8,128)(2,1)S(1)} %collective-permute-done.23.side_ref, ...), custom_call_target="tpu_custom_call" | custom-call | tf_op jit(solution)/shard_map/assemble/pallas_call | solution.py:415
  (91 shorter events, 12.8 us)
Async XLA Ops:
  0.0 69.4 %collective-permute-start.5 = (bf16[512,2560]{1,0:T(8,128)(2,1)}, bf16[512,2560]{1,0:T(8,128)(2,1)}, u32[]{:S(2)}, u32[]{:S(2)}) collective-permute-start(bf16[512,2560]{1,0:T(8,128)(2,1)} %bitcast.11), channel_id=1, source_target_pairs={{0,2},{2,0},{1,3},{3,1},{4,6},{6,4},{5,7},{7,5},{8,10},{10,8},{9,1... | collective-permute-start | bytes 7864328 | tf_op jit(solution)/shard_map/ppermute | solution.py:277
  2.9 30.8 %copy-start.16 = (s32[8]{0:T(128)S(1)}, s32[8]{0:T(128)}, u32[]{:S(2)}) copy-start(s32[8]{0:T(128)} %param.11) | copy-start | bytes 100
  2.9 30.8 %copy-start.17 = (s32[16,1]{0,1:T(1,128)S(1)}, s32[16,1]{0,1:T(1,128)}, u32[]{:S(2)}) copy-start(s32[16,1]{0,1:T(1,128)} %param.10) | copy-start | bytes 196
  2.9 30.8 %copy-start.2 = (bf16[2,256,2048]{2,1,0:T(8,128)(2,1)S(1)}, bf16[2,256,2048]{2,1,0:T(8,128)(2,1)}, u32[]{:S(2)}) copy-start(bf16[2,256,2048]{2,1,0:T(8,128)(2,1)} %param.8) | copy-start | bytes 6291460
  4.2 12.5 %collective-permute-start.2 = (bf16[64,2560]{1,0:T(8,128)(2,1)S(1)}, bf16[64,2560]{1,0:T(8,128)(2,1)S(1)}, u32[]{:S(2)}, u32[]{:S(2)}) collective-permute-start(bf16[64,2560]{1,0:T(8,128)(2,1)S(1)} %get-tuple-element.65), channel_id=1, source_target_pairs={{0,4},{4,8},{8,12},{12,0},{1,5},{5,9},{9,13},{13,1},{2,6},{6,10},{... | collective-permute-start | bytes 983048 | tf_op jit(solution)/shard_map/ppermute | solution.py:274
  5.8 18.6 %collective-permute-start = (bf16[64,2560]{1,0:T(8,128)(2,1)S(1)}, bf16[64,2560]{1,0:T(8,128)(2,1)}, u32[]{:S(2)}, u32[]{:S(2)}) collective-permute-start(bf16[64,2560]{1,0:T(8,128)(2,1)S(1)} %get-tuple-element.65), channel_id=1, source_target_pairs={{0,12},{4,0},{8,4},{12,8},{1,13},{5,1},{9,5},{13,9},{2,14},{6,2},{... | collective-permute-start | bytes 983048 | tf_op jit(solution)/shard_map/ppermute | solution.py:274
  8.2 25.0 %copy-start.12 = (bf16[8,2560]{1,0:T(8,128)(2,1)}, bf16[8,2560]{1,0:T(8,128)(2,1)S(1)}, u32[]{:S(2)}) copy-start(bf16[8,2560]{1,0:T(8,128)(2,1)S(1)} %fusion.13) | copy-start | bytes 122884
  16.7 17.0 %copy-start.3 = (bf16[64,2560]{1,0:T(8,128)(2,1)}, bf16[64,2560]{1,0:T(8,128)(2,1)S(1)}, u32[]{:S(2)}) copy-start(bf16[64,2560]{1,0:T(8,128)(2,1)S(1)} %collective-permute-done.2.refs_4_) | copy-start | bytes 983044
  16.7 8.7 %collective-permute-start.6 = (bf16[64,2560]{1,0:T(8,128)(2,1)S(1)}, bf16[64,2560]{1,0:T(8,128)(2,1)S(1)}, u32[]{:S(2)}, u32[]{:S(2)}) collective-permute-start(bf16[64,2560]{1,0:T(8,128)(2,1)S(1)} %collective-permute-done.2.refs_4_), channel_id=1, source_target_pairs={{0,16},{16,0},{1,17},{17,1},{2,18},{18,2},{3,19},{19,3},{4,20},{20... | collective-permute-start | bytes 983048 | tf_op jit(solution)/shard_map/ppermute | solution.py:304
  18.3 14.9 %collective-permute-start.9 = (bf16[64,2560]{1,0:T(8,128)(2,1)S(1)}, bf16[64,2560]{1,0:T(8,128)(2,1)}, u32[]{:S(2)}, u32[]{:S(2)}) collective-permute-start(bf16[64,2560]{1,0:T(8,128)(2,1)S(1)} %collective-permute-done.2.refs_4_), channel_id=1, source_target_pairs={{0,4},{4,8},{8,12},{12,0},{1,5},{5,9},{9,13},{13,1},{2,6},{6,10},{... | collective-permute-start | bytes 983048 | tf_op jit(solution)/shard_map/ppermute | solution.py:274
  19.0 22.0 %collective-permute-start.3 = (bf16[72,2560]{1,0:T(8,128)(2,1)}, bf16[72,2560]{1,0:T(8,128)(2,1)}, u32[]{:S(2)}, u32[]{:S(2)}) collective-permute-start(bf16[72,2560]{1,0:T(8,128)(2,1)} %pad_maximum_fusion), channel_id=1, source_target_pairs={{0,4},{4,8},{8,12},{12,0},{1,5},{5,9},{9,13},{13,1},{2,6},{6,10},{... | collective-permute-start | bytes 1105928 | tf_op jit(solution)/shard_map/ppermute | solution.py:274
  24.5 24.3 %collective-permute-start.1 = (bf16[72,2560]{1,0:T(8,128)(2,1)}, bf16[72,2560]{1,0:T(8,128)(2,1)}, u32[]{:S(2)}, u32[]{:S(2)}) collective-permute-start(bf16[72,2560]{1,0:T(8,128)(2,1)} %pad_maximum_fusion), channel_id=1, source_target_pairs={{0,12},{4,0},{8,4},{12,8},{1,13},{5,1},{9,5},{13,9},{2,14},{6,2},{... | collective-permute-start | bytes 1105928 | tf_op jit(solution)/shard_map/ppermute | solution.py:274
  26.2 10.6 %collective-permute-start.7 = (bf16[64,2560]{1,0:T(8,128)(2,1)}, bf16[64,2560]{1,0:T(8,128)(2,1)}, u32[]{:S(2)}, u32[]{:S(2)}) collective-permute-start(bf16[64,2560]{1,0:T(8,128)(2,1)} %collective-permute-done.refs_2_), channel_id=1, source_target_pairs={{0,16},{16,0},{1,17},{17,1},{2,18},{18,2},{3,19},{19,3},{4,20},{20... | collective-permute-start | bytes 983048 | tf_op jit(solution)/shard_map/ppermute | solution.py:304
  33.2 15.6 %collective-permute-start.10 = (bf16[64,2560]{1,0:T(8,128)(2,1)}, bf16[64,2560]{1,0:T(8,128)(2,1)}, u32[]{:S(2)}, u32[]{:S(2)}) collective-permute-start(bf16[64,2560]{1,0:T(8,128)(2,1)} %collective-permute-done.9.refs_2_), channel_id=1, source_target_pairs={{0,16},{16,0},{1,17},{17,1},{2,18},{18,2},{3,19},{19,3},{4,20},{20... | collective-permute-start | bytes 983048 | tf_op jit(solution)/shard_map/ppermute | solution.py:304
  33.8 26.8 %copy-start.1 = (bf16[256,2560]{1,0:T(8,128)(2,1)S(1)}, bf16[256,2560]{1,0:T(8,128)(2,1)}, u32[]{:S(2)}) copy-start(bf16[256,2560]{1,0:T(8,128)(2,1)} %refs_1_.3) | copy-start | bytes 3932164
  41.0 13.4 %collective-permute-start.8 = (bf16[72,2560]{1,0:T(8,128)(2,1)}, bf16[72,2560]{1,0:T(8,128)(2,1)}, u32[]{:S(2)}, u32[]{:S(2)}) collective-permute-start(bf16[72,2560]{1,0:T(8,128)(2,1)} %collective-permute-done.3.refs_5_), channel_id=1, source_target_pairs={{0,16},{16,0},{1,17},{17,1},{2,18},{18,2},{3,19},{19,3},{4,20},{20... | collective-permute-start | bytes 1105928 | tf_op jit(solution)/shard_map/ppermute | solution.py:304
  41.5 12.9 %collective-permute-start.4 = (bf16[72,2560]{1,0:T(8,128)(2,1)}, bf16[72,2560]{1,0:T(8,128)(2,1)}, u32[]{:S(2)}, u32[]{:S(2)}) collective-permute-start(bf16[72,2560]{1,0:T(8,128)(2,1)} %collective-permute-done.3.refs_5_), channel_id=1, source_target_pairs={{0,4},{4,8},{8,12},{12,0},{1,5},{5,9},{9,13},{13,1},{2,6},{6,10},{... | collective-permute-start | bytes 1105928 | tf_op jit(solution)/shard_map/ppermute | solution.py:274
  48.8 11.8 %collective-permute-start.11 = (bf16[72,2560]{1,0:T(8,128)(2,1)}, bf16[72,2560]{1,0:T(8,128)(2,1)}, u32[]{:S(2)}, u32[]{:S(2)}) collective-permute-start(bf16[72,2560]{1,0:T(8,128)(2,1)} %collective-permute-done.1.refs_3_), channel_id=1, source_target_pairs={{0,16},{16,0},{1,17},{17,1},{2,18},{18,2},{3,19},{19,3},{4,20},{20... | collective-permute-start | bytes 1105928 | tf_op jit(solution)/shard_map/ppermute | solution.py:304
  54.4 25.1 %collective-permute-start.12 = (bf16[72,2560]{1,0:T(8,128)(2,1)}, bf16[72,2560]{1,0:T(8,128)(2,1)}, u32[]{:S(2)}, u32[]{:S(2)}) collective-permute-start(bf16[72,2560]{1,0:T(8,128)(2,1)} %collective-permute-done.4.refs_3_), channel_id=1, source_target_pairs={{0,16},{16,0},{1,17},{17,1},{2,18},{18,2},{3,19},{19,3},{4,20},{20... | collective-permute-start | bytes 1105928 | tf_op jit(solution)/shard_map/ppermute | solution.py:304
  55.6 15.1 %copy-start.15 = (s32[4]{0:T(128)S(1)}, s32[4]{0:T(128)}, u32[]{:S(2)}) copy-start(s32[4]{0:T(128)} %constant.99.clone) | copy-start | bytes 52
  69.4 17.1 %collective-permute-start.14 = (f32[1,512,128]{2,1,0:T(8,128)}, f32[1,512,128]{2,1,0:T(8,128)}, u32[]{:S(2)}, u32[]{:S(2)}) collective-permute-start(f32[1,512,128]{2,1,0:T(8,128)} %get-tuple-element.54), channel_id=1, source_target_pairs={{0,1},{1,0},{2,3},{3,2},{4,5},{5,4},{6,7},{7,6},{8,9},{9,8},{10,11... | collective-permute-start | bytes 786440 | tf_op jit(solution)/shard_map/ppermute | solution.py:344
  70.1 18.9 %collective-permute-start.18 = (bf16[576,512]{1,0:T(8,128)(2,1)}, bf16[576,512]{1,0:T(8,128)(2,1)}, u32[]{:S(2)}, u32[]{:S(2)}) collective-permute-start(bf16[576,512]{1,0:T(8,128)(2,1)} %constant_dynamic-update-slice_fusion.16), channel_id=1, source_target_pairs={{0,2},{2,0},{1,3},{3,1},{4,6},{6,4},{5,7},{7,5},{8,10},{10,8},{9,1... | collective-permute-start | bytes 1769480 | tf_op jit(solution)/shard_map/ppermute | solution.py:380
  70.7 16.3 %collective-permute-start.13 = (f32[2,512,128]{2,1,0:T(8,128)}, f32[2,512,128]{2,1,0:T(8,128)S(1)}, u32[]{:S(2)}, u32[]{:S(2)}) collective-permute-start(f32[2,512,128]{2,1,0:T(8,128)} %copy-done.11), channel_id=1, source_target_pairs={{0,1},{1,0},{2,3},{3,2},{4,5},{5,4},{6,7},{7,6},{8,9},{9,8},{10,11... | collective-permute-start | bytes 1572872 | tf_op jit(solution)/shard_map/ppermute | solution.py:344
  85.9 3.1 %collective-permute-start.17 = (f32[2,512,128]{2,1,0:T(8,128)S(1)}, f32[2,512,128]{2,1,0:T(8,128)S(1)}, u32[]{:S(2)}, u32[]{:S(2)}) collective-permute-start(f32[2,512,128]{2,1,0:T(8,128)S(1)} %get-tuple-element.57), channel_id=1, source_target_pairs={{0,1},{1,0},{2,3},{3,2},{4,5},{5,4},{6,7},{7,6},{8,9},{9,8},{10,11... | collective-permute-start | bytes 1572872 | tf_op jit(solution)/shard_map/ppermute | solution.py:344
  86.3 2.7 %collective-permute-start.15 = (f32[2,512,128]{2,1,0:T(8,128)S(1)}, f32[2,512,128]{2,1,0:T(8,128)S(1)}, u32[]{:S(2)}, u32[]{:S(2)}) collective-permute-start(f32[2,512,128]{2,1,0:T(8,128)S(1)} %get-tuple-element.55), channel_id=1, source_target_pairs={{0,1},{1,0},{2,3},{3,2},{4,5},{5,4},{6,7},{7,6},{8,9},{9,8},{10,11... | collective-permute-start | bytes 1572872 | tf_op jit(solution)/shard_map/ppermute | solution.py:344
  86.5 2.5 %collective-permute-start.16 = (f32[1,512,128]{2,1,0:T(8,128)S(1)}, f32[1,512,128]{2,1,0:T(8,128)S(1)}, u32[]{:S(2)}, u32[]{:S(2)}) collective-permute-start(f32[1,512,128]{2,1,0:T(8,128)S(1)} %get-tuple-element.56), channel_id=1, source_target_pairs={{0,1},{1,0},{2,3},{3,2},{4,5},{5,4},{6,7},{7,6},{8,9},{9,8},{10,11... | collective-permute-start | bytes 786440 | tf_op jit(solution)/shard_map/ppermute | solution.py:344
  91.6 6.4 %collective-permute-start.19 = (f32[1,136,128]{2,1,0:T(8,128)S(1)}, f32[1,136,128]{2,1,0:T(8,128)S(1)}, u32[]{:S(2)}, u32[]{:S(2)}) collective-permute-start(f32[1,136,128]{2,1,0:T(8,128)S(1)} %get-tuple-element.69), channel_id=1, source_target_pairs={{0,4},{4,8},{8,12},{12,0},{1,5},{5,9},{9,13},{13,1},{2,6},{6,10},{... | collective-permute-start | bytes 208904 | tf_op jit(solution)/shard_map/ppermute | solution.py:274
  92.2 8.7 %collective-permute-start.20 = (f32[1,136,128]{2,1,0:T(8,128)S(1)}, f32[1,136,128]{2,1,0:T(8,128)S(1)}, u32[]{:S(2)}, u32[]{:S(2)}) collective-permute-start(f32[1,136,128]{2,1,0:T(8,128)S(1)} %get-tuple-element.68), channel_id=1, source_target_pairs={{0,8},{4,12},{8,0},{12,4},{1,9},{5,13},{9,1},{13,5},{2,10},{6,14},... | collective-permute-start | bytes 208904 | tf_op jit(solution)/shard_map/ppermute | solution.py:274
  95.9 5.1 %collective-permute-start.21 = (f32[1,136,128]{2,1,0:T(8,128)S(1)}, f32[1,136,128]{2,1,0:T(8,128)S(1)}, u32[]{:S(2)}, u32[]{:S(2)}) collective-permute-start(f32[1,136,128]{2,1,0:T(8,128)S(1)} %get-tuple-element.67), channel_id=1, source_target_pairs={{0,12},{4,0},{8,4},{12,8},{1,13},{5,1},{9,5},{13,9},{2,14},{6,2},{... | collective-permute-start | bytes 208904 | tf_op jit(solution)/shard_map/ppermute | solution.py:274
  101.2 3.8 %collective-permute-start.23 = (bf16[1,16,512]{2,1,0:T(8,128)(2,1)S(1)}, bf16[1,16,512]{2,1,0:T(8,128)(2,1)S(1)}, u32[]{:S(2)}, u32[]{:S(2)}) collective-permute-start(bf16[1,16,512]{2,1,0:T(8,128)(2,1)S(1)} %get-tuple-element.95), channel_id=1, source_target_pairs={{0,2},{2,0},{1,3},{3,1},{4,6},{6,4},{5,7},{7,5},{8,10},{10,8},{9,1... | collective-permute-start | bytes 49160 | tf_op jit(solution)/shard_map/ppermute | solution.py:407
  102.8 3.2 %collective-permute-start.24 = (bf16[1,16,512]{2,1,0:T(8,128)(2,1)S(1)}, bf16[1,16,512]{2,1,0:T(8,128)(2,1)S(1)}, u32[]{:S(2)}, u32[]{:S(2)}) collective-permute-start(bf16[1,16,512]{2,1,0:T(8,128)(2,1)S(1)} %get-tuple-element.95), channel_id=1, source_target_pairs={{0,3},{3,0},{1,2},{2,1},{4,7},{7,4},{5,6},{6,5},{8,11},{11,8},{9,1... | collective-permute-start | bytes 49160 | tf_op jit(solution)/shard_map/ppermute | solution.py:408
  102.8 1.5 %collective-permute-start.22 = (bf16[1,16,512]{2,1,0:T(8,128)(2,1)S(1)}, bf16[1,16,512]{2,1,0:T(8,128)(2,1)S(1)}, u32[]{:S(2)}, u32[]{:S(2)}) collective-permute-start(bf16[1,16,512]{2,1,0:T(8,128)(2,1)S(1)} %get-tuple-element.96.mine_ref), channel_id=1, source_target_pairs={{0,1},{1,0},{2,3},{3,2},{4,5},{5,4},{6,7},{7,6},{8,9},{9,8},{10,11... | collective-permute-start | bytes 49160 | tf_op jit(solution)/shard_map/ppermute | solution.py:406
  (11 other events, 64.9 us)

commit v10 on v6

--- a/solution.py
+++ b/solution.py
@@ -11,6 +11,8 @@
 HEAD_DIM = 64
 EMPTY = -3e38
 FIRST_EIGHTHS = 4
+ROW_COPIES = 4
+PROJECT_LIMIT = 30 * 1024 * 1024
 VMEM_LIMIT = 22 * 1024 * 1024
 SWAP = [(0, 1), (1, 0)]
 CROSS = [(0, 3), (3, 0), (1, 2), (2, 1)]
@@ -25,34 +27,32 @@
     return picked
 
 
-def project_kernel(flag_ref, partner_ref, hidden_ref, *refs, blocks, sends):
-    *refs, rows_ref, semaphore = refs
+def project_kernel(flag_ref, hidden_ref, partner_ref, *refs, blocks, sends):
+    *refs, rows_ref, block_ref, semaphores = refs
     keep_ref, *send_refs = refs[-1 - len(sends) :]
     slots = [(ref, at) for ref in send_refs for at in range(ref.shape[0])]
     core, same = flag_ref[0], flag_ref[1]
     half = keep_ref.shape[2]
-    copy = pltpu.make_async_copy(partner_ref, rows_ref, semaphore)
-    copy.start()
-    for source in range(2):
-        if source == 1:
+    step = rows_ref.shape[0] // ROW_COPIES
+    copies = []
+    for part in range(ROW_COPIES):
+        rows = pl.ds(part * step, step)
+        copies.append(pltpu.make_async_copy(partner_ref.at[rows], rows_ref.at[rows], semaphores.at[part]))
+        copies[-1].start()
+    for at, (came, swapped) in enumerate(blocks):
+        if not swapped:
+            block_ref[at, :half] = refs[came][pl.ds(pl.multiple_of(core * half, half), half), :]
+            block_ref[at, half:] = refs[came][pl.ds(pl.multiple_of((1 - core) * half, half), half), :]
+        for pieces, where in ((came, (1 - same) * half), (swapped, same * half)) if swapped else ():
+            for operand, first, length in pieces:
+                place = pl.multiple_of(where + first, 16)
+                block_ref[at, pl.ds(place, length)] = refs[operand][:length]
+    for source, source_ref in enumerate((hidden_ref, rows_ref)):
+        for copy in copies if source else []:
             copy.wait()
-        for at, pieces in enumerate(blocks):
-            if len(pieces) == 1:
-                whole = refs[pieces[0][0]]
-                keep = whole[pl.ds(pl.multiple_of(core * half, half), half), :]
-                send = whole[pl.ds(pl.multiple_of((1 - core) * half, half), half), :]
-            else:
-                parts = [refs[piece][:length] for piece, length in pieces]
-                first, second = (
-                    jnp.concatenate(part, axis=0) for part in (parts[: len(parts) // 2], parts[len(parts) // 2 :])
-                )
-                keep = jnp.where(same == 1, first, second)
-                send = jnp.where(same == 1, second, first)
+        for at in range(len(blocks)):
             product = lax.dot_general(
-                (rows_ref if source else hidden_ref)[...],
-                jnp.concatenate([keep, send], axis=0),
-                (((1,), (1,)), ((), ())),
-                preferred_element_type=jnp.float32,
+                source_ref[...], block_ref[at], (((1,), (1,)), ((), ())), preferred_element_type=jnp.float32
             )
             keep_ref[source * len(blocks) + at] = product[:, :half]
             send_ref, slot = slots[source * len(blocks) + at]
@@ -193,19 +193,23 @@
     return [pl.BlockSpec(memory_space=pltpu.SMEM)] * count
 
 
-def project(flags, hidden, partner, weights, blocks, sends, half, name):
+def project(flags, hidden, partner, weights, blocks, sends, half):
     rows, units = hidden.shape
     counts = [2 * len(blocks)] + sends
     return pl.pallas_call(
         functools.partial(project_kernel, blocks=blocks, sends=sends),
         out_shape=[jax.ShapeDtypeStruct((count, rows, half), jnp.float32) for count in counts],
-        in_specs=in_smem(1) + [pl.BlockSpec(memory_space=pl.ANY)] + in_vmem(1 + len(weights)),
+        in_specs=in_smem(1) + in_vmem(1) + [pl.BlockSpec(memory_space=pl.ANY)] + in_vmem(len(weights)),
         out_specs=in_vmem(len(counts)),
-        scratch_shapes=[pltpu.VMEM((rows, units), hidden.dtype), pltpu.SemaphoreType.DMA(())],
-        compiler_params=pltpu.CompilerParams(vmem_limit_bytes=VMEM_LIMIT),
+        scratch_shapes=[
+            pltpu.VMEM((rows, units), hidden.dtype),
+            pltpu.VMEM((len(blocks), 2 * half, units), hidden.dtype),
+            pltpu.SemaphoreType.DMA((ROW_COPIES,)),
+        ],
+        compiler_params=pltpu.CompilerParams(vmem_limit_bytes=PROJECT_LIMIT),
         cost_estimate=pl.CostEstimate(flops=1, bytes_accessed=1, transcendentals=0),
-        name=name,
-    )(flags, partner, hidden, *weights)
+        name="project",
+    )(flags, hidden, partner, *weights)
 
 
 def after(array, earlier):
@@ -273,34 +277,35 @@
         for at in range(2):
             below.append(shifted(after(sent[at], below[-1:]), 1))
             above.append(shifted(after(sent[at], above[-1:]), -1))
-        opposite = [shifted(after(below[0], below[1:]), 1), shifted(below[1], 1)]
-        spreads = [sent[1], above[1], opposite[1], below[1]]
+        opposite = [shifted(piece, 1) for piece in below]
+        spreads = [piece[1][-8:] for piece in (sent, above, opposite, below)]
+        *spreads, leaving, _ = lax.optimization_barrier(
+            (*spreads, jnp.pad(leaving, ((0, highs * query_len), (0, 0))), partner_hidden)
+        )
         own_queries, partner_queries = (from_rows(spreads, slot, (query_len, held)) for slot in range(2))
+        leaving = lax.dynamic_update_slice(leaving, partner_queries, (rows, 0))
+        first, second = lengths
         swapped = []
-        for at, piece in enumerate([below[0], above[0], below[1], above[1]] + opposite):
+        for at, piece in enumerate([below[0], above[0], opposite[0], below[1], above[1], opposite[1]]):
             swapped.append(lax.ppermute(after(piece, swapped[max(at - 2, 0) : max(at - 1, 0)]), "groups", SWAP))
-        weights = [down_weight] + above + swapped[1:4:2] + below + swapped[0:4:2] + opposite + swapped[4:]
         flags = jnp.stack([core, (group == core).astype(core.dtype)])
-        blocks_of = [[(0, shard)]] + [list(zip(range(at, at + 4), 2 * lengths)) for at in (1, 5, 0)]
+        weights = [down_weight] + above + below + opposite + swapped
+        starts = list(zip((0, first), lengths))
+        blocks_of = [(0, None)]
+        for came, other in ((1, 8), (3, 7), (5, 9)):
+            blocks_of.append(tuple([(of + at * hop, *starts[at]) for at in range(2)] for of, hop in ((came, 1), (other, 3))))
         spots = lax.rem(high + jnp.array([0, 1, 3, 2], jnp.int32), highs)
         spots = jnp.stack([(spots * 2 + side) * stride + core * span, spots * span])
         own_residual = passages
 
-        kept, *away = project(
-            flags, hidden, partner_hidden, weights[:9], blocks_of[:3], [2, 2, 2], half, "project_near"
-        )
-        flags, kept, *away = lax.optimization_barrier((flags, kept, *away))
-        late_kept, *late_away = project(
-            flags, hidden, partner_hidden, weights[9:], blocks_of[3:], [2], half, "project_far"
-        )
-        others = [lax.ppermute(piece, "mp", SWAP) for piece in away + late_away]
-        summands = [kept, late_kept] + others
-        pieces = [(at // 3, (0, at), (2 + at // 2, at % 2), at % 3) for at in range(6)]
-        pieces += [(source, (1, source), (5, source), 3) for source in range(2)]
+        kept, *away = project(flags, hidden, partner_hidden, weights, blocks_of, [2, 2, 2, 2], half)
+        summands = [kept] + [lax.ppermute(piece, "mp", SWAP) for piece in away]
+        pieces = [(at // 4, (0, at), (1 + at // 2, at % 2), at % 4) for at in range(8)]
         origin = high
     else:
         queries = lax.all_gather(queries, ("high", "low"), axis=0, tiled=True)
         own_queries, partner_queries = (queries[:, slot].reshape(-1, held) for slot in range(2))
+        leaving = jnp.concatenate([leaving, partner_queries], axis=0)
         weight = lax.all_gather(down_weight, ("high", "low"), axis=0, tiled=True)
         weight = jnp.where(core == 0, weight, jnp.roll(weight, held, axis=0))
         spots = jnp.zeros((2, 1), jnp.int32)
@@ -327,7 +332,6 @@
         [lax.dynamic_slice_in_dim(owner_place, at, blocks) for at in (own_at, partner_at)]
     )
 
-    leaving = jnp.concatenate([leaving, partner_queries], axis=0)
     partner = lax.ppermute(leaving, "side", SWAP)
     packed = (members, 2 * held // 128 * query_len + 8, 128)
     operands = summands + [own_residual, partner]

time: 100 us -> 102 us (1.020)
  starting transfers between devices: 26.5 us -> 35 us
  waiting for transfers between devices: 51.1 us -> 47.6 us
  Pallas kernels: 14.2 us -> 12.1 us
  other arithmetic: 2.89 us -> 1.2 us
    ppermute x9, waiting for transfers between devices: 23.3 us -> 17.1 us  [shifted(): lax.ppermute(array, 'high', [(at, (at + shift) % highs) for at in range(h...]
    ppermute x9, starting transfers between devices: 13 us -> 19.1 us  [shifted(): lax.ppermute(array, 'high', [(at, (at + shift) % highs) for at in range(h...]
    ppermute x6, waiting for transfers between devices: 16.4 us -> 20.7 us  [body(): lax.ppermute(after(piece, swapped[max(at - 2, 0):max(at - 1, 0)]), 'group...]
    pallas_call x2 -> x1, Pallas kernels: 10.8 us -> 8.68 us  [project(): pl.pallas_call(functools.partial(project_kernel, blocks=blocks, sends=sen...]
    unnamed x13 -> x31, local copies, waits for them, and re-layouts: 1.35 us -> 3.3 us
    dynamic_slice x2, local copies, waits for them, and re-layouts: 2.68 us -> 0.95 us  [features(): lax.dynamic_slice_in_dim(array, start, span, axis=array.ndim - 1)]
    ppermute x1, starting transfers between devices: 1.73 us -> 0.39 us  [body(): by_side = lax.ppermute(away, 'side', SWAP)]
    ppermute x1, starting transfers between devices: 1.65 us -> 2.94 us  [body(): partner_hidden = lax.ppermute(hidden, 'side', SWAP)]
  transfers between devices with their start and end apart: 24 -> 24, of which waited for: 17 -> 18; matrix products, arithmetic and copies ran while one was open for 6% -> 3% of each run, Pallas kernels for 11% -> 9%
where the time goes in v10:
time: 102 us
  waiting for transfers between devices  47.6 us (47%)
  starting transfers between devices  35 us (34%)
  Pallas kernels  12.1 us (12%)
  local copies, waits for them, and re-layouts  5.64 us (6%)
  other arithmetic  1.2 us (1%)
    ppermute x6, waiting for transfers between devices, body(): lax.ppermute(after(piece, swapped[max(at - 2, 0):max(at - 1, 0)]), 'group...  20.7 us
    ppermute x9, starting transfers between devices, shifted(): lax.ppermute(array, 'high', [(at, (at + shift) % highs) for at in range(h...  19.1 us
    ppermute x9, waiting for transfers between devices, shifted(): lax.ppermute(array, 'high', [(at, (at + shift) % highs) for at in range(h...  17.1 us
    pallas_call x1, Pallas kernels, project(): pl.pallas_call(functools.partial(project_kernel, blocks=blocks, sends=sen...  8.68 us
    ppermute x6, starting transfers between devices, body(): lax.ppermute(after(piece, swapped[max(at - 2, 0):max(at - 1, 0)]), 'group...  7.82 us
    ppermute x1, waiting for transfers between devices, body(): partner_hidden = lax.ppermute(hidden, 'side', SWAP)  5.23 us
    unnamed x31, local copies, waits for them, and re-layouts  3.3 us
    ppermute x4, waiting for transfers between devices, body(): summands = [kept] + [lax.ppermute(piece, 'mp', SWAP) for piece in away]  3.1 us
  transfers between devices with their start and end apart: 24, of which 18 were waited for; matrix products, arithmetic and copies ran while one was open for 3% of the time, Pallas kernels for 9%

profile of v10, /device:TPU:0, one launch (start us, length us, event | category | flops | bytes accessed | tf_op | source)
XLA Modules:
  0.0 101.8 jit_solution(5249619487799153894)
XLA Ops:
  0.0 2.9 %collective-permute-start.5 = (bf16[512,2560]{1,0:T(8,128)(2,1)}, bf16[512,2560]{1,0:T(8,128)(2,1)}, u32[]{:S(2)}, u32[]{:S(2)}) collective-permute-start(bf16[512,2560]{1,0:T(8,128)(2,1)} %bitcast.13), channel_id=1, source_target_pairs={{0,2},{2,0},{1,3},{3,1},{4,6},{6,4},{5,7},{7,5},{8,10},{10,8},{9,1... | collective-permute-start | bytes 7864328 | tf_op jit(solution)/shard_map/ppermute | solution.py:263
  2.9 1.3 %constant_dynamic-slice_fusion.4 = (bf16[64,2560]{1,0:T(8,128)(2,1)S(1)}, bf16[64,2560]{1,0:T(8,128)(2,1)S(1)}) fusion(bf16[256,2560]{1,0:T(8,128)(2,1)} %refs_0_.1, s32[]{:T(128)S(6)} %select_n.73, s32[]{:T(128)S(6)} %select_n.72), kind=kLoop, calls=%fused_computation.41 | loop fusion | bytes 1310728 | tf_op jit(solution)/shard_map/dynamic_slice | solution.py:272
  4.2 1.6 %collective-permute-start.2 = (bf16[64,2560]{1,0:T(8,128)(2,1)S(1)}, bf16[64,2560]{1,0:T(8,128)(2,1)S(1)}, u32[]{:S(2)}, u32[]{:S(2)}) collective-permute-start(bf16[64,2560]{1,0:T(8,128)(2,1)S(1)} %get-tuple-element.43), channel_id=1, source_target_pairs={{0,4},{4,8},{8,12},{12,0},{1,5},{5,9},{9,13},{13,1},{2,6},{6,10},{... | collective-permute-start | bytes 983048 | tf_op jit(solution)/shard_map/ppermute | solution.py:260
  5.8 2.2 %collective-permute-start = (bf16[64,2560]{1,0:T(8,128)(2,1)S(1)}, bf16[64,2560]{1,0:T(8,128)(2,1)S(1)}, u32[]{:S(2)}, u32[]{:S(2)}) collective-permute-start(bf16[64,2560]{1,0:T(8,128)(2,1)S(1)} %get-tuple-element.43), channel_id=1, source_target_pairs={{0,12},{4,0},{8,4},{12,8},{1,13},{5,1},{9,5},{13,9},{2,14},{6,2},{... | collective-permute-start | bytes 983048 | tf_op jit(solution)/shard_map/ppermute | solution.py:260
  8.1 0.8 constant_dynamic-slice_fusion.13
  8.9 0.8 pad_maximum_fusion
  9.7 7.0 %collective-permute-done.2.refs_3_ = bf16[64,2560]{1,0:T(8,128)(2,1)S(1)} collective-permute-done((bf16[64,2560]{1,0:T(8,128)(2,1)S(1)}, bf16[64,2560]{1,0:T(8,128)(2,1)S(1)}, u32[]{:S(2)}, u32[]{:S(2)}) %collective-permute-start.2) | collective-permute-done | bytes 327712 | tf_op jit(solution)/shard_map/ppermute | solution.py:260
  16.7 5.5 %collective-permute-start.6 = (bf16[64,2560]{1,0:T(8,128)(2,1)S(1)}, bf16[64,2560]{1,0:T(8,128)(2,1)}, u32[]{:S(2)}, u32[]{:S(2)}) collective-permute-start(bf16[64,2560]{1,0:T(8,128)(2,1)S(1)} %collective-permute-done.2.refs_3_), channel_id=1, source_target_pairs={{0,4},{4,8},{8,12},{12,0},{1,5},{5,9},{9,13},{13,1},{2,6},{6,10},{... | collective-permute-start | bytes 983048 | tf_op jit(solution)/shard_map/ppermute | solution.py:260
  22.5 1.5 %collective-permute-start.8 = (bf16[64,2560]{1,0:T(8,128)(2,1)S(1)}, bf16[64,2560]{1,0:T(8,128)(2,1)S(1)}, u32[]{:S(2)}, u32[]{:S(2)}) collective-permute-start(bf16[64,2560]{1,0:T(8,128)(2,1)S(1)} %collective-permute-done.refs_1_), channel_id=1, source_target_pairs={{0,16},{16,0},{1,17},{17,1},{2,18},{18,2},{3,19},{19,3},{4,20},{20... | collective-permute-start | bytes 983048 | tf_op jit(solution)/shard_map/ppermute | solution.py:290
  25.4 7.8 %collective-permute-done.8.refs_8_ = bf16[64,2560]{1,0:T(8,128)(2,1)S(1)} collective-permute-done((bf16[64,2560]{1,0:T(8,128)(2,1)S(1)}, bf16[64,2560]{1,0:T(8,128)(2,1)S(1)}, u32[]{:S(2)}, u32[]{:S(2)}) %collective-permute-start.8) | collective-permute-done | bytes 327712 | tf_op jit(solution)/shard_map/ppermute | solution.py:290
  33.9 2.8 %collective-permute-start.1 = (bf16[72,2560]{1,0:T(8,128)(2,1)}, bf16[72,2560]{1,0:T(8,128)(2,1)S(1)}, u32[]{:S(2)}, u32[]{:S(2)}) collective-permute-start(bf16[72,2560]{1,0:T(8,128)(2,1)} %pad_maximum_fusion), channel_id=1, source_target_pairs={{0,12},{4,0},{8,4},{12,8},{1,13},{5,1},{9,5},{13,9},{2,14},{6,2},{... | collective-permute-start | bytes 1105928 | tf_op jit(solution)/shard_map/ppermute | solution.py:260
  36.7 1.5 %collective-permute-start.10 = (bf16[72,2560]{1,0:T(8,128)(2,1)S(1)}, bf16[72,2560]{1,0:T(8,128)(2,1)}, u32[]{:S(2)}, u32[]{:S(2)}) collective-permute-start(bf16[72,2560]{1,0:T(8,128)(2,1)S(1)} %collective-permute-done.3.refs_4_), channel_id=1, source_target_pairs={{0,16},{16,0},{1,17},{17,1},{2,18},{18,2},{3,19},{19,3},{4,20},{20... | collective-permute-start | bytes 1105928 | tf_op jit(solution)/shard_map/ppermute | solution.py:290
  38.3 1.4 %collective-permute-done.6.refs_5_ = bf16[64,2560]{1,0:T(8,128)(2,1)} collective-permute-done((bf16[64,2560]{1,0:T(8,128)(2,1)S(1)}, bf16[64,2560]{1,0:T(8,128)(2,1)}, u32[]{:S(2)}, u32[]{:S(2)}) %collective-permute-start.6) | collective-permute-done | bytes 327712 | tf_op jit(solution)/shard_map/ppermute | solution.py:260
  40.3 2.2 %collective-permute-start.9 = (bf16[64,2560]{1,0:T(8,128)(2,1)}, bf16[64,2560]{1,0:T(8,128)(2,1)S(1)}, u32[]{:S(2)}, u32[]{:S(2)}) collective-permute-start(bf16[64,2560]{1,0:T(8,128)(2,1)} %collective-permute-done.6.refs_5_), channel_id=1, source_target_pairs={{0,16},{16,0},{1,17},{17,1},{2,18},{18,2},{3,19},{19,3},{4,20},{20... | collective-permute-start | bytes 983048 | tf_op jit(solution)/shard_map/ppermute | solution.py:290
  42.9 4.5 %collective-permute-done.1.refs_2_ = bf16[72,2560]{1,0:T(8,128)(2,1)S(1)} collective-permute-done((bf16[72,2560]{1,0:T(8,128)(2,1)}, bf16[72,2560]{1,0:T(8,128)(2,1)S(1)}, u32[]{:S(2)}, u32[]{:S(2)}) %collective-permute-start.1) | collective-permute-done | bytes 368672 | tf_op jit(solution)/shard_map/ppermute | solution.py:260
  47.4 5.4 %collective-permute-done.9.refs_9_ = bf16[64,2560]{1,0:T(8,128)(2,1)S(1)} collective-permute-done((bf16[64,2560]{1,0:T(8,128)(2,1)}, bf16[64,2560]{1,0:T(8,128)(2,1)S(1)}, u32[]{:S(2)}, u32[]{:S(2)}) %collective-permute-start.9) | collective-permute-done | bytes 327712 | tf_op jit(solution)/shard_map/ppermute | solution.py:290
  52.8 1.5 %collective-permute-start.11 = (bf16[72,2560]{1,0:T(8,128)(2,1)S(1)}, bf16[72,2560]{1,0:T(8,128)(2,1)S(1)}, u32[]{:S(2)}, u32[]{:S(2)}) collective-permute-start(bf16[72,2560]{1,0:T(8,128)(2,1)S(1)} %collective-permute-done.1.refs_2_), channel_id=1, source_target_pairs={{0,16},{16,0},{1,17},{17,1},{2,18},{18,2},{3,19},{19,3},{4,20},{20... | collective-permute-start | bytes 1105928 | tf_op jit(solution)/shard_map/ppermute | solution.py:290
  54.9 5.2 %collective-permute-done.5.partner_ref = bf16[512,2560]{1,0:T(8,128)(2,1)} collective-permute-done((bf16[512,2560]{1,0:T(8,128)(2,1)}, bf16[512,2560]{1,0:T(8,128)(2,1)}, u32[]{:S(2)}, u32[]{:S(2)}) %collective-permute-start.5) | collective-permute-done | bytes 2621472 | tf_op jit(solution)/shard_map/ppermute | solution.py:263
  60.2 1.8 %collective-permute-start.17 = (bf16[576,512]{1,0:T(8,128)(2,1)S(1)}, bf16[576,512]{1,0:T(8,128)(2,1)S(1)}, u32[]{:S(2)}, u32[]{:S(2)}) collective-permute-start(bf16[576,512]{1,0:T(8,128)(2,1)S(1)} %constant_dynamic-update-slice_fusion.16), channel_id=1, source_target_pairs={{0,2},{2,0},{1,3},{3,1},{4,6},{6,4},{5,7},{7,5},{8,10},{10,8},{9,1... | collective-permute-start | bytes 1769480 | tf_op jit(solution)/shard_map/ppermute | solution.py:335
  62.1 2.3 %collective-permute-done.11.refs_11_ = bf16[72,2560]{1,0:T(8,128)(2,1)S(1)} collective-permute-done((bf16[72,2560]{1,0:T(8,128)(2,1)S(1)}, bf16[72,2560]{1,0:T(8,128)(2,1)S(1)}, u32[]{:S(2)}, u32[]{:S(2)}) %collective-permute-start.11) | collective-permute-done | bytes 368672 | tf_op jit(solution)/shard_map/ppermute | solution.py:290
  64.4 4.6 %collective-permute-done.12.refs_12_ = bf16[72,2560]{1,0:T(8,128)(2,1)S(1)} collective-permute-done((bf16[72,2560]{1,0:T(8,128)(2,1)S(1)}, bf16[72,2560]{1,0:T(8,128)(2,1)S(1)}, u32[]{:S(2)}, u32[]{:S(2)}) %collective-permute-start.12) | collective-permute-done | bytes 368672 | tf_op jit(solution)/shard_map/ppermute | solution.py:290
  69.0 1.7 %copy-done.2 = bf16[2,256,2560]{2,1,0:T(8,128)(2,1)S(1)} copy-done((bf16[2,256,2560]{2,1,0:T(8,128)(2,1)S(1)}, bf16[2,256,2560]{2,1,0:T(8,128)(2,1)}, u32[]{:S(2)}) %copy-start.2) | copy-done | bytes 2621464
  70.8 8.7 %project.1 = (f32[8,512,128]{2,1,0:T(8,128)S(1)}, f32[2,512,128]{2,1,0:T(8,128)S(1)}, f32[2,512,128]{2,1,0:T(8,128)S(1)}, f32[2,512,128]{2,1,0:T(8,128)S(1)}, f32[2,512,128]{2,1,0:T(8,128)S(1)}) custom-call(s32[2]{0:T(128)S(1)} %pad_add_fusion.3.flag_ref, bf16[512,2560]{1,0:T(8,128)(2,1)S(1)} %bitcast.14, ...), custom_call_target="tpu_custom_call" | custom-call | flops 1 | bytes 1 | tf_op jit(solution)/shard_map/project/pallas_call | solution.py:199
  80.6 0.8 collective-permute-done.13.refs_1_
  83.7 2.0 %attend.1 = f32[4,136,128]{2,1,0:T(8,128)S(1)} custom-call(s32[4]{0:T(128)S(1)} %pad_add_fusion.2.place_ref, s32[2,4]{1,0:T(2,128)S(1)} %pad_add_fusion.spot_ref, bf16[64,512]{1,0:T(8,128)(2,1)S(1)} %get-tuple-element.58.query_ref, f32[8,512,128]{2,1,0:T(8,128)S(1)} %get-tuple-element.31.refs_0_, f32[2,512,128]{2,1,0:T(8,128)S(1)} %collective-permute-done.13.refs_1_, ...), custom_call_target="tpu_custom_call" | custom-call | tf_op jit(solution)/shard_map/attend/pallas_call | solution.py:338
  85.7 4.5 %collective-permute-start.18 = (f32[1,136,128]{2,1,0:T(8,128)S(1)}, f32[1,136,128]{2,1,0:T(8,128)S(1)}, u32[]{:S(2)}, u32[]{:S(2)}) collective-permute-start(f32[1,136,128]{2,1,0:T(8,128)S(1)} %get-tuple-element.47), channel_id=1, source_target_pairs={{0,4},{4,8},{8,12},{12,0},{1,5},{5,9},{9,13},{13,1},{2,6},{6,10},{... | collective-permute-start | bytes 208904 | tf_op jit(solution)/shard_map/ppermute | solution.py:260
  90.3 2.4 %collective-permute-start.20 = (f32[1,136,128]{2,1,0:T(8,128)S(1)}, f32[1,136,128]{2,1,0:T(8,128)S(1)}, u32[]{:S(2)}, u32[]{:S(2)}) collective-permute-start(f32[1,136,128]{2,1,0:T(8,128)S(1)} %get-tuple-element.45), channel_id=1, source_target_pairs={{0,12},{4,0},{8,4},{12,8},{1,13},{5,1},{9,5},{13,9},{2,14},{6,2},{... | collective-permute-start | bytes 208904 | tf_op jit(solution)/shard_map/ppermute | solution.py:260
  92.8 3.7 %collective-permute-done.19.refs_2_ = f32[1,136,128]{2,1,0:T(8,128)S(1)} collective-permute-done((f32[1,136,128]{2,1,0:T(8,128)S(1)}, f32[1,136,128]{2,1,0:T(8,128)S(1)}, u32[]{:S(2)}, u32[]{:S(2)}) %collective-permute-start.19) | collective-permute-done | bytes 69664 | tf_op jit(solution)/shard_map/ppermute | solution.py:260
  97.2 0.9 collective-permute-start.23
  98.1 0.9 collective-permute-start.21
  99.0 0.8 collective-permute-done.21.core_ref
  100.6 1.2 %assemble.1 = bf16[1,16,2048]{2,1,0:T(8,128)(2,1)} custom-call(s32[2]{0:T(128)S(1)} %pad_add_fusion.1.flag_ref, bf16[1,16,512]{2,1,0:T(8,128)(2,1)S(1)} %get-tuple-element.74.mine_ref, bf16[1,16,512]{2,1,0:T(8,128)(2,1)S(1)} %collective-permute-done.21.core_ref, bf16[1,16,512]{2,1,0:T(8,128)(2,1)S(1)} %collective-permute-done.22.side_ref, ...), custom_call_target="tpu_custom_call" | custom-call | tf_op jit(solution)/shard_map/assemble/pallas_call | solution.py:370
  (75 shorter events, 9.1 us)
Async XLA Ops:
  0.0 60.1 %collective-permute-start.5 = (bf16[512,2560]{1,0:T(8,128)(2,1)}, bf16[512,2560]{1,0:T(8,128)(2,1)}, u32[]{:S(2)}, u32[]{:S(2)}) collective-permute-start(bf16[512,2560]{1,0:T(8,128)(2,1)} %bitcast.13), channel_id=1, source_target_pairs={{0,2},{2,0},{1,3},{3,1},{4,6},{6,4},{5,7},{7,5},{8,10},{10,8},{9,1... | collective-permute-start | bytes 7864328 | tf_op jit(solution)/shard_map/ppermute | solution.py:263
  2.9 21.9 %copy-start.10 = (s32[8]{0:T(128)S(1)}, s32[8]{0:T(128)}, u32[]{:S(2)}) copy-start(s32[8]{0:T(128)} %param.11) | copy-start | bytes 100
  2.9 21.9 %copy-start.11 = (s32[16,1]{0,1:T(1,128)S(1)}, s32[16,1]{0,1:T(1,128)}, u32[]{:S(2)}) copy-start(s32[16,1]{0,1:T(1,128)} %param.10) | copy-start | bytes 196
  2.9 39.7 %copy-start = (bf16[2,256,2048]{2,1,0:T(8,128)(2,1)S(1)}, bf16[2,256,2048]{2,1,0:T(8,128)(2,1)}, u32[]{:S(2)}) copy-start(bf16[2,256,2048]{2,1,0:T(8,128)(2,1)} %param.8) | copy-start | bytes 6291460
  4.2 12.5 %collective-permute-start.2 = (bf16[64,2560]{1,0:T(8,128)(2,1)S(1)}, bf16[64,2560]{1,0:T(8,128)(2,1)S(1)}, u32[]{:S(2)}, u32[]{:S(2)}) collective-permute-start(bf16[64,2560]{1,0:T(8,128)(2,1)S(1)} %get-tuple-element.43), channel_id=1, source_target_pairs={{0,4},{4,8},{8,12},{12,0},{1,5},{5,9},{9,13},{13,1},{2,6},{6,10},{... | collective-permute-start | bytes 983048 | tf_op jit(solution)/shard_map/ppermute | solution.py:260
  5.8 16.7 %collective-permute-start = (bf16[64,2560]{1,0:T(8,128)(2,1)S(1)}, bf16[64,2560]{1,0:T(8,128)(2,1)S(1)}, u32[]{:S(2)}, u32[]{:S(2)}) collective-permute-start(bf16[64,2560]{1,0:T(8,128)(2,1)S(1)} %get-tuple-element.43), channel_id=1, source_target_pairs={{0,12},{4,0},{8,4},{12,8},{1,13},{5,1},{9,5},{13,9},{2,14},{6,2},{... | collective-permute-start | bytes 983048 | tf_op jit(solution)/shard_map/ppermute | solution.py:260
  16.7 20.0 %collective-permute-start.3 = (bf16[72,2560]{1,0:T(8,128)(2,1)}, bf16[72,2560]{1,0:T(8,128)(2,1)S(1)}, u32[]{:S(2)}, u32[]{:S(2)}) collective-permute-start(bf16[72,2560]{1,0:T(8,128)(2,1)} %pad_maximum_fusion), channel_id=1, source_target_pairs={{0,4},{4,8},{8,12},{12,0},{1,5},{5,9},{9,13},{13,1},{2,6},{6,10},{... | collective-permute-start | bytes 1105928 | tf_op jit(solution)/shard_map/ppermute | solution.py:260
  16.7 22.9 %collective-permute-start.6 = (bf16[64,2560]{1,0:T(8,128)(2,1)S(1)}, bf16[64,2560]{1,0:T(8,128)(2,1)}, u32[]{:S(2)}, u32[]{:S(2)}) collective-permute-start(bf16[64,2560]{1,0:T(8,128)(2,1)S(1)} %collective-permute-done.2.refs_3_), channel_id=1, source_target_pairs={{0,4},{4,8},{8,12},{12,0},{1,5},{5,9},{9,13},{13,1},{2,6},{6,10},{... | collective-permute-start | bytes 983048 | tf_op jit(solution)/shard_map/ppermute | solution.py:260
  22.5 10.6 %collective-permute-start.8 = (bf16[64,2560]{1,0:T(8,128)(2,1)S(1)}, bf16[64,2560]{1,0:T(8,128)(2,1)S(1)}, u32[]{:S(2)}, u32[]{:S(2)}) collective-permute-start(bf16[64,2560]{1,0:T(8,128)(2,1)S(1)} %collective-permute-done.refs_1_), channel_id=1, source_target_pairs={{0,16},{16,0},{1,17},{17,1},{2,18},{18,2},{3,19},{19,3},{4,20},{20... | collective-permute-start | bytes 983048 | tf_op jit(solution)/shard_map/ppermute | solution.py:290
  24.9 15.4 %collective-permute-start.7 = (bf16[64,2560]{1,0:T(8,128)(2,1)S(1)}, bf16[64,2560]{1,0:T(8,128)(2,1)}, u32[]{:S(2)}, u32[]{:S(2)}) collective-permute-start(bf16[64,2560]{1,0:T(8,128)(2,1)S(1)} %collective-permute-done.2.refs_3_), channel_id=1, source_target_pairs={{0,16},{16,0},{1,17},{17,1},{2,18},{18,2},{3,19},{19,3},{4,20},{20... | collective-permute-start | bytes 983048 | tf_op jit(solution)/shard_map/ppermute | solution.py:290
  33.9 13.5 %collective-permute-start.1 = (bf16[72,2560]{1,0:T(8,128)(2,1)}, bf16[72,2560]{1,0:T(8,128)(2,1)S(1)}, u32[]{:S(2)}, u32[]{:S(2)}) collective-permute-start(bf16[72,2560]{1,0:T(8,128)(2,1)} %pad_maximum_fusion), channel_id=1, source_target_pairs={{0,12},{4,0},{8,4},{12,8},{1,13},{5,1},{9,5},{13,9},{2,14},{6,2},{... | collective-permute-start | bytes 1105928 | tf_op jit(solution)/shard_map/ppermute | solution.py:260
  36.7 17.6 %collective-permute-start.10 = (bf16[72,2560]{1,0:T(8,128)(2,1)S(1)}, bf16[72,2560]{1,0:T(8,128)(2,1)}, u32[]{:S(2)}, u32[]{:S(2)}) collective-permute-start(bf16[72,2560]{1,0:T(8,128)(2,1)S(1)} %collective-permute-done.3.refs_4_), channel_id=1, source_target_pairs={{0,16},{16,0},{1,17},{17,1},{2,18},{18,2},{3,19},{19,3},{4,20},{20... | collective-permute-start | bytes 1105928 | tf_op jit(solution)/shard_map/ppermute | solution.py:290
  39.6 14.7 %collective-permute-start.4 = (bf16[72,2560]{1,0:T(8,128)(2,1)S(1)}, bf16[72,2560]{1,0:T(8,128)(2,1)S(1)}, u32[]{:S(2)}, u32[]{:S(2)}) collective-permute-start(bf16[72,2560]{1,0:T(8,128)(2,1)S(1)} %collective-permute-done.3.refs_4_), channel_id=1, source_target_pairs={{0,4},{4,8},{8,12},{12,0},{1,5},{5,9},{9,13},{13,1},{2,6},{6,10},{... | collective-permute-start | bytes 1105928 | tf_op jit(solution)/shard_map/ppermute | solution.py:260
  40.3 12.5 %collective-permute-start.9 = (bf16[64,2560]{1,0:T(8,128)(2,1)}, bf16[64,2560]{1,0:T(8,128)(2,1)S(1)}, u32[]{:S(2)}, u32[]{:S(2)}) collective-permute-start(bf16[64,2560]{1,0:T(8,128)(2,1)} %collective-permute-done.6.refs_5_), channel_id=1, source_target_pairs={{0,16},{16,0},{1,17},{17,1},{2,18},{18,2},{3,19},{19,3},{4,20},{20... | collective-permute-start | bytes 983048 | tf_op jit(solution)/shard_map/ppermute | solution.py:290
  42.6 17.5 %copy-start.8 = (bf16[8,2560]{1,0:T(8,128)(2,1)S(1)}, bf16[8,2560]{1,0:T(8,128)(2,1)}, u32[]{:S(2)}) copy-start(bf16[8,2560]{1,0:T(8,128)(2,1)} %copy-done.7) | copy-start | bytes 122884
  42.6 26.4 %copy-start.1 = (bf16[256,2560]{1,0:T(8,128)(2,1)S(1)}, bf16[256,2560]{1,0:T(8,128)(2,1)}, u32[]{:S(2)}) copy-start(bf16[256,2560]{1,0:T(8,128)(2,1)} %refs_0_.1) | copy-start | bytes 3932164
  42.6 26.4 %copy-start.4 = (bf16[64,2560]{1,0:T(8,128)(2,1)S(1)}, bf16[64,2560]{1,0:T(8,128)(2,1)}, u32[]{:S(2)}) copy-start(bf16[64,2560]{1,0:T(8,128)(2,1)} %copy-done.3) | copy-start | bytes 983044
  42.7 26.4 %copy-start.6 = (bf16[64,2560]{1,0:T(8,128)(2,1)S(1)}, bf16[64,2560]{1,0:T(8,128)(2,1)}, u32[]{:S(2)}) copy-start(bf16[64,2560]{1,0:T(8,128)(2,1)} %copy-done.5) | copy-start | bytes 983044
  52.8 11.5 %collective-permute-start.11 = (bf16[72,2560]{1,0:T(8,128)(2,1)S(1)}, bf16[72,2560]{1,0:T(8,128)(2,1)S(1)}, u32[]{:S(2)}, u32[]{:S(2)}) collective-permute-start(bf16[72,2560]{1,0:T(8,128)(2,1)S(1)} %collective-permute-done.1.refs_2_), channel_id=1, source_target_pairs={{0,16},{16,0},{1,17},{17,1},{2,18},{18,2},{3,19},{19,3},{4,20},{20... | collective-permute-start | bytes 1105928 | tf_op jit(solution)/shard_map/ppermute | solution.py:290
  54.4 14.6 %collective-permute-start.12 = (bf16[72,2560]{1,0:T(8,128)(2,1)S(1)}, bf16[72,2560]{1,0:T(8,128)(2,1)S(1)}, u32[]{:S(2)}, u32[]{:S(2)}) collective-permute-start(bf16[72,2560]{1,0:T(8,128)(2,1)S(1)} %collective-permute-done.4.refs_6_), channel_id=1, source_target_pairs={{0,16},{16,0},{1,17},{17,1},{2,18},{18,2},{3,19},{19,3},{4,20},{20... | collective-permute-start | bytes 1105928 | tf_op jit(solution)/shard_map/ppermute | solution.py:290
  60.2 23.5 %collective-permute-start.17 = (bf16[576,512]{1,0:T(8,128)(2,1)S(1)}, bf16[576,512]{1,0:T(8,128)(2,1)S(1)}, u32[]{:S(2)}, u32[]{:S(2)}) collective-permute-start(bf16[576,512]{1,0:T(8,128)(2,1)S(1)} %constant_dynamic-update-slice_fusion.16), channel_id=1, source_target_pairs={{0,2},{2,0},{1,3},{3,1},{4,6},{6,4},{5,7},{7,5},{8,10},{10,8},{9,1... | collective-permute-start | bytes 1769480 | tf_op jit(solution)/shard_map/ppermute | solution.py:335
  62.0 18.5 %copy-start.9 = (s32[4]{0:T(128)S(1)}, s32[4]{0:T(128)}, u32[]{:S(2)}) copy-start(s32[4]{0:T(128)} %constant.99.clone) | copy-start | bytes 52
  79.4 2.0 %collective-permute-start.13 = (f32[2,512,128]{2,1,0:T(8,128)S(1)}, f32[2,512,128]{2,1,0:T(8,128)S(1)}, u32[]{:S(2)}, u32[]{:S(2)}) collective-permute-start(f32[2,512,128]{2,1,0:T(8,128)S(1)} %get-tuple-element.32), channel_id=1, source_target_pairs={{0,1},{1,0},{2,3},{3,2},{4,5},{5,4},{6,7},{7,6},{8,9},{9,8},{10,11... | collective-permute-start | bytes 1572872 | tf_op jit(solution)/shard_map/ppermute | solution.py:302
  79.5 2.6 %collective-permute-start.14 = (f32[2,512,128]{2,1,0:T(8,128)S(1)}, f32[2,512,128]{2,1,0:T(8,128)S(1)}, u32[]{:S(2)}, u32[]{:S(2)}) collective-permute-start(f32[2,512,128]{2,1,0:T(8,128)S(1)} %get-tuple-element.33), channel_id=1, source_target_pairs={{0,1},{1,0},{2,3},{3,2},{4,5},{5,4},{6,7},{7,6},{8,9},{9,8},{10,11... | collective-permute-start | bytes 1572872 | tf_op jit(solution)/shard_map/ppermute | solution.py:302
  80.0 2.9 %collective-permute-start.15 = (f32[2,512,128]{2,1,0:T(8,128)S(1)}, f32[2,512,128]{2,1,0:T(8,128)S(1)}, u32[]{:S(2)}, u32[]{:S(2)}) collective-permute-start(f32[2,512,128]{2,1,0:T(8,128)S(1)} %get-tuple-element.34), channel_id=1, source_target_pairs={{0,1},{1,0},{2,3},{3,2},{4,5},{5,4},{6,7},{7,6},{8,9},{9,8},{10,11... | collective-permute-start | bytes 1572872 | tf_op jit(solution)/shard_map/ppermute | solution.py:302
  80.1 3.6 %collective-permute-start.16 = (f32[2,512,128]{2,1,0:T(8,128)S(1)}, f32[2,512,128]{2,1,0:T(8,128)S(1)}, u32[]{:S(2)}, u32[]{:S(2)}) collective-permute-start(f32[2,512,128]{2,1,0:T(8,128)S(1)} %get-tuple-element.35), channel_id=1, source_target_pairs={{0,1},{1,0},{2,3},{3,2},{4,5},{5,4},{6,7},{7,6},{8,9},{9,8},{10,11... | collective-permute-start | bytes 1572872 | tf_op jit(solution)/shard_map/ppermute | solution.py:302
  85.7 7.1 %collective-permute-start.18 = (f32[1,136,128]{2,1,0:T(8,128)S(1)}, f32[1,136,128]{2,1,0:T(8,128)S(1)}, u32[]{:S(2)}, u32[]{:S(2)}) collective-permute-start(f32[1,136,128]{2,1,0:T(8,128)S(1)} %get-tuple-element.47), channel_id=1, source_target_pairs={{0,4},{4,8},{8,12},{12,0},{1,5},{5,9},{9,13},{13,1},{2,6},{6,10},{... | collective-permute-start | bytes 208904 | tf_op jit(solution)/shard_map/ppermute | solution.py:260
  90.3 6.2 %collective-permute-start.19 = (f32[1,136,128]{2,1,0:T(8,128)S(1)}, f32[1,136,128]{2,1,0:T(8,128)S(1)}, u32[]{:S(2)}, u32[]{:S(2)}) collective-permute-start(f32[1,136,128]{2,1,0:T(8,128)S(1)} %get-tuple-element.46), channel_id=1, source_target_pairs={{0,8},{4,12},{8,0},{12,4},{1,9},{5,13},{9,1},{13,5},{2,10},{6,14},... | collective-permute-start | bytes 208904 | tf_op jit(solution)/shard_map/ppermute | solution.py:260
  90.3 6.2 %collective-permute-start.20 = (f32[1,136,128]{2,1,0:T(8,128)S(1)}, f32[1,136,128]{2,1,0:T(8,128)S(1)}, u32[]{:S(2)}, u32[]{:S(2)}) collective-permute-start(f32[1,136,128]{2,1,0:T(8,128)S(1)} %get-tuple-element.45), channel_id=1, source_target_pairs={{0,12},{4,0},{8,4},{12,8},{1,13},{5,1},{9,5},{13,9},{2,14},{6,2},{... | collective-permute-start | bytes 208904 | tf_op jit(solution)/shard_map/ppermute | solution.py:260
  96.8 3.8 %collective-permute-start.22 = (bf16[1,16,512]{2,1,0:T(8,128)(2,1)S(1)}, bf16[1,16,512]{2,1,0:T(8,128)(2,1)S(1)}, u32[]{:S(2)}, u32[]{:S(2)}) collective-permute-start(bf16[1,16,512]{2,1,0:T(8,128)(2,1)S(1)} %get-tuple-element.73), channel_id=1, source_target_pairs={{0,2},{2,0},{1,3},{3,1},{4,6},{6,4},{5,7},{7,5},{8,10},{10,8},{9,1... | collective-permute-start | bytes 49160 | tf_op jit(solution)/shard_map/ppermute | solution.py:362
  97.2 3.4 %collective-permute-start.23 = (bf16[1,16,512]{2,1,0:T(8,128)(2,1)S(1)}, bf16[1,16,512]{2,1,0:T(8,128)(2,1)S(1)}, u32[]{:S(2)}, u32[]{:S(2)}) collective-permute-start(bf16[1,16,512]{2,1,0:T(8,128)(2,1)S(1)} %get-tuple-element.73), channel_id=1, source_target_pairs={{0,3},{3,0},{1,2},{2,1},{4,7},{7,4},{5,6},{6,5},{8,11},{11,8},{9,1... | collective-permute-start | bytes 49160 | tf_op jit(solution)/shard_map/ppermute | solution.py:363
  98.1 1.7 %collective-permute-start.21 = (bf16[1,16,512]{2,1,0:T(8,128)(2,1)S(1)}, bf16[1,16,512]{2,1,0:T(8,128)(2,1)S(1)}, u32[]{:S(2)}, u32[]{:S(2)}) collective-permute-start(bf16[1,16,512]{2,1,0:T(8,128)(2,1)S(1)} %get-tuple-element.74.mine_ref), channel_id=1, source_target_pairs={{0,1},{1,0},{2,3},{3,2},{4,5},{5,4},{6,7},{7,6},{8,9},{9,8},{10,11... | collective-permute-start | bytes 49160 | tf_op jit(solution)/shard_map/ppermute | solution.py:361
  (4 other events, 4.0 us)

commit v11 on v10

--- a/solution.py
+++ b/solution.py
@@ -10,9 +10,9 @@
 
 HEAD_DIM = 64
 EMPTY = -3e38
-FIRST_EIGHTHS = 4
+FIRST_EIGHTHS = 3
 ROW_COPIES = 4
-PROJECT_LIMIT = 30 * 1024 * 1024
+PROJECT_LIMIT = 24 * 1024 * 1024
 VMEM_LIMIT = 22 * 1024 * 1024
 SWAP = [(0, 1), (1, 0)]
 CROSS = [(0, 3), (3, 0), (1, 2), (2, 1)]
@@ -27,36 +27,51 @@
     return picked
 
 
-def project_kernel(flag_ref, hidden_ref, partner_ref, *refs, blocks, sends):
-    *refs, rows_ref, block_ref, semaphores = refs
-    keep_ref, *send_refs = refs[-1 - len(sends) :]
-    slots = [(ref, at) for ref in send_refs for at in range(ref.shape[0])]
-    core, same = flag_ref[0], flag_ref[1]
-    half = keep_ref.shape[2]
+def join(block_ref, at, block, refs, core, same):
+    came, swapped = block
+    half = block_ref.shape[1] // 2
+    if not swapped:
+        block_ref[at, :half] = refs[came][pl.ds(pl.multiple_of(core * half, half), half), :]
+        block_ref[at, half:] = refs[came][pl.ds(pl.multiple_of((1 - core) * half, half), half), :]
+        return
+    for pieces, where in ((came, (1 - same) * half), (swapped, same * half)):
+        for operand, first, length in pieces:
+            block_ref[at, pl.ds(pl.multiple_of(where + first, 16), length)] = refs[operand][:length]
+
+
+def multiply(rows, block, keep_ref, send_ref, at, where):
+    slot = at % send_ref.shape[0]
+    product = lax.dot_general(rows, block, (((1,), (1,)), ((), ())), preferred_element_type=jnp.float32)
+    half = product.shape[1] // 2
+    keep_ref[at, where, :] = product[:, :half]
+    send_ref[slot, where, :] = product[:, half:]
+
+
+def join_kernel(flag_ref, *refs, sources, blocks):
+    *refs, keep_ref, send_ref, block_ref = refs
+    for at, block in enumerate(blocks):
+        join(block_ref, at, block, refs[sources:], flag_ref[0], flag_ref[1])
+    for source in range(sources):
+        for at in range(len(blocks)):
+            multiply(
+                refs[source][...], block_ref[at], keep_ref, send_ref, source * len(blocks) + at, slice(None)
+            )
+
+
+def partner_kernel(partner_ref, block_ref, keep_ref, send_ref, rows_ref, last_ref, semaphores):
     step = rows_ref.shape[0] // ROW_COPIES
     copies = []
     for part in range(ROW_COPIES):
         rows = pl.ds(part * step, step)
         copies.append(pltpu.make_async_copy(partner_ref.at[rows], rows_ref.at[rows], semaphores.at[part]))
         copies[-1].start()
-    for at, (came, swapped) in enumerate(blocks):
-        if not swapped:
-            block_ref[at, :half] = refs[came][pl.ds(pl.multiple_of(core * half, half), half), :]
-            block_ref[at, half:] = refs[came][pl.ds(pl.multiple_of((1 - core) * half, half), half), :]
-        for pieces, where in ((came, (1 - same) * half), (swapped, same * half)) if swapped else ():
-            for operand, first, length in pieces:
-                place = pl.multiple_of(where + first, 16)
-                block_ref[at, pl.ds(place, length)] = refs[operand][:length]
-    for source, source_ref in enumerate((hidden_ref, rows_ref)):
-        for copy in copies if source else []:
+    for part in range(2):
+        where = slice(part * rows_ref.shape[0] // 2, (part + 1) * rows_ref.shape[0] // 2)
+        for copy in copies[part * ROW_COPIES // 2 : (part + 1) * ROW_COPIES // 2]:
             copy.wait()
-        for at in range(len(blocks)):
-            product = lax.dot_general(
-                source_ref[...], block_ref[at], (((1,), (1,)), ((), ())), preferred_element_type=jnp.float32
-            )
-            keep_ref[source * len(blocks) + at] = product[:, :half]
-            send_ref, slot = slots[source * len(blocks) + at]
-            send_ref[slot] = product[:, half:]
+        for at in range(block_ref.shape[0]):
+            last = at == block_ref.shape[0] - 1
+            multiply(rows_ref[where, :], block_ref[at], keep_ref, last_ref if last else send_ref, at, where)
 
 
 def attend_kernel(place_ref, spot_ref, query_ref, *refs, pieces):
@@ -193,23 +208,17 @@
     return [pl.BlockSpec(memory_space=pltpu.SMEM)] * count
 
 
-def project(flags, hidden, partner, weights, blocks, sends, half):
-    rows, units = hidden.shape
-    counts = [2 * len(blocks)] + sends
+def project(kernel, name, operands, placed, counts, rows, half, handed, scratch):
     return pl.pallas_call(
-        functools.partial(project_kernel, blocks=blocks, sends=sends),
-        out_shape=[jax.ShapeDtypeStruct((count, rows, half), jnp.float32) for count in counts],
-        in_specs=in_smem(1) + in_vmem(1) + [pl.BlockSpec(memory_space=pl.ANY)] + in_vmem(len(weights)),
-        out_specs=in_vmem(len(counts)),
-        scratch_shapes=[
-            pltpu.VMEM((rows, units), hidden.dtype),
-            pltpu.VMEM((len(blocks), 2 * half, units), hidden.dtype),
-            pltpu.SemaphoreType.DMA((ROW_COPIES,)),
-        ],
+        kernel,
+        out_shape=[jax.ShapeDtypeStruct((count, rows, half), jnp.float32) for count in counts] + handed,
+        in_specs=placed,
+        out_specs=in_vmem(2 + len(handed)),
+        scratch_shapes=scratch,
         compiler_params=pltpu.CompilerParams(vmem_limit_bytes=PROJECT_LIMIT),
         cost_estimate=pl.CostEstimate(flops=1, bytes_accessed=1, transcendentals=0),
-        name="project",
-    )(flags, hidden, partner, *weights)
+        name=name,
+    )(*operands)
 
 
 def after(array, earlier):
@@ -289,18 +298,38 @@
         for at, piece in enumerate([below[0], above[0], opposite[0], below[1], above[1], opposite[1]]):
             swapped.append(lax.ppermute(after(piece, swapped[max(at - 2, 0) : max(at - 1, 0)]), "groups", SWAP))
         flags = jnp.stack([core, (group == core).astype(core.dtype)])
-        weights = [down_weight] + above + below + opposite + swapped
+        near_pieces = [down_weight] + above + below + swapped[:2] + swapped[3:5]
+        far_pieces = opposite + swapped[2::3]
         starts = list(zip((0, first), lengths))
-        blocks_of = [(0, None)]
-        for came, other in ((1, 8), (3, 7), (5, 9)):
-            blocks_of.append(tuple([(of + at * hop, *starts[at]) for at in range(2)] for of, hop in ((came, 1), (other, 3))))
+        near = [(0, None)]
+        for came, other in ((1, 6), (3, 5)):
+            near.append(tuple([(of + at * hop, *starts[at]) for at in range(2)] for of, hop in ((came, 1), (other, 2))))
+        far = [tuple([(of + at, *starts[at]) for at in range(2)] for of in (0, 2))]
         spots = lax.rem(high + jnp.array([0, 1, 3, 2], jnp.int32), highs)
         spots = jnp.stack([(spots * 2 + side) * stride + core * span, spots * span])
         own_residual = passages
 
-        kept, *away = project(flags, hidden, partner_hidden, weights, blocks_of, [2, 2, 2, 2], half)
-        summands = [kept] + [lax.ppermute(piece, "mp", SWAP) for piece in away]
-        pieces = [(at // 4, (0, at), (1 + at // 2, at % 2), at % 4) for at in range(8)]
+        joined = jax.ShapeDtypeStruct((len(near), shard, units), down_weight.dtype)
+        kept, away, joined = project(
+            functools.partial(join_kernel, sources=1, blocks=near), "project_own", [flags, hidden] + near_pieces,
+            in_smem(1) + in_vmem(1 + len(near_pieces)), [len(near)] * 2, rows, half, [joined], [],
+        )
+        partner_kept, partner_away, partner_rows, partner_last = project(
+            partner_kernel, "project_partner", [partner_hidden, joined],
+            [pl.BlockSpec(memory_space=pl.ANY)] + in_vmem(1), [len(near), len(near) - 1], rows, half,
+            [jax.ShapeDtypeStruct(hidden.shape, hidden.dtype), jax.ShapeDtypeStruct((1, rows, half), jnp.float32)],
+            [pltpu.SemaphoreType.DMA((ROW_COPIES,))],
+        )
+        far_kept, far_away = project(
+            functools.partial(join_kernel, sources=2, blocks=far), "project_far",
+            [flags, hidden, partner_rows] + far_pieces, in_smem(1) + in_vmem(2 + len(far_pieces)), [2, 2], rows, half,
+            [], [pltpu.VMEM((1, shard, units), down_weight.dtype)],
+        )
+        summands = [kept, partner_kept, far_kept]
+        summands += [lax.ppermute(piece, "mp", SWAP) for piece in (away, partner_away, partner_last, far_away)]
+        pieces = [(0, (0, at), (3, at), at) for at in range(3)]
+        pieces += [(1, (1, at), (4 + at // 2, at % 2), at) for at in range(3)]
+        pieces += [(source, (2, source), (6, source), 3) for source in range(2)]
         origin = high
     else:
         queries = lax.all_gather(queries, ("high", "low"), axis=0, tiled=True)

time: 102 us -> 108 us (1.059)
  starting transfers between devices: 35 us -> 23.5 us
  local copies, waits for them, and re-layouts: 5.64 us -> 13.7 us
  Pallas kernels: 12.1 us -> 16.3 us
  waiting for transfers between devices: 47.6 us -> 51.4 us
    ppermute x9, waiting for transfers between devices: 17.1 us -> 37.8 us  [shifted(): lax.ppermute(array, 'high', [(at, (at + shift) % highs) for at in range(h...]
    ppermute x6, waiting for transfers between devices: 20.7 us -> 7.13 us  [body(): lax.ppermute(after(piece, swapped[max(at - 2, 0):max(at - 1, 0)]), 'group...]
    ppermute x9, starting transfers between devices: 19.1 us -> 13 us  [shifted(): lax.ppermute(array, 'high', [(at, (at + shift) % highs) for at in range(h...]
    ppermute x1, waiting for transfers between devices: 5.23 us -> 0.01 us  [body(): partner_hidden = lax.ppermute(hidden, 'side', SWAP)]
    unnamed x31 -> x39, local copies, waits for them, and re-layouts: 3.3 us -> 8.12 us
    ppermute x6, starting transfers between devices: 7.82 us -> 4.05 us  [body(): lax.ppermute(after(piece, swapped[max(at - 2, 0):max(at - 1, 0)]), 'group...]
    pallas_call x1 -> x3, Pallas kernels: 8.68 us -> 12.1 us  [project(): pl.pallas_call(kernel, out_shape=[jax.ShapeDtypeStruct((count, rows, half...]
    ppermute x1, waiting for transfers between devices: 0.01 us -> 2.68 us  [body(): partner = lax.ppermute(leaving, 'side', SWAP)]
  transfers between devices with their start and end apart: 24 -> 24, of which waited for: 18 -> 13; matrix products, arithmetic and copies ran while one was open for 3% -> 7% of each run, Pallas kernels for 9% -> 11%
where the time goes in v11:
time: 108 us; the launch traced here: 107 us
  waiting for transfers between devices  51.4 us (48%)
  starting transfers between devices  23.5 us (22%)
  Pallas kernels  16.3 us (15%)
  local copies, waits for them, and re-layouts  13.7 us (13%)
  other arithmetic  2.08 us (2%)
    ppermute x9, waiting for transfers between devices, shifted(): lax.ppermute(array, 'high', [(at, (at + shift) % highs) for at in range(h...  37.8 us
    ppermute x9, starting transfers between devices, shifted(): lax.ppermute(array, 'high', [(at, (at + shift) % highs) for at in range(h...  13 us
    pallas_call x3, Pallas kernels, project(): pl.pallas_call(kernel, out_shape=[jax.ShapeDtypeStruct((count, rows, half...  12.1 us
    unnamed x39, local copies, waits for them, and re-layouts  8.12 us
    ppermute x6, waiting for transfers between devices, body(): lax.ppermute(after(piece, swapped[max(at - 2, 0):max(at - 1, 0)]), 'group...  7.13 us
    ppermute x6, starting transfers between devices, body(): lax.ppermute(after(piece, swapped[max(at - 2, 0):max(at - 1, 0)]), 'group...  4.05 us
    ppermute x1, starting transfers between devices, body(): partner_hidden = lax.ppermute(hidden, 'side', SWAP)  2.94 us
    pallas_call x1, Pallas kernels, body(): pl.pallas_call(functools.partial(attend_kernel, pieces=pieces), out_shape...  2.71 us
  transfers between devices with their start and end apart: 24, of which 13 were waited for; matrix products, arithmetic and copies ran while one was open for 7% of the time, Pallas kernels for 11%

profile of v11, /device:TPU:0, one launch (start us, length us, event | category | flops | bytes accessed | tf_op | source)
XLA Modules:
  0.0 107.2 jit_solution(849715699528530342)
XLA Ops:
  0.0 2.9 %collective-permute-start.5 = (bf16[512,2560]{1,0:T(8,128)(2,1)}, bf16[512,2560]{1,0:T(8,128)(2,1)}, u32[]{:S(2)}, u32[]{:S(2)}) collective-permute-start(bf16[512,2560]{1,0:T(8,128)(2,1)} %bitcast.11), channel_id=1, source_target_pairs={{0,2},{2,0},{1,3},{3,1},{4,6},{6,4},{5,7},{7,5},{8,10},{10,8},{9,1... | collective-permute-start | bytes 7864328 | tf_op jit(solution)/shard_map/ppermute | solution.py:272
  2.9 1.0 constant_dynamic-slice_fusion.4
  3.9 3.7 %collective-permute-start = (bf16[48,2560]{1,0:T(8,128)(2,1)S(1)}, bf16[48,2560]{1,0:T(8,128)(2,1)}, u32[]{:S(2)}, u32[]{:S(2)}) collective-permute-start(bf16[48,2560]{1,0:T(8,128)(2,1)S(1)} %constant_dynamic-slice_fusion.4), channel_id=1, source_target_pairs={{0,12},{4,0},{8,4},{12,8},{1,13},{5,1},{9,5},{13,9},{2,14},{6,2},{... | collective-permute-start | bytes 737288 | tf_op jit(solution)/shard_map/ppermute | solution.py:269
  8.4 1.0 constant_dynamic-slice_fusion.5
  9.5 9.3 %collective-permute-done.2.refs_4_ = bf16[48,2560]{1,0:T(8,128)(2,1)} collective-permute-done((bf16[48,2560]{1,0:T(8,128)(2,1)S(1)}, bf16[48,2560]{1,0:T(8,128)(2,1)}, u32[]{:S(2)}, u32[]{:S(2)}) %collective-permute-start.2) | collective-permute-done | bytes 245792 | tf_op jit(solution)/shard_map/ppermute | solution.py:269
  18.8 1.5 %collective-permute-start.6 = (bf16[48,2560]{1,0:T(8,128)(2,1)}, bf16[48,2560]{1,0:T(8,128)(2,1)S(1)}, u32[]{:S(2)}, u32[]{:S(2)}) collective-permute-start(bf16[48,2560]{1,0:T(8,128)(2,1)} %collective-permute-done.2.refs_4_), channel_id=1, source_target_pairs={{0,16},{16,0},{1,17},{17,1},{2,18},{18,2},{3,19},{19,3},{4,20},{20... | collective-permute-start | bytes 737288 | tf_op jit(solution)/shard_map/ppermute | solution.py:299
  20.3 1.6 %collective-permute-start.9 = (bf16[48,2560]{1,0:T(8,128)(2,1)}, bf16[48,2560]{1,0:T(8,128)(2,1)}, u32[]{:S(2)}, u32[]{:S(2)}) collective-permute-start(bf16[48,2560]{1,0:T(8,128)(2,1)} %collective-permute-done.2.refs_4_), channel_id=1, source_target_pairs={{0,4},{4,8},{8,12},{12,0},{1,5},{5,9},{9,13},{13,1},{2,6},{6,10},{... | collective-permute-start | bytes 737288 | tf_op jit(solution)/shard_map/ppermute | solution.py:269
  22.7 3.8 %collective-permute-start.1 = (bf16[88,2560]{1,0:T(8,128)(2,1)}, bf16[88,2560]{1,0:T(8,128)(2,1)S(1)}, u32[]{:S(2)}, u32[]{:S(2)}) collective-permute-start(bf16[88,2560]{1,0:T(8,128)(2,1)} %pad_maximum_fusion), channel_id=1, source_target_pairs={{0,12},{4,0},{8,4},{12,8},{1,13},{5,1},{9,5},{13,9},{2,14},{6,2},{... | collective-permute-start | bytes 1351688 | tf_op jit(solution)/shard_map/ppermute | solution.py:269
  27.8 3.7 %collective-permute-done.9.refs_2_ = bf16[48,2560]{1,0:T(8,128)(2,1)} collective-permute-done((bf16[48,2560]{1,0:T(8,128)(2,1)}, bf16[48,2560]{1,0:T(8,128)(2,1)}, u32[]{:S(2)}, u32[]{:S(2)}) %collective-permute-start.9) | collective-permute-done | bytes 245792 | tf_op jit(solution)/shard_map/ppermute | solution.py:269
  32.1 1.2 %constant_dynamic-slice_fusion.3 = (bf16[512,128]{1,0:T(8,128)(2,1)S(1)}, bf16[512,128]{1,0:T(8,128)(2,1)S(1)}, bf16[512,128]{1,0:T(8,128)(2,1)S(1)}, bf16[512,128]{1,0:T(8,128)(2,1)S(1)}) fusion(bf16[512,2048]{1,0:T(8,128)(2,1)} %bitcast.14, s32[]{:T(128)S(6)} %select_n.68, s32[]{:T(128)S(6)} %select_n.71, s32[]{:T(128)S(6)} %select_n.70, s32[]{:T(128)S(6)} %select_n.69), kind=kLoop, calls=%fused_computation.40 | loop fusion | bytes 1048592 | tf_op jit(solution)/shard_map/dynamic_slice | solution.py:265
  33.3 2.4 %collective-permute-done.7.refs_7_ = bf16[48,2560]{1,0:T(8,128)(2,1)} collective-permute-done((bf16[48,2560]{1,0:T(8,128)(2,1)}, bf16[48,2560]{1,0:T(8,128)(2,1)}, u32[]{:S(2)}, u32[]{:S(2)}) %collective-permute-start.7) | collective-permute-done | bytes 245792 | tf_op jit(solution)/shard_map/ppermute | solution.py:299
  35.7 5.3 %collective-permute-done.3.refs_5_ = bf16[88,2560]{1,0:T(8,128)(2,1)S(1)} collective-permute-done((bf16[88,2560]{1,0:T(8,128)(2,1)}, bf16[88,2560]{1,0:T(8,128)(2,1)S(1)}, u32[]{:S(2)}, u32[]{:S(2)}) %collective-permute-start.3) | collective-permute-done | bytes 450592 | tf_op jit(solution)/shard_map/ppermute | solution.py:269
  41.4 9.1 %collective-permute-done.1.refs_3_ = bf16[88,2560]{1,0:T(8,128)(2,1)S(1)} collective-permute-done((bf16[88,2560]{1,0:T(8,128)(2,1)}, bf16[88,2560]{1,0:T(8,128)(2,1)S(1)}, u32[]{:S(2)}, u32[]{:S(2)}) %collective-permute-start.1) | collective-permute-done | bytes 450592 | tf_op jit(solution)/shard_map/ppermute | solution.py:269
  51.1 0.9 fusion.6
  52.1 5.6 %collective-permute-done.4.refs_3_ = bf16[88,2560]{1,0:T(8,128)(2,1)} collective-permute-done((bf16[88,2560]{1,0:T(8,128)(2,1)S(1)}, bf16[88,2560]{1,0:T(8,128)(2,1)}, u32[]{:S(2)}, u32[]{:S(2)}) %collective-permute-start.4) | collective-permute-done | bytes 450592 | tf_op jit(solution)/shard_map/ppermute | solution.py:269
  59.0 4.7 %collective-permute-done.11.refs_9_ = bf16[88,2560]{1,0:T(8,128)(2,1)S(1)} collective-permute-done((bf16[88,2560]{1,0:T(8,128)(2,1)S(1)}, bf16[88,2560]{1,0:T(8,128)(2,1)S(1)}, u32[]{:S(2)}, u32[]{:S(2)}) %collective-permute-start.11) | collective-permute-done | bytes 450592 | tf_op jit(solution)/shard_map/ppermute | solution.py:299
  63.7 1.3 %copy-done.4 = bf16[256,2560]{1,0:T(8,128)(2,1)S(1)} copy-done((bf16[256,2560]{1,0:T(8,128)(2,1)S(1)}, bf16[256,2560]{1,0:T(8,128)(2,1)}, u32[]{:S(2)}) %copy-start.4) | copy-done | bytes 1310744
  65.0 1.0 copy-done.6
  66.1 1.0 copy-done.8
  67.1 4.6 %project_own.1 = (f32[3,512,128]{2,1,0:T(8,128)S(1)}, f32[3,512,128]{2,1,0:T(8,128)}, bf16[3,256,2560]{2,1,0:T(8,128)(2,1)S(1)}) custom-call(s32[2]{0:T(128)S(1)} %pad_add_fusion.3.flag_ref, bf16[512,2560]{1,0:T(8,128)(2,1)S(1)} %bitcast.12, bf16[256,2560]{1,0:T(8,128)(2,1)S(1)} %copy-done.4, bf16[48,2560]{1,0:T(8,128)(2,1)} %collective-permute-done.refs_2_, ...), custom_call_target="tpu_custom_call" | custom-call | flops 1 | bytes 1 | tf_op jit(solution)/shard_map/project_own/pallas_call | solution.py:212
  71.6 1.9 %copy-done.1 = bf16[3,256,2560]{2,1,0:T(8,128)(2,1)} copy-done((bf16[3,256,2560]{2,1,0:T(8,128)(2,1)}, bf16[3,256,2560]{2,1,0:T(8,128)(2,1)S(1)}, u32[]{:S(2)}) %copy-start.1) | copy-done | bytes 3932184
  74.8 2.1 %copy-done.2 = bf16[3,256,2560]{2,1,0:T(8,128)(2,1)S(1)} copy-done((bf16[3,256,2560]{2,1,0:T(8,128)(2,1)S(1)}, bf16[3,256,2560]{2,1,0:T(8,128)(2,1)}, u32[]{:S(2)}) %copy-start.2) | copy-done | bytes 3932184
  76.9 4.4 %project_partner.1 = (f32[3,512,128]{2,1,0:T(8,128)S(1)}, f32[2,512,128]{2,1,0:T(8,128)S(1)}, bf16[512,2560]{1,0:T(8,128)(2,1)S(1)}, f32[1,512,128]{2,1,0:T(8,128)S(1)}) custom-call(bf16[512,2560]{1,0:T(8,128)(2,1)} %collective-permute-done.5.partner_ref, bf16[3,256,2560]{2,1,0:T(8,128)(2,1)S(1)} %copy-done.2), custom_call_target="tpu_custom_call" | custom-call | flops 1 | bytes 1 | tf_op jit(solution)/shard_map/project_partner/pallas_call | solution.py:212
  81.4 3.1 %project_far.1 = (f32[2,512,128]{2,1,0:T(8,128)S(1)}, f32[2,512,128]{2,1,0:T(8,128)S(1)}) custom-call(s32[2]{0:T(128)S(1)} %pad_add_fusion.3.flag_ref, bf16[512,2560]{1,0:T(8,128)(2,1)S(1)} %bitcast.13, bf16[512,2560]{1,0:T(8,128)(2,1)S(1)} %get-tuple-element.37.refs_1_, bf16[48,2560]{1,0:T(8,128)(2,1)} %collective-permute-done.9.refs_2_, ...), custom_call_target="tpu_custom_call" | custom-call | flops 1 | bytes 1 | tf_op jit(solution)/shard_map/project_far/pallas_call | solution.py:212
  85.5 2.1 %collective-permute-done.15.refs_5_ = f32[1,512,128]{2,1,0:T(8,128)S(1)} collective-permute-done((f32[1,512,128]{2,1,0:T(8,128)S(1)}, f32[1,512,128]{2,1,0:T(8,128)S(1)}, u32[]{:S(2)}, u32[]{:S(2)}) %collective-permute-start.15) | collective-permute-done | bytes 262176 | tf_op jit(solution)/shard_map/ppermute | solution.py:329
  87.6 2.7 %collective-permute-done.17.refs_8_ = bf16[576,512]{1,0:T(8,128)(2,1)} collective-permute-done((bf16[576,512]{1,0:T(8,128)(2,1)}, bf16[576,512]{1,0:T(8,128)(2,1)}, u32[]{:S(2)}, u32[]{:S(2)}) %collective-permute-start.17) | collective-permute-done | bytes 589856 | tf_op jit(solution)/shard_map/ppermute | solution.py:364
  90.3 2.7 %attend.1 = f32[4,136,128]{2,1,0:T(8,128)S(1)} custom-call(s32[4]{0:T(128)S(1)} %pad_add_fusion.2.place_ref, s32[2,4]{1,0:T(2,128)S(1)} %pad_add_fusion.spot_ref, bf16[64,512]{1,0:T(8,128)(2,1)S(1)} %get-tuple-element.64.query_ref, f32[3,512,128]{2,1,0:T(8,128)S(1)} %get-tuple-element.34.refs_0_, f32[3,512,128]{2,1,0:T(8,128)S(1)} %get-tuple-element.36.refs_1_, ...), custom_call_target="tpu_custom_call" | custom-call | tf_op jit(solution)/shard_map/attend/pallas_call | solution.py:367
  93.9 3.0 %collective-permute-start.20 = (f32[1,136,128]{2,1,0:T(8,128)S(1)}, f32[1,136,128]{2,1,0:T(8,128)S(1)}, u32[]{:S(2)}, u32[]{:S(2)}) collective-permute-start(f32[1,136,128]{2,1,0:T(8,128)S(1)} %get-tuple-element.51), channel_id=1, source_target_pairs={{0,12},{4,0},{8,4},{12,8},{1,13},{5,1},{9,5},{13,9},{2,14},{6,2},{... | collective-permute-start | bytes 208904 | tf_op jit(solution)/shard_map/ppermute | solution.py:269
  96.9 3.1 %collective-permute-done.18.refs_1_ = f32[1,136,128]{2,1,0:T(8,128)S(1)} collective-permute-done((f32[1,136,128]{2,1,0:T(8,128)S(1)}, f32[1,136,128]{2,1,0:T(8,128)S(1)}, u32[]{:S(2)}, u32[]{:S(2)}) %collective-permute-start.18) | collective-permute-done | bytes 69664 | tf_op jit(solution)/shard_map/ppermute | solution.py:269
  100.0 1.8 %collective-permute-done.19.refs_2_ = f32[1,136,128]{2,1,0:T(8,128)S(1)} collective-permute-done((f32[1,136,128]{2,1,0:T(8,128)S(1)}, f32[1,136,128]{2,1,0:T(8,128)S(1)}, u32[]{:S(2)}, u32[]{:S(2)}) %collective-permute-start.19) | collective-permute-done | bytes 69664 | tf_op jit(solution)/shard_map/ppermute | solution.py:269
  102.7 1.6 %collective-permute-start.21 = (bf16[1,16,512]{2,1,0:T(8,128)(2,1)S(1)}, bf16[1,16,512]{2,1,0:T(8,128)(2,1)S(1)}, u32[]{:S(2)}, u32[]{:S(2)}) collective-permute-start(bf16[1,16,512]{2,1,0:T(8,128)(2,1)S(1)} %get-tuple-element.80.mine_ref), channel_id=1, source_target_pairs={{0,1},{1,0},{2,3},{3,2},{4,5},{5,4},{6,7},{7,6},{8,9},{9,8},{10,11... | collective-permute-start | bytes 49160 | tf_op jit(solution)/shard_map/ppermute | solution.py:390
  106.0 1.2 %assemble.1 = bf16[1,16,2048]{2,1,0:T(8,128)(2,1)} custom-call(s32[2]{0:T(128)S(1)} %pad_add_fusion.1.flag_ref, bf16[1,16,512]{2,1,0:T(8,128)(2,1)S(1)} %get-tuple-element.80.mine_ref, bf16[1,16,512]{2,1,0:T(8,128)(2,1)S(1)} %collective-permute-done.21.core_ref, bf16[1,16,512]{2,1,0:T(8,128)(2,1)S(1)} %collective-permute-done.22.side_ref, ...), custom_call_target="tpu_custom_call" | custom-call | tf_op jit(solution)/shard_map/assemble/pallas_call | solution.py:399
  (86 shorter events, 11.5 us)
Async XLA Ops:
  0.0 73.5 %collective-permute-start.5 = (bf16[512,2560]{1,0:T(8,128)(2,1)}, bf16[512,2560]{1,0:T(8,128)(2,1)}, u32[]{:S(2)}, u32[]{:S(2)}) collective-permute-start(bf16[512,2560]{1,0:T(8,128)(2,1)} %bitcast.11), channel_id=1, source_target_pairs={{0,2},{2,0},{1,3},{3,1},{4,6},{6,4},{5,7},{7,5},{8,10},{10,8},{9,1... | collective-permute-start | bytes 7864328 | tf_op jit(solution)/shard_map/ppermute | solution.py:272
  2.9 29.1 %copy-start.14 = (s32[8]{0:T(128)S(1)}, s32[8]{0:T(128)}, u32[]{:S(2)}) copy-start(s32[8]{0:T(128)} %param.11) | copy-start | bytes 100
  2.9 29.1 %copy-start.15 = (s32[16,1]{0,1:T(1,128)S(1)}, s32[16,1]{0,1:T(1,128)}, u32[]{:S(2)}) copy-start(s32[16,1]{0,1:T(1,128)} %param.10) | copy-start | bytes 196
  3.9 18.8 %collective-permute-start = (bf16[48,2560]{1,0:T(8,128)(2,1)S(1)}, bf16[48,2560]{1,0:T(8,128)(2,1)}, u32[]{:S(2)}, u32[]{:S(2)}) collective-permute-start(bf16[48,2560]{1,0:T(8,128)(2,1)S(1)} %constant_dynamic-slice_fusion.4), channel_id=1, source_target_pairs={{0,12},{4,0},{8,4},{12,8},{1,13},{5,1},{9,5},{13,9},{2,14},{6,2},{... | collective-permute-start | bytes 737288 | tf_op jit(solution)/shard_map/ppermute | solution.py:269
  7.6 11.2 %collective-permute-start.2 = (bf16[48,2560]{1,0:T(8,128)(2,1)S(1)}, bf16[48,2560]{1,0:T(8,128)(2,1)}, u32[]{:S(2)}, u32[]{:S(2)}) collective-permute-start(bf16[48,2560]{1,0:T(8,128)(2,1)S(1)} %constant_dynamic-slice_fusion.4), channel_id=1, source_target_pairs={{0,4},{4,8},{8,12},{12,0},{1,5},{5,9},{9,13},{13,1},{2,6},{6,10},{... | collective-permute-start | bytes 737288 | tf_op jit(solution)/shard_map/ppermute | solution.py:269
  9.5 17.1 %copy-start.11 = (bf16[8,2560]{1,0:T(8,128)(2,1)}, bf16[8,2560]{1,0:T(8,128)(2,1)S(1)}, u32[]{:S(2)}) copy-start(bf16[8,2560]{1,0:T(8,128)(2,1)S(1)} %fusion.13) | copy-start | bytes 122884
  18.8 7.8 %collective-permute-start.6 = (bf16[48,2560]{1,0:T(8,128)(2,1)}, bf16[48,2560]{1,0:T(8,128)(2,1)S(1)}, u32[]{:S(2)}, u32[]{:S(2)}) collective-permute-start(bf16[48,2560]{1,0:T(8,128)(2,1)} %collective-permute-done.2.refs_4_), channel_id=1, source_target_pairs={{0,16},{16,0},{1,17},{17,1},{2,18},{18,2},{3,19},{19,3},{4,20},{20... | collective-permute-start | bytes 737288 | tf_op jit(solution)/shard_map/ppermute | solution.py:299
  20.3 11.2 %collective-permute-start.9 = (bf16[48,2560]{1,0:T(8,128)(2,1)}, bf16[48,2560]{1,0:T(8,128)(2,1)}, u32[]{:S(2)}, u32[]{:S(2)}) collective-permute-start(bf16[48,2560]{1,0:T(8,128)(2,1)} %collective-permute-done.2.refs_4_), channel_id=1, source_target_pairs={{0,4},{4,8},{8,12},{12,0},{1,5},{5,9},{9,13},{13,1},{2,6},{6,10},{... | collective-permute-start | bytes 737288 | tf_op jit(solution)/shard_map/ppermute | solution.py:269
  21.9 41.8 %copy-start = (bf16[2,256,2560]{2,1,0:T(8,128)(2,1)S(1)}, bf16[2,256,2560]{2,1,0:T(8,128)(2,1)}, u32[]{:S(2)}) copy-start(bf16[2,256,2560]{2,1,0:T(8,128)(2,1)} %param.7) | copy-start | bytes 7864324
  22.7 18.2 %collective-permute-start.3 = (bf16[88,2560]{1,0:T(8,128)(2,1)}, bf16[88,2560]{1,0:T(8,128)(2,1)S(1)}, u32[]{:S(2)}, u32[]{:S(2)}) collective-permute-start(bf16[88,2560]{1,0:T(8,128)(2,1)} %pad_maximum_fusion), channel_id=1, source_target_pairs={{0,4},{4,8},{8,12},{12,0},{1,5},{5,9},{9,13},{13,1},{2,6},{6,10},{... | collective-permute-start | bytes 1351688 | tf_op jit(solution)/shard_map/ppermute | solution.py:269
  22.7 27.7 %collective-permute-start.1 = (bf16[88,2560]{1,0:T(8,128)(2,1)}, bf16[88,2560]{1,0:T(8,128)(2,1)S(1)}, u32[]{:S(2)}, u32[]{:S(2)}) collective-permute-start(bf16[88,2560]{1,0:T(8,128)(2,1)} %pad_maximum_fusion), channel_id=1, source_target_pairs={{0,12},{4,0},{8,4},{12,8},{1,13},{5,1},{9,5},{13,9},{2,14},{6,2},{... | collective-permute-start | bytes 1351688 | tf_op jit(solution)/shard_map/ppermute | solution.py:269
  27.3 8.4 %collective-permute-start.7 = (bf16[48,2560]{1,0:T(8,128)(2,1)}, bf16[48,2560]{1,0:T(8,128)(2,1)}, u32[]{:S(2)}, u32[]{:S(2)}) collective-permute-start(bf16[48,2560]{1,0:T(8,128)(2,1)} %collective-permute-done.refs_2_), channel_id=1, source_target_pairs={{0,16},{16,0},{1,17},{17,1},{2,18},{18,2},{3,19},{19,3},{4,20},{20... | collective-permute-start | bytes 737288 | tf_op jit(solution)/shard_map/ppermute | solution.py:299
  31.5 19.0 %collective-permute-start.10 = (bf16[48,2560]{1,0:T(8,128)(2,1)}, bf16[48,2560]{1,0:T(8,128)(2,1)}, u32[]{:S(2)}, u32[]{:S(2)}) collective-permute-start(bf16[48,2560]{1,0:T(8,128)(2,1)} %collective-permute-done.9.refs_2_), channel_id=1, source_target_pairs={{0,16},{16,0},{1,17},{17,1},{2,18},{18,2},{3,19},{19,3},{4,20},{20... | collective-permute-start | bytes 737288 | tf_op jit(solution)/shard_map/ppermute | solution.py:299
  32.0 31.7 %copy-start.10 = (bf16[48,2560]{1,0:T(8,128)(2,1)S(1)}, bf16[48,2560]{1,0:T(8,128)(2,1)}, u32[]{:S(2)}) copy-start(bf16[48,2560]{1,0:T(8,128)(2,1)} %copy-done.9) | copy-start | bytes 737284
  40.9 18.1 %copy-start.5 = (bf16[88,2560]{1,0:T(8,128)(2,1)}, bf16[88,2560]{1,0:T(8,128)(2,1)S(1)}, u32[]{:S(2)}) copy-start(bf16[88,2560]{1,0:T(8,128)(2,1)S(1)} %collective-permute-done.3.refs_5_) | copy-start | bytes 1351684
  40.9 11.1 %collective-permute-start.8 = (bf16[88,2560]{1,0:T(8,128)(2,1)S(1)}, bf16[88,2560]{1,0:T(8,128)(2,1)S(1)}, u32[]{:S(2)}, u32[]{:S(2)}) collective-permute-start(bf16[88,2560]{1,0:T(8,128)(2,1)S(1)} %collective-permute-done.3.refs_5_), channel_id=1, source_target_pairs={{0,16},{16,0},{1,17},{17,1},{2,18},{18,2},{3,19},{19,3},{4,20},{20... | collective-permute-start | bytes 1351688 | tf_op jit(solution)/shard_map/ppermute | solution.py:299
  41.4 16.2 %collective-permute-start.4 = (bf16[88,2560]{1,0:T(8,128)(2,1)S(1)}, bf16[88,2560]{1,0:T(8,128)(2,1)}, u32[]{:S(2)}, u32[]{:S(2)}) collective-permute-start(bf16[88,2560]{1,0:T(8,128)(2,1)S(1)} %collective-permute-done.3.refs_5_), channel_id=1, source_target_pairs={{0,4},{4,8},{8,12},{12,0},{1,5},{5,9},{9,13},{13,1},{2,6},{6,10},{... | collective-permute-start | bytes 1351688 | tf_op jit(solution)/shard_map/ppermute | solution.py:269
  50.5 8.5 %copy-start.7 = (bf16[88,2560]{1,0:T(8,128)(2,1)}, bf16[88,2560]{1,0:T(8,128)(2,1)S(1)}, u32[]{:S(2)}) copy-start(bf16[88,2560]{1,0:T(8,128)(2,1)S(1)} %collective-permute-done.1.refs_3_) | copy-start | bytes 1351684
  50.5 13.2 %collective-permute-start.11 = (bf16[88,2560]{1,0:T(8,128)(2,1)S(1)}, bf16[88,2560]{1,0:T(8,128)(2,1)S(1)}, u32[]{:S(2)}, u32[]{:S(2)}) collective-permute-start(bf16[88,2560]{1,0:T(8,128)(2,1)S(1)} %collective-permute-done.1.refs_3_), channel_id=1, source_target_pairs={{0,16},{16,0},{1,17},{17,1},{2,18},{18,2},{3,19},{19,3},{4,20},{20... | collective-permute-start | bytes 1351688 | tf_op jit(solution)/shard_map/ppermute | solution.py:299
  57.7 23.7 %collective-permute-start.12 = (bf16[88,2560]{1,0:T(8,128)(2,1)}, bf16[88,2560]{1,0:T(8,128)(2,1)}, u32[]{:S(2)}, u32[]{:S(2)}) collective-permute-start(bf16[88,2560]{1,0:T(8,128)(2,1)} %collective-permute-done.4.refs_3_), channel_id=1, source_target_pairs={{0,16},{16,0},{1,17},{17,1},{2,18},{18,2},{3,19},{19,3},{4,20},{20... | collective-permute-start | bytes 1351688 | tf_op jit(solution)/shard_map/ppermute | solution.py:299
  73.5 11.9 %collective-permute-start.13 = (f32[3,512,128]{2,1,0:T(8,128)}, f32[3,512,128]{2,1,0:T(8,128)}, u32[]{:S(2)}, u32[]{:S(2)}) collective-permute-start(f32[3,512,128]{2,1,0:T(8,128)} %get-tuple-element.40), channel_id=1, source_target_pairs={{0,1},{1,0},{2,3},{3,2},{4,5},{5,4},{6,7},{7,6},{8,9},{9,8},{10,11... | collective-permute-start | bytes 2359304 | tf_op jit(solution)/shard_map/ppermute | solution.py:329
  74.3 16.0 %collective-permute-start.17 = (bf16[576,512]{1,0:T(8,128)(2,1)}, bf16[576,512]{1,0:T(8,128)(2,1)}, u32[]{:S(2)}, u32[]{:S(2)}) collective-permute-start(bf16[576,512]{1,0:T(8,128)(2,1)} %constant_dynamic-update-slice_fusion.16), channel_id=1, source_target_pairs={{0,2},{2,0},{1,3},{3,1},{4,6},{6,4},{5,7},{7,5},{8,10},{10,8},{9,1... | collective-permute-start | bytes 1769480 | tf_op jit(solution)/shard_map/ppermute | solution.py:364
  81.4 8.9 %copy-start.3 = (bf16[2,256,2048]{2,1,0:T(8,128)(2,1)S(1)}, bf16[2,256,2048]{2,1,0:T(8,128)(2,1)}, u32[]{:S(2)}) copy-start(bf16[2,256,2048]{2,1,0:T(8,128)(2,1)} %param.8) | copy-start | bytes 6291460
  84.5 3.1 %collective-permute-start.16 = (f32[2,512,128]{2,1,0:T(8,128)S(1)}, f32[2,512,128]{2,1,0:T(8,128)S(1)}, u32[]{:S(2)}, u32[]{:S(2)}) collective-permute-start(f32[2,512,128]{2,1,0:T(8,128)S(1)} %get-tuple-element.43), channel_id=1, source_target_pairs={{0,1},{1,0},{2,3},{3,2},{4,5},{5,4},{6,7},{7,6},{8,9},{9,8},{10,11... | collective-permute-start | bytes 1572872 | tf_op jit(solution)/shard_map/ppermute | solution.py:329
  84.8 2.8 %collective-permute-start.14 = (f32[2,512,128]{2,1,0:T(8,128)S(1)}, f32[2,512,128]{2,1,0:T(8,128)S(1)}, u32[]{:S(2)}, u32[]{:S(2)}) collective-permute-start(f32[2,512,128]{2,1,0:T(8,128)S(1)} %get-tuple-element.41), channel_id=1, source_target_pairs={{0,1},{1,0},{2,3},{3,2},{4,5},{5,4},{6,7},{7,6},{8,9},{9,8},{10,11... | collective-permute-start | bytes 1572872 | tf_op jit(solution)/shard_map/ppermute | solution.py:329
  85.1 2.5 %collective-permute-start.15 = (f32[1,512,128]{2,1,0:T(8,128)S(1)}, f32[1,512,128]{2,1,0:T(8,128)S(1)}, u32[]{:S(2)}, u32[]{:S(2)}) collective-permute-start(f32[1,512,128]{2,1,0:T(8,128)S(1)} %get-tuple-element.42), channel_id=1, source_target_pairs={{0,1},{1,0},{2,3},{3,2},{4,5},{5,4},{6,7},{7,6},{8,9},{9,8},{10,11... | collective-permute-start | bytes 786440 | tf_op jit(solution)/shard_map/ppermute | solution.py:329
  93.1 6.9 %collective-permute-start.18 = (f32[1,136,128]{2,1,0:T(8,128)S(1)}, f32[1,136,128]{2,1,0:T(8,128)S(1)}, u32[]{:S(2)}, u32[]{:S(2)}) collective-permute-start(f32[1,136,128]{2,1,0:T(8,128)S(1)} %get-tuple-element.53), channel_id=1, source_target_pairs={{0,4},{4,8},{8,12},{12,0},{1,5},{5,9},{9,13},{13,1},{2,6},{6,10},{... | collective-permute-start | bytes 208904 | tf_op jit(solution)/shard_map/ppermute | solution.py:269
  93.6 8.2 %collective-permute-start.19 = (f32[1,136,128]{2,1,0:T(8,128)S(1)}, f32[1,136,128]{2,1,0:T(8,128)S(1)}, u32[]{:S(2)}, u32[]{:S(2)}) collective-permute-start(f32[1,136,128]{2,1,0:T(8,128)S(1)} %get-tuple-element.52), channel_id=1, source_target_pairs={{0,8},{4,12},{8,0},{12,4},{1,9},{5,13},{9,1},{13,5},{2,10},{6,14},... | collective-permute-start | bytes 208904 | tf_op jit(solution)/shard_map/ppermute | solution.py:269
  93.9 7.9 %collective-permute-start.20 = (f32[1,136,128]{2,1,0:T(8,128)S(1)}, f32[1,136,128]{2,1,0:T(8,128)S(1)}, u32[]{:S(2)}, u32[]{:S(2)}) collective-permute-start(f32[1,136,128]{2,1,0:T(8,128)S(1)} %get-tuple-element.51), channel_id=1, source_target_pairs={{0,12},{4,0},{8,4},{12,8},{1,13},{5,1},{9,5},{13,9},{2,14},{6,2},{... | collective-permute-start | bytes 208904 | tf_op jit(solution)/shard_map/ppermute | solution.py:269
  102.1 3.9 %collective-permute-start.22 = (bf16[1,16,512]{2,1,0:T(8,128)(2,1)S(1)}, bf16[1,16,512]{2,1,0:T(8,128)(2,1)S(1)}, u32[]{:S(2)}, u32[]{:S(2)}) collective-permute-start(bf16[1,16,512]{2,1,0:T(8,128)(2,1)S(1)} %get-tuple-element.79), channel_id=1, source_target_pairs={{0,2},{2,0},{1,3},{3,1},{4,6},{6,4},{5,7},{7,5},{8,10},{10,8},{9,1... | collective-permute-start | bytes 49160 | tf_op jit(solution)/shard_map/ppermute | solution.py:391
  102.7 3.3 %collective-permute-start.23 = (bf16[1,16,512]{2,1,0:T(8,128)(2,1)S(1)}, bf16[1,16,512]{2,1,0:T(8,128)(2,1)S(1)}, u32[]{:S(2)}, u32[]{:S(2)}) collective-permute-start(bf16[1,16,512]{2,1,0:T(8,128)(2,1)S(1)} %get-tuple-element.79), channel_id=1, source_target_pairs={{0,3},{3,0},{1,2},{2,1},{4,7},{7,4},{5,6},{6,5},{8,11},{11,8},{9,1... | collective-permute-start | bytes 49160 | tf_op jit(solution)/shard_map/ppermute | solution.py:392
  102.7 2.4 %collective-permute-start.21 = (bf16[1,16,512]{2,1,0:T(8,128)(2,1)S(1)}, bf16[1,16,512]{2,1,0:T(8,128)(2,1)S(1)}, u32[]{:S(2)}, u32[]{:S(2)}) collective-permute-start(bf16[1,16,512]{2,1,0:T(8,128)(2,1)S(1)} %get-tuple-element.80.mine_ref), channel_id=1, source_target_pairs={{0,1},{1,0},{2,3},{3,2},{4,5},{5,4},{6,7},{7,6},{8,9},{9,8},{10,11... | collective-permute-start | bytes 49160 | tf_op jit(solution)/shard_map/ppermute | solution.py:390
  (8 other events, 22.2 us)

commit v12 on v11

--- a/solution.py
+++ b/solution.py
@@ -10,7 +10,7 @@
 
 HEAD_DIM = 64
 EMPTY = -3e38
-FIRST_EIGHTHS = 3
+FIRST_EIGHTHS = 4
 ROW_COPIES = 4
 PROJECT_LIMIT = 24 * 1024 * 1024
 VMEM_LIMIT = 22 * 1024 * 1024
@@ -58,20 +58,23 @@
             )
 
 
-def partner_kernel(partner_ref, block_ref, keep_ref, send_ref, rows_ref, last_ref, semaphores):
+def near_kernel(flag_ref, hidden_ref, partner_ref, *refs, blocks, sends):
+    *refs, keep_ref, rows_ref, block_ref, semaphores = refs
+    refs, send_refs = refs[: len(refs) - len(sends)], refs[len(refs) - len(sends) :]
     step = rows_ref.shape[0] // ROW_COPIES
     copies = []
     for part in range(ROW_COPIES):
         rows = pl.ds(part * step, step)
         copies.append(pltpu.make_async_copy(partner_ref.at[rows], rows_ref.at[rows], semaphores.at[part]))
         copies[-1].start()
-    for part in range(2):
-        where = slice(part * rows_ref.shape[0] // 2, (part + 1) * rows_ref.shape[0] // 2)
-        for copy in copies[part * ROW_COPIES // 2 : (part + 1) * ROW_COPIES // 2]:
+    for source, source_ref in enumerate((hidden_ref, rows_ref)):
+        for copy in copies if source else []:
             copy.wait()
-        for at in range(block_ref.shape[0]):
-            last = at == block_ref.shape[0] - 1
-            multiply(rows_ref[where, :], block_ref[at], keep_ref, last_ref if last else send_ref, at, where)
+        for at, block in enumerate(blocks):
+            if not source:
+                join(block_ref, at, block, refs, flag_ref[0], flag_ref[1])
+            slot = source * len(blocks) + at
+            multiply(source_ref[...], block_ref[at], keep_ref, send_refs[slot // 2], slot, slice(None))
 
 
 def attend_kernel(place_ref, spot_ref, query_ref, *refs, pieces):
@@ -213,7 +216,7 @@
         kernel,
         out_shape=[jax.ShapeDtypeStruct((count, rows, half), jnp.float32) for count in counts] + handed,
         in_specs=placed,
-        out_specs=in_vmem(2 + len(handed)),
+        out_specs=in_vmem(len(counts) + len(handed)),
         scratch_shapes=scratch,
         compiler_params=pltpu.CompilerParams(vmem_limit_bytes=PROJECT_LIMIT),
         cost_estimate=pl.CostEstimate(flops=1, bytes_accessed=1, transcendentals=0),
@@ -309,27 +312,23 @@
         spots = jnp.stack([(spots * 2 + side) * stride + core * span, spots * span])
         own_residual = passages
 
-        joined = jax.ShapeDtypeStruct((len(near), shard, units), down_weight.dtype)
-        kept, away, joined = project(
-            functools.partial(join_kernel, sources=1, blocks=near), "project_own", [flags, hidden] + near_pieces,
-            in_smem(1) + in_vmem(1 + len(near_pieces)), [len(near)] * 2, rows, half, [joined], [],
-        )
-        partner_kept, partner_away, partner_rows, partner_last = project(
-            partner_kernel, "project_partner", [partner_hidden, joined],
-            [pl.BlockSpec(memory_space=pl.ANY)] + in_vmem(1), [len(near), len(near) - 1], rows, half,
-            [jax.ShapeDtypeStruct(hidden.shape, hidden.dtype), jax.ShapeDtypeStruct((1, rows, half), jnp.float32)],
-            [pltpu.SemaphoreType.DMA((ROW_COPIES,))],
+        sends = [2] * len(near)
+        *away, kept, partner_rows = project(
+            functools.partial(near_kernel, blocks=near, sends=sends), "project_near",
+            [flags, hidden, partner_hidden] + near_pieces,
+            in_smem(1) + in_vmem(1) + [pl.BlockSpec(memory_space=pl.ANY)] + in_vmem(len(near_pieces)),
+            sends + [2 * len(near)], rows, half, [jax.ShapeDtypeStruct(hidden.shape, hidden.dtype)],
+            [pltpu.VMEM((len(near), shard, units), down_weight.dtype), pltpu.SemaphoreType.DMA((ROW_COPIES,))],
         )
         far_kept, far_away = project(
             functools.partial(join_kernel, sources=2, blocks=far), "project_far",
             [flags, hidden, partner_rows] + far_pieces, in_smem(1) + in_vmem(2 + len(far_pieces)), [2, 2], rows, half,
             [], [pltpu.VMEM((1, shard, units), down_weight.dtype)],
         )
-        summands = [kept, partner_kept, far_kept]
-        summands += [lax.ppermute(piece, "mp", SWAP) for piece in (away, partner_away, partner_last, far_away)]
-        pieces = [(0, (0, at), (3, at), at) for at in range(3)]
-        pieces += [(1, (1, at), (4 + at // 2, at % 2), at) for at in range(3)]
-        pieces += [(source, (2, source), (6, source), 3) for source in range(2)]
+        summands = [kept, far_kept]
+        summands += [lax.ppermute(piece, "mp", SWAP) for piece in (*away, far_away)]
+        pieces = [(at // 3, (0, at), (2 + at // 2, at % 2), at % 3) for at in range(6)]
+        pieces += [(source, (1, source), (5, source), 3) for source in range(2)]
         origin = high
     else:
         queries = lax.all_gather(queries, ("high", "low"), axis=0, tiled=True)

time: 108 us -> 103 us (0.954)
  local copies, waits for them, and re-layouts: 13.7 us -> 6.36 us
  waiting for transfers between devices: 51.4 us -> 56.3 us
  Pallas kernels: 16.3 us -> 13.1 us
  starting transfers between devices: 23.5 us -> 25.4 us
    ppermute x6, waiting for transfers between devices: 7.13 us -> 26.4 us  [body(): lax.ppermute(after(piece, swapped[max(at - 2, 0):max(at - 1, 0)]), 'group...]
    ppermute x9, waiting for transfers between devices: 37.8 us -> 25.1 us  [shifted(): lax.ppermute(array, 'high', [(at, (at + shift) % highs) for at in range(h...]
    unnamed x39 -> x33, local copies, waits for them, and re-layouts: 8.12 us -> 4.82 us
    ppermute x1, waiting for transfers between devices: 2.68 us -> 0.01 us  [body(): partner = lax.ppermute(leaving, 'side', SWAP)]
    pallas_call x3 -> x2, Pallas kernels: 12.1 us -> 9.66 us  [project(): pl.pallas_call(kernel, out_shape=[jax.ShapeDtypeStruct((count, rows, half...]
    ppermute x6, starting transfers between devices: 4.05 us -> 6.1 us  [body(): lax.ppermute(after(piece, swapped[max(at - 2, 0):max(at - 1, 0)]), 'group...]
    dynamic_slice x2, local copies, waits for them, and re-layouts: 1.98 us -> 0.15 us  [features(): lax.dynamic_slice_in_dim(array, start, span, axis=array.ndim - 1)]
    ppermute x9, starting transfers between devices: 13 us -> 11.3 us  [shifted(): lax.ppermute(array, 'high', [(at, (at + shift) % highs) for at in range(h...]
  transfers between devices with their start and end apart: 24 -> 24, of which waited for: 13 -> 13; matrix products, arithmetic and copies ran while one was open for 7% -> 3% of each run, Pallas kernels for 11% -> 9%
where the time goes in v12:
time: 103 us
  waiting for transfers between devices  56.3 us (55%)
  starting transfers between devices  25.4 us (25%)
  Pallas kernels  13.1 us (13%)
  local copies, waits for them, and re-layouts  6.36 us (6%)
  other arithmetic  1.2 us (1%)
    ppermute x6, waiting for transfers between devices, body(): lax.ppermute(after(piece, swapped[max(at - 2, 0):max(at - 1, 0)]), 'group...  26.4 us
    ppermute x9, waiting for transfers between devices, shifted(): lax.ppermute(array, 'high', [(at, (at + shift) % highs) for at in range(h...  25.1 us
    ppermute x9, starting transfers between devices, shifted(): lax.ppermute(array, 'high', [(at, (at + shift) % highs) for at in range(h...  11.3 us
    pallas_call x2, Pallas kernels, project(): pl.pallas_call(kernel, out_shape=[jax.ShapeDtypeStruct((count, rows, half...  9.66 us
    ppermute x6, starting transfers between devices, body(): lax.ppermute(after(piece, swapped[max(at - 2, 0):max(at - 1, 0)]), 'group...  6.1 us
    unnamed x33, local copies, waits for them, and re-layouts  4.82 us
    ppermute x4, waiting for transfers between devices, body(): summands += [lax.ppermute(piece, 'mp', SWAP) for piece in (*away, far_away)]  3.1 us
    ppermute x1, starting transfers between devices, body(): partner_hidden = lax.ppermute(hidden, 'side', SWAP)  2.94 us
  transfers between devices with their start and end apart: 24, of which 13 were waited for; matrix products, arithmetic and copies ran while one was open for 3% of the time, Pallas kernels for 9%

profile of v12, /device:TPU:0, one launch (start us, length us, event | category | flops | bytes accessed | tf_op | source)
XLA Modules:
  0.0 102.6 jit_solution(412239573431967350)
XLA Ops:
  0.0 2.9 %collective-permute-start.5 = (bf16[512,2560]{1,0:T(8,128)(2,1)}, bf16[512,2560]{1,0:T(8,128)(2,1)}, u32[]{:S(2)}, u32[]{:S(2)}) collective-permute-start(bf16[512,2560]{1,0:T(8,128)(2,1)} %bitcast.11), channel_id=1, source_target_pairs={{0,2},{2,0},{1,3},{3,1},{4,6},{6,4},{5,7},{7,5},{8,10},{10,8},{9,1... | collective-permute-start | bytes 7864328 | tf_op jit(solution)/shard_map/ppermute | solution.py:275
  2.9 1.3 %constant_dynamic-slice_fusion.4 = (bf16[64,2560]{1,0:T(8,128)(2,1)S(1)}, bf16[64,2560]{1,0:T(8,128)(2,1)S(1)}) fusion(bf16[256,2560]{1,0:T(8,128)(2,1)} %refs_0_.1, s32[]{:T(128)S(6)} %select_n.73, s32[]{:T(128)S(6)} %select_n.72), kind=kLoop, calls=%fused_computation.41 | loop fusion | bytes 1310728 | tf_op jit(solution)/shard_map/dynamic_slice | solution.py:284
  4.2 3.7 %collective-permute-start = (bf16[64,2560]{1,0:T(8,128)(2,1)S(1)}, bf16[64,2560]{1,0:T(8,128)(2,1)S(1)}, u32[]{:S(2)}, u32[]{:S(2)}) collective-permute-start(bf16[64,2560]{1,0:T(8,128)(2,1)S(1)} %get-tuple-element.47), channel_id=1, source_target_pairs={{0,12},{4,0},{8,4},{12,8},{1,13},{5,1},{9,5},{13,9},{2,14},{6,2},{... | collective-permute-start | bytes 983048 | tf_op jit(solution)/shard_map/ppermute | solution.py:272
  7.9 0.8 pad_maximum_fusion
  8.7 13.9 %collective-permute-done.2.refs_3_ = bf16[64,2560]{1,0:T(8,128)(2,1)} collective-permute-done((bf16[64,2560]{1,0:T(8,128)(2,1)S(1)}, bf16[64,2560]{1,0:T(8,128)(2,1)}, u32[]{:S(2)}, u32[]{:S(2)}) %collective-permute-start.2) | collective-permute-done | bytes 327712 | tf_op jit(solution)/shard_map/ppermute | solution.py:272
  22.6 1.6 %collective-permute-start.3 = (bf16[72,2560]{1,0:T(8,128)(2,1)}, bf16[72,2560]{1,0:T(8,128)(2,1)S(1)}, u32[]{:S(2)}, u32[]{:S(2)}) collective-permute-start(bf16[72,2560]{1,0:T(8,128)(2,1)} %pad_maximum_fusion), channel_id=1, source_target_pairs={{0,4},{4,8},{8,12},{12,0},{1,5},{5,9},{9,13},{13,1},{2,6},{6,10},{... | collective-permute-start | bytes 1105928 | tf_op jit(solution)/shard_map/ppermute | solution.py:272
  24.2 1.5 %collective-permute-start.6 = (bf16[64,2560]{1,0:T(8,128)(2,1)}, bf16[64,2560]{1,0:T(8,128)(2,1)S(1)}, u32[]{:S(2)}, u32[]{:S(2)}) collective-permute-start(bf16[64,2560]{1,0:T(8,128)(2,1)} %collective-permute-done.2.refs_3_), channel_id=1, source_target_pairs={{0,16},{16,0},{1,17},{17,1},{2,18},{18,2},{3,19},{19,3},{4,20},{20... | collective-permute-start | bytes 983048 | tf_op jit(solution)/shard_map/ppermute | solution.py:302
  26.4 13.1 %collective-permute-done.7.refs_6_ = bf16[64,2560]{1,0:T(8,128)(2,1)S(1)} collective-permute-done((bf16[64,2560]{1,0:T(8,128)(2,1)S(1)}, bf16[64,2560]{1,0:T(8,128)(2,1)S(1)}, u32[]{:S(2)}, u32[]{:S(2)}) %collective-permute-start.7) | collective-permute-done | bytes 327712 | tf_op jit(solution)/shard_map/ppermute | solution.py:302
  39.5 0.8 copy-done.5
  40.2 2.2 %collective-permute-start.1 = (bf16[72,2560]{1,0:T(8,128)(2,1)}, bf16[72,2560]{1,0:T(8,128)(2,1)S(1)}, u32[]{:S(2)}, u32[]{:S(2)}) collective-permute-start(bf16[72,2560]{1,0:T(8,128)(2,1)} %pad_maximum_fusion), channel_id=1, source_target_pairs={{0,12},{4,0},{8,4},{12,8},{1,13},{5,1},{9,5},{13,9},{2,14},{6,2},{... | collective-permute-start | bytes 1105928 | tf_op jit(solution)/shard_map/ppermute | solution.py:272
  42.4 1.5 %collective-permute-start.8 = (bf16[72,2560]{1,0:T(8,128)(2,1)S(1)}, bf16[72,2560]{1,0:T(8,128)(2,1)}, u32[]{:S(2)}, u32[]{:S(2)}) collective-permute-start(bf16[72,2560]{1,0:T(8,128)(2,1)S(1)} %collective-permute-done.3.refs_4_), channel_id=1, source_target_pairs={{0,16},{16,0},{1,17},{17,1},{2,18},{18,2},{3,19},{19,3},{4,20},{20... | collective-permute-start | bytes 1105928 | tf_op jit(solution)/shard_map/ppermute | solution.py:302
  45.6 6.2 %collective-permute-done.1.refs_2_ = bf16[72,2560]{1,0:T(8,128)(2,1)S(1)} collective-permute-done((bf16[72,2560]{1,0:T(8,128)(2,1)}, bf16[72,2560]{1,0:T(8,128)(2,1)S(1)}, u32[]{:S(2)}, u32[]{:S(2)}) %collective-permute-start.1) | collective-permute-done | bytes 368672 | tf_op jit(solution)/shard_map/ppermute | solution.py:272
  51.8 6.3 %collective-permute-done.10.refs_4_ = bf16[64,2560]{1,0:T(8,128)(2,1)S(1)} collective-permute-done((bf16[64,2560]{1,0:T(8,128)(2,1)}, bf16[64,2560]{1,0:T(8,128)(2,1)S(1)}, u32[]{:S(2)}, u32[]{:S(2)}) %collective-permute-start.10) | collective-permute-done | bytes 327712 | tf_op jit(solution)/shard_map/ppermute | solution.py:302
  58.1 1.5 %collective-permute-start.11 = (bf16[72,2560]{1,0:T(8,128)(2,1)S(1)}, bf16[72,2560]{1,0:T(8,128)(2,1)S(1)}, u32[]{:S(2)}, u32[]{:S(2)}) collective-permute-start(bf16[72,2560]{1,0:T(8,128)(2,1)S(1)} %collective-permute-done.1.refs_2_), channel_id=1, source_target_pairs={{0,16},{16,0},{1,17},{17,1},{2,18},{18,2},{3,19},{19,3},{4,20},{20... | collective-permute-start | bytes 1105928 | tf_op jit(solution)/shard_map/ppermute | solution.py:302
  60.2 1.8 %collective-permute-start.17 = (bf16[576,512]{1,0:T(8,128)(2,1)S(1)}, bf16[576,512]{1,0:T(8,128)(2,1)S(1)}, u32[]{:S(2)}, u32[]{:S(2)}) collective-permute-start(bf16[576,512]{1,0:T(8,128)(2,1)S(1)} %constant_dynamic-update-slice_fusion.16), channel_id=1, source_target_pairs={{0,2},{2,0},{1,3},{3,1},{4,6},{6,4},{5,7},{7,5},{8,10},{10,8},{9,1... | collective-permute-start | bytes 1769480 | tf_op jit(solution)/shard_map/ppermute | solution.py:363
  62.1 6.9 %collective-permute-done.11.refs_8_ = bf16[72,2560]{1,0:T(8,128)(2,1)S(1)} collective-permute-done((bf16[72,2560]{1,0:T(8,128)(2,1)S(1)}, bf16[72,2560]{1,0:T(8,128)(2,1)S(1)}, u32[]{:S(2)}, u32[]{:S(2)}) %collective-permute-start.11) | collective-permute-done | bytes 368672 | tf_op jit(solution)/shard_map/ppermute | solution.py:302
  69.0 1.3 %copy-done.2 = bf16[256,2560]{1,0:T(8,128)(2,1)S(1)} copy-done((bf16[256,2560]{1,0:T(8,128)(2,1)S(1)}, bf16[256,2560]{1,0:T(8,128)(2,1)}, u32[]{:S(2)}) %copy-start.2) | copy-done | bytes 1310744
  70.3 1.0 copy-done.4
  71.3 1.0 copy-done.6
  72.3 7.0 %project_near.1 = (f32[2,512,128]{2,1,0:T(8,128)S(1)}, f32[2,512,128]{2,1,0:T(8,128)S(1)}, f32[2,512,128]{2,1,0:T(8,128)S(1)}, f32[6,512,128]{2,1,0:T(8,128)S(1)}, bf16[512,2560]{1,0:T(8,128)(2,1)S(1)}) custom-call(s32[2]{0:T(128)S(1)} %pad_add_fusion.3.flag_ref, bf16[512,2560]{1,0:T(8,128)(2,1)S(1)} %bitcast.12, ...), custom_call_target="tpu_custom_call" | custom-call | flops 1 | bytes 1 | tf_op jit(solution)/shard_map/project_near/pallas_call | solution.py:215
  79.4 2.6 %project_far.1 = (f32[2,512,128]{2,1,0:T(8,128)S(1)}, f32[2,512,128]{2,1,0:T(8,128)S(1)}) custom-call(s32[2]{0:T(128)S(1)} %pad_add_fusion.3.flag_ref, bf16[512,2560]{1,0:T(8,128)(2,1)S(1)} %bitcast.13, bf16[512,2560]{1,0:T(8,128)(2,1)S(1)} %get-tuple-element.33.refs_1_, bf16[64,2560]{1,0:T(8,128)(2,1)} %collective-permute-done.9.refs_2_, ...), custom_call_target="tpu_custom_call" | custom-call | flops 1 | bytes 1 | tf_op jit(solution)/shard_map/project_far/pallas_call | solution.py:215
  83.1 0.8 collective-permute-done.16.refs_5_
  84.0 0.7 collective-permute-done.13.refs_2_
  84.7 0.7 collective-permute-done.14.refs_3_
  86.2 2.0 %attend.1 = f32[4,136,128]{2,1,0:T(8,128)S(1)} custom-call(s32[4]{0:T(128)S(1)} %pad_add_fusion.2.place_ref, s32[2,4]{1,0:T(2,128)S(1)} %pad_add_fusion.spot_ref, bf16[64,512]{1,0:T(8,128)(2,1)S(1)} %get-tuple-element.62.query_ref, f32[6,512,128]{2,1,0:T(8,128)S(1)} %get-tuple-element.32.refs_0_, f32[2,512,128]{2,1,0:T(8,128)S(1)} %get-tuple-element.35.refs_1_, ...), custom_call_target="tpu_custom_call" | custom-call | tf_op jit(solution)/shard_map/attend/pallas_call | solution.py:366
  88.6 3.5 %collective-permute-start.20 = (f32[1,136,128]{2,1,0:T(8,128)S(1)}, f32[1,136,128]{2,1,0:T(8,128)S(1)}, u32[]{:S(2)}, u32[]{:S(2)}) collective-permute-start(f32[1,136,128]{2,1,0:T(8,128)S(1)} %get-tuple-element.49), channel_id=1, source_target_pairs={{0,12},{4,0},{8,4},{12,8},{1,13},{5,1},{9,5},{13,9},{2,14},{6,2},{... | collective-permute-start | bytes 208904 | tf_op jit(solution)/shard_map/ppermute | solution.py:272
  92.1 3.0 %collective-permute-done.18.refs_1_ = f32[1,136,128]{2,1,0:T(8,128)S(1)} collective-permute-done((f32[1,136,128]{2,1,0:T(8,128)S(1)}, f32[1,136,128]{2,1,0:T(8,128)S(1)}, u32[]{:S(2)}, u32[]{:S(2)}) %collective-permute-start.18) | collective-permute-done | bytes 69664 | tf_op jit(solution)/shard_map/ppermute | solution.py:272
  95.2 2.0 %collective-permute-done.19.refs_2_ = f32[1,136,128]{2,1,0:T(8,128)S(1)} collective-permute-done((f32[1,136,128]{2,1,0:T(8,128)S(1)}, f32[1,136,128]{2,1,0:T(8,128)S(1)}, u32[]{:S(2)}, u32[]{:S(2)}) %collective-permute-start.19) | collective-permute-done | bytes 69664 | tf_op jit(solution)/shard_map/ppermute | solution.py:272
  98.1 1.6 %collective-permute-start.21 = (bf16[1,16,512]{2,1,0:T(8,128)(2,1)S(1)}, bf16[1,16,512]{2,1,0:T(8,128)(2,1)S(1)}, u32[]{:S(2)}, u32[]{:S(2)}) collective-permute-start(bf16[1,16,512]{2,1,0:T(8,128)(2,1)S(1)} %get-tuple-element.78.mine_ref), channel_id=1, source_target_pairs={{0,1},{1,0},{2,3},{3,2},{4,5},{5,4},{6,7},{7,6},{8,9},{9,8},{10,11... | collective-permute-start | bytes 49160 | tf_op jit(solution)/shard_map/ppermute | solution.py:389
  99.8 0.8 collective-permute-done.21.core_ref
  100.5 0.9 collective-permute-done.22.side_ref
  101.4 1.2 %assemble.1 = bf16[1,16,2048]{2,1,0:T(8,128)(2,1)} custom-call(s32[2]{0:T(128)S(1)} %pad_add_fusion.1.flag_ref, bf16[1,16,512]{2,1,0:T(8,128)(2,1)S(1)} %get-tuple-element.78.mine_ref, bf16[1,16,512]{2,1,0:T(8,128)(2,1)S(1)} %collective-permute-done.21.core_ref, bf16[1,16,512]{2,1,0:T(8,128)(2,1)S(1)} %collective-permute-done.22.side_ref, ...), custom_call_target="tpu_custom_call" | custom-call | tf_op jit(solution)/shard_map/assemble/pallas_call | solution.py:398
  (78 shorter events, 6.1 us)
Async XLA Ops:
  0.0 7.9 %copy-start.9 = (bf16[1,16,2048]{2,1,0:T(8,128)(2,1)S(1)}, bf16[1,16,2048]{2,1,0:T(8,128)(2,1)}, u32[]{:S(2)}) copy-start(bf16[1,16,2048]{2,1,0:T(8,128)(2,1)} %param.12) | copy-start | bytes 196612
  0.0 60.1 %collective-permute-start.5 = (bf16[512,2560]{1,0:T(8,128)(2,1)}, bf16[512,2560]{1,0:T(8,128)(2,1)}, u32[]{:S(2)}, u32[]{:S(2)}) collective-permute-start(bf16[512,2560]{1,0:T(8,128)(2,1)} %bitcast.11), channel_id=1, source_target_pairs={{0,2},{2,0},{1,3},{3,1},{4,6},{6,4},{5,7},{7,5},{8,10},{10,8},{9,1... | collective-permute-start | bytes 7864328 | tf_op jit(solution)/shard_map/ppermute | solution.py:275
  2.9 23.3 %copy-start.11 = (s32[8]{0:T(128)S(1)}, s32[8]{0:T(128)}, u32[]{:S(2)}) copy-start(s32[8]{0:T(128)} %param.11) | copy-start | bytes 100
  2.9 23.3 %copy-start.12 = (s32[16,1]{0,1:T(1,128)S(1)}, s32[16,1]{0,1:T(1,128)}, u32[]{:S(2)}) copy-start(s32[16,1]{0,1:T(1,128)} %param.10) | copy-start | bytes 196
  2.9 42.4 %copy-start.1 = (bf16[2,256,2048]{2,1,0:T(8,128)(2,1)S(1)}, bf16[2,256,2048]{2,1,0:T(8,128)(2,1)}, u32[]{:S(2)}) copy-start(bf16[2,256,2048]{2,1,0:T(8,128)(2,1)} %param.8) | copy-start | bytes 6291460
  4.2 21.5 %collective-permute-start = (bf16[64,2560]{1,0:T(8,128)(2,1)S(1)}, bf16[64,2560]{1,0:T(8,128)(2,1)S(1)}, u32[]{:S(2)}, u32[]{:S(2)}) collective-permute-start(bf16[64,2560]{1,0:T(8,128)(2,1)S(1)} %get-tuple-element.47), channel_id=1, source_target_pairs={{0,12},{4,0},{8,4},{12,8},{1,13},{5,1},{9,5},{13,9},{2,14},{6,2},{... | collective-permute-start | bytes 983048 | tf_op jit(solution)/shard_map/ppermute | solution.py:272
  7.9 14.7 %collective-permute-start.2 = (bf16[64,2560]{1,0:T(8,128)(2,1)S(1)}, bf16[64,2560]{1,0:T(8,128)(2,1)}, u32[]{:S(2)}, u32[]{:S(2)}) collective-permute-start(bf16[64,2560]{1,0:T(8,128)(2,1)S(1)} %get-tuple-element.47), channel_id=1, source_target_pairs={{0,4},{4,8},{8,12},{12,0},{1,5},{5,9},{9,13},{13,1},{2,6},{6,10},{... | collective-permute-start | bytes 983048 | tf_op jit(solution)/shard_map/ppermute | solution.py:272
  22.6 19.8 %collective-permute-start.3 = (bf16[72,2560]{1,0:T(8,128)(2,1)}, bf16[72,2560]{1,0:T(8,128)(2,1)S(1)}, u32[]{:S(2)}, u32[]{:S(2)}) collective-permute-start(bf16[72,2560]{1,0:T(8,128)(2,1)} %pad_maximum_fusion), channel_id=1, source_target_pairs={{0,4},{4,8},{8,12},{12,0},{1,5},{5,9},{9,13},{13,1},{2,6},{6,10},{... | collective-permute-start | bytes 1105928 | tf_op jit(solution)/shard_map/ppermute | solution.py:272
  24.2 19.7 %collective-permute-start.6 = (bf16[64,2560]{1,0:T(8,128)(2,1)}, bf16[64,2560]{1,0:T(8,128)(2,1)S(1)}, u32[]{:S(2)}, u32[]{:S(2)}) collective-permute-start(bf16[64,2560]{1,0:T(8,128)(2,1)} %collective-permute-done.2.refs_3_), channel_id=1, source_target_pairs={{0,16},{16,0},{1,17},{17,1},{2,18},{18,2},{3,19},{19,3},{4,20},{20... | collective-permute-start | bytes 983048 | tf_op jit(solution)/shard_map/ppermute | solution.py:302
  25.7 13.7 %collective-permute-start.7 = (bf16[64,2560]{1,0:T(8,128)(2,1)S(1)}, bf16[64,2560]{1,0:T(8,128)(2,1)S(1)}, u32[]{:S(2)}, u32[]{:S(2)}) collective-permute-start(bf16[64,2560]{1,0:T(8,128)(2,1)S(1)} %collective-permute-done.refs_1_), channel_id=1, source_target_pairs={{0,16},{16,0},{1,17},{17,1},{2,18},{18,2},{3,19},{19,3},{4,20},{20... | collective-permute-start | bytes 983048 | tf_op jit(solution)/shard_map/ppermute | solution.py:302
  26.3 18.4 %collective-permute-start.9 = (bf16[64,2560]{1,0:T(8,128)(2,1)}, bf16[64,2560]{1,0:T(8,128)(2,1)}, u32[]{:S(2)}, u32[]{:S(2)}) collective-permute-start(bf16[64,2560]{1,0:T(8,128)(2,1)} %collective-permute-done.2.refs_3_), channel_id=1, source_target_pairs={{0,4},{4,8},{8,12},{12,0},{1,5},{5,9},{9,13},{13,1},{2,6},{6,10},{... | collective-permute-start | bytes 983048 | tf_op jit(solution)/shard_map/ppermute | solution.py:272
  40.2 11.5 %collective-permute-start.1 = (bf16[72,2560]{1,0:T(8,128)(2,1)}, bf16[72,2560]{1,0:T(8,128)(2,1)S(1)}, u32[]{:S(2)}, u32[]{:S(2)}) collective-permute-start(bf16[72,2560]{1,0:T(8,128)(2,1)} %pad_maximum_fusion), channel_id=1, source_target_pairs={{0,12},{4,0},{8,4},{12,8},{1,13},{5,1},{9,5},{13,9},{2,14},{6,2},{... | collective-permute-start | bytes 1105928 | tf_op jit(solution)/shard_map/ppermute | solution.py:272
  42.4 17.2 %collective-permute-start.8 = (bf16[72,2560]{1,0:T(8,128)(2,1)S(1)}, bf16[72,2560]{1,0:T(8,128)(2,1)}, u32[]{:S(2)}, u32[]{:S(2)}) collective-permute-start(bf16[72,2560]{1,0:T(8,128)(2,1)S(1)} %collective-permute-done.3.refs_4_), channel_id=1, source_target_pairs={{0,16},{16,0},{1,17},{17,1},{2,18},{18,2},{3,19},{19,3},{4,20},{20... | collective-permute-start | bytes 1105928 | tf_op jit(solution)/shard_map/ppermute | solution.py:302
  44.7 14.9 %collective-permute-start.4 = (bf16[72,2560]{1,0:T(8,128)(2,1)S(1)}, bf16[72,2560]{1,0:T(8,128)(2,1)S(1)}, u32[]{:S(2)}, u32[]{:S(2)}) collective-permute-start(bf16[72,2560]{1,0:T(8,128)(2,1)S(1)} %collective-permute-done.3.refs_4_), channel_id=1, source_target_pairs={{0,4},{4,8},{8,12},{12,0},{1,5},{5,9},{9,13},{13,1},{2,6},{6,10},{... | collective-permute-start | bytes 1105928 | tf_op jit(solution)/shard_map/ppermute | solution.py:272
  44.7 13.3 %collective-permute-start.10 = (bf16[64,2560]{1,0:T(8,128)(2,1)}, bf16[64,2560]{1,0:T(8,128)(2,1)S(1)}, u32[]{:S(2)}, u32[]{:S(2)}) collective-permute-start(bf16[64,2560]{1,0:T(8,128)(2,1)} %collective-permute-done.9.refs_2_), channel_id=1, source_target_pairs={{0,16},{16,0},{1,17},{17,1},{2,18},{18,2},{3,19},{19,3},{4,20},{20... | collective-permute-start | bytes 983048 | tf_op jit(solution)/shard_map/ppermute | solution.py:302
  45.3 14.8 %copy-start.8 = (bf16[8,2560]{1,0:T(8,128)(2,1)S(1)}, bf16[8,2560]{1,0:T(8,128)(2,1)}, u32[]{:S(2)}) copy-start(bf16[8,2560]{1,0:T(8,128)(2,1)} %copy-done.7) | copy-start | bytes 122884
  45.3 23.7 %copy-start = (bf16[2,256,2560]{2,1,0:T(8,128)(2,1)S(1)}, bf16[2,256,2560]{2,1,0:T(8,128)(2,1)}, u32[]{:S(2)}) copy-start(bf16[2,256,2560]{2,1,0:T(8,128)(2,1)} %param.7) | copy-start | bytes 7864324
  58.1 11.0 %collective-permute-start.11 = (bf16[72,2560]{1,0:T(8,128)(2,1)S(1)}, bf16[72,2560]{1,0:T(8,128)(2,1)S(1)}, u32[]{:S(2)}, u32[]{:S(2)}) collective-permute-start(bf16[72,2560]{1,0:T(8,128)(2,1)S(1)} %collective-permute-done.1.refs_2_), channel_id=1, source_target_pairs={{0,16},{16,0},{1,17},{17,1},{2,18},{18,2},{3,19},{19,3},{4,20},{20... | collective-permute-start | bytes 1105928 | tf_op jit(solution)/shard_map/ppermute | solution.py:302
  59.6 19.8 %collective-permute-start.12 = (bf16[72,2560]{1,0:T(8,128)(2,1)S(1)}, bf16[72,2560]{1,0:T(8,128)(2,1)S(1)}, u32[]{:S(2)}, u32[]{:S(2)}) collective-permute-start(bf16[72,2560]{1,0:T(8,128)(2,1)S(1)} %collective-permute-done.4.refs_3_), channel_id=1, source_target_pairs={{0,16},{16,0},{1,17},{17,1},{2,18},{18,2},{3,19},{19,3},{4,20},{20... | collective-permute-start | bytes 1105928 | tf_op jit(solution)/shard_map/ppermute | solution.py:302
  60.2 26.0 %collective-permute-start.17 = (bf16[576,512]{1,0:T(8,128)(2,1)S(1)}, bf16[576,512]{1,0:T(8,128)(2,1)S(1)}, u32[]{:S(2)}, u32[]{:S(2)}) collective-permute-start(bf16[576,512]{1,0:T(8,128)(2,1)S(1)} %constant_dynamic-update-slice_fusion.16), channel_id=1, source_target_pairs={{0,2},{2,0},{1,3},{3,1},{4,6},{6,4},{5,7},{7,5},{8,10},{10,8},{9,1... | collective-permute-start | bytes 1769480 | tf_op jit(solution)/shard_map/ppermute | solution.py:363
  69.0 1.3 %copy-start.2 = (bf16[256,2560]{1,0:T(8,128)(2,1)S(1)}, bf16[256,2560]{1,0:T(8,128)(2,1)}, u32[]{:S(2)}) copy-start(bf16[256,2560]{1,0:T(8,128)(2,1)} %refs_0_.1) | copy-start | bytes 3932164
  79.4 3.7 %copy-start.10 = (s32[4]{0:T(128)S(1)}, s32[4]{0:T(128)}, u32[]{:S(2)}) copy-start(s32[4]{0:T(128)} %constant.99.clone) | copy-start | bytes 52
  82.0 2.0 %collective-permute-start.16 = (f32[2,512,128]{2,1,0:T(8,128)S(1)}, f32[2,512,128]{2,1,0:T(8,128)S(1)}, u32[]{:S(2)}, u32[]{:S(2)}) collective-permute-start(f32[2,512,128]{2,1,0:T(8,128)S(1)} %get-tuple-element.39), channel_id=1, source_target_pairs={{0,1},{1,0},{2,3},{3,2},{4,5},{5,4},{6,7},{7,6},{8,9},{9,8},{10,11... | collective-permute-start | bytes 1572872 | tf_op jit(solution)/shard_map/ppermute | solution.py:329
  82.1 2.6 %collective-permute-start.13 = (f32[2,512,128]{2,1,0:T(8,128)S(1)}, f32[2,512,128]{2,1,0:T(8,128)S(1)}, u32[]{:S(2)}, u32[]{:S(2)}) collective-permute-start(f32[2,512,128]{2,1,0:T(8,128)S(1)} %get-tuple-element.36), channel_id=1, source_target_pairs={{0,1},{1,0},{2,3},{3,2},{4,5},{5,4},{6,7},{7,6},{8,9},{9,8},{10,11... | collective-permute-start | bytes 1572872 | tf_op jit(solution)/shard_map/ppermute | solution.py:329
  82.6 2.9 %collective-permute-start.14 = (f32[2,512,128]{2,1,0:T(8,128)S(1)}, f32[2,512,128]{2,1,0:T(8,128)S(1)}, u32[]{:S(2)}, u32[]{:S(2)}) collective-permute-start(f32[2,512,128]{2,1,0:T(8,128)S(1)} %get-tuple-element.37), channel_id=1, source_target_pairs={{0,1},{1,0},{2,3},{3,2},{4,5},{5,4},{6,7},{7,6},{8,9},{9,8},{10,11... | collective-permute-start | bytes 1572872 | tf_op jit(solution)/shard_map/ppermute | solution.py:329
  82.6 3.6 %collective-permute-start.15 = (f32[2,512,128]{2,1,0:T(8,128)S(1)}, f32[2,512,128]{2,1,0:T(8,128)S(1)}, u32[]{:S(2)}, u32[]{:S(2)}) collective-permute-start(f32[2,512,128]{2,1,0:T(8,128)S(1)} %get-tuple-element.38), channel_id=1, source_target_pairs={{0,1},{1,0},{2,3},{3,2},{4,5},{5,4},{6,7},{7,6},{8,9},{9,8},{10,11... | collective-permute-start | bytes 1572872 | tf_op jit(solution)/shard_map/ppermute | solution.py:329
  88.3 6.9 %collective-permute-start.18 = (f32[1,136,128]{2,1,0:T(8,128)S(1)}, f32[1,136,128]{2,1,0:T(8,128)S(1)}, u32[]{:S(2)}, u32[]{:S(2)}) collective-permute-start(f32[1,136,128]{2,1,0:T(8,128)S(1)} %get-tuple-element.51), channel_id=1, source_target_pairs={{0,4},{4,8},{8,12},{12,0},{1,5},{5,9},{9,13},{13,1},{2,6},{6,10},{... | collective-permute-start | bytes 208904 | tf_op jit(solution)/shard_map/ppermute | solution.py:272
  88.3 8.9 %collective-permute-start.19 = (f32[1,136,128]{2,1,0:T(8,128)S(1)}, f32[1,136,128]{2,1,0:T(8,128)S(1)}, u32[]{:S(2)}, u32[]{:S(2)}) collective-permute-start(f32[1,136,128]{2,1,0:T(8,128)S(1)} %get-tuple-element.50), channel_id=1, source_target_pairs={{0,8},{4,12},{8,0},{12,4},{1,9},{5,13},{9,1},{13,5},{2,10},{6,14},... | collective-permute-start | bytes 208904 | tf_op jit(solution)/shard_map/ppermute | solution.py:272
  88.6 8.6 %collective-permute-start.20 = (f32[1,136,128]{2,1,0:T(8,128)S(1)}, f32[1,136,128]{2,1,0:T(8,128)S(1)}, u32[]{:S(2)}, u32[]{:S(2)}) collective-permute-start(f32[1,136,128]{2,1,0:T(8,128)S(1)} %get-tuple-element.49), channel_id=1, source_target_pairs={{0,12},{4,0},{8,4},{12,8},{1,13},{5,1},{9,5},{13,9},{2,14},{6,2},{... | collective-permute-start | bytes 208904 | tf_op jit(solution)/shard_map/ppermute | solution.py:272
  97.5 3.9 %collective-permute-start.22 = (bf16[1,16,512]{2,1,0:T(8,128)(2,1)S(1)}, bf16[1,16,512]{2,1,0:T(8,128)(2,1)S(1)}, u32[]{:S(2)}, u32[]{:S(2)}) collective-permute-start(bf16[1,16,512]{2,1,0:T(8,128)(2,1)S(1)} %get-tuple-element.77), channel_id=1, source_target_pairs={{0,2},{2,0},{1,3},{3,1},{4,6},{6,4},{5,7},{7,5},{8,10},{10,8},{9,1... | collective-permute-start | bytes 49160 | tf_op jit(solution)/shard_map/ppermute | solution.py:390
  98.1 3.3 %collective-permute-start.23 = (bf16[1,16,512]{2,1,0:T(8,128)(2,1)S(1)}, bf16[1,16,512]{2,1,0:T(8,128)(2,1)S(1)}, u32[]{:S(2)}, u32[]{:S(2)}) collective-permute-start(bf16[1,16,512]{2,1,0:T(8,128)(2,1)S(1)} %get-tuple-element.77), channel_id=1, source_target_pairs={{0,3},{3,0},{1,2},{2,1},{4,7},{7,4},{5,6},{6,5},{8,11},{11,8},{9,1... | collective-permute-start | bytes 49160 | tf_op jit(solution)/shard_map/ppermute | solution.py:391
  98.1 2.4 %collective-permute-start.21 = (bf16[1,16,512]{2,1,0:T(8,128)(2,1)S(1)}, bf16[1,16,512]{2,1,0:T(8,128)(2,1)S(1)}, u32[]{:S(2)}, u32[]{:S(2)}) collective-permute-start(bf16[1,16,512]{2,1,0:T(8,128)(2,1)S(1)} %get-tuple-element.78.mine_ref), channel_id=1, source_target_pairs={{0,1},{1,0},{2,3},{3,2},{4,5},{5,4},{6,7},{7,6},{8,9},{9,8},{10,11... | collective-permute-start | bytes 49160 | tf_op jit(solution)/shard_map/ppermute | solution.py:389
  (5 other events, 4.2 us)

commit v13 on v5

--- a/solution.py
+++ b/solution.py
@@ -255,12 +255,11 @@
             for first, length in zip((0, lengths[0]), lengths)
         ]
         sent[1] = jnp.concatenate([sent[1], with_rows(queries, units)], axis=0)
-        below = [shifted(sent[0], 1)]
-        sent = [after(piece, below) for piece in sent]
-        below.append(shifted(sent[1], 1))
-        above = [shifted(sent[0], -1)]
-        above.append(shifted(after(sent[1], above), -1))
-        opposite = [shifted(after(below[0], below[1:]), 1), shifted(below[1], 1)]
+        below, above = [], []
+        for at in range(2):
+            below.append(shifted(after(sent[at], below[-1:]), 1))
+            above.append(shifted(after(sent[at], above[-1:] or below[:1]), -1))
+        opposite = [jnp.concatenate([shifted(after(below[0], below[1:]), 1), shifted(below[1], 1)], axis=0)]
         around = [from_rows(piece[-1][-8:], queries.shape) for piece in (above, opposite, below)]
         queries = jnp.concatenate([queries] + around, axis=0)
         swapped = []
@@ -268,29 +267,34 @@
             swapped.append(lax.ppermute(after(piece, swapped[max(at - 2, 0) : max(at - 1, 0)]), "groups", SWAP))
         weights = [down_weight] + above + swapped[1:4:2] + below + swapped[0:4:2] + opposite + swapped[4:]
         flags = jnp.stack([core, (group == core).astype(core.dtype)])
-        blocks_of = [[(1, shard)]] + [list(zip(range(at, at + 4), 2 * lengths)) for at in (2, 6, 10)]
+        blocks_of = [[(2, shard)], list(zip(range(3, 7), 2 * lengths)), list(zip(range(7, 11), 2 * lengths))]
         spots = lax.rem(high + jnp.array([0, 1, 3, 2], jnp.int32), highs)
         spots = jnp.stack([(spots * 2 + side) * stride + core * span, spots * span])
         own_residual = passages
 
-        flags = after(flags, swapped[4:5])
         kept, *away = project(
-            flags, [hidden] + weights[:9], [(0, blocks_of[at]) for at in range(3)], [3], half, 1, "project_own"
+            flags,
+            [hidden, partner_hidden] + weights[:9],
+            [(source, blocks_of[at]) for source in range(2) for at in range(3)],
+            [2, 2, 2],
+            half,
+            24 * rows * half * units,
+            "project_near",
         )
         flags, kept, *away = lax.optimization_barrier((flags, kept, *away))
         late_kept, *late_away = project(
             flags,
-            [hidden] + weights + [partner_hidden],
-            [(14, blocks_of[at]) for at in range(4)] + [(0, blocks_of[3])],
-            [2, 2, 1],
+            [hidden, partner_hidden] + weights[9:],
+            [(source, [(2, half), (3, half)]) for source in range(2)],
+            [2],
             half,
             1,
-            "project_rest",
+            "project_far",
         )
         others = [lax.ppermute(piece, "mp", SWAP) for piece in away + late_away]
         summands = [kept, late_kept] + others
-        pieces = [(0, (0, at), (2, at), at) for at in range(3)] + [(0, (1, 4), (5, 0), 3)]
-        pieces += [(1, (1, at), (3 + at // 2, at % 2), at) for at in range(4)]
+        pieces = [(at // 3, (0, at), (2 + at // 2, at % 2), at % 3) for at in range(6)]
+        pieces += [(source, (1, source), (5, source), 3) for source in range(2)]
         origin = high
     else:
         queries = lax.all_gather(queries, ("high", "low"), axis=0, tiled=True)

time: 112 us -> 95.5 us (0.85)
  local copies, waits for them, and re-layouts: 14.3 us -> 1.62 us
  waiting for transfers between devices: 57 us -> 52.4 us
  starting transfers between devices: 24.1 us -> 27.8 us
  Pallas kernels: 14.3 us -> 12.7 us
  other arithmetic: 2.04 us -> 0.51 us
    unnamed x52 -> x17, local copies, waits for them, and re-layouts: 10.2 us -> 0.06 us
    ppermute x6 -> x5, waiting for transfers between devices: 15.6 us -> 9.16 us  [body(): lax.ppermute(after(piece, swapped[max(at - 2, 0):max(at - 1, 0)]), 'group...]
    ppermute x1, waiting for transfers between devices: 0.01 us -> 4.99 us  [body(): partner_hidden = lax.ppermute(hidden, 'side', SWAP)]
    ppermute x9, starting transfers between devices: 12.7 us -> 15.9 us  [shifted(): lax.ppermute(array, 'high', [(at, (at + shift) % highs) for at in range(h...]
    ppermute x9, waiting for transfers between devices: 36.8 us -> 34.5 us  [shifted(): lax.ppermute(array, 'high', [(at, (at + shift) % highs) for at in range(h...]
    dynamic_slice x2, local copies, waits for them, and re-layouts: 2.08 us -> 0.15 us  [features(): lax.dynamic_slice_in_dim(array, start, span, axis=array.ndim - 1)]
    ppermute x1, starting transfers between devices: 0.01 us -> 1.56 us  [body(): partner = lax.ppermute(leaving, 'side', SWAP)]
    ppermute x1, waiting for transfers between devices: 1.71 us -> 0.24 us  [body(): partner = lax.ppermute(leaving, 'side', SWAP)]
  transfers between devices with their start and end apart: 24 -> 23, of which waited for: 14 -> 15; matrix products, arithmetic and copies ran while one was open for 4% -> 1% of each run, Pallas kernels for 9% -> 10%
where the time goes in v13:
time: 95.5 us; the launch traced here: 95.3 us
  waiting for transfers between devices  52.4 us (55%)
  starting transfers between devices  27.8 us (29%)
  Pallas kernels  12.7 us (13%)
  local copies, waits for them, and re-layouts  1.62 us (2%)
    ppermute x9, waiting for transfers between devices, shifted(): lax.ppermute(array, 'high', [(at, (at + shift) % highs) for at in range(h...  34.5 us
    ppermute x9, starting transfers between devices, shifted(): lax.ppermute(array, 'high', [(at, (at + shift) % highs) for at in range(h...  15.9 us
    pallas_call x2, Pallas kernels, project(): pl.pallas_call(functools.partial(project_kernel, jobs=jobs, sends=sends),...  9.31 us
    ppermute x5, waiting for transfers between devices, body(): lax.ppermute(after(piece, swapped[max(at - 2, 0):max(at - 1, 0)]), 'group...  9.16 us
    ppermute x5, starting transfers between devices, body(): lax.ppermute(after(piece, swapped[max(at - 2, 0):max(at - 1, 0)]), 'group...  5.92 us
    ppermute x1, waiting for transfers between devices, body(): partner_hidden = lax.ppermute(hidden, 'side', SWAP)  4.99 us
    pallas_call x1, Pallas kernels, body(): pl.pallas_call(functools.partial(attend_kernel, pieces=pieces), out_shape...  2.01 us
  transfers between devices with their start and end apart: 23, of which 15 were waited for; matrix products, arithmetic and copies ran while one was open for 1% of the time, Pallas kernels for 10%

profile of v13, /device:TPU:0, one launch (start us, length us, event | category | flops | bytes accessed | tf_op | source)
XLA Modules:
  0.0 95.3 jit_solution(10772685281888116593)
XLA Ops:
  0.0 1.3 %constant_dynamic-slice_fusion.4 = (bf16[64,2560]{1,0:T(8,128)(2,1)S(1)}, bf16[64,2560]{1,0:T(8,128)(2,1)S(1)}) fusion(bf16[256,2560]{1,0:T(8,128)(2,1)} %refs_2_.1, s32[]{:T(128)S(6)} %select_n.73, s32[]{:T(128)S(6)} %select_n.72), kind=kLoop, calls=%fused_computation.24 | loop fusion | bytes 1310728 | tf_op jit(solution)/shard_map/dynamic_slice | solution.py:254
  1.3 3.1 %collective-permute-start = (bf16[64,2560]{1,0:T(8,128)(2,1)S(1)}, bf16[64,2560]{1,0:T(8,128)(2,1)S(1)}, u32[]{:S(2)}, u32[]{:S(2)}) collective-permute-start(bf16[64,2560]{1,0:T(8,128)(2,1)S(1)} %get-tuple-element.23), channel_id=1, source_target_pairs={{0,4},{4,8},{8,12},{12,0},{1,5},{5,9},{9,13},{13,1},{2,6},{6,10},{... | collective-permute-start | bytes 983048 | tf_op jit(solution)/shard_map/ppermute | solution.py:242
  4.4 1.5 %collective-permute-start.5 = (bf16[512,2560]{1,0:T(8,128)(2,1)}, bf16[512,2560]{1,0:T(8,128)(2,1)}, u32[]{:S(2)}, u32[]{:S(2)}) collective-permute-start(bf16[512,2560]{1,0:T(8,128)(2,1)} %bitcast.21), channel_id=1, source_target_pairs={{0,2},{2,0},{1,3},{3,1},{4,6},{6,4},{5,7},{7,5},{8,10},{10,8},{9,1... | collective-permute-start | bytes 7864328 | tf_op jit(solution)/shard_map/ppermute | solution.py:245
  6.1 8.0 %collective-permute-done.refs_7_ = bf16[64,2560]{1,0:T(8,128)(2,1)S(1)} collective-permute-done((bf16[64,2560]{1,0:T(8,128)(2,1)S(1)}, bf16[64,2560]{1,0:T(8,128)(2,1)S(1)}, u32[]{:S(2)}, u32[]{:S(2)}) %collective-permute-start) | collective-permute-done | bytes 327712 | tf_op jit(solution)/shard_map/ppermute | solution.py:242
  14.1 3.8 %collective-permute-start.1 = (bf16[64,2560]{1,0:T(8,128)(2,1)}, bf16[64,2560]{1,0:T(8,128)(2,1)S(1)}, u32[]{:S(2)}, u32[]{:S(2)}) collective-permute-start(bf16[64,2560]{1,0:T(8,128)(2,1)} %copy-done.3), channel_id=1, source_target_pairs={{0,12},{4,0},{8,4},{12,8},{1,13},{5,1},{9,5},{13,9},{2,14},{6,2},{... | collective-permute-start | bytes 983048 | tf_op jit(solution)/shard_map/ppermute | solution.py:242
  18.0 1.5 %collective-permute-start.8 = (bf16[64,2560]{1,0:T(8,128)(2,1)S(1)}, bf16[64,2560]{1,0:T(8,128)(2,1)S(1)}, u32[]{:S(2)}, u32[]{:S(2)}) collective-permute-start(bf16[64,2560]{1,0:T(8,128)(2,1)S(1)} %collective-permute-done.refs_7_), channel_id=1, source_target_pairs={{0,16},{16,0},{1,17},{17,1},{2,18},{18,2},{3,19},{19,3},{4,20},{20... | collective-permute-start | bytes 983048 | tf_op jit(solution)/shard_map/ppermute | solution.py:267
  19.8 11.4 %collective-permute-done.1.refs_3_ = bf16[64,2560]{1,0:T(8,128)(2,1)S(1)} collective-permute-done((bf16[64,2560]{1,0:T(8,128)(2,1)}, bf16[64,2560]{1,0:T(8,128)(2,1)S(1)}, u32[]{:S(2)}, u32[]{:S(2)}) %collective-permute-start.1) | collective-permute-done | bytes 327712 | tf_op jit(solution)/shard_map/ppermute | solution.py:242
  31.1 1.9 %collective-permute-start.2 = (bf16[72,2560]{1,0:T(8,128)(2,1)S(1)}, bf16[72,2560]{1,0:T(8,128)(2,1)S(1)}, u32[]{:S(2)}, u32[]{:S(2)}) collective-permute-start(bf16[72,2560]{1,0:T(8,128)(2,1)S(1)} %pad_maximum_fusion.1), channel_id=1, source_target_pairs={{0,12},{4,0},{8,4},{12,8},{1,13},{5,1},{9,5},{13,9},{2,14},{6,2},{... | collective-permute-start | bytes 1105928 | tf_op jit(solution)/shard_map/ppermute | solution.py:242
  33.1 1.3 %collective-permute-start.6 = (bf16[64,2560]{1,0:T(8,128)(2,1)S(1)}, bf16[64,2560]{1,0:T(8,128)(2,1)S(1)}, u32[]{:S(2)}, u32[]{:S(2)}) collective-permute-start(bf16[64,2560]{1,0:T(8,128)(2,1)S(1)} %collective-permute-done.1.refs_3_), channel_id=1, source_target_pairs={{0,16},{16,0},{1,17},{17,1},{2,18},{18,2},{3,19},{19,3},{4,20},{20... | collective-permute-start | bytes 983048 | tf_op jit(solution)/shard_map/ppermute | solution.py:267
  34.4 0.8 collective-permute-start.9
  35.3 8.4 %collective-permute-done.6.refs_5_ = bf16[64,2560]{1,0:T(8,128)(2,1)S(1)} collective-permute-done((bf16[64,2560]{1,0:T(8,128)(2,1)S(1)}, bf16[64,2560]{1,0:T(8,128)(2,1)S(1)}, u32[]{:S(2)}, u32[]{:S(2)}) %collective-permute-start.6) | collective-permute-done | bytes 327712 | tf_op jit(solution)/shard_map/ppermute | solution.py:267
  43.9 1.3 %collective-permute-start.7 = (bf16[72,2560]{1,0:T(8,128)(2,1)S(1)}, bf16[72,2560]{1,0:T(8,128)(2,1)S(1)}, u32[]{:S(2)}, u32[]{:S(2)}) collective-permute-start(bf16[72,2560]{1,0:T(8,128)(2,1)S(1)} %collective-permute-done.2.refs_4_), channel_id=1, source_target_pairs={{0,16},{16,0},{1,17},{17,1},{2,18},{18,2},{3,19},{19,3},{4,20},{20... | collective-permute-start | bytes 1105928 | tf_op jit(solution)/shard_map/ppermute | solution.py:267
  45.2 6.2 %collective-permute-done.10 = bf16[64,2560]{1,0:T(8,128)(2,1)S(1)} collective-permute-done((bf16[64,2560]{1,0:T(8,128)(2,1)S(1)}, bf16[64,2560]{1,0:T(8,128)(2,1)S(1)}, u32[]{:S(2)}, u32[]{:S(2)}) %collective-permute-start.10) | collective-permute-done | bytes 327712 | tf_op jit(solution)/shard_map/ppermute | solution.py:242
  51.4 5.3 %collective-permute-done.4 = bf16[72,2560]{1,0:T(8,128)(2,1)S(1)} collective-permute-done((bf16[72,2560]{1,0:T(8,128)(2,1)S(1)}, bf16[72,2560]{1,0:T(8,128)(2,1)S(1)}, u32[]{:S(2)}, u32[]{:S(2)}) %collective-permute-start.4) | collective-permute-done | bytes 368672 | tf_op jit(solution)/shard_map/ppermute | solution.py:242
  56.7 1.1 %collective-permute-start.11 = (bf16[136,2560]{1,0:T(8,128)(2,1)S(1)}, bf16[136,2560]{1,0:T(8,128)(2,1)S(1)}, u32[]{:S(2)}, u32[]{:S(2)}) collective-permute-start(bf16[136,2560]{1,0:T(8,128)(2,1)S(1)} %constant_dynamic-update-slice_fusion.refs_2_), channel_id=1, source_target_pairs={{0,16},{16,0},{1,17},{17,1},{2,18},{18,2},{3,19},{19,3},{4,20},{20... | collective-permute-start | bytes 2088968 | tf_op jit(solution)/shard_map/ppermute | solution.py:267
  57.9 1.6 %collective-permute-start.16 = (bf16[576,512]{1,0:T(8,128)(2,1)S(1)}, bf16[576,512]{1,0:T(8,128)(2,1)S(1)}, u32[]{:S(2)}, u32[]{:S(2)}) collective-permute-start(bf16[576,512]{1,0:T(8,128)(2,1)S(1)} %pad_maximum_fusion), channel_id=1, source_target_pairs={{0,2},{2,0},{1,3},{3,1},{4,6},{6,4},{5,7},{7,5},{8,10},{10,8},{9,1... | collective-permute-start | bytes 1769480 | tf_op jit(solution)/shard_map/ppermute | solution.py:328
  59.5 5.0 %collective-permute-done.5.refs_1_ = bf16[512,2560]{1,0:T(8,128)(2,1)} collective-permute-done((bf16[512,2560]{1,0:T(8,128)(2,1)}, bf16[512,2560]{1,0:T(8,128)(2,1)}, u32[]{:S(2)}, u32[]{:S(2)}) %collective-permute-start.5) | collective-permute-done | bytes 2621472 | tf_op jit(solution)/shard_map/ppermute | solution.py:245
  64.5 6.0 %project_near.1 = (f32[6,512,128]{2,1,0:T(8,128)S(1)}, f32[2,512,128]{2,1,0:T(8,128)S(1)}, f32[2,512,128]{2,1,0:T(8,128)S(1)}, f32[2,512,128]{2,1,0:T(8,128)S(1)}) custom-call(s32[2]{0:T(128)S(1)} %pad_add_fusion.3.flag_ref, bf16[512,2560]{1,0:T(8,128)(2,1)S(1)} %bitcast.22, bf16[512,2560]{1,0:T(8,128)(2,1)} %collective-permute-done.5.refs_1_, ...), custom_call_target="tpu_custom_call" | custom-call | flops 4026531840 | bytes 1 | tf_op jit(solution)/shard_map/project_near/pallas_call | solution.py:190
  71.2 0.7 collective-permute-done.11.refs_3_
  71.9 3.3 %project_far.1 = (f32[2,512,128]{2,1,0:T(8,128)S(1)}, f32[2,512,128]{2,1,0:T(8,128)S(1)}) custom-call(s32[2]{0:T(128)S(1)} %pad_add_fusion.3.flag_ref, bf16[512,2560]{1,0:T(8,128)(2,1)S(1)} %bitcast.23, bf16[512,2560]{1,0:T(8,128)(2,1)} %collective-permute-done.5.refs_1_, bf16[136,2560]{1,0:T(8,128)(2,1)S(1)} %constant_dynamic-update-slice_fusion.refs_2_, ...), custom_call_target="tpu_custom_call" | custom-call | flops 1 | bytes 1 | tf_op jit(solution)/shard_map/project_far/pallas_call | solution.py:190
  75.6 1.6 %collective-permute-done.15.refs_5_ = f32[2,512,128]{2,1,0:T(8,128)S(1)} collective-permute-done((f32[2,512,128]{2,1,0:T(8,128)S(1)}, f32[2,512,128]{2,1,0:T(8,128)S(1)}, u32[]{:S(2)}, u32[]{:S(2)}) %collective-permute-start.15) | collective-permute-done | bytes 524320 | tf_op jit(solution)/shard_map/ppermute | solution.py:294
  77.2 2.0 %attend.1 = f32[4,136,128]{2,1,0:T(8,128)S(1)} custom-call(s32[4]{0:T(128)S(1)} %pad_add_fusion.2.place_ref, s32[2,4]{1,0:T(2,128)S(1)} %pad_add_fusion.spot_ref, bf16[4,16,512]{2,1,0:T(8,128)(2,1)S(1)} %get-tuple-element.66.query_ref, f32[6,512,128]{2,1,0:T(8,128)S(1)} %get-tuple-element.32.refs_0_, f32[2,512,128]{2,1,0:T(8,128)S(1)} %get-tuple-element.36.refs_1_, ...), custom_call_target="tpu_custom_call" | custom-call | tf_op jit(solution)/shard_map/attend/pallas_call | solution.py:331
  79.2 1.8 %collective-permute-start.17 = (f32[1,136,128]{2,1,0:T(8,128)S(1)}, f32[1,136,128]{2,1,0:T(8,128)S(1)}, u32[]{:S(2)}, u32[]{:S(2)}) collective-permute-start(f32[1,136,128]{2,1,0:T(8,128)S(1)} %get-tuple-element.63), channel_id=1, source_target_pairs={{0,4},{4,8},{8,12},{12,0},{1,5},{5,9},{9,13},{13,1},{2,6},{6,10},{... | collective-permute-start | bytes 208904 | tf_op jit(solution)/shard_map/ppermute | solution.py:242
  81.0 3.5 %collective-permute-start.18 = (f32[1,136,128]{2,1,0:T(8,128)S(1)}, f32[1,136,128]{2,1,0:T(8,128)S(1)}, u32[]{:S(2)}, u32[]{:S(2)}) collective-permute-start(f32[1,136,128]{2,1,0:T(8,128)S(1)} %get-tuple-element.62), channel_id=1, source_target_pairs={{0,8},{4,12},{8,0},{12,4},{1,9},{5,13},{9,1},{13,5},{2,10},{6,14},... | collective-permute-start | bytes 208904 | tf_op jit(solution)/shard_map/ppermute | solution.py:242
  84.5 1.5 %collective-permute-start.19 = (f32[1,136,128]{2,1,0:T(8,128)S(1)}, f32[1,136,128]{2,1,0:T(8,128)S(1)}, u32[]{:S(2)}, u32[]{:S(2)}) collective-permute-start(f32[1,136,128]{2,1,0:T(8,128)S(1)} %get-tuple-element.61), channel_id=1, source_target_pairs={{0,12},{4,0},{8,4},{12,8},{1,13},{5,1},{9,5},{13,9},{2,14},{6,2},{... | collective-permute-start | bytes 208904 | tf_op jit(solution)/shard_map/ppermute | solution.py:242
  86.0 0.5 collective-permute-done.17.refs_1_
  86.5 2.9 %collective-permute-done.18.refs_2_ = f32[1,136,128]{2,1,0:T(8,128)S(1)} collective-permute-done((f32[1,136,128]{2,1,0:T(8,128)S(1)}, f32[1,136,128]{2,1,0:T(8,128)S(1)}, u32[]{:S(2)}, u32[]{:S(2)}) %collective-permute-start.18) | collective-permute-done | bytes 69664 | tf_op jit(solution)/shard_map/ppermute | solution.py:242
  89.9 1.0 %collective-permute-start.21 = (bf16[1,16,512]{2,1,0:T(8,128)(2,1)S(1)}, bf16[1,16,512]{2,1,0:T(8,128)(2,1)S(1)}, u32[]{:S(2)}, u32[]{:S(2)}) collective-permute-start(bf16[1,16,512]{2,1,0:T(8,128)(2,1)S(1)} %get-tuple-element.75), channel_id=1, source_target_pairs={{0,2},{2,0},{1,3},{3,1},{4,6},{6,4},{5,7},{7,5},{8,10},{10,8},{9,1... | collective-permute-start | bytes 49160 | tf_op jit(solution)/shard_map/ppermute | solution.py:355
  91.1 1.0 %collective-permute-start.20 = (bf16[1,16,512]{2,1,0:T(8,128)(2,1)S(1)}, bf16[1,16,512]{2,1,0:T(8,128)(2,1)S(1)}, u32[]{:S(2)}, u32[]{:S(2)}) collective-permute-start(bf16[1,16,512]{2,1,0:T(8,128)(2,1)S(1)} %get-tuple-element.76.mine_ref), channel_id=1, source_target_pairs={{0,1},{1,0},{2,3},{3,2},{4,5},{5,4},{6,7},{7,6},{8,9},{9,8},{10,11... | collective-permute-start | bytes 49160 | tf_op jit(solution)/shard_map/ppermute | solution.py:354
  92.2 0.8 collective-permute-done.20.core_ref
  93.0 0.8 collective-permute-done.21.side_ref
  94.1 1.2 %assemble.1 = bf16[1,16,2048]{2,1,0:T(8,128)(2,1)} custom-call(s32[2]{0:T(128)S(1)} %pad_add_fusion.1.flag_ref, bf16[1,16,512]{2,1,0:T(8,128)(2,1)S(1)} %get-tuple-element.76.mine_ref, bf16[1,16,512]{2,1,0:T(8,128)(2,1)S(1)} %collective-permute-done.20.core_ref, bf16[1,16,512]{2,1,0:T(8,128)(2,1)S(1)} %collective-permute-done.21.side_ref, ...), custom_call_target="tpu_custom_call" | custom-call | tf_op jit(solution)/shard_map/assemble/pallas_call | solution.py:363
  (65 shorter events, 3.1 us)
Async XLA Ops:
  0.0 5.9 %copy-start.4 = (bf16[1,16,2048]{2,1,0:T(8,128)(2,1)S(1)}, bf16[1,16,2048]{2,1,0:T(8,128)(2,1)}, u32[]{:S(2)}) copy-start(bf16[1,16,2048]{2,1,0:T(8,128)(2,1)} %param.12) | copy-start | bytes 196612
  0.0 5.9 %copy-start.6 = (s32[8]{0:T(128)S(1)}, s32[8]{0:T(128)}, u32[]{:S(2)}) copy-start(s32[8]{0:T(128)} %param.11) | copy-start | bytes 100
  0.0 5.9 %copy-start.7 = (s32[16,1]{0,1:T(1,128)S(1)}, s32[16,1]{0,1:T(1,128)}, u32[]{:S(2)}) copy-start(s32[16,1]{0,1:T(1,128)} %param.10) | copy-start | bytes 196
  0.0 19.6 %copy-start = (bf16[2,256,2048]{2,1,0:T(8,128)(2,1)S(1)}, bf16[2,256,2048]{2,1,0:T(8,128)(2,1)}, u32[]{:S(2)}) copy-start(bf16[2,256,2048]{2,1,0:T(8,128)(2,1)} %param.8) | copy-start | bytes 6291460
  1.3 4.8 %copy-start.3 = (bf16[64,2560]{1,0:T(8,128)(2,1)}, bf16[64,2560]{1,0:T(8,128)(2,1)S(1)}, u32[]{:S(2)}) copy-start(bf16[64,2560]{1,0:T(8,128)(2,1)S(1)} %get-tuple-element.23) | copy-start | bytes 983044
  1.3 12.8 %collective-permute-start = (bf16[64,2560]{1,0:T(8,128)(2,1)S(1)}, bf16[64,2560]{1,0:T(8,128)(2,1)S(1)}, u32[]{:S(2)}, u32[]{:S(2)}) collective-permute-start(bf16[64,2560]{1,0:T(8,128)(2,1)S(1)} %get-tuple-element.23), channel_id=1, source_target_pairs={{0,4},{4,8},{8,12},{12,0},{1,5},{5,9},{9,13},{13,1},{2,6},{6,10},{... | collective-permute-start | bytes 983048 | tf_op jit(solution)/shard_map/ppermute | solution.py:242
  4.4 60.1 %collective-permute-start.5 = (bf16[512,2560]{1,0:T(8,128)(2,1)}, bf16[512,2560]{1,0:T(8,128)(2,1)}, u32[]{:S(2)}, u32[]{:S(2)}) collective-permute-start(bf16[512,2560]{1,0:T(8,128)(2,1)} %bitcast.21), channel_id=1, source_target_pairs={{0,2},{2,0},{1,3},{3,1},{4,6},{6,4},{5,7},{7,5},{8,10},{10,8},{9,1... | collective-permute-start | bytes 7864328 | tf_op jit(solution)/shard_map/ppermute | solution.py:245
  14.1 20.2 %collective-permute-start.3 = (bf16[72,2560]{1,0:T(8,128)(2,1)S(1)}, bf16[72,2560]{1,0:T(8,128)(2,1)S(1)}, u32[]{:S(2)}, u32[]{:S(2)}) collective-permute-start(bf16[72,2560]{1,0:T(8,128)(2,1)S(1)} %pad_maximum_fusion.1), channel_id=1, source_target_pairs={{0,4},{4,8},{8,12},{12,0},{1,5},{5,9},{9,13},{13,1},{2,6},{6,10},{... | collective-permute-start | bytes 1105928 | tf_op jit(solution)/shard_map/ppermute | solution.py:242
  14.1 17.0 %collective-permute-start.1 = (bf16[64,2560]{1,0:T(8,128)(2,1)}, bf16[64,2560]{1,0:T(8,128)(2,1)S(1)}, u32[]{:S(2)}, u32[]{:S(2)}) collective-permute-start(bf16[64,2560]{1,0:T(8,128)(2,1)} %copy-done.3), channel_id=1, source_target_pairs={{0,12},{4,0},{8,4},{12,8},{1,13},{5,1},{9,5},{13,9},{2,14},{6,2},{... | collective-permute-start | bytes 983048 | tf_op jit(solution)/shard_map/ppermute | solution.py:242
  18.0 16.3 %collective-permute-start.8 = (bf16[64,2560]{1,0:T(8,128)(2,1)S(1)}, bf16[64,2560]{1,0:T(8,128)(2,1)S(1)}, u32[]{:S(2)}, u32[]{:S(2)}) collective-permute-start(bf16[64,2560]{1,0:T(8,128)(2,1)S(1)} %collective-permute-done.refs_7_), channel_id=1, source_target_pairs={{0,16},{16,0},{1,17},{17,1},{2,18},{18,2},{3,19},{19,3},{4,20},{20... | collective-permute-start | bytes 983048 | tf_op jit(solution)/shard_map/ppermute | solution.py:267
  19.6 44.9 %copy-start.2 = (bf16[256,2560]{1,0:T(8,128)(2,1)S(1)}, bf16[256,2560]{1,0:T(8,128)(2,1)}, u32[]{:S(2)}) copy-start(bf16[256,2560]{1,0:T(8,128)(2,1)} %refs_2_.1) | copy-start | bytes 3932164
  31.1 12.8 %collective-permute-start.2 = (bf16[72,2560]{1,0:T(8,128)(2,1)S(1)}, bf16[72,2560]{1,0:T(8,128)(2,1)S(1)}, u32[]{:S(2)}, u32[]{:S(2)}) collective-permute-start(bf16[72,2560]{1,0:T(8,128)(2,1)S(1)} %pad_maximum_fusion.1), channel_id=1, source_target_pairs={{0,12},{4,0},{8,4},{12,8},{1,13},{5,1},{9,5},{13,9},{2,14},{6,2},{... | collective-permute-start | bytes 1105928 | tf_op jit(solution)/shard_map/ppermute | solution.py:242
  33.1 10.6 %collective-permute-start.6 = (bf16[64,2560]{1,0:T(8,128)(2,1)S(1)}, bf16[64,2560]{1,0:T(8,128)(2,1)S(1)}, u32[]{:S(2)}, u32[]{:S(2)}) collective-permute-start(bf16[64,2560]{1,0:T(8,128)(2,1)S(1)} %collective-permute-done.1.refs_3_), channel_id=1, source_target_pairs={{0,16},{16,0},{1,17},{17,1},{2,18},{18,2},{3,19},{19,3},{4,20},{20... | collective-permute-start | bytes 983048 | tf_op jit(solution)/shard_map/ppermute | solution.py:267
  34.4 22.4 %collective-permute-start.9 = (bf16[72,2560]{1,0:T(8,128)(2,1)S(1)}, bf16[72,2560]{1,0:T(8,128)(2,1)S(1)}, u32[]{:S(2)}, u32[]{:S(2)}) collective-permute-start(bf16[72,2560]{1,0:T(8,128)(2,1)S(1)} %collective-permute-done.3.refs_8_), channel_id=1, source_target_pairs={{0,16},{16,0},{1,17},{17,1},{2,18},{18,2},{3,19},{19,3},{4,20},{20... | collective-permute-start | bytes 1105928 | tf_op jit(solution)/shard_map/ppermute | solution.py:267
  35.1 16.2 %collective-permute-start.10 = (bf16[64,2560]{1,0:T(8,128)(2,1)S(1)}, bf16[64,2560]{1,0:T(8,128)(2,1)S(1)}, u32[]{:S(2)}, u32[]{:S(2)}) collective-permute-start(bf16[64,2560]{1,0:T(8,128)(2,1)S(1)} %collective-permute-done.refs_7_), channel_id=1, source_target_pairs={{0,4},{4,8},{8,12},{12,0},{1,5},{5,9},{9,13},{13,1},{2,6},{6,10},{... | collective-permute-start | bytes 983048 | tf_op jit(solution)/shard_map/ppermute | solution.py:242
  43.7 13.0 %collective-permute-start.4 = (bf16[72,2560]{1,0:T(8,128)(2,1)S(1)}, bf16[72,2560]{1,0:T(8,128)(2,1)S(1)}, u32[]{:S(2)}, u32[]{:S(2)}) collective-permute-start(bf16[72,2560]{1,0:T(8,128)(2,1)S(1)} %collective-permute-done.3.refs_8_), channel_id=1, source_target_pairs={{0,4},{4,8},{8,12},{12,0},{1,5},{5,9},{9,13},{13,1},{2,6},{6,10},{... | collective-permute-start | bytes 1105928 | tf_op jit(solution)/shard_map/ppermute | solution.py:242
  43.9 15.6 %collective-permute-start.7 = (bf16[72,2560]{1,0:T(8,128)(2,1)S(1)}, bf16[72,2560]{1,0:T(8,128)(2,1)S(1)}, u32[]{:S(2)}, u32[]{:S(2)}) collective-permute-start(bf16[72,2560]{1,0:T(8,128)(2,1)S(1)} %collective-permute-done.2.refs_4_), channel_id=1, source_target_pairs={{0,16},{16,0},{1,17},{17,1},{2,18},{18,2},{3,19},{19,3},{4,20},{20... | collective-permute-start | bytes 1105928 | tf_op jit(solution)/shard_map/ppermute | solution.py:267
  51.4 13.1 %copy-start.1 = (bf16[2,256,2560]{2,1,0:T(8,128)(2,1)S(1)}, bf16[2,256,2560]{2,1,0:T(8,128)(2,1)}, u32[]{:S(2)}) copy-start(bf16[2,256,2560]{2,1,0:T(8,128)(2,1)} %param.7) | copy-start | bytes 7864324
  56.7 15.2 %collective-permute-start.11 = (bf16[136,2560]{1,0:T(8,128)(2,1)S(1)}, bf16[136,2560]{1,0:T(8,128)(2,1)S(1)}, u32[]{:S(2)}, u32[]{:S(2)}) collective-permute-start(bf16[136,2560]{1,0:T(8,128)(2,1)S(1)} %constant_dynamic-update-slice_fusion.refs_2_), channel_id=1, source_target_pairs={{0,16},{16,0},{1,17},{17,1},{2,18},{18,2},{3,19},{19,3},{4,20},{20... | collective-permute-start | bytes 2088968 | tf_op jit(solution)/shard_map/ppermute | solution.py:267
  57.9 17.6 %collective-permute-start.16 = (bf16[576,512]{1,0:T(8,128)(2,1)S(1)}, bf16[576,512]{1,0:T(8,128)(2,1)S(1)}, u32[]{:S(2)}, u32[]{:S(2)}) collective-permute-start(bf16[576,512]{1,0:T(8,128)(2,1)S(1)} %pad_maximum_fusion), channel_id=1, source_target_pairs={{0,2},{2,0},{1,3},{3,1},{4,6},{6,4},{5,7},{7,5},{8,10},{10,8},{9,1... | collective-permute-start | bytes 1769480 | tf_op jit(solution)/shard_map/ppermute | solution.py:328
  70.5 4.8 %copy-start.5 = (s32[4]{0:T(128)S(1)}, s32[4]{0:T(128)}, u32[]{:S(2)}) copy-start(s32[4]{0:T(128)} %constant.97.clone) | copy-start | bytes 52
  70.5 5.0 %collective-permute-start.12 = (f32[2,512,128]{2,1,0:T(8,128)S(1)}, f32[2,512,128]{2,1,0:T(8,128)S(1)}, u32[]{:S(2)}, u32[]{:S(2)}) collective-permute-start(f32[2,512,128]{2,1,0:T(8,128)S(1)} %get-tuple-element.37), channel_id=1, source_target_pairs={{0,1},{1,0},{2,3},{3,2},{4,5},{5,4},{6,7},{7,6},{8,9},{9,8},{10,11... | collective-permute-start | bytes 1572872 | tf_op jit(solution)/shard_map/ppermute | solution.py:294
  70.6 5.0 %collective-permute-start.13 = (f32[2,512,128]{2,1,0:T(8,128)S(1)}, f32[2,512,128]{2,1,0:T(8,128)S(1)}, u32[]{:S(2)}, u32[]{:S(2)}) collective-permute-start(f32[2,512,128]{2,1,0:T(8,128)S(1)} %get-tuple-element.38), channel_id=1, source_target_pairs={{0,1},{1,0},{2,3},{3,2},{4,5},{5,4},{6,7},{7,6},{8,9},{9,8},{10,11... | collective-permute-start | bytes 1572872 | tf_op jit(solution)/shard_map/ppermute | solution.py:294
  71.1 4.5 %collective-permute-start.14 = (f32[2,512,128]{2,1,0:T(8,128)S(1)}, f32[2,512,128]{2,1,0:T(8,128)S(1)}, u32[]{:S(2)}, u32[]{:S(2)}) collective-permute-start(f32[2,512,128]{2,1,0:T(8,128)S(1)} %get-tuple-element.39), channel_id=1, source_target_pairs={{0,1},{1,0},{2,3},{3,2},{4,5},{5,4},{6,7},{7,6},{8,9},{9,8},{10,11... | collective-permute-start | bytes 1572872 | tf_op jit(solution)/shard_map/ppermute | solution.py:294
  75.2 2.0 %collective-permute-start.15 = (f32[2,512,128]{2,1,0:T(8,128)S(1)}, f32[2,512,128]{2,1,0:T(8,128)S(1)}, u32[]{:S(2)}, u32[]{:S(2)}) collective-permute-start(f32[2,512,128]{2,1,0:T(8,128)S(1)} %get-tuple-element.40), channel_id=1, source_target_pairs={{0,1},{1,0},{2,3},{3,2},{4,5},{5,4},{6,7},{7,6},{8,9},{9,8},{10,11... | collective-permute-start | bytes 1572872 | tf_op jit(solution)/shard_map/ppermute | solution.py:294
  79.2 7.3 %collective-permute-start.17 = (f32[1,136,128]{2,1,0:T(8,128)S(1)}, f32[1,136,128]{2,1,0:T(8,128)S(1)}, u32[]{:S(2)}, u32[]{:S(2)}) collective-permute-start(f32[1,136,128]{2,1,0:T(8,128)S(1)} %get-tuple-element.63), channel_id=1, source_target_pairs={{0,4},{4,8},{8,12},{12,0},{1,5},{5,9},{9,13},{13,1},{2,6},{6,10},{... | collective-permute-start | bytes 208904 | tf_op jit(solution)/shard_map/ppermute | solution.py:242
  81.0 8.4 %collective-permute-start.18 = (f32[1,136,128]{2,1,0:T(8,128)S(1)}, f32[1,136,128]{2,1,0:T(8,128)S(1)}, u32[]{:S(2)}, u32[]{:S(2)}) collective-permute-start(f32[1,136,128]{2,1,0:T(8,128)S(1)} %get-tuple-element.62), channel_id=1, source_target_pairs={{0,8},{4,12},{8,0},{12,4},{1,9},{5,13},{9,1},{13,5},{2,10},{6,14},... | collective-permute-start | bytes 208904 | tf_op jit(solution)/shard_map/ppermute | solution.py:242
  84.5 5.2 %collective-permute-start.19 = (f32[1,136,128]{2,1,0:T(8,128)S(1)}, f32[1,136,128]{2,1,0:T(8,128)S(1)}, u32[]{:S(2)}, u32[]{:S(2)}) collective-permute-start(f32[1,136,128]{2,1,0:T(8,128)S(1)} %get-tuple-element.61), channel_id=1, source_target_pairs={{0,12},{4,0},{8,4},{12,8},{1,13},{5,1},{9,5},{13,9},{2,14},{6,2},{... | collective-permute-start | bytes 208904 | tf_op jit(solution)/shard_map/ppermute | solution.py:242
  89.9 3.8 %collective-permute-start.21 = (bf16[1,16,512]{2,1,0:T(8,128)(2,1)S(1)}, bf16[1,16,512]{2,1,0:T(8,128)(2,1)S(1)}, u32[]{:S(2)}, u32[]{:S(2)}) collective-permute-start(bf16[1,16,512]{2,1,0:T(8,128)(2,1)S(1)} %get-tuple-element.75), channel_id=1, source_target_pairs={{0,2},{2,0},{1,3},{3,1},{4,6},{6,4},{5,7},{7,5},{8,10},{10,8},{9,1... | collective-permute-start | bytes 49160 | tf_op jit(solution)/shard_map/ppermute | solution.py:355
  90.9 3.2 %collective-permute-start.22 = (bf16[1,16,512]{2,1,0:T(8,128)(2,1)S(1)}, bf16[1,16,512]{2,1,0:T(8,128)(2,1)S(1)}, u32[]{:S(2)}, u32[]{:S(2)}) collective-permute-start(bf16[1,16,512]{2,1,0:T(8,128)(2,1)S(1)} %get-tuple-element.75), channel_id=1, source_target_pairs={{0,3},{3,0},{1,2},{2,1},{4,7},{7,4},{5,6},{6,5},{8,11},{11,8},{9,1... | collective-permute-start | bytes 49160 | tf_op jit(solution)/shard_map/ppermute | solution.py:356
  91.1 1.9 %collective-permute-start.20 = (bf16[1,16,512]{2,1,0:T(8,128)(2,1)S(1)}, bf16[1,16,512]{2,1,0:T(8,128)(2,1)S(1)}, u32[]{:S(2)}, u32[]{:S(2)}) collective-permute-start(bf16[1,16,512]{2,1,0:T(8,128)(2,1)S(1)} %get-tuple-element.76.mine_ref), channel_id=1, source_target_pairs={{0,1},{1,0},{2,3},{3,2},{4,5},{5,4},{6,7},{7,6},{8,9},{9,8},{10,11... | collective-permute-start | bytes 49160 | tf_op jit(solution)/shard_map/ppermute | solution.py:354

commit v14 on v13

--- a/solution.py
+++ b/solution.py
@@ -10,7 +10,7 @@
 
 HEAD_DIM = 64
 EMPTY = -3e38
-FIRST_EIGHTHS = 4
+FIRST_EIGHTHS = 5
 VMEM_LIMIT = 22 * 1024 * 1024
 SWAP = [(0, 1), (1, 0)]
 CROSS = [(0, 3), (3, 0), (1, 2), (2, 1)]
@@ -259,12 +259,13 @@
         for at in range(2):
             below.append(shifted(after(sent[at], below[-1:]), 1))
             above.append(shifted(after(sent[at], above[-1:] or below[:1]), -1))
-        opposite = [jnp.concatenate([shifted(after(below[0], below[1:]), 1), shifted(below[1], 1)], axis=0)]
+        opposite = [shifted(after(below[0], below[1:]), 1), shifted(below[1], 1)]
         around = [from_rows(piece[-1][-8:], queries.shape) for piece in (above, opposite, below)]
+        opposite = [jnp.concatenate([opposite[0], opposite[1][: lengths[1]]], axis=0)]
         queries = jnp.concatenate([queries] + around, axis=0)
         swapped = []
         for at, piece in enumerate([below[0], above[0], below[1], above[1]] + opposite):
-            swapped.append(lax.ppermute(after(piece, swapped[max(at - 2, 0) : max(at - 1, 0)]), "groups", SWAP))
+            swapped.append(lax.ppermute(after(piece, swapped[2:] if at == 4 else swapped[max(at - 2, 0) : max(at - 1, 0)]), "groups", SWAP))
         weights = [down_weight] + above + swapped[1:4:2] + below + swapped[0:4:2] + opposite + swapped[4:]
         flags = jnp.stack([core, (group == core).astype(core.dtype)])
         blocks_of = [[(2, shard)], list(zip(range(3, 7), 2 * lengths)), list(zip(range(7, 11), 2 * lengths))]

time: 95.5 us -> 104 us (1.089)
  waiting for transfers between devices: 52.4 us -> 57.8 us
  local copies, waits for them, and re-layouts: 1.62 us -> 3.26 us
    ppermute x5, waiting for transfers between devices: 9.16 us -> 14.2 us  [body(): lax.ppermute(after(piece, swapped[2:] if at == 4 else swapped[max(at - 2,...]
    ppermute x1, waiting for transfers between devices: 4.99 us -> 0.01 us  [body(): partner_hidden = lax.ppermute(hidden, 'side', SWAP)]
    ppermute x9, waiting for transfers between devices: 34.5 us -> 39 us  [shifted(): lax.ppermute(array, 'high', [(at, (at + shift) % highs) for at in range(h...]
    ppermute x5, starting transfers between devices: 5.92 us -> 8.76 us  [body(): lax.ppermute(after(piece, swapped[2:] if at == 4 else swapped[max(at - 2,...]
    ppermute x9, starting transfers between devices: 15.9 us -> 14 us  [shifted(): lax.ppermute(array, 'high', [(at, (at + shift) % highs) for at in range(h...]
    dynamic_slice x1 -> x2, local copies, waits for them, and re-layouts: 1.27 us -> 2.14 us  [body(): lax.dynamic_slice_in_dim(down_weight, group * half + first, length, axis=0)]
  transfers between devices with their start and end apart: 23 -> 23, of which waited for: 15 -> 14; matrix products, arithmetic and copies ran while one was open for 1% -> 3% of each run, Pallas kernels for 10% -> 9%
where the time goes in v14:
time: 104 us
  waiting for transfers between devices  57.8 us (56%)
  starting transfers between devices  28.7 us (28%)
  Pallas kernels  12.7 us (12%)
  local copies, waits for them, and re-layouts  3.26 us (3%)
  other arithmetic  1.22 us (1%)
    ppermute x9, waiting for transfers between devices, shifted(): lax.ppermute(array, 'high', [(at, (at + shift) % highs) for at in range(h...  39 us
    ppermute x5, waiting for transfers between devices, body(): lax.ppermute(after(piece, swapped[2:] if at == 4 else swapped[max(at - 2,...  14.2 us
    ppermute x9, starting transfers between devices, shifted(): lax.ppermute(array, 'high', [(at, (at + shift) % highs) for at in range(h...  14 us
    pallas_call x2, Pallas kernels, project(): pl.pallas_call(functools.partial(project_kernel, jobs=jobs, sends=sends),...  9.32 us
    ppermute x5, starting transfers between devices, body(): lax.ppermute(after(piece, swapped[2:] if at == 4 else swapped[max(at - 2,...  8.76 us
    dynamic_slice x2, local copies, waits for them, and re-layouts, body(): lax.dynamic_slice_in_dim(down_weight, group * half + first, length, axis=0)  2.14 us
  transfers between devices with their start and end apart: 23, of which 14 were waited for; matrix products, arithmetic and copies ran while one was open for 3% of the time, Pallas kernels for 9%

profile of v14, /device:TPU:0, one launch (start us, length us, event | category | flops | bytes accessed | tf_op | source)
XLA Modules:
  0.0 104.0 jit_solution(18117690021998907247)
XLA Ops:
  0.0 1.2 %constant_dynamic-slice_fusion.4 = bf16[80,2560]{1,0:T(8,128)(2,1)S(1)} fusion(bf16[256,2560]{1,0:T(8,128)(2,1)} %refs_2_.1, s32[]{:T(128)S(6)} %select_n.73), kind=kLoop, calls=%fused_computation.23 | loop fusion | bytes 819204 | tf_op jit(solution)/shard_map/dynamic_slice | solution.py:254
  1.2 3.1 %collective-permute-start = (bf16[80,2560]{1,0:T(8,128)(2,1)S(1)}, bf16[80,2560]{1,0:T(8,128)(2,1)S(1)}, u32[]{:S(2)}, u32[]{:S(2)}) collective-permute-start(bf16[80,2560]{1,0:T(8,128)(2,1)S(1)} %constant_dynamic-slice_fusion.4), channel_id=1, source_target_pairs={{0,4},{4,8},{8,12},{12,0},{1,5},{5,9},{9,13},{13,1},{2,6},{6,10},{... | collective-permute-start | bytes 1228808 | tf_op jit(solution)/shard_map/ppermute | solution.py:242
  4.3 1.5 %collective-permute-start.5 = (bf16[512,2560]{1,0:T(8,128)(2,1)}, bf16[512,2560]{1,0:T(8,128)(2,1)}, u32[]{:S(2)}, u32[]{:S(2)}) collective-permute-start(bf16[512,2560]{1,0:T(8,128)(2,1)} %bitcast.21), channel_id=1, source_target_pairs={{0,2},{2,0},{1,3},{3,1},{4,6},{6,4},{5,7},{7,5},{8,10},{10,8},{9,1... | collective-permute-start | bytes 7864328 | tf_op jit(solution)/shard_map/ppermute | solution.py:245
  5.8 0.8 constant_dynamic-slice_fusion.13
  7.4 1.0 constant_dynamic-slice_fusion.5
  8.5 7.3 %collective-permute-done.refs_7_ = bf16[80,2560]{1,0:T(8,128)(2,1)S(1)} collective-permute-done((bf16[80,2560]{1,0:T(8,128)(2,1)S(1)}, bf16[80,2560]{1,0:T(8,128)(2,1)S(1)}, u32[]{:S(2)}, u32[]{:S(2)}) %collective-permute-start) | collective-permute-done | bytes 409632 | tf_op jit(solution)/shard_map/ppermute | solution.py:242
  16.0 3.9 %collective-permute-start.1 = (bf16[80,2560]{1,0:T(8,128)(2,1)S(1)}, bf16[80,2560]{1,0:T(8,128)(2,1)S(1)}, u32[]{:S(2)}, u32[]{:S(2)}) collective-permute-start(bf16[80,2560]{1,0:T(8,128)(2,1)S(1)} %constant_dynamic-slice_fusion.4), channel_id=1, source_target_pairs={{0,12},{4,0},{8,4},{12,8},{1,13},{5,1},{9,5},{13,9},{2,14},{6,2},{... | collective-permute-start | bytes 1228808 | tf_op jit(solution)/shard_map/ppermute | solution.py:242
  19.8 1.5 %collective-permute-start.8 = (bf16[80,2560]{1,0:T(8,128)(2,1)S(1)}, bf16[80,2560]{1,0:T(8,128)(2,1)S(1)}, u32[]{:S(2)}, u32[]{:S(2)}) collective-permute-start(bf16[80,2560]{1,0:T(8,128)(2,1)S(1)} %collective-permute-done.refs_7_), channel_id=1, source_target_pairs={{0,16},{16,0},{1,17},{17,1},{2,18},{18,2},{3,19},{19,3},{4,20},{20... | collective-permute-start | bytes 1228808 | tf_op jit(solution)/shard_map/ppermute | solution.py:268
  21.4 5.9 %collective-permute-done.3.refs_8_ = bf16[56,2560]{1,0:T(8,128)(2,1)S(1)} collective-permute-done((bf16[56,2560]{1,0:T(8,128)(2,1)S(1)}, bf16[56,2560]{1,0:T(8,128)(2,1)S(1)}, u32[]{:S(2)}, u32[]{:S(2)}) %collective-permute-start.3) | collective-permute-done | bytes 286752 | tf_op jit(solution)/shard_map/ppermute | solution.py:242
  27.4 5.6 %collective-permute-done.1.refs_3_ = bf16[80,2560]{1,0:T(8,128)(2,1)S(1)} collective-permute-done((bf16[80,2560]{1,0:T(8,128)(2,1)S(1)}, bf16[80,2560]{1,0:T(8,128)(2,1)S(1)}, u32[]{:S(2)}, u32[]{:S(2)}) %collective-permute-start.1) | collective-permute-done | bytes 409632 | tf_op jit(solution)/shard_map/ppermute | solution.py:242
  33.0 3.2 %collective-permute-start.2 = (bf16[56,2560]{1,0:T(8,128)(2,1)S(1)}, bf16[56,2560]{1,0:T(8,128)(2,1)S(1)}, u32[]{:S(2)}, u32[]{:S(2)}) collective-permute-start(bf16[56,2560]{1,0:T(8,128)(2,1)S(1)} %pad_maximum_fusion.2), channel_id=1, source_target_pairs={{0,12},{4,0},{8,4},{12,8},{1,13},{5,1},{9,5},{13,9},{2,14},{6,2},{... | collective-permute-start | bytes 860168 | tf_op jit(solution)/shard_map/ppermute | solution.py:242
  36.1 1.5 %collective-permute-start.9 = (bf16[56,2560]{1,0:T(8,128)(2,1)S(1)}, bf16[56,2560]{1,0:T(8,128)(2,1)S(1)}, u32[]{:S(2)}, u32[]{:S(2)}) collective-permute-start(bf16[56,2560]{1,0:T(8,128)(2,1)S(1)} %collective-permute-done.3.refs_8_), channel_id=1, source_target_pairs={{0,16},{16,0},{1,17},{17,1},{2,18},{18,2},{3,19},{19,3},{4,20},{20... | collective-permute-start | bytes 860168 | tf_op jit(solution)/shard_map/ppermute | solution.py:268
  37.7 13.4 %collective-permute-done.4 = bf16[56,2560]{1,0:T(8,128)(2,1)S(1)} collective-permute-done((bf16[56,2560]{1,0:T(8,128)(2,1)S(1)}, bf16[56,2560]{1,0:T(8,128)(2,1)S(1)}, u32[]{:S(2)}, u32[]{:S(2)}) %collective-permute-start.4) | collective-permute-done | bytes 286752 | tf_op jit(solution)/shard_map/ppermute | solution.py:242
  51.1 1.5 %collective-permute-start.6 = (bf16[80,2560]{1,0:T(8,128)(2,1)S(1)}, bf16[80,2560]{1,0:T(8,128)(2,1)S(1)}, u32[]{:S(2)}, u32[]{:S(2)}) collective-permute-start(bf16[80,2560]{1,0:T(8,128)(2,1)S(1)} %collective-permute-done.1.refs_3_), channel_id=1, source_target_pairs={{0,16},{16,0},{1,17},{17,1},{2,18},{18,2},{3,19},{19,3},{4,20},{20... | collective-permute-start | bytes 1228808 | tf_op jit(solution)/shard_map/ppermute | solution.py:268
  52.6 1.7 %collective-permute-done.2.refs_4_ = bf16[56,2560]{1,0:T(8,128)(2,1)S(1)} collective-permute-done((bf16[56,2560]{1,0:T(8,128)(2,1)S(1)}, bf16[56,2560]{1,0:T(8,128)(2,1)S(1)}, u32[]{:S(2)}, u32[]{:S(2)}) %collective-permute-start.2) | collective-permute-done | bytes 286752 | tf_op jit(solution)/shard_map/ppermute | solution.py:242
  54.4 6.2 %collective-permute-done.6.refs_5_ = bf16[80,2560]{1,0:T(8,128)(2,1)S(1)} collective-permute-done((bf16[80,2560]{1,0:T(8,128)(2,1)S(1)}, bf16[80,2560]{1,0:T(8,128)(2,1)S(1)}, u32[]{:S(2)}, u32[]{:S(2)}) %collective-permute-start.6) | collective-permute-done | bytes 409632 | tf_op jit(solution)/shard_map/ppermute | solution.py:268
  60.6 1.8 %collective-permute-start.7 = (bf16[56,2560]{1,0:T(8,128)(2,1)S(1)}, bf16[56,2560]{1,0:T(8,128)(2,1)S(1)}, u32[]{:S(2)}, u32[]{:S(2)}) collective-permute-start(bf16[56,2560]{1,0:T(8,128)(2,1)S(1)} %collective-permute-done.2.refs_4_), channel_id=1, source_target_pairs={{0,16},{16,0},{1,17},{17,1},{2,18},{18,2},{3,19},{19,3},{4,20},{20... | collective-permute-start | bytes 860168 | tf_op jit(solution)/shard_map/ppermute | solution.py:268
  62.5 6.9 %collective-permute-done.7.refs_6_ = bf16[56,2560]{1,0:T(8,128)(2,1)S(1)} collective-permute-done((bf16[56,2560]{1,0:T(8,128)(2,1)S(1)}, bf16[56,2560]{1,0:T(8,128)(2,1)S(1)}, u32[]{:S(2)}, u32[]{:S(2)}) %collective-permute-start.7) | collective-permute-done | bytes 286752 | tf_op jit(solution)/shard_map/ppermute | solution.py:268
  69.4 2.3 %collective-permute-start.11 = (bf16[128,2560]{1,0:T(8,128)(2,1)S(1)}, bf16[128,2560]{1,0:T(8,128)(2,1)S(1)}, u32[]{:S(2)}, u32[]{:S(2)}) collective-permute-start(bf16[128,2560]{1,0:T(8,128)(2,1)S(1)} %pad_maximum_fusion.refs_2_), channel_id=1, source_target_pairs={{0,16},{16,0},{1,17},{17,1},{2,18},{18,2},{3,19},{19,3},{4,20},{20... | collective-permute-start | bytes 1966088 | tf_op jit(solution)/shard_map/ppermute | solution.py:268
  71.9 1.6 %collective-permute-start.16 = (bf16[576,512]{1,0:T(8,128)(2,1)S(1)}, bf16[576,512]{1,0:T(8,128)(2,1)S(1)}, u32[]{:S(2)}, u32[]{:S(2)}) collective-permute-start(bf16[576,512]{1,0:T(8,128)(2,1)S(1)} %pad_maximum_fusion.1), channel_id=1, source_target_pairs={{0,2},{2,0},{1,3},{3,1},{4,6},{6,4},{5,7},{7,5},{8,10},{10,8},{9,1... | collective-permute-start | bytes 1769480 | tf_op jit(solution)/shard_map/ppermute | solution.py:329
  73.4 6.0 %project_near.1 = (f32[6,512,128]{2,1,0:T(8,128)S(1)}, f32[2,512,128]{2,1,0:T(8,128)S(1)}, f32[2,512,128]{2,1,0:T(8,128)S(1)}, f32[2,512,128]{2,1,0:T(8,128)S(1)}) custom-call(s32[2]{0:T(128)S(1)} %pad_add_fusion.3.flag_ref, bf16[512,2560]{1,0:T(8,128)(2,1)S(1)} %bitcast.22, bf16[512,2560]{1,0:T(8,128)(2,1)} %collective-permute-done.5.refs_1_, ...), custom_call_target="tpu_custom_call" | custom-call | flops 4026531840 | bytes 1 | tf_op jit(solution)/shard_map/project_near/pallas_call | solution.py:190
  80.1 1.1 %collective-permute-done.11.refs_3_ = bf16[128,2560]{1,0:T(8,128)(2,1)S(1)} collective-permute-done((bf16[128,2560]{1,0:T(8,128)(2,1)S(1)}, bf16[128,2560]{1,0:T(8,128)(2,1)S(1)}, u32[]{:S(2)}, u32[]{:S(2)}) %collective-permute-start.11) | collective-permute-done | bytes 655392 | tf_op jit(solution)/shard_map/ppermute | solution.py:268
  81.3 3.3 %project_far.1 = (f32[2,512,128]{2,1,0:T(8,128)S(1)}, f32[2,512,128]{2,1,0:T(8,128)S(1)}) custom-call(s32[2]{0:T(128)S(1)} %pad_add_fusion.3.flag_ref, bf16[512,2560]{1,0:T(8,128)(2,1)S(1)} %bitcast.23, bf16[512,2560]{1,0:T(8,128)(2,1)} %collective-permute-done.5.refs_1_, bf16[128,2560]{1,0:T(8,128)(2,1)S(1)} %pad_maximum_fusion.refs_2_, ...), custom_call_target="tpu_custom_call" | custom-call | flops 1 | bytes 1 | tf_op jit(solution)/shard_map/project_far/pallas_call | solution.py:190
  84.7 1.8 %collective-permute-done.15.refs_5_ = f32[2,512,128]{2,1,0:T(8,128)S(1)} collective-permute-done((f32[2,512,128]{2,1,0:T(8,128)S(1)}, f32[2,512,128]{2,1,0:T(8,128)S(1)}, u32[]{:S(2)}, u32[]{:S(2)}) %collective-permute-start.15) | collective-permute-done | bytes 524320 | tf_op jit(solution)/shard_map/ppermute | solution.py:295
  86.5 2.0 %attend.1 = f32[4,136,128]{2,1,0:T(8,128)S(1)} custom-call(s32[4]{0:T(128)S(1)} %pad_add_fusion.2.place_ref, s32[2,4]{1,0:T(2,128)S(1)} %pad_add_fusion.spot_ref, bf16[4,16,512]{2,1,0:T(8,128)(2,1)S(1)} %get-tuple-element.64.query_ref, f32[6,512,128]{2,1,0:T(8,128)S(1)} %get-tuple-element.32.refs_0_, f32[2,512,128]{2,1,0:T(8,128)S(1)} %get-tuple-element.36.refs_1_, ...), custom_call_target="tpu_custom_call" | custom-call | tf_op jit(solution)/shard_map/attend/pallas_call | solution.py:332
  88.6 0.8 collective-permute-start.18
  89.4 3.0 %collective-permute-start.19 = (f32[1,136,128]{2,1,0:T(8,128)S(1)}, f32[1,136,128]{2,1,0:T(8,128)S(1)}, u32[]{:S(2)}, u32[]{:S(2)}) collective-permute-start(f32[1,136,128]{2,1,0:T(8,128)S(1)} %get-tuple-element.59), channel_id=1, source_target_pairs={{0,12},{4,0},{8,4},{12,8},{1,13},{5,1},{9,5},{13,9},{2,14},{6,2},{... | collective-permute-start | bytes 208904 | tf_op jit(solution)/shard_map/ppermute | solution.py:242
  92.4 3.1 %collective-permute-done.17.refs_1_ = f32[1,136,128]{2,1,0:T(8,128)S(1)} collective-permute-done((f32[1,136,128]{2,1,0:T(8,128)S(1)}, f32[1,136,128]{2,1,0:T(8,128)S(1)}, u32[]{:S(2)}, u32[]{:S(2)}) %collective-permute-start.17) | collective-permute-done | bytes 69664 | tf_op jit(solution)/shard_map/ppermute | solution.py:242
  95.5 2.0 %collective-permute-done.18.refs_2_ = f32[1,136,128]{2,1,0:T(8,128)S(1)} collective-permute-done((f32[1,136,128]{2,1,0:T(8,128)S(1)}, f32[1,136,128]{2,1,0:T(8,128)S(1)}, u32[]{:S(2)}, u32[]{:S(2)}) %collective-permute-start.18) | collective-permute-done | bytes 69664 | tf_op jit(solution)/shard_map/ppermute | solution.py:242
  97.8 1.9 %collective-permute-start.21 = (bf16[1,16,512]{2,1,0:T(8,128)(2,1)S(1)}, bf16[1,16,512]{2,1,0:T(8,128)(2,1)S(1)}, u32[]{:S(2)}, u32[]{:S(2)}) collective-permute-start(bf16[1,16,512]{2,1,0:T(8,128)(2,1)S(1)} %get-tuple-element.73), channel_id=1, source_target_pairs={{0,2},{2,0},{1,3},{3,1},{4,6},{6,4},{5,7},{7,5},{8,10},{10,8},{9,1... | collective-permute-start | bytes 49160 | tf_op jit(solution)/shard_map/ppermute | solution.py:356
  101.6 1.2 %collective-permute-done.22.both_ref = bf16[1,16,512]{2,1,0:T(8,128)(2,1)S(1)} collective-permute-done((bf16[1,16,512]{2,1,0:T(8,128)(2,1)S(1)}, bf16[1,16,512]{2,1,0:T(8,128)(2,1)S(1)}, u32[]{:S(2)}, u32[]{:S(2)}) %collective-permute-start.22) | collective-permute-done | bytes 16416 | tf_op jit(solution)/shard_map/ppermute | solution.py:357
  102.8 1.2 %assemble.1 = bf16[1,16,2048]{2,1,0:T(8,128)(2,1)} custom-call(s32[2]{0:T(128)S(1)} %pad_add_fusion.1.flag_ref, bf16[1,16,512]{2,1,0:T(8,128)(2,1)S(1)} %get-tuple-element.74.mine_ref, bf16[1,16,512]{2,1,0:T(8,128)(2,1)S(1)} %collective-permute-done.20.core_ref, bf16[1,16,512]{2,1,0:T(8,128)(2,1)S(1)} %collective-permute-done.21.side_ref, ...), custom_call_target="tpu_custom_call" | custom-call | tf_op jit(solution)/shard_map/assemble/pallas_call | solution.py:364
  (58 shorter events, 4.4 us)
Async XLA Ops:
  0.0 15.8 %copy-start = (bf16[2,256,2048]{2,1,0:T(8,128)(2,1)S(1)}, bf16[2,256,2048]{2,1,0:T(8,128)(2,1)}, u32[]{:S(2)}) copy-start(bf16[2,256,2048]{2,1,0:T(8,128)(2,1)} %param.8) | copy-start | bytes 6291460
  1.2 14.6 %collective-permute-start = (bf16[80,2560]{1,0:T(8,128)(2,1)S(1)}, bf16[80,2560]{1,0:T(8,128)(2,1)S(1)}, u32[]{:S(2)}, u32[]{:S(2)}) collective-permute-start(bf16[80,2560]{1,0:T(8,128)(2,1)S(1)} %constant_dynamic-slice_fusion.4), channel_id=1, source_target_pairs={{0,4},{4,8},{8,12},{12,0},{1,5},{5,9},{9,13},{13,1},{2,6},{6,10},{... | collective-permute-start | bytes 1228808 | tf_op jit(solution)/shard_map/ppermute | solution.py:242
  4.3 69.2 %collective-permute-start.5 = (bf16[512,2560]{1,0:T(8,128)(2,1)}, bf16[512,2560]{1,0:T(8,128)(2,1)}, u32[]{:S(2)}, u32[]{:S(2)}) collective-permute-start(bf16[512,2560]{1,0:T(8,128)(2,1)} %bitcast.21), channel_id=1, source_target_pairs={{0,2},{2,0},{1,3},{3,1},{4,6},{6,4},{5,7},{7,5},{8,10},{10,8},{9,1... | collective-permute-start | bytes 7864328 | tf_op jit(solution)/shard_map/ppermute | solution.py:245
  15.8 11.6 %collective-permute-start.3 = (bf16[56,2560]{1,0:T(8,128)(2,1)S(1)}, bf16[56,2560]{1,0:T(8,128)(2,1)S(1)}, u32[]{:S(2)}, u32[]{:S(2)}) collective-permute-start(bf16[56,2560]{1,0:T(8,128)(2,1)S(1)} %pad_maximum_fusion.2), channel_id=1, source_target_pairs={{0,4},{4,8},{8,12},{12,0},{1,5},{5,9},{9,13},{13,1},{2,6},{6,10},{... | collective-permute-start | bytes 860168 | tf_op jit(solution)/shard_map/ppermute | solution.py:242
  16.0 17.0 %collective-permute-start.1 = (bf16[80,2560]{1,0:T(8,128)(2,1)S(1)}, bf16[80,2560]{1,0:T(8,128)(2,1)S(1)}, u32[]{:S(2)}, u32[]{:S(2)}) collective-permute-start(bf16[80,2560]{1,0:T(8,128)(2,1)S(1)} %constant_dynamic-slice_fusion.4), channel_id=1, source_target_pairs={{0,12},{4,0},{8,4},{12,8},{1,13},{5,1},{9,5},{13,9},{2,14},{6,2},{... | collective-permute-start | bytes 1228808 | tf_op jit(solution)/shard_map/ppermute | solution.py:242
  19.8 16.3 %collective-permute-start.8 = (bf16[80,2560]{1,0:T(8,128)(2,1)S(1)}, bf16[80,2560]{1,0:T(8,128)(2,1)S(1)}, u32[]{:S(2)}, u32[]{:S(2)}) collective-permute-start(bf16[80,2560]{1,0:T(8,128)(2,1)S(1)} %collective-permute-done.refs_7_), channel_id=1, source_target_pairs={{0,16},{16,0},{1,17},{17,1},{2,18},{18,2},{3,19},{19,3},{4,20},{20... | collective-permute-start | bytes 1228808 | tf_op jit(solution)/shard_map/ppermute | solution.py:268
  27.3 35.1 %collective-permute-start.10 = (bf16[80,2560]{1,0:T(8,128)(2,1)S(1)}, bf16[80,2560]{1,0:T(8,128)(2,1)S(1)}, u32[]{:S(2)}, u32[]{:S(2)}) collective-permute-start(bf16[80,2560]{1,0:T(8,128)(2,1)S(1)} %collective-permute-done.refs_7_), channel_id=1, source_target_pairs={{0,4},{4,8},{8,12},{12,0},{1,5},{5,9},{9,13},{13,1},{2,6},{6,10},{... | collective-permute-start | bytes 1228808 | tf_op jit(solution)/shard_map/ppermute | solution.py:242
  27.3 23.7 %collective-permute-start.4 = (bf16[56,2560]{1,0:T(8,128)(2,1)S(1)}, bf16[56,2560]{1,0:T(8,128)(2,1)S(1)}, u32[]{:S(2)}, u32[]{:S(2)}) collective-permute-start(bf16[56,2560]{1,0:T(8,128)(2,1)S(1)} %collective-permute-done.3.refs_8_), channel_id=1, source_target_pairs={{0,4},{4,8},{8,12},{12,0},{1,5},{5,9},{9,13},{13,1},{2,6},{6,10},{... | collective-permute-start | bytes 860168 | tf_op jit(solution)/shard_map/ppermute | solution.py:242
  27.3 46.1 %copy-start.2 = (bf16[256,2560]{1,0:T(8,128)(2,1)S(1)}, bf16[256,2560]{1,0:T(8,128)(2,1)}, u32[]{:S(2)}) copy-start(bf16[256,2560]{1,0:T(8,128)(2,1)} %refs_2_.1) | copy-start | bytes 3932164
  33.0 21.4 %collective-permute-start.2 = (bf16[56,2560]{1,0:T(8,128)(2,1)S(1)}, bf16[56,2560]{1,0:T(8,128)(2,1)S(1)}, u32[]{:S(2)}, u32[]{:S(2)}) collective-permute-start(bf16[56,2560]{1,0:T(8,128)(2,1)S(1)} %pad_maximum_fusion.2), channel_id=1, source_target_pairs={{0,12},{4,0},{8,4},{12,8},{1,13},{5,1},{9,5},{13,9},{2,14},{6,2},{... | collective-permute-start | bytes 860168 | tf_op jit(solution)/shard_map/ppermute | solution.py:242
  36.1 26.3 %collective-permute-start.9 = (bf16[56,2560]{1,0:T(8,128)(2,1)S(1)}, bf16[56,2560]{1,0:T(8,128)(2,1)S(1)}, u32[]{:S(2)}, u32[]{:S(2)}) collective-permute-start(bf16[56,2560]{1,0:T(8,128)(2,1)S(1)} %collective-permute-done.3.refs_8_), channel_id=1, source_target_pairs={{0,16},{16,0},{1,17},{17,1},{2,18},{18,2},{3,19},{19,3},{4,20},{20... | collective-permute-start | bytes 860168 | tf_op jit(solution)/shard_map/ppermute | solution.py:268
  51.1 9.5 %collective-permute-start.6 = (bf16[80,2560]{1,0:T(8,128)(2,1)S(1)}, bf16[80,2560]{1,0:T(8,128)(2,1)S(1)}, u32[]{:S(2)}, u32[]{:S(2)}) collective-permute-start(bf16[80,2560]{1,0:T(8,128)(2,1)S(1)} %collective-permute-done.1.refs_3_), channel_id=1, source_target_pairs={{0,16},{16,0},{1,17},{17,1},{2,18},{18,2},{3,19},{19,3},{4,20},{20... | collective-permute-start | bytes 1228808 | tf_op jit(solution)/shard_map/ppermute | solution.py:268
  54.4 19.0 %copy-start.1 = (bf16[2,256,2560]{2,1,0:T(8,128)(2,1)S(1)}, bf16[2,256,2560]{2,1,0:T(8,128)(2,1)}, u32[]{:S(2)}) copy-start(bf16[2,256,2560]{2,1,0:T(8,128)(2,1)} %param.7) | copy-start | bytes 7864324
  60.6 8.9 %collective-permute-start.7 = (bf16[56,2560]{1,0:T(8,128)(2,1)S(1)}, bf16[56,2560]{1,0:T(8,128)(2,1)S(1)}, u32[]{:S(2)}, u32[]{:S(2)}) collective-permute-start(bf16[56,2560]{1,0:T(8,128)(2,1)S(1)} %collective-permute-done.2.refs_4_), channel_id=1, source_target_pairs={{0,16},{16,0},{1,17},{17,1},{2,18},{18,2},{3,19},{19,3},{4,20},{20... | collective-permute-start | bytes 860168 | tf_op jit(solution)/shard_map/ppermute | solution.py:268
  69.4 11.8 %collective-permute-start.11 = (bf16[128,2560]{1,0:T(8,128)(2,1)S(1)}, bf16[128,2560]{1,0:T(8,128)(2,1)S(1)}, u32[]{:S(2)}, u32[]{:S(2)}) collective-permute-start(bf16[128,2560]{1,0:T(8,128)(2,1)S(1)} %pad_maximum_fusion.refs_2_), channel_id=1, source_target_pairs={{0,16},{16,0},{1,17},{17,1},{2,18},{18,2},{3,19},{19,3},{4,20},{20... | collective-permute-start | bytes 1966088 | tf_op jit(solution)/shard_map/ppermute | solution.py:268
  71.9 12.8 %collective-permute-start.16 = (bf16[576,512]{1,0:T(8,128)(2,1)S(1)}, bf16[576,512]{1,0:T(8,128)(2,1)S(1)}, u32[]{:S(2)}, u32[]{:S(2)}) collective-permute-start(bf16[576,512]{1,0:T(8,128)(2,1)S(1)} %pad_maximum_fusion.1), channel_id=1, source_target_pairs={{0,2},{2,0},{1,3},{3,1},{4,6},{6,4},{5,7},{7,5},{8,10},{10,8},{9,1... | collective-permute-start | bytes 1769480 | tf_op jit(solution)/shard_map/ppermute | solution.py:329
  79.5 5.2 %copy-start.3 = (s32[4]{0:T(128)S(1)}, s32[4]{0:T(128)}, u32[]{:S(2)}) copy-start(s32[4]{0:T(128)} %constant.97.clone) | copy-start | bytes 52
  79.5 5.2 %collective-permute-start.12 = (f32[2,512,128]{2,1,0:T(8,128)S(1)}, f32[2,512,128]{2,1,0:T(8,128)S(1)}, u32[]{:S(2)}, u32[]{:S(2)}) collective-permute-start(f32[2,512,128]{2,1,0:T(8,128)S(1)} %get-tuple-element.37), channel_id=1, source_target_pairs={{0,1},{1,0},{2,3},{3,2},{4,5},{5,4},{6,7},{7,6},{8,9},{9,8},{10,11... | collective-permute-start | bytes 1572872 | tf_op jit(solution)/shard_map/ppermute | solution.py:295
  79.6 5.2 %collective-permute-start.13 = (f32[2,512,128]{2,1,0:T(8,128)S(1)}, f32[2,512,128]{2,1,0:T(8,128)S(1)}, u32[]{:S(2)}, u32[]{:S(2)}) collective-permute-start(f32[2,512,128]{2,1,0:T(8,128)S(1)} %get-tuple-element.38), channel_id=1, source_target_pairs={{0,1},{1,0},{2,3},{3,2},{4,5},{5,4},{6,7},{7,6},{8,9},{9,8},{10,11... | collective-permute-start | bytes 1572872 | tf_op jit(solution)/shard_map/ppermute | solution.py:295
  80.1 4.7 %collective-permute-start.14 = (f32[2,512,128]{2,1,0:T(8,128)S(1)}, f32[2,512,128]{2,1,0:T(8,128)S(1)}, u32[]{:S(2)}, u32[]{:S(2)}) collective-permute-start(f32[2,512,128]{2,1,0:T(8,128)S(1)} %get-tuple-element.39), channel_id=1, source_target_pairs={{0,1},{1,0},{2,3},{3,2},{4,5},{5,4},{6,7},{7,6},{8,9},{9,8},{10,11... | collective-permute-start | bytes 1572872 | tf_op jit(solution)/shard_map/ppermute | solution.py:295
  84.6 2.0 %collective-permute-start.15 = (f32[2,512,128]{2,1,0:T(8,128)S(1)}, f32[2,512,128]{2,1,0:T(8,128)S(1)}, u32[]{:S(2)}, u32[]{:S(2)}) collective-permute-start(f32[2,512,128]{2,1,0:T(8,128)S(1)} %get-tuple-element.40), channel_id=1, source_target_pairs={{0,1},{1,0},{2,3},{3,2},{4,5},{5,4},{6,7},{7,6},{8,9},{9,8},{10,11... | collective-permute-start | bytes 1572872 | tf_op jit(solution)/shard_map/ppermute | solution.py:295
  88.6 6.9 %collective-permute-start.17 = (f32[1,136,128]{2,1,0:T(8,128)S(1)}, f32[1,136,128]{2,1,0:T(8,128)S(1)}, u32[]{:S(2)}, u32[]{:S(2)}) collective-permute-start(f32[1,136,128]{2,1,0:T(8,128)S(1)} %get-tuple-element.61), channel_id=1, source_target_pairs={{0,4},{4,8},{8,12},{12,0},{1,5},{5,9},{9,13},{13,1},{2,6},{6,10},{... | collective-permute-start | bytes 208904 | tf_op jit(solution)/shard_map/ppermute | solution.py:242
  88.6 8.9 %collective-permute-start.18 = (f32[1,136,128]{2,1,0:T(8,128)S(1)}, f32[1,136,128]{2,1,0:T(8,128)S(1)}, u32[]{:S(2)}, u32[]{:S(2)}) collective-permute-start(f32[1,136,128]{2,1,0:T(8,128)S(1)} %get-tuple-element.60), channel_id=1, source_target_pairs={{0,8},{4,12},{8,0},{12,4},{1,9},{5,13},{9,1},{13,5},{2,10},{6,14},... | collective-permute-start | bytes 208904 | tf_op jit(solution)/shard_map/ppermute | solution.py:242
  89.4 8.1 %collective-permute-start.19 = (f32[1,136,128]{2,1,0:T(8,128)S(1)}, f32[1,136,128]{2,1,0:T(8,128)S(1)}, u32[]{:S(2)}, u32[]{:S(2)}) collective-permute-start(f32[1,136,128]{2,1,0:T(8,128)S(1)} %get-tuple-element.59), channel_id=1, source_target_pairs={{0,12},{4,0},{8,4},{12,8},{1,13},{5,1},{9,5},{13,9},{2,14},{6,2},{... | collective-permute-start | bytes 208904 | tf_op jit(solution)/shard_map/ppermute | solution.py:242
  97.8 3.8 %collective-permute-start.21 = (bf16[1,16,512]{2,1,0:T(8,128)(2,1)S(1)}, bf16[1,16,512]{2,1,0:T(8,128)(2,1)S(1)}, u32[]{:S(2)}, u32[]{:S(2)}) collective-permute-start(bf16[1,16,512]{2,1,0:T(8,128)(2,1)S(1)} %get-tuple-element.73), channel_id=1, source_target_pairs={{0,2},{2,0},{1,3},{3,1},{4,6},{6,4},{5,7},{7,5},{8,10},{10,8},{9,1... | collective-permute-start | bytes 49160 | tf_op jit(solution)/shard_map/ppermute | solution.py:356
  99.7 3.2 %collective-permute-start.22 = (bf16[1,16,512]{2,1,0:T(8,128)(2,1)S(1)}, bf16[1,16,512]{2,1,0:T(8,128)(2,1)S(1)}, u32[]{:S(2)}, u32[]{:S(2)}) collective-permute-start(bf16[1,16,512]{2,1,0:T(8,128)(2,1)S(1)} %get-tuple-element.73), channel_id=1, source_target_pairs={{0,3},{3,0},{1,2},{2,1},{4,7},{7,4},{5,6},{6,5},{8,11},{11,8},{9,1... | collective-permute-start | bytes 49160 | tf_op jit(solution)/shard_map/ppermute | solution.py:357
  99.7 1.2 %collective-permute-start.20 = (bf16[1,16,512]{2,1,0:T(8,128)(2,1)S(1)}, bf16[1,16,512]{2,1,0:T(8,128)(2,1)S(1)}, u32[]{:S(2)}, u32[]{:S(2)}) collective-permute-start(bf16[1,16,512]{2,1,0:T(8,128)(2,1)S(1)} %get-tuple-element.74.mine_ref), channel_id=1, source_target_pairs={{0,1},{1,0},{2,3},{3,2},{4,5},{5,4},{6,7},{7,6},{8,9},{9,8},{10,11... | collective-permute-start | bytes 49160 | tf_op jit(solution)/shard_map/ppermute | solution.py:355

commit v15 on v13

--- a/solution.py
+++ b/solution.py
@@ -11,6 +11,7 @@
 HEAD_DIM = 64
 EMPTY = -3e38
 FIRST_EIGHTHS = 4
+ROW_COPIES = 4
 VMEM_LIMIT = 22 * 1024 * 1024
 SWAP = [(0, 1), (1, 0)]
 CROSS = [(0, 3), (3, 0), (1, 2), (2, 1)]
@@ -25,7 +26,18 @@
     return picked
 
 
-def project_kernel(flag_ref, *refs, jobs, sends):
+def project_kernel(flag_ref, *refs, jobs, sends, copied):
+    copies = []
+    if copied:
+        *refs, rows_ref, semaphores = refs
+        step = rows_ref.shape[0] // ROW_COPIES
+        for part in range(ROW_COPIES):
+            rows = pl.ds(part * step, step)
+            copies.append(
+                pltpu.make_async_copy(refs[copied].at[rows], rows_ref.at[rows], semaphores.at[part])
+            )
+            copies[-1].start()
+        refs[copied] = rows_ref
     keep_ref, *send_refs = refs[-1 - len(sends) :]
     slots = [(ref, at) for ref in send_refs for at in range(ref.shape[0])]
     core, same = flag_ref[0], flag_ref[1]
@@ -42,6 +54,10 @@
             )
             keep = jnp.where(same == 1, first, second)
             send = jnp.where(same == 1, second, first)
+        if copied and rows_of == copied:
+            for copy in copies:
+                copy.wait()
+            copies = []
         product = lax.dot_general(
             refs[rows_of][...],
             jnp.concatenate([keep, send], axis=0),
@@ -184,14 +200,19 @@
     return [pl.BlockSpec(memory_space=pltpu.SMEM)] * count
 
 
-def project(flags, operands, jobs, sends, half, flops, name):
+def project(flags, operands, jobs, sends, half, flops, copied, name):
     rows, units = operands[0].shape
     shapes = [jax.ShapeDtypeStruct((count, rows, half), jnp.float32) for count in [len(jobs)] + sends]
+    placed = in_vmem(len(operands))
+    if copied:
+        placed[copied] = pl.BlockSpec(memory_space=pl.ANY)
+    rows_held = [pltpu.VMEM((rows, units), operands[0].dtype), pltpu.SemaphoreType.DMA((ROW_COPIES,))]
     return pl.pallas_call(
-        functools.partial(project_kernel, jobs=jobs, sends=sends),
+        functools.partial(project_kernel, jobs=jobs, sends=sends, copied=copied),
         out_shape=shapes,
-        in_specs=in_smem(1) + in_vmem(len(operands)),
+        in_specs=in_smem(1) + placed,
         out_specs=in_vmem(len(shapes)),
+        scratch_shapes=rows_held if copied else [],
         compiler_params=pltpu.CompilerParams(vmem_limit_bytes=VMEM_LIMIT),
         cost_estimate=pl.CostEstimate(flops=flops, bytes_accessed=1, transcendentals=0),
         name=name,
@@ -259,8 +280,9 @@
         for at in range(2):
             below.append(shifted(after(sent[at], below[-1:]), 1))
             above.append(shifted(after(sent[at], above[-1:] or below[:1]), -1))
-        opposite = [jnp.concatenate([shifted(after(below[0], below[1:]), 1), shifted(below[1], 1)], axis=0)]
+        opposite = [shifted(after(below[0], below[1:]), 1), shifted(below[1], 1)]
         around = [from_rows(piece[-1][-8:], queries.shape) for piece in (above, opposite, below)]
+        opposite = [jnp.concatenate([opposite[0], opposite[1][: lengths[1]]], axis=0)]
         queries = jnp.concatenate([queries] + around, axis=0)
         swapped = []
         for at, piece in enumerate([below[0], above[0], below[1], above[1]] + opposite):
@@ -279,6 +301,7 @@
             [2, 2, 2],
             half,
             24 * rows * half * units,
+            0,
             "project_near",
         )
         flags, kept, *away = lax.optimization_barrier((flags, kept, *away))
@@ -288,6 +311,7 @@
             [(source, [(2, half), (3, half)]) for source in range(2)],
             [2],
             half,
+            1,
             1,
             "project_far",
         )

time: 95.5 us -> 96.2 us (level)
  Pallas kernels: 12.7 us -> 14.3 us
  waiting for transfers between devices: 52.4 us -> 51.3 us
    pallas_call x2, Pallas kernels: 9.31 us -> 10.9 us  [project(): pl.pallas_call(functools.partial(project_kernel, jobs=jobs, sends=sends,...]
  transfers between devices with their start and end apart: 23 -> 23, of which waited for: 15 -> 13; matrix products, arithmetic and copies ran while one was open for 1% -> 1% of each run, Pallas kernels for 10% -> 11%
where the time goes in v15:
time: 96.2 us; the launch traced here: 96 us
  waiting for transfers between devices  51.3 us (53%)
  starting transfers between devices  28 us (29%)
  Pallas kernels  14.3 us (15%)
  local copies, waits for them, and re-layouts  1.59 us (2%)
    ppermute x9, waiting for transfers between devices, shifted(): lax.ppermute(array, 'high', [(at, (at + shift) % highs) for at in range(h...  34.5 us
    ppermute x9, starting transfers between devices, shifted(): lax.ppermute(array, 'high', [(at, (at + shift) % highs) for at in range(h...  15.7 us
    pallas_call x2, Pallas kernels, project(): pl.pallas_call(functools.partial(project_kernel, jobs=jobs, sends=sends,...  10.9 us
    ppermute x5, waiting for transfers between devices, body(): lax.ppermute(after(piece, swapped[max(at - 2, 0):max(at - 1, 0)]), 'group...  8.45 us
    ppermute x5, starting transfers between devices, body(): lax.ppermute(after(piece, swapped[max(at - 2, 0):max(at - 1, 0)]), 'group...  5.92 us
    ppermute x1, waiting for transfers between devices, body(): partner_hidden = lax.ppermute(hidden, 'side', SWAP)  4.97 us
    pallas_call x1, Pallas kernels, body(): pl.pallas_call(functools.partial(attend_kernel, pieces=pieces), out_shape...  1.99 us
  transfers between devices with their start and end apart: 23, of which 13 were waited for; matrix products, arithmetic and copies ran while one was open for 1% of the time, Pallas kernels for 11%

profile of v15, /device:TPU:0, one launch (start us, length us, event | category | flops | bytes accessed | tf_op | source)
XLA Modules:
  0.0 96.0 jit_solution(6125822174375598631)
XLA Ops:
  0.0 1.3 %constant_dynamic-slice_fusion.4 = (bf16[64,2560]{1,0:T(8,128)(2,1)S(1)}, bf16[64,2560]{1,0:T(8,128)(2,1)S(1)}) fusion(bf16[256,2560]{1,0:T(8,128)(2,1)} %refs_2_.1, s32[]{:T(128)S(6)} %select_n.73, s32[]{:T(128)S(6)} %select_n.72), kind=kLoop, calls=%fused_computation.23 | loop fusion | bytes 1310728 | tf_op jit(solution)/shard_map/dynamic_slice | solution.py:275
  1.3 3.1 %collective-permute-start = (bf16[64,2560]{1,0:T(8,128)(2,1)S(1)}, bf16[64,2560]{1,0:T(8,128)(2,1)S(1)}, u32[]{:S(2)}, u32[]{:S(2)}) collective-permute-start(bf16[64,2560]{1,0:T(8,128)(2,1)S(1)} %get-tuple-element.23), channel_id=1, source_target_pairs={{0,4},{4,8},{8,12},{12,0},{1,5},{5,9},{9,13},{13,1},{2,6},{6,10},{... | collective-permute-start | bytes 983048 | tf_op jit(solution)/shard_map/ppermute | solution.py:263
  4.4 1.5 %collective-permute-start.5 = (bf16[512,2560]{1,0:T(8,128)(2,1)}, bf16[512,2560]{1,0:T(8,128)(2,1)}, u32[]{:S(2)}, u32[]{:S(2)}) collective-permute-start(bf16[512,2560]{1,0:T(8,128)(2,1)} %bitcast.21), channel_id=1, source_target_pairs={{0,2},{2,0},{1,3},{3,1},{4,6},{6,4},{5,7},{7,5},{8,10},{10,8},{9,1... | collective-permute-start | bytes 7864328 | tf_op jit(solution)/shard_map/ppermute | solution.py:266
  6.1 8.0 %collective-permute-done.refs_7_ = bf16[64,2560]{1,0:T(8,128)(2,1)S(1)} collective-permute-done((bf16[64,2560]{1,0:T(8,128)(2,1)S(1)}, bf16[64,2560]{1,0:T(8,128)(2,1)S(1)}, u32[]{:S(2)}, u32[]{:S(2)}) %collective-permute-start) | collective-permute-done | bytes 327712 | tf_op jit(solution)/shard_map/ppermute | solution.py:263
  14.1 3.8 %collective-permute-start.1 = (bf16[64,2560]{1,0:T(8,128)(2,1)}, bf16[64,2560]{1,0:T(8,128)(2,1)S(1)}, u32[]{:S(2)}, u32[]{:S(2)}) collective-permute-start(bf16[64,2560]{1,0:T(8,128)(2,1)} %copy-done.3), channel_id=1, source_target_pairs={{0,12},{4,0},{8,4},{12,8},{1,13},{5,1},{9,5},{13,9},{2,14},{6,2},{... | collective-permute-start | bytes 983048 | tf_op jit(solution)/shard_map/ppermute | solution.py:263
  18.0 1.5 %collective-permute-start.8 = (bf16[64,2560]{1,0:T(8,128)(2,1)S(1)}, bf16[64,2560]{1,0:T(8,128)(2,1)S(1)}, u32[]{:S(2)}, u32[]{:S(2)}) collective-permute-start(bf16[64,2560]{1,0:T(8,128)(2,1)S(1)} %collective-permute-done.refs_7_), channel_id=1, source_target_pairs={{0,16},{16,0},{1,17},{17,1},{2,18},{18,2},{3,19},{19,3},{4,20},{20... | collective-permute-start | bytes 983048 | tf_op jit(solution)/shard_map/ppermute | solution.py:289
  19.8 11.4 %collective-permute-done.1.refs_3_ = bf16[64,2560]{1,0:T(8,128)(2,1)S(1)} collective-permute-done((bf16[64,2560]{1,0:T(8,128)(2,1)}, bf16[64,2560]{1,0:T(8,128)(2,1)S(1)}, u32[]{:S(2)}, u32[]{:S(2)}) %collective-permute-start.1) | collective-permute-done | bytes 327712 | tf_op jit(solution)/shard_map/ppermute | solution.py:263
  31.1 1.9 %collective-permute-start.2 = (bf16[72,2560]{1,0:T(8,128)(2,1)S(1)}, bf16[72,2560]{1,0:T(8,128)(2,1)S(1)}, u32[]{:S(2)}, u32[]{:S(2)}) collective-permute-start(bf16[72,2560]{1,0:T(8,128)(2,1)S(1)} %pad_maximum_fusion.2), channel_id=1, source_target_pairs={{0,12},{4,0},{8,4},{12,8},{1,13},{5,1},{9,5},{13,9},{2,14},{6,2},{... | collective-permute-start | bytes 1105928 | tf_op jit(solution)/shard_map/ppermute | solution.py:263
  33.1 1.3 %collective-permute-start.6 = (bf16[64,2560]{1,0:T(8,128)(2,1)S(1)}, bf16[64,2560]{1,0:T(8,128)(2,1)S(1)}, u32[]{:S(2)}, u32[]{:S(2)}) collective-permute-start(bf16[64,2560]{1,0:T(8,128)(2,1)S(1)} %collective-permute-done.1.refs_3_), channel_id=1, source_target_pairs={{0,16},{16,0},{1,17},{17,1},{2,18},{18,2},{3,19},{19,3},{4,20},{20... | collective-permute-start | bytes 983048 | tf_op jit(solution)/shard_map/ppermute | solution.py:289
  34.4 0.8 collective-permute-start.9
  35.3 8.4 %collective-permute-done.6.refs_5_ = bf16[64,2560]{1,0:T(8,128)(2,1)S(1)} collective-permute-done((bf16[64,2560]{1,0:T(8,128)(2,1)S(1)}, bf16[64,2560]{1,0:T(8,128)(2,1)S(1)}, u32[]{:S(2)}, u32[]{:S(2)}) %collective-permute-start.6) | collective-permute-done | bytes 327712 | tf_op jit(solution)/shard_map/ppermute | solution.py:289
  43.9 1.3 %collective-permute-start.7 = (bf16[72,2560]{1,0:T(8,128)(2,1)S(1)}, bf16[72,2560]{1,0:T(8,128)(2,1)S(1)}, u32[]{:S(2)}, u32[]{:S(2)}) collective-permute-start(bf16[72,2560]{1,0:T(8,128)(2,1)S(1)} %collective-permute-done.2.refs_4_), channel_id=1, source_target_pairs={{0,16},{16,0},{1,17},{17,1},{2,18},{18,2},{3,19},{19,3},{4,20},{20... | collective-permute-start | bytes 1105928 | tf_op jit(solution)/shard_map/ppermute | solution.py:289
  45.2 7.0 %collective-permute-done.4 = bf16[72,2560]{1,0:T(8,128)(2,1)S(1)} collective-permute-done((bf16[72,2560]{1,0:T(8,128)(2,1)S(1)}, bf16[72,2560]{1,0:T(8,128)(2,1)S(1)}, u32[]{:S(2)}, u32[]{:S(2)}) %collective-permute-start.4) | collective-permute-done | bytes 368672 | tf_op jit(solution)/shard_map/ppermute | solution.py:263
  52.2 4.5 %collective-permute-done.10 = bf16[64,2560]{1,0:T(8,128)(2,1)S(1)} collective-permute-done((bf16[64,2560]{1,0:T(8,128)(2,1)S(1)}, bf16[64,2560]{1,0:T(8,128)(2,1)S(1)}, u32[]{:S(2)}, u32[]{:S(2)}) %collective-permute-start.10) | collective-permute-done | bytes 327712 | tf_op jit(solution)/shard_map/ppermute | solution.py:263
  56.7 1.1 %collective-permute-start.11 = (bf16[128,2560]{1,0:T(8,128)(2,1)S(1)}, bf16[128,2560]{1,0:T(8,128)(2,1)S(1)}, u32[]{:S(2)}, u32[]{:S(2)}) collective-permute-start(bf16[128,2560]{1,0:T(8,128)(2,1)S(1)} %pad_maximum_fusion.refs_2_), channel_id=1, source_target_pairs={{0,16},{16,0},{1,17},{17,1},{2,18},{18,2},{3,19},{19,3},{4,20},{20... | collective-permute-start | bytes 1966088 | tf_op jit(solution)/shard_map/ppermute | solution.py:289
  58.0 1.6 %collective-permute-start.16 = (bf16[576,512]{1,0:T(8,128)(2,1)S(1)}, bf16[576,512]{1,0:T(8,128)(2,1)S(1)}, u32[]{:S(2)}, u32[]{:S(2)}) collective-permute-start(bf16[576,512]{1,0:T(8,128)(2,1)S(1)} %pad_maximum_fusion.1), channel_id=1, source_target_pairs={{0,2},{2,0},{1,3},{3,1},{4,6},{6,4},{5,7},{7,5},{8,10},{10,8},{9,1... | collective-permute-start | bytes 1769480 | tf_op jit(solution)/shard_map/ppermute | solution.py:352
  59.5 5.0 %collective-permute-done.5.refs_1_ = bf16[512,2560]{1,0:T(8,128)(2,1)} collective-permute-done((bf16[512,2560]{1,0:T(8,128)(2,1)}, bf16[512,2560]{1,0:T(8,128)(2,1)}, u32[]{:S(2)}, u32[]{:S(2)}) %collective-permute-start.5) | collective-permute-done | bytes 2621472 | tf_op jit(solution)/shard_map/ppermute | solution.py:266
  64.5 6.0 %project_near.1 = (f32[6,512,128]{2,1,0:T(8,128)S(1)}, f32[2,512,128]{2,1,0:T(8,128)S(1)}, f32[2,512,128]{2,1,0:T(8,128)S(1)}, f32[2,512,128]{2,1,0:T(8,128)S(1)}) custom-call(s32[2]{0:T(128)S(1)} %pad_add_fusion.3.flag_ref, bf16[512,2560]{1,0:T(8,128)(2,1)S(1)} %bitcast.22, bf16[512,2560]{1,0:T(8,128)(2,1)} %collective-permute-done.5.refs_1_, ...), custom_call_target="tpu_custom_call" | custom-call | flops 4026531840 | bytes 1 | tf_op jit(solution)/shard_map/project_near/pallas_call | solution.py:210
  70.6 0.5 collective-permute-start.13
  71.2 4.9 %project_far.1 = (f32[2,512,128]{2,1,0:T(8,128)S(1)}, f32[2,512,128]{2,1,0:T(8,128)S(1)}) custom-call(s32[2]{0:T(128)S(1)} %pad_add_fusion.3.flag_ref, bf16[512,2560]{1,0:T(8,128)(2,1)S(1)} %bitcast.23, bf16[512,2560]{1,0:T(8,128)(2,1)} %collective-permute-done.5.refs_1_, bf16[128,2560]{1,0:T(8,128)(2,1)S(1)} %pad_maximum_fusion.refs_2_, ...), custom_call_target="tpu_custom_call" | custom-call | flops 1 | bytes 1 | tf_op jit(solution)/shard_map/project_far/pallas_call | solution.py:210
  76.7 1.5 %collective-permute-done.15.refs_5_ = f32[2,512,128]{2,1,0:T(8,128)S(1)} collective-permute-done((f32[2,512,128]{2,1,0:T(8,128)S(1)}, f32[2,512,128]{2,1,0:T(8,128)S(1)}, u32[]{:S(2)}, u32[]{:S(2)}) %collective-permute-start.15) | collective-permute-done | bytes 524320 | tf_op jit(solution)/shard_map/ppermute | solution.py:318
  78.1 2.0 %attend.1 = f32[4,136,128]{2,1,0:T(8,128)S(1)} custom-call(s32[4]{0:T(128)S(1)} %pad_add_fusion.2.place_ref, s32[2,4]{1,0:T(2,128)S(1)} %pad_add_fusion.spot_ref, bf16[4,16,512]{2,1,0:T(8,128)(2,1)S(1)} %get-tuple-element.66.query_ref, f32[6,512,128]{2,1,0:T(8,128)S(1)} %get-tuple-element.32.refs_0_, f32[2,512,128]{2,1,0:T(8,128)S(1)} %get-tuple-element.36.refs_1_, ...), custom_call_target="tpu_custom_call" | custom-call | tf_op jit(solution)/shard_map/attend/pallas_call | solution.py:355
  80.2 1.6 %collective-permute-start.17 = (f32[1,136,128]{2,1,0:T(8,128)S(1)}, f32[1,136,128]{2,1,0:T(8,128)S(1)}, u32[]{:S(2)}, u32[]{:S(2)}) collective-permute-start(f32[1,136,128]{2,1,0:T(8,128)S(1)} %get-tuple-element.63), channel_id=1, source_target_pairs={{0,4},{4,8},{8,12},{12,0},{1,5},{5,9},{9,13},{13,1},{2,6},{6,10},{... | collective-permute-start | bytes 208904 | tf_op jit(solution)/shard_map/ppermute | solution.py:263
  81.8 3.4 %collective-permute-start.18 = (f32[1,136,128]{2,1,0:T(8,128)S(1)}, f32[1,136,128]{2,1,0:T(8,128)S(1)}, u32[]{:S(2)}, u32[]{:S(2)}) collective-permute-start(f32[1,136,128]{2,1,0:T(8,128)S(1)} %get-tuple-element.62), channel_id=1, source_target_pairs={{0,8},{4,12},{8,0},{12,4},{1,9},{5,13},{9,1},{13,5},{2,10},{6,14},... | collective-permute-start | bytes 208904 | tf_op jit(solution)/shard_map/ppermute | solution.py:263
  85.3 1.5 %collective-permute-start.19 = (f32[1,136,128]{2,1,0:T(8,128)S(1)}, f32[1,136,128]{2,1,0:T(8,128)S(1)}, u32[]{:S(2)}, u32[]{:S(2)}) collective-permute-start(f32[1,136,128]{2,1,0:T(8,128)S(1)} %get-tuple-element.61), channel_id=1, source_target_pairs={{0,12},{4,0},{8,4},{12,8},{1,13},{5,1},{9,5},{13,9},{2,14},{6,2},{... | collective-permute-start | bytes 208904 | tf_op jit(solution)/shard_map/ppermute | solution.py:263
  86.8 0.5 collective-permute-done.17.refs_1_
  87.3 3.0 %collective-permute-done.18.refs_2_ = f32[1,136,128]{2,1,0:T(8,128)S(1)} collective-permute-done((f32[1,136,128]{2,1,0:T(8,128)S(1)}, f32[1,136,128]{2,1,0:T(8,128)S(1)}, u32[]{:S(2)}, u32[]{:S(2)}) %collective-permute-start.18) | collective-permute-done | bytes 69664 | tf_op jit(solution)/shard_map/ppermute | solution.py:263
  90.7 1.0 %collective-permute-start.21 = (bf16[1,16,512]{2,1,0:T(8,128)(2,1)S(1)}, bf16[1,16,512]{2,1,0:T(8,128)(2,1)S(1)}, u32[]{:S(2)}, u32[]{:S(2)}) collective-permute-start(bf16[1,16,512]{2,1,0:T(8,128)(2,1)S(1)} %get-tuple-element.75), channel_id=1, source_target_pairs={{0,2},{2,0},{1,3},{3,1},{4,6},{6,4},{5,7},{7,5},{8,10},{10,8},{9,1... | collective-permute-start | bytes 49160 | tf_op jit(solution)/shard_map/ppermute | solution.py:379
  91.9 1.0 %collective-permute-start.20 = (bf16[1,16,512]{2,1,0:T(8,128)(2,1)S(1)}, bf16[1,16,512]{2,1,0:T(8,128)(2,1)S(1)}, u32[]{:S(2)}, u32[]{:S(2)}) collective-permute-start(bf16[1,16,512]{2,1,0:T(8,128)(2,1)S(1)} %get-tuple-element.76.mine_ref), channel_id=1, source_target_pairs={{0,1},{1,0},{2,3},{3,2},{4,5},{5,4},{6,7},{7,6},{8,9},{9,8},{10,11... | collective-permute-start | bytes 49160 | tf_op jit(solution)/shard_map/ppermute | solution.py:378
  93.0 0.8 collective-permute-done.20.core_ref
  93.7 0.8 collective-permute-done.21.side_ref
  94.9 1.2 %assemble.1 = bf16[1,16,2048]{2,1,0:T(8,128)(2,1)} custom-call(s32[2]{0:T(128)S(1)} %pad_add_fusion.1.flag_ref, bf16[1,16,512]{2,1,0:T(8,128)(2,1)S(1)} %get-tuple-element.76.mine_ref, bf16[1,16,512]{2,1,0:T(8,128)(2,1)S(1)} %collective-permute-done.20.core_ref, bf16[1,16,512]{2,1,0:T(8,128)(2,1)S(1)} %collective-permute-done.21.side_ref, ...), custom_call_target="tpu_custom_call" | custom-call | tf_op jit(solution)/shard_map/assemble/pallas_call | solution.py:387
  (65 shorter events, 2.8 us)
Async XLA Ops:
  0.0 5.9 %copy-start.4 = (bf16[1,16,2048]{2,1,0:T(8,128)(2,1)S(1)}, bf16[1,16,2048]{2,1,0:T(8,128)(2,1)}, u32[]{:S(2)}) copy-start(bf16[1,16,2048]{2,1,0:T(8,128)(2,1)} %param.12) | copy-start | bytes 196612
  0.0 5.9 %copy-start.6 = (s32[8]{0:T(128)S(1)}, s32[8]{0:T(128)}, u32[]{:S(2)}) copy-start(s32[8]{0:T(128)} %param.11) | copy-start | bytes 100
  0.0 5.9 %copy-start.7 = (s32[16,1]{0,1:T(1,128)S(1)}, s32[16,1]{0,1:T(1,128)}, u32[]{:S(2)}) copy-start(s32[16,1]{0,1:T(1,128)} %param.10) | copy-start | bytes 196
  0.0 19.6 %copy-start = (bf16[2,256,2048]{2,1,0:T(8,128)(2,1)S(1)}, bf16[2,256,2048]{2,1,0:T(8,128)(2,1)}, u32[]{:S(2)}) copy-start(bf16[2,256,2048]{2,1,0:T(8,128)(2,1)} %param.8) | copy-start | bytes 6291460
  1.3 4.8 %copy-start.3 = (bf16[64,2560]{1,0:T(8,128)(2,1)}, bf16[64,2560]{1,0:T(8,128)(2,1)S(1)}, u32[]{:S(2)}) copy-start(bf16[64,2560]{1,0:T(8,128)(2,1)S(1)} %get-tuple-element.23) | copy-start | bytes 983044
  1.3 12.8 %collective-permute-start = (bf16[64,2560]{1,0:T(8,128)(2,1)S(1)}, bf16[64,2560]{1,0:T(8,128)(2,1)S(1)}, u32[]{:S(2)}, u32[]{:S(2)}) collective-permute-start(bf16[64,2560]{1,0:T(8,128)(2,1)S(1)} %get-tuple-element.23), channel_id=1, source_target_pairs={{0,4},{4,8},{8,12},{12,0},{1,5},{5,9},{9,13},{13,1},{2,6},{6,10},{... | collective-permute-start | bytes 983048 | tf_op jit(solution)/shard_map/ppermute | solution.py:263
  4.4 60.1 %collective-permute-start.5 = (bf16[512,2560]{1,0:T(8,128)(2,1)}, bf16[512,2560]{1,0:T(8,128)(2,1)}, u32[]{:S(2)}, u32[]{:S(2)}) collective-permute-start(bf16[512,2560]{1,0:T(8,128)(2,1)} %bitcast.21), channel_id=1, source_target_pairs={{0,2},{2,0},{1,3},{3,1},{4,6},{6,4},{5,7},{7,5},{8,10},{10,8},{9,1... | collective-permute-start | bytes 7864328 | tf_op jit(solution)/shard_map/ppermute | solution.py:266
  14.1 20.2 %collective-permute-start.3 = (bf16[72,2560]{1,0:T(8,128)(2,1)S(1)}, bf16[72,2560]{1,0:T(8,128)(2,1)S(1)}, u32[]{:S(2)}, u32[]{:S(2)}) collective-permute-start(bf16[72,2560]{1,0:T(8,128)(2,1)S(1)} %pad_maximum_fusion.2), channel_id=1, source_target_pairs={{0,4},{4,8},{8,12},{12,0},{1,5},{5,9},{9,13},{13,1},{2,6},{6,10},{... | collective-permute-start | bytes 1105928 | tf_op jit(solution)/shard_map/ppermute | solution.py:263
  14.1 17.0 %collective-permute-start.1 = (bf16[64,2560]{1,0:T(8,128)(2,1)}, bf16[64,2560]{1,0:T(8,128)(2,1)S(1)}, u32[]{:S(2)}, u32[]{:S(2)}) collective-permute-start(bf16[64,2560]{1,0:T(8,128)(2,1)} %copy-done.3), channel_id=1, source_target_pairs={{0,12},{4,0},{8,4},{12,8},{1,13},{5,1},{9,5},{13,9},{2,14},{6,2},{... | collective-permute-start | bytes 983048 | tf_op jit(solution)/shard_map/ppermute | solution.py:263
  18.0 16.3 %collective-permute-start.8 = (bf16[64,2560]{1,0:T(8,128)(2,1)S(1)}, bf16[64,2560]{1,0:T(8,128)(2,1)S(1)}, u32[]{:S(2)}, u32[]{:S(2)}) collective-permute-start(bf16[64,2560]{1,0:T(8,128)(2,1)S(1)} %collective-permute-done.refs_7_), channel_id=1, source_target_pairs={{0,16},{16,0},{1,17},{17,1},{2,18},{18,2},{3,19},{19,3},{4,20},{20... | collective-permute-start | bytes 983048 | tf_op jit(solution)/shard_map/ppermute | solution.py:289
  31.1 12.8 %collective-permute-start.2 = (bf16[72,2560]{1,0:T(8,128)(2,1)S(1)}, bf16[72,2560]{1,0:T(8,128)(2,1)S(1)}, u32[]{:S(2)}, u32[]{:S(2)}) collective-permute-start(bf16[72,2560]{1,0:T(8,128)(2,1)S(1)} %pad_maximum_fusion.2), channel_id=1, source_target_pairs={{0,12},{4,0},{8,4},{12,8},{1,13},{5,1},{9,5},{13,9},{2,14},{6,2},{... | collective-permute-start | bytes 1105928 | tf_op jit(solution)/shard_map/ppermute | solution.py:263
  33.1 10.6 %collective-permute-start.6 = (bf16[64,2560]{1,0:T(8,128)(2,1)S(1)}, bf16[64,2560]{1,0:T(8,128)(2,1)S(1)}, u32[]{:S(2)}, u32[]{:S(2)}) collective-permute-start(bf16[64,2560]{1,0:T(8,128)(2,1)S(1)} %collective-permute-done.1.refs_3_), channel_id=1, source_target_pairs={{0,16},{16,0},{1,17},{17,1},{2,18},{18,2},{3,19},{19,3},{4,20},{20... | collective-permute-start | bytes 983048 | tf_op jit(solution)/shard_map/ppermute | solution.py:289
  34.4 22.4 %collective-permute-start.9 = (bf16[72,2560]{1,0:T(8,128)(2,1)S(1)}, bf16[72,2560]{1,0:T(8,128)(2,1)S(1)}, u32[]{:S(2)}, u32[]{:S(2)}) collective-permute-start(bf16[72,2560]{1,0:T(8,128)(2,1)S(1)} %collective-permute-done.3.refs_8_), channel_id=1, source_target_pairs={{0,16},{16,0},{1,17},{17,1},{2,18},{18,2},{3,19},{19,3},{4,20},{20... | collective-permute-start | bytes 1105928 | tf_op jit(solution)/shard_map/ppermute | solution.py:289
  35.1 17.1 %collective-permute-start.4 = (bf16[72,2560]{1,0:T(8,128)(2,1)S(1)}, bf16[72,2560]{1,0:T(8,128)(2,1)S(1)}, u32[]{:S(2)}, u32[]{:S(2)}) collective-permute-start(bf16[72,2560]{1,0:T(8,128)(2,1)S(1)} %collective-permute-done.3.refs_8_), channel_id=1, source_target_pairs={{0,4},{4,8},{8,12},{12,0},{1,5},{5,9},{9,13},{13,1},{2,6},{6,10},{... | collective-permute-start | bytes 1105928 | tf_op jit(solution)/shard_map/ppermute | solution.py:263
  43.7 13.0 %collective-permute-start.10 = (bf16[64,2560]{1,0:T(8,128)(2,1)S(1)}, bf16[64,2560]{1,0:T(8,128)(2,1)S(1)}, u32[]{:S(2)}, u32[]{:S(2)}) collective-permute-start(bf16[64,2560]{1,0:T(8,128)(2,1)S(1)} %collective-permute-done.refs_7_), channel_id=1, source_target_pairs={{0,4},{4,8},{8,12},{12,0},{1,5},{5,9},{9,13},{13,1},{2,6},{6,10},{... | collective-permute-start | bytes 983048 | tf_op jit(solution)/shard_map/ppermute | solution.py:263
  43.9 15.6 %collective-permute-start.7 = (bf16[72,2560]{1,0:T(8,128)(2,1)S(1)}, bf16[72,2560]{1,0:T(8,128)(2,1)S(1)}, u32[]{:S(2)}, u32[]{:S(2)}) collective-permute-start(bf16[72,2560]{1,0:T(8,128)(2,1)S(1)} %collective-permute-done.2.refs_4_), channel_id=1, source_target_pairs={{0,16},{16,0},{1,17},{17,1},{2,18},{18,2},{3,19},{19,3},{4,20},{20... | collective-permute-start | bytes 1105928 | tf_op jit(solution)/shard_map/ppermute | solution.py:289
  45.2 19.3 %copy-start.2 = (bf16[256,2560]{1,0:T(8,128)(2,1)S(1)}, bf16[256,2560]{1,0:T(8,128)(2,1)}, u32[]{:S(2)}) copy-start(bf16[256,2560]{1,0:T(8,128)(2,1)} %refs_2_.1) | copy-start | bytes 3932164
  52.2 12.3 %copy-start.1 = (bf16[2,256,2560]{2,1,0:T(8,128)(2,1)S(1)}, bf16[2,256,2560]{2,1,0:T(8,128)(2,1)}, u32[]{:S(2)}) copy-start(bf16[2,256,2560]{2,1,0:T(8,128)(2,1)} %param.7) | copy-start | bytes 7864324
  56.7 14.4 %collective-permute-start.11 = (bf16[128,2560]{1,0:T(8,128)(2,1)S(1)}, bf16[128,2560]{1,0:T(8,128)(2,1)S(1)}, u32[]{:S(2)}, u32[]{:S(2)}) collective-permute-start(bf16[128,2560]{1,0:T(8,128)(2,1)S(1)} %pad_maximum_fusion.refs_2_), channel_id=1, source_target_pairs={{0,16},{16,0},{1,17},{17,1},{2,18},{18,2},{3,19},{19,3},{4,20},{20... | collective-permute-start | bytes 1966088 | tf_op jit(solution)/shard_map/ppermute | solution.py:289
  58.0 18.7 %collective-permute-start.16 = (bf16[576,512]{1,0:T(8,128)(2,1)S(1)}, bf16[576,512]{1,0:T(8,128)(2,1)S(1)}, u32[]{:S(2)}, u32[]{:S(2)}) collective-permute-start(bf16[576,512]{1,0:T(8,128)(2,1)S(1)} %pad_maximum_fusion.1), channel_id=1, source_target_pairs={{0,2},{2,0},{1,3},{3,1},{4,6},{6,4},{5,7},{7,5},{8,10},{10,8},{9,1... | collective-permute-start | bytes 1769480 | tf_op jit(solution)/shard_map/ppermute | solution.py:352
  70.5 6.1 %copy-start.5 = (s32[4]{0:T(128)S(1)}, s32[4]{0:T(128)}, u32[]{:S(2)}) copy-start(s32[4]{0:T(128)} %constant.97.clone) | copy-start | bytes 52
  70.5 6.1 %collective-permute-start.12 = (f32[2,512,128]{2,1,0:T(8,128)S(1)}, f32[2,512,128]{2,1,0:T(8,128)S(1)}, u32[]{:S(2)}, u32[]{:S(2)}) collective-permute-start(f32[2,512,128]{2,1,0:T(8,128)S(1)} %get-tuple-element.37), channel_id=1, source_target_pairs={{0,1},{1,0},{2,3},{3,2},{4,5},{5,4},{6,7},{7,6},{8,9},{9,8},{10,11... | collective-permute-start | bytes 1572872 | tf_op jit(solution)/shard_map/ppermute | solution.py:318
  70.6 6.1 %collective-permute-start.13 = (f32[2,512,128]{2,1,0:T(8,128)S(1)}, f32[2,512,128]{2,1,0:T(8,128)S(1)}, u32[]{:S(2)}, u32[]{:S(2)}) collective-permute-start(f32[2,512,128]{2,1,0:T(8,128)S(1)} %get-tuple-element.38), channel_id=1, source_target_pairs={{0,1},{1,0},{2,3},{3,2},{4,5},{5,4},{6,7},{7,6},{8,9},{9,8},{10,11... | collective-permute-start | bytes 1572872 | tf_op jit(solution)/shard_map/ppermute | solution.py:318
  71.1 5.6 %collective-permute-start.14 = (f32[2,512,128]{2,1,0:T(8,128)S(1)}, f32[2,512,128]{2,1,0:T(8,128)S(1)}, u32[]{:S(2)}, u32[]{:S(2)}) collective-permute-start(f32[2,512,128]{2,1,0:T(8,128)S(1)} %get-tuple-element.39), channel_id=1, source_target_pairs={{0,1},{1,0},{2,3},{3,2},{4,5},{5,4},{6,7},{7,6},{8,9},{9,8},{10,11... | collective-permute-start | bytes 1572872 | tf_op jit(solution)/shard_map/ppermute | solution.py:318
  76.1 2.0 %collective-permute-start.15 = (f32[2,512,128]{2,1,0:T(8,128)S(1)}, f32[2,512,128]{2,1,0:T(8,128)S(1)}, u32[]{:S(2)}, u32[]{:S(2)}) collective-permute-start(f32[2,512,128]{2,1,0:T(8,128)S(1)} %get-tuple-element.40), channel_id=1, source_target_pairs={{0,1},{1,0},{2,3},{3,2},{4,5},{5,4},{6,7},{7,6},{8,9},{9,8},{10,11... | collective-permute-start | bytes 1572872 | tf_op jit(solution)/shard_map/ppermute | solution.py:318
  80.2 7.1 %collective-permute-start.17 = (f32[1,136,128]{2,1,0:T(8,128)S(1)}, f32[1,136,128]{2,1,0:T(8,128)S(1)}, u32[]{:S(2)}, u32[]{:S(2)}) collective-permute-start(f32[1,136,128]{2,1,0:T(8,128)S(1)} %get-tuple-element.63), channel_id=1, source_target_pairs={{0,4},{4,8},{8,12},{12,0},{1,5},{5,9},{9,13},{13,1},{2,6},{6,10},{... | collective-permute-start | bytes 208904 | tf_op jit(solution)/shard_map/ppermute | solution.py:263
  81.8 8.4 %collective-permute-start.18 = (f32[1,136,128]{2,1,0:T(8,128)S(1)}, f32[1,136,128]{2,1,0:T(8,128)S(1)}, u32[]{:S(2)}, u32[]{:S(2)}) collective-permute-start(f32[1,136,128]{2,1,0:T(8,128)S(1)} %get-tuple-element.62), channel_id=1, source_target_pairs={{0,8},{4,12},{8,0},{12,4},{1,9},{5,13},{9,1},{13,5},{2,10},{6,14},... | collective-permute-start | bytes 208904 | tf_op jit(solution)/shard_map/ppermute | solution.py:263
  85.3 5.2 %collective-permute-start.19 = (f32[1,136,128]{2,1,0:T(8,128)S(1)}, f32[1,136,128]{2,1,0:T(8,128)S(1)}, u32[]{:S(2)}, u32[]{:S(2)}) collective-permute-start(f32[1,136,128]{2,1,0:T(8,128)S(1)} %get-tuple-element.61), channel_id=1, source_target_pairs={{0,12},{4,0},{8,4},{12,8},{1,13},{5,1},{9,5},{13,9},{2,14},{6,2},{... | collective-permute-start | bytes 208904 | tf_op jit(solution)/shard_map/ppermute | solution.py:263
  90.7 3.8 %collective-permute-start.21 = (bf16[1,16,512]{2,1,0:T(8,128)(2,1)S(1)}, bf16[1,16,512]{2,1,0:T(8,128)(2,1)S(1)}, u32[]{:S(2)}, u32[]{:S(2)}) collective-permute-start(bf16[1,16,512]{2,1,0:T(8,128)(2,1)S(1)} %get-tuple-element.75), channel_id=1, source_target_pairs={{0,2},{2,0},{1,3},{3,1},{4,6},{6,4},{5,7},{7,5},{8,10},{10,8},{9,1... | collective-permute-start | bytes 49160 | tf_op jit(solution)/shard_map/ppermute | solution.py:379
  91.7 3.2 %collective-permute-start.22 = (bf16[1,16,512]{2,1,0:T(8,128)(2,1)S(1)}, bf16[1,16,512]{2,1,0:T(8,128)(2,1)S(1)}, u32[]{:S(2)}, u32[]{:S(2)}) collective-permute-start(bf16[1,16,512]{2,1,0:T(8,128)(2,1)S(1)} %get-tuple-element.75), channel_id=1, source_target_pairs={{0,3},{3,0},{1,2},{2,1},{4,7},{7,4},{5,6},{6,5},{8,11},{11,8},{9,1... | collective-permute-start | bytes 49160 | tf_op jit(solution)/shard_map/ppermute | solution.py:380
  91.9 1.9 %collective-permute-start.20 = (bf16[1,16,512]{2,1,0:T(8,128)(2,1)S(1)}, bf16[1,16,512]{2,1,0:T(8,128)(2,1)S(1)}, u32[]{:S(2)}, u32[]{:S(2)}) collective-permute-start(bf16[1,16,512]{2,1,0:T(8,128)(2,1)S(1)} %get-tuple-element.76.mine_ref), channel_id=1, source_target_pairs={{0,1},{1,0},{2,3},{3,2},{4,5},{5,4},{6,7},{7,6},{8,9},{9,8},{10,11... | collective-permute-start | bytes 49160 | tf_op jit(solution)/shard_map/ppermute | solution.py:378

commit v16 on v13

--- a/solution.py
+++ b/solution.py
@@ -259,8 +259,9 @@
         for at in range(2):
             below.append(shifted(after(sent[at], below[-1:]), 1))
             above.append(shifted(after(sent[at], above[-1:] or below[:1]), -1))
-        opposite = [jnp.concatenate([shifted(after(below[0], below[1:]), 1), shifted(below[1], 1)], axis=0)]
+        opposite = [shifted(after(below[0], below[1:]), 1), shifted(below[1], 1)]
         around = [from_rows(piece[-1][-8:], queries.shape) for piece in (above, opposite, below)]
+        opposite = [jnp.concatenate([opposite[0], opposite[1][: lengths[1]]], axis=0)]
         queries = jnp.concatenate([queries] + around, axis=0)
         swapped = []
         for at, piece in enumerate([below[0], above[0], below[1], above[1]] + opposite):

time: 95.5 us -> 94.6 us (level)
  waiting for transfers between devices: 52.4 us -> 51.3 us
  transfers between devices with their start and end apart: 23 -> 23, of which waited for: 15 -> 14; matrix products, arithmetic and copies ran while one was open for 1% -> 1% of each run, Pallas kernels for 10% -> 10%
where the time goes in v16:
time: 94.6 us; the launch traced here: 94.4 us
  waiting for transfers between devices  51.3 us (54%)
  starting transfers between devices  28 us (30%)
  Pallas kernels  12.7 us (13%)
  local copies, waits for them, and re-layouts  1.59 us (2%)
    ppermute x9, waiting for transfers between devices, shifted(): lax.ppermute(array, 'high', [(at, (at + shift) % highs) for at in range(h...  34.5 us
    ppermute x9, starting transfers between devices, shifted(): lax.ppermute(array, 'high', [(at, (at + shift) % highs) for at in range(h...  15.7 us
    pallas_call x2, Pallas kernels, project(): pl.pallas_call(functools.partial(project_kernel, jobs=jobs, sends=sends),...  9.32 us
    ppermute x5, waiting for transfers between devices, body(): lax.ppermute(after(piece, swapped[max(at - 2, 0):max(at - 1, 0)]), 'group...  8.45 us
    ppermute x5, starting transfers between devices, body(): lax.ppermute(after(piece, swapped[max(at - 2, 0):max(at - 1, 0)]), 'group...  5.92 us
    ppermute x1, waiting for transfers between devices, body(): partner_hidden = lax.ppermute(hidden, 'side', SWAP)  4.97 us
    pallas_call x1, Pallas kernels, body(): pl.pallas_call(functools.partial(attend_kernel, pieces=pieces), out_shape...  2 us
  transfers between devices with their start and end apart: 23, of which 14 were waited for; matrix products, arithmetic and copies ran while one was open for 1% of the time, Pallas kernels for 10%

profile of v16, /device:TPU:0, one launch (start us, length us, event | category | flops | bytes accessed | tf_op | source)
XLA Modules:
  0.0 94.4 jit_solution(9590566036767870832)
XLA Ops:
  0.0 1.3 %constant_dynamic-slice_fusion.4 = (bf16[64,2560]{1,0:T(8,128)(2,1)S(1)}, bf16[64,2560]{1,0:T(8,128)(2,1)S(1)}) fusion(bf16[256,2560]{1,0:T(8,128)(2,1)} %refs_2_.1, s32[]{:T(128)S(6)} %select_n.73, s32[]{:T(128)S(6)} %select_n.72), kind=kLoop, calls=%fused_computation.23 | loop fusion | bytes 1310728 | tf_op jit(solution)/shard_map/dynamic_slice | solution.py:254
  1.3 3.1 %collective-permute-start = (bf16[64,2560]{1,0:T(8,128)(2,1)S(1)}, bf16[64,2560]{1,0:T(8,128)(2,1)S(1)}, u32[]{:S(2)}, u32[]{:S(2)}) collective-permute-start(bf16[64,2560]{1,0:T(8,128)(2,1)S(1)} %get-tuple-element.23), channel_id=1, source_target_pairs={{0,4},{4,8},{8,12},{12,0},{1,5},{5,9},{9,13},{13,1},{2,6},{6,10},{... | collective-permute-start | bytes 983048 | tf_op jit(solution)/shard_map/ppermute | solution.py:242
  4.4 1.5 %collective-permute-start.5 = (bf16[512,2560]{1,0:T(8,128)(2,1)}, bf16[512,2560]{1,0:T(8,128)(2,1)}, u32[]{:S(2)}, u32[]{:S(2)}) collective-permute-start(bf16[512,2560]{1,0:T(8,128)(2,1)} %bitcast.21), channel_id=1, source_target_pairs={{0,2},{2,0},{1,3},{3,1},{4,6},{6,4},{5,7},{7,5},{8,10},{10,8},{9,1... | collective-permute-start | bytes 7864328 | tf_op jit(solution)/shard_map/ppermute | solution.py:245
  6.1 8.0 %collective-permute-done.refs_7_ = bf16[64,2560]{1,0:T(8,128)(2,1)S(1)} collective-permute-done((bf16[64,2560]{1,0:T(8,128)(2,1)S(1)}, bf16[64,2560]{1,0:T(8,128)(2,1)S(1)}, u32[]{:S(2)}, u32[]{:S(2)}) %collective-permute-start) | collective-permute-done | bytes 327712 | tf_op jit(solution)/shard_map/ppermute | solution.py:242
  14.1 3.8 %collective-permute-start.1 = (bf16[64,2560]{1,0:T(8,128)(2,1)}, bf16[64,2560]{1,0:T(8,128)(2,1)S(1)}, u32[]{:S(2)}, u32[]{:S(2)}) collective-permute-start(bf16[64,2560]{1,0:T(8,128)(2,1)} %copy-done.3), channel_id=1, source_target_pairs={{0,12},{4,0},{8,4},{12,8},{1,13},{5,1},{9,5},{13,9},{2,14},{6,2},{... | collective-permute-start | bytes 983048 | tf_op jit(solution)/shard_map/ppermute | solution.py:242
  18.0 1.5 %collective-permute-start.8 = (bf16[64,2560]{1,0:T(8,128)(2,1)S(1)}, bf16[64,2560]{1,0:T(8,128)(2,1)S(1)}, u32[]{:S(2)}, u32[]{:S(2)}) collective-permute-start(bf16[64,2560]{1,0:T(8,128)(2,1)S(1)} %collective-permute-done.refs_7_), channel_id=1, source_target_pairs={{0,16},{16,0},{1,17},{17,1},{2,18},{18,2},{3,19},{19,3},{4,20},{20... | collective-permute-start | bytes 983048 | tf_op jit(solution)/shard_map/ppermute | solution.py:268
  19.8 11.4 %collective-permute-done.1.refs_3_ = bf16[64,2560]{1,0:T(8,128)(2,1)S(1)} collective-permute-done((bf16[64,2560]{1,0:T(8,128)(2,1)}, bf16[64,2560]{1,0:T(8,128)(2,1)S(1)}, u32[]{:S(2)}, u32[]{:S(2)}) %collective-permute-start.1) | collective-permute-done | bytes 327712 | tf_op jit(solution)/shard_map/ppermute | solution.py:242
  31.1 1.9 %collective-permute-start.2 = (bf16[72,2560]{1,0:T(8,128)(2,1)S(1)}, bf16[72,2560]{1,0:T(8,128)(2,1)S(1)}, u32[]{:S(2)}, u32[]{:S(2)}) collective-permute-start(bf16[72,2560]{1,0:T(8,128)(2,1)S(1)} %pad_maximum_fusion.2), channel_id=1, source_target_pairs={{0,12},{4,0},{8,4},{12,8},{1,13},{5,1},{9,5},{13,9},{2,14},{6,2},{... | collective-permute-start | bytes 1105928 | tf_op jit(solution)/shard_map/ppermute | solution.py:242
  33.1 1.3 %collective-permute-start.6 = (bf16[64,2560]{1,0:T(8,128)(2,1)S(1)}, bf16[64,2560]{1,0:T(8,128)(2,1)S(1)}, u32[]{:S(2)}, u32[]{:S(2)}) collective-permute-start(bf16[64,2560]{1,0:T(8,128)(2,1)S(1)} %collective-permute-done.1.refs_3_), channel_id=1, source_target_pairs={{0,16},{16,0},{1,17},{17,1},{2,18},{18,2},{3,19},{19,3},{4,20},{20... | collective-permute-start | bytes 983048 | tf_op jit(solution)/shard_map/ppermute | solution.py:268
  34.4 0.8 collective-permute-start.9
  35.3 8.4 %collective-permute-done.6.refs_5_ = bf16[64,2560]{1,0:T(8,128)(2,1)S(1)} collective-permute-done((bf16[64,2560]{1,0:T(8,128)(2,1)S(1)}, bf16[64,2560]{1,0:T(8,128)(2,1)S(1)}, u32[]{:S(2)}, u32[]{:S(2)}) %collective-permute-start.6) | collective-permute-done | bytes 327712 | tf_op jit(solution)/shard_map/ppermute | solution.py:268
  43.9 1.3 %collective-permute-start.7 = (bf16[72,2560]{1,0:T(8,128)(2,1)S(1)}, bf16[72,2560]{1,0:T(8,128)(2,1)S(1)}, u32[]{:S(2)}, u32[]{:S(2)}) collective-permute-start(bf16[72,2560]{1,0:T(8,128)(2,1)S(1)} %collective-permute-done.2.refs_4_), channel_id=1, source_target_pairs={{0,16},{16,0},{1,17},{17,1},{2,18},{18,2},{3,19},{19,3},{4,20},{20... | collective-permute-start | bytes 1105928 | tf_op jit(solution)/shard_map/ppermute | solution.py:268
  45.2 7.0 %collective-permute-done.4 = bf16[72,2560]{1,0:T(8,128)(2,1)S(1)} collective-permute-done((bf16[72,2560]{1,0:T(8,128)(2,1)S(1)}, bf16[72,2560]{1,0:T(8,128)(2,1)S(1)}, u32[]{:S(2)}, u32[]{:S(2)}) %collective-permute-start.4) | collective-permute-done | bytes 368672 | tf_op jit(solution)/shard_map/ppermute | solution.py:242
  52.2 4.5 %collective-permute-done.10 = bf16[64,2560]{1,0:T(8,128)(2,1)S(1)} collective-permute-done((bf16[64,2560]{1,0:T(8,128)(2,1)S(1)}, bf16[64,2560]{1,0:T(8,128)(2,1)S(1)}, u32[]{:S(2)}, u32[]{:S(2)}) %collective-permute-start.10) | collective-permute-done | bytes 327712 | tf_op jit(solution)/shard_map/ppermute | solution.py:242
  56.7 1.1 %collective-permute-start.11 = (bf16[128,2560]{1,0:T(8,128)(2,1)S(1)}, bf16[128,2560]{1,0:T(8,128)(2,1)S(1)}, u32[]{:S(2)}, u32[]{:S(2)}) collective-permute-start(bf16[128,2560]{1,0:T(8,128)(2,1)S(1)} %pad_maximum_fusion.refs_2_), channel_id=1, source_target_pairs={{0,16},{16,0},{1,17},{17,1},{2,18},{18,2},{3,19},{19,3},{4,20},{20... | collective-permute-start | bytes 1966088 | tf_op jit(solution)/shard_map/ppermute | solution.py:268
  58.0 1.6 %collective-permute-start.16 = (bf16[576,512]{1,0:T(8,128)(2,1)S(1)}, bf16[576,512]{1,0:T(8,128)(2,1)S(1)}, u32[]{:S(2)}, u32[]{:S(2)}) collective-permute-start(bf16[576,512]{1,0:T(8,128)(2,1)S(1)} %pad_maximum_fusion.1), channel_id=1, source_target_pairs={{0,2},{2,0},{1,3},{3,1},{4,6},{6,4},{5,7},{7,5},{8,10},{10,8},{9,1... | collective-permute-start | bytes 1769480 | tf_op jit(solution)/shard_map/ppermute | solution.py:329
  59.5 5.0 %collective-permute-done.5.refs_1_ = bf16[512,2560]{1,0:T(8,128)(2,1)} collective-permute-done((bf16[512,2560]{1,0:T(8,128)(2,1)}, bf16[512,2560]{1,0:T(8,128)(2,1)}, u32[]{:S(2)}, u32[]{:S(2)}) %collective-permute-start.5) | collective-permute-done | bytes 2621472 | tf_op jit(solution)/shard_map/ppermute | solution.py:245
  64.5 6.0 %project_near.1 = (f32[6,512,128]{2,1,0:T(8,128)S(1)}, f32[2,512,128]{2,1,0:T(8,128)S(1)}, f32[2,512,128]{2,1,0:T(8,128)S(1)}, f32[2,512,128]{2,1,0:T(8,128)S(1)}) custom-call(s32[2]{0:T(128)S(1)} %pad_add_fusion.3.flag_ref, bf16[512,2560]{1,0:T(8,128)(2,1)S(1)} %bitcast.22, bf16[512,2560]{1,0:T(8,128)(2,1)} %collective-permute-done.5.refs_1_, ...), custom_call_target="tpu_custom_call" | custom-call | flops 4026531840 | bytes 1 | tf_op jit(solution)/shard_map/project_near/pallas_call | solution.py:190
  71.2 3.3 %project_far.1 = (f32[2,512,128]{2,1,0:T(8,128)S(1)}, f32[2,512,128]{2,1,0:T(8,128)S(1)}) custom-call(s32[2]{0:T(128)S(1)} %pad_add_fusion.3.flag_ref, bf16[512,2560]{1,0:T(8,128)(2,1)S(1)} %bitcast.23, bf16[512,2560]{1,0:T(8,128)(2,1)} %collective-permute-done.5.refs_1_, bf16[128,2560]{1,0:T(8,128)(2,1)S(1)} %pad_maximum_fusion.refs_2_, ...), custom_call_target="tpu_custom_call" | custom-call | flops 1 | bytes 1 | tf_op jit(solution)/shard_map/project_far/pallas_call | solution.py:190
  75.0 0.5 collective-permute-done.16.refs_7_
  75.6 1.0 %collective-permute-done.15.refs_5_ = f32[2,512,128]{2,1,0:T(8,128)S(1)} collective-permute-done((f32[2,512,128]{2,1,0:T(8,128)S(1)}, f32[2,512,128]{2,1,0:T(8,128)S(1)}, u32[]{:S(2)}, u32[]{:S(2)}) %collective-permute-start.15) | collective-permute-done | bytes 524320 | tf_op jit(solution)/shard_map/ppermute | solution.py:295
  76.5 2.0 %attend.1 = f32[4,136,128]{2,1,0:T(8,128)S(1)} custom-call(s32[4]{0:T(128)S(1)} %pad_add_fusion.2.place_ref, s32[2,4]{1,0:T(2,128)S(1)} %pad_add_fusion.spot_ref, bf16[4,16,512]{2,1,0:T(8,128)(2,1)S(1)} %get-tuple-element.66.query_ref, f32[6,512,128]{2,1,0:T(8,128)S(1)} %get-tuple-element.32.refs_0_, f32[2,512,128]{2,1,0:T(8,128)S(1)} %get-tuple-element.36.refs_1_, ...), custom_call_target="tpu_custom_call" | custom-call | tf_op jit(solution)/shard_map/attend/pallas_call | solution.py:332
  78.6 1.6 %collective-permute-start.17 = (f32[1,136,128]{2,1,0:T(8,128)S(1)}, f32[1,136,128]{2,1,0:T(8,128)S(1)}, u32[]{:S(2)}, u32[]{:S(2)}) collective-permute-start(f32[1,136,128]{2,1,0:T(8,128)S(1)} %get-tuple-element.63), channel_id=1, source_target_pairs={{0,4},{4,8},{8,12},{12,0},{1,5},{5,9},{9,13},{13,1},{2,6},{6,10},{... | collective-permute-start | bytes 208904 | tf_op jit(solution)/shard_map/ppermute | solution.py:242
  80.2 3.4 %collective-permute-start.18 = (f32[1,136,128]{2,1,0:T(8,128)S(1)}, f32[1,136,128]{2,1,0:T(8,128)S(1)}, u32[]{:S(2)}, u32[]{:S(2)}) collective-permute-start(f32[1,136,128]{2,1,0:T(8,128)S(1)} %get-tuple-element.62), channel_id=1, source_target_pairs={{0,8},{4,12},{8,0},{12,4},{1,9},{5,13},{9,1},{13,5},{2,10},{6,14},... | collective-permute-start | bytes 208904 | tf_op jit(solution)/shard_map/ppermute | solution.py:242
  83.6 1.5 %collective-permute-start.19 = (f32[1,136,128]{2,1,0:T(8,128)S(1)}, f32[1,136,128]{2,1,0:T(8,128)S(1)}, u32[]{:S(2)}, u32[]{:S(2)}) collective-permute-start(f32[1,136,128]{2,1,0:T(8,128)S(1)} %get-tuple-element.61), channel_id=1, source_target_pairs={{0,12},{4,0},{8,4},{12,8},{1,13},{5,1},{9,5},{13,9},{2,14},{6,2},{... | collective-permute-start | bytes 208904 | tf_op jit(solution)/shard_map/ppermute | solution.py:242
  85.1 0.5 collective-permute-done.17.refs_1_
  85.6 3.0 %collective-permute-done.18.refs_2_ = f32[1,136,128]{2,1,0:T(8,128)S(1)} collective-permute-done((f32[1,136,128]{2,1,0:T(8,128)S(1)}, f32[1,136,128]{2,1,0:T(8,128)S(1)}, u32[]{:S(2)}, u32[]{:S(2)}) %collective-permute-start.18) | collective-permute-done | bytes 69664 | tf_op jit(solution)/shard_map/ppermute | solution.py:242
  89.0 1.0 %collective-permute-start.21 = (bf16[1,16,512]{2,1,0:T(8,128)(2,1)S(1)}, bf16[1,16,512]{2,1,0:T(8,128)(2,1)S(1)}, u32[]{:S(2)}, u32[]{:S(2)}) collective-permute-start(bf16[1,16,512]{2,1,0:T(8,128)(2,1)S(1)} %get-tuple-element.75), channel_id=1, source_target_pairs={{0,2},{2,0},{1,3},{3,1},{4,6},{6,4},{5,7},{7,5},{8,10},{10,8},{9,1... | collective-permute-start | bytes 49160 | tf_op jit(solution)/shard_map/ppermute | solution.py:356
  90.2 1.0 %collective-permute-start.20 = (bf16[1,16,512]{2,1,0:T(8,128)(2,1)S(1)}, bf16[1,16,512]{2,1,0:T(8,128)(2,1)S(1)}, u32[]{:S(2)}, u32[]{:S(2)}) collective-permute-start(bf16[1,16,512]{2,1,0:T(8,128)(2,1)S(1)} %get-tuple-element.76.mine_ref), channel_id=1, source_target_pairs={{0,1},{1,0},{2,3},{3,2},{4,5},{5,4},{6,7},{7,6},{8,9},{9,8},{10,11... | collective-permute-start | bytes 49160 | tf_op jit(solution)/shard_map/ppermute | solution.py:355
  91.3 0.8 collective-permute-done.20.core_ref
  92.1 0.8 collective-permute-done.21.side_ref
  93.2 1.2 %assemble.1 = bf16[1,16,2048]{2,1,0:T(8,128)(2,1)} custom-call(s32[2]{0:T(128)S(1)} %pad_add_fusion.1.flag_ref, bf16[1,16,512]{2,1,0:T(8,128)(2,1)S(1)} %get-tuple-element.76.mine_ref, bf16[1,16,512]{2,1,0:T(8,128)(2,1)S(1)} %collective-permute-done.20.core_ref, bf16[1,16,512]{2,1,0:T(8,128)(2,1)S(1)} %collective-permute-done.21.side_ref, ...), custom_call_target="tpu_custom_call" | custom-call | tf_op jit(solution)/shard_map/assemble/pallas_call | solution.py:364
  (65 shorter events, 3.3 us)
Async XLA Ops:
  0.0 5.9 %copy-start.4 = (bf16[1,16,2048]{2,1,0:T(8,128)(2,1)S(1)}, bf16[1,16,2048]{2,1,0:T(8,128)(2,1)}, u32[]{:S(2)}) copy-start(bf16[1,16,2048]{2,1,0:T(8,128)(2,1)} %param.12) | copy-start | bytes 196612
  0.0 5.9 %copy-start.6 = (s32[8]{0:T(128)S(1)}, s32[8]{0:T(128)}, u32[]{:S(2)}) copy-start(s32[8]{0:T(128)} %param.11) | copy-start | bytes 100
  0.0 5.9 %copy-start.7 = (s32[16,1]{0,1:T(1,128)S(1)}, s32[16,1]{0,1:T(1,128)}, u32[]{:S(2)}) copy-start(s32[16,1]{0,1:T(1,128)} %param.10) | copy-start | bytes 196
  0.0 19.6 %copy-start = (bf16[2,256,2048]{2,1,0:T(8,128)(2,1)S(1)}, bf16[2,256,2048]{2,1,0:T(8,128)(2,1)}, u32[]{:S(2)}) copy-start(bf16[2,256,2048]{2,1,0:T(8,128)(2,1)} %param.8) | copy-start | bytes 6291460
  1.3 4.8 %copy-start.3 = (bf16[64,2560]{1,0:T(8,128)(2,1)}, bf16[64,2560]{1,0:T(8,128)(2,1)S(1)}, u32[]{:S(2)}) copy-start(bf16[64,2560]{1,0:T(8,128)(2,1)S(1)} %get-tuple-element.23) | copy-start | bytes 983044
  1.3 12.8 %collective-permute-start = (bf16[64,2560]{1,0:T(8,128)(2,1)S(1)}, bf16[64,2560]{1,0:T(8,128)(2,1)S(1)}, u32[]{:S(2)}, u32[]{:S(2)}) collective-permute-start(bf16[64,2560]{1,0:T(8,128)(2,1)S(1)} %get-tuple-element.23), channel_id=1, source_target_pairs={{0,4},{4,8},{8,12},{12,0},{1,5},{5,9},{9,13},{13,1},{2,6},{6,10},{... | collective-permute-start | bytes 983048 | tf_op jit(solution)/shard_map/ppermute | solution.py:242
  4.4 60.1 %collective-permute-start.5 = (bf16[512,2560]{1,0:T(8,128)(2,1)}, bf16[512,2560]{1,0:T(8,128)(2,1)}, u32[]{:S(2)}, u32[]{:S(2)}) collective-permute-start(bf16[512,2560]{1,0:T(8,128)(2,1)} %bitcast.21), channel_id=1, source_target_pairs={{0,2},{2,0},{1,3},{3,1},{4,6},{6,4},{5,7},{7,5},{8,10},{10,8},{9,1... | collective-permute-start | bytes 7864328 | tf_op jit(solution)/shard_map/ppermute | solution.py:245
  14.1 20.2 %collective-permute-start.3 = (bf16[72,2560]{1,0:T(8,128)(2,1)S(1)}, bf16[72,2560]{1,0:T(8,128)(2,1)S(1)}, u32[]{:S(2)}, u32[]{:S(2)}) collective-permute-start(bf16[72,2560]{1,0:T(8,128)(2,1)S(1)} %pad_maximum_fusion.2), channel_id=1, source_target_pairs={{0,4},{4,8},{8,12},{12,0},{1,5},{5,9},{9,13},{13,1},{2,6},{6,10},{... | collective-permute-start | bytes 1105928 | tf_op jit(solution)/shard_map/ppermute | solution.py:242
  14.1 17.0 %collective-permute-start.1 = (bf16[64,2560]{1,0:T(8,128)(2,1)}, bf16[64,2560]{1,0:T(8,128)(2,1)S(1)}, u32[]{:S(2)}, u32[]{:S(2)}) collective-permute-start(bf16[64,2560]{1,0:T(8,128)(2,1)} %copy-done.3), channel_id=1, source_target_pairs={{0,12},{4,0},{8,4},{12,8},{1,13},{5,1},{9,5},{13,9},{2,14},{6,2},{... | collective-permute-start | bytes 983048 | tf_op jit(solution)/shard_map/ppermute | solution.py:242
  18.0 16.3 %collective-permute-start.8 = (bf16[64,2560]{1,0:T(8,128)(2,1)S(1)}, bf16[64,2560]{1,0:T(8,128)(2,1)S(1)}, u32[]{:S(2)}, u32[]{:S(2)}) collective-permute-start(bf16[64,2560]{1,0:T(8,128)(2,1)S(1)} %collective-permute-done.refs_7_), channel_id=1, source_target_pairs={{0,16},{16,0},{1,17},{17,1},{2,18},{18,2},{3,19},{19,3},{4,20},{20... | collective-permute-start | bytes 983048 | tf_op jit(solution)/shard_map/ppermute | solution.py:268
  31.1 12.8 %collective-permute-start.2 = (bf16[72,2560]{1,0:T(8,128)(2,1)S(1)}, bf16[72,2560]{1,0:T(8,128)(2,1)S(1)}, u32[]{:S(2)}, u32[]{:S(2)}) collective-permute-start(bf16[72,2560]{1,0:T(8,128)(2,1)S(1)} %pad_maximum_fusion.2), channel_id=1, source_target_pairs={{0,12},{4,0},{8,4},{12,8},{1,13},{5,1},{9,5},{13,9},{2,14},{6,2},{... | collective-permute-start | bytes 1105928 | tf_op jit(solution)/shard_map/ppermute | solution.py:242
  33.1 10.6 %collective-permute-start.6 = (bf16[64,2560]{1,0:T(8,128)(2,1)S(1)}, bf16[64,2560]{1,0:T(8,128)(2,1)S(1)}, u32[]{:S(2)}, u32[]{:S(2)}) collective-permute-start(bf16[64,2560]{1,0:T(8,128)(2,1)S(1)} %collective-permute-done.1.refs_3_), channel_id=1, source_target_pairs={{0,16},{16,0},{1,17},{17,1},{2,18},{18,2},{3,19},{19,3},{4,20},{20... | collective-permute-start | bytes 983048 | tf_op jit(solution)/shard_map/ppermute | solution.py:268
  34.4 22.4 %collective-permute-start.9 = (bf16[72,2560]{1,0:T(8,128)(2,1)S(1)}, bf16[72,2560]{1,0:T(8,128)(2,1)S(1)}, u32[]{:S(2)}, u32[]{:S(2)}) collective-permute-start(bf16[72,2560]{1,0:T(8,128)(2,1)S(1)} %collective-permute-done.3.refs_8_), channel_id=1, source_target_pairs={{0,16},{16,0},{1,17},{17,1},{2,18},{18,2},{3,19},{19,3},{4,20},{20... | collective-permute-start | bytes 1105928 | tf_op jit(solution)/shard_map/ppermute | solution.py:268
  35.1 17.1 %collective-permute-start.4 = (bf16[72,2560]{1,0:T(8,128)(2,1)S(1)}, bf16[72,2560]{1,0:T(8,128)(2,1)S(1)}, u32[]{:S(2)}, u32[]{:S(2)}) collective-permute-start(bf16[72,2560]{1,0:T(8,128)(2,1)S(1)} %collective-permute-done.3.refs_8_), channel_id=1, source_target_pairs={{0,4},{4,8},{8,12},{12,0},{1,5},{5,9},{9,13},{13,1},{2,6},{6,10},{... | collective-permute-start | bytes 1105928 | tf_op jit(solution)/shard_map/ppermute | solution.py:242
  43.7 13.0 %collective-permute-start.10 = (bf16[64,2560]{1,0:T(8,128)(2,1)S(1)}, bf16[64,2560]{1,0:T(8,128)(2,1)S(1)}, u32[]{:S(2)}, u32[]{:S(2)}) collective-permute-start(bf16[64,2560]{1,0:T(8,128)(2,1)S(1)} %collective-permute-done.refs_7_), channel_id=1, source_target_pairs={{0,4},{4,8},{8,12},{12,0},{1,5},{5,9},{9,13},{13,1},{2,6},{6,10},{... | collective-permute-start | bytes 983048 | tf_op jit(solution)/shard_map/ppermute | solution.py:242
  43.9 15.6 %collective-permute-start.7 = (bf16[72,2560]{1,0:T(8,128)(2,1)S(1)}, bf16[72,2560]{1,0:T(8,128)(2,1)S(1)}, u32[]{:S(2)}, u32[]{:S(2)}) collective-permute-start(bf16[72,2560]{1,0:T(8,128)(2,1)S(1)} %collective-permute-done.2.refs_4_), channel_id=1, source_target_pairs={{0,16},{16,0},{1,17},{17,1},{2,18},{18,2},{3,19},{19,3},{4,20},{20... | collective-permute-start | bytes 1105928 | tf_op jit(solution)/shard_map/ppermute | solution.py:268
  45.2 19.3 %copy-start.2 = (bf16[256,2560]{1,0:T(8,128)(2,1)S(1)}, bf16[256,2560]{1,0:T(8,128)(2,1)}, u32[]{:S(2)}) copy-start(bf16[256,2560]{1,0:T(8,128)(2,1)} %refs_2_.1) | copy-start | bytes 3932164
  52.2 12.3 %copy-start.1 = (bf16[2,256,2560]{2,1,0:T(8,128)(2,1)S(1)}, bf16[2,256,2560]{2,1,0:T(8,128)(2,1)}, u32[]{:S(2)}) copy-start(bf16[2,256,2560]{2,1,0:T(8,128)(2,1)} %param.7) | copy-start | bytes 7864324
  56.7 14.4 %collective-permute-start.11 = (bf16[128,2560]{1,0:T(8,128)(2,1)S(1)}, bf16[128,2560]{1,0:T(8,128)(2,1)S(1)}, u32[]{:S(2)}, u32[]{:S(2)}) collective-permute-start(bf16[128,2560]{1,0:T(8,128)(2,1)S(1)} %pad_maximum_fusion.refs_2_), channel_id=1, source_target_pairs={{0,16},{16,0},{1,17},{17,1},{2,18},{18,2},{3,19},{19,3},{4,20},{20... | collective-permute-start | bytes 1966088 | tf_op jit(solution)/shard_map/ppermute | solution.py:268
  58.0 17.6 %collective-permute-start.16 = (bf16[576,512]{1,0:T(8,128)(2,1)S(1)}, bf16[576,512]{1,0:T(8,128)(2,1)S(1)}, u32[]{:S(2)}, u32[]{:S(2)}) collective-permute-start(bf16[576,512]{1,0:T(8,128)(2,1)S(1)} %pad_maximum_fusion.1), channel_id=1, source_target_pairs={{0,2},{2,0},{1,3},{3,1},{4,6},{6,4},{5,7},{7,5},{8,10},{10,8},{9,1... | collective-permute-start | bytes 1769480 | tf_op jit(solution)/shard_map/ppermute | solution.py:329
  70.5 4.5 %copy-start.5 = (s32[4]{0:T(128)S(1)}, s32[4]{0:T(128)}, u32[]{:S(2)}) copy-start(s32[4]{0:T(128)} %constant.97.clone) | copy-start | bytes 52
  70.5 5.0 %collective-permute-start.12 = (f32[2,512,128]{2,1,0:T(8,128)S(1)}, f32[2,512,128]{2,1,0:T(8,128)S(1)}, u32[]{:S(2)}, u32[]{:S(2)}) collective-permute-start(f32[2,512,128]{2,1,0:T(8,128)S(1)} %get-tuple-element.37), channel_id=1, source_target_pairs={{0,1},{1,0},{2,3},{3,2},{4,5},{5,4},{6,7},{7,6},{8,9},{9,8},{10,11... | collective-permute-start | bytes 1572872 | tf_op jit(solution)/shard_map/ppermute | solution.py:295
  70.6 5.0 %collective-permute-start.13 = (f32[2,512,128]{2,1,0:T(8,128)S(1)}, f32[2,512,128]{2,1,0:T(8,128)S(1)}, u32[]{:S(2)}, u32[]{:S(2)}) collective-permute-start(f32[2,512,128]{2,1,0:T(8,128)S(1)} %get-tuple-element.38), channel_id=1, source_target_pairs={{0,1},{1,0},{2,3},{3,2},{4,5},{5,4},{6,7},{7,6},{8,9},{9,8},{10,11... | collective-permute-start | bytes 1572872 | tf_op jit(solution)/shard_map/ppermute | solution.py:295
  71.1 4.5 %collective-permute-start.14 = (f32[2,512,128]{2,1,0:T(8,128)S(1)}, f32[2,512,128]{2,1,0:T(8,128)S(1)}, u32[]{:S(2)}, u32[]{:S(2)}) collective-permute-start(f32[2,512,128]{2,1,0:T(8,128)S(1)} %get-tuple-element.39), channel_id=1, source_target_pairs={{0,1},{1,0},{2,3},{3,2},{4,5},{5,4},{6,7},{7,6},{8,9},{9,8},{10,11... | collective-permute-start | bytes 1572872 | tf_op jit(solution)/shard_map/ppermute | solution.py:295
  74.5 2.0 %collective-permute-start.15 = (f32[2,512,128]{2,1,0:T(8,128)S(1)}, f32[2,512,128]{2,1,0:T(8,128)S(1)}, u32[]{:S(2)}, u32[]{:S(2)}) collective-permute-start(f32[2,512,128]{2,1,0:T(8,128)S(1)} %get-tuple-element.40), channel_id=1, source_target_pairs={{0,1},{1,0},{2,3},{3,2},{4,5},{5,4},{6,7},{7,6},{8,9},{9,8},{10,11... | collective-permute-start | bytes 1572872 | tf_op jit(solution)/shard_map/ppermute | solution.py:295
  78.6 7.1 %collective-permute-start.17 = (f32[1,136,128]{2,1,0:T(8,128)S(1)}, f32[1,136,128]{2,1,0:T(8,128)S(1)}, u32[]{:S(2)}, u32[]{:S(2)}) collective-permute-start(f32[1,136,128]{2,1,0:T(8,128)S(1)} %get-tuple-element.63), channel_id=1, source_target_pairs={{0,4},{4,8},{8,12},{12,0},{1,5},{5,9},{9,13},{13,1},{2,6},{6,10},{... | collective-permute-start | bytes 208904 | tf_op jit(solution)/shard_map/ppermute | solution.py:242
  80.2 8.4 %collective-permute-start.18 = (f32[1,136,128]{2,1,0:T(8,128)S(1)}, f32[1,136,128]{2,1,0:T(8,128)S(1)}, u32[]{:S(2)}, u32[]{:S(2)}) collective-permute-start(f32[1,136,128]{2,1,0:T(8,128)S(1)} %get-tuple-element.62), channel_id=1, source_target_pairs={{0,8},{4,12},{8,0},{12,4},{1,9},{5,13},{9,1},{13,5},{2,10},{6,14},... | collective-permute-start | bytes 208904 | tf_op jit(solution)/shard_map/ppermute | solution.py:242
  83.6 5.2 %collective-permute-start.19 = (f32[1,136,128]{2,1,0:T(8,128)S(1)}, f32[1,136,128]{2,1,0:T(8,128)S(1)}, u32[]{:S(2)}, u32[]{:S(2)}) collective-permute-start(f32[1,136,128]{2,1,0:T(8,128)S(1)} %get-tuple-element.61), channel_id=1, source_target_pairs={{0,12},{4,0},{8,4},{12,8},{1,13},{5,1},{9,5},{13,9},{2,14},{6,2},{... | collective-permute-start | bytes 208904 | tf_op jit(solution)/shard_map/ppermute | solution.py:242
  89.0 3.8 %collective-permute-start.21 = (bf16[1,16,512]{2,1,0:T(8,128)(2,1)S(1)}, bf16[1,16,512]{2,1,0:T(8,128)(2,1)S(1)}, u32[]{:S(2)}, u32[]{:S(2)}) collective-permute-start(bf16[1,16,512]{2,1,0:T(8,128)(2,1)S(1)} %get-tuple-element.75), channel_id=1, source_target_pairs={{0,2},{2,0},{1,3},{3,1},{4,6},{6,4},{5,7},{7,5},{8,10},{10,8},{9,1... | collective-permute-start | bytes 49160 | tf_op jit(solution)/shard_map/ppermute | solution.py:356
  90.1 3.2 %collective-permute-start.22 = (bf16[1,16,512]{2,1,0:T(8,128)(2,1)S(1)}, bf16[1,16,512]{2,1,0:T(8,128)(2,1)S(1)}, u32[]{:S(2)}, u32[]{:S(2)}) collective-permute-start(bf16[1,16,512]{2,1,0:T(8,128)(2,1)S(1)} %get-tuple-element.75), channel_id=1, source_target_pairs={{0,3},{3,0},{1,2},{2,1},{4,7},{7,4},{5,6},{6,5},{8,11},{11,8},{9,1... | collective-permute-start | bytes 49160 | tf_op jit(solution)/shard_map/ppermute | solution.py:357
  90.2 1.8 %collective-permute-start.20 = (bf16[1,16,512]{2,1,0:T(8,128)(2,1)S(1)}, bf16[1,16,512]{2,1,0:T(8,128)(2,1)S(1)}, u32[]{:S(2)}, u32[]{:S(2)}) collective-permute-start(bf16[1,16,512]{2,1,0:T(8,128)(2,1)S(1)} %get-tuple-element.76.mine_ref), channel_id=1, source_target_pairs={{0,1},{1,0},{2,3},{3,2},{4,5},{5,4},{6,7},{7,6},{8,9},{9,8},{10,11... | collective-permute-start | bytes 49160 | tf_op jit(solution)/shard_map/ppermute | solution.py:355

commit v17 on v16

--- a/solution.py
+++ b/solution.py
@@ -10,7 +10,7 @@
 
 HEAD_DIM = 64
 EMPTY = -3e38
-FIRST_EIGHTHS = 4
+FIRST_EIGHTHS = 3
 VMEM_LIMIT = 22 * 1024 * 1024
 SWAP = [(0, 1), (1, 0)]
 CROSS = [(0, 3), (3, 0), (1, 2), (2, 1)]

time: 94.6 us -> 95 us (level)
  waiting for transfers between devices: 51.3 us -> 48.6 us
  local copies, waits for them, and re-layouts: 1.59 us -> 3.27 us
  other arithmetic: 0.55 us -> 1.93 us
    ppermute x5, waiting for transfers between devices: 8.45 us -> 7.12 us  [body(): lax.ppermute(after(piece, swapped[max(at - 2, 0):max(at - 1, 0)]), 'group...]
    ppermute x9, waiting for transfers between devices: 34.5 us -> 33.3 us  [shifted(): lax.ppermute(array, 'high', [(at, (at + shift) % highs) for at in range(h...]
    dynamic_slice x1 -> x2, local copies, waits for them, and re-layouts: 1.27 us -> 2.14 us  [body(): lax.dynamic_slice_in_dim(down_weight, group * half + first, length, axis=0)]
  transfers between devices with their start and end apart: 23 -> 23, of which waited for: 14 -> 16; matrix products, arithmetic and copies ran while one was open for 1% -> 4% of each run, Pallas kernels for 10% -> 10%
where the time goes in v17:
time: 95 us; the launch traced here: 94.7 us
  waiting for transfers between devices  48.6 us (51%)
  starting transfers between devices  28 us (29%)
  Pallas kernels  12.7 us (13%)
  local copies, waits for them, and re-layouts  3.27 us (3%)
  other arithmetic  1.93 us (2%)
    ppermute x9, waiting for transfers between devices, shifted(): lax.ppermute(array, 'high', [(at, (at + shift) % highs) for at in range(h...  33.3 us
    ppermute x9, starting transfers between devices, shifted(): lax.ppermute(array, 'high', [(at, (at + shift) % highs) for at in range(h...  16 us
    pallas_call x2, Pallas kernels, project(): pl.pallas_call(functools.partial(project_kernel, jobs=jobs, sends=sends),...  9.32 us
    ppermute x5, waiting for transfers between devices, body(): lax.ppermute(after(piece, swapped[max(at - 2, 0):max(at - 1, 0)]), 'group...  7.12 us
    ppermute x5, starting transfers between devices, body(): lax.ppermute(after(piece, swapped[max(at - 2, 0):max(at - 1, 0)]), 'group...  5.89 us
    ppermute x1, waiting for transfers between devices, body(): partner_hidden = lax.ppermute(hidden, 'side', SWAP)  4.54 us
    dynamic_slice x2, local copies, waits for them, and re-layouts, body(): lax.dynamic_slice_in_dim(down_weight, group * half + first, length, axis=0)  2.14 us
    pallas_call x1, Pallas kernels, body(): pl.pallas_call(functools.partial(attend_kernel, pieces=pieces), out_shape...  1.99 us
  transfers between devices with their start and end apart: 23, of which 16 were waited for; matrix products, arithmetic and copies ran while one was open for 4% of the time, Pallas kernels for 10%

profile of v17, /device:TPU:0, one launch (start us, length us, event | category | flops | bytes accessed | tf_op | source)
XLA Modules:
  0.0 94.7 jit_solution(16524350956992832971)
XLA Ops:
  0.0 1.1 %constant_dynamic-slice_fusion.4 = bf16[48,2560]{1,0:T(8,128)(2,1)S(1)} fusion(bf16[256,2560]{1,0:T(8,128)(2,1)} %refs_2_.1, s32[]{:T(128)S(6)} %select_n.73), kind=kLoop, calls=%fused_computation.23 | loop fusion | bytes 491524 | tf_op jit(solution)/shard_map/dynamic_slice | solution.py:254
  1.1 3.1 %collective-permute-start = (bf16[48,2560]{1,0:T(8,128)(2,1)S(1)}, bf16[48,2560]{1,0:T(8,128)(2,1)S(1)}, u32[]{:S(2)}, u32[]{:S(2)}) collective-permute-start(bf16[48,2560]{1,0:T(8,128)(2,1)S(1)} %constant_dynamic-slice_fusion.4), channel_id=1, source_target_pairs={{0,4},{4,8},{8,12},{12,0},{1,5},{5,9},{9,13},{13,1},{2,6},{6,10},{... | collective-permute-start | bytes 737288 | tf_op jit(solution)/shard_map/ppermute | solution.py:242
  4.2 1.5 %collective-permute-start.5 = (bf16[512,2560]{1,0:T(8,128)(2,1)}, bf16[512,2560]{1,0:T(8,128)(2,1)}, u32[]{:S(2)}, u32[]{:S(2)}) collective-permute-start(bf16[512,2560]{1,0:T(8,128)(2,1)} %bitcast.21), channel_id=1, source_target_pairs={{0,2},{2,0},{1,3},{3,1},{4,6},{6,4},{5,7},{7,5},{8,10},{10,8},{9,1... | collective-permute-start | bytes 7864328 | tf_op jit(solution)/shard_map/ppermute | solution.py:245
  5.7 0.8 constant_dynamic-slice_fusion.13
  6.5 1.0 %constant_dynamic-slice_fusion.5 = bf16[80,2560]{1,0:T(8,128)(2,1)S(1)} fusion(bf16[256,2560]{1,0:T(8,128)(2,1)} %refs_2_.1, s32[]{:T(128)S(6)} %select_n.72), kind=kLoop, calls=%fused_computation.24 | loop fusion | bytes 819204 | tf_op jit(solution)/shard_map/dynamic_slice | solution.py:254
  7.7 0.8 pad_maximum_fusion.2
  9.1 3.1 %collective-permute-done.refs_7_ = bf16[48,2560]{1,0:T(8,128)(2,1)S(1)} collective-permute-done((bf16[48,2560]{1,0:T(8,128)(2,1)S(1)}, bf16[48,2560]{1,0:T(8,128)(2,1)S(1)}, u32[]{:S(2)}, u32[]{:S(2)}) %collective-permute-start) | collective-permute-done | bytes 245792 | tf_op jit(solution)/shard_map/ppermute | solution.py:242
  12.2 3.8 %collective-permute-start.1 = (bf16[48,2560]{1,0:T(8,128)(2,1)S(1)}, bf16[48,2560]{1,0:T(8,128)(2,1)S(1)}, u32[]{:S(2)}, u32[]{:S(2)}) collective-permute-start(bf16[48,2560]{1,0:T(8,128)(2,1)S(1)} %constant_dynamic-slice_fusion.4), channel_id=1, source_target_pairs={{0,12},{4,0},{8,4},{12,8},{1,13},{5,1},{9,5},{13,9},{2,14},{6,2},{... | collective-permute-start | bytes 737288 | tf_op jit(solution)/shard_map/ppermute | solution.py:242
  16.1 1.5 %collective-permute-start.8 = (bf16[48,2560]{1,0:T(8,128)(2,1)S(1)}, bf16[48,2560]{1,0:T(8,128)(2,1)S(1)}, u32[]{:S(2)}, u32[]{:S(2)}) collective-permute-start(bf16[48,2560]{1,0:T(8,128)(2,1)S(1)} %collective-permute-done.refs_7_), channel_id=1, source_target_pairs={{0,16},{16,0},{1,17},{17,1},{2,18},{18,2},{3,19},{19,3},{4,20},{20... | collective-permute-start | bytes 737288 | tf_op jit(solution)/shard_map/ppermute | solution.py:268
  17.8 11.1 %collective-permute-done.1.refs_3_ = bf16[48,2560]{1,0:T(8,128)(2,1)S(1)} collective-permute-done((bf16[48,2560]{1,0:T(8,128)(2,1)S(1)}, bf16[48,2560]{1,0:T(8,128)(2,1)S(1)}, u32[]{:S(2)}, u32[]{:S(2)}) %collective-permute-start.1) | collective-permute-done | bytes 245792 | tf_op jit(solution)/shard_map/ppermute | solution.py:242
  29.0 2.3 %collective-permute-start.2 = (bf16[88,2560]{1,0:T(8,128)(2,1)}, bf16[88,2560]{1,0:T(8,128)(2,1)S(1)}, u32[]{:S(2)}, u32[]{:S(2)}) collective-permute-start(bf16[88,2560]{1,0:T(8,128)(2,1)} %pad_maximum_fusion.2), channel_id=1, source_target_pairs={{0,12},{4,0},{8,4},{12,8},{1,13},{5,1},{9,5},{13,9},{2,14},{6,2},{... | collective-permute-start | bytes 1351688 | tf_op jit(solution)/shard_map/ppermute | solution.py:242
  31.4 1.3 %collective-permute-start.6 = (bf16[48,2560]{1,0:T(8,128)(2,1)S(1)}, bf16[48,2560]{1,0:T(8,128)(2,1)S(1)}, u32[]{:S(2)}, u32[]{:S(2)}) collective-permute-start(bf16[48,2560]{1,0:T(8,128)(2,1)S(1)} %collective-permute-done.1.refs_3_), channel_id=1, source_target_pairs={{0,16},{16,0},{1,17},{17,1},{2,18},{18,2},{3,19},{19,3},{4,20},{20... | collective-permute-start | bytes 737288 | tf_op jit(solution)/shard_map/ppermute | solution.py:268
  33.4 6.8 %collective-permute-done.6.refs_5_ = bf16[48,2560]{1,0:T(8,128)(2,1)S(1)} collective-permute-done((bf16[48,2560]{1,0:T(8,128)(2,1)S(1)}, bf16[48,2560]{1,0:T(8,128)(2,1)S(1)}, u32[]{:S(2)}, u32[]{:S(2)}) %collective-permute-start.6) | collective-permute-done | bytes 245792 | tf_op jit(solution)/shard_map/ppermute | solution.py:268
  40.2 2.2 %collective-permute-done.2.refs_4_ = bf16[88,2560]{1,0:T(8,128)(2,1)S(1)} collective-permute-done((bf16[88,2560]{1,0:T(8,128)(2,1)}, bf16[88,2560]{1,0:T(8,128)(2,1)S(1)}, u32[]{:S(2)}, u32[]{:S(2)}) %collective-permute-start.2) | collective-permute-done | bytes 450592 | tf_op jit(solution)/shard_map/ppermute | solution.py:242
  42.4 1.3 %collective-permute-start.7 = (bf16[88,2560]{1,0:T(8,128)(2,1)S(1)}, bf16[88,2560]{1,0:T(8,128)(2,1)S(1)}, u32[]{:S(2)}, u32[]{:S(2)}) collective-permute-start(bf16[88,2560]{1,0:T(8,128)(2,1)S(1)} %collective-permute-done.2.refs_4_), channel_id=1, source_target_pairs={{0,16},{16,0},{1,17},{17,1},{2,18},{18,2},{3,19},{19,3},{4,20},{20... | collective-permute-start | bytes 1351688 | tf_op jit(solution)/shard_map/ppermute | solution.py:268
  43.7 10.5 %collective-permute-done.4 = bf16[88,2560]{1,0:T(8,128)(2,1)S(1)} collective-permute-done((bf16[88,2560]{1,0:T(8,128)(2,1)S(1)}, bf16[88,2560]{1,0:T(8,128)(2,1)S(1)}, u32[]{:S(2)}, u32[]{:S(2)}) %collective-permute-start.4) | collective-permute-done | bytes 450592 | tf_op jit(solution)/shard_map/ppermute | solution.py:242
  54.2 2.7 %collective-permute-done.10 = bf16[48,2560]{1,0:T(8,128)(2,1)S(1)} collective-permute-done((bf16[48,2560]{1,0:T(8,128)(2,1)S(1)}, bf16[48,2560]{1,0:T(8,128)(2,1)S(1)}, u32[]{:S(2)}, u32[]{:S(2)}) %collective-permute-start.10) | collective-permute-done | bytes 245792 | tf_op jit(solution)/shard_map/ppermute | solution.py:242
  57.0 1.1 %collective-permute-start.11 = (bf16[128,2560]{1,0:T(8,128)(2,1)S(1)}, bf16[128,2560]{1,0:T(8,128)(2,1)S(1)}, u32[]{:S(2)}, u32[]{:S(2)}) collective-permute-start(bf16[128,2560]{1,0:T(8,128)(2,1)S(1)} %pad_maximum_fusion.refs_2_), channel_id=1, source_target_pairs={{0,16},{16,0},{1,17},{17,1},{2,18},{18,2},{3,19},{19,3},{4,20},{20... | collective-permute-start | bytes 1966088 | tf_op jit(solution)/shard_map/ppermute | solution.py:268
  58.2 1.6 %collective-permute-start.16 = (bf16[576,512]{1,0:T(8,128)(2,1)S(1)}, bf16[576,512]{1,0:T(8,128)(2,1)S(1)}, u32[]{:S(2)}, u32[]{:S(2)}) collective-permute-start(bf16[576,512]{1,0:T(8,128)(2,1)S(1)} %pad_maximum_fusion.1), channel_id=1, source_target_pairs={{0,2},{2,0},{1,3},{3,1},{4,6},{6,4},{5,7},{7,5},{8,10},{10,8},{9,1... | collective-permute-start | bytes 1769480 | tf_op jit(solution)/shard_map/ppermute | solution.py:329
  59.8 4.5 %collective-permute-done.5.refs_1_ = bf16[512,2560]{1,0:T(8,128)(2,1)} collective-permute-done((bf16[512,2560]{1,0:T(8,128)(2,1)}, bf16[512,2560]{1,0:T(8,128)(2,1)}, u32[]{:S(2)}, u32[]{:S(2)}) %collective-permute-start.5) | collective-permute-done | bytes 2621472 | tf_op jit(solution)/shard_map/ppermute | solution.py:245
  64.3 6.0 %project_near.1 = (f32[6,512,128]{2,1,0:T(8,128)S(1)}, f32[2,512,128]{2,1,0:T(8,128)S(1)}, f32[2,512,128]{2,1,0:T(8,128)S(1)}, f32[2,512,128]{2,1,0:T(8,128)S(1)}) custom-call(s32[2]{0:T(128)S(1)} %pad_add_fusion.3.flag_ref, bf16[512,2560]{1,0:T(8,128)(2,1)S(1)} %bitcast.22, bf16[512,2560]{1,0:T(8,128)(2,1)} %collective-permute-done.5.refs_1_, ...), custom_call_target="tpu_custom_call" | custom-call | flops 4026531840 | bytes 1 | tf_op jit(solution)/shard_map/project_near/pallas_call | solution.py:190
  71.3 3.3 %project_far.1 = (f32[2,512,128]{2,1,0:T(8,128)S(1)}, f32[2,512,128]{2,1,0:T(8,128)S(1)}) custom-call(s32[2]{0:T(128)S(1)} %pad_add_fusion.3.flag_ref, bf16[512,2560]{1,0:T(8,128)(2,1)S(1)} %bitcast.23, bf16[512,2560]{1,0:T(8,128)(2,1)} %collective-permute-done.5.refs_1_, bf16[128,2560]{1,0:T(8,128)(2,1)S(1)} %pad_maximum_fusion.refs_2_, ...), custom_call_target="tpu_custom_call" | custom-call | flops 1 | bytes 1 | tf_op jit(solution)/shard_map/project_far/pallas_call | solution.py:190
  75.4 1.2 %collective-permute-done.15.refs_5_ = f32[2,512,128]{2,1,0:T(8,128)S(1)} collective-permute-done((f32[2,512,128]{2,1,0:T(8,128)S(1)}, f32[2,512,128]{2,1,0:T(8,128)S(1)}, u32[]{:S(2)}, u32[]{:S(2)}) %collective-permute-start.15) | collective-permute-done | bytes 524320 | tf_op jit(solution)/shard_map/ppermute | solution.py:295
  76.6 2.0 %attend.1 = f32[4,136,128]{2,1,0:T(8,128)S(1)} custom-call(s32[4]{0:T(128)S(1)} %pad_add_fusion.2.place_ref, s32[2,4]{1,0:T(2,128)S(1)} %pad_add_fusion.spot_ref, bf16[4,16,512]{2,1,0:T(8,128)(2,1)S(1)} %get-tuple-element.64.query_ref, f32[6,512,128]{2,1,0:T(8,128)S(1)} %get-tuple-element.32.refs_0_, f32[2,512,128]{2,1,0:T(8,128)S(1)} %get-tuple-element.36.refs_1_, ...), custom_call_target="tpu_custom_call" | custom-call | tf_op jit(solution)/shard_map/attend/pallas_call | solution.py:332
  78.6 1.8 %collective-permute-start.17 = (f32[1,136,128]{2,1,0:T(8,128)S(1)}, f32[1,136,128]{2,1,0:T(8,128)S(1)}, u32[]{:S(2)}, u32[]{:S(2)}) collective-permute-start(f32[1,136,128]{2,1,0:T(8,128)S(1)} %get-tuple-element.61), channel_id=1, source_target_pairs={{0,4},{4,8},{8,12},{12,0},{1,5},{5,9},{9,13},{13,1},{2,6},{6,10},{... | collective-permute-start | bytes 208904 | tf_op jit(solution)/shard_map/ppermute | solution.py:242
  80.4 3.5 %collective-permute-start.18 = (f32[1,136,128]{2,1,0:T(8,128)S(1)}, f32[1,136,128]{2,1,0:T(8,128)S(1)}, u32[]{:S(2)}, u32[]{:S(2)}) collective-permute-start(f32[1,136,128]{2,1,0:T(8,128)S(1)} %get-tuple-element.60), channel_id=1, source_target_pairs={{0,8},{4,12},{8,0},{12,4},{1,9},{5,13},{9,1},{13,5},{2,10},{6,14},... | collective-permute-start | bytes 208904 | tf_op jit(solution)/shard_map/ppermute | solution.py:242
  83.9 1.5 %collective-permute-start.19 = (f32[1,136,128]{2,1,0:T(8,128)S(1)}, f32[1,136,128]{2,1,0:T(8,128)S(1)}, u32[]{:S(2)}, u32[]{:S(2)}) collective-permute-start(f32[1,136,128]{2,1,0:T(8,128)S(1)} %get-tuple-element.59), channel_id=1, source_target_pairs={{0,12},{4,0},{8,4},{12,8},{1,13},{5,1},{9,5},{13,9},{2,14},{6,2},{... | collective-permute-start | bytes 208904 | tf_op jit(solution)/shard_map/ppermute | solution.py:242
  85.9 2.9 %collective-permute-done.18.refs_2_ = f32[1,136,128]{2,1,0:T(8,128)S(1)} collective-permute-done((f32[1,136,128]{2,1,0:T(8,128)S(1)}, f32[1,136,128]{2,1,0:T(8,128)S(1)}, u32[]{:S(2)}, u32[]{:S(2)}) %collective-permute-start.18) | collective-permute-done | bytes 69664 | tf_op jit(solution)/shard_map/ppermute | solution.py:242
  89.3 1.1 %collective-permute-start.21 = (bf16[1,16,512]{2,1,0:T(8,128)(2,1)S(1)}, bf16[1,16,512]{2,1,0:T(8,128)(2,1)S(1)}, u32[]{:S(2)}, u32[]{:S(2)}) collective-permute-start(bf16[1,16,512]{2,1,0:T(8,128)(2,1)S(1)} %get-tuple-element.73), channel_id=1, source_target_pairs={{0,2},{2,0},{1,3},{3,1},{4,6},{6,4},{5,7},{7,5},{8,10},{10,8},{9,1... | collective-permute-start | bytes 49160 | tf_op jit(solution)/shard_map/ppermute | solution.py:356
  90.5 1.0 %collective-permute-start.20 = (bf16[1,16,512]{2,1,0:T(8,128)(2,1)S(1)}, bf16[1,16,512]{2,1,0:T(8,128)(2,1)S(1)}, u32[]{:S(2)}, u32[]{:S(2)}) collective-permute-start(bf16[1,16,512]{2,1,0:T(8,128)(2,1)S(1)} %get-tuple-element.74.mine_ref), channel_id=1, source_target_pairs={{0,1},{1,0},{2,3},{3,2},{4,5},{5,4},{6,7},{7,6},{8,9},{9,8},{10,11... | collective-permute-start | bytes 49160 | tf_op jit(solution)/shard_map/ppermute | solution.py:355
  91.6 0.8 collective-permute-done.20.core_ref
  93.5 1.2 %assemble.1 = bf16[1,16,2048]{2,1,0:T(8,128)(2,1)} custom-call(s32[2]{0:T(128)S(1)} %pad_add_fusion.1.flag_ref, bf16[1,16,512]{2,1,0:T(8,128)(2,1)S(1)} %get-tuple-element.74.mine_ref, bf16[1,16,512]{2,1,0:T(8,128)(2,1)S(1)} %collective-permute-done.20.core_ref, bf16[1,16,512]{2,1,0:T(8,128)(2,1)S(1)} %collective-permute-done.21.side_ref, ...), custom_call_target="tpu_custom_call" | custom-call | tf_op jit(solution)/shard_map/assemble/pallas_call | solution.py:364
  (64 shorter events, 6.2 us)
Async XLA Ops:
  0.0 7.6 %copy-start.5 = (s32[8]{0:T(128)S(1)}, s32[8]{0:T(128)}, u32[]{:S(2)}) copy-start(s32[8]{0:T(128)} %param.11) | copy-start | bytes 100
  0.0 7.6 %copy-start.6 = (s32[16,1]{0,1:T(1,128)S(1)}, s32[16,1]{0,1:T(1,128)}, u32[]{:S(2)}) copy-start(s32[16,1]{0,1:T(1,128)} %param.10) | copy-start | bytes 196
  0.0 17.7 %copy-start = (bf16[2,256,2048]{2,1,0:T(8,128)(2,1)S(1)}, bf16[2,256,2048]{2,1,0:T(8,128)(2,1)}, u32[]{:S(2)}) copy-start(bf16[2,256,2048]{2,1,0:T(8,128)(2,1)} %param.8) | copy-start | bytes 6291460
  1.1 11.1 %collective-permute-start = (bf16[48,2560]{1,0:T(8,128)(2,1)S(1)}, bf16[48,2560]{1,0:T(8,128)(2,1)S(1)}, u32[]{:S(2)}, u32[]{:S(2)}) collective-permute-start(bf16[48,2560]{1,0:T(8,128)(2,1)S(1)} %constant_dynamic-slice_fusion.4), channel_id=1, source_target_pairs={{0,4},{4,8},{8,12},{12,0},{1,5},{5,9},{9,13},{13,1},{2,6},{6,10},{... | collective-permute-start | bytes 737288 | tf_op jit(solution)/shard_map/ppermute | solution.py:242
  4.2 60.1 %collective-permute-start.5 = (bf16[512,2560]{1,0:T(8,128)(2,1)}, bf16[512,2560]{1,0:T(8,128)(2,1)}, u32[]{:S(2)}, u32[]{:S(2)}) collective-permute-start(bf16[512,2560]{1,0:T(8,128)(2,1)} %bitcast.21), channel_id=1, source_target_pairs={{0,2},{2,0},{1,3},{3,1},{4,6},{6,4},{5,7},{7,5},{8,10},{10,8},{9,1... | collective-permute-start | bytes 7864328 | tf_op jit(solution)/shard_map/ppermute | solution.py:245
  12.2 20.4 %collective-permute-start.3 = (bf16[88,2560]{1,0:T(8,128)(2,1)}, bf16[88,2560]{1,0:T(8,128)(2,1)S(1)}, u32[]{:S(2)}, u32[]{:S(2)}) collective-permute-start(bf16[88,2560]{1,0:T(8,128)(2,1)} %pad_maximum_fusion.2), channel_id=1, source_target_pairs={{0,4},{4,8},{8,12},{12,0},{1,5},{5,9},{9,13},{13,1},{2,6},{6,10},{... | collective-permute-start | bytes 1351688 | tf_op jit(solution)/shard_map/ppermute | solution.py:242
  12.2 16.8 %collective-permute-start.1 = (bf16[48,2560]{1,0:T(8,128)(2,1)S(1)}, bf16[48,2560]{1,0:T(8,128)(2,1)S(1)}, u32[]{:S(2)}, u32[]{:S(2)}) collective-permute-start(bf16[48,2560]{1,0:T(8,128)(2,1)S(1)} %constant_dynamic-slice_fusion.4), channel_id=1, source_target_pairs={{0,12},{4,0},{8,4},{12,8},{1,13},{5,1},{9,5},{13,9},{2,14},{6,2},{... | collective-permute-start | bytes 737288 | tf_op jit(solution)/shard_map/ppermute | solution.py:242
  16.1 16.5 %collective-permute-start.8 = (bf16[48,2560]{1,0:T(8,128)(2,1)S(1)}, bf16[48,2560]{1,0:T(8,128)(2,1)S(1)}, u32[]{:S(2)}, u32[]{:S(2)}) collective-permute-start(bf16[48,2560]{1,0:T(8,128)(2,1)S(1)} %collective-permute-done.refs_7_), channel_id=1, source_target_pairs={{0,16},{16,0},{1,17},{17,1},{2,18},{18,2},{3,19},{19,3},{4,20},{20... | collective-permute-start | bytes 737288 | tf_op jit(solution)/shard_map/ppermute | solution.py:268
  17.8 40.3 %copy-start.3 = (bf16[1,2,16,512]{3,2,0,1:T(8,128)(2,1)S(1)}, bf16[1,2,16,512]{3,2,0,1:T(8,128)(2,1)}, u32[]{:S(2)}) copy-start(bf16[1,2,16,512]{3,2,0,1:T(8,128)(2,1)} %fusion.19) | copy-start | bytes 98308
  29.0 13.4 %collective-permute-start.2 = (bf16[88,2560]{1,0:T(8,128)(2,1)}, bf16[88,2560]{1,0:T(8,128)(2,1)S(1)}, u32[]{:S(2)}, u32[]{:S(2)}) collective-permute-start(bf16[88,2560]{1,0:T(8,128)(2,1)} %pad_maximum_fusion.2), channel_id=1, source_target_pairs={{0,12},{4,0},{8,4},{12,8},{1,13},{5,1},{9,5},{13,9},{2,14},{6,2},{... | collective-permute-start | bytes 1351688 | tf_op jit(solution)/shard_map/ppermute | solution.py:242
  31.4 8.9 %collective-permute-start.6 = (bf16[48,2560]{1,0:T(8,128)(2,1)S(1)}, bf16[48,2560]{1,0:T(8,128)(2,1)S(1)}, u32[]{:S(2)}, u32[]{:S(2)}) collective-permute-start(bf16[48,2560]{1,0:T(8,128)(2,1)S(1)} %collective-permute-done.1.refs_3_), channel_id=1, source_target_pairs={{0,16},{16,0},{1,17},{17,1},{2,18},{18,2},{3,19},{19,3},{4,20},{20... | collective-permute-start | bytes 737288 | tf_op jit(solution)/shard_map/ppermute | solution.py:268
  32.6 24.4 %collective-permute-start.9 = (bf16[88,2560]{1,0:T(8,128)(2,1)S(1)}, bf16[88,2560]{1,0:T(8,128)(2,1)S(1)}, u32[]{:S(2)}, u32[]{:S(2)}) collective-permute-start(bf16[88,2560]{1,0:T(8,128)(2,1)S(1)} %collective-permute-done.3.refs_8_), channel_id=1, source_target_pairs={{0,16},{16,0},{1,17},{17,1},{2,18},{18,2},{3,19},{19,3},{4,20},{20... | collective-permute-start | bytes 1351688 | tf_op jit(solution)/shard_map/ppermute | solution.py:268
  33.4 20.8 %collective-permute-start.4 = (bf16[88,2560]{1,0:T(8,128)(2,1)S(1)}, bf16[88,2560]{1,0:T(8,128)(2,1)S(1)}, u32[]{:S(2)}, u32[]{:S(2)}) collective-permute-start(bf16[88,2560]{1,0:T(8,128)(2,1)S(1)} %collective-permute-done.3.refs_8_), channel_id=1, source_target_pairs={{0,4},{4,8},{8,12},{12,0},{1,5},{5,9},{9,13},{13,1},{2,6},{6,10},{... | collective-permute-start | bytes 1351688 | tf_op jit(solution)/shard_map/ppermute | solution.py:242
  40.2 16.7 %collective-permute-start.10 = (bf16[48,2560]{1,0:T(8,128)(2,1)S(1)}, bf16[48,2560]{1,0:T(8,128)(2,1)S(1)}, u32[]{:S(2)}, u32[]{:S(2)}) collective-permute-start(bf16[48,2560]{1,0:T(8,128)(2,1)S(1)} %collective-permute-done.refs_7_), channel_id=1, source_target_pairs={{0,4},{4,8},{8,12},{12,0},{1,5},{5,9},{9,13},{13,1},{2,6},{6,10},{... | collective-permute-start | bytes 737288 | tf_op jit(solution)/shard_map/ppermute | solution.py:242
  42.4 17.4 %collective-permute-start.7 = (bf16[88,2560]{1,0:T(8,128)(2,1)S(1)}, bf16[88,2560]{1,0:T(8,128)(2,1)S(1)}, u32[]{:S(2)}, u32[]{:S(2)}) collective-permute-start(bf16[88,2560]{1,0:T(8,128)(2,1)S(1)} %collective-permute-done.2.refs_4_), channel_id=1, source_target_pairs={{0,16},{16,0},{1,17},{17,1},{2,18},{18,2},{3,19},{19,3},{4,20},{20... | collective-permute-start | bytes 1351688 | tf_op jit(solution)/shard_map/ppermute | solution.py:268
  54.2 10.1 %copy-start.2 = (bf16[256,2560]{1,0:T(8,128)(2,1)S(1)}, bf16[256,2560]{1,0:T(8,128)(2,1)}, u32[]{:S(2)}) copy-start(bf16[256,2560]{1,0:T(8,128)(2,1)} %refs_2_.1) | copy-start | bytes 3932164
  54.2 10.1 %copy-start.1 = (bf16[2,256,2560]{2,1,0:T(8,128)(2,1)S(1)}, bf16[2,256,2560]{2,1,0:T(8,128)(2,1)}, u32[]{:S(2)}) copy-start(bf16[2,256,2560]{2,1,0:T(8,128)(2,1)} %param.7) | copy-start | bytes 7864324
  57.0 14.3 %collective-permute-start.11 = (bf16[128,2560]{1,0:T(8,128)(2,1)S(1)}, bf16[128,2560]{1,0:T(8,128)(2,1)S(1)}, u32[]{:S(2)}, u32[]{:S(2)}) collective-permute-start(bf16[128,2560]{1,0:T(8,128)(2,1)S(1)} %pad_maximum_fusion.refs_2_), channel_id=1, source_target_pairs={{0,16},{16,0},{1,17},{17,1},{2,18},{18,2},{3,19},{19,3},{4,20},{20... | collective-permute-start | bytes 1966088 | tf_op jit(solution)/shard_map/ppermute | solution.py:268
  58.2 17.2 %collective-permute-start.16 = (bf16[576,512]{1,0:T(8,128)(2,1)S(1)}, bf16[576,512]{1,0:T(8,128)(2,1)S(1)}, u32[]{:S(2)}, u32[]{:S(2)}) collective-permute-start(bf16[576,512]{1,0:T(8,128)(2,1)S(1)} %pad_maximum_fusion.1), channel_id=1, source_target_pairs={{0,2},{2,0},{1,3},{3,1},{4,6},{6,4},{5,7},{7,5},{8,10},{10,8},{9,1... | collective-permute-start | bytes 1769480 | tf_op jit(solution)/shard_map/ppermute | solution.py:329
  70.3 4.5 %copy-start.4 = (s32[4]{0:T(128)S(1)}, s32[4]{0:T(128)}, u32[]{:S(2)}) copy-start(s32[4]{0:T(128)} %constant.97.clone) | copy-start | bytes 52
  70.4 5.0 %collective-permute-start.12 = (f32[2,512,128]{2,1,0:T(8,128)S(1)}, f32[2,512,128]{2,1,0:T(8,128)S(1)}, u32[]{:S(2)}, u32[]{:S(2)}) collective-permute-start(f32[2,512,128]{2,1,0:T(8,128)S(1)} %get-tuple-element.37), channel_id=1, source_target_pairs={{0,1},{1,0},{2,3},{3,2},{4,5},{5,4},{6,7},{7,6},{8,9},{9,8},{10,11... | collective-permute-start | bytes 1572872 | tf_op jit(solution)/shard_map/ppermute | solution.py:295
  70.4 4.9 %collective-permute-start.13 = (f32[2,512,128]{2,1,0:T(8,128)S(1)}, f32[2,512,128]{2,1,0:T(8,128)S(1)}, u32[]{:S(2)}, u32[]{:S(2)}) collective-permute-start(f32[2,512,128]{2,1,0:T(8,128)S(1)} %get-tuple-element.38), channel_id=1, source_target_pairs={{0,1},{1,0},{2,3},{3,2},{4,5},{5,4},{6,7},{7,6},{8,9},{9,8},{10,11... | collective-permute-start | bytes 1572872 | tf_op jit(solution)/shard_map/ppermute | solution.py:295
  70.9 4.5 %collective-permute-start.14 = (f32[2,512,128]{2,1,0:T(8,128)S(1)}, f32[2,512,128]{2,1,0:T(8,128)S(1)}, u32[]{:S(2)}, u32[]{:S(2)}) collective-permute-start(f32[2,512,128]{2,1,0:T(8,128)S(1)} %get-tuple-element.39), channel_id=1, source_target_pairs={{0,1},{1,0},{2,3},{3,2},{4,5},{5,4},{6,7},{7,6},{8,9},{9,8},{10,11... | collective-permute-start | bytes 1572872 | tf_op jit(solution)/shard_map/ppermute | solution.py:295
  74.6 2.0 %collective-permute-start.15 = (f32[2,512,128]{2,1,0:T(8,128)S(1)}, f32[2,512,128]{2,1,0:T(8,128)S(1)}, u32[]{:S(2)}, u32[]{:S(2)}) collective-permute-start(f32[2,512,128]{2,1,0:T(8,128)S(1)} %get-tuple-element.40), channel_id=1, source_target_pairs={{0,1},{1,0},{2,3},{3,2},{4,5},{5,4},{6,7},{7,6},{8,9},{9,8},{10,11... | collective-permute-start | bytes 1572872 | tf_op jit(solution)/shard_map/ppermute | solution.py:295
  78.6 7.4 %collective-permute-start.17 = (f32[1,136,128]{2,1,0:T(8,128)S(1)}, f32[1,136,128]{2,1,0:T(8,128)S(1)}, u32[]{:S(2)}, u32[]{:S(2)}) collective-permute-start(f32[1,136,128]{2,1,0:T(8,128)S(1)} %get-tuple-element.61), channel_id=1, source_target_pairs={{0,4},{4,8},{8,12},{12,0},{1,5},{5,9},{9,13},{13,1},{2,6},{6,10},{... | collective-permute-start | bytes 208904 | tf_op jit(solution)/shard_map/ppermute | solution.py:242
  80.4 8.5 %collective-permute-start.18 = (f32[1,136,128]{2,1,0:T(8,128)S(1)}, f32[1,136,128]{2,1,0:T(8,128)S(1)}, u32[]{:S(2)}, u32[]{:S(2)}) collective-permute-start(f32[1,136,128]{2,1,0:T(8,128)S(1)} %get-tuple-element.60), channel_id=1, source_target_pairs={{0,8},{4,12},{8,0},{12,4},{1,9},{5,13},{9,1},{13,5},{2,10},{6,14},... | collective-permute-start | bytes 208904 | tf_op jit(solution)/shard_map/ppermute | solution.py:242
  83.9 5.2 %collective-permute-start.19 = (f32[1,136,128]{2,1,0:T(8,128)S(1)}, f32[1,136,128]{2,1,0:T(8,128)S(1)}, u32[]{:S(2)}, u32[]{:S(2)}) collective-permute-start(f32[1,136,128]{2,1,0:T(8,128)S(1)} %get-tuple-element.59), channel_id=1, source_target_pairs={{0,12},{4,0},{8,4},{12,8},{1,13},{5,1},{9,5},{13,9},{2,14},{6,2},{... | collective-permute-start | bytes 208904 | tf_op jit(solution)/shard_map/ppermute | solution.py:242
  89.3 3.8 %collective-permute-start.21 = (bf16[1,16,512]{2,1,0:T(8,128)(2,1)S(1)}, bf16[1,16,512]{2,1,0:T(8,128)(2,1)S(1)}, u32[]{:S(2)}, u32[]{:S(2)}) collective-permute-start(bf16[1,16,512]{2,1,0:T(8,128)(2,1)S(1)} %get-tuple-element.73), channel_id=1, source_target_pairs={{0,2},{2,0},{1,3},{3,1},{4,6},{6,4},{5,7},{7,5},{8,10},{10,8},{9,1... | collective-permute-start | bytes 49160 | tf_op jit(solution)/shard_map/ppermute | solution.py:356
  90.4 3.2 %collective-permute-start.22 = (bf16[1,16,512]{2,1,0:T(8,128)(2,1)S(1)}, bf16[1,16,512]{2,1,0:T(8,128)(2,1)S(1)}, u32[]{:S(2)}, u32[]{:S(2)}) collective-permute-start(bf16[1,16,512]{2,1,0:T(8,128)(2,1)S(1)} %get-tuple-element.73), channel_id=1, source_target_pairs={{0,3},{3,0},{1,2},{2,1},{4,7},{7,4},{5,6},{6,5},{8,11},{11,8},{9,1... | collective-permute-start | bytes 49160 | tf_op jit(solution)/shard_map/ppermute | solution.py:357
  90.5 1.9 %collective-permute-start.20 = (bf16[1,16,512]{2,1,0:T(8,128)(2,1)S(1)}, bf16[1,16,512]{2,1,0:T(8,128)(2,1)S(1)}, u32[]{:S(2)}, u32[]{:S(2)}) collective-permute-start(bf16[1,16,512]{2,1,0:T(8,128)(2,1)S(1)} %get-tuple-element.74.mine_ref), channel_id=1, source_target_pairs={{0,1},{1,0},{2,3},{3,2},{4,5},{5,4},{6,7},{7,6},{8,9},{9,8},{10,11... | collective-permute-start | bytes 49160 | tf_op jit(solution)/shard_map/ppermute | solution.py:355

commit v18 on v16

--- a/solution.py
+++ b/solution.py
@@ -264,7 +264,7 @@
         opposite = [jnp.concatenate([opposite[0], opposite[1][: lengths[1]]], axis=0)]
         queries = jnp.concatenate([queries] + around, axis=0)
         swapped = []
-        for at, piece in enumerate([below[0], above[0], below[1], above[1]] + opposite):
+        for at, piece in enumerate([below[0], above[0], below[1][: lengths[1]], above[1][: lengths[1]]] + opposite):
             swapped.append(lax.ppermute(after(piece, swapped[max(at - 2, 0) : max(at - 1, 0)]), "groups", SWAP))
         weights = [down_weight] + above + swapped[1:4:2] + below + swapped[0:4:2] + opposite + swapped[4:]
         flags = jnp.stack([core, (group == core).astype(core.dtype)])

time: 94.6 us -> 94.6 us (level)
    ppermute x5, waiting for transfers between devices: 8.45 us -> 1.21 us  [body(): lax.ppermute(after(piece, swapped[max(at - 2, 0):max(at - 1, 0)]), 'group...]
    ppermute x9, waiting for transfers between devices: 34.5 us -> 41.1 us  [shifted(): lax.ppermute(array, 'high', [(at, (at + shift) % highs) for at in range(h...]
  transfers between devices with their start and end apart: 23 -> 23, of which waited for: 14 -> 15; matrix products, arithmetic and copies ran while one was open for 1% -> 1% of each run, Pallas kernels for 10% -> 10%
where the time goes in v18:
time: 94.6 us; the launch traced here: 94.4 us
  waiting for transfers between devices  50.7 us (54%)
  starting transfers between devices  28.6 us (30%)
  Pallas kernels  12.7 us (13%)
  local copies, waits for them, and re-layouts  1.64 us (2%)
    ppermute x9, waiting for transfers between devices, shifted(): lax.ppermute(array, 'high', [(at, (at + shift) % highs) for at in range(h...  41.1 us
    ppermute x9, starting transfers between devices, shifted(): lax.ppermute(array, 'high', [(at, (at + shift) % highs) for at in range(h...  15.9 us
    pallas_call x2, Pallas kernels, project(): pl.pallas_call(functools.partial(project_kernel, jobs=jobs, sends=sends),...  9.32 us
    ppermute x5, starting transfers between devices, body(): lax.ppermute(after(piece, swapped[max(at - 2, 0):max(at - 1, 0)]), 'group...  6.28 us
    ppermute x1, waiting for transfers between devices, body(): partner_hidden = lax.ppermute(hidden, 'side', SWAP)  4.97 us
    pallas_call x1, Pallas kernels, body(): pl.pallas_call(functools.partial(attend_kernel, pieces=pieces), out_shape...  1.96 us
  transfers between devices with their start and end apart: 23, of which 15 were waited for; matrix products, arithmetic and copies ran while one was open for 1% of the time, Pallas kernels for 10%

profile of v18, /device:TPU:0, one launch (start us, length us, event | category | flops | bytes accessed | tf_op | source)
XLA Modules:
  0.0 94.4 jit_solution(2884671842551129835)
XLA Ops:
  0.0 1.3 %constant_dynamic-slice_fusion.4 = (bf16[64,2560]{1,0:T(8,128)(2,1)S(1)}, bf16[64,2560]{1,0:T(8,128)(2,1)S(1)}) fusion(bf16[256,2560]{1,0:T(8,128)(2,1)} %refs_2_.1, s32[]{:T(128)S(6)} %select_n.73, s32[]{:T(128)S(6)} %select_n.72), kind=kLoop, calls=%fused_computation.23 | loop fusion | bytes 1310728 | tf_op jit(solution)/shard_map/dynamic_slice | solution.py:254
  1.3 3.1 %collective-permute-start = (bf16[64,2560]{1,0:T(8,128)(2,1)S(1)}, bf16[64,2560]{1,0:T(8,128)(2,1)S(1)}, u32[]{:S(2)}, u32[]{:S(2)}) collective-permute-start(bf16[64,2560]{1,0:T(8,128)(2,1)S(1)} %get-tuple-element.23), channel_id=1, source_target_pairs={{0,4},{4,8},{8,12},{12,0},{1,5},{5,9},{9,13},{13,1},{2,6},{6,10},{... | collective-permute-start | bytes 983048 | tf_op jit(solution)/shard_map/ppermute | solution.py:242
  4.4 1.5 %collective-permute-start.5 = (bf16[512,2560]{1,0:T(8,128)(2,1)}, bf16[512,2560]{1,0:T(8,128)(2,1)}, u32[]{:S(2)}, u32[]{:S(2)}) collective-permute-start(bf16[512,2560]{1,0:T(8,128)(2,1)} %bitcast.21), channel_id=1, source_target_pairs={{0,2},{2,0},{1,3},{3,1},{4,6},{6,4},{5,7},{7,5},{8,10},{10,8},{9,1... | collective-permute-start | bytes 7864328 | tf_op jit(solution)/shard_map/ppermute | solution.py:245
  6.1 8.0 %collective-permute-done.refs_7_ = bf16[64,2560]{1,0:T(8,128)(2,1)S(1)} collective-permute-done((bf16[64,2560]{1,0:T(8,128)(2,1)S(1)}, bf16[64,2560]{1,0:T(8,128)(2,1)S(1)}, u32[]{:S(2)}, u32[]{:S(2)}) %collective-permute-start) | collective-permute-done | bytes 327712 | tf_op jit(solution)/shard_map/ppermute | solution.py:242
  14.1 3.8 %collective-permute-start.1 = (bf16[64,2560]{1,0:T(8,128)(2,1)}, bf16[64,2560]{1,0:T(8,128)(2,1)S(1)}, u32[]{:S(2)}, u32[]{:S(2)}) collective-permute-start(bf16[64,2560]{1,0:T(8,128)(2,1)} %copy-done.3), channel_id=1, source_target_pairs={{0,12},{4,0},{8,4},{12,8},{1,13},{5,1},{9,5},{13,9},{2,14},{6,2},{... | collective-permute-start | bytes 983048 | tf_op jit(solution)/shard_map/ppermute | solution.py:242
  18.0 1.5 %collective-permute-start.8 = (bf16[64,2560]{1,0:T(8,128)(2,1)S(1)}, bf16[64,2560]{1,0:T(8,128)(2,1)S(1)}, u32[]{:S(2)}, u32[]{:S(2)}) collective-permute-start(bf16[64,2560]{1,0:T(8,128)(2,1)S(1)} %collective-permute-done.refs_7_), channel_id=1, source_target_pairs={{0,16},{16,0},{1,17},{17,1},{2,18},{18,2},{3,19},{19,3},{4,20},{20... | collective-permute-start | bytes 983048 | tf_op jit(solution)/shard_map/ppermute | solution.py:268
  19.8 11.4 %collective-permute-done.1.refs_3_ = bf16[64,2560]{1,0:T(8,128)(2,1)S(1)} collective-permute-done((bf16[64,2560]{1,0:T(8,128)(2,1)}, bf16[64,2560]{1,0:T(8,128)(2,1)S(1)}, u32[]{:S(2)}, u32[]{:S(2)}) %collective-permute-start.1) | collective-permute-done | bytes 327712 | tf_op jit(solution)/shard_map/ppermute | solution.py:242
  31.1 1.9 %collective-permute-start.2 = (bf16[72,2560]{1,0:T(8,128)(2,1)S(1)}, bf16[72,2560]{1,0:T(8,128)(2,1)S(1)}, u32[]{:S(2)}, u32[]{:S(2)}) collective-permute-start(bf16[72,2560]{1,0:T(8,128)(2,1)S(1)} %pad_maximum_fusion.2), channel_id=1, source_target_pairs={{0,12},{4,0},{8,4},{12,8},{1,13},{5,1},{9,5},{13,9},{2,14},{6,2},{... | collective-permute-start | bytes 1105928 | tf_op jit(solution)/shard_map/ppermute | solution.py:242
  33.1 1.3 %collective-permute-start.6 = (bf16[64,2560]{1,0:T(8,128)(2,1)S(1)}, bf16[64,2560]{1,0:T(8,128)(2,1)S(1)}, u32[]{:S(2)}, u32[]{:S(2)}) collective-permute-start(bf16[64,2560]{1,0:T(8,128)(2,1)S(1)} %collective-permute-done.1.refs_3_), channel_id=1, source_target_pairs={{0,16},{16,0},{1,17},{17,1},{2,18},{18,2},{3,19},{19,3},{4,20},{20... | collective-permute-start | bytes 983048 | tf_op jit(solution)/shard_map/ppermute | solution.py:268
  34.4 0.8 collective-permute-start.9
  35.4 6.7 %collective-permute-done.2.refs_4_ = bf16[72,2560]{1,0:T(8,128)(2,1)S(1)} collective-permute-done((bf16[72,2560]{1,0:T(8,128)(2,1)S(1)}, bf16[72,2560]{1,0:T(8,128)(2,1)S(1)}, u32[]{:S(2)}, u32[]{:S(2)}) %collective-permute-start.2) | collective-permute-done | bytes 368672 | tf_op jit(solution)/shard_map/ppermute | solution.py:242
  42.5 1.2 %collective-permute-done.6.refs_5_ = bf16[64,2560]{1,0:T(8,128)(2,1)S(1)} collective-permute-done((bf16[64,2560]{1,0:T(8,128)(2,1)S(1)}, bf16[64,2560]{1,0:T(8,128)(2,1)S(1)}, u32[]{:S(2)}, u32[]{:S(2)}) %collective-permute-start.6) | collective-permute-done | bytes 327712 | tf_op jit(solution)/shard_map/ppermute | solution.py:268
  43.7 1.6 %collective-permute-start.7 = (bf16[64,2560]{1,0:T(8,128)(2,1)S(1)}, bf16[64,2560]{1,0:T(8,128)(2,1)S(1)}, u32[]{:S(2)}, u32[]{:S(2)}) collective-permute-start(bf16[64,2560]{1,0:T(8,128)(2,1)S(1)} %slice.140), channel_id=1, source_target_pairs={{0,16},{16,0},{1,17},{17,1},{2,18},{18,2},{3,19},{19,3},{4,20},{20... | collective-permute-start | bytes 983048 | tf_op jit(solution)/shard_map/ppermute | solution.py:268
  45.3 6.9 %collective-permute-done.4 = bf16[72,2560]{1,0:T(8,128)(2,1)S(1)} collective-permute-done((bf16[72,2560]{1,0:T(8,128)(2,1)S(1)}, bf16[72,2560]{1,0:T(8,128)(2,1)S(1)}, u32[]{:S(2)}, u32[]{:S(2)}) %collective-permute-start.4) | collective-permute-done | bytes 368672 | tf_op jit(solution)/shard_map/ppermute | solution.py:242
  52.2 4.5 %collective-permute-done.10 = bf16[64,2560]{1,0:T(8,128)(2,1)S(1)} collective-permute-done((bf16[64,2560]{1,0:T(8,128)(2,1)S(1)}, bf16[64,2560]{1,0:T(8,128)(2,1)S(1)}, u32[]{:S(2)}, u32[]{:S(2)}) %collective-permute-start.10) | collective-permute-done | bytes 327712 | tf_op jit(solution)/shard_map/ppermute | solution.py:242
  56.7 1.1 %collective-permute-start.11 = (bf16[128,2560]{1,0:T(8,128)(2,1)S(1)}, bf16[128,2560]{1,0:T(8,128)(2,1)S(1)}, u32[]{:S(2)}, u32[]{:S(2)}) collective-permute-start(bf16[128,2560]{1,0:T(8,128)(2,1)S(1)} %pad_maximum_fusion.refs_2_), channel_id=1, source_target_pairs={{0,16},{16,0},{1,17},{17,1},{2,18},{18,2},{3,19},{19,3},{4,20},{20... | collective-permute-start | bytes 1966088 | tf_op jit(solution)/shard_map/ppermute | solution.py:268
  58.0 1.6 %collective-permute-start.16 = (bf16[576,512]{1,0:T(8,128)(2,1)S(1)}, bf16[576,512]{1,0:T(8,128)(2,1)S(1)}, u32[]{:S(2)}, u32[]{:S(2)}) collective-permute-start(bf16[576,512]{1,0:T(8,128)(2,1)S(1)} %pad_maximum_fusion.1), channel_id=1, source_target_pairs={{0,2},{2,0},{1,3},{3,1},{4,6},{6,4},{5,7},{7,5},{8,10},{10,8},{9,1... | collective-permute-start | bytes 1769480 | tf_op jit(solution)/shard_map/ppermute | solution.py:329
  59.5 5.0 %collective-permute-done.5.refs_1_ = bf16[512,2560]{1,0:T(8,128)(2,1)} collective-permute-done((bf16[512,2560]{1,0:T(8,128)(2,1)}, bf16[512,2560]{1,0:T(8,128)(2,1)}, u32[]{:S(2)}, u32[]{:S(2)}) %collective-permute-start.5) | collective-permute-done | bytes 2621472 | tf_op jit(solution)/shard_map/ppermute | solution.py:245
  64.5 6.0 %project_near.1 = (f32[6,512,128]{2,1,0:T(8,128)S(1)}, f32[2,512,128]{2,1,0:T(8,128)S(1)}, f32[2,512,128]{2,1,0:T(8,128)S(1)}, f32[2,512,128]{2,1,0:T(8,128)S(1)}) custom-call(s32[2]{0:T(128)S(1)} %pad_add_fusion.3.flag_ref, bf16[512,2560]{1,0:T(8,128)(2,1)S(1)} %bitcast.22, bf16[512,2560]{1,0:T(8,128)(2,1)} %collective-permute-done.5.refs_1_, ...), custom_call_target="tpu_custom_call" | custom-call | flops 4026531840 | bytes 1 | tf_op jit(solution)/shard_map/project_near/pallas_call | solution.py:190
  71.2 3.3 %project_far.1 = (f32[2,512,128]{2,1,0:T(8,128)S(1)}, f32[2,512,128]{2,1,0:T(8,128)S(1)}) custom-call(s32[2]{0:T(128)S(1)} %pad_add_fusion.3.flag_ref, bf16[512,2560]{1,0:T(8,128)(2,1)S(1)} %bitcast.23, bf16[512,2560]{1,0:T(8,128)(2,1)} %collective-permute-done.5.refs_1_, bf16[128,2560]{1,0:T(8,128)(2,1)S(1)} %pad_maximum_fusion.refs_2_, ...), custom_call_target="tpu_custom_call" | custom-call | flops 1 | bytes 1 | tf_op jit(solution)/shard_map/project_far/pallas_call | solution.py:190
  75.0 0.5 collective-permute-done.16.refs_7_
  75.6 1.0 %collective-permute-done.15.refs_5_ = f32[2,512,128]{2,1,0:T(8,128)S(1)} collective-permute-done((f32[2,512,128]{2,1,0:T(8,128)S(1)}, f32[2,512,128]{2,1,0:T(8,128)S(1)}, u32[]{:S(2)}, u32[]{:S(2)}) %collective-permute-start.15) | collective-permute-done | bytes 524320 | tf_op jit(solution)/shard_map/ppermute | solution.py:295
  76.5 2.0 %attend.1 = f32[4,136,128]{2,1,0:T(8,128)S(1)} custom-call(s32[4]{0:T(128)S(1)} %pad_add_fusion.2.place_ref, s32[2,4]{1,0:T(2,128)S(1)} %pad_add_fusion.spot_ref, bf16[4,16,512]{2,1,0:T(8,128)(2,1)S(1)} %get-tuple-element.66.query_ref, f32[6,512,128]{2,1,0:T(8,128)S(1)} %get-tuple-element.32.refs_0_, f32[2,512,128]{2,1,0:T(8,128)S(1)} %get-tuple-element.36.refs_1_, ...), custom_call_target="tpu_custom_call" | custom-call | tf_op jit(solution)/shard_map/attend/pallas_call | solution.py:332
  78.5 1.6 %collective-permute-start.17 = (f32[1,136,128]{2,1,0:T(8,128)S(1)}, f32[1,136,128]{2,1,0:T(8,128)S(1)}, u32[]{:S(2)}, u32[]{:S(2)}) collective-permute-start(f32[1,136,128]{2,1,0:T(8,128)S(1)} %get-tuple-element.63), channel_id=1, source_target_pairs={{0,4},{4,8},{8,12},{12,0},{1,5},{5,9},{9,13},{13,1},{2,6},{6,10},{... | collective-permute-start | bytes 208904 | tf_op jit(solution)/shard_map/ppermute | solution.py:242
  80.2 3.4 %collective-permute-start.18 = (f32[1,136,128]{2,1,0:T(8,128)S(1)}, f32[1,136,128]{2,1,0:T(8,128)S(1)}, u32[]{:S(2)}, u32[]{:S(2)}) collective-permute-start(f32[1,136,128]{2,1,0:T(8,128)S(1)} %get-tuple-element.62), channel_id=1, source_target_pairs={{0,8},{4,12},{8,0},{12,4},{1,9},{5,13},{9,1},{13,5},{2,10},{6,14},... | collective-permute-start | bytes 208904 | tf_op jit(solution)/shard_map/ppermute | solution.py:242
  83.6 1.5 %collective-permute-start.19 = (f32[1,136,128]{2,1,0:T(8,128)S(1)}, f32[1,136,128]{2,1,0:T(8,128)S(1)}, u32[]{:S(2)}, u32[]{:S(2)}) collective-permute-start(f32[1,136,128]{2,1,0:T(8,128)S(1)} %get-tuple-element.61), channel_id=1, source_target_pairs={{0,12},{4,0},{8,4},{12,8},{1,13},{5,1},{9,5},{13,9},{2,14},{6,2},{... | collective-permute-start | bytes 208904 | tf_op jit(solution)/shard_map/ppermute | solution.py:242
  85.6 3.0 %collective-permute-done.18.refs_2_ = f32[1,136,128]{2,1,0:T(8,128)S(1)} collective-permute-done((f32[1,136,128]{2,1,0:T(8,128)S(1)}, f32[1,136,128]{2,1,0:T(8,128)S(1)}, u32[]{:S(2)}, u32[]{:S(2)}) %collective-permute-start.18) | collective-permute-done | bytes 69664 | tf_op jit(solution)/shard_map/ppermute | solution.py:242
  89.0 1.0 %collective-permute-start.21 = (bf16[1,16,512]{2,1,0:T(8,128)(2,1)S(1)}, bf16[1,16,512]{2,1,0:T(8,128)(2,1)S(1)}, u32[]{:S(2)}, u32[]{:S(2)}) collective-permute-start(bf16[1,16,512]{2,1,0:T(8,128)(2,1)S(1)} %get-tuple-element.75), channel_id=1, source_target_pairs={{0,2},{2,0},{1,3},{3,1},{4,6},{6,4},{5,7},{7,5},{8,10},{10,8},{9,1... | collective-permute-start | bytes 49160 | tf_op jit(solution)/shard_map/ppermute | solution.py:356
  90.2 1.0 %collective-permute-start.20 = (bf16[1,16,512]{2,1,0:T(8,128)(2,1)S(1)}, bf16[1,16,512]{2,1,0:T(8,128)(2,1)S(1)}, u32[]{:S(2)}, u32[]{:S(2)}) collective-permute-start(bf16[1,16,512]{2,1,0:T(8,128)(2,1)S(1)} %get-tuple-element.76.mine_ref), channel_id=1, source_target_pairs={{0,1},{1,0},{2,3},{3,2},{4,5},{5,4},{6,7},{7,6},{8,9},{9,8},{10,11... | collective-permute-start | bytes 49160 | tf_op jit(solution)/shard_map/ppermute | solution.py:355
  91.3 0.8 collective-permute-done.20.core_ref
  92.1 0.8 collective-permute-done.21.side_ref
  93.2 1.2 %assemble.1 = bf16[1,16,2048]{2,1,0:T(8,128)(2,1)} custom-call(s32[2]{0:T(128)S(1)} %pad_add_fusion.1.flag_ref, bf16[1,16,512]{2,1,0:T(8,128)(2,1)S(1)} %get-tuple-element.76.mine_ref, bf16[1,16,512]{2,1,0:T(8,128)(2,1)S(1)} %collective-permute-done.20.core_ref, bf16[1,16,512]{2,1,0:T(8,128)(2,1)S(1)} %collective-permute-done.21.side_ref, ...), custom_call_target="tpu_custom_call" | custom-call | tf_op jit(solution)/shard_map/assemble/pallas_call | solution.py:364
  (67 shorter events, 4.2 us)
Async XLA Ops:
  0.0 5.9 %copy-start.4 = (bf16[1,16,2048]{2,1,0:T(8,128)(2,1)S(1)}, bf16[1,16,2048]{2,1,0:T(8,128)(2,1)}, u32[]{:S(2)}) copy-start(bf16[1,16,2048]{2,1,0:T(8,128)(2,1)} %param.12) | copy-start | bytes 196612
  0.0 5.9 %copy-start.6 = (s32[8]{0:T(128)S(1)}, s32[8]{0:T(128)}, u32[]{:S(2)}) copy-start(s32[8]{0:T(128)} %param.11) | copy-start | bytes 100
  0.0 5.9 %copy-start.7 = (s32[16,1]{0,1:T(1,128)S(1)}, s32[16,1]{0,1:T(1,128)}, u32[]{:S(2)}) copy-start(s32[16,1]{0,1:T(1,128)} %param.10) | copy-start | bytes 196
  0.0 19.6 %copy-start = (bf16[2,256,2048]{2,1,0:T(8,128)(2,1)S(1)}, bf16[2,256,2048]{2,1,0:T(8,128)(2,1)}, u32[]{:S(2)}) copy-start(bf16[2,256,2048]{2,1,0:T(8,128)(2,1)} %param.8) | copy-start | bytes 6291460
  1.3 4.8 %copy-start.3 = (bf16[64,2560]{1,0:T(8,128)(2,1)}, bf16[64,2560]{1,0:T(8,128)(2,1)S(1)}, u32[]{:S(2)}) copy-start(bf16[64,2560]{1,0:T(8,128)(2,1)S(1)} %get-tuple-element.23) | copy-start | bytes 983044
  1.3 12.8 %collective-permute-start = (bf16[64,2560]{1,0:T(8,128)(2,1)S(1)}, bf16[64,2560]{1,0:T(8,128)(2,1)S(1)}, u32[]{:S(2)}, u32[]{:S(2)}) collective-permute-start(bf16[64,2560]{1,0:T(8,128)(2,1)S(1)} %get-tuple-element.23), channel_id=1, source_target_pairs={{0,4},{4,8},{8,12},{12,0},{1,5},{5,9},{9,13},{13,1},{2,6},{6,10},{... | collective-permute-start | bytes 983048 | tf_op jit(solution)/shard_map/ppermute | solution.py:242
  4.4 60.1 %collective-permute-start.5 = (bf16[512,2560]{1,0:T(8,128)(2,1)}, bf16[512,2560]{1,0:T(8,128)(2,1)}, u32[]{:S(2)}, u32[]{:S(2)}) collective-permute-start(bf16[512,2560]{1,0:T(8,128)(2,1)} %bitcast.21), channel_id=1, source_target_pairs={{0,2},{2,0},{1,3},{3,1},{4,6},{6,4},{5,7},{7,5},{8,10},{10,8},{9,1... | collective-permute-start | bytes 7864328 | tf_op jit(solution)/shard_map/ppermute | solution.py:245
  14.1 20.2 %collective-permute-start.3 = (bf16[72,2560]{1,0:T(8,128)(2,1)S(1)}, bf16[72,2560]{1,0:T(8,128)(2,1)S(1)}, u32[]{:S(2)}, u32[]{:S(2)}) collective-permute-start(bf16[72,2560]{1,0:T(8,128)(2,1)S(1)} %pad_maximum_fusion.2), channel_id=1, source_target_pairs={{0,4},{4,8},{8,12},{12,0},{1,5},{5,9},{9,13},{13,1},{2,6},{6,10},{... | collective-permute-start | bytes 1105928 | tf_op jit(solution)/shard_map/ppermute | solution.py:242
  14.1 17.0 %collective-permute-start.1 = (bf16[64,2560]{1,0:T(8,128)(2,1)}, bf16[64,2560]{1,0:T(8,128)(2,1)S(1)}, u32[]{:S(2)}, u32[]{:S(2)}) collective-permute-start(bf16[64,2560]{1,0:T(8,128)(2,1)} %copy-done.3), channel_id=1, source_target_pairs={{0,12},{4,0},{8,4},{12,8},{1,13},{5,1},{9,5},{13,9},{2,14},{6,2},{... | collective-permute-start | bytes 983048 | tf_op jit(solution)/shard_map/ppermute | solution.py:242
  18.0 16.4 %collective-permute-start.8 = (bf16[64,2560]{1,0:T(8,128)(2,1)S(1)}, bf16[64,2560]{1,0:T(8,128)(2,1)S(1)}, u32[]{:S(2)}, u32[]{:S(2)}) collective-permute-start(bf16[64,2560]{1,0:T(8,128)(2,1)S(1)} %collective-permute-done.refs_7_), channel_id=1, source_target_pairs={{0,16},{16,0},{1,17},{17,1},{2,18},{18,2},{3,19},{19,3},{4,20},{20... | collective-permute-start | bytes 983048 | tf_op jit(solution)/shard_map/ppermute | solution.py:268
  31.1 11.0 %collective-permute-start.2 = (bf16[72,2560]{1,0:T(8,128)(2,1)S(1)}, bf16[72,2560]{1,0:T(8,128)(2,1)S(1)}, u32[]{:S(2)}, u32[]{:S(2)}) collective-permute-start(bf16[72,2560]{1,0:T(8,128)(2,1)S(1)} %pad_maximum_fusion.2), channel_id=1, source_target_pairs={{0,12},{4,0},{8,4},{12,8},{1,13},{5,1},{9,5},{13,9},{2,14},{6,2},{... | collective-permute-start | bytes 1105928 | tf_op jit(solution)/shard_map/ppermute | solution.py:242
  33.1 10.6 %collective-permute-start.6 = (bf16[64,2560]{1,0:T(8,128)(2,1)S(1)}, bf16[64,2560]{1,0:T(8,128)(2,1)S(1)}, u32[]{:S(2)}, u32[]{:S(2)}) collective-permute-start(bf16[64,2560]{1,0:T(8,128)(2,1)S(1)} %collective-permute-done.1.refs_3_), channel_id=1, source_target_pairs={{0,16},{16,0},{1,17},{17,1},{2,18},{18,2},{3,19},{19,3},{4,20},{20... | collective-permute-start | bytes 983048 | tf_op jit(solution)/shard_map/ppermute | solution.py:268
  34.4 22.3 %collective-permute-start.9 = (bf16[64,2560]{1,0:T(8,128)(2,1)S(1)}, bf16[64,2560]{1,0:T(8,128)(2,1)S(1)}, u32[]{:S(2)}, u32[]{:S(2)}) collective-permute-start(bf16[64,2560]{1,0:T(8,128)(2,1)S(1)} %slice.141), channel_id=1, source_target_pairs={{0,16},{16,0},{1,17},{17,1},{2,18},{18,2},{3,19},{19,3},{4,20},{20... | collective-permute-start | bytes 983048 | tf_op jit(solution)/shard_map/ppermute | solution.py:268
  35.2 17.0 %collective-permute-start.4 = (bf16[72,2560]{1,0:T(8,128)(2,1)S(1)}, bf16[72,2560]{1,0:T(8,128)(2,1)S(1)}, u32[]{:S(2)}, u32[]{:S(2)}) collective-permute-start(bf16[72,2560]{1,0:T(8,128)(2,1)S(1)} %collective-permute-done.3.refs_8_), channel_id=1, source_target_pairs={{0,4},{4,8},{8,12},{12,0},{1,5},{5,9},{9,13},{13,1},{2,6},{6,10},{... | collective-permute-start | bytes 1105928 | tf_op jit(solution)/shard_map/ppermute | solution.py:242
  42.1 14.6 %collective-permute-start.10 = (bf16[64,2560]{1,0:T(8,128)(2,1)S(1)}, bf16[64,2560]{1,0:T(8,128)(2,1)S(1)}, u32[]{:S(2)}, u32[]{:S(2)}) collective-permute-start(bf16[64,2560]{1,0:T(8,128)(2,1)S(1)} %collective-permute-done.refs_7_), channel_id=1, source_target_pairs={{0,4},{4,8},{8,12},{12,0},{1,5},{5,9},{9,13},{13,1},{2,6},{6,10},{... | collective-permute-start | bytes 983048 | tf_op jit(solution)/shard_map/ppermute | solution.py:242
  43.7 15.8 %collective-permute-start.7 = (bf16[64,2560]{1,0:T(8,128)(2,1)S(1)}, bf16[64,2560]{1,0:T(8,128)(2,1)S(1)}, u32[]{:S(2)}, u32[]{:S(2)}) collective-permute-start(bf16[64,2560]{1,0:T(8,128)(2,1)S(1)} %slice.140), channel_id=1, source_target_pairs={{0,16},{16,0},{1,17},{17,1},{2,18},{18,2},{3,19},{19,3},{4,20},{20... | collective-permute-start | bytes 983048 | tf_op jit(solution)/shard_map/ppermute | solution.py:268
  45.3 19.2 %copy-start.2 = (bf16[256,2560]{1,0:T(8,128)(2,1)S(1)}, bf16[256,2560]{1,0:T(8,128)(2,1)}, u32[]{:S(2)}) copy-start(bf16[256,2560]{1,0:T(8,128)(2,1)} %refs_2_.1) | copy-start | bytes 3932164
  52.2 12.3 %copy-start.1 = (bf16[2,256,2560]{2,1,0:T(8,128)(2,1)S(1)}, bf16[2,256,2560]{2,1,0:T(8,128)(2,1)}, u32[]{:S(2)}) copy-start(bf16[2,256,2560]{2,1,0:T(8,128)(2,1)} %param.7) | copy-start | bytes 7864324
  56.7 14.4 %collective-permute-start.11 = (bf16[128,2560]{1,0:T(8,128)(2,1)S(1)}, bf16[128,2560]{1,0:T(8,128)(2,1)S(1)}, u32[]{:S(2)}, u32[]{:S(2)}) collective-permute-start(bf16[128,2560]{1,0:T(8,128)(2,1)S(1)} %pad_maximum_fusion.refs_2_), channel_id=1, source_target_pairs={{0,16},{16,0},{1,17},{17,1},{2,18},{18,2},{3,19},{19,3},{4,20},{20... | collective-permute-start | bytes 1966088 | tf_op jit(solution)/shard_map/ppermute | solution.py:268
  58.0 17.6 %collective-permute-start.16 = (bf16[576,512]{1,0:T(8,128)(2,1)S(1)}, bf16[576,512]{1,0:T(8,128)(2,1)S(1)}, u32[]{:S(2)}, u32[]{:S(2)}) collective-permute-start(bf16[576,512]{1,0:T(8,128)(2,1)S(1)} %pad_maximum_fusion.1), channel_id=1, source_target_pairs={{0,2},{2,0},{1,3},{3,1},{4,6},{6,4},{5,7},{7,5},{8,10},{10,8},{9,1... | collective-permute-start | bytes 1769480 | tf_op jit(solution)/shard_map/ppermute | solution.py:329
  70.5 4.5 %copy-start.5 = (s32[4]{0:T(128)S(1)}, s32[4]{0:T(128)}, u32[]{:S(2)}) copy-start(s32[4]{0:T(128)} %constant.97.clone) | copy-start | bytes 52
  70.5 5.0 %collective-permute-start.12 = (f32[2,512,128]{2,1,0:T(8,128)S(1)}, f32[2,512,128]{2,1,0:T(8,128)S(1)}, u32[]{:S(2)}, u32[]{:S(2)}) collective-permute-start(f32[2,512,128]{2,1,0:T(8,128)S(1)} %get-tuple-element.37), channel_id=1, source_target_pairs={{0,1},{1,0},{2,3},{3,2},{4,5},{5,4},{6,7},{7,6},{8,9},{9,8},{10,11... | collective-permute-start | bytes 1572872 | tf_op jit(solution)/shard_map/ppermute | solution.py:295
  70.6 5.0 %collective-permute-start.13 = (f32[2,512,128]{2,1,0:T(8,128)S(1)}, f32[2,512,128]{2,1,0:T(8,128)S(1)}, u32[]{:S(2)}, u32[]{:S(2)}) collective-permute-start(f32[2,512,128]{2,1,0:T(8,128)S(1)} %get-tuple-element.38), channel_id=1, source_target_pairs={{0,1},{1,0},{2,3},{3,2},{4,5},{5,4},{6,7},{7,6},{8,9},{9,8},{10,11... | collective-permute-start | bytes 1572872 | tf_op jit(solution)/shard_map/ppermute | solution.py:295
  71.1 4.5 %collective-permute-start.14 = (f32[2,512,128]{2,1,0:T(8,128)S(1)}, f32[2,512,128]{2,1,0:T(8,128)S(1)}, u32[]{:S(2)}, u32[]{:S(2)}) collective-permute-start(f32[2,512,128]{2,1,0:T(8,128)S(1)} %get-tuple-element.39), channel_id=1, source_target_pairs={{0,1},{1,0},{2,3},{3,2},{4,5},{5,4},{6,7},{7,6},{8,9},{9,8},{10,11... | collective-permute-start | bytes 1572872 | tf_op jit(solution)/shard_map/ppermute | solution.py:295
  74.5 2.0 %collective-permute-start.15 = (f32[2,512,128]{2,1,0:T(8,128)S(1)}, f32[2,512,128]{2,1,0:T(8,128)S(1)}, u32[]{:S(2)}, u32[]{:S(2)}) collective-permute-start(f32[2,512,128]{2,1,0:T(8,128)S(1)} %get-tuple-element.40), channel_id=1, source_target_pairs={{0,1},{1,0},{2,3},{3,2},{4,5},{5,4},{6,7},{7,6},{8,9},{9,8},{10,11... | collective-permute-start | bytes 1572872 | tf_op jit(solution)/shard_map/ppermute | solution.py:295
  78.5 7.1 %collective-permute-start.17 = (f32[1,136,128]{2,1,0:T(8,128)S(1)}, f32[1,136,128]{2,1,0:T(8,128)S(1)}, u32[]{:S(2)}, u32[]{:S(2)}) collective-permute-start(f32[1,136,128]{2,1,0:T(8,128)S(1)} %get-tuple-element.63), channel_id=1, source_target_pairs={{0,4},{4,8},{8,12},{12,0},{1,5},{5,9},{9,13},{13,1},{2,6},{6,10},{... | collective-permute-start | bytes 208904 | tf_op jit(solution)/shard_map/ppermute | solution.py:242
  80.2 8.4 %collective-permute-start.18 = (f32[1,136,128]{2,1,0:T(8,128)S(1)}, f32[1,136,128]{2,1,0:T(8,128)S(1)}, u32[]{:S(2)}, u32[]{:S(2)}) collective-permute-start(f32[1,136,128]{2,1,0:T(8,128)S(1)} %get-tuple-element.62), channel_id=1, source_target_pairs={{0,8},{4,12},{8,0},{12,4},{1,9},{5,13},{9,1},{13,5},{2,10},{6,14},... | collective-permute-start | bytes 208904 | tf_op jit(solution)/shard_map/ppermute | solution.py:242
  83.6 5.2 %collective-permute-start.19 = (f32[1,136,128]{2,1,0:T(8,128)S(1)}, f32[1,136,128]{2,1,0:T(8,128)S(1)}, u32[]{:S(2)}, u32[]{:S(2)}) collective-permute-start(f32[1,136,128]{2,1,0:T(8,128)S(1)} %get-tuple-element.61), channel_id=1, source_target_pairs={{0,12},{4,0},{8,4},{12,8},{1,13},{5,1},{9,5},{13,9},{2,14},{6,2},{... | collective-permute-start | bytes 208904 | tf_op jit(solution)/shard_map/ppermute | solution.py:242
  89.0 3.8 %collective-permute-start.21 = (bf16[1,16,512]{2,1,0:T(8,128)(2,1)S(1)}, bf16[1,16,512]{2,1,0:T(8,128)(2,1)S(1)}, u32[]{:S(2)}, u32[]{:S(2)}) collective-permute-start(bf16[1,16,512]{2,1,0:T(8,128)(2,1)S(1)} %get-tuple-element.75), channel_id=1, source_target_pairs={{0,2},{2,0},{1,3},{3,1},{4,6},{6,4},{5,7},{7,5},{8,10},{10,8},{9,1... | collective-permute-start | bytes 49160 | tf_op jit(solution)/shard_map/ppermute | solution.py:356
  90.1 3.2 %collective-permute-start.22 = (bf16[1,16,512]{2,1,0:T(8,128)(2,1)S(1)}, bf16[1,16,512]{2,1,0:T(8,128)(2,1)S(1)}, u32[]{:S(2)}, u32[]{:S(2)}) collective-permute-start(bf16[1,16,512]{2,1,0:T(8,128)(2,1)S(1)} %get-tuple-element.75), channel_id=1, source_target_pairs={{0,3},{3,0},{1,2},{2,1},{4,7},{7,4},{5,6},{6,5},{8,11},{11,8},{9,1... | collective-permute-start | bytes 49160 | tf_op jit(solution)/shard_map/ppermute | solution.py:357
  90.2 1.9 %collective-permute-start.20 = (bf16[1,16,512]{2,1,0:T(8,128)(2,1)S(1)}, bf16[1,16,512]{2,1,0:T(8,128)(2,1)S(1)}, u32[]{:S(2)}, u32[]{:S(2)}) collective-permute-start(bf16[1,16,512]{2,1,0:T(8,128)(2,1)S(1)} %get-tuple-element.76.mine_ref), channel_id=1, source_target_pairs={{0,1},{1,0},{2,3},{3,2},{4,5},{5,4},{6,7},{7,6},{8,9},{9,8},{10,11... | collective-permute-start | bytes 49160 | tf_op jit(solution)/shard_map/ppermute | solution.py:355
